TPU v7x, 32 devices: a whole 2x2x4 slice. The times are simulated.
32 devices in a mesh: dp: 4 (over y, x), ctx: 8 (over z, core).
Axes of the slice: x: 2, y: 2, z: 4, core: 2. Of those that a mesh axis runs over, the one named last changes fastest.
Arguments:
- queries: bfloat16 [4, 2048, 2048], P('dp', 'ctx'), may hold values from -6 to 6
- keys: bfloat16 [4, 2048, 2048], P('dp', 'ctx'), may hold values from -6 to 6
- values: bfloat16 [4, 2048, 2048], P('dp', 'ctx'), may hold values from -6 to 6
- out_grad: bfloat16 [4, 2048, 2048], P('dp', 'ctx'), may hold values from -6 to 6
- segment_ids: int32 [4, 2048], P('dp', 'ctx'), may hold values from 0 to 31, never falling along the last dimension, each value on 1 to 256 neighbouring positions
- image_flags: int32 [4, 32], P('dp'), may hold values 0 or 1
- gain: float32 [2048], replicated, may hold values from 0.25 to 1.75
Outputs:
- output: bfloat16 [4, 2048, 2048], P('dp', 'ctx')
- grad_queries: bfloat16 [4, 2048, 2048], P('dp', 'ctx')
- grad_keys: bfloat16 [4, 2048, 2048], P('dp', 'ctx')
- grad_values: bfloat16 [4, 2048, 2048], P('dp', 'ctx')
- grad_gain: float32 [2048], P(('dp', 'ctx'))
Inputs may be any that keep to these rules, and one draw needn't show every extreme that they name: `segment_ids`: along each sequence the ids never fall, every id from 0 to 31 occurs, and each segment covers 1 to 256 consecutive tokens; some segment covers exactly 256.
All inputs are finite; a program needn't handle non-finite values. No bound on the sum of `image_flags` on one device may be relied on, other than what follows from the above.
Results may differ from a plain program's by a relative error of at most 0.0085.
Values sent between devices are 32-bit elements; how exact they have to be, the bound alone decides.
No kernel may reach another device: no remote copies, remote signals or barrier semaphores. Data moves between devices by JAX's collectives and lax.ppermute only.
A program may use at most 128 MiB of HBM per device.

v0:
```python
import jax
import jax.numpy as jnp
from jax import lax
from jax.sharding import PartitionSpec as P

E = 64


def passed_along(block, axis, distance):
    devices = range(lax.axis_size(axis))
    route = [(i - distance, i) for i in devices if i - distance in devices]
    return lax.ppermute(block, axis, route)


def from_partner(block, axis, stride):
    count = lax.axis_size(axis)
    route = []
    for low in range(count):
        high = low | 1 << stride
        if high != low and high < count:
            route += [(low, high), (high, low)]
    return lax.ppermute(block, axis, route)


def plain(form, a, b):
    return jnp.einsum(form, a, b, preferred_element_type=jnp.float32)


def split_state(state):
    high = state.astype(jnp.bfloat16)
    low = (state - high.astype(jnp.float32)).astype(jnp.bfloat16)
    return (high, low)


def state_product(form, data, state):
    high, low = split_state(state)
    return plain(form, data, high) + plain(form, data, low)


def on_device(queries, keys, values, out_grad, segment_ids, image_flags, gain):
    rows = queries.shape[1]
    heads = queries.shape[2] // E
    q = queries[0].reshape(rows, heads, E)
    k = keys[0].reshape(rows, heads, E)
    v = values[0].reshape(rows, heads, E)
    dy = out_grad[0].reshape(rows, heads, E).astype(jnp.float32)
    seg = segment_ids[0]
    table = image_flags[0]
    onehot = seg[:, None] == jnp.arange(table.shape[0], dtype=jnp.int32)[None, :]
    img = jnp.sum(jnp.where(onehot, table[None, :], 0), axis=1)
    pos = jnp.arange(rows)
    causal = pos[:, None] >= pos[None, :]
    same = seg[:, None] == seg[None, :]
    mask = causal | same & (img[:, None] == 1)
    seg_float = seg.astype(jnp.float32)
    zero_state = jnp.zeros((heads, E, E), jnp.float32)
    parts = lax.axis_size("ctx")
    kv_local = plain("tha,thb->hab", k, v)
    first_sel = seg == seg[0]
    n_local = plain("tha,thb->hab", jnp.where(first_sel[:, None, None], k, jnp.zeros_like(k)), v)
    n_next, next_first = passed_along((n_local, seg_float[:1]), "ctx", -1)
    on_next = ((img == 1) & (seg_float == next_first[0])).astype(jnp.float32)[:, None, None]
    place = lax.axis_index("ctx")
    prefix = zero_state
    total = kv_local
    for bit in range(parts.bit_length() - 1):
        other = from_partner(total, "ctx", bit)
        upper = place >> bit & 1 == 1
        prefix = jnp.where(upper, prefix + other, prefix)
        total = total + other
    scores = plain("tha,sha->hts", q, k)
    probs = jnp.where(mask[None], scores, 0.0).astype(jnp.bfloat16)
    attn = state_product("tha,hab->thb", q, prefix) + on_next * state_product(
        "tha,hab->thb", q, n_next
    )
    attn = attn + plain("hts,shb->thb", probs, v)
    gains = gain.reshape(heads, E)
    scale = lax.rsqrt(jnp.mean(attn * attn, axis=-1, keepdims=True) + 1e-06)
    normed = attn * scale
    output = (normed * gains).astype(jnp.bfloat16)
    ga = dy * gains
    da = scale * (ga - normed * jnp.mean(ga * normed, axis=-1, keepdims=True))
    dab = da.astype(jnp.bfloat16)
    gain_part = jnp.sum(dy * normed, axis=0).reshape(heads * E)
    grad_gain = lax.psum_scatter(gain_part, ("dp", "ctx"), scatter_dimension=0, tiled=True)
    qd_local = plain("tha,thb->hab", q, dab)
    last_sel = (seg == seg[-1]) & (img == 1)
    g_local = plain("tha,thb->hab", jnp.where(last_sel[:, None, None], q, jnp.zeros_like(q)), dab)
    g_prev, prev_last = passed_along((g_local, seg_float[-1:]), "ctx", 1)
    on_prev = (seg_float == prev_last[0]).astype(jnp.float32)[:, None, None]
    place = lax.axis_index("ctx")
    below = zero_state
    whole = qd_local
    for bit in range(parts.bit_length() - 1):
        other = from_partner(whole, "ctx", bit)
        upper = place >> bit & 1 == 1
        below = jnp.where(upper, below + other, below)
        whole = whole + other
    suffix = whole - below - qd_local
    dscores = plain("thb,shb->hts", dab, v)
    dprobs = jnp.where(mask[None], dscores, 0.0).astype(jnp.bfloat16)
    grad_q = state_product("thb,hab->tha", dab, prefix) + on_next * state_product(
        "thb,hab->tha", dab, n_next
    )
    grad_q = grad_q + plain("hts,sha->tha", dprobs, k)
    grad_k = state_product("shb,hab->sha", v, suffix) + on_prev * state_product(
        "shb,hab->sha", v, g_prev
    )
    grad_k = grad_k + plain("hts,tha->sha", dprobs, q)
    grad_v = state_product("sha,hab->shb", k, suffix) + on_prev * state_product(
        "sha,hab->shb", k, g_prev
    )
    grad_v = grad_v + plain("hts,thb->shb", probs, dab)
    shape = (1, rows, heads * E)
    return (
        output.reshape(shape),
        grad_q.astype(jnp.bfloat16).reshape(shape),
        grad_k.astype(jnp.bfloat16).reshape(shape),
        grad_v.astype(jnp.bfloat16).reshape(shape),
        grad_gain,
    )


def solution(mesh):
    return jax.shard_map(
        on_device,
        mesh=mesh,
        in_specs=(
            P("dp", "ctx", None),
            P("dp", "ctx", None),
            P("dp", "ctx", None),
            P("dp", "ctx", None),
            P("dp", "ctx"),
            P("dp", None),
            P(),
        ),
        out_specs=(
            P("dp", "ctx", None),
            P("dp", "ctx", None),
            P("dp", "ctx", None),
            P("dp", "ctx", None),
            P(("dp", "ctx")),
        ),
        check_vma=False,
    )
```

profile of v0, /device:TPU:0, one launch (start us, length us, event | category | flops | bytes accessed | tf_op | source)
XLA Modules:
  0.0 238.6 jit_solution(8033500469579354947)
XLA Ops:
  5.2 2.5 %collective-permute-start.8 = (f32[1]{0:T(128)}, f32[1]{0:T(128)}, u32[]{:S(2)}, u32[]{:S(2)}) collective-permute-start(f32[1]{0:T(128)} %get-tuple-element.34), channel_id=1, source_target_pairs={{0,1},{1,2},{2,3},{3,4},{4,5},{5,6},{6,7},{8,9},{9,10},{10,11},{11... | collective-permute-start | bytes 20 | tf_op jit(solution)/shard_map/ppermute | solution.py:12
  16.2 3.8 %collective-permute-start.1 = (f32[32,64,64]{2,1,0:T(8,128)S(1)}, f32[32,64,64]{2,1,0:T(8,128)S(1)}, u32[]{:S(2)}, u32[]{:S(2)}) collective-permute-start(f32[32,64,64]{2,1,0:T(8,128)S(1)} %add.109), channel_id=1, source_target_pairs={{0,2},{2,0},{1,3},{3,1},{4,6},{6,4},{5,7},{7,5},{8,10},{10,8},{9,1... | collective-permute-start | bytes 1572872 | tf_op jit(solution)/shard_map/ppermute | solution.py:22
  24.0 19.5 %collective-permute-done.1 = f32[32,64,64]{2,1,0:T(8,128)S(1)} collective-permute-done((f32[32,64,64]{2,1,0:T(8,128)S(1)}, f32[32,64,64]{2,1,0:T(8,128)S(1)}, u32[]{:S(2)}, u32[]{:S(2)}) %collective-permute-start.1) | collective-permute-done | bytes 524320 | tf_op jit(solution)/shard_map/ppermute | solution.py:22
  45.6 2.6 %collective-permute-start.2 = (f32[32,64,64]{2,1,0:T(8,128)}, f32[32,64,64]{2,1,0:T(8,128)}, u32[]{:S(2)}, u32[]{:S(2)}) collective-permute-start(f32[32,64,64]{2,1,0:T(8,128)} %add.111), channel_id=1, source_target_pairs={{0,4},{4,0},{1,5},{5,1},{2,6},{6,2},{3,7},{7,3},{8,12},{12,8},{9,1... | collective-permute-start | bytes 1572872 | tf_op jit(solution)/shard_map/ppermute | solution.py:22
  48.2 2.7 %fusion.38 = f32[32,256,64]{1,2,0:T(8,128)} fusion(bf16[32,256,256]{2,1,0:T(8,128)(2,1)S(1)} %select_convert_fusion.1, bf16[256,32,64]{0,2,1:T(8,128)(2,1)S(1)} %bitcast.70), kind=kOutput, calls=%fused_computation.68 | convolution fusion | flops 268435456 | bytes 7340032 | tf_op jit(solution)/shard_map/hts,shb->thb/dot_general | solution.py:26
  50.9 2.6 %copy.91 = f32[1,256,2048]{1,2,0:T(8,128)} copy(bf16[1,256,2048]{2,1,0:T(8,128)(2,1)} %param.10) | data formatting | bytes 3145728 | tf_op jit(solution)/shard_map/convert_element_type | solution.py:46
  53.6 2.1 fusion.26
  55.8 38.2 %collective-permute-done.2 = f32[32,64,64]{2,1,0:T(8,128)} collective-permute-done((f32[32,64,64]{2,1,0:T(8,128)}, f32[32,64,64]{2,1,0:T(8,128)}, u32[]{:S(2)}, u32[]{:S(2)}) %collective-permute-start.2) | collective-permute-done | bytes 524320 | tf_op jit(solution)/shard_map/ppermute | solution.py:22
  97.6 2.3 multiply_reduce_fusion.2
  107.1 3.4 %collective-permute-start.9 = (f32[32,64,64]{2,1,0:T(8,128)}, f32[32,64,64]{2,1,0:T(8,128)}, u32[]{:S(2)}, u32[]{:S(2)}) collective-permute-start(f32[32,64,64]{2,1,0:T(8,128)} %fusion.4), channel_id=1, source_target_pairs={{0,1},{1,2},{2,3},{3,4},{4,5},{5,6},{6,7},{8,9},{9,10},{10,11},{11... | collective-permute-start | bytes 1572872 | tf_op jit(solution)/shard_map/ppermute | solution.py:12
  111.9 2.0 fusion.25
  113.9 3.2 %fusion.1 = bf16[256,32,64]{0,2,1:T(8,128)(2,1)} fusion(f32[32,256,64]{1,2,0:T(8,128)S(1)} %fusion.39, f32[32,64,256]{2,1,0:T(8,128)S(1)} %fusion.25, f32[32,64,256]{2,1,0:T(8,128)S(1)} %fusion.29, f32[32,64,256]{2,1,0:T(8,128)S(1)} %fusion.33, bf16[256,32,64]{0,2,1:T(8,128)(2,1)S(1)} %get-tuple-element.29, f32[256]{0:T(256)S(1)} %get-tuple-element.32, ...), kind=kOutput, calls=%fused_computation.5 | convolution fusion | flops 70385664 | bytes 11011072 | tf_op jit(solution)/shard_map/thb,hab->tha/dot_general | solution.py:26
  118.3 2.2 fusion.40
  120.4 2.3 copy.98
  122.7 2.3 copy.97
  125.0 40.8 %all-reduce = f32[2048]{0:T(1024)S(1)} all-reduce(f32[2048]{0:T(1024)S(1)} %reshape.137), channel_id=2, replica_groups=mesh['dp'=4,'ctx'=8] {'dp','ctx'}, use_global_device_ids=true, to_apply=%region_4.5.clone | all-reduce | flops 2048 | bytes 16384
  166.5 4.4 %fusion.41 = f32[32,256,64]{1,2,0:T(8,128)} fusion(bf16[256,32,64]{0,2,1:T(8,128)(2,1)S(1)} %bitcast.91, bf16[32,256,256]{2,1,0:T(8,128)(2,1)} %copy-done.3), kind=kOutput, calls=%fused_computation.71 | convolution fusion | flops 268435456 | bytes 7340032 | tf_op jit(solution)/shard_map/hts,tha->sha/dot_general | solution.py:26
  172.9 2.0 fusion.15
  175.0 3.5 %fusion.16 = f32[32,64,256]{2,1,0:T(8,128)} fusion(bf16[256,32,64]{0,2,1:T(8,128)(2,1)S(1)} %bitcast.72, f32[32,64,64]{2,1,0:T(8,128)} %collective-permute-done.9), kind=kOutput, calls=%fused_computation.46 | convolution fusion | flops 67633152 | bytes 3670016 | tf_op jit(solution)/shard_map/shb,hab->sha/dot_general | solution.py:26
  178.4 41.1 %collective-permute-done.7 = f32[32,64,64]{2,1,0:T(8,128)S(1)} collective-permute-done((f32[32,64,64]{2,1,0:T(8,128)S(1)}, f32[32,64,64]{2,1,0:T(8,128)S(1)}, u32[]{:S(2)}, u32[]{:S(2)}) %collective-permute-start.7) | collective-permute-done | bytes 524320 | tf_op jit(solution)/shard_map/ppermute | solution.py:22
  226.2 2.9 %add_convert_fusion = bf16[32,64,256]{2,1,0:T(8,128)(2,1)} fusion(f32[32,64,256]{2,1,0:T(8,128)S(1)} %copy-done.7, f32[32,64,256]{2,1,0:T(8,128)S(1)} %fusion.15, f32[32,64,256]{2,1,0:T(8,128)S(1)} %fusion.17, f32[32,64,256]{2,1,0:T(8,128)S(1)} %fusion.21, bf16[256,32,64]{0,2,1:T(8,128)(2,1)S(1)} %bitcast.83, f32[256]{0:T(256)S(1)} %get-tuple-element.31, ...), kind=kOutput, calls=%fused_computation.8 | convolution fusion | flops 70385664 | bytes 11011072 | tf_op jit(solution)/shard_map/sha,hab->shb/dot_general | solution.py:26
  229.1 2.4 %copy.100 = bf16[1,256,2048]{2,1,0:T(8,128)(2,1)} copy(bf16[1,256,2048]{1,2,0:T(8,128)(2,1)} %bitcast.97) | data formatting | bytes 2097152
  231.5 4.8 %fusion = bf16[256,32,64]{0,2,1:T(8,128)(2,1)} fusion(f32[32,256,64]{1,2,0:T(8,128)S(1)} %copy-done.8, f32[32,64,256]{2,1,0:T(8,128)} %fusion.16, f32[32,64,256]{2,1,0:T(8,128)} %fusion.19, f32[32,64,256]{2,1,0:T(8,128)} %fusion.22, bf16[256,32,64]{0,2,1:T(8,128)(2,1)S(1)} %bitcast.75, f32[256]{0:T(256)S(1)} %get-tuple-element.31, ...), kind=kOutput, calls=%fused_computation.3 | convolution fusion | flops 70385664 | bytes 11011072 | tf_op jit(solution)/shard_map/shb,hab->sha/dot_general | solution.py:26
  236.3 2.3 copy.99
  (85 shorter events, 41.8 us)
Async XLA Ops:
  2.8 1.9 copy-start.14
  2.8 6.9 %copy-start.16 = (s32[1,32]{1,0:T(1,128)S(1)}, s32[1,32]{1,0:T(1,128)}, u32[]{:S(2)}) copy-start(s32[1,32]{1,0:T(1,128)} %param.12) | copy-start | bytes 388
  4.2 10.3 %collective-permute-start = (f32[32,64,64]{2,1,0:T(8,128)}, f32[32,64,64]{2,1,0:T(8,128)}, u32[]{:S(2)}, u32[]{:S(2)}) collective-permute-start(f32[32,64,64]{2,1,0:T(8,128)} %fusion.37), channel_id=1, source_target_pairs={{0,1},{1,0},{2,3},{3,2},{4,5},{5,4},{6,7},{7,6},{8,9},{9,8},{10,11... | collective-permute-start | bytes 1572872 | tf_op jit(solution)/shard_map/ppermute | solution.py:22
  5.2 6.8 %collective-permute-start.8 = (f32[1]{0:T(128)}, f32[1]{0:T(128)}, u32[]{:S(2)}, u32[]{:S(2)}) collective-permute-start(f32[1]{0:T(128)} %get-tuple-element.34), channel_id=1, source_target_pairs={{0,1},{1,2},{2,3},{3,4},{4,5},{5,6},{6,7},{8,9},{9,10},{10,11},{11... | collective-permute-start | bytes 20 | tf_op jit(solution)/shard_map/ppermute | solution.py:12
  7.8 4.8 %collective-permute-start.3 = (f32[1]{0:T(128)}, f32[1]{0:T(128)}, u32[]{:S(2)}, u32[]{:S(2)}) collective-permute-start(f32[1]{0:T(128)} %get-tuple-element.35), channel_id=1, source_target_pairs={{1,0},{2,1},{3,2},{4,3},{5,4},{6,5},{7,6},{9,8},{10,9},{11,10},{12... | collective-permute-start | bytes 20 | tf_op jit(solution)/shard_map/ppermute | solution.py:12
  16.2 27.3 %collective-permute-start.1 = (f32[32,64,64]{2,1,0:T(8,128)S(1)}, f32[32,64,64]{2,1,0:T(8,128)S(1)}, u32[]{:S(2)}, u32[]{:S(2)}) collective-permute-start(f32[32,64,64]{2,1,0:T(8,128)S(1)} %add.109), channel_id=1, source_target_pairs={{0,2},{2,0},{1,3},{3,1},{4,6},{6,4},{5,7},{7,5},{8,10},{10,8},{9,1... | collective-permute-start | bytes 1572872 | tf_op jit(solution)/shard_map/ppermute | solution.py:22
  21.4 32.2 %collective-permute-start.4 = (f32[32,64,64]{2,1,0:T(8,128)}, f32[32,64,64]{2,1,0:T(8,128)}, u32[]{:S(2)}, u32[]{:S(2)}) collective-permute-start(f32[32,64,64]{2,1,0:T(8,128)} %fusion.6), channel_id=1, source_target_pairs={{1,0},{2,1},{3,2},{4,3},{5,4},{6,5},{7,6},{9,8},{10,9},{11,10},{12... | collective-permute-start | bytes 1572872 | tf_op jit(solution)/shard_map/ppermute | solution.py:12
  24.0 26.9 %copy-start.1 = (bf16[32,256,256]{2,1,0:T(8,128)(2,1)}, bf16[32,256,256]{2,1,0:T(8,128)(2,1)S(1)}, u32[]{:S(2)}) copy-start(bf16[32,256,256]{2,1,0:T(8,128)(2,1)S(1)} %select_convert_fusion.1) | copy-start | bytes 12582916
  45.6 48.4 %collective-permute-start.2 = (f32[32,64,64]{2,1,0:T(8,128)}, f32[32,64,64]{2,1,0:T(8,128)}, u32[]{:S(2)}, u32[]{:S(2)}) collective-permute-start(f32[32,64,64]{2,1,0:T(8,128)} %add.111), channel_id=1, source_target_pairs={{0,4},{4,0},{1,5},{5,1},{2,6},{6,2},{3,7},{7,3},{8,12},{12,8},{9,1... | collective-permute-start | bytes 1572872 | tf_op jit(solution)/shard_map/ppermute | solution.py:22
  50.9 2.6 %copy-start.15 = (f32[2048]{0:T(1024)S(1)}, f32[2048]{0:T(1024)}, u32[]{:S(2)}) copy-start(f32[2048]{0:T(1024)} %param.13) | copy-start | bytes 24580
  53.6 40.4 %copy-start.10 = (f32[32,64,64]{2,1,0:T(8,128)S(1)}, f32[32,64,64]{2,1,0:T(8,128)}, u32[]{:S(2)}) copy-start(f32[32,64,64]{2,1,0:T(8,128)} %copy-done.9) | copy-start | bytes 1572868
  97.6 2.4 copy-start
  103.4 13.6 %copy-start.4 = (f32[32,64,64]{2,1,0:T(8,128)}, f32[32,64,64]{2,1,0:T(8,128)S(1)}, u32[]{:S(2)}) copy-start(f32[32,64,64]{2,1,0:T(8,128)S(1)} %convolution_bitcast_fusion) | copy-start | bytes 1572868
  104.7 5.8 %copy-start.3 = (bf16[32,256,256]{2,1,0:T(8,128)(2,1)}, bf16[32,256,256]{2,1,0:T(8,128)(2,1)S(1)}, u32[]{:S(2)}) copy-start(bf16[32,256,256]{2,1,0:T(8,128)(2,1)S(1)} %select_convert_fusion) | copy-start | bytes 12582916
  105.6 11.4 %collective-permute-start.5 = (f32[32,64,64]{2,1,0:T(8,128)S(1)}, f32[32,64,64]{2,1,0:T(8,128)S(1)}, u32[]{:S(2)}, u32[]{:S(2)}) collective-permute-start(f32[32,64,64]{2,1,0:T(8,128)S(1)} %convolution_bitcast_fusion), channel_id=1, source_target_pairs={{0,1},{1,0},{2,3},{3,2},{4,5},{5,4},{6,7},{7,6},{8,9},{9,8},{10,11... | collective-permute-start | bytes 1572872 | tf_op jit(solution)/shard_map/ppermute | solution.py:22
  107.1 65.8 %collective-permute-start.9 = (f32[32,64,64]{2,1,0:T(8,128)}, f32[32,64,64]{2,1,0:T(8,128)}, u32[]{:S(2)}, u32[]{:S(2)}) collective-permute-start(f32[32,64,64]{2,1,0:T(8,128)} %fusion.4), channel_id=1, source_target_pairs={{0,1},{1,2},{2,3},{3,4},{4,5},{5,6},{6,7},{8,9},{9,10},{10,11},{11... | collective-permute-start | bytes 1572872 | tf_op jit(solution)/shard_map/ppermute | solution.py:12
  113.9 4.4 %copy-start.2 = (bf16[32,256,256]{2,1,0:T(8,128)(2,1)S(1)}, bf16[32,256,256]{2,1,0:T(8,128)(2,1)}, u32[]{:S(2)}) copy-start(bf16[32,256,256]{2,1,0:T(8,128)(2,1)} %copy-done.1) | copy-start | bytes 12582916
  117.0 3.4 %copy-start.11 = (f32[32,64,64]{2,1,0:T(8,128)}, f32[32,64,64]{2,1,0:T(8,128)S(1)}, u32[]{:S(2)}) copy-start(f32[32,64,64]{2,1,0:T(8,128)S(1)} %collective-permute-done.5) | copy-start | bytes 1572868
  118.3 52.6 %collective-permute-start.6 = (f32[32,64,64]{2,1,0:T(8,128)}, f32[32,64,64]{2,1,0:T(8,128)}, u32[]{:S(2)}, u32[]{:S(2)}) collective-permute-start(f32[32,64,64]{2,1,0:T(8,128)} %add.125), channel_id=1, source_target_pairs={{0,2},{2,0},{1,3},{3,1},{4,6},{6,4},{5,7},{7,5},{8,10},{10,8},{9,1... | collective-permute-start | bytes 1572872 | tf_op jit(solution)/shard_map/ppermute | solution.py:22
  172.5 47.0 %collective-permute-start.7 = (f32[32,64,64]{2,1,0:T(8,128)S(1)}, f32[32,64,64]{2,1,0:T(8,128)S(1)}, u32[]{:S(2)}, u32[]{:S(2)}) collective-permute-start(f32[32,64,64]{2,1,0:T(8,128)S(1)} %add.126), channel_id=1, source_target_pairs={{0,4},{4,0},{1,5},{5,1},{2,6},{6,2},{3,7},{7,3},{8,12},{12,8},{9,1... | collective-permute-start | bytes 1572872 | tf_op jit(solution)/shard_map/ppermute | solution.py:22
  175.0 44.6 %copy-start.5 = (f32[32,64,64]{2,1,0:T(8,128)S(1)}, f32[32,64,64]{2,1,0:T(8,128)}, u32[]{:S(2)}) copy-start(f32[32,64,64]{2,1,0:T(8,128)} %copy-done.4) | copy-start | bytes 1572868
  175.0 44.6 %copy-start.12 = (f32[32,64,64]{2,1,0:T(8,128)S(1)}, f32[32,64,64]{2,1,0:T(8,128)}, u32[]{:S(2)}) copy-start(f32[32,64,64]{2,1,0:T(8,128)} %copy-done.11) | copy-start | bytes 1572868
  224.2 2.1 copy-start.7
  229.1 2.4 %copy-start.8 = (f32[32,256,64]{1,2,0:T(8,128)S(1)}, f32[32,256,64]{1,2,0:T(8,128)}, u32[]{:S(2)}) copy-start(f32[32,256,64]{1,2,0:T(8,128)} %fusion.41) | copy-start | bytes 6291460
  (3 other events, 4.1 us)
where the time goes:
time: 239 us
  waiting for transfers between devices  99.4 us (42%)
  matrix products  47 us (20%)
  blocking collectives  40.8 us (17%)
  local copies, waits for them, and re-layouts  19.7 us (8%)
  starting transfers between devices  15.8 us (7%)
  other arithmetic  14.8 us (6%)
    ppermute x6, waiting for transfers between devices, from_partner(): return lax.ppermute(block, axis, route)  98.8 us
    dot_general x26, matrix products, plain(): return jnp.einsum(form, a, b, preferred_element_type=jnp.float32)  47 us
    unnamed x1, blocking collectives  40.8 us
    unnamed x42, local copies, waits for them, and re-layouts  15.8 us
    ppermute x4, starting transfers between devices, passed_along(): return lax.ppermute(block, axis, route)  8.46 us
    ppermute x6, starting transfers between devices, from_partner(): return lax.ppermute(block, axis, route)  7.33 us
  transfers between devices with their start and end apart: 10, of which 4 were waited for; matrix products, arithmetic and copies ran while one was open for 19% of the time, Pallas kernels for 0%

commit v1 on v0

v1 whole, which is shorter than its diff:
```python
import functools

import jax
import jax.numpy as jnp
from jax import lax
from jax.experimental import pallas as pl
from jax.experimental.pallas import tpu as pltpu
from jax.sharding import PartitionSpec as P

E = 64
PAIR = 2 * E
GROUPS = 2
EXTRA = 8
F32 = jnp.float32
BF16 = jnp.bfloat16


def dot(a, b, ca, cb):
    return lax.dot_general(a, b, (((ca,), (cb,)), ((), ())), preferred_element_type=F32)


def low_lanes(rows, cols):
    lane = lax.broadcasted_iota(jnp.int32, (rows, cols), 1)
    return lane % PAIR < E


def fold(product):
    return jnp.where(low_lanes(E, product.shape[1]), product[:E], product[E:])


def split(state):
    high = state.astype(BF16)
    return high, (state - high.astype(F32)).astype(BF16)


def spread(state):
    low = low_lanes(*state.shape)
    zero = jnp.zeros_like(state)
    return jnp.concatenate([jnp.where(low, state, zero), jnp.where(low, zero, state)], axis=0)


def heads_of(pair):
    low = low_lanes(*pair.shape)
    zero = jnp.zeros_like(pair)
    return jnp.where(low, pair, zero), jnp.where(low, zero, pair)


def twice(x):
    return jnp.concatenate([x, x], axis=1)


def pair_at(ref, p):
    return ref[:, p * PAIR:(p + 1) * PAIR]


def rows_of(value, p):
    return value[p * E:(p + 1) * E]


def state_pair(a, b, sel):
    return fold(dot(a, jnp.concatenate([b, b * sel], axis=1), 0, 0))


def put_states(step, states, marks, keep, send, part):
    for p, state in enumerate(states):
        part[0, p * E:(p + 1) * E] = state[:, PAIR:]
    part[0, len(states) * E:] = jnp.broadcast_to(marks, (EXTRA, PAIR))

    @pl.when(step == 0)
    def _():
        for p, state in enumerate(states):
            keep[p * E:(p + 1) * E] = state[:, :PAIR]

    @pl.when(step == 1)
    def _():
        for p, state in enumerate(states):
            send[p * E:(p + 1) * E] = state[:, :PAIR]


def states_kernel(core, k, v, segs, keep, send, part):
    first = (segs[...] == segs[0:1]).astype(BF16)
    count = k.shape[1] // PAIR
    states = [state_pair(pair_at(k, p), pair_at(v, p), first) for p in range(count)]
    put_states(pl.program_id(0), states, segs[0:1], keep, send, part)


def local_kernel(core, q, k, v, mask, attn, probs):
    m = mask[...]
    for p in range(q.shape[1] // PAIR):
        kp = pair_at(k, p)
        total = None
        for h, (qh, vh) in enumerate(zip(heads_of(pair_at(q, p)), heads_of(pair_at(v, p)))):
            prob = dot(qh, kp, 1, 1).astype(BF16) * m
            probs[2 * p + h] = prob
            term = dot(prob, vh, 1, 0)
            total = term if total is None else total + term
        attn[:, p * PAIR:(p + 1) * PAIR] = total


def head_mean(x):
    high, low = split(x)
    ones = spread(jnp.full((E, PAIR), 1.0 / E, BF16))
    return dot(jnp.concatenate([high, low], axis=1), jnp.concatenate([ones, ones], axis=0), 1, 0)


def side_by_side(state, part):
    sh, sl = split(state)
    ph, pll = split(part)
    left = jnp.concatenate([spread(sh), spread(sl)], axis=0)
    right = jnp.concatenate([spread(ph), spread(pll)], axis=0)
    return jnp.concatenate([left, right], axis=1)


def stacked(state, part):
    sh, sl = split(state)
    ph, pll = split(part)
    top = jnp.concatenate([spread(sh), spread(sl)], axis=1)
    bottom = jnp.concatenate([spread(ph), spread(pll)], axis=1)
    return jnp.concatenate([top, bottom], axis=0)


def norm_kernel(core, q, dy, local, gain, segs, imgs, pre_keep, pre_recv, nxt, *rest):
    out, dab, gsum, keep, send, part = rest[-6:]
    step = pl.program_id(0)
    count = q.shape[1] // PAIR
    prefix = jnp.where(step == 0, pre_keep[...], pre_recv[...])
    on_next = (imgs[...] == nxt[0, count * E:count * E + 1]).astype(F32)
    last = (imgs[...] == segs[segs.shape[0] - 1:]).astype(BF16)
    states = []
    for p in range(count):
        lanes = slice(p * PAIR, (p + 1) * PAIR)
        qp = q[:, lanes]
        far = dot(twice(qp), side_by_side(rows_of(prefix, p), nxt[0, p * E:(p + 1) * E]), 1, 0)
        attn = local[:, lanes] + far[:, :PAIR] + on_next * far[:, PAIR:]
        scale = lax.rsqrt(head_mean(attn * attn) + 1e-06)
        normed = attn * scale
        g = gain[:, lanes]
        out[:, lanes] = (normed * g).astype(BF16)
        dyp = dy[:, lanes].astype(F32)
        gsum[:, lanes] = jnp.sum(dyp * normed, axis=0, keepdims=True)
        ga = dyp * g
        da = (scale * (ga - normed * head_mean(ga * normed))).astype(BF16)
        dab[:, lanes] = da
        states.append(state_pair(qp, da, last))
    put_states(step, states, segs[segs.shape[0] - 1:], keep, send, part)


def inner_kernel(core, q, k, v, dab, probs, mask, imgs, pre_keep, pre_recv, nxt, *rest):
    gq, gk, gv = rest[-3:]
    step = pl.program_id(0)
    count = q.shape[1] // PAIR
    m = mask[...]
    prefix = jnp.where(step == 0, pre_keep[...], pre_recv[...])
    on_next = (imgs[...] == nxt[0, count * E:count * E + 1]).astype(F32)
    for p in range(count):
        lanes = slice(p * PAIR, (p + 1) * PAIR)
        da = dab[:, lanes]
        vp = v[:, lanes]
        far = dot(twice(da), stacked(rows_of(prefix, p), nxt[0, p * E:(p + 1) * E]), 1, 1)
        tq = far[:, :PAIR] + on_next * far[:, PAIR:]
        tk = tv = None
        das = heads_of(da)
        for h, (qh, kh, dh) in enumerate(zip(heads_of(q[:, lanes]), heads_of(k[:, lanes]), das)):
            dprob = dot(dh, vp, 1, 1).astype(BF16) * m
            tq = tq + dot(dprob, kh, 1, 0)
            a = dot(dprob, qh, 0, 0)
            b = dot(probs[2 * p + h], dh, 0, 0)
            tk = a if tk is None else tk + a
            tv = b if tv is None else tv + b
        gq[:, lanes] = tq.astype(BF16)
        gk[:, lanes] = tk
        gv[:, lanes] = tv


def outer_kernel(core, k, v, gk_in, gv_in, segs, suf_keep, suf_recv, prv, *rest):
    gk, gv = rest[-2:]
    step = pl.program_id(0)
    count = k.shape[1] // PAIR
    suffix = jnp.where(step == 0, suf_keep[...], suf_recv[...])
    on_prev = (segs[...] == prv[0, count * E:count * E + 1]).astype(F32)
    for p in range(count):
        lanes = slice(p * PAIR, (p + 1) * PAIR)
        s = rows_of(suffix, p)
        g = prv[0, p * E:(p + 1) * E]
        far = dot(twice(v[:, lanes]), stacked(s, g), 1, 1)
        gk[:, lanes] = (gk_in[:, lanes] + far[:, :PAIR] + on_prev * far[:, PAIR:]).astype(BF16)
        far = dot(twice(k[:, lanes]), side_by_side(s, g), 1, 0)
        gv[:, lanes] = (gv_in[:, lanes] + far[:, :PAIR] + on_prev * far[:, PAIR:]).astype(BF16)


def partner(x, axis, bit):
    route = [(i, i ^ (1 << bit)) for i in range(lax.axis_size(axis))]
    return lax.ppermute(x, axis, route)


def shifted(x, distance):
    count = lax.axis_size("ctx")
    return lax.ppermute(x, "ctx", [(i, i + distance) for i in range(count) if 0 <= i + distance < count])


def chips_before(own, towards):
    chips = lax.axis_size("ctx") // 2
    if chips > 8:
        total = shifted(own, 2 * towards)
        span = 1
        while span < chips:
            total = total + shifted(total, 2 * towards * span)
            span *= 2
        return total
    before = jnp.zeros_like(own)
    for hop in range(chips - 1):
        source = hop if towards == 1 else chips - 1 - hop
        route = [(2 * source + c, 2 * (source + towards) + c) for c in range(2)]
        before = before + lax.ppermute(own + before, "ctx", route)
    return before


def scan(keep, send, towards):
    core = lax.axis_index("ctx") & 1
    received = partner(send, "ctx", 0)
    before = chips_before(keep + received, towards)
    is_source = core == (0 if towards == 1 else 1)
    mine = jnp.where(is_source, before, before + received)
    theirs = partner(jnp.where(is_source, before + keep, before), "ctx", 0)
    return mine, theirs


def scatter_sum(x):
    devices = lax.axis_size("dp") * lax.axis_size("ctx")
    x = x.reshape(devices, -1)
    for axis in ("dp", "ctx"):
        for bit in reversed(range(lax.axis_size(axis).bit_length() - 1)):
            upper = lax.axis_index(axis) >> bit & 1 == 1
            half = x.shape[0] // 2
            low, high = x[:half], x[half:]
            x = jnp.where(upper, high, low) + partner(jnp.where(upper, low, high), axis, bit)
    return x.reshape(-1)


def on_device(queries, keys, values, out_grad, segment_ids, image_flags, gain):
    rows, width = queries.shape[1:]
    q, k, v, dy = (x[0] for x in (queries, keys, values, out_grad))
    seg = segment_ids[0]
    table = image_flags[0]
    gain_row = gain.reshape(1, width)
    core = (lax.axis_index("ctx") & 1).reshape(1).astype(jnp.int32)
    onehot = seg[:, None] == jnp.arange(table.shape[0], dtype=jnp.int32)[None, :]
    img = jnp.sum(jnp.where(onehot, table[None, :], 0), axis=1)
    imgseg = jnp.where(img == 1, seg, -1)
    pos = jnp.arange(rows)
    mask = (pos[:, None] >= pos[None, :]) | (imgseg[:, None] == seg[None, :])
    mask = mask.astype(BF16)
    segs = jnp.broadcast_to(seg.astype(F32)[:, None], (rows, PAIR))
    imgs = jnp.broadcast_to(imgseg.astype(F32)[:, None], (rows, PAIR))

    lanes = width // GROUPS // 2
    half_rows = lanes // PAIR * E
    heads = lanes // E

    def call(kernel, group, ins, outs, alias, flops):
        def wide(i, c):
            return (0, 2 * group + (i + c[0]) % 2)

        def own(i, c):
            return (0, (i + c[0]) % 2)

        def whole(i, c):
            return (0, 0)

        specs = {
            "wide": pl.BlockSpec((rows, lanes), wide),
            "block": pl.BlockSpec((rows, lanes), own),
            "row": pl.BlockSpec((1, lanes), wide),
            "rowblock": pl.BlockSpec((1, lanes), own),
            "half": pl.BlockSpec((half_rows, PAIR), whole),
            "part": pl.BlockSpec((1, half_rows + EXTRA, PAIR), lambda i, c: ((i + c[0]) % 2, 0, 0)),
            "segs": pl.BlockSpec((rows, PAIR), whole),
            "mask": pl.BlockSpec((rows, rows), whole),
            "probs": pl.BlockSpec((heads, rows, rows), lambda i, c: ((i + c[0]) % 2, 0, 0)),
            "any": pl.BlockSpec(memory_space=pl.ANY),
        }
        shapes = {
            "wide": (rows, width),
            "block": (rows, 2 * lanes),
            "rowblock": (1, 2 * lanes),
            "half": (half_rows, PAIR),
            "part": (2, half_rows + EXTRA, PAIR),
            "probs": (2 * heads, rows, rows),
        }
        operands = [x for _, x in ins]
        kinds = [kind for kind, _ in ins]
        aliases = {}
        for out_at, x in alias:
            if x is not None:
                aliases[1 + len(operands)] = out_at
                operands.append(x)
                kinds.append("any")
        out_shape = [jax.ShapeDtypeStruct(shapes[kind], dtype) for kind, dtype in outs]
        moved = sum(rows * 2 * lanes * 2 for kind in kinds if kind in ("wide", "block"))
        moved += sum(rows * 2 * lanes * 2 for kind, _ in outs if kind in ("wide", "block"))
        return pl.pallas_call(
            kernel,
            grid_spec=pltpu.PrefetchScalarGridSpec(
                num_scalar_prefetch=1,
                grid=(2,),
                in_specs=[specs[kind] for kind in kinds],
                out_specs=[specs[kind] for kind, _ in outs],
            ),
            out_shape=out_shape,
            input_output_aliases=aliases,
            compiler_params=pltpu.CompilerParams(vmem_limit_bytes=40 * 2**20),
            cost_estimate=pl.CostEstimate(flops=flops, bytes_accessed=moved, transcendentals=0),
        )(core, *operands)

    unit = 2 * rows * rows * PAIR * 2 * heads
    prefix, nexts = [], []
    for g in range(GROUPS):
        keep, send, n = call(
            states_kernel, g, [("wide", k), ("wide", v), ("segs", segs)],
            [("half", F32), ("half", F32), ("part", F32)], [], unit)
        prefix.append(scan(keep, send, 1))
        nexts.append(shifted(n, -1))
    local = [
        call(local_kernel, g, [("wide", q), ("wide", k), ("wide", v), ("mask", mask)],
             [("block", F32), ("probs", BF16)], [], 4 * unit)
        for g in range(GROUPS)
    ]
    output = grad_q = grad_k = grad_v = None
    suffix, prevs, inner, gsums = [], [], [], []
    for g in range(GROUPS):
        attn, probs = local[g]
        output, dab, gsum, keep, send, part = call(
            norm_kernel, g,
            [("wide", q), ("wide", dy), ("block", attn), ("row", gain_row), ("segs", segs), ("segs", imgs),
             ("half", prefix[g][0]), ("half", prefix[g][1]), ("part", nexts[g])],
            [("wide", BF16), ("block", BF16), ("rowblock", F32), ("half", F32), ("half", F32), ("part", F32)],
            [(0, output)], 2 * unit)
        gsums.append(gsum)
        suffix.append(scan(keep, send, -1))
        prevs.append(shifted(part, 1))
        grad_q, gk, gv = call(
            inner_kernel, g,
            [("wide", q), ("wide", k), ("wide", v), ("block", dab), ("probs", probs), ("mask", mask), ("segs", imgs),
             ("half", prefix[g][0]), ("half", prefix[g][1]), ("part", nexts[g])],
            [("wide", BF16), ("block", F32), ("block", F32)],
            [(0, grad_q)], 8 * unit)
        inner.append((gk, gv))
    grad_gain = scatter_sum(jnp.concatenate(gsums, axis=1))
    for g in range(GROUPS):
        gk, gv = inner[g]
        grad_k, grad_v = call(
            outer_kernel, g,
            [("wide", k), ("wide", v), ("block", gk), ("block", gv), ("segs", segs),
             ("half", suffix[g][0]), ("half", suffix[g][1]), ("part", prevs[g])],
            [("wide", BF16), ("wide", BF16)],
            [(0, grad_k), (1, grad_v)], 2 * unit)
    return output[None], grad_q[None], grad_k[None], grad_v[None], grad_gain


def solution(mesh):
    return jax.shard_map(
        on_device,
        mesh=mesh,
        in_specs=(
            P("dp", "ctx", None),
            P("dp", "ctx", None),
            P("dp", "ctx", None),
            P("dp", "ctx", None),
            P("dp", "ctx"),
            P("dp", None),
            P(),
        ),
        out_specs=(
            P("dp", "ctx", None),
            P("dp", "ctx", None),
            P("dp", "ctx", None),
            P("dp", "ctx", None),
            P(("dp", "ctx")),
        ),
        check_vma=False,
    )
```

time: 239 us -> 119 us (0.50)
  waiting for transfers between devices: 99.4 us -> 18.7 us
  matrix products: 47 us -> 0 us
  blocking collectives: 40.8 us -> 0 us
  Pallas kernels: 0 us -> 34.8 us
  starting transfers between devices: 15.8 us -> 40.7 us
  other arithmetic: 14.8 us -> 7.44 us
  local copies, waits for them, and re-layouts: 19.7 us -> 15.3 us
    ppermute x10 -> x29, waiting for transfers between devices: 99.4 us -> 18.7 us  [the longest x12 16.3 us: chips_before(): before = before + lax.ppermute(own + before, 'ctx', route)]
    dot_general x26 -> x0, matrix products: 47 us -> none  [plain(): return jnp.einsum(form, a, b, preferred_element_type=jnp.float32)]
    unnamed x1 -> x0, blocking collectives: 40.8 us -> none
    pallas_call x0 -> x10, Pallas kernels: none -> 34.8 us  [call(): pl.pallas_call(kernel, grid_spec=pltpu.PrefetchScalarGridSpec(num_scalar_...]
    ppermute x10 -> x29, starting transfers between devices: 15.8 us -> 40.7 us  [the longest x13 17.9 us: partner(): return lax.ppermute(x, axis, route)]
    convert_element_type x1 -> x0, local copies, waits for them, and re-layouts: 2.62 us -> none  [on_device(): dy = out_grad[0].reshape(rows, heads, E).astype(jnp.float32)]
    unnamed x42 -> x86, local copies, waits for them, and re-layouts: 15.8 us -> 14.4 us
    add x4 -> x16, other arithmetic: 5.7 us -> 5.2 us  [the longest x8 3.74 us: chips_before(): before = before + lax.ppermute(own + before, 'ctx', route)]
  transfers between devices with their start and end apart: 10 -> 29, of which waited for: 4 -> 4; matrix products, arithmetic and copies ran while one was open for 19% -> 5% of each run, Pallas kernels for 0% -> 21%
where the time goes in v1:
time: 119 us; the launch traced here: 118 us
  starting transfers between devices  40.7 us (34%)
  Pallas kernels  34.8 us (29%)
  waiting for transfers between devices  18.7 us (16%)
  local copies, waits for them, and re-layouts  15.3 us (13%)
  other arithmetic  7.44 us (6%)
  between operations  1.31 us (1%)
    pallas_call x10, Pallas kernels, call(): pl.pallas_call(kernel, grid_spec=pltpu.PrefetchScalarGridSpec(num_scalar_...  34.8 us
    ppermute x13, starting transfers between devices, partner(): return lax.ppermute(x, axis, route)  17.9 us
    ppermute x12, waiting for transfers between devices, chips_before(): before = before + lax.ppermute(own + before, 'ctx', route)  16.3 us
    ppermute x12, starting transfers between devices, chips_before(): before = before + lax.ppermute(own + before, 'ctx', route)  15.8 us
    unnamed x86, local copies, waits for them, and re-layouts  14.4 us
    ppermute x4, starting transfers between devices, shifted(): lax.ppermute(x, 'ctx', [(i, i + distance) for i in range(count) if 0 <= i...  7.04 us
    add x8, other arithmetic, chips_before(): before = before + lax.ppermute(own + before, 'ctx', route)  3.74 us
  transfers between devices with their start and end apart: 29, of which 4 were waited for; matrix products, arithmetic and copies ran while one was open for 5% of the time, Pallas kernels for 21%

profile of v1, /device:TPU:0, one launch (start us, length us, event | category | flops | bytes accessed | tf_op | source)
XLA Modules:
  0.0 118.2 jit_solution(17379816702114053926)
XLA Ops:
  3.9 1.4 %shard_map.113 = (f32[256,128]{1,0:T(8,128)S(1)}, f32[256,128]{1,0:T(8,128)S(1)}, f32[2,264,128]{2,1,0:T(8,128)}) custom-call(s32[1]{0:T(128)} %bitcast.core, bf16[256,2048]{1,0:T(8,128)(2,1)S(1)} %bitcast.14, bf16[256,2048]{1,0:T(8,128)(2,1)S(1)} %bitcast.22, f32[256,128]{1,0:T(8,128)S(1)} %broadcast_in_dim.50.segs), custom_call_target="tpu_custom_call" | custom-call | flops 268435456 | bytes 1048576 | tf_op jit(solution)/shard_map/pallas_call | solution.py:301
  5.7 1.4 %collective-permute-start.11 = (f32[2,264,128]{2,1,0:T(8,128)}, f32[2,264,128]{2,1,0:T(8,128)}, u32[]{:S(2)}, u32[]{:S(2)}) collective-permute-start(f32[2,264,128]{2,1,0:T(8,128)} %get-tuple-element.44), channel_id=1, source_target_pairs={{1,0},{2,1},{3,2},{4,3},{5,4},{6,5},{7,6},{9,8},{10,9},{11,10},{12... | collective-permute-start | bytes 811016 | tf_op jit(solution)/shard_map/ppermute | solution.py:198
  7.1 1.4 %shard_map.111 = (f32[256,128]{1,0:T(8,128)S(1)}, f32[256,128]{1,0:T(8,128)S(1)}, f32[2,264,128]{2,1,0:T(8,128)}) custom-call(s32[1]{0:T(128)} %bitcast.core, bf16[256,2048]{1,0:T(8,128)(2,1)S(1)} %bitcast.15, bf16[256,2048]{1,0:T(8,128)(2,1)S(1)} %bitcast.23, f32[256,128]{1,0:T(8,128)S(1)} %broadcast_in_dim.50.segs), custom_call_target="tpu_custom_call" | custom-call | flops 268435456 | bytes 1048576 | tf_op jit(solution)/shard_map/pallas_call | solution.py:301
  11.1 5.3 %collective-permute-start.7 = (f32[256,128]{1,0:T(8,128)S(1)}, f32[256,128]{1,0:T(8,128)S(1)}, u32[]{:S(2)}, u32[]{:S(2)}) collective-permute-start(f32[256,128]{1,0:T(8,128)S(1)} %add.106), channel_id=1, source_target_pairs={{0,2},{1,3},{8,10},{9,11},{16,18},{17,19},{24,26},{25,27}} | collective-permute-start | bytes 393224 | tf_op jit(solution)/shard_map/ppermute | solution.py:214
  17.1 1.9 %collective-permute-start.1 = (f32[256,128]{1,0:T(8,128)}, f32[256,128]{1,0:T(8,128)}, u32[]{:S(2)}, u32[]{:S(2)}) collective-permute-start(f32[256,128]{1,0:T(8,128)} %add.99), channel_id=1, source_target_pairs={{0,2},{1,3},{8,10},{9,11},{16,18},{17,19},{24,26},{25,27}} | collective-permute-start | bytes 393224 | tf_op jit(solution)/shard_map/ppermute | solution.py:214
  23.9 2.3 %shard_map.112 = (f32[256,1024]{1,0:T(8,128)S(1)}, bf16[16,256,256]{2,1,0:T(8,128)(2,1)S(1)}) custom-call(s32[1]{0:T(128)} %bitcast.core, bf16[256,2048]{1,0:T(8,128)(2,1)S(1)} %bitcast.32, bf16[256,2048]{1,0:T(8,128)(2,1)S(1)} %bitcast.16, bf16[256,2048]{1,0:T(8,128)(2,1)S(1)} %bitcast.24, bf16[256,256]{1,0:T(8,128)(2,1)S(1)} %copy-done.16), custom_call_target="tpu_custom_call" | custom-call | flops 1073741824 | bytes 2097152 | tf_op jit(solution)/shard_map/pallas_call | solution.py:301
  33.4 2.3 %shard_map.110 = (f32[256,1024]{1,0:T(8,128)S(1)}, bf16[16,256,256]{2,1,0:T(8,128)(2,1)S(1)}) custom-call(s32[1]{0:T(128)} %bitcast.core, bf16[256,2048]{1,0:T(8,128)(2,1)S(1)} %bitcast.33, bf16[256,2048]{1,0:T(8,128)(2,1)S(1)} %bitcast.17, bf16[256,2048]{1,0:T(8,128)(2,1)S(1)} %bitcast.25, bf16[256,256]{1,0:T(8,128)(2,1)S(1)} %copy-done.17), custom_call_target="tpu_custom_call" | custom-call | flops 1073741824 | bytes 2097152 | tf_op jit(solution)/shard_map/pallas_call | solution.py:301
  35.7 1.3 %copy-done.29 = bf16[16,256,256]{2,1,0:T(8,128)(2,1)} copy-done((bf16[16,256,256]{2,1,0:T(8,128)(2,1)}, bf16[16,256,256]{2,1,0:T(8,128)(2,1)S(1)}, u32[]{:S(2)}) %copy-start.29) | copy-done | bytes 2097176
  37.2 6.0 %shard_map.114 = (bf16[256,2048]{1,0:T(8,128)(2,1)}, bf16[256,1024]{1,0:T(8,128)(2,1)S(1)}, f32[1,1024]{1,0:T(1,128)S(1)}, f32[256,128]{1,0:T(8,128)S(1)}, f32[2...) custom-call(s32[1]{0:T(128)} %bitcast.core, bf16[256,2048]{1,0:T(8,128)(2,1)S(1)} %bitcast.34, ...), custom_call_target="tpu_custom_call" | custom-call | flops 536870912 | bytes 2621440 | tf_op jit(solution)/shard_map/pallas_call | solution.py:301
  44.1 6.1 %shard_map.115 = (bf16[256,2048]{1,0:T(8,128)(2,1)}, bf16[256,1024]{1,0:T(8,128)(2,1)S(1)}, f32[1,1024]{1,0:T(1,128)S(1)}, f32[256,128]{1,0:T(8,128)S(1)}, f32[2...) custom-call(s32[1]{0:T(128)} %bitcast.core, bf16[256,2048]{1,0:T(8,128)(2,1)S(1)} %bitcast.35, ...), custom_call_target="tpu_custom_call", output_to_operand_aliasing={{0}: (10, {})} | custom-call | flops 536870912 | bytes 2621440 | tf_op jit(solution)/shard_map/pallas_call | solution.py:301
  53.0 1.6 %collective-permute-start.24 = (f32[16,64]{1,0:T(8,128)}, f32[16,64]{1,0:T(8,128)}, u32[]{:S(2)}, u32[]{:S(2)}) collective-permute-start(f32[16,64]{1,0:T(8,128)} %select_n.139), channel_id=1, source_target_pairs={{0,16},{8,24},{16,0},{24,8},{1,17},{9,25},{17,1},{25,9},{2,18},{10... | collective-permute-start | bytes 12296 | tf_op jit(solution)/shard_map/ppermute | solution.py:193
  54.6 2.3 %collective-permute-done.24 = f32[16,64]{1,0:T(8,128)} collective-permute-done((f32[16,64]{1,0:T(8,128)}, f32[16,64]{1,0:T(8,128)}, u32[]{:S(2)}, u32[]{:S(2)}) %collective-permute-start.24) | collective-permute-done | bytes 4128 | tf_op jit(solution)/shard_map/ppermute | solution.py:193
  57.7 1.5 %collective-permute-start.25 = (f32[8,64]{1,0:T(8,128)S(1)}, f32[8,64]{1,0:T(8,128)S(1)}, u32[]{:S(2)}, u32[]{:S(2)}) collective-permute-start(f32[8,64]{1,0:T(8,128)S(1)} %slice_select_fusion), channel_id=1, source_target_pairs={{0,8},{8,0},{16,24},{24,16},{1,9},{9,1},{17,25},{25,17},{2,10},{10... | collective-permute-start | bytes 6152 | tf_op jit(solution)/shard_map/ppermute | solution.py:193
  59.2 2.4 %collective-permute-start.23 = (f32[2,264,128]{2,1,0:T(8,128)}, f32[2,264,128]{2,1,0:T(8,128)S(1)}, u32[]{:S(2)}, u32[]{:S(2)}) collective-permute-start(f32[2,264,128]{2,1,0:T(8,128)} %copy-done.26), channel_id=1, source_target_pairs={{0,1},{1,2},{2,3},{3,4},{4,5},{5,6},{6,7},{8,9},{9,10},{10,11},{11... | collective-permute-start | bytes 811016 | tf_op jit(solution)/shard_map/ppermute | solution.py:198
  61.6 4.2 %collective-permute-start.12 = (f32[256,128]{1,0:T(8,128)}, f32[256,128]{1,0:T(8,128)S(1)}, u32[]{:S(2)}, u32[]{:S(2)}) collective-permute-start(f32[256,128]{1,0:T(8,128)} %copy-done.27), channel_id=1, source_target_pairs={{0,1},{1,0},{2,3},{3,2},{4,5},{5,4},{6,7},{7,6},{8,9},{9,8},{10,11... | collective-permute-start | bytes 393224 | tf_op jit(solution)/shard_map/ppermute | solution.py:193
  65.9 1.9 %collective-permute-start.17 = (f32[2,264,128]{2,1,0:T(8,128)}, f32[2,264,128]{2,1,0:T(8,128)S(1)}, u32[]{:S(2)}, u32[]{:S(2)}) collective-permute-start(f32[2,264,128]{2,1,0:T(8,128)} %copy-done.25), channel_id=1, source_target_pairs={{0,1},{1,2},{2,3},{3,4},{4,5},{5,6},{6,7},{8,9},{9,10},{10,11},{11... | collective-permute-start | bytes 811016 | tf_op jit(solution)/shard_map/ppermute | solution.py:198
  67.9 6.9 %collective-permute-start.26 = (f32[4,64]{1,0:T(4,128)S(1)}, f32[4,64]{1,0:T(4,128)S(1)}, u32[]{:S(2)}, u32[]{:S(2)}) collective-permute-start(f32[4,64]{1,0:T(4,128)S(1)} %slice_select_fusion.1), channel_id=1, source_target_pairs={{0,4},{1,5},{2,6},{3,7},{4,0},{5,1},{6,2},{7,3},{8,12},{9,13},{10,... | collective-permute-start | bytes 3080 | tf_op jit(solution)/shard_map/ppermute | solution.py:193
  78.5 1.6 %copy-done.32 = bf16[16,256,256]{2,1,0:T(8,128)(2,1)S(1)} copy-done((bf16[16,256,256]{2,1,0:T(8,128)(2,1)S(1)}, bf16[16,256,256]{2,1,0:T(8,128)(2,1)}, u32[]{:S(2)}) %copy-start.32) | copy-done | bytes 2097176
  80.1 5.6 %shard_map.116 = (bf16[256,2048]{1,0:T(8,128)(2,1)}, f32[256,1024]{1,0:T(8,128)S(1)}, f32[256,1024]{1,0:T(8,128)S(1)}) custom-call(s32[1]{0:T(128)} %bitcast.core, bf16[256,2048]{1,0:T(8,128)(2,1)S(1)} %bitcast.36, bf16[256,2048]{1,0:T(8,128)(2,1)S(1)} %bitcast.18, bf16[256,2048]{1,0:T(8,128)(2,1)S(1)} %bitcast.26, bf16[256,1024]{1,0:T(8,128)(2,1)S(1)} %copy-done.24, ...), custom_call_target="tpu_custom_call" | custom-call | flops 2147483648 | bytes 3670016 | tf_op jit(solution)/shard_map/pallas_call | solution.py:301
  86.7 5.5 %shard_map.117 = (bf16[256,2048]{1,0:T(8,128)(2,1)}, f32[256,1024]{1,0:T(8,128)S(1)}, f32[256,1024]{1,0:T(8,128)S(1)}) custom-call(s32[1]{0:T(128)} %bitcast.core, bf16[256,2048]{1,0:T(8,128)(2,1)S(1)} %bitcast.37, bf16[256,2048]{1,0:T(8,128)(2,1)S(1)} %bitcast.19, bf16[256,2048]{1,0:T(8,128)(2,1)S(1)} %bitcast.27, ...), custom_call_target="tpu_custom_call", output_to_operand_aliasing={{0}: (11, {})} | custom-call | flops 2147483648 | bytes 3670016 | tf_op jit(solution)/shard_map/pallas_call | solution.py:301
  97.8 11.8 %collective-permute-done.21 = f32[256,128]{1,0:T(8,128)S(1)} collective-permute-done((f32[256,128]{1,0:T(8,128)S(1)}, f32[256,128]{1,0:T(8,128)S(1)}, u32[]{:S(2)}, u32[]{:S(2)}) %collective-permute-start.21) | collective-permute-done | bytes 131104 | tf_op jit(solution)/shard_map/ppermute | solution.py:214
  110.0 3.3 %collective-permute-done.15 = f32[256,128]{1,0:T(8,128)S(1)} collective-permute-done((f32[256,128]{1,0:T(8,128)S(1)}, f32[256,128]{1,0:T(8,128)S(1)}, u32[]{:S(2)}, u32[]{:S(2)}) %collective-permute-start.15) | collective-permute-done | bytes 131104 | tf_op jit(solution)/shard_map/ppermute | solution.py:214
  114.0 2.1 %shard_map.118 = (bf16[256,2048]{1,0:T(8,128)(2,1)}, bf16[256,2048]{1,0:T(8,128)(2,1)}) custom-call(s32[1]{0:T(128)} %bitcast.core, bf16[256,2048]{1,0:T(8,128)(2,1)S(1)} %bitcast.20, bf16[256,2048]{1,0:T(8,128)(2,1)S(1)} %bitcast.28, f32[256,1024]{1,0:T(8,128)S(1)} %get-tuple-element.58.gk_in, f32[256,1024]{1,0:T(8,128)S(1)} %get-tuple-element.59.gv_in, ...), custom_call_target="tpu_custom_call" | custom-call | flops 536870912 | bytes 3145728 | tf_op jit(solution)/shard_map/pallas_call | solution.py:301
  116.1 2.1 %shard_map.119 = (bf16[256,2048]{1,0:T(8,128)(2,1)}, bf16[256,2048]{1,0:T(8,128)(2,1)}) custom-call(s32[1]{0:T(128)} %bitcast.core, bf16[256,2048]{1,0:T(8,128)(2,1)S(1)} %bitcast.21, bf16[256,2048]{1,0:T(8,128)(2,1)S(1)} %bitcast.29, f32[256,1024]{1,0:T(8,128)S(1)} %get-tuple-element.53.gk_in, ...), custom_call_target="tpu_custom_call", output_to_operand_aliasing={{0}: (9, {}), {1}: (10, {})} | custom-call | flops 536870912 | bytes 3145728 | tf_op jit(solution)/shard_map/pallas_call | solution.py:301
  (164 shorter events, 34.5 us)
Async XLA Ops:
  5.3 5.8 %collective-permute-start.6 = (f32[256,128]{1,0:T(8,128)S(1)}, f32[256,128]{1,0:T(8,128)S(1)}, u32[]{:S(2)}, u32[]{:S(2)}) collective-permute-start(f32[256,128]{1,0:T(8,128)S(1)} %get-tuple-element.43), channel_id=1, source_target_pairs={{0,1},{1,0},{2,3},{3,2},{4,5},{5,4},{6,7},{7,6},{8,9},{9,8},{10,11... | collective-permute-start | bytes 393224 | tf_op jit(solution)/shard_map/ppermute | solution.py:193
  5.7 31.3 %collective-permute-start.11 = (f32[2,264,128]{2,1,0:T(8,128)}, f32[2,264,128]{2,1,0:T(8,128)}, u32[]{:S(2)}, u32[]{:S(2)}) collective-permute-start(f32[2,264,128]{2,1,0:T(8,128)} %get-tuple-element.44), channel_id=1, source_target_pairs={{1,0},{2,1},{3,2},{4,3},{5,4},{6,5},{7,6},{9,8},{10,9},{11,10},{12... | collective-permute-start | bytes 811016 | tf_op jit(solution)/shard_map/ppermute | solution.py:198
  8.6 7.9 %collective-permute-start = (f32[256,128]{1,0:T(8,128)S(1)}, f32[256,128]{1,0:T(8,128)S(1)}, u32[]{:S(2)}, u32[]{:S(2)}) collective-permute-start(f32[256,128]{1,0:T(8,128)S(1)} %get-tuple-element.39), channel_id=1, source_target_pairs={{0,1},{1,0},{2,3},{3,2},{4,5},{5,4},{6,7},{7,6},{8,9},{9,8},{10,11... | collective-permute-start | bytes 393224 | tf_op jit(solution)/shard_map/ppermute | solution.py:193
  9.7 34.3 %collective-permute-start.5 = (f32[2,264,128]{2,1,0:T(8,128)}, f32[2,264,128]{2,1,0:T(8,128)}, u32[]{:S(2)}, u32[]{:S(2)}) collective-permute-start(f32[2,264,128]{2,1,0:T(8,128)} %get-tuple-element.40), channel_id=1, source_target_pairs={{1,0},{2,1},{3,2},{4,3},{5,4},{6,5},{7,6},{9,8},{10,9},{11,10},{12... | collective-permute-start | bytes 811016 | tf_op jit(solution)/shard_map/ppermute | solution.py:198
  11.1 9.1 %collective-permute-start.7 = (f32[256,128]{1,0:T(8,128)S(1)}, f32[256,128]{1,0:T(8,128)S(1)}, u32[]{:S(2)}, u32[]{:S(2)}) collective-permute-start(f32[256,128]{1,0:T(8,128)S(1)} %add.106), channel_id=1, source_target_pairs={{0,2},{1,3},{8,10},{9,11},{16,18},{17,19},{24,26},{25,27}} | collective-permute-start | bytes 393224 | tf_op jit(solution)/shard_map/ppermute | solution.py:214
  17.1 10.4 %collective-permute-start.1 = (f32[256,128]{1,0:T(8,128)}, f32[256,128]{1,0:T(8,128)}, u32[]{:S(2)}, u32[]{:S(2)}) collective-permute-start(f32[256,128]{1,0:T(8,128)} %add.99), channel_id=1, source_target_pairs={{0,2},{1,3},{8,10},{9,11},{16,18},{17,19},{24,26},{25,27}} | collective-permute-start | bytes 393224 | tf_op jit(solution)/shard_map/ppermute | solution.py:214
  20.9 8.3 %collective-permute-start.8 = (f32[256,128]{1,0:T(8,128)}, f32[256,128]{1,0:T(8,128)}, u32[]{:S(2)}, u32[]{:S(2)}) collective-permute-start(f32[256,128]{1,0:T(8,128)} %add.107), channel_id=1, source_target_pairs={{2,4},{3,5},{10,12},{11,13},{18,20},{19,21},{26,28},{27,29}} | collective-permute-start | bytes 393224 | tf_op jit(solution)/shard_map/ppermute | solution.py:214
  28.6 2.3 %collective-permute-start.2 = (f32[256,128]{1,0:T(8,128)S(1)}, f32[256,128]{1,0:T(8,128)S(1)}, u32[]{:S(2)}, u32[]{:S(2)}) collective-permute-start(f32[256,128]{1,0:T(8,128)S(1)} %add.100), channel_id=1, source_target_pairs={{2,4},{3,5},{10,12},{11,13},{18,20},{19,21},{26,28},{27,29}} | collective-permute-start | bytes 393224 | tf_op jit(solution)/shard_map/ppermute | solution.py:214
  30.2 2.4 %collective-permute-start.9 = (f32[256,128]{1,0:T(8,128)S(1)}, f32[256,128]{1,0:T(8,128)S(1)}, u32[]{:S(2)}, u32[]{:S(2)}) collective-permute-start(f32[256,128]{1,0:T(8,128)S(1)} %get-tuple-element.75), channel_id=1, source_target_pairs={{4,6},{5,7},{12,14},{13,15},{20,22},{21,23},{28,30},{29,31}} | collective-permute-start | bytes 393224 | tf_op jit(solution)/shard_map/ppermute | solution.py:214
  32.7 4.4 %collective-permute-start.10 = (f32[256,128]{1,0:T(8,128)S(1)}, f32[256,128]{1,0:T(8,128)S(1)}, u32[]{:S(2)}, u32[]{:S(2)}) collective-permute-start(f32[256,128]{1,0:T(8,128)S(1)} %get-tuple-element.85), channel_id=1, source_target_pairs={{0,1},{1,0},{2,3},{3,2},{4,5},{5,4},{6,7},{7,6},{8,9},{9,8},{10,11... | collective-permute-start | bytes 393224 | tf_op jit(solution)/shard_map/ppermute | solution.py:193
  32.8 11.2 %collective-permute-start.4 = (f32[256,128]{1,0:T(8,128)S(1)}, f32[256,128]{1,0:T(8,128)S(1)}, u32[]{:S(2)}, u32[]{:S(2)}) collective-permute-start(f32[256,128]{1,0:T(8,128)S(1)} %get-tuple-element.87), channel_id=1, source_target_pairs={{0,1},{1,0},{2,3},{3,2},{4,5},{5,4},{6,7},{7,6},{8,9},{9,8},{10,11... | collective-permute-start | bytes 393224 | tf_op jit(solution)/shard_map/ppermute | solution.py:193
  53.0 4.0 %collective-permute-start.24 = (f32[16,64]{1,0:T(8,128)}, f32[16,64]{1,0:T(8,128)}, u32[]{:S(2)}, u32[]{:S(2)}) collective-permute-start(f32[16,64]{1,0:T(8,128)} %select_n.139), channel_id=1, source_target_pairs={{0,16},{8,24},{16,0},{24,8},{1,17},{9,25},{17,1},{25,9},{2,18},{10... | collective-permute-start | bytes 12296 | tf_op jit(solution)/shard_map/ppermute | solution.py:193
  57.7 10.2 %collective-permute-start.25 = (f32[8,64]{1,0:T(8,128)S(1)}, f32[8,64]{1,0:T(8,128)S(1)}, u32[]{:S(2)}, u32[]{:S(2)}) collective-permute-start(f32[8,64]{1,0:T(8,128)S(1)} %slice_select_fusion), channel_id=1, source_target_pairs={{0,8},{8,0},{16,24},{24,16},{1,9},{9,1},{17,25},{25,17},{2,10},{10... | collective-permute-start | bytes 6152 | tf_op jit(solution)/shard_map/ppermute | solution.py:193
  59.2 33.0 %collective-permute-start.18 = (f32[256,128]{1,0:T(8,128)}, f32[256,128]{1,0:T(8,128)S(1)}, u32[]{:S(2)}, u32[]{:S(2)}) collective-permute-start(f32[256,128]{1,0:T(8,128)} %copy-done.28), channel_id=1, source_target_pairs={{0,1},{1,0},{2,3},{3,2},{4,5},{5,4},{6,7},{7,6},{8,9},{9,8},{10,11... | collective-permute-start | bytes 393224 | tf_op jit(solution)/shard_map/ppermute | solution.py:193
  59.2 54.8 %collective-permute-start.23 = (f32[2,264,128]{2,1,0:T(8,128)}, f32[2,264,128]{2,1,0:T(8,128)S(1)}, u32[]{:S(2)}, u32[]{:S(2)}) collective-permute-start(f32[2,264,128]{2,1,0:T(8,128)} %copy-done.26), channel_id=1, source_target_pairs={{0,1},{1,2},{2,3},{3,4},{4,5},{5,6},{6,7},{8,9},{9,10},{10,11},{11... | collective-permute-start | bytes 811016 | tf_op jit(solution)/shard_map/ppermute | solution.py:198
  61.6 31.3 %collective-permute-start.12 = (f32[256,128]{1,0:T(8,128)}, f32[256,128]{1,0:T(8,128)S(1)}, u32[]{:S(2)}, u32[]{:S(2)}) collective-permute-start(f32[256,128]{1,0:T(8,128)} %copy-done.27), channel_id=1, source_target_pairs={{0,1},{1,0},{2,3},{3,2},{4,5},{5,4},{6,7},{7,6},{8,9},{9,8},{10,11... | collective-permute-start | bytes 393224 | tf_op jit(solution)/shard_map/ppermute | solution.py:193
  65.9 50.2 %collective-permute-start.17 = (f32[2,264,128]{2,1,0:T(8,128)}, f32[2,264,128]{2,1,0:T(8,128)S(1)}, u32[]{:S(2)}, u32[]{:S(2)}) collective-permute-start(f32[2,264,128]{2,1,0:T(8,128)} %copy-done.25), channel_id=1, source_target_pairs={{0,1},{1,2},{2,3},{3,4},{4,5},{5,6},{6,7},{8,9},{9,10},{10,11},{11... | collective-permute-start | bytes 811016 | tf_op jit(solution)/shard_map/ppermute | solution.py:198
  67.9 17.9 %collective-permute-start.26 = (f32[4,64]{1,0:T(4,128)S(1)}, f32[4,64]{1,0:T(4,128)S(1)}, u32[]{:S(2)}, u32[]{:S(2)}) collective-permute-start(f32[4,64]{1,0:T(4,128)S(1)} %slice_select_fusion.1), channel_id=1, source_target_pairs={{0,4},{1,5},{2,6},{3,7},{4,0},{5,1},{6,2},{7,3},{8,12},{9,13},{10,... | collective-permute-start | bytes 3080 | tf_op jit(solution)/shard_map/ppermute | solution.py:193
  85.8 7.1 %collective-permute-start.27 = (f32[2,64]{1,0:T(2,128)S(1)}, f32[2,64]{1,0:T(2,128)S(1)}, u32[]{:S(2)}, u32[]{:S(2)}) collective-permute-start(f32[2,64]{1,0:T(2,128)S(1)} %broadcast_select_fusion.2), channel_id=1, source_target_pairs={{0,2},{1,3},{2,0},{3,1},{4,6},{5,7},{6,4},{7,5},{8,10},{9,11},{10,... | collective-permute-start | bytes 1544 | tf_op jit(solution)/shard_map/ppermute | solution.py:193
  94.4 19.1 %collective-permute-start.28 = (f32[1,64]{1,0:T(1,128)S(1)}, f32[1,64]{1,0:T(1,128)S(1)}, u32[]{:S(2)}, u32[]{:S(2)}) collective-permute-start(f32[1,64]{1,0:T(1,128)S(1)} %broadcast_select_fusion.3), channel_id=1, source_target_pairs={{0,1},{1,0},{2,3},{3,2},{4,5},{5,4},{6,7},{7,6},{8,9},{9,8},{10,11... | collective-permute-start | bytes 776 | tf_op jit(solution)/shard_map/ppermute | solution.py:193
  95.2 14.4 %collective-permute-start.21 = (f32[256,128]{1,0:T(8,128)S(1)}, f32[256,128]{1,0:T(8,128)S(1)}, u32[]{:S(2)}, u32[]{:S(2)}) collective-permute-start(f32[256,128]{1,0:T(8,128)S(1)} %get-tuple-element.71), channel_id=1, source_target_pairs={{2,0},{3,1},{10,8},{11,9},{18,16},{19,17},{26,24},{27,25}} | collective-permute-start | bytes 393224 | tf_op jit(solution)/shard_map/ppermute | solution.py:214
  96.5 16.8 %collective-permute-start.15 = (f32[256,128]{1,0:T(8,128)S(1)}, f32[256,128]{1,0:T(8,128)S(1)}, u32[]{:S(2)}, u32[]{:S(2)}) collective-permute-start(f32[256,128]{1,0:T(8,128)S(1)} %get-tuple-element.73), channel_id=1, source_target_pairs={{2,0},{3,1},{10,8},{11,9},{18,16},{19,17},{26,24},{27,25}} | collective-permute-start | bytes 393224 | tf_op jit(solution)/shard_map/ppermute | solution.py:214
  109.7 4.3 %collective-permute-start.22 = (f32[256,128]{1,0:T(8,128)S(1)}, f32[256,128]{1,0:T(8,128)S(1)}, u32[]{:S(2)}, u32[]{:S(2)}) collective-permute-start(f32[256,128]{1,0:T(8,128)S(1)} %get-tuple-element.81), channel_id=1, source_target_pairs={{0,1},{1,0},{2,3},{3,2},{4,5},{5,4},{6,7},{7,6},{8,9},{9,8},{10,11... | collective-permute-start | bytes 393224 | tf_op jit(solution)/shard_map/ppermute | solution.py:193
  113.4 2.7 %collective-permute-start.16 = (f32[256,128]{1,0:T(8,128)S(1)}, f32[256,128]{1,0:T(8,128)S(1)}, u32[]{:S(2)}, u32[]{:S(2)}) collective-permute-start(f32[256,128]{1,0:T(8,128)S(1)} %get-tuple-element.83), channel_id=1, source_target_pairs={{0,1},{1,0},{2,3},{3,2},{4,5},{5,4},{6,7},{7,6},{8,9},{9,8},{10,11... | collective-permute-start | bytes 393224 | tf_op jit(solution)/shard_map/ppermute | solution.py:193
  (48 other events, 246.6 us)

commit v2 on v1

--- a/solution.py
+++ b/solution.py
@@ -126,22 +126,26 @@
     prefix = jnp.where(step == 0, pre_keep[...], pre_recv[...])
     on_next = (imgs[...] == nxt[0, count * E:count * E + 1]).astype(F32)
     last = (imgs[...] == segs[segs.shape[0] - 1:]).astype(BF16)
-    states = []
-    for p in range(count):
-        lanes = slice(p * PAIR, (p + 1) * PAIR)
-        qp = q[:, lanes]
-        far = dot(twice(qp), side_by_side(rows_of(prefix, p), nxt[0, p * E:(p + 1) * E]), 1, 0)
-        attn = local[:, lanes] + far[:, :PAIR] + on_next * far[:, PAIR:]
-        scale = lax.rsqrt(head_mean(attn * attn) + 1e-06)
-        normed = attn * scale
-        g = gain[:, lanes]
-        out[:, lanes] = (normed * g).astype(BF16)
-        dyp = dy[:, lanes].astype(F32)
-        gsum[:, lanes] = jnp.sum(dyp * normed, axis=0, keepdims=True)
-        ga = dyp * g
-        da = (scale * (ga - normed * head_mean(ga * normed))).astype(BF16)
-        dab[:, lanes] = da
-        states.append(state_pair(qp, da, last))
+    pairs = [slice(p * PAIR, (p + 1) * PAIR) for p in range(count)]
+    fars = [
+        dot(twice(q[:, at]), side_by_side(rows_of(prefix, p), nxt[0, p * E:(p + 1) * E]), 1, 0)
+        for p, at in enumerate(pairs)
+    ]
+    attns = [local[:, at] + far[:, :PAIR] + on_next * far[:, PAIR:] for at, far in zip(pairs, fars)]
+    squares = [head_mean(attn * attn) for attn in attns]
+    scales = [lax.rsqrt(square + 1e-06) for square in squares]
+    normeds = [attn * scale for attn, scale in zip(attns, scales)]
+    gas = [dy[:, at].astype(F32) * gain[:, at] for at in pairs]
+    means = [head_mean(ga * normed) for ga, normed in zip(gas, normeds)]
+    das = [
+        (scale * (ga - normed * mean)).astype(BF16)
+        for scale, ga, normed, mean in zip(scales, gas, normeds, means)
+    ]
+    states = [state_pair(q[:, at], da, last) for at, da in zip(pairs, das)]
+    for at, normed, da in zip(pairs, normeds, das):
+        dab[:, at] = da
+        out[:, at] = (normed * gain[:, at]).astype(BF16)
+        gsum[:, at] = jnp.sum(dy[:, at].astype(F32) * normed, axis=0, keepdims=True)
     put_states(step, states, segs[segs.shape[0] - 1:], keep, send, part)
 
 
@@ -226,15 +230,10 @@
 
 
 def scatter_sum(x):
+    axes = ("dp", "ctx")
     devices = lax.axis_size("dp") * lax.axis_size("ctx")
-    x = x.reshape(devices, -1)
-    for axis in ("dp", "ctx"):
-        for bit in reversed(range(lax.axis_size(axis).bit_length() - 1)):
-            upper = lax.axis_index(axis) >> bit & 1 == 1
-            half = x.shape[0] // 2
-            low, high = x[:half], x[half:]
-            x = jnp.where(upper, high, low) + partner(jnp.where(upper, low, high), axis, bit)
-    return x.reshape(-1)
+    terms = lax.all_to_all(x.reshape(devices, -1), axes, 0, 0, tiled=True)
+    return jnp.sum(terms, axis=0)
 
 
 def on_device(queries, keys, values, out_grad, segment_ids, image_flags, gain):
@@ -257,7 +256,7 @@
     half_rows = lanes // PAIR * E
     heads = lanes // E
 
-    def call(kernel, group, ins, outs, alias, flops):
+    def call(kernel, group, ins, outs, alias, micros):
         def wide(i, c):
             return (0, 2 * group + (i + c[0]) % 2)
 
@@ -308,21 +307,20 @@
             ),
             out_shape=out_shape,
             input_output_aliases=aliases,
-            compiler_params=pltpu.CompilerParams(vmem_limit_bytes=40 * 2**20),
-            cost_estimate=pl.CostEstimate(flops=flops, bytes_accessed=moved, transcendentals=0),
+            compiler_params=pltpu.CompilerParams(vmem_limit_bytes=16 * 2**20),
+            cost_estimate=pl.CostEstimate(flops=int(micros * 1.15e9), bytes_accessed=moved, transcendentals=0),
         )(core, *operands)
 
-    unit = 2 * rows * rows * PAIR * 2 * heads
     prefix, nexts = [], []
     for g in range(GROUPS):
         keep, send, n = call(
             states_kernel, g, [("wide", k), ("wide", v), ("segs", segs)],
-            [("half", F32), ("half", F32), ("part", F32)], [], unit)
+            [("half", F32), ("half", F32), ("part", F32)], [], 1.4)
         prefix.append(scan(keep, send, 1))
         nexts.append(shifted(n, -1))
     local = [
         call(local_kernel, g, [("wide", q), ("wide", k), ("wide", v), ("mask", mask)],
-             [("block", F32), ("probs", BF16)], [], 4 * unit)
+             [("block", F32), ("probs", BF16)], [], 2.3)
         for g in range(GROUPS)
     ]
     output = grad_q = grad_k = grad_v = None
@@ -334,7 +332,7 @@
             [("wide", q), ("wide", dy), ("block", attn), ("row", gain_row), ("segs", segs), ("segs", imgs),
              ("half", prefix[g][0]), ("half", prefix[g][1]), ("part", nexts[g])],
             [("wide", BF16), ("block", BF16), ("rowblock", F32), ("half", F32), ("half", F32), ("part", F32)],
-            [(0, output)], 2 * unit)
+            [(0, output)], 4.0)
         gsums.append(gsum)
         suffix.append(scan(keep, send, -1))
         prevs.append(shifted(part, 1))
@@ -343,7 +341,7 @@
             [("wide", q), ("wide", k), ("wide", v), ("block", dab), ("probs", probs), ("mask", mask), ("segs", imgs),
              ("half", prefix[g][0]), ("half", prefix[g][1]), ("part", nexts[g])],
             [("wide", BF16), ("block", F32), ("block", F32)],
-            [(0, grad_q)], 8 * unit)
+            [(0, grad_q)], 5.5)
         inner.append((gk, gv))
     grad_gain = scatter_sum(jnp.concatenate(gsums, axis=1))
     for g in range(GROUPS):
@@ -353,7 +351,7 @@
             [("wide", k), ("wide", v), ("block", gk), ("block", gv), ("segs", segs),
              ("half", suffix[g][0]), ("half", suffix[g][1]), ("part", prevs[g])],
             [("wide", BF16), ("wide", BF16)],
-            [(0, grad_k), (1, grad_v)], 2 * unit)
+            [(0, grad_k), (1, grad_v)], 2.1)
     return output[None], grad_q[None], grad_k[None], grad_v[None], grad_gain
 
 

time: 119 us -> 112 us (0.941)
  waiting for transfers between devices: 18.7 us -> 9.72 us
  Pallas kernels: 34.8 us -> 28.6 us
  other arithmetic: 7.44 us -> 12.8 us
  local copies, waits for them, and re-layouts: 15.3 us -> 20 us
  starting transfers between devices: 40.7 us -> 38.4 us
    ppermute x13 -> x8, starting transfers between devices: 17.9 us -> 6.7 us  [partner(): return lax.ppermute(x, axis, route)]
    all_to_all x0 -> x1, starting transfers between devices: none -> 7.62 us  [scatter_sum(): terms = lax.all_to_all(x.reshape(devices, -1), axes, 0, 0, tiled=True)]
    ppermute x12, waiting for transfers between devices: 16.3 us -> 8.96 us  [chips_before(): before = before + lax.ppermute(own + before, 'ctx', route)]
    pallas_call x10, Pallas kernels: 34.8 us -> 28.6 us  [call(): pl.pallas_call(kernel, grid_spec=pltpu.PrefetchScalarGridSpec(num_scalar_...]
    unnamed x86 -> x72, local copies, waits for them, and re-layouts: 14.4 us -> 18.5 us
    select_n x4, other arithmetic: 0.14 us -> 2.85 us  [scan(): theirs = partner(jnp.where(is_source, before + keep, before), 'ctx', 0)]
    add x4, other arithmetic: 0.74 us -> 2.78 us  [scan(): before = chips_before(keep + received, towards)]
    ppermute x13 -> x8, waiting for transfers between devices: 2.36 us -> 0.74 us  [partner(): return lax.ppermute(x, axis, route)]
  transfers between devices with their start and end apart: 29 -> 25, of which waited for: 4 -> 4; matrix products, arithmetic and copies ran while one was open for 5% -> 11% of each run, Pallas kernels for 21% -> 22%
where the time goes in v2:
time: 112 us; the launch traced here: 111 us
  starting transfers between devices  38.4 us (34%)
  Pallas kernels  28.6 us (26%)
  local copies, waits for them, and re-layouts  20 us (18%)
  other arithmetic  12.8 us (11%)
  waiting for transfers between devices  9.72 us (9%)
  between operations  1.15 us (1%)
    pallas_call x10, Pallas kernels, call(): pl.pallas_call(kernel, grid_spec=pltpu.PrefetchScalarGridSpec(num_scalar_...  28.6 us
    unnamed x72, local copies, waits for them, and re-layouts  18.5 us
    ppermute x12, starting transfers between devices, chips_before(): before = before + lax.ppermute(own + before, 'ctx', route)  15.8 us
    ppermute x12, waiting for transfers between devices, chips_before(): before = before + lax.ppermute(own + before, 'ctx', route)  8.96 us
    ppermute x4, starting transfers between devices, shifted(): lax.ppermute(x, 'ctx', [(i, i + distance) for i in range(count) if 0 <= i...  8.29 us
    all_to_all x1, starting transfers between devices, scatter_sum(): terms = lax.all_to_all(x.reshape(devices, -1), axes, 0, 0, tiled=True)  7.62 us
    ppermute x8, starting transfers between devices, partner(): return lax.ppermute(x, axis, route)  6.7 us
    add x8, other arithmetic, chips_before(): before = before + lax.ppermute(own + before, 'ctx', route)  3.66 us
  transfers between devices with their start and end apart: 25, of which 4 were waited for; matrix products, arithmetic and copies ran while one was open for 11% of the time, Pallas kernels for 22%

profile of v2, /device:TPU:0, one launch (start us, length us, event | category | flops | bytes accessed | tf_op | source)
XLA Modules:
  0.0 110.7 jit_solution(7276967229589153600)
XLA Ops:
  3.9 1.4 %shard_map.113 = (f32[256,128]{1,0:T(8,128)S(1)}, f32[256,128]{1,0:T(8,128)S(1)}, f32[2,264,128]{2,1,0:T(8,128)}) custom-call(s32[1]{0:T(128)} %bitcast.core, bf16[256,2048]{1,0:T(8,128)(2,1)S(1)} %bitcast.21, bf16[256,2048]{1,0:T(8,128)(2,1)S(1)} %bitcast.29, f32[256,128]{1,0:T(8,128)S(1)} %broadcast_in_dim.50.segs), custom_call_target="tpu_custom_call" | custom-call | flops 1610000000 | bytes 1048576 | tf_op jit(solution)/shard_map/pallas_call | solution.py:300
  5.7 1.4 %collective-permute-start.11 = (f32[2,264,128]{2,1,0:T(8,128)}, f32[2,264,128]{2,1,0:T(8,128)S(1)}, u32[]{:S(2)}, u32[]{:S(2)}) collective-permute-start(f32[2,264,128]{2,1,0:T(8,128)} %get-tuple-element.44), channel_id=1, source_target_pairs={{1,0},{2,1},{3,2},{4,3},{5,4},{6,5},{7,6},{9,8},{10,9},{11,10},{12... | collective-permute-start | bytes 811016 | tf_op jit(solution)/shard_map/ppermute | solution.py:202
  7.2 1.4 %shard_map.111 = (f32[256,128]{1,0:T(8,128)S(1)}, f32[256,128]{1,0:T(8,128)S(1)}, f32[2,264,128]{2,1,0:T(8,128)}) custom-call(s32[1]{0:T(128)} %bitcast.core, bf16[256,2048]{1,0:T(8,128)(2,1)S(1)} %bitcast.22, bf16[256,2048]{1,0:T(8,128)(2,1)S(1)} %bitcast.30, f32[256,128]{1,0:T(8,128)S(1)} %broadcast_in_dim.50.segs), custom_call_target="tpu_custom_call" | custom-call | flops 1610000000 | bytes 1048576 | tf_op jit(solution)/shard_map/pallas_call | solution.py:300
  12.8 5.1 %collective-permute-start.7 = (f32[256,128]{1,0:T(8,128)S(1)}, f32[256,128]{1,0:T(8,128)S(1)}, u32[]{:S(2)}, u32[]{:S(2)}) collective-permute-start(f32[256,128]{1,0:T(8,128)S(1)} %add.91), channel_id=1, source_target_pairs={{0,2},{1,3},{8,10},{9,11},{16,18},{17,19},{24,26},{25,27}} | collective-permute-start | bytes 393224 | tf_op jit(solution)/shard_map/ppermute | solution.py:218
  19.2 2.3 %shard_map.112 = (f32[256,1024]{1,0:T(8,128)S(1)}, bf16[16,256,256]{2,1,0:T(8,128)(2,1)S(1)}) custom-call(s32[1]{0:T(128)} %bitcast.core, bf16[256,2048]{1,0:T(8,128)(2,1)S(1)} %bitcast.15, bf16[256,2048]{1,0:T(8,128)(2,1)S(1)} %bitcast.23, bf16[256,2048]{1,0:T(8,128)(2,1)S(1)} %bitcast.31, bf16[256,256]{1,0:T(8,128)(2,1)S(1)} %fusion.1.mask), custom_call_target="tpu_custom_call" | custom-call | flops 2644999936 | bytes 2097152 | tf_op jit(solution)/shard_map/pallas_call | solution.py:300
  21.6 1.3 %copy-done.23 = bf16[16,256,256]{2,1,0:T(8,128)(2,1)} copy-done((bf16[16,256,256]{2,1,0:T(8,128)(2,1)}, bf16[16,256,256]{2,1,0:T(8,128)(2,1)S(1)}, u32[]{:S(2)}) %copy-start.23) | copy-done | bytes 2097176
  25.6 2.4 %shard_map.110 = (f32[256,1024]{1,0:T(8,128)S(1)}, bf16[16,256,256]{2,1,0:T(8,128)(2,1)S(1)}) custom-call(s32[1]{0:T(128)} %bitcast.core, bf16[256,2048]{1,0:T(8,128)(2,1)S(1)} %bitcast.16, bf16[256,2048]{1,0:T(8,128)(2,1)S(1)} %bitcast.24, bf16[256,2048]{1,0:T(8,128)(2,1)S(1)} %bitcast.32, bf16[256,256]{1,0:T(8,128)(2,1)S(1)} %fusion.1.mask), custom_call_target="tpu_custom_call" | custom-call | flops 2644999936 | bytes 2097152 | tf_op jit(solution)/shard_map/pallas_call | solution.py:300
  33.1 3.0 %shard_map.114 = (bf16[256,2048]{1,0:T(8,128)(2,1)}, bf16[256,1024]{1,0:T(8,128)(2,1)S(1)}, f32[1,1024]{1,0:T(1,128)S(1)}, f32[256,128]{1,0:T(8,128)S(1)}, f32[256,128]{1,0:T(8,128)}, /*index=5*/f32[2,264,128]{2,1,0:T(8,128)}) custom-call(s32[1]{0:T(128)} %bitcast.core, bf16[256,2048]{1,0:T(8,128)(2,1)S(1)} %bitcast.17, bf16[256,2048]{1,0:T(8,128)(2,1)S(1)} %bitcast.13, ...), custom_call_target="tpu_custom_call" | custom-call | flops 4600000000 | bytes 2621440 | tf_op jit(solution)/shard_map/pallas_call | solution.py:300
  37.0 3.0 %collective-permute-start.23 = (f32[2,264,128]{2,1,0:T(8,128)}, f32[2,264,128]{2,1,0:T(8,128)}, u32[]{:S(2)}, u32[]{:S(2)}) collective-permute-start(f32[2,264,128]{2,1,0:T(8,128)} %get-tuple-element.62), channel_id=1, source_target_pairs={{0,1},{1,2},{2,3},{3,4},{4,5},{5,6},{6,7},{8,9},{9,10},{10,11},{11... | collective-permute-start | bytes 811016 | tf_op jit(solution)/shard_map/ppermute | solution.py:202
  40.0 3.0 %shard_map.115 = (bf16[256,2048]{1,0:T(8,128)(2,1)}, bf16[256,1024]{1,0:T(8,128)(2,1)S(1)}, f32[1,1024]{1,0:T(1,128)S(1)}, f32[256,128]{1,0:T(8,128)S(1)}, f32[256,128]{1,0:T(8,128)}, /*index=5*/f32[2,264,128]{2,1,0:T(8,128)}) custom-call(s32[1]{0:T(128)} %bitcast.core, bf16[256,2048]{1,0:T(8,128)(2,1)S(1)} %bitcast.18, ...), custom_call_target="tpu_custom_call", output_to_operand_aliasing={{0}: (10, {})} | custom-call | flops 4600000000 | bytes 2621440 | tf_op jit(solution)/shard_map/pallas_call | solution.py:300
  43.8 4.2 %collective-permute-start.12 = (f32[256,128]{1,0:T(8,128)}, f32[256,128]{1,0:T(8,128)}, u32[]{:S(2)}, u32[]{:S(2)}) collective-permute-start(f32[256,128]{1,0:T(8,128)} %get-tuple-element.56), channel_id=1, source_target_pairs={{0,1},{1,0},{2,3},{3,2},{4,5},{5,4},{6,7},{7,6},{8,9},{9,8},{10,11... | collective-permute-start | bytes 393224 | tf_op jit(solution)/shard_map/ppermute | solution.py:197
  48.0 2.6 %collective-permute-start.17 = (f32[2,264,128]{2,1,0:T(8,128)}, f32[2,264,128]{2,1,0:T(8,128)}, u32[]{:S(2)}, u32[]{:S(2)}) collective-permute-start(f32[2,264,128]{2,1,0:T(8,128)} %get-tuple-element.57), channel_id=1, source_target_pairs={{0,1},{1,2},{2,3},{3,4},{4,5},{5,6},{6,7},{8,9},{9,10},{10,11},{11... | collective-permute-start | bytes 811016 | tf_op jit(solution)/shard_map/ppermute | solution.py:202
  51.3 1.4 %all_to_all.6 = f32[32,1,64]{2,0,1:T(8,128)} reshape(f32[2048]{0:T(1024)} %maximum_reduce_fusion) | data formatting | bytes 16384 | tf_op jit(solution)/shard_map/all_to_all | solution.py:235
  52.6 7.6 %all-to-all-start = ((f32[32,1,64]{2,1,0:T(1,128)}), f32[32,1,64]{2,1,0:T(1,128)}, u32[]{:S(2)}, u32[]{:S(2)}) async-start(f32[32,1,64]{2,1,0:T(1,128)} %bitcast.39), calls=%async_computation | async-start | bytes 32768 | tf_op jit(solution)/shard_map/all_to_all | solution.py:235
  64.0 1.6 %copy-done.24 = bf16[16,256,256]{2,1,0:T(8,128)(2,1)S(1)} copy-done((bf16[16,256,256]{2,1,0:T(8,128)(2,1)S(1)}, bf16[16,256,256]{2,1,0:T(8,128)(2,1)}, u32[]{:S(2)}) %copy-start.24) | copy-done | bytes 2097176
  66.6 4.6 %shard_map.116 = (bf16[256,2048]{1,0:T(8,128)(2,1)}, f32[256,1024]{1,0:T(8,128)S(1)}, f32[256,1024]{1,0:T(8,128)S(1)}) custom-call(s32[1]{0:T(128)} %bitcast.core, bf16[256,2048]{1,0:T(8,128)(2,1)S(1)} %bitcast.19, bf16[256,2048]{1,0:T(8,128)(2,1)S(1)} %bitcast.25, bf16[256,2048]{1,0:T(8,128)(2,1)S(1)} %bitcast.33, bf16[256,1024]{1,0:T(8,128)(2,1)S(1)} %copy-done.28, ...), custom_call_target="tpu_custom_call" | custom-call | flops 6325000192 | bytes 3670016 | tf_op jit(solution)/shard_map/pallas_call | solution.py:300
  74.1 1.3 %collective-permute-start.13 = (f32[256,128]{1,0:T(8,128)S(1)}, f32[256,128]{1,0:T(8,128)}, u32[]{:S(2)}, u32[]{:S(2)}) collective-permute-start(f32[256,128]{1,0:T(8,128)S(1)} %add.98), channel_id=1, source_target_pairs={{6,4},{7,5},{14,12},{15,13},{22,20},{23,21},{30,28},{31,29}} | collective-permute-start | bytes 393224 | tf_op jit(solution)/shard_map/ppermute | solution.py:218
  76.2 1.3 %collective-permute-start.20 = (f32[256,128]{1,0:T(8,128)}, f32[256,128]{1,0:T(8,128)}, u32[]{:S(2)}, u32[]{:S(2)}) collective-permute-start(f32[256,128]{1,0:T(8,128)} %add.106), channel_id=1, source_target_pairs={{4,2},{5,3},{12,10},{13,11},{20,18},{21,19},{28,26},{29,27}} | collective-permute-start | bytes 393224 | tf_op jit(solution)/shard_map/ppermute | solution.py:218
  77.5 4.7 %shard_map.117 = (bf16[256,2048]{1,0:T(8,128)(2,1)}, f32[256,1024]{1,0:T(8,128)S(1)}, f32[256,1024]{1,0:T(8,128)S(1)}) custom-call(s32[1]{0:T(128)} %bitcast.core, bf16[256,2048]{1,0:T(8,128)(2,1)S(1)} %bitcast.20, bf16[256,2048]{1,0:T(8,128)(2,1)S(1)} %bitcast.26, bf16[256,2048]{1,0:T(8,128)(2,1)S(1)} %bitcast.34, ...), custom_call_target="tpu_custom_call", output_to_operand_aliasing={{0}: (11, {})} | custom-call | flops 6325000192 | bytes 3670016 | tf_op jit(solution)/shard_map/pallas_call | solution.py:300
  84.2 1.4 %reduce_sum.19 = f32[64]{0:T(128)} reduce(f32[32,1,64]{2,1,0:T(1,128)} %all-to-all-done, f32[]{:T(128)} %constant.3.clone.1), dimensions={0,1}, to_apply=%region_1.2 | reduce | flops 1984 | bytes 8452 | tf_op jit(solution)/shard_map/reduce_sum | solution.py:236
  91.7 3.9 %collective-permute-done.21 = f32[256,128]{1,0:T(8,128)S(1)} collective-permute-done((f32[256,128]{1,0:T(8,128)S(1)}, f32[256,128]{1,0:T(8,128)S(1)}, u32[]{:S(2)}, u32[]{:S(2)}) %collective-permute-start.21) | collective-permute-done | bytes 131104 | tf_op jit(solution)/shard_map/ppermute | solution.py:218
  96.7 4.8 %collective-permute-done.15 = f32[256,128]{1,0:T(8,128)S(1)} collective-permute-done((f32[256,128]{1,0:T(8,128)S(1)}, f32[256,128]{1,0:T(8,128)S(1)}, u32[]{:S(2)}, u32[]{:S(2)}) %collective-permute-start.15) | collective-permute-done | bytes 131104 | tf_op jit(solution)/shard_map/ppermute | solution.py:218
  105.0 2.9 %shard_map.118 = (bf16[256,2048]{1,0:T(8,128)(2,1)}, bf16[256,2048]{1,0:T(8,128)(2,1)}) custom-call(s32[1]{0:T(128)} %bitcast.core, bf16[256,2048]{1,0:T(8,128)(2,1)S(1)} %bitcast.27, bf16[256,2048]{1,0:T(8,128)(2,1)S(1)} %bitcast.35, f32[256,1024]{1,0:T(8,128)S(1)} %copy-done.18, f32[256,1024]{1,0:T(8,128)S(1)} %copy-done.20, ...), custom_call_target="tpu_custom_call" | custom-call | flops 2415000064 | bytes 3145728 | tf_op jit(solution)/shard_map/pallas_call | solution.py:300
  107.9 2.8 %shard_map.119 = (bf16[256,2048]{1,0:T(8,128)(2,1)}, bf16[256,2048]{1,0:T(8,128)(2,1)}) custom-call(s32[1]{0:T(128)} %bitcast.core, bf16[256,2048]{1,0:T(8,128)(2,1)S(1)} %bitcast.28, bf16[256,2048]{1,0:T(8,128)(2,1)S(1)} %bitcast.36, f32[256,1024]{1,0:T(8,128)S(1)} %copy-done.14, ...), custom_call_target="tpu_custom_call", output_to_operand_aliasing={{0}: (9, {}), {1}: (10, {})} | custom-call | flops 2415000064 | bytes 3145728 | tf_op jit(solution)/shard_map/pallas_call | solution.py:300
  (133 shorter events, 40.0 us)
Async XLA Ops:
  5.3 6.7 %collective-permute-start.6 = (f32[256,128]{1,0:T(8,128)S(1)}, f32[256,128]{1,0:T(8,128)}, u32[]{:S(2)}, u32[]{:S(2)}) collective-permute-start(f32[256,128]{1,0:T(8,128)S(1)} %get-tuple-element.43), channel_id=1, source_target_pairs={{0,1},{1,0},{2,3},{3,2},{4,5},{5,4},{6,7},{7,6},{8,9},{9,8},{10,11... | collective-permute-start | bytes 393224 | tf_op jit(solution)/shard_map/ppermute | solution.py:197
  5.7 26.5 %collective-permute-start.11 = (f32[2,264,128]{2,1,0:T(8,128)}, f32[2,264,128]{2,1,0:T(8,128)S(1)}, u32[]{:S(2)}, u32[]{:S(2)}) collective-permute-start(f32[2,264,128]{2,1,0:T(8,128)} %get-tuple-element.44), channel_id=1, source_target_pairs={{1,0},{2,1},{3,2},{4,3},{5,4},{6,5},{7,6},{9,8},{10,9},{11,10},{12... | collective-permute-start | bytes 811016 | tf_op jit(solution)/shard_map/ppermute | solution.py:202
  8.6 14.3 %collective-permute-start = (f32[256,128]{1,0:T(8,128)S(1)}, f32[256,128]{1,0:T(8,128)S(1)}, u32[]{:S(2)}, u32[]{:S(2)}) collective-permute-start(f32[256,128]{1,0:T(8,128)S(1)} %get-tuple-element.39), channel_id=1, source_target_pairs={{0,1},{1,0},{2,3},{3,2},{4,5},{5,4},{6,7},{7,6},{8,9},{9,8},{10,11... | collective-permute-start | bytes 393224 | tf_op jit(solution)/shard_map/ppermute | solution.py:197
  9.7 30.3 %collective-permute-start.5 = (f32[2,264,128]{2,1,0:T(8,128)}, f32[2,264,128]{2,1,0:T(8,128)S(1)}, u32[]{:S(2)}, u32[]{:S(2)}) collective-permute-start(f32[2,264,128]{2,1,0:T(8,128)} %get-tuple-element.40), channel_id=1, source_target_pairs={{1,0},{2,1},{3,2},{4,3},{5,4},{6,5},{7,6},{9,8},{10,9},{11,10},{12... | collective-permute-start | bytes 811016 | tf_op jit(solution)/shard_map/ppermute | solution.py:202
  12.8 12.1 %collective-permute-start.7 = (f32[256,128]{1,0:T(8,128)S(1)}, f32[256,128]{1,0:T(8,128)S(1)}, u32[]{:S(2)}, u32[]{:S(2)}) collective-permute-start(f32[256,128]{1,0:T(8,128)S(1)} %add.91), channel_id=1, source_target_pairs={{0,2},{1,3},{8,10},{9,11},{16,18},{17,19},{24,26},{25,27}} | collective-permute-start | bytes 393224 | tf_op jit(solution)/shard_map/ppermute | solution.py:218
  23.6 4.7 %collective-permute-start.1 = (f32[256,128]{1,0:T(8,128)S(1)}, f32[256,128]{1,0:T(8,128)S(1)}, u32[]{:S(2)}, u32[]{:S(2)}) collective-permute-start(f32[256,128]{1,0:T(8,128)S(1)} %add.84), channel_id=1, source_target_pairs={{0,2},{1,3},{8,10},{9,11},{16,18},{17,19},{24,26},{25,27}} | collective-permute-start | bytes 393224 | tf_op jit(solution)/shard_map/ppermute | solution.py:218
  24.9 4.2 %collective-permute-start.8 = (f32[256,128]{1,0:T(8,128)S(1)}, f32[256,128]{1,0:T(8,128)S(1)}, u32[]{:S(2)}, u32[]{:S(2)}) collective-permute-start(f32[256,128]{1,0:T(8,128)S(1)} %add.92), channel_id=1, source_target_pairs={{2,4},{3,5},{10,12},{11,13},{18,20},{19,21},{26,28},{27,29}} | collective-permute-start | bytes 393224 | tf_op jit(solution)/shard_map/ppermute | solution.py:218
  28.3 1.5 %collective-permute-start.2 = (f32[256,128]{1,0:T(8,128)S(1)}, f32[256,128]{1,0:T(8,128)S(1)}, u32[]{:S(2)}, u32[]{:S(2)}) collective-permute-start(f32[256,128]{1,0:T(8,128)S(1)} %add.85), channel_id=1, source_target_pairs={{2,4},{3,5},{10,12},{11,13},{18,20},{19,21},{26,28},{27,29}} | collective-permute-start | bytes 393224 | tf_op jit(solution)/shard_map/ppermute | solution.py:218
  29.9 1.8 %collective-permute-start.3 = (f32[256,128]{1,0:T(8,128)S(1)}, f32[256,128]{1,0:T(8,128)S(1)}, u32[]{:S(2)}, u32[]{:S(2)}) collective-permute-start(f32[256,128]{1,0:T(8,128)S(1)} %get-tuple-element.75), channel_id=1, source_target_pairs={{4,6},{5,7},{12,14},{13,15},{20,22},{21,23},{28,30},{29,31}} | collective-permute-start | bytes 393224 | tf_op jit(solution)/shard_map/ppermute | solution.py:218
  31.5 1.4 %collective-permute-start.10 = (f32[256,128]{1,0:T(8,128)S(1)}, f32[256,128]{1,0:T(8,128)S(1)}, u32[]{:S(2)}, u32[]{:S(2)}) collective-permute-start(f32[256,128]{1,0:T(8,128)S(1)} %get-tuple-element.83), channel_id=1, source_target_pairs={{0,1},{1,0},{2,3},{3,2},{4,5},{5,4},{6,7},{7,6},{8,9},{9,8},{10,11... | collective-permute-start | bytes 393224 | tf_op jit(solution)/shard_map/ppermute | solution.py:197
  31.7 8.2 %collective-permute-start.4 = (f32[256,128]{1,0:T(8,128)S(1)}, f32[256,128]{1,0:T(8,128)S(1)}, u32[]{:S(2)}, u32[]{:S(2)}) collective-permute-start(f32[256,128]{1,0:T(8,128)S(1)} %get-tuple-element.85), channel_id=1, source_target_pairs={{0,1},{1,0},{2,3},{3,2},{4,5},{5,4},{6,7},{7,6},{8,9},{9,8},{10,11... | collective-permute-start | bytes 393224 | tf_op jit(solution)/shard_map/ppermute | solution.py:197
  36.9 23.4 %collective-permute-start.18 = (f32[256,128]{1,0:T(8,128)}, f32[256,128]{1,0:T(8,128)}, u32[]{:S(2)}, u32[]{:S(2)}) collective-permute-start(f32[256,128]{1,0:T(8,128)} %get-tuple-element.61), channel_id=1, source_target_pairs={{0,1},{1,0},{2,3},{3,2},{4,5},{5,4},{6,7},{7,6},{8,9},{9,8},{10,11... | collective-permute-start | bytes 393224 | tf_op jit(solution)/shard_map/ppermute | solution.py:197
  37.0 65.5 %collective-permute-start.23 = (f32[2,264,128]{2,1,0:T(8,128)}, f32[2,264,128]{2,1,0:T(8,128)}, u32[]{:S(2)}, u32[]{:S(2)}) collective-permute-start(f32[2,264,128]{2,1,0:T(8,128)} %get-tuple-element.62), channel_id=1, source_target_pairs={{0,1},{1,2},{2,3},{3,4},{4,5},{5,6},{6,7},{8,9},{9,10},{10,11},{11... | collective-permute-start | bytes 811016 | tf_op jit(solution)/shard_map/ppermute | solution.py:202
  43.8 29.4 %collective-permute-start.12 = (f32[256,128]{1,0:T(8,128)}, f32[256,128]{1,0:T(8,128)}, u32[]{:S(2)}, u32[]{:S(2)}) collective-permute-start(f32[256,128]{1,0:T(8,128)} %get-tuple-element.56), channel_id=1, source_target_pairs={{0,1},{1,0},{2,3},{3,2},{4,5},{5,4},{6,7},{7,6},{8,9},{9,8},{10,11... | collective-permute-start | bytes 393224 | tf_op jit(solution)/shard_map/ppermute | solution.py:197
  48.0 59.8 %collective-permute-start.17 = (f32[2,264,128]{2,1,0:T(8,128)}, f32[2,264,128]{2,1,0:T(8,128)}, u32[]{:S(2)}, u32[]{:S(2)}) collective-permute-start(f32[2,264,128]{2,1,0:T(8,128)} %get-tuple-element.57), channel_id=1, source_target_pairs={{0,1},{1,2},{2,3},{3,4},{4,5},{5,6},{6,7},{8,9},{9,10},{10,11},{11... | collective-permute-start | bytes 811016 | tf_op jit(solution)/shard_map/ppermute | solution.py:202
  52.6 31.6 %all-to-all-start = ((f32[32,1,64]{2,1,0:T(1,128)}), f32[32,1,64]{2,1,0:T(1,128)}, u32[]{:S(2)}, u32[]{:S(2)}) async-start(f32[32,1,64]{2,1,0:T(1,128)} %bitcast.39), calls=%async_computation | async-start | bytes 32768 | tf_op jit(solution)/shard_map/all_to_all | solution.py:235
  61.2 14.3 %collective-permute-start.19 = (f32[256,128]{1,0:T(8,128)S(1)}, f32[256,128]{1,0:T(8,128)S(1)}, u32[]{:S(2)}, u32[]{:S(2)}) collective-permute-start(f32[256,128]{1,0:T(8,128)S(1)} %add.105), channel_id=1, source_target_pairs={{6,4},{7,5},{14,12},{15,13},{22,20},{23,21},{30,28},{31,29}} | collective-permute-start | bytes 393224 | tf_op jit(solution)/shard_map/ppermute | solution.py:218
  74.1 11.4 %collective-permute-start.13 = (f32[256,128]{1,0:T(8,128)S(1)}, f32[256,128]{1,0:T(8,128)}, u32[]{:S(2)}, u32[]{:S(2)}) collective-permute-start(f32[256,128]{1,0:T(8,128)S(1)} %add.98), channel_id=1, source_target_pairs={{6,4},{7,5},{14,12},{15,13},{22,20},{23,21},{30,28},{31,29}} | collective-permute-start | bytes 393224 | tf_op jit(solution)/shard_map/ppermute | solution.py:218
  76.2 11.0 %collective-permute-start.20 = (f32[256,128]{1,0:T(8,128)}, f32[256,128]{1,0:T(8,128)}, u32[]{:S(2)}, u32[]{:S(2)}) collective-permute-start(f32[256,128]{1,0:T(8,128)} %add.106), channel_id=1, source_target_pairs={{4,2},{5,3},{12,10},{13,11},{20,18},{21,19},{28,26},{29,27}} | collective-permute-start | bytes 393224 | tf_op jit(solution)/shard_map/ppermute | solution.py:218
  86.5 3.0 %collective-permute-start.14 = (f32[256,128]{1,0:T(8,128)S(1)}, f32[256,128]{1,0:T(8,128)S(1)}, u32[]{:S(2)}, u32[]{:S(2)}) collective-permute-start(f32[256,128]{1,0:T(8,128)S(1)} %add.99), channel_id=1, source_target_pairs={{4,2},{5,3},{12,10},{13,11},{20,18},{21,19},{28,26},{29,27}} | collective-permute-start | bytes 393224 | tf_op jit(solution)/shard_map/ppermute | solution.py:218
  88.2 7.5 %collective-permute-start.21 = (f32[256,128]{1,0:T(8,128)S(1)}, f32[256,128]{1,0:T(8,128)S(1)}, u32[]{:S(2)}, u32[]{:S(2)}) collective-permute-start(f32[256,128]{1,0:T(8,128)S(1)} %get-tuple-element.69), channel_id=1, source_target_pairs={{2,0},{3,1},{10,8},{11,9},{18,16},{19,17},{26,24},{27,25}} | collective-permute-start | bytes 393224 | tf_op jit(solution)/shard_map/ppermute | solution.py:218
  90.4 11.0 %collective-permute-start.15 = (f32[256,128]{1,0:T(8,128)S(1)}, f32[256,128]{1,0:T(8,128)S(1)}, u32[]{:S(2)}, u32[]{:S(2)}) collective-permute-start(f32[256,128]{1,0:T(8,128)S(1)} %get-tuple-element.71), channel_id=1, source_target_pairs={{2,0},{3,1},{10,8},{11,9},{18,16},{19,17},{26,24},{27,25}} | collective-permute-start | bytes 393224 | tf_op jit(solution)/shard_map/ppermute | solution.py:218
  96.6 5.9 %collective-permute-start.22 = (f32[256,128]{1,0:T(8,128)S(1)}, f32[256,128]{1,0:T(8,128)S(1)}, u32[]{:S(2)}, u32[]{:S(2)}) collective-permute-start(f32[256,128]{1,0:T(8,128)S(1)} %get-tuple-element.79), channel_id=1, source_target_pairs={{0,1},{1,0},{2,3},{3,2},{4,5},{5,4},{6,7},{7,6},{8,9},{9,8},{10,11... | collective-permute-start | bytes 393224 | tf_op jit(solution)/shard_map/ppermute | solution.py:197
  102.4 5.5 %collective-permute-start.16 = (f32[256,128]{1,0:T(8,128)S(1)}, f32[256,128]{1,0:T(8,128)S(1)}, u32[]{:S(2)}, u32[]{:S(2)}) collective-permute-start(f32[256,128]{1,0:T(8,128)S(1)} %get-tuple-element.81), channel_id=1, source_target_pairs={{0,1},{1,0},{2,3},{3,2},{4,5},{5,4},{6,7},{7,6},{8,9},{9,8},{10,11... | collective-permute-start | bytes 393224 | tf_op jit(solution)/shard_map/ppermute | solution.py:197
  (37 other events, 162.6 us)

commit v3 on v2

v3 whole, which is shorter than its diff:
```python
import functools

import jax
import jax.numpy as jnp
from jax import lax
from jax.experimental import pallas as pl
from jax.experimental.pallas import tpu as pltpu
from jax.sharding import PartitionSpec as P

E = 64
PAIR = 2 * E
GROUPS = 2
EXTRA = 8
VMEM = 10 * 2**20
F32 = jnp.float32
BF16 = jnp.bfloat16


def dot(a, b, ca, cb):
    return lax.dot_general(a, b, (((ca,), (cb,)), ((), ())), preferred_element_type=F32)


def low_lanes(rows, cols):
    lane = lax.broadcasted_iota(jnp.int32, (rows, cols), 1)
    return lane % PAIR < E


def fold(product):
    return jnp.where(low_lanes(E, product.shape[1]), product[:E], product[E:])


def split(state):
    high = state.astype(BF16)
    return high, (state - high.astype(F32)).astype(BF16)


def spread(state):
    low = low_lanes(*state.shape)
    zero = jnp.zeros_like(state)
    return jnp.concatenate([jnp.where(low, state, zero), jnp.where(low, zero, state)], axis=0)


def heads_of(pair):
    low = low_lanes(*pair.shape)
    zero = jnp.zeros_like(pair)
    return jnp.where(low, pair, zero), jnp.where(low, zero, pair)


def twice(x):
    return jnp.concatenate([x, x], axis=1)


def pair_at(ref, p):
    return ref[:, p * PAIR:(p + 1) * PAIR]


def rows_of(value, p):
    return value[p * E:(p + 1) * E]


def state_pair(a, b):
    return fold(dot(a, b, 0, 0))


def edge(seg, table, last):
    row = seg[...]
    count = row.shape[1]
    own = row[:, count - 1:] if last else row[:, :1]
    size = jnp.sum((row == own).astype(F32), axis=1, keepdims=True)
    at = lax.broadcasted_iota(jnp.int32, (count, PAIR), 0).astype(F32)
    rows = at >= count - size if last else at < size
    ids = lax.broadcasted_iota(jnp.int32, table.shape, 1)
    flag = jnp.sum(jnp.where(ids == own, table[...], 0).astype(F32), axis=1, keepdims=True)
    return rows, own.astype(F32), flag


def states_kernel(group, core, k, v, *rest):
    keep, send, k_buf, v_buf, sems = rest[-5:]
    lanes = k_buf.shape[2]
    copies = []
    for half in (1, 0):
        at = pl.multiple_of((2 * group + (half + core[0]) % 2) * lanes, lanes)
        for i, (array, buf) in enumerate(((k, k_buf), (v, v_buf))):
            copies.append(pltpu.make_async_copy(array.at[:, pl.ds(at, lanes)], buf.at[half], sems.at[half, i]))
    for copy in copies:
        copy.start()
    for half, out in ((1, send), (0, keep)):
        copies.pop(0).wait()
        copies.pop(0).wait()
        for p in range(lanes // PAIR):
            at = slice(p * PAIR, (p + 1) * PAIR)
            out[p * E:(p + 1) * E] = state_pair(k_buf[half, :, at], v_buf[half, :, at])


def part_kernel(last, a, b, seg, table, *rest):
    out = rest[-1]
    count = a.shape[1] // PAIR
    rows, own, flag = edge(seg, table, last)
    sel = rows.astype(F32) * jnp.where(flag == 1, 1.0, 0.0) if last else rows.astype(F32)
    sel = sel.astype(BF16)
    for p in range(count):
        out[0, p * E:(p + 1) * E] = state_pair(pair_at(a, p), pair_at(b, p) * sel)
    out[0, count * E:] = jnp.broadcast_to(own, (EXTRA, PAIR))


def local_kernel(core, q, k, v, mask, *rest):
    attn, token = rest[-2:]
    m = mask[...]
    token[...] = jnp.zeros_like(token)
    for p in range(q.shape[1] // PAIR):
        kp = pair_at(k, p)
        total = None
        for qh, vh in zip(heads_of(pair_at(q, p)), heads_of(pair_at(v, p))):
            prob = dot(qh, kp, 1, 1).astype(BF16) * m
            term = dot(prob, vh, 1, 0)
            total = term if total is None else total + term
        attn[:, p * PAIR:(p + 1) * PAIR] = total


def head_mean(x):
    high, low = split(x)
    ones = spread(jnp.full((E, PAIR), 1.0 / E, BF16))
    return dot(jnp.concatenate([high, low], axis=1), jnp.concatenate([ones, ones], axis=0), 1, 0)


def side_by_side(state, part):
    sh, sl = split(state)
    ph, pll = split(part)
    left = jnp.concatenate([spread(sh), spread(sl)], axis=0)
    right = jnp.concatenate([spread(ph), spread(pll)], axis=0)
    return jnp.concatenate([left, right], axis=1)


def stacked(state, part):
    sh, sl = split(state)
    ph, pll = split(part)
    top = jnp.concatenate([spread(sh), spread(sl)], axis=1)
    bottom = jnp.concatenate([spread(ph), spread(pll)], axis=1)
    return jnp.concatenate([top, bottom], axis=0)


def on_rows(seg, table, last, part, count):
    rows, own, flag = edge(seg, table, last)
    met = part[0, count * E:count * E + 1] == own
    if last:
        met = met & (flag == 1)
    return rows.astype(F32) * met.astype(F32)


def norm_kernel(core, q, dy, local, gain, seg, table, pre_keep, pre_recv, nxt, *rest):
    out, dab, gsum, keep, send = rest[-5:]
    step = pl.program_id(0)
    count = q.shape[1] // PAIR
    prefix = jnp.where(step == 0, pre_keep[...], pre_recv[...])
    on_next = on_rows(seg, table, True, nxt, count)
    pairs = [slice(p * PAIR, (p + 1) * PAIR) for p in range(count)]
    fars = [
        dot(twice(q[:, at]), side_by_side(rows_of(prefix, p), nxt[0, p * E:(p + 1) * E]), 1, 0)
        for p, at in enumerate(pairs)
    ]
    attns = [local[:, at] + far[:, :PAIR] + on_next * far[:, PAIR:] for at, far in zip(pairs, fars)]
    squares = [head_mean(attn * attn) for attn in attns]
    scales = [lax.rsqrt(square + 1e-06) for square in squares]
    normeds = [attn * scale for attn, scale in zip(attns, scales)]
    gas = [dy[:, at].astype(F32) * gain[:, at] for at in pairs]
    means = [head_mean(ga * normed) for ga, normed in zip(gas, normeds)]
    das = [
        (scale * (ga - normed * mean)).astype(BF16)
        for scale, ga, normed, mean in zip(scales, gas, normeds, means)
    ]
    states = [state_pair(q[:, at], da) for at, da in zip(pairs, das)]
    for at, normed, da in zip(pairs, normeds, das):
        dab[:, at] = da
        out[:, at] = (normed * gain[:, at]).astype(BF16)
        gsum[:, at] = jnp.sum(dy[:, at].astype(F32) * normed, axis=0, keepdims=True)

    @pl.when(step == 0)
    def _():
        for p, state in enumerate(states):
            keep[p * E:(p + 1) * E] = state

    @pl.when(step == 1)
    def _():
        for p, state in enumerate(states):
            send[p * E:(p + 1) * E] = state


def inner_kernel(core, q, k, v, dab, mask, mask_t, seg, table, pre_keep, pre_recv, nxt, *rest):
    gq, gk, gv, token = rest[-4:]
    step = pl.program_id(0)
    count = q.shape[1] // PAIR
    m, mt = mask[...], mask_t[...]
    token[...] = jnp.zeros_like(token)
    prefix = jnp.where(step == 0, pre_keep[...], pre_recv[...])
    on_next = on_rows(seg, table, True, nxt, count)
    for p in range(count):
        lanes = slice(p * PAIR, (p + 1) * PAIR)
        da = dab[:, lanes]
        kp, vp = k[:, lanes], v[:, lanes]
        far = dot(twice(da), stacked(rows_of(prefix, p), nxt[0, p * E:(p + 1) * E]), 1, 1)
        tq = far[:, :PAIR] + on_next * far[:, PAIR:]
        tk = tv = None
        for qh, kh, dh in zip(heads_of(q[:, lanes]), heads_of(kp), heads_of(da)):
            dprob = dot(dh, vp, 1, 1).astype(BF16) * m
            prob_t = dot(kp, qh, 1, 1).astype(BF16) * mt
            tq = tq + dot(dprob, kh, 1, 0)
            a = dot(dprob, qh, 0, 0)
            b = dot(prob_t, dh, 1, 0)
            tk = a if tk is None else tk + a
            tv = b if tv is None else tv + b
        gq[:, lanes] = tq.astype(BF16)
        gk[:, lanes] = tk
        gv[:, lanes] = tv


def outer_kernel(core, k, v, gk_in, gv_in, seg, table, suf_keep, suf_recv, prv, *rest):
    gk, gv = rest[-2:]
    step = pl.program_id(0)
    count = k.shape[1] // PAIR
    suffix = jnp.where(step == 0, suf_keep[...], suf_recv[...])
    on_prev = on_rows(seg, table, False, prv, count)
    for p in range(count):
        lanes = slice(p * PAIR, (p + 1) * PAIR)
        s = rows_of(suffix, p)
        g = prv[0, p * E:(p + 1) * E]
        far = dot(twice(v[:, lanes]), stacked(s, g), 1, 1)
        gk[:, lanes] = (gk_in[:, lanes] + far[:, :PAIR] + on_prev * far[:, PAIR:]).astype(BF16)
        far = dot(twice(k[:, lanes]), side_by_side(s, g), 1, 0)
        gv[:, lanes] = (gv_in[:, lanes] + far[:, :PAIR] + on_prev * far[:, PAIR:]).astype(BF16)


def partner(x, axis, bit):
    route = [(i, i ^ (1 << bit)) for i in range(lax.axis_size(axis))]
    return lax.ppermute(x, axis, route)


def shifted(x, distance):
    count = lax.axis_size("ctx")
    return lax.ppermute(x, "ctx", [(i, i + distance) for i in range(count) if 0 <= i + distance < count])


def chips_before(owns, towards, works):
    chips = lax.axis_size("ctx") // 2
    if chips > 8:
        for work in works:
            work(owns)
        totals = [shifted(own, 2 * towards) for own in owns]
        span = 1
        while span < chips:
            totals = [total + shifted(total, 2 * towards * span) for total in totals]
            span *= 2
        return totals
    befores = [None] * len(owns)
    for hop in range(max(chips - 1, len(works))):
        totals = [own if before is None else own + before for own, before in zip(owns, befores)]
        source = hop if towards == 1 else chips - 1 - hop
        token = works[hop](totals) if hop < len(works) else 0.0
        if hop < chips - 1:
            route = [(2 * source + c, 2 * (source + towards) + c) for c in range(2)]
            arrived = [lax.ppermute(total, "ctx", route) + token for total in totals]
            befores = [a if before is None else before + a for before, a in zip(befores, arrived)]
    return befores


def within_chip(keep, send):
    received = partner(send, "ctx", 0)
    return received, keep + received


def to_cores(before, keep, received, towards):
    is_source = lax.axis_index("ctx") & 1 == (0 if towards == 1 else 1)
    mine = jnp.where(is_source, before, before + received)
    return mine, partner(jnp.where(is_source, before + keep, before), "ctx", 0)


def scatter_sum(x):
    axes = ("dp", "ctx")
    devices = lax.axis_size("dp") * lax.axis_size("ctx")
    terms = lax.all_to_all(x.reshape(devices, -1), axes, 0, 0, tiled=True)
    return jnp.sum(terms, axis=0)


def on_device(queries, keys, values, out_grad, segment_ids, image_flags, gain):
    rows, width = queries.shape[1:]
    q, k, v, dy = (x[0] for x in (queries, keys, values, out_grad))
    seg = segment_ids[0]
    table = image_flags[0]
    gain_row = gain.reshape(1, width)
    core = (lax.axis_index("ctx") & 1).reshape(1).astype(jnp.int32)
    onehot = seg[:, None] == jnp.arange(table.shape[0], dtype=jnp.int32)[None, :]
    img = jnp.sum(jnp.where(onehot, table[None, :], 0), axis=1)
    imgseg = jnp.where(img == 1, seg, -1)
    pos = jnp.arange(rows)
    mask = ((pos[:, None] >= pos[None, :]) | (imgseg[:, None] == seg[None, :])).astype(BF16)
    mask_t = ((pos[:, None] <= pos[None, :]) | (seg[:, None] == imgseg[None, :])).astype(BF16)

    lanes = width // GROUPS // 2
    half_rows = lanes // PAIR * E
    heads = lanes // E

    def call(kernel, group, ins, outs, micros, after=(), alias=(), scratch=(), steps=(2,), prefetch=True):
        def at(i, c=None):
            return (i + c[0]) % 2 if prefetch else i

        def wide(*args):
            return (0, 2 * group + at(*args))

        def own(*args):
            return (0, at(*args))

        def whole(*args):
            return (0, 0)

        def part(*args):
            return (2 * group + at(*args), 0, 0)

        specs = {
            "wide": pl.BlockSpec((rows, lanes), wide),
            "block": pl.BlockSpec((rows, lanes), own),
            "row": pl.BlockSpec((1, lanes), wide),
            "rowblock": pl.BlockSpec((1, lanes), own),
            "half": pl.BlockSpec((half_rows, PAIR), whole),
            "part": pl.BlockSpec((1, half_rows + EXTRA, PAIR), part),
            "seg": pl.BlockSpec((1, rows), whole),
            "table": pl.BlockSpec((1, table.shape[0]), whole),
            "mask": pl.BlockSpec((rows, rows), whole),
            "token": pl.BlockSpec((8, PAIR), whole),
            "any": pl.BlockSpec(memory_space=pl.ANY),
            "hbm": pl.BlockSpec(memory_space=pltpu.HBM),
        }
        shapes = {
            "wide": (rows, width),
            "block": (rows, 2 * lanes),
            "rowblock": (1, 2 * lanes),
            "half": (half_rows, PAIR),
            "part": (2 * GROUPS, half_rows + EXTRA, PAIR),
            "token": (8, PAIR),
        }
        operands = [x for _, x in ins] + list(after)
        kinds = [kind for kind, _ in ins] + ["any"] * len(after)
        aliases = {}
        for out_at, x in alias:
            if x is not None:
                aliases[prefetch + len(operands)] = out_at
                operands.append(x)
                kinds.append("any")
        out_shape = [jax.ShapeDtypeStruct(shapes[kind], dtype) for kind, dtype in outs]
        moved = sum(rows * 2 * lanes * 2 for kind in kinds if kind in ("wide", "block"))
        moved += sum(rows * 2 * lanes * 2 for kind, _ in outs if kind in ("wide", "block"))
        return pl.pallas_call(
            kernel,
            grid_spec=pltpu.PrefetchScalarGridSpec(
                num_scalar_prefetch=int(prefetch),
                grid=steps,
                in_specs=[specs[kind] for kind in kinds],
                out_specs=[specs[kind] for kind, _ in outs],
                scratch_shapes=scratch,
            ),
            out_shape=out_shape,
            input_output_aliases=aliases,
            compiler_params=pltpu.CompilerParams(vmem_limit_bytes=VMEM),
            cost_estimate=pl.CostEstimate(flops=int(micros * 1.15e9), bytes_accessed=moved, transcendentals=0),
        )(*([core] if prefetch else []), *operands)

    edges = [("seg", segment_ids), ("table", image_flags)]
    groups = range(GROUPS)

    def phase(pieces, towards, works):
        befores = chips_before([own for _, _, own in pieces], towards, works)
        return [to_cores(before, keep, received, towards) for before, (keep, received, _) in zip(befores, pieces)]

    pieces = []
    buffers = [pltpu.VMEM((2, rows, lanes), BF16)] * 2 + [pltpu.SemaphoreType.DMA((2, 2))]
    for g in groups:
        keep, send = call(
            functools.partial(states_kernel, g), g, [("hbm", k), ("hbm", v)],
            [("half", F32), ("half", F32)], 1.2, scratch=buffers, steps=())
        pieces.append((keep, *within_chip(keep, send)))

    found = {}

    def early_work(g):
        def work(totals):
            if g == 0:
                found["nxt"], = call(
                    functools.partial(part_kernel, False), 0, [("wide", k), ("wide", v), *edges],
                    [("part", F32)], 2.0, after=totals, steps=(2 * GROUPS,), prefetch=False)
                totals = [found["nxt"]]
            found["local", g], token = call(
                local_kernel, g, [("wide", q), ("wide", k), ("wide", v), ("mask", mask)],
                [("block", F32), ("token", F32)], 2.3, after=totals)
            return token[:1, :1]
        return work

    prefix = phase(pieces, 1, [early_work(g) for g in groups])
    nxt = shifted(found["nxt"], -1)

    output = dab = grad_q = grad_k = grad_v = None
    pieces, gsums = [], []
    for g in groups:
        output, dab, gsum, keep, send = call(
            norm_kernel, g,
            [("wide", q), ("wide", dy), ("block", found["local", g]), ("row", gain_row), *edges,
             ("half", prefix[g][0]), ("half", prefix[g][1]), ("part", nxt)],
            [("wide", BF16), ("wide", BF16), ("rowblock", F32), ("half", F32), ("half", F32)],
            3.0, after=[own for _, _, own in pieces], alias=[(0, output), (1, dab)])
        gsums.append(gsum)
        pieces.append((keep, *within_chip(keep, send)))

    def late_work(g):
        def work(totals):
            if g == 0:
                found["prv"], = call(
                    functools.partial(part_kernel, True), 0, [("wide", q), ("wide", dab), *edges],
                    [("part", F32)], 2.0, after=totals, steps=(2 * GROUPS,), prefetch=False)
                totals = [found["prv"]]
            found["gq"], gk, gv, token = call(
                inner_kernel, g,
                [("wide", q), ("wide", k), ("wide", v), ("wide", dab), ("mask", mask), ("mask", mask_t), *edges,
                 ("half", prefix[g][0]), ("half", prefix[g][1]), ("part", nxt)],
                [("wide", BF16), ("block", F32), ("block", F32), ("token", F32)],
                5.5, after=totals, alias=[(0, found.get("gq"))])
            found["inner", g] = gk, gv
            return token[:1, :1]
        return work

    suffix = phase(pieces, -1, [late_work(g) for g in groups])
    prv = shifted(found["prv"], 1)
    grad_q = found["gq"]
    grad_gain = scatter_sum(jnp.concatenate(gsums, axis=1))
    for g in groups:
        gk, gv = found["inner", g]
        grad_k, grad_v = call(
            outer_kernel, g,
            [("wide", k), ("wide", v), ("block", gk), ("block", gv), *edges,
             ("half", suffix[g][0]), ("half", suffix[g][1]), ("part", prv)],
            [("wide", BF16), ("wide", BF16)],
            2.1, alias=[(0, grad_k), (1, grad_v)])
    return output[None], grad_q[None], grad_k[None], grad_v[None], grad_gain


def solution(mesh):
    return jax.shard_map(
        on_device,
        mesh=mesh,
        in_specs=(
            P("dp", "ctx", None),
            P("dp", "ctx", None),
            P("dp", "ctx", None),
            P("dp", "ctx", None),
            P("dp", "ctx"),
            P("dp", None),
            P(),
        ),
        out_specs=(
            P("dp", "ctx", None),
            P("dp", "ctx", None),
            P("dp", "ctx", None),
            P("dp", "ctx", None),
            P(("dp", "ctx")),
        ),
        check_vma=False,
    )
```

time: 112 us -> 104 us (0.929)
  local copies, waits for them, and re-layouts: 20 us -> 12 us
  starting transfers between devices: 38.4 us -> 30.7 us
  Pallas kernels: 28.6 us -> 34.8 us
  waiting for transfers between devices: 9.72 us -> 14.2 us
  other arithmetic: 12.8 us -> 10.5 us
    unnamed x72 -> x44, local copies, waits for them, and re-layouts: 18.5 us -> 9.2 us
    all_to_all x1, waiting for transfers between devices: 0.01 us -> 6.39 us  [scatter_sum(): terms = lax.all_to_all(x.reshape(devices, -1), axes, 0, 0, tiled=True)]
    pallas_call x10 -> x12, Pallas kernels: 28.6 us -> 34.8 us  [call(): pl.pallas_call(kernel, grid_spec=pltpu.PrefetchScalarGridSpec(num_scalar_...]
    ppermute x4 -> x2, starting transfers between devices: 8.29 us -> 3.11 us  [shifted(): lax.ppermute(x, 'ctx', [(i, i + distance) for i in range(count) if 0 <= i...]
    add x12, other arithmetic: 6.43 us -> 8.63 us  [the longest x8 8.57 us: chips_before(): own + before]
    slice x0 -> x4, local copies, waits for them, and re-layouts: none -> 2.17 us  [work(): return token[:1, :1]]
    ppermute x12, waiting for transfers between devices: 8.96 us -> 6.88 us  [chips_before(): arrived = [lax.ppermute(total, 'ctx', route) + token for total in totals]]
    select_n x4 -> x6, other arithmetic: 2.85 us -> 1.06 us  [the longest x4 1.04 us: to_cores(): jnp.where(is_source, before + keep, before)]
  transfers between devices with their start and end apart: 25 -> 23, of which waited for: 4 -> 4; matrix products, arithmetic and copies ran while one was open for 11% -> 10% of each run, Pallas kernels for 22% -> 27%
where the time goes in v3:
time: 104 us; the launch traced here: 103 us
  Pallas kernels  34.8 us (33%)
  starting transfers between devices  30.7 us (30%)
  waiting for transfers between devices  14.2 us (14%)
  local copies, waits for them, and re-layouts  12 us (12%)
  other arithmetic  10.5 us (10%)
  between operations  1.14 us (1%)
    pallas_call x12, Pallas kernels, call(): pl.pallas_call(kernel, grid_spec=pltpu.PrefetchScalarGridSpec(num_scalar_...  34.8 us
    ppermute x12, starting transfers between devices, chips_before(): arrived = [lax.ppermute(total, 'ctx', route) + token for total in totals]  14.7 us
    unnamed x44, local copies, waits for them, and re-layouts  9.2 us
    add x8, other arithmetic, chips_before(): own + before  8.57 us
    ppermute x12, waiting for transfers between devices, chips_before(): arrived = [lax.ppermute(total, 'ctx', route) + token for total in totals]  6.88 us
    all_to_all x1, starting transfers between devices, scatter_sum(): terms = lax.all_to_all(x.reshape(devices, -1), axes, 0, 0, tiled=True)  6.66 us
    all_to_all x1, waiting for transfers between devices, scatter_sum(): terms = lax.all_to_all(x.reshape(devices, -1), axes, 0, 0, tiled=True)  6.39 us
    ppermute x8, starting transfers between devices, partner(): return lax.ppermute(x, axis, route)  6.21 us
  transfers between devices with their start and end apart: 23, of which 4 were waited for; matrix products, arithmetic and copies ran while one was open for 10% of the time, Pallas kernels for 27%

profile of v3, /device:TPU:0, one launch (start us, length us, event | category | flops | bytes accessed | tf_op | source)
XLA Modules:
  0.0 103.3 jit_solution(7845662595512175779)
XLA Ops:
  6.1 4.9 %collective-permute-start.3 = (f32[256,128]{1,0:T(8,128)S(1)}, f32[256,128]{1,0:T(8,128)S(1)}, u32[]{:S(2)}, u32[]{:S(2)}) collective-permute-start(f32[256,128]{1,0:T(8,128)S(1)} %add.149.rest_1_), channel_id=1, source_target_pairs={{0,2},{1,3},{8,10},{9,11},{16,18},{17,19},{24,26},{25,27}} | collective-permute-start | bytes 393224 | tf_op jit(solution)/shard_map/ppermute | solution.py:260
  11.0 1.4 %collective-permute-start.1 = (f32[256,128]{1,0:T(8,128)S(1)}, f32[256,128]{1,0:T(8,128)S(1)}, u32[]{:S(2)}, u32[]{:S(2)}) collective-permute-start(f32[256,128]{1,0:T(8,128)S(1)} %add.148.rest_0_), channel_id=1, source_target_pairs={{0,2},{1,3},{8,10},{9,11},{16,18},{17,19},{24,26},{25,27}} | collective-permute-start | bytes 393224 | tf_op jit(solution)/shard_map/ppermute | solution.py:260
  12.5 2.6 %shard_map.112.rest_0_ = f32[4,264,128]{2,1,0:T(8,128)} custom-call(bf16[256,2048]{1,0:T(8,128)(2,1)S(1)} %bitcast.33, bf16[256,2048]{1,0:T(8,128)(2,1)S(1)} %bitcast.42, s32[1,256]{1,0:T(1,128)S(1)} %copy-done, s32[1,32]{1,0:T(1,128)S(1)} %copy-done.1, f32[256,128]{1,0:T(8,128)S(1)} %add.148.rest_0_, f32[256,128]{1,0:T(8,128)S(1)} %add.149.rest_1_), custom_call_target="tpu_custom_call" | custom-call | flops 2300000000 | bytes 1048576 | tf_op jit(solution)/shard_map/pallas_call | solution.py:350
  15.1 2.3 %shard_map.113 = (f32[256,1024]{1,0:T(8,128)S(1)}, f32[8,128]{1,0:T(8,128)S(1)}) custom-call(s32[1]{0:T(128)} %bitcast.core, bf16[256,2048]{1,0:T(8,128)(2,1)S(1)} %bitcast.24, bf16[256,2048]{1,0:T(8,128)(2,1)S(1)} %bitcast.34, bf16[256,2048]{1,0:T(8,128)(2,1)S(1)} %bitcast.43, bf16[256,256]{1,0:T(8,128)(2,1)S(1)} %get-tuple-element.84.mask, ...), custom_call_target="tpu_custom_call" | custom-call | flops 2644999936 | bytes 2097152 | tf_op jit(solution)/shard_map/pallas_call | solution.py:350
  21.0 2.4 %shard_map.114 = (f32[256,1024]{1,0:T(8,128)S(1)}, f32[8,128]{1,0:T(8,128)S(1)}) custom-call(s32[1]{0:T(128)} %bitcast.core, bf16[256,2048]{1,0:T(8,128)(2,1)S(1)} %bitcast.25, bf16[256,2048]{1,0:T(8,128)(2,1)S(1)} %bitcast.35, bf16[256,2048]{1,0:T(8,128)(2,1)S(1)} %bitcast.44, bf16[256,256]{1,0:T(8,128)(2,1)S(1)} %get-tuple-element.84.mask, ...), custom_call_target="tpu_custom_call" | custom-call | flops 2644999936 | bytes 2097152 | tf_op jit(solution)/shard_map/pallas_call | solution.py:350
  24.9 2.0 %fusion.6 = (f32[256,128]{1,0:T(8,128)}, f32[256,128]{1,0:T(8,128)S(1)}) fusion(f32[256,128]{1,0:T(8,128)S(1)} %add.148.rest_0_, f32[256,128]{1,0:T(8,128)S(1)} %collective-permute-done.8, f32[]{:T(128)} %bitcast.9, f32[256,128]{1,0:T(8,128)S(1)} %collective-permute-done.1, f32[]{:T(128)} %bitcast.7), kind=kLoop, calls=%fused_computation.30 | loop fusion | flops 131072 | bytes 655368 | tf_op jit(solution)/shard_map/add | solution.py:255
  27.6 1.3 %collective-permute-start.7 = (f32[4,264,128]{2,1,0:T(8,128)}, f32[4,264,128]{2,1,0:T(8,128)}, u32[]{:S(2)}, u32[]{:S(2)}) collective-permute-start(f32[4,264,128]{2,1,0:T(8,128)} %shard_map.112.rest_0_), channel_id=1, source_target_pairs={{1,0},{2,1},{3,2},{4,3},{5,4},{6,5},{7,6},{9,8},{10,9},{11,10},{12... | collective-permute-start | bytes 1622024 | tf_op jit(solution)/shard_map/ppermute | solution.py:239
  32.6 1.3 %fusion.7 = (f32[256,128]{1,0:T(8,128)S(1)}, f32[256,128]{1,0:T(8,128)S(1)}) fusion(f32[256,128]{1,0:T(8,128)S(1)} %add.149.rest_1_, f32[256,128]{1,0:T(8,128)S(1)} %collective-permute-done.4, f32[]{:T(128)} %bitcast.9, f32[256,128]{1,0:T(8,128)S(1)} %collective-permute-done.3, f32[]{:T(128)} %bitcast.7), kind=kLoop, calls=%fused_computation.31 | loop fusion | flops 131072 | bytes 655368 | tf_op jit(solution)/shard_map/add | solution.py:255
  34.6 3.7 %shard_map.115 = (bf16[256,2048]{1,0:T(8,128)(2,1)}, bf16[256,2048]{1,0:T(8,128)(2,1)S(1)}, f32[1,1024]{1,0:T(1,128)S(1)}, f32[256,128]{1,0:T(8,128)S(1)}, f32[256,128]{1,0:T(8,128)S(1)}) custom-call(s32[1]{0:T(128)} %bitcast.core, bf16[256,2048]{1,0:T(8,128)(2,1)S(1)} %bitcast.26, bf16[256,2048]{1,0:T(8,128)(2,1)S(1)} %bitcast.22, ...), custom_call_target="tpu_custom_call" | custom-call | flops 3449999872 | bytes 2621440 | tf_op jit(solution)/shard_map/pallas_call | solution.py:350
  38.3 3.8 %collective-permute-start.11 = (f32[256,128]{1,0:T(8,128)S(1)}, f32[256,128]{1,0:T(8,128)S(1)}, u32[]{:S(2)}, u32[]{:S(2)}) collective-permute-start(f32[256,128]{1,0:T(8,128)S(1)} %get-tuple-element.44), channel_id=1, source_target_pairs={{0,1},{1,0},{2,3},{3,2},{4,5},{5,4},{6,7},{7,6},{8,9},{9,8},{10,11... | collective-permute-start | bytes 393224 | tf_op jit(solution)/shard_map/ppermute | solution.py:234
  43.7 3.6 %shard_map.116 = (bf16[256,2048]{1,0:T(8,128)(2,1)}, bf16[256,2048]{1,0:T(8,128)(2,1)S(1)}, f32[1,1024]{1,0:T(1,128)S(1)}, f32[256,128]{1,0:T(8,128)S(1)}, f32[256,128]{1,0:T(8,128)S(1)}) custom-call(s32[1]{0:T(128)} %bitcast.core, bf16[256,2048]{1,0:T(8,128)(2,1)S(1)} %bitcast.27, ...), custom_call_target="tpu_custom_call", output_to_operand_aliasing={{0}: (11, {}), {1}: (12, {})} | custom-call | flops 3449999872 | bytes 2621440 | tf_op jit(solution)/shard_map/pallas_call | solution.py:350
  49.4 6.7 %all-to-all-start = ((f32[32,1,64]{2,1,0:T(1,128)}), f32[32,1,64]{2,1,0:T(1,128)S(1)}, u32[]{:S(2)}, u32[]{:S(2)}) async-start(f32[32,1,64]{2,1,0:T(1,128)} %bitcast.17), calls=%async_computation | async-start | bytes 32768 | tf_op jit(solution)/shard_map/all_to_all | solution.py:279
  56.7 6.4 %all-to-all-done = f32[32,1,64]{2,1,0:T(1,128)S(1)} async-done(((f32[32,1,64]{2,1,0:T(1,128)}), f32[32,1,64]{2,1,0:T(1,128)S(1)}, u32[]{:S(2)}, u32[]{:S(2)}) %all-to-all-start) | async-done | bytes 8224 | tf_op jit(solution)/shard_map/all_to_all | solution.py:279
  66.2 1.8 %shard_map.117.rest_0_ = f32[4,264,128]{2,1,0:T(8,128)S(1)} custom-call(bf16[256,2048]{1,0:T(8,128)(2,1)S(1)} %bitcast.28, bf16[256,2048]{1,0:T(8,128)(2,1)S(1)} %copy-done.11, s32[1,256]{1,0:T(1,128)S(1)} %copy-done, s32[1,32]{1,0:T(1,128)S(1)} %copy-done.1, f32[256,128]{1,0:T(8,128)S(1)} %add.170.rest_0_, f32[256,128]{1,0:T(8,128)S(1)} %add.171.rest_1_), custom_call_target="tpu_custom_call" | custom-call | flops 2300000000 | bytes 1048576 | tf_op jit(solution)/shard_map/pallas_call | solution.py:350
  68.0 1.8 %collective-permute-start.18 = (f32[4,264,128]{2,1,0:T(8,128)S(1)}, f32[4,264,128]{2,1,0:T(8,128)S(1)}, u32[]{:S(2)}, u32[]{:S(2)}) collective-permute-start(f32[4,264,128]{2,1,0:T(8,128)S(1)} %shard_map.117.rest_0_), channel_id=1, source_target_pairs={{0,1},{1,2},{2,3},{3,4},{4,5},{5,6},{6,7},{8,9},{9,10},{10,11},{11... | collective-permute-start | bytes 1622024 | tf_op jit(solution)/shard_map/ppermute | solution.py:239
  69.9 6.4 %shard_map.118 = (bf16[256,2048]{1,0:T(8,128)(2,1)}, f32[256,1024]{1,0:T(8,128)S(1)}, f32[256,1024]{1,0:T(8,128)S(1)}, f32[8,128]{1,0:T(8,128)S(1)}) custom-call(s32[1]{0:T(128)} %bitcast.core, bf16[256,2048]{1,0:T(8,128)(2,1)S(1)} %bitcast.29, bf16[256,2048]{1,0:T(8,128)(2,1)S(1)} %bitcast.36, bf16[256,2048]{1,0:T(8,128)(2,1)S(1)} %bitcast.45, ...), custom_call_target="tpu_custom_call" | custom-call | flops 6325000192 | bytes 3670016 | tf_op jit(solution)/shard_map/pallas_call | solution.py:350
  79.7 6.4 %shard_map.119 = (bf16[256,2048]{1,0:T(8,128)(2,1)}, f32[256,1024]{1,0:T(8,128)S(1)}, f32[256,1024]{1,0:T(8,128)S(1)}, f32[8,128]{1,0:T(8,128)S(1)}) custom-call(s32[1]{0:T(128)} %bitcast.core, bf16[256,2048]{1,0:T(8,128)(2,1)S(1)} %bitcast.30, bf16[256,2048]{1,0:T(8,128)(2,1)S(1)} %bitcast.37, ...), custom_call_target="tpu_custom_call", output_to_operand_aliasing={{0}: (14, {})} | custom-call | flops 6325000192 | bytes 3670016 | tf_op jit(solution)/shard_map/pallas_call | solution.py:350
  86.7 1.3 %fusion.4 = (f32[256,128]{1,0:T(8,128)S(1)}, f32[256,128]{1,0:T(8,128)S(1)}) fusion(f32[256,128]{1,0:T(8,128)S(1)} %add.170.rest_0_, f32[256,128]{1,0:T(8,128)S(1)} %collective-permute-done.19, f32[]{:T(128)} %bitcast.14, f32[256,128]{1,0:T(8,128)S(1)} %collective-permute-done.12, f32[]{:T(128)} %bitcast.12), kind=kLoop, calls=%fused_computation.28 | loop fusion | flops 131072 | bytes 655368 | tf_op jit(solution)/shard_map/add | solution.py:255
  88.0 1.4 %collective-permute-start.20 = (f32[256,128]{1,0:T(8,128)S(1)}, f32[256,128]{1,0:T(8,128)S(1)}, u32[]{:S(2)}, u32[]{:S(2)}) collective-permute-start(f32[256,128]{1,0:T(8,128)S(1)} %get-tuple-element.65), channel_id=1, source_target_pairs={{2,0},{3,1},{10,8},{11,9},{18,16},{19,17},{26,24},{27,25}} | collective-permute-start | bytes 393224 | tf_op jit(solution)/shard_map/ppermute | solution.py:260
  89.4 1.3 %fusion.5 = (f32[256,128]{1,0:T(8,128)S(1)}, f32[256,128]{1,0:T(8,128)S(1)}) fusion(f32[256,128]{1,0:T(8,128)S(1)} %add.171.rest_1_, f32[256,128]{1,0:T(8,128)S(1)} %collective-permute-done.15, f32[]{:T(128)} %bitcast.14, f32[256,128]{1,0:T(8,128)S(1)} %collective-permute-done.14, f32[]{:T(128)} %bitcast.12), kind=kLoop, calls=%fused_computation.29 | loop fusion | flops 131072 | bytes 655368 | tf_op jit(solution)/shard_map/add | solution.py:255
  92.0 4.4 %collective-permute-done.20 = f32[256,128]{1,0:T(8,128)S(1)} collective-permute-done((f32[256,128]{1,0:T(8,128)S(1)}, f32[256,128]{1,0:T(8,128)S(1)}, u32[]{:S(2)}, u32[]{:S(2)}) %collective-permute-start.20) | collective-permute-done | bytes 131104 | tf_op jit(solution)/shard_map/ppermute | solution.py:260
  96.5 2.5 %collective-permute-done.16 = f32[256,128]{1,0:T(8,128)S(1)} collective-permute-done((f32[256,128]{1,0:T(8,128)S(1)}, f32[256,128]{1,0:T(8,128)S(1)}, u32[]{:S(2)}, u32[]{:S(2)}) %collective-permute-start.16) | collective-permute-done | bytes 131104 | tf_op jit(solution)/shard_map/ppermute | solution.py:260
  99.1 2.1 %shard_map.120 = (bf16[256,2048]{1,0:T(8,128)(2,1)}, bf16[256,2048]{1,0:T(8,128)(2,1)}) custom-call(s32[1]{0:T(128)} %bitcast.core, bf16[256,2048]{1,0:T(8,128)(2,1)S(1)} %bitcast.38, bf16[256,2048]{1,0:T(8,128)(2,1)S(1)} %bitcast.47, f32[256,1024]{1,0:T(8,128)S(1)} %get-tuple-element.57.gk_in, f32[256,1024]{1,0:T(8,128)S(1)} %get-tuple-element.58.gv_in, ...), custom_call_target="tpu_custom_call" | custom-call | flops 2415000064 | bytes 3145728 | tf_op jit(solution)/shard_map/pallas_call | solution.py:350
  101.3 2.1 %shard_map.121 = (bf16[256,2048]{1,0:T(8,128)(2,1)}, bf16[256,2048]{1,0:T(8,128)(2,1)}) custom-call(s32[1]{0:T(128)} %bitcast.core, bf16[256,2048]{1,0:T(8,128)(2,1)S(1)} %bitcast.39, bf16[256,2048]{1,0:T(8,128)(2,1)S(1)} %bitcast.48, f32[256,1024]{1,0:T(8,128)S(1)} %get-tuple-element.54.gk_in, ...), custom_call_target="tpu_custom_call", output_to_operand_aliasing={{0}: (10, {}), {1}: (11, {})} | custom-call | flops 2415000064 | bytes 3145728 | tf_op jit(solution)/shard_map/pallas_call | solution.py:350
  (105 shorter events, 28.2 us)
Async XLA Ops:
  3.8 2.3 %collective-permute-start.2 = (f32[256,128]{1,0:T(8,128)S(1)}, f32[256,128]{1,0:T(8,128)S(1)}, u32[]{:S(2)}, u32[]{:S(2)}) collective-permute-start(f32[256,128]{1,0:T(8,128)S(1)} %get-tuple-element.38), channel_id=1, source_target_pairs={{0,1},{1,0},{2,3},{3,2},{4,5},{5,4},{6,7},{7,6},{8,9},{9,8},{10,11... | collective-permute-start | bytes 393224 | tf_op jit(solution)/shard_map/ppermute | solution.py:234
  5.0 6.0 %collective-permute-start = (f32[256,128]{1,0:T(8,128)S(1)}, f32[256,128]{1,0:T(8,128)S(1)}, u32[]{:S(2)}, u32[]{:S(2)}) collective-permute-start(f32[256,128]{1,0:T(8,128)S(1)} %get-tuple-element.36), channel_id=1, source_target_pairs={{0,1},{1,0},{2,3},{3,2},{4,5},{5,4},{6,7},{7,6},{8,9},{9,8},{10,11... | collective-permute-start | bytes 393224 | tf_op jit(solution)/shard_map/ppermute | solution.py:234
  6.1 14.2 %collective-permute-start.3 = (f32[256,128]{1,0:T(8,128)S(1)}, f32[256,128]{1,0:T(8,128)S(1)}, u32[]{:S(2)}, u32[]{:S(2)}) collective-permute-start(f32[256,128]{1,0:T(8,128)S(1)} %add.149.rest_1_), channel_id=1, source_target_pairs={{0,2},{1,3},{8,10},{9,11},{16,18},{17,19},{24,26},{25,27}} | collective-permute-start | bytes 393224 | tf_op jit(solution)/shard_map/ppermute | solution.py:260
  11.0 7.9 %collective-permute-start.1 = (f32[256,128]{1,0:T(8,128)S(1)}, f32[256,128]{1,0:T(8,128)S(1)}, u32[]{:S(2)}, u32[]{:S(2)}) collective-permute-start(f32[256,128]{1,0:T(8,128)S(1)} %add.148.rest_0_), channel_id=1, source_target_pairs={{0,2},{1,3},{8,10},{9,11},{16,18},{17,19},{24,26},{25,27}} | collective-permute-start | bytes 393224 | tf_op jit(solution)/shard_map/ppermute | solution.py:260
  19.6 5.3 %collective-permute-start.8 = (f32[256,128]{1,0:T(8,128)S(1)}, f32[256,128]{1,0:T(8,128)S(1)}, u32[]{:S(2)}, u32[]{:S(2)}) collective-permute-start(f32[256,128]{1,0:T(8,128)S(1)} %add_add_fusion.7.rest_0_), channel_id=1, source_target_pairs={{2,4},{3,5},{10,12},{11,13},{18,20},{19,21},{26,28},{27,29}} | collective-permute-start | bytes 393224 | tf_op jit(solution)/shard_map/ppermute | solution.py:260
  24.9 9.7 %copy-start.2 = (bf16[1,256,2048]{2,1,0:T(8,128)(2,1)S(1)}, bf16[1,256,2048]{2,1,0:T(8,128)(2,1)}, u32[]{:S(2)}) copy-start(bf16[1,256,2048]{2,1,0:T(8,128)(2,1)} %param.10) | copy-start | bytes 3145732
  26.9 2.8 %collective-permute-start.9 = (f32[256,128]{1,0:T(8,128)}, f32[256,128]{1,0:T(8,128)S(1)}, u32[]{:S(2)}, u32[]{:S(2)}) collective-permute-start(f32[256,128]{1,0:T(8,128)} %get-tuple-element.69), channel_id=1, source_target_pairs={{4,6},{5,7},{12,14},{13,15},{20,22},{21,23},{28,30},{29,31}} | collective-permute-start | bytes 393224 | tf_op jit(solution)/shard_map/ppermute | solution.py:260
  27.6 6.9 %collective-permute-start.7 = (f32[4,264,128]{2,1,0:T(8,128)}, f32[4,264,128]{2,1,0:T(8,128)}, u32[]{:S(2)}, u32[]{:S(2)}) collective-permute-start(f32[4,264,128]{2,1,0:T(8,128)} %shard_map.112.rest_0_), channel_id=1, source_target_pairs={{1,0},{2,1},{3,2},{4,3},{5,4},{6,5},{7,6},{9,8},{10,9},{11,10},{12... | collective-permute-start | bytes 1622024 | tf_op jit(solution)/shard_map/ppermute | solution.py:239
  28.9 3.6 %collective-permute-start.4 = (f32[256,128]{1,0:T(8,128)S(1)}, f32[256,128]{1,0:T(8,128)S(1)}, u32[]{:S(2)}, u32[]{:S(2)}) collective-permute-start(f32[256,128]{1,0:T(8,128)S(1)} %add_add_fusion.6.rest_1_), channel_id=1, source_target_pairs={{2,4},{3,5},{10,12},{11,13},{18,20},{19,21},{26,28},{27,29}} | collective-permute-start | bytes 393224 | tf_op jit(solution)/shard_map/ppermute | solution.py:260
  31.4 3.2 %collective-permute-start.10 = (f32[256,128]{1,0:T(8,128)S(1)}, f32[256,128]{1,0:T(8,128)S(1)}, u32[]{:S(2)}, u32[]{:S(2)}) collective-permute-start(f32[256,128]{1,0:T(8,128)S(1)} %get-tuple-element.79), channel_id=1, source_target_pairs={{0,1},{1,0},{2,3},{3,2},{4,5},{5,4},{6,7},{7,6},{8,9},{9,8},{10,11... | collective-permute-start | bytes 393224 | tf_op jit(solution)/shard_map/ppermute | solution.py:234
  33.9 8.2 %collective-permute-start.5 = (f32[256,128]{1,0:T(8,128)S(1)}, f32[256,128]{1,0:T(8,128)S(1)}, u32[]{:S(2)}, u32[]{:S(2)}) collective-permute-start(f32[256,128]{1,0:T(8,128)S(1)} %get-tuple-element.71), channel_id=1, source_target_pairs={{4,6},{5,7},{12,14},{13,15},{20,22},{21,23},{28,30},{29,31}} | collective-permute-start | bytes 393224 | tf_op jit(solution)/shard_map/ppermute | solution.py:260
  38.3 4.8 %collective-permute-start.11 = (f32[256,128]{1,0:T(8,128)S(1)}, f32[256,128]{1,0:T(8,128)S(1)}, u32[]{:S(2)}, u32[]{:S(2)}) collective-permute-start(f32[256,128]{1,0:T(8,128)S(1)} %get-tuple-element.44), channel_id=1, source_target_pairs={{0,1},{1,0},{2,3},{3,2},{4,5},{5,4},{6,7},{7,6},{8,9},{9,8},{10,11... | collective-permute-start | bytes 393224 | tf_op jit(solution)/shard_map/ppermute | solution.py:234
  42.1 1.6 %collective-permute-start.6 = (f32[256,128]{1,0:T(8,128)S(1)}, f32[256,128]{1,0:T(8,128)S(1)}, u32[]{:S(2)}, u32[]{:S(2)}) collective-permute-start(f32[256,128]{1,0:T(8,128)S(1)} %get-tuple-element.81), channel_id=1, source_target_pairs={{0,1},{1,0},{2,3},{3,2},{4,5},{5,4},{6,7},{7,6},{8,9},{9,8},{10,11... | collective-permute-start | bytes 393224 | tf_op jit(solution)/shard_map/ppermute | solution.py:234
  48.3 15.4 %collective-permute-start.13 = (f32[256,128]{1,0:T(8,128)S(1)}, f32[256,128]{1,0:T(8,128)S(1)}, u32[]{:S(2)}, u32[]{:S(2)}) collective-permute-start(f32[256,128]{1,0:T(8,128)S(1)} %get-tuple-element.50), channel_id=1, source_target_pairs={{0,1},{1,0},{2,3},{3,2},{4,5},{5,4},{6,7},{7,6},{8,9},{9,8},{10,11... | collective-permute-start | bytes 393224 | tf_op jit(solution)/shard_map/ppermute | solution.py:234
  49.4 13.7 %all-to-all-start = ((f32[32,1,64]{2,1,0:T(1,128)}), f32[32,1,64]{2,1,0:T(1,128)S(1)}, u32[]{:S(2)}, u32[]{:S(2)}) async-start(f32[32,1,64]{2,1,0:T(1,128)} %bitcast.17), calls=%async_computation | async-start | bytes 32768 | tf_op jit(solution)/shard_map/all_to_all | solution.py:279
  56.0 20.8 %collective-permute-start.12 = (f32[256,128]{1,0:T(8,128)S(1)}, f32[256,128]{1,0:T(8,128)S(1)}, u32[]{:S(2)}, u32[]{:S(2)}) collective-permute-start(f32[256,128]{1,0:T(8,128)S(1)} %add.170.rest_0_), channel_id=1, source_target_pairs={{6,4},{7,5},{14,12},{15,13},{22,20},{23,21},{30,28},{31,29}} | collective-permute-start | bytes 393224 | tf_op jit(solution)/shard_map/ppermute | solution.py:260
  64.3 13.8 %collective-permute-start.14 = (f32[256,128]{1,0:T(8,128)S(1)}, f32[256,128]{1,0:T(8,128)S(1)}, u32[]{:S(2)}, u32[]{:S(2)}) collective-permute-start(f32[256,128]{1,0:T(8,128)S(1)} %add.171.rest_1_), channel_id=1, source_target_pairs={{6,4},{7,5},{14,12},{15,13},{22,20},{23,21},{30,28},{31,29}} | collective-permute-start | bytes 393224 | tf_op jit(solution)/shard_map/ppermute | solution.py:260
  68.0 31.1 %collective-permute-start.18 = (f32[4,264,128]{2,1,0:T(8,128)S(1)}, f32[4,264,128]{2,1,0:T(8,128)S(1)}, u32[]{:S(2)}, u32[]{:S(2)}) collective-permute-start(f32[4,264,128]{2,1,0:T(8,128)S(1)} %shard_map.117.rest_0_), channel_id=1, source_target_pairs={{0,1},{1,2},{2,3},{3,4},{4,5},{5,6},{6,7},{8,9},{9,10},{10,11},{11... | collective-permute-start | bytes 1622024 | tf_op jit(solution)/shard_map/ppermute | solution.py:239
  77.5 9.2 %collective-permute-start.19 = (f32[256,128]{1,0:T(8,128)S(1)}, f32[256,128]{1,0:T(8,128)S(1)}, u32[]{:S(2)}, u32[]{:S(2)}) collective-permute-start(f32[256,128]{1,0:T(8,128)S(1)} %add_add_fusion.5.rest_0_), channel_id=1, source_target_pairs={{4,2},{5,3},{12,10},{13,11},{20,18},{21,19},{28,26},{29,27}} | collective-permute-start | bytes 393224 | tf_op jit(solution)/shard_map/ppermute | solution.py:260
  78.8 10.6 %collective-permute-start.15 = (f32[256,128]{1,0:T(8,128)S(1)}, f32[256,128]{1,0:T(8,128)S(1)}, u32[]{:S(2)}, u32[]{:S(2)}) collective-permute-start(f32[256,128]{1,0:T(8,128)S(1)} %add_add_fusion.4.rest_1_), channel_id=1, source_target_pairs={{4,2},{5,3},{12,10},{13,11},{20,18},{21,19},{28,26},{29,27}} | collective-permute-start | bytes 393224 | tf_op jit(solution)/shard_map/ppermute | solution.py:260
  88.0 8.4 %collective-permute-start.20 = (f32[256,128]{1,0:T(8,128)S(1)}, f32[256,128]{1,0:T(8,128)S(1)}, u32[]{:S(2)}, u32[]{:S(2)}) collective-permute-start(f32[256,128]{1,0:T(8,128)S(1)} %get-tuple-element.65), channel_id=1, source_target_pairs={{2,0},{3,1},{10,8},{11,9},{18,16},{19,17},{26,24},{27,25}} | collective-permute-start | bytes 393224 | tf_op jit(solution)/shard_map/ppermute | solution.py:260
  90.7 8.3 %collective-permute-start.16 = (f32[256,128]{1,0:T(8,128)S(1)}, f32[256,128]{1,0:T(8,128)S(1)}, u32[]{:S(2)}, u32[]{:S(2)}) collective-permute-start(f32[256,128]{1,0:T(8,128)S(1)} %get-tuple-element.67), channel_id=1, source_target_pairs={{2,0},{3,1},{10,8},{11,9},{18,16},{19,17},{26,24},{27,25}} | collective-permute-start | bytes 393224 | tf_op jit(solution)/shard_map/ppermute | solution.py:260
  96.4 2.7 %collective-permute-start.21 = (f32[256,128]{1,0:T(8,128)S(1)}, f32[256,128]{1,0:T(8,128)S(1)}, u32[]{:S(2)}, u32[]{:S(2)}) collective-permute-start(f32[256,128]{1,0:T(8,128)S(1)} %get-tuple-element.75), channel_id=1, source_target_pairs={{0,1},{1,0},{2,3},{3,2},{4,5},{5,4},{6,7},{7,6},{8,9},{9,8},{10,11... | collective-permute-start | bytes 393224 | tf_op jit(solution)/shard_map/ppermute | solution.py:234
  99.0 2.2 %collective-permute-start.17 = (f32[256,128]{1,0:T(8,128)S(1)}, f32[256,128]{1,0:T(8,128)S(1)}, u32[]{:S(2)}, u32[]{:S(2)}) collective-permute-start(f32[256,128]{1,0:T(8,128)S(1)} %get-tuple-element.77), channel_id=1, source_target_pairs={{0,1},{1,0},{2,3},{3,2},{4,5},{5,4},{6,7},{7,6},{8,9},{9,8},{10,11... | collective-permute-start | bytes 393224 | tf_op jit(solution)/shard_map/ppermute | solution.py:234
  (21 other events, 55.9 us)

commit v4 on v3

--- a/solution.py
+++ b/solution.py
@@ -254,7 +254,7 @@
     for hop in range(max(chips - 1, len(works))):
         totals = [own if before is None else own + before for own, before in zip(owns, befores)]
         source = hop if towards == 1 else chips - 1 - hop
-        token = works[hop](totals) if hop < len(works) else 0.0
+        token = works[hop](totals) if hop < len(works) else jnp.zeros((1, PAIR), F32)
         if hop < chips - 1:
             route = [(2 * source + c, 2 * (source + towards) + c) for c in range(2)]
             arrived = [lax.ppermute(total, "ctx", route) + token for total in totals]
@@ -273,11 +273,16 @@
     return mine, partner(jnp.where(is_source, before + keep, before), "ctx", 0)
 
 
+def in_hbm(x):
+    return pltpu.with_memory_space_constraint(x, pltpu.HBM)
+
+
 def scatter_sum(x):
     axes = ("dp", "ctx")
-    devices = lax.axis_size("dp") * lax.axis_size("ctx")
-    terms = lax.all_to_all(x.reshape(devices, -1), axes, 0, 0, tiled=True)
-    return jnp.sum(terms, axis=0)
+    terms = lax.all_gather(x[0], axes)
+    count = x.shape[1] // terms.shape[0]
+    own = lax.dynamic_slice_in_dim(terms, lax.axis_index(axes) * count, count, 1)
+    return jnp.sum(own, axis=0)
 
 
 def on_device(queries, keys, values, out_grad, segment_ids, image_flags, gain):
@@ -324,7 +329,9 @@
             "seg": pl.BlockSpec((1, rows), whole),
             "table": pl.BlockSpec((1, table.shape[0]), whole),
             "mask": pl.BlockSpec((rows, rows), whole),
-            "token": pl.BlockSpec((8, PAIR), whole),
+            "token": pl.BlockSpec((1, PAIR), whole),
+            "after2": pl.BlockSpec((8, PAIR), whole),
+            "after3": pl.BlockSpec((1, 8, PAIR), lambda *args: (0, 0, 0)),
             "any": pl.BlockSpec(memory_space=pl.ANY),
             "hbm": pl.BlockSpec(memory_space=pltpu.HBM),
         }
@@ -334,17 +341,20 @@
             "rowblock": (1, 2 * lanes),
             "half": (half_rows, PAIR),
             "part": (2 * GROUPS, half_rows + EXTRA, PAIR),
-            "token": (8, PAIR),
+            "token": (1, PAIR),
         }
         operands = [x for _, x in ins] + list(after)
-        kinds = [kind for kind, _ in ins] + ["any"] * len(after)
+        kinds = [kind for kind, _ in ins] + [f"after{x.ndim}" for x in after]
         aliases = {}
         for out_at, x in alias:
             if x is not None:
                 aliases[prefetch + len(operands)] = out_at
                 operands.append(x)
                 kinds.append("any")
-        out_shape = [jax.ShapeDtypeStruct(shapes[kind], dtype) for kind, dtype in outs]
+        out_shape = [
+            pltpu.HBM(shapes[kind], dtype) if kind in ("block", "wide") else jax.ShapeDtypeStruct(shapes[kind], dtype)
+            for kind, dtype in outs
+        ]
         moved = sum(rows * 2 * lanes * 2 for kind in kinds if kind in ("wide", "block"))
         moved += sum(rows * 2 * lanes * 2 for kind, _ in outs if kind in ("wide", "block"))
         return pl.pallas_call(
@@ -373,7 +383,7 @@
     buffers = [pltpu.VMEM((2, rows, lanes), BF16)] * 2 + [pltpu.SemaphoreType.DMA((2, 2))]
     for g in groups:
         keep, send = call(
-            functools.partial(states_kernel, g), g, [("hbm", k), ("hbm", v)],
+            functools.partial(states_kernel, g), g, [("hbm", in_hbm(k)), ("hbm", in_hbm(v))],
             [("half", F32), ("half", F32)], 1.2, scratch=buffers, steps=())
         pieces.append((keep, *within_chip(keep, send)))
 
@@ -389,7 +399,7 @@
             found["local", g], token = call(
                 local_kernel, g, [("wide", q), ("wide", k), ("wide", v), ("mask", mask)],
                 [("block", F32), ("token", F32)], 2.3, after=totals)
-            return token[:1, :1]
+            return token
         return work
 
     prefix = phase(pieces, 1, [early_work(g) for g in groups])
@@ -421,7 +431,7 @@
                 [("wide", BF16), ("block", F32), ("block", F32), ("token", F32)],
                 5.5, after=totals, alias=[(0, found.get("gq"))])
             found["inner", g] = gk, gv
-            return token[:1, :1]
+            return token
         return work
 
     suffix = phase(pieces, -1, [late_work(g) for g in groups])

time: 104 us -> 130 us (1.25)
  blocking collectives: 0 us -> 53.7 us
  starting transfers between devices: 30.7 us -> 20.8 us
  other arithmetic: 10.5 us -> 2.01 us
  local copies, waits for them, and re-layouts: 12 us -> 3.86 us
  waiting for transfers between devices: 14.2 us -> 8.08 us
  Pallas kernels: 34.8 us -> 39.4 us
    all_gather x0 -> x1, blocking collectives: none -> 53.7 us  [scatter_sum(): terms = lax.all_gather(x[0], axes)]
    add x8 -> x4, other arithmetic: 8.57 us -> 0.93 us  [chips_before(): own + before]
    all_to_all x1 -> x0, starting transfers between devices: 6.66 us -> none  [scatter_sum(): terms = lax.all_to_all(x.reshape(devices, -1), axes, 0, 0, tiled=True)]
    all_to_all x1 -> x0, waiting for transfers between devices: 6.39 us -> none  [scatter_sum(): terms = lax.all_to_all(x.reshape(devices, -1), axes, 0, 0, tiled=True)]
    unnamed x44 -> x40, local copies, waits for them, and re-layouts: 9.2 us -> 3.86 us
    pallas_call x12, Pallas kernels: 34.8 us -> 39.4 us  [call(): pl.pallas_call(kernel, grid_spec=pltpu.PrefetchScalarGridSpec(num_scalar_...]
    ppermute x8, starting transfers between devices: 6.21 us -> 3.04 us  [partner(): return lax.ppermute(x, axis, route)]
    slice x4 -> x0, local copies, waits for them, and re-layouts: 2.17 us -> none  [work(): return token[:1, :1]]
  transfers between devices with their start and end apart: 23 -> 22, of which waited for: 4 -> 5; matrix products, arithmetic and copies ran while one was open for 10% -> 1% of each run, Pallas kernels for 27% -> 25%
where the time goes in v4:
time: 130 us; the launch traced here: 129 us
  blocking collectives  53.7 us (41%)
  Pallas kernels  39.4 us (30%)
  starting transfers between devices  20.8 us (16%)
  waiting for transfers between devices  8.08 us (6%)
  local copies, waits for them, and re-layouts  3.86 us (3%)
  other arithmetic  2.01 us (2%)
    all_gather x1, blocking collectives, scatter_sum(): terms = lax.all_gather(x[0], axes)  53.7 us
    pallas_call x12, Pallas kernels, call(): pl.pallas_call(kernel, grid_spec=pltpu.PrefetchScalarGridSpec(num_scalar_...  39.4 us
    ppermute x12, starting transfers between devices, chips_before(): arrived = [lax.ppermute(total, 'ctx', route) + token for total in totals]  14.4 us
    ppermute x12, waiting for transfers between devices, chips_before(): arrived = [lax.ppermute(total, 'ctx', route) + token for total in totals]  5.91 us
    unnamed x40, local copies, waits for them, and re-layouts  3.86 us
    ppermute x2, starting transfers between devices, shifted(): lax.ppermute(x, 'ctx', [(i, i + distance) for i in range(count) if 0 <= i...  3.35 us
    ppermute x8, starting transfers between devices, partner(): return lax.ppermute(x, axis, route)  3.04 us
  transfers between devices with their start and end apart: 22, of which 5 were waited for; matrix products, arithmetic and copies ran while one was open for 1% of the time, Pallas kernels for 25%

profile of v4, /device:TPU:0, one launch (start us, length us, event | category | flops | bytes accessed | tf_op | source)
XLA Modules:
  0.0 128.9 jit_solution(3208082705836949858)
XLA Ops:
  0.6 1.6 %shard_map.111 = (f32[256,128]{1,0:T(8,128)S(1)}, f32[256,128]{1,0:T(8,128)S(1)}) custom-call(s32[1]{0:T(128)} %bitcast.core, bf16[256,2048]{1,0:T(8,128)(2,1)} %bitcast.38, bf16[256,2048]{1,0:T(8,128)(2,1)} %bitcast.47), custom_call_target="tpu_custom_call" | custom-call | flops 1380000000 | tf_op jit(solution)/shard_map/pallas_call | solution.py:360
  2.8 1.8 %shard_map.110 = (f32[256,128]{1,0:T(8,128)S(1)}, f32[256,128]{1,0:T(8,128)S(1)}) custom-call(s32[1]{0:T(128)} %bitcast.core, bf16[256,2048]{1,0:T(8,128)(2,1)} %bitcast.39, bf16[256,2048]{1,0:T(8,128)(2,1)} %bitcast.48), custom_call_target="tpu_custom_call" | custom-call | flops 1380000000 | tf_op jit(solution)/shard_map/pallas_call | solution.py:360
  5.6 4.9 %collective-permute-start.3 = (f32[256,128]{1,0:T(8,128)S(1)}, f32[256,128]{1,0:T(8,128)S(1)}, u32[]{:S(2)}, u32[]{:S(2)}) collective-permute-start(f32[256,128]{1,0:T(8,128)S(1)} %add.155.rest_1_), channel_id=1, source_target_pairs={{0,2},{1,3},{8,10},{9,11},{16,18},{17,19},{24,26},{25,27}} | collective-permute-start | bytes 393224 | tf_op jit(solution)/shard_map/ppermute | solution.py:260
  10.6 1.4 %collective-permute-start.1 = (f32[256,128]{1,0:T(8,128)S(1)}, f32[256,128]{1,0:T(8,128)S(1)}, u32[]{:S(2)}, u32[]{:S(2)}) collective-permute-start(f32[256,128]{1,0:T(8,128)S(1)} %add.154.rest_0_), channel_id=1, source_target_pairs={{0,2},{1,3},{8,10},{9,11},{16,18},{17,19},{24,26},{25,27}} | collective-permute-start | bytes 393224 | tf_op jit(solution)/shard_map/ppermute | solution.py:260
  12.1 2.6 %shard_map.112.rest_0_ = f32[4,264,128]{2,1,0:T(8,128)} custom-call(bf16[256,2048]{1,0:T(8,128)(2,1)S(1)} %bitcast.40, bf16[256,2048]{1,0:T(8,128)(2,1)S(1)} %bitcast.49, s32[1,256]{1,0:T(1,128)S(1)} %copy-done, s32[1,32]{1,0:T(1,128)S(1)} %copy-done.1, f32[256,128]{1,0:T(8,128)S(1)} %add.154.rest_0_, f32[256,128]{1,0:T(8,128)S(1)} %add.155.rest_1_), custom_call_target="tpu_custom_call" | custom-call | flops 2300000000 | bytes 1048576 | tf_op jit(solution)/shard_map/pallas_call | solution.py:360
  14.7 1.3 collective-permute-start.7
  16.0 3.7 %shard_map.113 = (f32[256,1024]{1,0:T(8,128)}, f32[1,128]{1,0:T(1,128)S(1)}) custom-call(s32[1]{0:T(128)} %bitcast.core, bf16[256,2048]{1,0:T(8,128)(2,1)S(1)} %bitcast.31, bf16[256,2048]{1,0:T(8,128)(2,1)S(1)} %bitcast.41, bf16[256,2048]{1,0:T(8,128)(2,1)S(1)} %bitcast.50, bf16[256,256]{1,0:T(8,128)(2,1)S(1)} %get-tuple-element.86.mask, ...), custom_call_target="tpu_custom_call" | custom-call | flops 2644999936 | bytes 2097152 | tf_op jit(solution)/shard_map/pallas_call | solution.py:360
  21.1 3.1 %shard_map.114 = (f32[256,1024]{1,0:T(8,128)}, f32[1,128]{1,0:T(1,128)S(1)}) custom-call(s32[1]{0:T(128)} %bitcast.core, bf16[256,2048]{1,0:T(8,128)(2,1)S(1)} %bitcast.32, bf16[256,2048]{1,0:T(8,128)(2,1)S(1)} %bitcast.42, bf16[256,2048]{1,0:T(8,128)(2,1)S(1)} %bitcast.51, bf16[256,256]{1,0:T(8,128)(2,1)S(1)} %get-tuple-element.86.mask, ...), custom_call_target="tpu_custom_call" | custom-call | flops 2644999936 | bytes 2097152 | tf_op jit(solution)/shard_map/pallas_call | solution.py:360
  25.7 1.2 collective-permute-start.10
  27.9 1.2 copy-done.15
  29.1 3.7 %shard_map.115 = (bf16[256,2048]{1,0:T(8,128)(2,1)}, bf16[256,2048]{1,0:T(8,128)(2,1)}, f32[1,1024]{1,0:T(1,128)S(1)}, f32[256,128]{1,0:T(8,128)S(1)}, f32[256,128]{1,0:T(8,128)S(1)}) custom-call(s32[1]{0:T(128)} %bitcast.core, bf16[256,2048]{1,0:T(8,128)(2,1)S(1)} %bitcast.33, bf16[256,2048]{1,0:T(8,128)(2,1)S(1)} %bitcast.29, f32[256,1024]{1,0:T(8,128)S(1)} %copy-done.15, ...), custom_call_target="tpu_custom_call" | custom-call | flops 3449999872 | bytes 2621440 | tf_op jit(solution)/shard_map/pallas_call | solution.py:360
  33.4 0.9 collective-permute-done.11
  34.8 3.7 %shard_map.116 = (bf16[256,2048]{1,0:T(8,128)(2,1)}, bf16[256,2048]{1,0:T(8,128)(2,1)}, f32[1,1024]{1,0:T(1,128)S(1)}, f32[256,128]{1,0:T(8,128)S(1)}, f32[256,128]{1,0:T(8,128)S(1)}) custom-call(s32[1]{0:T(128)} %bitcast.core, bf16[256,2048]{1,0:T(8,128)(2,1)S(1)} %bitcast.34, ...), custom_call_target="tpu_custom_call", output_to_operand_aliasing={{0}: (11, {}), {1}: (12, {})} | custom-call | flops 3449999872 | bytes 2621440 | tf_op jit(solution)/shard_map/pallas_call | solution.py:360
  41.1 1.2 copy-done.13
  42.3 1.8 %shard_map.117.rest_0_ = f32[4,264,128]{2,1,0:T(8,128)S(1)} custom-call(bf16[256,2048]{1,0:T(8,128)(2,1)S(1)} %bitcast.35, bf16[256,2048]{1,0:T(8,128)(2,1)S(1)} %copy-done.13, s32[1,256]{1,0:T(1,128)S(1)} %copy-done, s32[1,32]{1,0:T(1,128)S(1)} %copy-done.1, f32[256,128]{1,0:T(8,128)S(1)} %add.176.rest_0_, f32[256,128]{1,0:T(8,128)S(1)} %add.177.rest_1_), custom_call_target="tpu_custom_call" | custom-call | flops 2300000000 | bytes 1048576 | tf_op jit(solution)/shard_map/pallas_call | solution.py:360
  44.2 6.6 %shard_map.118 = (bf16[256,2048]{1,0:T(8,128)(2,1)}, f32[256,1024]{1,0:T(8,128)}, f32[256,1024]{1,0:T(8,128)}, f32[1,128]{1,0:T(1,128)S(1)}) custom-call(s32[1]{0:T(128)} %bitcast.core, bf16[256,2048]{1,0:T(8,128)(2,1)S(1)} %bitcast.36, bf16[256,2048]{1,0:T(8,128)(2,1)S(1)} %bitcast.43, bf16[256,2048]{1,0:T(8,128)(2,1)S(1)} %bitcast.52, ...), custom_call_target="tpu_custom_call" | custom-call | flops 6325000192 | bytes 3670016 | tf_op jit(solution)/shard_map/pallas_call | solution.py:360
  52.2 6.7 %shard_map.119 = (bf16[256,2048]{1,0:T(8,128)(2,1)}, f32[256,1024]{1,0:T(8,128)}, f32[256,1024]{1,0:T(8,128)}, f32[1,128]{1,0:T(1,128)S(1)}) custom-call(s32[1]{0:T(128)} %bitcast.core, bf16[256,2048]{1,0:T(8,128)(2,1)S(1)} %bitcast.37, bf16[256,2048]{1,0:T(8,128)(2,1)S(1)} %bitcast.44, ...), custom_call_target="tpu_custom_call", output_to_operand_aliasing={{0}: (14, {})} | custom-call | flops 6325000192 | bytes 3670016 | tf_op jit(solution)/shard_map/pallas_call | solution.py:360
  59.0 1.4 %collective-permute-start.20 = (f32[256,128]{1,0:T(8,128)S(1)}, f32[256,128]{1,0:T(8,128)S(1)}, u32[]{:S(2)}, u32[]{:S(2)}) collective-permute-start(f32[256,128]{1,0:T(8,128)S(1)} %get-tuple-element.65), channel_id=1, source_target_pairs={{2,0},{3,1},{10,8},{11,9},{18,16},{19,17},{26,24},{27,25}} | collective-permute-start | bytes 393224 | tf_op jit(solution)/shard_map/ppermute | solution.py:260
  60.5 2.1 %collective-permute-start.18 = (f32[4,264,128]{2,1,0:T(8,128)S(1)}, f32[4,264,128]{2,1,0:T(8,128)S(1)}, u32[]{:S(2)}, u32[]{:S(2)}) collective-permute-start(f32[4,264,128]{2,1,0:T(8,128)S(1)} %shard_map.117.rest_0_), channel_id=1, source_target_pairs={{0,1},{1,2},{2,3},{3,4},{4,5},{5,6},{6,7},{8,9},{9,10},{10,11},{11... | collective-permute-start | bytes 1622024 | tf_op jit(solution)/shard_map/ppermute | solution.py:239
  62.5 53.7 %all-gather = f32[32,1,2048]{2,1,0:T(1,128)S(1)} all-gather(f32[1,1,2048]{2,1,0:T(1,128)S(1)} %maximum_bitcast_fusion), channel_id=1, replica_groups=mesh['dp'=4,'ctx'=8] {'dp','ctx'}, dimensions={0}, use_global_device_ids=true | all-gather | bytes 270336 | tf_op jit(solution)/shard_map/all_gather | solution.py:282
  116.9 1.3 collective-permute-start.16
  118.6 5.9 %collective-permute-done.16 = f32[256,128]{1,0:T(8,128)S(1)} collective-permute-done((f32[256,128]{1,0:T(8,128)S(1)}, f32[256,128]{1,0:T(8,128)S(1)}, u32[]{:S(2)}, u32[]{:S(2)}) %collective-permute-start.16) | collective-permute-done | bytes 131104 | tf_op jit(solution)/shard_map/ppermute | solution.py:260
  124.7 2.1 %shard_map.120 = (bf16[256,2048]{1,0:T(8,128)(2,1)}, bf16[256,2048]{1,0:T(8,128)(2,1)}) custom-call(s32[1]{0:T(128)} %bitcast.core, bf16[256,2048]{1,0:T(8,128)(2,1)S(1)} %bitcast.45, bf16[256,2048]{1,0:T(8,128)(2,1)S(1)} %bitcast.54, f32[256,1024]{1,0:T(8,128)S(1)} %copy-done.11, f32[256,1024]{1,0:T(8,128)S(1)} %copy-done.12, s32[1,256]{1,0:T(1,128)S(1)} %copy-done, ...), custom_call_target="tpu_custom_call" | custom-call | flops 2415000064 | bytes 3145728 | tf_op jit(solution)/shard_map/pallas_call | solution.py:360
  126.8 2.1 %shard_map.121 = (bf16[256,2048]{1,0:T(8,128)(2,1)}, bf16[256,2048]{1,0:T(8,128)(2,1)}) custom-call(s32[1]{0:T(128)} %bitcast.core, bf16[256,2048]{1,0:T(8,128)(2,1)S(1)} %bitcast.46, bf16[256,2048]{1,0:T(8,128)(2,1)S(1)} %bitcast.55, f32[256,1024]{1,0:T(8,128)S(1)} %copy-done.9, ...), custom_call_target="tpu_custom_call", output_to_operand_aliasing={{0}: (10, {}), {1}: (11, {})} | custom-call | flops 2415000064 | bytes 3145728 | tf_op jit(solution)/shard_map/pallas_call | solution.py:360
  (91 shorter events, 11.9 us)
Async XLA Ops:
  2.3 3.3 %collective-permute-start.2 = (f32[256,128]{1,0:T(8,128)S(1)}, f32[256,128]{1,0:T(8,128)S(1)}, u32[]{:S(2)}, u32[]{:S(2)}) collective-permute-start(f32[256,128]{1,0:T(8,128)S(1)} %get-tuple-element.38), channel_id=1, source_target_pairs={{0,1},{1,0},{2,3},{3,2},{4,5},{5,4},{6,7},{7,6},{8,9},{9,8},{10,11... | collective-permute-start | bytes 393224 | tf_op jit(solution)/shard_map/ppermute | solution.py:234
  4.6 6.0 %collective-permute-start = (f32[256,128]{1,0:T(8,128)S(1)}, f32[256,128]{1,0:T(8,128)S(1)}, u32[]{:S(2)}, u32[]{:S(2)}) collective-permute-start(f32[256,128]{1,0:T(8,128)S(1)} %get-tuple-element.36), channel_id=1, source_target_pairs={{0,1},{1,0},{2,3},{3,2},{4,5},{5,4},{6,7},{7,6},{8,9},{9,8},{10,11... | collective-permute-start | bytes 393224 | tf_op jit(solution)/shard_map/ppermute | solution.py:234
  5.6 14.1 %collective-permute-start.3 = (f32[256,128]{1,0:T(8,128)S(1)}, f32[256,128]{1,0:T(8,128)S(1)}, u32[]{:S(2)}, u32[]{:S(2)}) collective-permute-start(f32[256,128]{1,0:T(8,128)S(1)} %add.155.rest_1_), channel_id=1, source_target_pairs={{0,2},{1,3},{8,10},{9,11},{16,18},{17,19},{24,26},{25,27}} | collective-permute-start | bytes 393224 | tf_op jit(solution)/shard_map/ppermute | solution.py:260
  10.6 9.1 %collective-permute-start.1 = (f32[256,128]{1,0:T(8,128)S(1)}, f32[256,128]{1,0:T(8,128)S(1)}, u32[]{:S(2)}, u32[]{:S(2)}) collective-permute-start(f32[256,128]{1,0:T(8,128)S(1)} %add.154.rest_0_), channel_id=1, source_target_pairs={{0,2},{1,3},{8,10},{9,11},{16,18},{17,19},{24,26},{25,27}} | collective-permute-start | bytes 393224 | tf_op jit(solution)/shard_map/ppermute | solution.py:260
  14.7 13.2 %collective-permute-start.7 = (f32[4,264,128]{2,1,0:T(8,128)}, f32[4,264,128]{2,1,0:T(8,128)}, u32[]{:S(2)}, u32[]{:S(2)}) collective-permute-start(f32[4,264,128]{2,1,0:T(8,128)} %shard_map.112.rest_0_), channel_id=1, source_target_pairs={{1,0},{2,1},{3,2},{4,3},{5,4},{6,5},{7,6},{9,8},{10,9},{11,10},{12... | collective-permute-start | bytes 1622024 | tf_op jit(solution)/shard_map/ppermute | solution.py:239
  19.7 4.4 %collective-permute-start.4 = (f32[256,128]{1,0:T(8,128)S(1)}, f32[256,128]{1,0:T(8,128)S(1)}, u32[]{:S(2)}, u32[]{:S(2)}) collective-permute-start(f32[256,128]{1,0:T(8,128)S(1)} %get-tuple-element.91.rest_1_), channel_id=1, source_target_pairs={{2,4},{3,5},{10,12},{11,13},{18,20},{19,21},{26,28},{27,29}} | collective-permute-start | bytes 393224 | tf_op jit(solution)/shard_map/ppermute | solution.py:260
  20.4 3.8 %collective-permute-start.8 = (f32[256,128]{1,0:T(8,128)S(1)}, f32[256,128]{1,0:T(8,128)S(1)}, u32[]{:S(2)}, u32[]{:S(2)}) collective-permute-start(f32[256,128]{1,0:T(8,128)S(1)} %get-tuple-element.92.rest_0_), channel_id=1, source_target_pairs={{2,4},{3,5},{10,12},{11,13},{18,20},{19,21},{26,28},{27,29}} | collective-permute-start | bytes 393224 | tf_op jit(solution)/shard_map/ppermute | solution.py:260
  25.0 0.7 collective-permute-start.9
  25.7 2.2 %collective-permute-start.10 = (f32[256,128]{1,0:T(8,128)S(1)}, f32[256,128]{1,0:T(8,128)S(1)}, u32[]{:S(2)}, u32[]{:S(2)}) collective-permute-start(f32[256,128]{1,0:T(8,128)S(1)} %get-tuple-element.79), channel_id=1, source_target_pairs={{0,1},{1,0},{2,3},{3,2},{4,5},{5,4},{6,7},{7,6},{8,9},{9,8},{10,11... | collective-permute-start | bytes 393224 | tf_op jit(solution)/shard_map/ppermute | solution.py:234
  26.9 6.4 %collective-permute-start.5 = (f32[256,128]{1,0:T(8,128)S(1)}, f32[256,128]{1,0:T(8,128)S(1)}, u32[]{:S(2)}, u32[]{:S(2)}) collective-permute-start(f32[256,128]{1,0:T(8,128)S(1)} %copy-done.19), channel_id=1, source_target_pairs={{4,6},{5,7},{12,14},{13,15},{20,22},{21,23},{28,30},{29,31}} | collective-permute-start | bytes 393224 | tf_op jit(solution)/shard_map/ppermute | solution.py:260
  32.8 1.5 %collective-permute-start.11 = (f32[256,128]{1,0:T(8,128)S(1)}, f32[256,128]{1,0:T(8,128)S(1)}, u32[]{:S(2)}, u32[]{:S(2)}) collective-permute-start(f32[256,128]{1,0:T(8,128)S(1)} %get-tuple-element.44), channel_id=1, source_target_pairs={{0,1},{1,0},{2,3},{3,2},{4,5},{5,4},{6,7},{7,6},{8,9},{9,8},{10,11... | collective-permute-start | bytes 393224 | tf_op jit(solution)/shard_map/ppermute | solution.py:234
  33.3 1.4 %collective-permute-start.6 = (f32[256,128]{1,0:T(8,128)S(1)}, f32[256,128]{1,0:T(8,128)S(1)}, u32[]{:S(2)}, u32[]{:S(2)}) collective-permute-start(f32[256,128]{1,0:T(8,128)S(1)} %get-tuple-element.81), channel_id=1, source_target_pairs={{0,1},{1,0},{2,3},{3,2},{4,5},{5,4},{6,7},{7,6},{8,9},{9,8},{10,11... | collective-permute-start | bytes 393224 | tf_op jit(solution)/shard_map/ppermute | solution.py:234
  38.4 1.3 %collective-permute-start.13 = (f32[256,128]{1,0:T(8,128)S(1)}, f32[256,128]{1,0:T(8,128)S(1)}, u32[]{:S(2)}, u32[]{:S(2)}) collective-permute-start(f32[256,128]{1,0:T(8,128)S(1)} %get-tuple-element.50), channel_id=1, source_target_pairs={{0,1},{1,0},{2,3},{3,2},{4,5},{5,4},{6,7},{7,6},{8,9},{9,8},{10,11... | collective-permute-start | bytes 393224 | tf_op jit(solution)/shard_map/ppermute | solution.py:234
  38.6 12.2 %collective-permute-start.12 = (f32[256,128]{1,0:T(8,128)S(1)}, f32[256,128]{1,0:T(8,128)S(1)}, u32[]{:S(2)}, u32[]{:S(2)}) collective-permute-start(f32[256,128]{1,0:T(8,128)S(1)} %add.176.rest_0_), channel_id=1, source_target_pairs={{6,4},{7,5},{14,12},{15,13},{22,20},{23,21},{30,28},{31,29}} | collective-permute-start | bytes 393224 | tf_op jit(solution)/shard_map/ppermute | solution.py:260
  40.4 10.4 %collective-permute-start.14 = (f32[256,128]{1,0:T(8,128)S(1)}, f32[256,128]{1,0:T(8,128)S(1)}, u32[]{:S(2)}, u32[]{:S(2)}) collective-permute-start(f32[256,128]{1,0:T(8,128)S(1)} %add.177.rest_1_), channel_id=1, source_target_pairs={{6,4},{7,5},{14,12},{15,13},{22,20},{23,21},{30,28},{31,29}} | collective-permute-start | bytes 393224 | tf_op jit(solution)/shard_map/ppermute | solution.py:260
  50.8 8.1 %collective-permute-start.15 = (f32[256,128]{1,0:T(8,128)S(1)}, f32[256,128]{1,0:T(8,128)S(1)}, u32[]{:S(2)}, u32[]{:S(2)}) collective-permute-start(f32[256,128]{1,0:T(8,128)S(1)} %get-tuple-element.89.rest_1_), channel_id=1, source_target_pairs={{4,2},{5,3},{12,10},{13,11},{20,18},{21,19},{28,26},{29,27}} | collective-permute-start | bytes 393224 | tf_op jit(solution)/shard_map/ppermute | solution.py:260
  51.5 7.4 %collective-permute-start.19 = (f32[256,128]{1,0:T(8,128)S(1)}, f32[256,128]{1,0:T(8,128)S(1)}, u32[]{:S(2)}, u32[]{:S(2)}) collective-permute-start(f32[256,128]{1,0:T(8,128)S(1)} %get-tuple-element.90.rest_0_), channel_id=1, source_target_pairs={{4,2},{5,3},{12,10},{13,11},{20,18},{21,19},{28,26},{29,27}} | collective-permute-start | bytes 393224 | tf_op jit(solution)/shard_map/ppermute | solution.py:260
  58.9 65.7 %copy-start.12 = (f32[256,1024]{1,0:T(8,128)S(1)}, f32[256,1024]{1,0:T(8,128)}, u32[]{:S(2)}) copy-start(f32[256,1024]{1,0:T(8,128)} %get-tuple-element.58.gv_in) | copy-start | bytes 3145732
  59.0 65.6 %copy-start.11 = (f32[256,1024]{1,0:T(8,128)S(1)}, f32[256,1024]{1,0:T(8,128)}, u32[]{:S(2)}) copy-start(f32[256,1024]{1,0:T(8,128)} %get-tuple-element.57.gk_in) | copy-start | bytes 3145732
  59.0 59.1 %collective-permute-start.20 = (f32[256,128]{1,0:T(8,128)S(1)}, f32[256,128]{1,0:T(8,128)S(1)}, u32[]{:S(2)}, u32[]{:S(2)}) collective-permute-start(f32[256,128]{1,0:T(8,128)S(1)} %get-tuple-element.65), channel_id=1, source_target_pairs={{2,0},{3,1},{10,8},{11,9},{18,16},{19,17},{26,24},{27,25}} | collective-permute-start | bytes 393224 | tf_op jit(solution)/shard_map/ppermute | solution.py:260
  60.5 64.2 %collective-permute-start.18 = (f32[4,264,128]{2,1,0:T(8,128)S(1)}, f32[4,264,128]{2,1,0:T(8,128)S(1)}, u32[]{:S(2)}, u32[]{:S(2)}) collective-permute-start(f32[4,264,128]{2,1,0:T(8,128)S(1)} %shard_map.117.rest_0_), channel_id=1, source_target_pairs={{0,1},{1,2},{2,3},{3,4},{4,5},{5,6},{6,7},{8,9},{9,10},{10,11},{11... | collective-permute-start | bytes 1622024 | tf_op jit(solution)/shard_map/ppermute | solution.py:239
  116.9 7.6 %collective-permute-start.16 = (f32[256,128]{1,0:T(8,128)S(1)}, f32[256,128]{1,0:T(8,128)S(1)}, u32[]{:S(2)}, u32[]{:S(2)}) collective-permute-start(f32[256,128]{1,0:T(8,128)S(1)} %get-tuple-element.83), channel_id=1, source_target_pairs={{2,0},{3,1},{10,8},{11,9},{18,16},{19,17},{26,24},{27,25}} | collective-permute-start | bytes 393224 | tf_op jit(solution)/shard_map/ppermute | solution.py:260
  118.2 6.4 %collective-permute-start.21 = (f32[256,128]{1,0:T(8,128)S(1)}, f32[256,128]{1,0:T(8,128)S(1)}, u32[]{:S(2)}, u32[]{:S(2)}) collective-permute-start(f32[256,128]{1,0:T(8,128)S(1)} %get-tuple-element.75), channel_id=1, source_target_pairs={{0,1},{1,0},{2,3},{3,2},{4,5},{5,4},{6,7},{7,6},{8,9},{9,8},{10,11... | collective-permute-start | bytes 393224 | tf_op jit(solution)/shard_map/ppermute | solution.py:234
  124.5 2.2 %collective-permute-start.17 = (f32[256,128]{1,0:T(8,128)S(1)}, f32[256,128]{1,0:T(8,128)S(1)}, u32[]{:S(2)}, u32[]{:S(2)}) collective-permute-start(f32[256,128]{1,0:T(8,128)S(1)} %get-tuple-element.77), channel_id=1, source_target_pairs={{0,1},{1,0},{2,3},{3,2},{4,5},{5,4},{6,7},{7,6},{8,9},{9,8},{10,11... | collective-permute-start | bytes 393224 | tf_op jit(solution)/shard_map/ppermute | solution.py:234
  (18 other events, 112.8 us)

commit v5 on v4

--- a/solution.py
+++ b/solution.py
@@ -93,7 +93,8 @@
 
 
 def part_kernel(last, a, b, seg, table, *rest):
-    out = rest[-1]
+    out, token = rest[-2:]
+    token[...] = jnp.zeros_like(token)
     count = a.shape[1] // PAIR
     rows, own, flag = edge(seg, table, last)
     sel = rows.astype(F32) * jnp.where(flag == 1, 1.0, 0.0) if last else rows.astype(F32)
@@ -256,8 +257,11 @@
         source = hop if towards == 1 else chips - 1 - hop
         token = works[hop](totals) if hop < len(works) else jnp.zeros((1, PAIR), F32)
         if hop < chips - 1:
-            route = [(2 * source + c, 2 * (source + towards) + c) for c in range(2)]
-            arrived = [lax.ppermute(total, "ctx", route) + token for total in totals]
+            target = source + towards
+            mate = {source: target, target: source}
+            route = [(2 * z + c, 2 * mate.get(z, z) + c) for z in range(chips) for c in range(2)]
+            is_target = lax.axis_index("ctx") // 2 == target
+            arrived = [jnp.where(is_target, lax.ppermute(total, "ctx", route), 0.0) + token for total in totals]
             befores = [a if before is None else before + a for before, a in zip(befores, arrived)]
     return befores
 
@@ -277,12 +281,12 @@
     return pltpu.with_memory_space_constraint(x, pltpu.HBM)
 
 
-def scatter_sum(x):
+def scatter_sum(x, token):
     axes = ("dp", "ctx")
-    terms = lax.all_gather(x[0], axes)
-    count = x.shape[1] // terms.shape[0]
-    own = lax.dynamic_slice_in_dim(terms, lax.axis_index(axes) * count, count, 1)
-    return jnp.sum(own, axis=0)
+    devices = lax.axis_size("dp") * lax.axis_size("ctx")
+    x = x.reshape(devices, -1)
+    terms = lax.all_to_all(x + token[:, :x.shape[1]], axes, 0, 0, tiled=True)
+    return jnp.sum(terms, axis=0)
 
 
 def on_device(queries, keys, values, out_grad, segment_ids, image_flags, gain):
@@ -389,20 +393,21 @@
 
     found = {}
 
-    def early_work(g):
+    def early_parts(totals):
+        found["nxt"], token = call(
+            functools.partial(part_kernel, False), 0, [("wide", k), ("wide", v), *edges],
+            [("part", F32), ("token", F32)], 2.0, after=totals, steps=(2 * GROUPS,), prefetch=False)
+        return token
+
+    def local_of(g):
         def work(totals):
-            if g == 0:
-                found["nxt"], = call(
-                    functools.partial(part_kernel, False), 0, [("wide", k), ("wide", v), *edges],
-                    [("part", F32)], 2.0, after=totals, steps=(2 * GROUPS,), prefetch=False)
-                totals = [found["nxt"]]
             found["local", g], token = call(
                 local_kernel, g, [("wide", q), ("wide", k), ("wide", v), ("mask", mask)],
                 [("block", F32), ("token", F32)], 2.3, after=totals)
             return token
         return work
 
-    prefix = phase(pieces, 1, [early_work(g) for g in groups])
+    prefix = phase(pieces, 1, [early_parts, *map(local_of, groups)])
     nxt = shifted(found["nxt"], -1)
 
     output = dab = grad_q = grad_k = grad_v = None
@@ -417,13 +422,14 @@
         gsums.append(gsum)
         pieces.append((keep, *within_chip(keep, send)))
 
-    def late_work(g):
+    def late_parts(totals):
+        found["prv"], token = call(
+            functools.partial(part_kernel, True), 0, [("wide", q), ("wide", dab), *edges],
+            [("part", F32), ("token", F32)], 2.0, after=totals, steps=(2 * GROUPS,), prefetch=False)
+        return token
+
+    def inner_of(g):
         def work(totals):
-            if g == 0:
-                found["prv"], = call(
-                    functools.partial(part_kernel, True), 0, [("wide", q), ("wide", dab), *edges],
-                    [("part", F32)], 2.0, after=totals, steps=(2 * GROUPS,), prefetch=False)
-                totals = [found["prv"]]
             found["gq"], gk, gv, token = call(
                 inner_kernel, g,
                 [("wide", q), ("wide", k), ("wide", v), ("wide", dab), ("mask", mask), ("mask", mask_t), *edges,
@@ -431,13 +437,14 @@
                 [("wide", BF16), ("block", F32), ("block", F32), ("token", F32)],
                 5.5, after=totals, alias=[(0, found.get("gq"))])
             found["inner", g] = gk, gv
+            found["token"] = token
             return token
         return work
 
-    suffix = phase(pieces, -1, [late_work(g) for g in groups])
+    suffix = phase(pieces, -1, [late_parts, *map(inner_of, groups)])
     prv = shifted(found["prv"], 1)
     grad_q = found["gq"]
-    grad_gain = scatter_sum(jnp.concatenate(gsums, axis=1))
+    grad_gain = scatter_sum(jnp.concatenate(gsums, axis=1), found["token"])
     for g in groups:
         gk, gv = found["inner", g]
         grad_k, grad_v = call(

time: 130 us -> 110 us (0.85)
  blocking collectives: 53.7 us -> 10.9 us
  starting transfers between devices: 20.8 us -> 46.1 us
  waiting for transfers between devices: 8.08 us -> 3.05 us
  local copies, waits for them, and re-layouts: 3.86 us -> 7 us
  Pallas kernels: 39.4 us -> 37.4 us
  other arithmetic: 2.01 us -> 3.78 us
    all_gather x1 -> x0, blocking collectives: 53.7 us -> none  [scatter_sum(): terms = lax.all_gather(x[0], axes)]
    ppermute x12, starting transfers between devices: 14.4 us -> 38.6 us  [chips_before(): lax.ppermute(total, 'ctx', route)]
    all_to_all x0 -> x1, blocking collectives: none -> 10.9 us  [scatter_sum(): terms = lax.all_to_all(x + token[:, :x.shape[1]], axes, 0, 0, tiled=True)]
    ppermute x12, waiting for transfers between devices: 5.91 us -> 0.86 us  [chips_before(): lax.ppermute(total, 'ctx', route)]
    pallas_call x12, Pallas kernels: 39.4 us -> 37.4 us  [call(): pl.pallas_call(kernel, grid_spec=pltpu.PrefetchScalarGridSpec(num_scalar_...]
    unnamed x40 -> x42, local copies, waits for them, and re-layouts: 3.86 us -> 5.63 us
    reshape x0 -> x1, local copies, waits for them, and re-layouts: none -> 1.36 us  [scatter_sum(): x = x.reshape(devices, -1)]
  transfers between devices with their start and end apart: 22 -> 22, of which waited for: 5 -> 4; matrix products, arithmetic and copies ran while one was open for 1% -> 5% of each run, Pallas kernels for 25% -> 25%
where the time goes in v5:
time: 110 us; the launch traced here: 109 us
  starting transfers between devices  46.1 us (42%)
  Pallas kernels  37.4 us (34%)
  blocking collectives  10.9 us (10%)
  local copies, waits for them, and re-layouts  7 us (6%)
  other arithmetic  3.78 us (3%)
  waiting for transfers between devices  3.05 us (3%)
    ppermute x12, starting transfers between devices, chips_before(): lax.ppermute(total, 'ctx', route)  38.6 us
    pallas_call x12, Pallas kernels, call(): pl.pallas_call(kernel, grid_spec=pltpu.PrefetchScalarGridSpec(num_scalar_...  37.4 us
    all_to_all x1, blocking collectives, scatter_sum(): terms = lax.all_to_all(x + token[:, :x.shape[1]], axes, 0, 0, tiled=True)  10.9 us
    unnamed x42, local copies, waits for them, and re-layouts  5.63 us
    ppermute x2, starting transfers between devices, shifted(): lax.ppermute(x, 'ctx', [(i, i + distance) for i in range(count) if 0 <= i...  4.42 us
    ppermute x8, starting transfers between devices, partner(): return lax.ppermute(x, axis, route)  3.17 us
  transfers between devices with their start and end apart: 22, of which 4 were waited for; matrix products, arithmetic and copies ran while one was open for 5% of the time, Pallas kernels for 25%

profile of v5, /device:TPU:0, one launch (start us, length us, event | category | flops | bytes accessed | tf_op | source)
XLA Modules:
  0.0 109.3 jit_solution(3720555291012186315)
XLA Ops:
  0.6 1.6 %shard_map.111 = (f32[256,128]{1,0:T(8,128)S(1)}, f32[256,128]{1,0:T(8,128)S(1)}) custom-call(s32[1]{0:T(128)} %bitcast.core, bf16[256,2048]{1,0:T(8,128)(2,1)} %bitcast.43, bf16[256,2048]{1,0:T(8,128)(2,1)} %bitcast.52), custom_call_target="tpu_custom_call" | custom-call | flops 1380000000 | tf_op jit(solution)/shard_map/pallas_call | solution.py:364
  2.8 1.7 %shard_map.110 = (f32[256,128]{1,0:T(8,128)S(1)}, f32[256,128]{1,0:T(8,128)S(1)}) custom-call(s32[1]{0:T(128)} %bitcast.core, bf16[256,2048]{1,0:T(8,128)(2,1)} %bitcast.44, bf16[256,2048]{1,0:T(8,128)(2,1)} %bitcast.53), custom_call_target="tpu_custom_call" | custom-call | flops 1380000000 | tf_op jit(solution)/shard_map/pallas_call | solution.py:364
  5.6 4.9 %collective-permute-start.4 = (f32[256,128]{1,0:T(8,128)S(1)}, f32[256,128]{1,0:T(8,128)S(1)}, u32[]{:S(2)}, u32[]{:S(2)}) collective-permute-start(f32[256,128]{1,0:T(8,128)S(1)} %add.197.rest_1_), channel_id=1, source_target_pairs={{0,2},{1,3},{2,0},{3,1},{4,4},{5,5},{6,6},{7,7},{8,10},{9,11},{10,... | collective-permute-start | bytes 393224 | tf_op jit(solution)/shard_map/ppermute | solution.py:264
  10.6 2.1 %collective-permute-start.1 = (f32[256,128]{1,0:T(8,128)S(1)}, f32[256,128]{1,0:T(8,128)S(1)}, u32[]{:S(2)}, u32[]{:S(2)}) collective-permute-start(f32[256,128]{1,0:T(8,128)S(1)} %add.196.rest_0_), channel_id=1, source_target_pairs={{0,2},{1,3},{2,0},{3,1},{4,4},{5,5},{6,6},{7,7},{8,10},{9,11},{10,... | collective-permute-start | bytes 393224 | tf_op jit(solution)/shard_map/ppermute | solution.py:264
  12.7 1.2 %copy-done.5 = bf16[1,256,2048]{2,1,0:T(8,128)(2,1)S(1)} copy-done((bf16[1,256,2048]{2,1,0:T(8,128)(2,1)S(1)}, bf16[1,256,2048]{2,1,0:T(8,128)(2,1)}, u32[]{:S(2)}) %copy-start.5) | copy-done | bytes 1048600
  13.9 1.7 %shard_map.112 = (f32[4,264,128]{2,1,0:T(8,128)S(1)}, f32[1,128]{1,0:T(1,128)S(1)}) custom-call(bf16[256,2048]{1,0:T(8,128)(2,1)S(1)} %bitcast.45, bf16[256,2048]{1,0:T(8,128)(2,1)S(1)} %bitcast.54, s32[1,256]{1,0:T(1,128)S(1)} %copy-done, s32[1,32]{1,0:T(1,128)S(1)} %copy-done.1, f32[256,128]{1,0:T(8,128)S(1)} %add.196.rest_0_, f32[256,128]{1,0:T(8,128)S(1)} %add.197.rest_1_), custom_call_target="tpu_custom_call" | custom-call | flops 2300000000 | bytes 1048576 | tf_op jit(solution)/shard_map/pallas_call | solution.py:364
  15.6 1.3 %collective-permute-start.8 = (f32[4,264,128]{2,1,0:T(8,128)S(1)}, f32[4,264,128]{2,1,0:T(8,128)S(1)}, u32[]{:S(2)}, u32[]{:S(2)}) collective-permute-start(f32[4,264,128]{2,1,0:T(8,128)S(1)} %get-tuple-element.47), channel_id=1, source_target_pairs={{1,0},{2,1},{3,2},{4,3},{5,4},{6,5},{7,6},{9,8},{10,9},{11,10},{12... | collective-permute-start | bytes 1622024 | tf_op jit(solution)/shard_map/ppermute | solution.py:240
  19.2 3.1 %shard_map.113 = (f32[256,1024]{1,0:T(8,128)}, f32[1,128]{1,0:T(1,128)S(1)}) custom-call(s32[1]{0:T(128)} %bitcast.core, bf16[256,2048]{1,0:T(8,128)(2,1)S(1)} %bitcast.36, bf16[256,2048]{1,0:T(8,128)(2,1)S(1)} %bitcast.46, bf16[256,2048]{1,0:T(8,128)(2,1)S(1)} %bitcast.55, bf16[256,256]{1,0:T(8,128)(2,1)S(1)} %get-tuple-element.94.mask, ...), custom_call_target="tpu_custom_call" | custom-call | flops 2644999936 | bytes 2097152 | tf_op jit(solution)/shard_map/pallas_call | solution.py:364
  23.7 3.1 %shard_map.114 = (f32[256,1024]{1,0:T(8,128)}, f32[1,128]{1,0:T(1,128)S(1)}) custom-call(s32[1]{0:T(128)} %bitcast.core, bf16[256,2048]{1,0:T(8,128)(2,1)S(1)} %bitcast.37, bf16[256,2048]{1,0:T(8,128)(2,1)S(1)} %bitcast.47, bf16[256,2048]{1,0:T(8,128)(2,1)S(1)} %bitcast.56, bf16[256,256]{1,0:T(8,128)(2,1)S(1)} %get-tuple-element.94.mask, ...), custom_call_target="tpu_custom_call" | custom-call | flops 2644999936 | bytes 2097152 | tf_op jit(solution)/shard_map/pallas_call | solution.py:364
  28.3 3.0 %shard_map.115 = (bf16[256,2048]{1,0:T(8,128)(2,1)}, bf16[256,2048]{1,0:T(8,128)(2,1)}, f32[1,1024]{1,0:T(1,128)S(1)}, f32[256,128]{1,0:T(8,128)S(1)}, f32[256,128]{1,0:T(8,128)S(1)}) custom-call(s32[1]{0:T(128)} %bitcast.core, bf16[256,2048]{1,0:T(8,128)(2,1)S(1)} %bitcast.38, bf16[256,2048]{1,0:T(8,128)(2,1)S(1)} %bitcast.34, f32[256,1024]{1,0:T(8,128)S(1)} %copy-done.18, ...), custom_call_target="tpu_custom_call" | custom-call | flops 3449999872 | bytes 2621440 | tf_op jit(solution)/shard_map/pallas_call | solution.py:364
  32.9 2.9 %shard_map.116 = (bf16[256,2048]{1,0:T(8,128)(2,1)}, bf16[256,2048]{1,0:T(8,128)(2,1)}, f32[1,1024]{1,0:T(1,128)S(1)}, f32[256,128]{1,0:T(8,128)S(1)}, f32[256,128]{1,0:T(8,128)S(1)}) custom-call(s32[1]{0:T(128)} %bitcast.core, bf16[256,2048]{1,0:T(8,128)(2,1)S(1)} %bitcast.39, ...), custom_call_target="tpu_custom_call", output_to_operand_aliasing={{0}: (11, {}), {1}: (12, {})} | custom-call | flops 3449999872 | bytes 2621440 | tf_op jit(solution)/shard_map/pallas_call | solution.py:364
  36.1 1.3 %collective-permute-start.12 = (f32[256,128]{1,0:T(8,128)S(1)}, f32[256,128]{1,0:T(8,128)}, u32[]{:S(2)}, u32[]{:S(2)}) collective-permute-start(f32[256,128]{1,0:T(8,128)S(1)} %add.222.rest_0_), channel_id=1, source_target_pairs={{0,0},{1,1},{2,2},{3,3},{4,6},{5,7},{6,4},{7,5},{8,8},{9,9},{10,10... | collective-permute-start | bytes 393224 | tf_op jit(solution)/shard_map/ppermute | solution.py:264
  38.0 1.4 %reshape.75 = f32[32,1,64]{2,0,1:T(8,128)} reshape(f32[2048]{0:T(1024)} %maximum_reduce_fusion) | data formatting | bytes 16384 | tf_op jit(solution)/shard_map/reshape | solution.py:287
  42.2 2.6 %shard_map.117 = (f32[4,264,128]{2,1,0:T(8,128)}, f32[1,128]{1,0:T(1,128)S(1)}) custom-call(bf16[256,2048]{1,0:T(8,128)(2,1)S(1)} %bitcast.40, bf16[256,2048]{1,0:T(8,128)(2,1)S(1)} %copy-done.16, s32[1,256]{1,0:T(1,128)S(1)} %copy-done, s32[1,32]{1,0:T(1,128)S(1)} %copy-done.1, f32[256,128]{1,0:T(8,128)S(1)} %add.222.rest_0_, f32[256,128]{1,0:T(8,128)S(1)} %add.223.rest_1_), custom_call_target="tpu_custom_call" | custom-call | flops 2300000000 | bytes 1048576 | tf_op jit(solution)/shard_map/pallas_call | solution.py:364
  44.8 3.1 %collective-permute-start.19 = (f32[4,264,128]{2,1,0:T(8,128)}, f32[4,264,128]{2,1,0:T(8,128)}, u32[]{:S(2)}, u32[]{:S(2)}) collective-permute-start(f32[4,264,128]{2,1,0:T(8,128)} %get-tuple-element.64), channel_id=1, source_target_pairs={{0,1},{1,2},{2,3},{3,4},{4,5},{5,6},{6,7},{8,9},{9,10},{10,11},{11... | collective-permute-start | bytes 1622024 | tf_op jit(solution)/shard_map/ppermute | solution.py:240
  49.4 5.9 %shard_map.118 = (bf16[256,2048]{1,0:T(8,128)(2,1)}, f32[256,1024]{1,0:T(8,128)}, f32[256,1024]{1,0:T(8,128)}, f32[1,128]{1,0:T(1,128)S(1)}) custom-call(s32[1]{0:T(128)} %bitcast.core, bf16[256,2048]{1,0:T(8,128)(2,1)S(1)} %bitcast.41, bf16[256,2048]{1,0:T(8,128)(2,1)S(1)} %bitcast.48, bf16[256,2048]{1,0:T(8,128)(2,1)S(1)} %bitcast.57, ...), custom_call_target="tpu_custom_call" | custom-call | flops 6325000192 | bytes 3670016 | tf_op jit(solution)/shard_map/pallas_call | solution.py:364
  55.4 23.5 %collective-permute-start.20 = (f32[256,128]{1,0:T(8,128)S(1)}, f32[256,128]{1,0:T(8,128)S(1)}, u32[]{:S(2)}, u32[]{:S(2)}) collective-permute-start(f32[256,128]{1,0:T(8,128)S(1)} %get-tuple-element.91.rest_0_), channel_id=1, source_target_pairs={{0,2},{1,3},{2,0},{3,1},{4,4},{5,5},{6,6},{7,7},{8,10},{9,11},{10,... | collective-permute-start | bytes 393224 | tf_op jit(solution)/shard_map/ppermute | solution.py:264
  78.9 2.1 %collective-permute-start.17 = (f32[256,128]{1,0:T(8,128)S(1)}, f32[256,128]{1,0:T(8,128)S(1)}, u32[]{:S(2)}, u32[]{:S(2)}) collective-permute-start(f32[256,128]{1,0:T(8,128)S(1)} %get-tuple-element.73.rest_1_), channel_id=1, source_target_pairs={{0,2},{1,3},{2,0},{3,1},{4,4},{5,5},{6,6},{7,7},{8,10},{9,11},{10,... | collective-permute-start | bytes 393224 | tf_op jit(solution)/shard_map/ppermute | solution.py:264
  81.0 6.0 %shard_map.119 = (bf16[256,2048]{1,0:T(8,128)(2,1)}, f32[256,1024]{1,0:T(8,128)}, f32[256,1024]{1,0:T(8,128)}, f32[1,128]{1,0:T(1,128)S(1)}) custom-call(s32[1]{0:T(128)} %bitcast.core, bf16[256,2048]{1,0:T(8,128)(2,1)S(1)} %bitcast.42, bf16[256,2048]{1,0:T(8,128)(2,1)S(1)} %bitcast.49, ...), custom_call_target="tpu_custom_call", output_to_operand_aliasing={{0}: (14, {})} | custom-call | flops 6325000192 | bytes 3670016 | tf_op jit(solution)/shard_map/pallas_call | solution.py:364
  88.1 1.4 %collective-permute-start.21 = (f32[256,128]{1,0:T(8,128)S(1)}, f32[256,128]{1,0:T(8,128)S(1)}, u32[]{:S(2)}, u32[]{:S(2)}) collective-permute-start(f32[256,128]{1,0:T(8,128)S(1)} %get-tuple-element.83), channel_id=1, source_target_pairs={{0,1},{1,0},{2,3},{3,2},{4,5},{5,4},{6,7},{7,6},{8,9},{9,8},{10,11... | collective-permute-start | bytes 393224 | tf_op jit(solution)/shard_map/ppermute | solution.py:235
  89.6 10.9 %all_to_all.6 = f32[32,1,64]{2,1,0:T(1,128)S(1)} all-to-all(f32[32,1,64]{2,1,0:T(1,128)S(1)} %bitcast.63), channel_id=1, replica_groups=mesh['dp'=4,'ctx'=8] {'dp','ctx'}, dimensions={0} | all-to-all | bytes 16384 | tf_op jit(solution)/shard_map/all_to_all | solution.py:288
  102.3 1.2 %copy-done.15 = f32[256,1024]{1,0:T(8,128)S(1)} copy-done((f32[256,1024]{1,0:T(8,128)S(1)}, f32[256,1024]{1,0:T(8,128)}, u32[]{:S(2)}) %copy-start.15) | copy-done | bytes 1048600
  103.5 2.9 %shard_map.120 = (bf16[256,2048]{1,0:T(8,128)(2,1)}, bf16[256,2048]{1,0:T(8,128)(2,1)}) custom-call(s32[1]{0:T(128)} %bitcast.core, bf16[256,2048]{1,0:T(8,128)(2,1)S(1)} %bitcast.50, bf16[256,2048]{1,0:T(8,128)(2,1)S(1)} %bitcast.59, f32[256,1024]{1,0:T(8,128)S(1)} %copy-done.14, f32[256,1024]{1,0:T(8,128)S(1)} %copy-done.15, s32[1,256]{1,0:T(1,128)S(1)} %copy-done, ...), custom_call_target="tpu_custom_call" | custom-call | flops 2415000064 | bytes 3145728 | tf_op jit(solution)/shard_map/pallas_call | solution.py:364
  106.5 2.8 %shard_map.121 = (bf16[256,2048]{1,0:T(8,128)(2,1)}, bf16[256,2048]{1,0:T(8,128)(2,1)}) custom-call(s32[1]{0:T(128)} %bitcast.core, bf16[256,2048]{1,0:T(8,128)(2,1)S(1)} %bitcast.51, bf16[256,2048]{1,0:T(8,128)(2,1)S(1)} %bitcast.60, f32[256,1024]{1,0:T(8,128)S(1)} %copy-done.12, ...), custom_call_target="tpu_custom_call", output_to_operand_aliasing={{0}: (10, {}), {1}: (11, {})} | custom-call | flops 2415000064 | bytes 3145728 | tf_op jit(solution)/shard_map/pallas_call | solution.py:364
  (94 shorter events, 16.4 us)
Async XLA Ops:
  2.3 3.3 %collective-permute-start.2 = (f32[256,128]{1,0:T(8,128)S(1)}, f32[256,128]{1,0:T(8,128)S(1)}, u32[]{:S(2)}, u32[]{:S(2)}) collective-permute-start(f32[256,128]{1,0:T(8,128)S(1)} %get-tuple-element.42), channel_id=1, source_target_pairs={{0,1},{1,0},{2,3},{3,2},{4,5},{5,4},{6,7},{7,6},{8,9},{9,8},{10,11... | collective-permute-start | bytes 393224 | tf_op jit(solution)/shard_map/ppermute | solution.py:235
  2.8 9.9 %copy-start.4 = (bf16[1,256,2048]{2,1,0:T(8,128)(2,1)S(1)}, bf16[1,256,2048]{2,1,0:T(8,128)(2,1)}, u32[]{:S(2)}) copy-start(bf16[1,256,2048]{2,1,0:T(8,128)(2,1)} %param.8) | copy-start | bytes 3145732
  4.5 6.0 %collective-permute-start = (f32[256,128]{1,0:T(8,128)S(1)}, f32[256,128]{1,0:T(8,128)S(1)}, u32[]{:S(2)}, u32[]{:S(2)}) collective-permute-start(f32[256,128]{1,0:T(8,128)S(1)} %get-tuple-element.40), channel_id=1, source_target_pairs={{0,1},{1,0},{2,3},{3,2},{4,5},{5,4},{6,7},{7,6},{8,9},{9,8},{10,11... | collective-permute-start | bytes 393224 | tf_op jit(solution)/shard_map/ppermute | solution.py:235
  5.6 11.3 %collective-permute-start.4 = (f32[256,128]{1,0:T(8,128)S(1)}, f32[256,128]{1,0:T(8,128)S(1)}, u32[]{:S(2)}, u32[]{:S(2)}) collective-permute-start(f32[256,128]{1,0:T(8,128)S(1)} %add.197.rest_1_), channel_id=1, source_target_pairs={{0,2},{1,3},{2,0},{3,1},{4,4},{5,5},{6,6},{7,7},{8,10},{9,11},{10,... | collective-permute-start | bytes 393224 | tf_op jit(solution)/shard_map/ppermute | solution.py:264
  10.6 7.2 %collective-permute-start.1 = (f32[256,128]{1,0:T(8,128)S(1)}, f32[256,128]{1,0:T(8,128)S(1)}, u32[]{:S(2)}, u32[]{:S(2)}) collective-permute-start(f32[256,128]{1,0:T(8,128)S(1)} %add.196.rest_0_), channel_id=1, source_target_pairs={{0,2},{1,3},{2,0},{3,1},{4,4},{5,5},{6,6},{7,7},{8,10},{9,11},{10,... | collective-permute-start | bytes 393224 | tf_op jit(solution)/shard_map/ppermute | solution.py:264
  15.6 12.7 %collective-permute-start.8 = (f32[4,264,128]{2,1,0:T(8,128)S(1)}, f32[4,264,128]{2,1,0:T(8,128)S(1)}, u32[]{:S(2)}, u32[]{:S(2)}) collective-permute-start(f32[4,264,128]{2,1,0:T(8,128)S(1)} %get-tuple-element.47), channel_id=1, source_target_pairs={{1,0},{2,1},{3,2},{4,3},{5,4},{6,5},{7,6},{9,8},{10,9},{11,10},{12... | collective-permute-start | bytes 1622024 | tf_op jit(solution)/shard_map/ppermute | solution.py:240
  17.8 4.5 %collective-permute-start.5 = (f32[256,128]{1,0:T(8,128)S(1)}, f32[256,128]{1,0:T(8,128)S(1)}, u32[]{:S(2)}, u32[]{:S(2)}) collective-permute-start(f32[256,128]{1,0:T(8,128)S(1)} %get-tuple-element.103.rest_1_), channel_id=1, source_target_pairs={{0,0},{1,1},{2,4},{3,5},{4,2},{5,3},{6,6},{7,7},{8,8},{9,9},{10,12... | collective-permute-start | bytes 393224 | tf_op jit(solution)/shard_map/ppermute | solution.py:264
  18.5 3.8 %collective-permute-start.3 = (f32[256,128]{1,0:T(8,128)S(1)}, f32[256,128]{1,0:T(8,128)S(1)}, u32[]{:S(2)}, u32[]{:S(2)}) collective-permute-start(f32[256,128]{1,0:T(8,128)S(1)} %get-tuple-element.104.rest_0_), channel_id=1, source_target_pairs={{0,0},{1,1},{2,4},{3,5},{4,2},{5,3},{6,6},{7,7},{8,8},{9,9},{10,12... | collective-permute-start | bytes 393224 | tf_op jit(solution)/shard_map/ppermute | solution.py:264
  22.3 4.4 %collective-permute-start.9 = (f32[256,128]{1,0:T(8,128)S(1)}, f32[256,128]{1,0:T(8,128)S(1)}, u32[]{:S(2)}, u32[]{:S(2)}) collective-permute-start(f32[256,128]{1,0:T(8,128)S(1)} %get-tuple-element.95.rest_0_), channel_id=1, source_target_pairs={{0,0},{1,1},{2,2},{3,3},{4,6},{5,7},{6,4},{7,5},{8,8},{9,9},{10,10... | collective-permute-start | bytes 393224 | tf_op jit(solution)/shard_map/ppermute | solution.py:264
  23.0 3.8 %collective-permute-start.6 = (f32[256,128]{1,0:T(8,128)S(1)}, f32[256,128]{1,0:T(8,128)S(1)}, u32[]{:S(2)}, u32[]{:S(2)}) collective-permute-start(f32[256,128]{1,0:T(8,128)S(1)} %get-tuple-element.77.rest_1_), channel_id=1, source_target_pairs={{0,0},{1,1},{2,2},{3,3},{4,6},{5,7},{6,4},{7,5},{8,8},{9,9},{10,10... | collective-permute-start | bytes 393224 | tf_op jit(solution)/shard_map/ppermute | solution.py:264
  26.9 1.4 %collective-permute-start.10 = (f32[256,128]{1,0:T(8,128)S(1)}, f32[256,128]{1,0:T(8,128)S(1)}, u32[]{:S(2)}, u32[]{:S(2)}) collective-permute-start(f32[256,128]{1,0:T(8,128)S(1)} %get-tuple-element.87), channel_id=1, source_target_pairs={{0,1},{1,0},{2,3},{3,2},{4,5},{5,4},{6,7},{7,6},{8,9},{9,8},{10,11... | collective-permute-start | bytes 393224 | tf_op jit(solution)/shard_map/ppermute | solution.py:235
  31.3 1.3 %collective-permute-start.11 = (f32[256,128]{1,0:T(8,128)S(1)}, f32[256,128]{1,0:T(8,128)S(1)}, u32[]{:S(2)}, u32[]{:S(2)}) collective-permute-start(f32[256,128]{1,0:T(8,128)S(1)} %get-tuple-element.50), channel_id=1, source_target_pairs={{0,1},{1,0},{2,3},{3,2},{4,5},{5,4},{6,7},{7,6},{8,9},{9,8},{10,11... | collective-permute-start | bytes 393224 | tf_op jit(solution)/shard_map/ppermute | solution.py:235
  31.6 1.3 %collective-permute-start.7 = (f32[256,128]{1,0:T(8,128)S(1)}, f32[256,128]{1,0:T(8,128)S(1)}, u32[]{:S(2)}, u32[]{:S(2)}) collective-permute-start(f32[256,128]{1,0:T(8,128)S(1)} %get-tuple-element.102), channel_id=1, source_target_pairs={{0,1},{1,0},{2,3},{3,2},{4,5},{5,4},{6,7},{7,6},{8,9},{9,8},{10,11... | collective-permute-start | bytes 393224 | tf_op jit(solution)/shard_map/ppermute | solution.py:235
  35.9 3.5 %collective-permute-start.13 = (f32[256,128]{1,0:T(8,128)S(1)}, f32[256,128]{1,0:T(8,128)}, u32[]{:S(2)}, u32[]{:S(2)}) collective-permute-start(f32[256,128]{1,0:T(8,128)S(1)} %get-tuple-element.56), channel_id=1, source_target_pairs={{0,1},{1,0},{2,3},{3,2},{4,5},{5,4},{6,7},{7,6},{8,9},{9,8},{10,11... | collective-permute-start | bytes 393224 | tf_op jit(solution)/shard_map/ppermute | solution.py:235
  36.1 11.9 %collective-permute-start.12 = (f32[256,128]{1,0:T(8,128)S(1)}, f32[256,128]{1,0:T(8,128)}, u32[]{:S(2)}, u32[]{:S(2)}) collective-permute-start(f32[256,128]{1,0:T(8,128)S(1)} %add.222.rest_0_), channel_id=1, source_target_pairs={{0,0},{1,1},{2,2},{3,3},{4,6},{5,7},{6,4},{7,5},{8,8},{9,9},{10,10... | collective-permute-start | bytes 393224 | tf_op jit(solution)/shard_map/ppermute | solution.py:264
  40.3 7.7 %collective-permute-start.15 = (f32[256,128]{1,0:T(8,128)S(1)}, f32[256,128]{1,0:T(8,128)S(1)}, u32[]{:S(2)}, u32[]{:S(2)}) collective-permute-start(f32[256,128]{1,0:T(8,128)S(1)} %add.223.rest_1_), channel_id=1, source_target_pairs={{0,0},{1,1},{2,2},{3,3},{4,6},{5,7},{6,4},{7,5},{8,8},{9,9},{10,10... | collective-permute-start | bytes 393224 | tf_op jit(solution)/shard_map/ppermute | solution.py:264
  44.8 56.2 %collective-permute-start.19 = (f32[4,264,128]{2,1,0:T(8,128)}, f32[4,264,128]{2,1,0:T(8,128)}, u32[]{:S(2)}, u32[]{:S(2)}) collective-permute-start(f32[4,264,128]{2,1,0:T(8,128)} %get-tuple-element.64), channel_id=1, source_target_pairs={{0,1},{1,2},{2,3},{3,4},{4,5},{5,6},{6,7},{8,9},{9,10},{10,11},{11... | collective-permute-start | bytes 1622024 | tf_op jit(solution)/shard_map/ppermute | solution.py:240
  48.0 7.3 %collective-permute-start.16 = (f32[256,128]{1,0:T(8,128)S(1)}, f32[256,128]{1,0:T(8,128)S(1)}, u32[]{:S(2)}, u32[]{:S(2)}) collective-permute-start(f32[256,128]{1,0:T(8,128)S(1)} %get-tuple-element.99.rest_1_), channel_id=1, source_target_pairs={{0,0},{1,1},{2,4},{3,5},{4,2},{5,3},{6,6},{7,7},{8,8},{9,9},{10,12... | collective-permute-start | bytes 393224 | tf_op jit(solution)/shard_map/ppermute | solution.py:264
  48.7 6.7 %collective-permute-start.14 = (f32[256,128]{1,0:T(8,128)S(1)}, f32[256,128]{1,0:T(8,128)S(1)}, u32[]{:S(2)}, u32[]{:S(2)}) collective-permute-start(f32[256,128]{1,0:T(8,128)S(1)} %get-tuple-element.100.rest_0_), channel_id=1, source_target_pairs={{0,0},{1,1},{2,4},{3,5},{4,2},{5,3},{6,6},{7,7},{8,8},{9,9},{10,12... | collective-permute-start | bytes 393224 | tf_op jit(solution)/shard_map/ppermute | solution.py:264
  55.4 31.6 %collective-permute-start.20 = (f32[256,128]{1,0:T(8,128)S(1)}, f32[256,128]{1,0:T(8,128)S(1)}, u32[]{:S(2)}, u32[]{:S(2)}) collective-permute-start(f32[256,128]{1,0:T(8,128)S(1)} %get-tuple-element.91.rest_0_), channel_id=1, source_target_pairs={{0,2},{1,3},{2,0},{3,1},{4,4},{5,5},{6,6},{7,7},{8,10},{9,11},{10,... | collective-permute-start | bytes 393224 | tf_op jit(solution)/shard_map/ppermute | solution.py:264
  78.9 8.1 %collective-permute-start.17 = (f32[256,128]{1,0:T(8,128)S(1)}, f32[256,128]{1,0:T(8,128)S(1)}, u32[]{:S(2)}, u32[]{:S(2)}) collective-permute-start(f32[256,128]{1,0:T(8,128)S(1)} %get-tuple-element.73.rest_1_), channel_id=1, source_target_pairs={{0,2},{1,3},{2,0},{3,1},{4,4},{5,5},{6,6},{7,7},{8,10},{9,11},{10,... | collective-permute-start | bytes 393224 | tf_op jit(solution)/shard_map/ppermute | solution.py:264
  87.0 14.0 %copy-start.8 = (bf16[1,256,2048]{2,1,0:T(8,128)(2,1)S(1)}, bf16[1,256,2048]{2,1,0:T(8,128)(2,1)}, u32[]{:S(2)}) copy-start(bf16[1,256,2048]{2,1,0:T(8,128)(2,1)} %param.9) | copy-start | bytes 3145732
  88.1 12.9 %collective-permute-start.21 = (f32[256,128]{1,0:T(8,128)S(1)}, f32[256,128]{1,0:T(8,128)S(1)}, u32[]{:S(2)}, u32[]{:S(2)}) collective-permute-start(f32[256,128]{1,0:T(8,128)S(1)} %get-tuple-element.83), channel_id=1, source_target_pairs={{0,1},{1,0},{2,3},{3,2},{4,5},{5,4},{6,7},{7,6},{8,9},{9,8},{10,11... | collective-permute-start | bytes 393224 | tf_op jit(solution)/shard_map/ppermute | solution.py:235
  101.1 5.4 %collective-permute-start.18 = (f32[256,128]{1,0:T(8,128)S(1)}, f32[256,128]{1,0:T(8,128)S(1)}, u32[]{:S(2)}, u32[]{:S(2)}) collective-permute-start(f32[256,128]{1,0:T(8,128)S(1)} %get-tuple-element.98), channel_id=1, source_target_pairs={{0,1},{1,0},{2,3},{3,2},{4,5},{5,4},{6,7},{7,6},{8,9},{9,8},{10,11... | collective-permute-start | bytes 393224 | tf_op jit(solution)/shard_map/ppermute | solution.py:235
  (19 other events, 64.3 us)

commit v6 on v4

--- a/solution.py
+++ b/solution.py
@@ -12,6 +12,7 @@
 GROUPS = 2
 EXTRA = 8
 VMEM = 10 * 2**20
+PINNED = ("block", "wide", "part")
 F32 = jnp.float32
 BF16 = jnp.bfloat16
 
@@ -75,7 +76,7 @@
 
 
 def states_kernel(group, core, k, v, *rest):
-    keep, send, k_buf, v_buf, sems = rest[-5:]
+    keep, send, zero, k_buf, v_buf, sems = rest[-6:]
     lanes = k_buf.shape[2]
     copies = []
     for half in (1, 0):
@@ -84,6 +85,7 @@
             copies.append(pltpu.make_async_copy(array.at[:, pl.ds(at, lanes)], buf.at[half], sems.at[half, i]))
     for copy in copies:
         copy.start()
+    zero[...] = jnp.zeros_like(zero)
     for half, out in ((1, send), (0, keep)):
         copies.pop(0).wait()
         copies.pop(0).wait()
@@ -92,12 +94,12 @@
             out[p * E:(p + 1) * E] = state_pair(k_buf[half, :, at], v_buf[half, :, at])
 
 
-def part_kernel(last, a, b, seg, table, *rest):
-    out = rest[-1]
+def part_kernel(a, b, seg, table, *rest):
+    out, token = rest[-2:]
+    token[...] = jnp.zeros_like(token)
     count = a.shape[1] // PAIR
-    rows, own, flag = edge(seg, table, last)
-    sel = rows.astype(F32) * jnp.where(flag == 1, 1.0, 0.0) if last else rows.astype(F32)
-    sel = sel.astype(BF16)
+    rows, own, _ = edge(seg, table, False)
+    sel = rows.astype(BF16)
     for p in range(count):
         out[0, p * E:(p + 1) * E] = state_pair(pair_at(a, p), pair_at(b, p) * sel)
     out[0, count * E:] = jnp.broadcast_to(own, (EXTRA, PAIR))
@@ -148,11 +150,13 @@
 
 
 def norm_kernel(core, q, dy, local, gain, seg, table, pre_keep, pre_recv, nxt, *rest):
-    out, dab, gsum, keep, send = rest[-5:]
+    out, dab, part, gsum, keep, send = rest[-6:]
     step = pl.program_id(0)
     count = q.shape[1] // PAIR
     prefix = jnp.where(step == 0, pre_keep[...], pre_recv[...])
     on_next = on_rows(seg, table, True, nxt, count)
+    last, own, flag = edge(seg, table, True)
+    last = (last.astype(F32) * jnp.where(flag == 1, 1.0, 0.0)).astype(BF16)
     pairs = [slice(p * PAIR, (p + 1) * PAIR) for p in range(count)]
     fars = [
         dot(twice(q[:, at]), side_by_side(rows_of(prefix, p), nxt[0, p * E:(p + 1) * E]), 1, 0)
@@ -168,21 +172,23 @@
         (scale * (ga - normed * mean)).astype(BF16)
         for scale, ga, normed, mean in zip(scales, gas, normeds, means)
     ]
-    states = [state_pair(q[:, at], da) for at, da in zip(pairs, das)]
-    for at, normed, da in zip(pairs, normeds, das):
+    states = [state_pair(q[:, at], jnp.concatenate([da, da * last], axis=1)) for at, da in zip(pairs, das)]
+    part[0, count * E:] = jnp.broadcast_to(own, (EXTRA, PAIR))
+    for p, (at, normed, da) in enumerate(zip(pairs, normeds, das)):
+        part[0, p * E:(p + 1) * E] = states[p][:, PAIR:]
         dab[:, at] = da
         out[:, at] = (normed * gain[:, at]).astype(BF16)
-        gsum[:, at] = jnp.sum(dy[:, at].astype(F32) * normed, axis=0, keepdims=True)
+        gsum[0, p:p + 1] = jnp.sum(dy[:, at].astype(F32) * normed, axis=0, keepdims=True)
 
     @pl.when(step == 0)
     def _():
         for p, state in enumerate(states):
-            keep[p * E:(p + 1) * E] = state
+            keep[p * E:(p + 1) * E] = state[:, :PAIR]
 
     @pl.when(step == 1)
     def _():
         for p, state in enumerate(states):
-            send[p * E:(p + 1) * E] = state
+            send[p * E:(p + 1) * E] = state[:, :PAIR]
 
 
 def inner_kernel(core, q, k, v, dab, mask, mask_t, seg, table, pre_keep, pre_recv, nxt, *rest):
@@ -214,7 +220,8 @@
 
 
 def outer_kernel(core, k, v, gk_in, gv_in, seg, table, suf_keep, suf_recv, prv, *rest):
-    gk, gv = rest[-2:]
+    gk, gv, token = rest[-3:]
+    token[...] = jnp.zeros_like(token)
     step = pl.program_id(0)
     count = k.shape[1] // PAIR
     suffix = jnp.where(step == 0, suf_keep[...], suf_recv[...])
@@ -239,35 +246,58 @@
     return lax.ppermute(x, "ctx", [(i, i + distance) for i in range(count) if 0 <= i + distance < count])
 
 
-def chips_before(owns, towards, works):
+def chip_rank(towards):
+    chip = lax.axis_index("ctx") // 2
+    return chip if towards == 1 else lax.axis_size("ctx") // 2 - 1 - chip
+
+
+def chips_before(own, towards):
     chips = lax.axis_size("ctx") // 2
-    if chips > 8:
-        for work in works:
-            work(owns)
-        totals = [shifted(own, 2 * towards) for own in owns]
-        span = 1
-        while span < chips:
-            totals = [total + shifted(total, 2 * towards * span) for total in totals]
-            span *= 2
-        return totals
-    befores = [None] * len(owns)
-    for hop in range(max(chips - 1, len(works))):
-        totals = [own if before is None else own + before for own, before in zip(owns, befores)]
-        source = hop if towards == 1 else chips - 1 - hop
-        token = works[hop](totals) if hop < len(works) else jnp.zeros((1, PAIR), F32)
-        if hop < chips - 1:
-            route = [(2 * source + c, 2 * (source + towards) + c) for c in range(2)]
-            arrived = [lax.ppermute(total, "ctx", route) + token for total in totals]
-            befores = [a if before is None else before + a for before, a in zip(befores, arrived)]
-    return befores
+    total = shifted(own, 2 * towards)
+    span = 1
+    while span < chips:
+        total = total + shifted(total, 2 * towards * span)
+        span *= 2
+    return total
+
+
+def pick(rank, cases):
+    value = cases[-1][1]
+    for at, case in cases[:-1]:
+        value = jnp.where(rank == at, case, value)
+    return value
+
+
+def chain_load(owns, arrived, step, towards):
+    chips = lax.axis_size("ctx") // 2
+    cases = [(step - g, own) for g, own in enumerate(owns) if 0 <= step - g <= chips - 2]
+    load = pick(chip_rank(towards), cases)
+    return load if arrived is None else load + arrived
+
+
+def chain_step(load, step, towards):
+    chips = lax.axis_size("ctx") // 2
+    route = []
+    for rank in range(chips - 1):
+        if 0 <= step - rank < GROUPS:
+            chip = rank if towards == 1 else chips - 1 - rank
+            route += [(2 * chip + c, 2 * (chip + towards) + c) for c in range(2)]
+    return lax.ppermute(load, "ctx", route)
+
+
+def chain_result(arrivals, group, towards):
+    chips = lax.axis_size("ctx") // 2
+    cases = [(rank, arrivals[group + rank - 1]) for rank in range(1, chips)]
+    return pick(chip_rank(towards), cases + [(0, jnp.zeros_like(arrivals[0]))])
 
 
 def within_chip(keep, send):
     received = partner(send, "ctx", 0)
-    return received, keep + received
-
-
-def to_cores(before, keep, received, towards):
+    return keep, received, keep + received
+
+
+def to_cores(before, piece, towards):
+    keep, received, _ = piece
     is_source = lax.axis_index("ctx") & 1 == (0 if towards == 1 else 1)
     mine = jnp.where(is_source, before, before + received)
     return mine, partner(jnp.where(is_source, before + keep, before), "ctx", 0)
@@ -277,28 +307,20 @@
     return pltpu.with_memory_space_constraint(x, pltpu.HBM)
 
 
-def scatter_sum(x):
-    axes = ("dp", "ctx")
-    terms = lax.all_gather(x[0], axes)
-    count = x.shape[1] // terms.shape[0]
-    own = lax.dynamic_slice_in_dim(terms, lax.axis_index(axes) * count, count, 1)
-    return jnp.sum(own, axis=0)
+def scatter_sum(x, axis):
+    for bit in reversed(range(lax.axis_size(axis).bit_length() - 1)):
+        upper = lax.axis_index(axis) >> bit & 1 == 1
+        low, high = jnp.split(x, 2, axis=0 if x.shape[0] > 1 else 1)
+        x = jnp.where(upper, high, low) + partner(jnp.where(upper, low, high), axis, bit)
+    return x
 
 
 def on_device(queries, keys, values, out_grad, segment_ids, image_flags, gain):
     rows, width = queries.shape[1:]
     q, k, v, dy = (x[0] for x in (queries, keys, values, out_grad))
-    seg = segment_ids[0]
     table = image_flags[0]
     gain_row = gain.reshape(1, width)
     core = (lax.axis_index("ctx") & 1).reshape(1).astype(jnp.int32)
-    onehot = seg[:, None] == jnp.arange(table.shape[0], dtype=jnp.int32)[None, :]
-    img = jnp.sum(jnp.where(onehot, table[None, :], 0), axis=1)
-    imgseg = jnp.where(img == 1, seg, -1)
-    pos = jnp.arange(rows)
-    mask = ((pos[:, None] >= pos[None, :]) | (imgseg[:, None] == seg[None, :])).astype(BF16)
-    mask_t = ((pos[:, None] <= pos[None, :]) | (seg[:, None] == imgseg[None, :])).astype(BF16)
-
     lanes = width // GROUPS // 2
     half_rows = lanes // PAIR * E
     heads = lanes // E
@@ -323,7 +345,8 @@
             "wide": pl.BlockSpec((rows, lanes), wide),
             "block": pl.BlockSpec((rows, lanes), own),
             "row": pl.BlockSpec((1, lanes), wide),
-            "rowblock": pl.BlockSpec((1, lanes), own),
+            "sums": pl.BlockSpec((1, lanes // PAIR, PAIR), part),
+            "zero": pl.BlockSpec((1, rows), whole),
             "half": pl.BlockSpec((half_rows, PAIR), whole),
             "part": pl.BlockSpec((1, half_rows + EXTRA, PAIR), part),
             "seg": pl.BlockSpec((1, rows), whole),
@@ -338,7 +361,8 @@
         shapes = {
             "wide": (rows, width),
             "block": (rows, 2 * lanes),
-            "rowblock": (1, 2 * lanes),
+            "sums": (2 * GROUPS, lanes // PAIR, PAIR),
+            "zero": (1, rows),
             "half": (half_rows, PAIR),
             "part": (2 * GROUPS, half_rows + EXTRA, PAIR),
             "token": (1, PAIR),
@@ -352,7 +376,7 @@
                 operands.append(x)
                 kinds.append("any")
         out_shape = [
-            pltpu.HBM(shapes[kind], dtype) if kind in ("block", "wide") else jax.ShapeDtypeStruct(shapes[kind], dtype)
+            pltpu.HBM(shapes[kind], dtype) if kind in PINNED and (kind != "block" or len(outs) == 2) else jax.ShapeDtypeStruct(shapes[kind], dtype)
             for kind, dtype in outs
         ]
         moved = sum(rows * 2 * lanes * 2 for kind in kinds if kind in ("wide", "block"))
@@ -374,78 +398,111 @@
 
     edges = [("seg", segment_ids), ("table", image_flags)]
     groups = range(GROUPS)
-
-    def phase(pieces, towards, works):
-        befores = chips_before([own for _, _, own in pieces], towards, works)
-        return [to_cores(before, keep, received, towards) for before, (keep, received, _) in zip(befores, pieces)]
-
-    pieces = []
+    chips = lax.axis_size("ctx") // 2
+    chained = GROUPS < chips <= 8
     buffers = [pltpu.VMEM((2, rows, lanes), BF16)] * 2 + [pltpu.SemaphoreType.DMA((2, 2))]
+
+    def own_states(g, after):
+        keep, send, zero = call(
+            functools.partial(states_kernel, g), g, [("hbm", in_hbm(k)), ("hbm", in_hbm(v))],
+            [("half", F32), ("half", F32), ("zero", jnp.int32)], 1.2, after=after, scratch=buffers, steps=(1,))
+        return within_chip(keep, send), zero
+
+    def local_attn(g, after):
+        return call(
+            local_kernel, g, [("wide", q), ("wide", k), ("wide", v), ("mask", mask)],
+            [("block", F32), ("token", F32)], 2.3, after=after)
+
+    def norm(g, prefix, before, after):
+        output, dab, prv, gsum, keep, send = call(
+            norm_kernel, g,
+            [("wide", q), ("wide", dy), ("block", local[g][0]), ("row", gain_row), *edges,
+             ("half", prefix[0]), ("half", prefix[1]), ("part", nxt)],
+            [("wide", BF16), ("wide", BF16), ("part", F32), ("sums", F32), ("half", F32), ("half", F32)],
+            3.0, after=after, alias=list(enumerate(before)))
+        return (output, dab, prv, gsum), within_chip(keep, send)
+
+    def inner(g, before, after):
+        return call(
+            inner_kernel, g,
+            [("wide", q), ("wide", k), ("wide", v), ("wide", in_hbm(dab)), ("mask", mask), ("mask", mask_t), *edges,
+             ("half", prefix[g][0]), ("half", prefix[g][1]), ("part", nxt)],
+            [("wide", BF16), ("block", F32), ("block", F32), ("token", F32)], 6.0, after=after, alias=[(0, before)])
+
+    def outer(g, suffix, before, after):
+        return call(
+            outer_kernel, g,
+            [("wide", k), ("wide", v), ("block", inners[g][1]), ("block", inners[g][2]), *edges,
+             ("half", suffix[0]), ("half", suffix[1]), ("part", prv)],
+            [("wide", BF16), ("wide", BF16), ("token", F32)], 2.1, after=after, alias=list(enumerate(before)))
+
+    steps = chips - 2 + GROUPS
+    owns, arrivals, local, prefix = [], [], [], []
+    piece, zero = own_states(0, [])
+    owns.append(piece)
+    for g in groups[1:]:
+        piece, zero = own_states(g, [owns[0][2]])
+        owns.append(piece)
+    seg = (segment_ids + zero)[0]
+    onehot = seg[:, None] == jnp.arange(table.shape[0], dtype=jnp.int32)[None, :]
+    img = jnp.sum(jnp.where(onehot, table[None, :], 0), axis=1)
+    imgseg = jnp.where(img == 1, seg, -1)
+    pos = jnp.arange(rows)
+    mask = ((pos[:, None] >= pos[None, :]) | (imgseg[:, None] == seg[None, :])).astype(BF16)
+    mask_t = ((pos[:, None] <= pos[None, :]) | (seg[:, None] == imgseg[None, :])).astype(BF16)
+    sums = [piece[2] for piece in owns]
+    load = chain_load(sums, None, 0, 1) if chained else sums[0]
+    local.append(local_attn(0, [load, sums[-1]]))
+    token = local[0][1]
+    nexts = None
+    for step in range(steps if chained else GROUPS):
+        if chained:
+            arrivals.append(chain_step(load, step, 1))
+        if step + 1 < steps and chained:
+            load = chain_load(sums, arrivals[-1] + token, step + 1, 1)
+        if step == 0:
+            nexts, token = call(
+                part_kernel, 0, [("wide", k), ("wide", v), *edges],
+                [("part", F32), ("token", F32)], 2.0, after=[load], steps=(2 * GROUPS,), prefetch=False)
+            nxt = shifted(nexts, -1)
+        elif step < GROUPS:
+            local.append(local_attn(step, [load, nexts]))
+            token = local[step][1]
+        else:
+            token = jnp.zeros((1, PAIR), F32)
+    befores = [chain_result(arrivals, g, 1) if chained else chips_before(sums[g], 1) for g in groups]
+    prefix = [to_cores(before, piece, 1) for before, piece in zip(befores, owns)]
+
+    norms, owns, arrivals = [None] * 4, [], []
     for g in groups:
-        keep, send = call(
-            functools.partial(states_kernel, g), g, [("hbm", in_hbm(k)), ("hbm", in_hbm(v))],
-            [("half", F32), ("half", F32)], 1.2, scratch=buffers, steps=())
-        pieces.append((keep, *within_chip(keep, send)))
-
-    found = {}
-
-    def early_work(g):
-        def work(totals):
-            if g == 0:
-                found["nxt"], = call(
-                    functools.partial(part_kernel, False), 0, [("wide", k), ("wide", v), *edges],
-                    [("part", F32)], 2.0, after=totals, steps=(2 * GROUPS,), prefetch=False)
-                totals = [found["nxt"]]
-            found["local", g], token = call(
-                local_kernel, g, [("wide", q), ("wide", k), ("wide", v), ("mask", mask)],
-                [("block", F32), ("token", F32)], 2.3, after=totals)
-            return token
-        return work
-
-    prefix = phase(pieces, 1, [early_work(g) for g in groups])
-    nxt = shifted(found["nxt"], -1)
-
-    output = dab = grad_q = grad_k = grad_v = None
-    pieces, gsums = [], []
+        norms, piece = norm(g, prefix[g], norms, [piece[2] for piece in owns])
+        owns.append(piece)
+    output, dab, prv, gsum = norms
+    prv = shifted(prv, 1)
+    sums = [piece[2] for piece in owns]
+    inners, outers, suffix = [], [None] * 2, []
+    token = None
+    for step in range(steps if chained else GROUPS):
+        if chained:
+            arrived = arrivals[-1] if arrivals else None
+            load = chain_load(sums, arrived if token is None else arrived + token, step, -1)
+            arrivals.append(chain_step(load, step, -1))
+        else:
+            load = sums[-1]
+        if 1 <= step <= GROUPS:
+            inners.append(inner(step - 1, inners[-1][0] if inners else None, [load, norms[2]]))
+            token = inners[-1][3]
+    while len(inners) < GROUPS:
+        inners.append(inner(len(inners), inners[-1][0] if inners else None, [load]))
+    gain_sum = scatter_sum(gsum.reshape(-1, PAIR) + inners[0][3], "dp")
+    grad_gain = scatter_sum(gain_sum + inners[-1][3], "ctx").reshape(-1)
+    grad_q = inners[-1][0]
     for g in groups:
-        output, dab, gsum, keep, send = call(
-            norm_kernel, g,
-            [("wide", q), ("wide", dy), ("block", found["local", g]), ("row", gain_row), *edges,
-             ("half", prefix[g][0]), ("half", prefix[g][1]), ("part", nxt)],
-            [("wide", BF16), ("wide", BF16), ("rowblock", F32), ("half", F32), ("half", F32)],
-            3.0, after=[own for _, _, own in pieces], alias=[(0, output), (1, dab)])
-        gsums.append(gsum)
-        pieces.append((keep, *within_chip(keep, send)))
-
-    def late_work(g):
-        def work(totals):
-            if g == 0:
-                found["prv"], = call(
-                    functools.partial(part_kernel, True), 0, [("wide", q), ("wide", dab), *edges],
-                    [("part", F32)], 2.0, after=totals, steps=(2 * GROUPS,), prefetch=False)
-                totals = [found["prv"]]
-            found["gq"], gk, gv, token = call(
-                inner_kernel, g,
-                [("wide", q), ("wide", k), ("wide", v), ("wide", dab), ("mask", mask), ("mask", mask_t), *edges,
-                 ("half", prefix[g][0]), ("half", prefix[g][1]), ("part", nxt)],
-                [("wide", BF16), ("block", F32), ("block", F32), ("token", F32)],
-                5.5, after=totals, alias=[(0, found.get("gq"))])
-            found["inner", g] = gk, gv
-            return token
-        return work
-
-    suffix = phase(pieces, -1, [late_work(g) for g in groups])
-    prv = shifted(found["prv"], 1)
-    grad_q = found["gq"]
-    grad_gain = scatter_sum(jnp.concatenate(gsums, axis=1))
-    for g in groups:
-        gk, gv = found["inner", g]
-        grad_k, grad_v = call(
-            outer_kernel, g,
-            [("wide", k), ("wide", v), ("block", gk), ("block", gv), *edges,
-             ("half", suffix[g][0]), ("half", suffix[g][1]), ("part", prv)],
-            [("wide", BF16), ("wide", BF16)],
-            2.1, alias=[(0, grad_k), (1, grad_v)])
+        if g and chained:
+            arrivals[-1] = arrivals[-1] + token
+        before = chain_result(arrivals, g, -1) if chained else chips_before(sums[g], -1)
+        *outers, token = outer(g, to_cores(before, owns[g], -1), outers, [])
+    grad_k, grad_v = outers
     return output[None], grad_q[None], grad_k[None], grad_v[None], grad_gain
 
 

time: 130 us -> 117 us (0.900)
  blocking collectives: 53.7 us -> 0 us
  starting transfers between devices: 20.8 us -> 43.6 us
  waiting for transfers between devices: 8.08 us -> 18.8 us
  local copies, waits for them, and re-layouts: 3.86 us -> 12 us
  Pallas kernels: 39.4 us -> 37.9 us
    all_gather x1 -> x0, blocking collectives: 53.7 us -> none  [scatter_sum(): terms = lax.all_gather(x[0], axes)]
    ppermute x8 -> x13, starting transfers between devices: 3.04 us -> 26.9 us  [partner(): return lax.ppermute(x, axis, route)]
    ppermute x8 -> x13, waiting for transfers between devices: 2.17 us -> 10.7 us  [partner(): return lax.ppermute(x, axis, route)]
    unnamed x40 -> x60, local copies, waits for them, and re-layouts: 3.86 us -> 12 us
    ppermute x12 -> x8, waiting for transfers between devices: 5.91 us -> 7.9 us  [chain_step(): return lax.ppermute(load, 'ctx', route)]
    pallas_call x12 -> x11, Pallas kernels: 39.4 us -> 37.9 us  [call(): pl.pallas_call(kernel, grid_spec=pltpu.PrefetchScalarGridSpec(num_scalar_...]
    ppermute x12 -> x8, starting transfers between devices: 14.4 us -> 13 us  [chain_step(): return lax.ppermute(load, 'ctx', route)]
  transfers between devices with their start and end apart: 22 -> 23, of which waited for: 5 -> 11; matrix products, arithmetic and copies ran while one was open for 1% -> 2% of each run, Pallas kernels for 25% -> 19%
where the time goes in v6:
time: 117 us; the launch traced here: 116 us
  starting transfers between devices  43.6 us (37%)
  Pallas kernels  37.9 us (32%)
  waiting for transfers between devices  18.8 us (16%)
  local copies, waits for them, and re-layouts  12 us (10%)
  other arithmetic  2.97 us (3%)
    pallas_call x11, Pallas kernels, call(): pl.pallas_call(kernel, grid_spec=pltpu.PrefetchScalarGridSpec(num_scalar_...  37.9 us
    ppermute x13, starting transfers between devices, partner(): return lax.ppermute(x, axis, route)  26.9 us
    ppermute x8, starting transfers between devices, chain_step(): return lax.ppermute(load, 'ctx', route)  13 us
    unnamed x60, local copies, waits for them, and re-layouts  12 us
    ppermute x13, waiting for transfers between devices, partner(): return lax.ppermute(x, axis, route)  10.7 us
    ppermute x8, waiting for transfers between devices, chain_step(): return lax.ppermute(load, 'ctx', route)  7.9 us
    ppermute x2, starting transfers between devices, shifted(): lax.ppermute(x, 'ctx', [(i, i + distance) for i in range(count) if 0 <= i...  3.71 us
  transfers between devices with their start and end apart: 23, of which 11 were waited for; matrix products, arithmetic and copies ran while one was open for 2% of the time, Pallas kernels for 19%

profile of v6, /device:TPU:0, one launch (start us, length us, event | category | flops | bytes accessed | tf_op | source)
XLA Modules:
  0.0 116.4 jit_solution(2279146240310022544)
XLA Ops:
  0.6 1.9 %shard_map.110 = (f32[256,128]{1,0:T(8,128)S(1)}, f32[256,128]{1,0:T(8,128)S(1)}, s32[1,256]{1,0:T(1,128)}) custom-call(s32[1]{0:T(128)} %bitcast.core, bf16[256,2048]{1,0:T(8,128)(2,1)} %bitcast.40, bf16[256,2048]{1,0:T(8,128)(2,1)} %bitcast.49), custom_call_target="tpu_custom_call" | custom-call | flops 1380000000 | tf_op jit(solution)/shard_map/pallas_call | solution.py:384
  4.1 1.8 %shard_map.111 = (f32[256,128]{1,0:T(8,128)S(1)}, f32[256,128]{1,0:T(8,128)S(1)}, s32[1,256]{1,0:T(1,128)S(1)}) custom-call(s32[1]{0:T(128)} %bitcast.core, bf16[256,2048]{1,0:T(8,128)(2,1)} %bitcast.41, bf16[256,2048]{1,0:T(8,128)(2,1)} %bitcast.50, f32[256,128]{1,0:T(8,128)S(1)} %add.149.rest_0_), custom_call_target="tpu_custom_call" | custom-call | flops 1380000000 | tf_op jit(solution)/shard_map/pallas_call | solution.py:384
  5.9 4.8 %collective-permute-start.2 = (f32[256,128]{1,0:T(8,128)S(1)}, f32[256,128]{1,0:T(8,128)S(1)}, u32[]{:S(2)}, u32[]{:S(2)}) collective-permute-start(f32[256,128]{1,0:T(8,128)S(1)} %add.149.rest_0_), channel_id=1, source_target_pairs={{0,2},{1,3},{8,10},{9,11},{16,18},{17,19},{24,26},{25,27}} | collective-permute-start | bytes 393224 | tf_op jit(solution)/shard_map/ppermute | solution.py:285
  12.4 3.1 %shard_map.112 = (f32[256,1024]{1,0:T(8,128)}, f32[1,128]{1,0:T(1,128)S(1)}) custom-call(s32[1]{0:T(128)} %bitcast.core, bf16[256,2048]{1,0:T(8,128)(2,1)S(1)} %bitcast.34, bf16[256,2048]{1,0:T(8,128)(2,1)S(1)} %bitcast.42, bf16[256,2048]{1,0:T(8,128)(2,1)S(1)} %bitcast.51, bf16[256,256]{1,0:T(8,128)(2,1)S(1)} %get-tuple-element.93.mask, ...), custom_call_target="tpu_custom_call" | custom-call | flops 2644999936 | bytes 2097152 | tf_op jit(solution)/shard_map/pallas_call | solution.py:384
  15.5 2.7 %collective-permute-start.3 = (f32[256,128]{1,0:T(8,128)S(1)}, f32[256,128]{1,0:T(8,128)S(1)}, u32[]{:S(2)}, u32[]{:S(2)}) collective-permute-start(f32[256,128]{1,0:T(8,128)S(1)} %add_add_fusion.4.rest_0_), channel_id=1, source_target_pairs={{0,2},{1,3},{2,4},{3,5},{8,10},{9,11},{10,12},{11,13},{16,18},{17,... | collective-permute-start | bytes 393224 | tf_op jit(solution)/shard_map/ppermute | solution.py:285
  18.2 2.6 %shard_map.113 = (f32[4,264,128]{2,1,0:T(8,128)}, f32[1,128]{1,0:T(1,128)S(1)}) custom-call(bf16[256,2048]{1,0:T(8,128)(2,1)S(1)} %bitcast.43, bf16[256,2048]{1,0:T(8,128)(2,1)S(1)} %bitcast.52, s32[1,256]{1,0:T(1,128)S(1)} %copy-done, s32[1,32]{1,0:T(1,128)S(1)} %copy-done.1, f32[256,128]{1,0:T(8,128)S(1)} %add_add_fusion.4.rest_0_), custom_call_target="tpu_custom_call" | custom-call | flops 2300000000 | bytes 1048576 | tf_op jit(solution)/shard_map/pallas_call | solution.py:384
  21.6 3.7 %shard_map.114 = (f32[256,1024]{1,0:T(8,128)}, f32[1,128]{1,0:T(1,128)S(1)}) custom-call(s32[1]{0:T(128)} %bitcast.core, bf16[256,2048]{1,0:T(8,128)(2,1)S(1)} %bitcast.35, bf16[256,2048]{1,0:T(8,128)(2,1)S(1)} %bitcast.44, bf16[256,2048]{1,0:T(8,128)(2,1)S(1)} %bitcast.53, bf16[256,256]{1,0:T(8,128)(2,1)S(1)} %get-tuple-element.93.mask, ...), custom_call_target="tpu_custom_call" | custom-call | flops 2644999936 | bytes 2097152 | tf_op jit(solution)/shard_map/pallas_call | solution.py:384
  28.8 1.3 %collective-permute-done.8.pre_recv = f32[256,128]{1,0:T(8,128)S(1)} collective-permute-done((f32[256,128]{1,0:T(8,128)S(1)}, f32[256,128]{1,0:T(8,128)S(1)}, u32[]{:S(2)}, u32[]{:S(2)}) %collective-permute-start.8) | collective-permute-done | bytes 131104 | tf_op jit(solution)/shard_map/ppermute | solution.py:241
  30.3 3.9 %shard_map.115 = (bf16[256,2048]{1,0:T(8,128)(2,1)}, bf16[256,2048]{1,0:T(8,128)(2,1)}, f32[4,264,128]{2,1,0:T(8,128)}, f32[4,4,128]{2,1,0:T(4,128)S(1)}, f32[25...) custom-call(s32[1]{0:T(128)} %bitcast.core, bf16[256,2048]{1,0:T(8,128)(2,1)S(1)} %bitcast.36, bf16[256,2048]{1,0:T(8,128)(2,1)S(1)} %bitcast.32, ...), custom_call_target="tpu_custom_call" | custom-call | flops 3449999872 | bytes 2621440 | tf_op jit(solution)/shard_map/pallas_call | solution.py:384
  34.2 8.9 %collective-permute-start.9 = (f32[256,128]{1,0:T(8,128)S(1)}, f32[256,128]{1,0:T(8,128)S(1)}, u32[]{:S(2)}, u32[]{:S(2)}) collective-permute-start(f32[256,128]{1,0:T(8,128)S(1)} %get-tuple-element.53), channel_id=1, source_target_pairs={{0,1},{1,0},{2,3},{3,2},{4,5},{5,4},{6,7},{7,6},{8,9},{9,8},{10,11... | collective-permute-start | bytes 393224 | tf_op jit(solution)/shard_map/ppermute | solution.py:241
  44.7 3.8 %shard_map.116 = (bf16[256,2048]{1,0:T(8,128)(2,1)}, bf16[256,2048]{1,0:T(8,128)(2,1)}, f32[4,264,128]{2,1,0:T(8,128)}, f32[4,4,128]{2,1,0:T(4,128)S(1)}, f32[25...) custom-call(s32[1]{0:T(128)} %bitcast.core, ...), custom_call_target="tpu_custom_call", output_to_operand_aliasing={{0}: (11, {}), {1}: (12, {}), {2}: (13, {}), {3}: (14, {})} | custom-call | flops 3449999872 | bytes 2621440 | tf_op jit(solution)/shard_map/pallas_call | solution.py:384
  53.1 6.5 %shard_map.117 = (bf16[256,2048]{1,0:T(8,128)(2,1)}, f32[256,1024]{1,0:T(8,128)S(1)}, f32[256,1024]{1,0:T(8,128)S(1)}, f32[1,128]{1,0:T(1,128)S(1)}) custom-call(s32[1]{0:T(128)} %bitcast.core, bf16[256,2048]{1,0:T(8,128)(2,1)S(1)} %bitcast.38, bf16[256,2048]{1,0:T(8,128)(2,1)S(1)} %bitcast.45, bf16[256,2048]{1,0:T(8,128)(2,1)S(1)} %bitcast.54, ...), custom_call_target="tpu_custom_call" | custom-call | flops 6899999744 | bytes 3670016 | tf_op jit(solution)/shard_map/pallas_call | solution.py:384
  61.6 1.5 %collective-permute-start.18 = (f32[8,128]{1,0:T(8,128)S(1)}, f32[8,128]{1,0:T(8,128)S(1)}, u32[]{:S(2)}, u32[]{:S(2)}) collective-permute-start(f32[8,128]{1,0:T(8,128)S(1)} %slice_select_fusion), channel_id=1, source_target_pairs={{0,16},{8,24},{16,0},{24,8},{1,17},{9,25},{17,1},{25,9},{2,18},{10... | collective-permute-start | bytes 12296 | tf_op jit(solution)/shard_map/ppermute | solution.py:241
  65.2 1.5 %collective-permute-start.19 = (f32[4,128]{1,0:T(4,128)S(1)}, f32[4,128]{1,0:T(4,128)S(1)}, u32[]{:S(2)}, u32[]{:S(2)}) collective-permute-start(f32[4,128]{1,0:T(4,128)S(1)} %slice_select_fusion.1), channel_id=1, source_target_pairs={{0,8},{8,0},{16,24},{24,16},{1,9},{9,1},{17,25},{25,17},{2,10},{10... | collective-permute-start | bytes 6152 | tf_op jit(solution)/shard_map/ppermute | solution.py:241
  68.9 6.5 %shard_map.118 = (bf16[256,2048]{1,0:T(8,128)(2,1)}, f32[256,1024]{1,0:T(8,128)S(1)}, f32[256,1024]{1,0:T(8,128)S(1)}, f32[1,128]{1,0:T(1,128)S(1)}) custom-call(s32[1]{0:T(128)} %bitcast.core, bf16[256,2048]{1,0:T(8,128)(2,1)S(1)} %bitcast.39, bf16[256,2048]{1,0:T(8,128)(2,1)S(1)} %bitcast.46, ...), custom_call_target="tpu_custom_call", output_to_operand_aliasing={{0}: (14, {})} | custom-call | flops 6899999744 | bytes 3670016 | tf_op jit(solution)/shard_map/pallas_call | solution.py:384
  77.4 11.8 %collective-permute-start.20 = (f32[2,128]{1,0:T(2,128)S(1)}, f32[2,128]{1,0:T(2,128)S(1)}, u32[]{:S(2)}, u32[]{:S(2)}) collective-permute-start(f32[2,128]{1,0:T(2,128)S(1)} %broadcast_select_fusion), channel_id=1, source_target_pairs={{0,4},{1,5},{2,6},{3,7},{4,0},{5,1},{6,2},{7,3},{8,12},{9,13},{10,... | collective-permute-start | bytes 3080 | tf_op jit(solution)/shard_map/ppermute | solution.py:241
  89.2 1.5 %collective-permute-done.20 = f32[2,128]{1,0:T(2,128)S(1)} collective-permute-done((f32[2,128]{1,0:T(2,128)S(1)}, f32[2,128]{1,0:T(2,128)S(1)}, u32[]{:S(2)}, u32[]{:S(2)}) %collective-permute-start.20) | collective-permute-done | bytes 1056 | tf_op jit(solution)/shard_map/ppermute | solution.py:241
  91.5 3.0 %collective-permute-done.21 = f32[1,128]{1,0:T(1,128)S(1)} collective-permute-done((f32[1,128]{1,0:T(1,128)S(1)}, f32[1,128]{1,0:T(1,128)S(1)}, u32[]{:S(2)}, u32[]{:S(2)}) %collective-permute-start.21) | collective-permute-done | bytes 544 | tf_op jit(solution)/shard_map/ppermute | solution.py:241
  94.5 2.4 %collective-permute-start.16 = (f32[4,264,128]{2,1,0:T(8,128)}, f32[4,264,128]{2,1,0:T(8,128)S(1)}, u32[]{:S(2)}, u32[]{:S(2)}) collective-permute-start(f32[4,264,128]{2,1,0:T(8,128)} %get-tuple-element.62.rest_1_), channel_id=1, source_target_pairs={{0,1},{1,2},{2,3},{3,4},{4,5},{5,6},{6,7},{8,9},{9,10},{10,11},{11... | collective-permute-start | bytes 1622024 | tf_op jit(solution)/shard_map/ppermute | solution.py:246
  98.8 6.1 %collective-permute-done.13 = f32[256,128]{1,0:T(8,128)S(1)} collective-permute-done((f32[256,128]{1,0:T(8,128)S(1)}, f32[256,128]{1,0:T(8,128)S(1)}, u32[]{:S(2)}, u32[]{:S(2)}) %collective-permute-start.13) | collective-permute-done | bytes 131104 | tf_op jit(solution)/shard_map/ppermute | solution.py:285
  109.0 2.1 %shard_map.119 = (bf16[256,2048]{1,0:T(8,128)(2,1)}, bf16[256,2048]{1,0:T(8,128)(2,1)}, f32[1,128]{1,0:T(1,128)S(1)}) custom-call(s32[1]{0:T(128)} %bitcast.core, bf16[256,2048]{1,0:T(8,128)(2,1)S(1)} %bitcast.47, bf16[256,2048]{1,0:T(8,128)(2,1)S(1)} %bitcast.56, f32[256,1024]{1,0:T(8,128)S(1)} %copy-done.19, f32[256,1024]{1,0:T(8,128)S(1)} %copy-done.21, ...), custom_call_target="tpu_custom_call" | custom-call | flops 2415000064 | bytes 3145728 | tf_op jit(solution)/shard_map/pallas_call | solution.py:384
  111.0 1.8 %collective-permute-done.14 = f32[256,128]{1,0:T(8,128)S(1)} collective-permute-done((f32[256,128]{1,0:T(8,128)S(1)}, f32[256,128]{1,0:T(8,128)S(1)}, u32[]{:S(2)}, u32[]{:S(2)}) %collective-permute-start.14) | collective-permute-done | bytes 131104 | tf_op jit(solution)/shard_map/ppermute | solution.py:285
  113.0 1.3 %collective-permute-done.17.suf_recv = f32[256,128]{1,0:T(8,128)S(1)} collective-permute-done((f32[256,128]{1,0:T(8,128)S(1)}, f32[256,128]{1,0:T(8,128)S(1)}, u32[]{:S(2)}, u32[]{:S(2)}) %collective-permute-start.17) | collective-permute-done | bytes 131104 | tf_op jit(solution)/shard_map/ppermute | solution.py:241
  114.3 2.1 %shard_map.120 = (bf16[256,2048]{1,0:T(8,128)(2,1)}, bf16[256,2048]{1,0:T(8,128)(2,1)}, f32[1,128]{1,0:T(1,128)}) custom-call(s32[1]{0:T(128)} %bitcast.core, bf16[256,2048]{1,0:T(8,128)(2,1)S(1)} %bitcast.48, bf16[256,2048]{1,0:T(8,128)(2,1)S(1)} %bitcast.57, f32[256,1024]{1,0:T(8,128)S(1)} %copy-done.15, ...), custom_call_target="tpu_custom_call", output_to_operand_aliasing={{0}: (10, {}), {1}: (11, {})} | custom-call | flops 2415000064 | bytes 3145728 | tf_op jit(solution)/shard_map/pallas_call | solution.py:384
  (124 shorter events, 28.6 us)
Async XLA Ops:
  2.6 1.5 %collective-permute-start = (f32[256,128]{1,0:T(8,128)S(1)}, f32[256,128]{1,0:T(8,128)S(1)}, u32[]{:S(2)}, u32[]{:S(2)}) collective-permute-start(f32[256,128]{1,0:T(8,128)S(1)} %get-tuple-element.42), channel_id=1, source_target_pairs={{0,1},{1,0},{2,3},{3,2},{4,5},{5,4},{6,7},{7,6},{8,9},{9,8},{10,11... | collective-permute-start | bytes 393224 | tf_op jit(solution)/shard_map/ppermute | solution.py:241
  5.9 9.6 %collective-permute-start.2 = (f32[256,128]{1,0:T(8,128)S(1)}, f32[256,128]{1,0:T(8,128)S(1)}, u32[]{:S(2)}, u32[]{:S(2)}) collective-permute-start(f32[256,128]{1,0:T(8,128)S(1)} %add.149.rest_0_), channel_id=1, source_target_pairs={{0,2},{1,3},{8,10},{9,11},{16,18},{17,19},{24,26},{25,27}} | collective-permute-start | bytes 393224 | tf_op jit(solution)/shard_map/ppermute | solution.py:285
  10.8 1.6 %collective-permute-start.1 = (f32[256,128]{1,0:T(8,128)S(1)}, f32[256,128]{1,0:T(8,128)S(1)}, u32[]{:S(2)}, u32[]{:S(2)}) collective-permute-start(f32[256,128]{1,0:T(8,128)S(1)} %get-tuple-element.45), channel_id=1, source_target_pairs={{0,1},{1,0},{2,3},{3,2},{4,5},{5,4},{6,7},{7,6},{8,9},{9,8},{10,11... | collective-permute-start | bytes 393224 | tf_op jit(solution)/shard_map/ppermute | solution.py:241
  15.5 5.3 %collective-permute-start.3 = (f32[256,128]{1,0:T(8,128)S(1)}, f32[256,128]{1,0:T(8,128)S(1)}, u32[]{:S(2)}, u32[]{:S(2)}) collective-permute-start(f32[256,128]{1,0:T(8,128)S(1)} %add_add_fusion.4.rest_0_), channel_id=1, source_target_pairs={{0,2},{1,3},{2,4},{3,5},{8,10},{9,11},{10,12},{11,13},{16,18},{17,... | collective-permute-start | bytes 393224 | tf_op jit(solution)/shard_map/ppermute | solution.py:285
  20.9 4.4 %collective-permute-start.4 = (f32[256,128]{1,0:T(8,128)S(1)}, f32[256,128]{1,0:T(8,128)S(1)}, u32[]{:S(2)}, u32[]{:S(2)}) collective-permute-start(f32[256,128]{1,0:T(8,128)S(1)} %add_add_fusion.3.rest_0_), channel_id=1, source_target_pairs={{2,4},{3,5},{4,6},{5,7},{10,12},{11,13},{12,14},{13,15},{18,20},{1... | collective-permute-start | bytes 393224 | tf_op jit(solution)/shard_map/ppermute | solution.py:285
  25.3 2.1 %collective-permute-start.5 = (f32[256,128]{1,0:T(8,128)S(1)}, f32[256,128]{1,0:T(8,128)S(1)}, u32[]{:S(2)}, u32[]{:S(2)}) collective-permute-start(f32[256,128]{1,0:T(8,128)S(1)} %add_add_fusion.2), channel_id=1, source_target_pairs={{4,6},{5,7},{12,14},{13,15},{20,22},{21,23},{28,30},{29,31}} | collective-permute-start | bytes 393224 | tf_op jit(solution)/shard_map/ppermute | solution.py:285
  26.1 4.2 %collective-permute-start.7 = (f32[4,264,128]{2,1,0:T(8,128)}, f32[4,264,128]{2,1,0:T(8,128)}, u32[]{:S(2)}, u32[]{:S(2)}) collective-permute-start(f32[4,264,128]{2,1,0:T(8,128)} %get-tuple-element.48.rest_1_), channel_id=1, source_target_pairs={{1,0},{2,1},{3,2},{4,3},{5,4},{6,5},{7,6},{9,8},{10,9},{11,10},{12... | collective-permute-start | bytes 1622024 | tf_op jit(solution)/shard_map/ppermute | solution.py:246
  27.5 2.6 %collective-permute-start.8 = (f32[256,128]{1,0:T(8,128)S(1)}, f32[256,128]{1,0:T(8,128)S(1)}, u32[]{:S(2)}, u32[]{:S(2)}) collective-permute-start(f32[256,128]{1,0:T(8,128)S(1)} %get-tuple-element.83), channel_id=1, source_target_pairs={{0,1},{1,0},{2,3},{3,2},{4,5},{5,4},{6,7},{7,6},{8,9},{9,8},{10,11... | collective-permute-start | bytes 393224 | tf_op jit(solution)/shard_map/ppermute | solution.py:241
  28.7 16.0 %collective-permute-start.6 = (f32[256,128]{1,0:T(8,128)S(1)}, f32[256,128]{1,0:T(8,128)S(1)}, u32[]{:S(2)}, u32[]{:S(2)}) collective-permute-start(f32[256,128]{1,0:T(8,128)S(1)} %get-tuple-element.89), channel_id=1, source_target_pairs={{0,1},{1,0},{2,3},{3,2},{4,5},{5,4},{6,7},{7,6},{8,9},{9,8},{10,11... | collective-permute-start | bytes 393224 | tf_op jit(solution)/shard_map/ppermute | solution.py:241
  34.2 9.9 %collective-permute-start.9 = (f32[256,128]{1,0:T(8,128)S(1)}, f32[256,128]{1,0:T(8,128)S(1)}, u32[]{:S(2)}, u32[]{:S(2)}) collective-permute-start(f32[256,128]{1,0:T(8,128)S(1)} %get-tuple-element.53), channel_id=1, source_target_pairs={{0,1},{1,0},{2,3},{3,2},{4,5},{5,4},{6,7},{7,6},{8,9},{9,8},{10,11... | collective-permute-start | bytes 393224 | tf_op jit(solution)/shard_map/ppermute | solution.py:241
  48.5 1.3 %collective-permute-start.10 = (f32[256,128]{1,0:T(8,128)S(1)}, f32[256,128]{1,0:T(8,128)S(1)}, u32[]{:S(2)}, u32[]{:S(2)}) collective-permute-start(f32[256,128]{1,0:T(8,128)S(1)} %get-tuple-element.61), channel_id=1, source_target_pairs={{0,1},{1,0},{2,3},{3,2},{4,5},{5,4},{6,7},{7,6},{8,9},{9,8},{10,11... | collective-permute-start | bytes 393224 | tf_op jit(solution)/shard_map/ppermute | solution.py:241
  48.8 1.0 collective-permute-start.11
  61.6 3.6 %collective-permute-start.18 = (f32[8,128]{1,0:T(8,128)S(1)}, f32[8,128]{1,0:T(8,128)S(1)}, u32[]{:S(2)}, u32[]{:S(2)}) collective-permute-start(f32[8,128]{1,0:T(8,128)S(1)} %slice_select_fusion), channel_id=1, source_target_pairs={{0,16},{8,24},{16,0},{24,8},{1,17},{9,25},{17,1},{25,9},{2,18},{10... | collective-permute-start | bytes 12296 | tf_op jit(solution)/shard_map/ppermute | solution.py:241
  63.1 3.6 %collective-permute-start.12 = (f32[256,128]{1,0:T(8,128)S(1)}, f32[256,128]{1,0:T(8,128)S(1)}, u32[]{:S(2)}, u32[]{:S(2)}) collective-permute-start(f32[256,128]{1,0:T(8,128)S(1)} %get-tuple-element.81.rest_0_), channel_id=1, source_target_pairs={{6,4},{7,5},{4,2},{5,3},{14,12},{15,13},{12,10},{13,11},{22,20},{2... | collective-permute-start | bytes 393224 | tf_op jit(solution)/shard_map/ppermute | solution.py:285
  65.2 12.2 %collective-permute-start.19 = (f32[4,128]{1,0:T(4,128)S(1)}, f32[4,128]{1,0:T(4,128)S(1)}, u32[]{:S(2)}, u32[]{:S(2)}) collective-permute-start(f32[4,128]{1,0:T(4,128)S(1)} %slice_select_fusion.1), channel_id=1, source_target_pairs={{0,8},{8,0},{16,24},{24,16},{1,9},{9,1},{17,25},{25,17},{2,10},{10... | collective-permute-start | bytes 6152 | tf_op jit(solution)/shard_map/ppermute | solution.py:241
  68.9 37.5 %copy-start.26 = (f32[256,128]{1,0:T(8,128)S(1)}, f32[256,128]{1,0:T(8,128)}, u32[]{:S(2)}) copy-start(f32[256,128]{1,0:T(8,128)} %copy-done.25) | copy-start | bytes 393220
  77.4 13.4 %collective-permute-start.20 = (f32[2,128]{1,0:T(2,128)S(1)}, f32[2,128]{1,0:T(2,128)S(1)}, u32[]{:S(2)}, u32[]{:S(2)}) collective-permute-start(f32[2,128]{1,0:T(2,128)S(1)} %broadcast_select_fusion), channel_id=1, source_target_pairs={{0,4},{1,5},{2,6},{3,7},{4,0},{5,1},{6,2},{7,3},{8,12},{9,13},{10,... | collective-permute-start | bytes 3080 | tf_op jit(solution)/shard_map/ppermute | solution.py:241
  90.8 3.6 %collective-permute-start.21 = (f32[1,128]{1,0:T(1,128)S(1)}, f32[1,128]{1,0:T(1,128)S(1)}, u32[]{:S(2)}, u32[]{:S(2)}) collective-permute-start(f32[1,128]{1,0:T(1,128)S(1)} %broadcast_select_fusion.1), channel_id=1, source_target_pairs={{0,2},{1,3},{2,0},{3,1},{4,6},{5,7},{6,4},{7,5},{8,10},{9,11},{10,... | collective-permute-start | bytes 1544 | tf_op jit(solution)/shard_map/ppermute | solution.py:241
  94.5 3.7 %collective-permute-start.22 = (f32[1,64]{1,0:T(1,128)S(1)}, f32[1,64]{1,0:T(1,128)S(1)}, u32[]{:S(2)}, u32[]{:S(2)}) collective-permute-start(f32[1,64]{1,0:T(1,128)S(1)} %broadcast_select_fusion.3), channel_id=1, source_target_pairs={{0,1},{1,0},{2,3},{3,2},{4,5},{5,4},{6,7},{7,6},{8,9},{9,8},{10,11... | collective-permute-start | bytes 776 | tf_op jit(solution)/shard_map/ppermute | solution.py:241
  94.5 12.0 %collective-permute-start.16 = (f32[4,264,128]{2,1,0:T(8,128)}, f32[4,264,128]{2,1,0:T(8,128)S(1)}, u32[]{:S(2)}, u32[]{:S(2)}) collective-permute-start(f32[4,264,128]{2,1,0:T(8,128)} %get-tuple-element.62.rest_1_), channel_id=1, source_target_pairs={{0,1},{1,2},{2,3},{3,4},{4,5},{5,6},{6,7},{8,9},{9,10},{10,11},{11... | collective-permute-start | bytes 1622024 | tf_op jit(solution)/shard_map/ppermute | solution.py:246
  96.9 8.0 %collective-permute-start.13 = (f32[256,128]{1,0:T(8,128)S(1)}, f32[256,128]{1,0:T(8,128)S(1)}, u32[]{:S(2)}, u32[]{:S(2)}) collective-permute-start(f32[256,128]{1,0:T(8,128)S(1)} %add_add_fusion.1.rest_0_), channel_id=1, source_target_pairs={{4,2},{5,3},{2,0},{3,1},{12,10},{13,11},{10,8},{11,9},{20,18},{21,... | collective-permute-start | bytes 393224 | tf_op jit(solution)/shard_map/ppermute | solution.py:285
  105.0 1.5 %collective-permute-start.15 = (f32[256,128]{1,0:T(8,128)S(1)}, f32[256,128]{1,0:T(8,128)S(1)}, u32[]{:S(2)}, u32[]{:S(2)}) collective-permute-start(f32[256,128]{1,0:T(8,128)S(1)} %get-tuple-element.79), channel_id=1, source_target_pairs={{0,1},{1,0},{2,3},{3,2},{4,5},{5,4},{6,7},{7,6},{8,9},{9,8},{10,11... | collective-permute-start | bytes 393224 | tf_op jit(solution)/shard_map/ppermute | solution.py:241
  105.2 7.7 %collective-permute-start.14 = (f32[256,128]{1,0:T(8,128)S(1)}, f32[256,128]{1,0:T(8,128)S(1)}, u32[]{:S(2)}, u32[]{:S(2)}) collective-permute-start(f32[256,128]{1,0:T(8,128)S(1)} %get-tuple-element.91), channel_id=1, source_target_pairs={{2,0},{3,1},{10,8},{11,9},{18,16},{19,17},{26,24},{27,25}} | collective-permute-start | bytes 393224 | tf_op jit(solution)/shard_map/ppermute | solution.py:285
  112.9 1.4 %collective-permute-start.17 = (f32[256,128]{1,0:T(8,128)S(1)}, f32[256,128]{1,0:T(8,128)S(1)}, u32[]{:S(2)}, u32[]{:S(2)}) collective-permute-start(f32[256,128]{1,0:T(8,128)S(1)} %get-tuple-element.77), channel_id=1, source_target_pairs={{0,1},{1,0},{2,3},{3,2},{4,5},{5,4},{6,7},{7,6},{8,9},{9,8},{10,11... | collective-permute-start | bytes 393224 | tf_op jit(solution)/shard_map/ppermute | solution.py:241
  (29 other events, 160.3 us)

commit v7 on v6

--- a/solution.py
+++ b/solution.py
@@ -12,7 +12,8 @@
 GROUPS = 2
 EXTRA = 8
 VMEM = 10 * 2**20
-PINNED = ("block", "wide", "part")
+SUB = 2
+PINNED = ("block", "wide")
 F32 = jnp.float32
 BF16 = jnp.bfloat16
 
@@ -55,8 +56,12 @@
     return ref[:, p * PAIR:(p + 1) * PAIR]
 
 
-def rows_of(value, p):
-    return value[p * E:(p + 1) * E]
+def rows_at(p):
+    return pl.ds(pl.multiple_of(p * E, E), E)
+
+
+def own_or_received(keep, received, own, p):
+    return jnp.where(own, keep[rows_at(p)], received[rows_at(p)])
 
 
 def state_pair(a, b):
@@ -75,23 +80,28 @@
     return rows, own.astype(F32), flag
 
 
-def states_kernel(group, core, k, v, *rest):
+def states_kernel(core, k, v, *rest):
     keep, send, zero, k_buf, v_buf, sems = rest[-6:]
     lanes = k_buf.shape[2]
+    count = lanes // PAIR
     copies = []
     for half in (1, 0):
-        at = pl.multiple_of((2 * group + (half + core[0]) % 2) * lanes, lanes)
-        for i, (array, buf) in enumerate(((k, k_buf), (v, v_buf))):
-            copies.append(pltpu.make_async_copy(array.at[:, pl.ds(at, lanes)], buf.at[half], sems.at[half, i]))
+        for group in range(GROUPS):
+            at = pl.multiple_of((2 * group + (half + core[0]) % 2) * lanes, lanes)
+            slot = 2 * group + half
+            for i, (array, buf) in enumerate(((k, k_buf), (v, v_buf))):
+                copies.append(pltpu.make_async_copy(array.at[:, pl.ds(at, lanes)], buf.at[slot], sems.at[slot, i]))
     for copy in copies:
         copy.start()
     zero[...] = jnp.zeros_like(zero)
     for half, out in ((1, send), (0, keep)):
-        copies.pop(0).wait()
-        copies.pop(0).wait()
-        for p in range(lanes // PAIR):
-            at = slice(p * PAIR, (p + 1) * PAIR)
-            out[p * E:(p + 1) * E] = state_pair(k_buf[half, :, at], v_buf[half, :, at])
+        for group in range(GROUPS):
+            copies.pop(0).wait()
+            copies.pop(0).wait()
+            for p in range(count):
+                at = slice(p * PAIR, (p + 1) * PAIR)
+                row = (group * count + p) * E
+                out[row:row + E] = state_pair(k_buf[2 * group + half, :, at], v_buf[2 * group + half, :, at])
 
 
 def part_kernel(a, b, seg, table, *rest):
@@ -141,25 +151,25 @@
     return jnp.concatenate([top, bottom], axis=0)
 
 
-def on_rows(seg, table, last, part, count):
+def on_rows(seg, table, last, part):
     rows, own, flag = edge(seg, table, last)
-    met = part[0, count * E:count * E + 1] == own
+    met = part[0, part.shape[1] - EXTRA:part.shape[1] - EXTRA + 1] == own
     if last:
         met = met & (flag == 1)
     return rows.astype(F32) * met.astype(F32)
 
 
 def norm_kernel(core, q, dy, local, gain, seg, table, pre_keep, pre_recv, nxt, *rest):
-    out, dab, part, gsum, keep, send = rest[-6:]
+    out, dab, part, gsum, keep, send, token = rest[-7:]
+    token[...] = jnp.zeros_like(token)
     step = pl.program_id(0)
     count = q.shape[1] // PAIR
-    prefix = jnp.where(step == 0, pre_keep[...], pre_recv[...])
-    on_next = on_rows(seg, table, True, nxt, count)
+    on_next = on_rows(seg, table, True, nxt)
     last, own, flag = edge(seg, table, True)
     last = (last.astype(F32) * jnp.where(flag == 1, 1.0, 0.0)).astype(BF16)
     pairs = [slice(p * PAIR, (p + 1) * PAIR) for p in range(count)]
     fars = [
-        dot(twice(q[:, at]), side_by_side(rows_of(prefix, p), nxt[0, p * E:(p + 1) * E]), 1, 0)
+        dot(twice(q[:, at]), side_by_side(own_or_received(pre_keep, pre_recv, step == 0, p), nxt[0, rows_at(p)]), 1, 0)
         for p, at in enumerate(pairs)
     ]
     attns = [local[:, at] + far[:, :PAIR] + on_next * far[:, PAIR:] for at, far in zip(pairs, fars)]
@@ -197,13 +207,13 @@
     count = q.shape[1] // PAIR
     m, mt = mask[...], mask_t[...]
     token[...] = jnp.zeros_like(token)
-    prefix = jnp.where(step == 0, pre_keep[...], pre_recv[...])
-    on_next = on_rows(seg, table, True, nxt, count)
+    on_next = on_rows(seg, table, True, nxt)
     for p in range(count):
+        at = step % SUB * count + p
         lanes = slice(p * PAIR, (p + 1) * PAIR)
         da = dab[:, lanes]
         kp, vp = k[:, lanes], v[:, lanes]
-        far = dot(twice(da), stacked(rows_of(prefix, p), nxt[0, p * E:(p + 1) * E]), 1, 1)
+        far = dot(twice(da), stacked(own_or_received(pre_keep, pre_recv, step < SUB, at), nxt[0, rows_at(at)]), 1, 1)
         tq = far[:, :PAIR] + on_next * far[:, PAIR:]
         tk = tv = None
         for qh, kh, dh in zip(heads_of(q[:, lanes]), heads_of(kp), heads_of(da)):
@@ -224,12 +234,12 @@
     token[...] = jnp.zeros_like(token)
     step = pl.program_id(0)
     count = k.shape[1] // PAIR
-    suffix = jnp.where(step == 0, suf_keep[...], suf_recv[...])
-    on_prev = on_rows(seg, table, False, prv, count)
+    on_prev = on_rows(seg, table, False, prv)
     for p in range(count):
         lanes = slice(p * PAIR, (p + 1) * PAIR)
-        s = rows_of(suffix, p)
-        g = prv[0, p * E:(p + 1) * E]
+        at = step % SUB * count + p
+        s = own_or_received(suf_keep, suf_recv, step < SUB, at)
+        g = prv[0, rows_at(at)]
         far = dot(twice(v[:, lanes]), stacked(s, g), 1, 1)
         gk[:, lanes] = (gk_in[:, lanes] + far[:, :PAIR] + on_prev * far[:, PAIR:]).astype(BF16)
         far = dot(twice(k[:, lanes]), side_by_side(s, g), 1, 0)
@@ -244,6 +254,10 @@
 def shifted(x, distance):
     count = lax.axis_size("ctx")
     return lax.ppermute(x, "ctx", [(i, i + distance) for i in range(count) if 0 <= i + distance < count])
+
+
+def nought(x):
+    return jnp.minimum(jnp.abs(x), 0.0)
 
 
 def chip_rank(towards):
@@ -307,12 +321,10 @@
     return pltpu.with_memory_space_constraint(x, pltpu.HBM)
 
 
-def scatter_sum(x, axis):
-    for bit in reversed(range(lax.axis_size(axis).bit_length() - 1)):
-        upper = lax.axis_index(axis) >> bit & 1 == 1
-        low, high = jnp.split(x, 2, axis=0 if x.shape[0] > 1 else 1)
-        x = jnp.where(upper, high, low) + partner(jnp.where(upper, low, high), axis, bit)
-    return x
+def scatter_step(x, axis, bit):
+    upper = lax.axis_index(axis) >> bit & 1 == 1
+    low, high = jnp.split(x, 2, axis=0 if x.shape[0] > 1 else 1)
+    return jnp.where(upper, high, low) + partner(jnp.where(upper, low, high), axis, bit)
 
 
 def on_device(queries, keys, values, out_grad, segment_ids, image_flags, gain):
@@ -325,29 +337,30 @@
     half_rows = lanes // PAIR * E
     heads = lanes // E
 
-    def call(kernel, group, ins, outs, micros, after=(), alias=(), scratch=(), steps=(2,), prefetch=True):
-        def at(i, c=None):
-            return (i + c[0]) % 2 if prefetch else i
+    def call(kernel, group, ins, outs, micros, after=(), alias=(), scratch=(), sub=1, prefetch=True, steps=None):
+        def half_of(i, c=None):
+            return (i // sub + c[0]) % 2 if prefetch else i // sub
 
         def wide(*args):
-            return (0, 2 * group + at(*args))
+            return (0, (2 * group + half_of(*args)) * sub + args[0] % sub)
 
         def own(*args):
-            return (0, at(*args))
+            return (0, half_of(*args) * sub + args[0] % sub)
 
         def whole(*args):
             return (0, 0)
 
         def part(*args):
-            return (2 * group + at(*args), 0, 0)
+            return (half_of(*args), 0, 0)
 
         specs = {
-            "wide": pl.BlockSpec((rows, lanes), wide),
-            "block": pl.BlockSpec((rows, lanes), own),
-            "row": pl.BlockSpec((1, lanes), wide),
+            "wide": pl.BlockSpec((rows, lanes // sub), wide),
+            "block": pl.BlockSpec((rows, lanes // sub), own),
+            "row": pl.BlockSpec((1, lanes // sub), wide),
             "sums": pl.BlockSpec((1, lanes // PAIR, PAIR), part),
             "zero": pl.BlockSpec((1, rows), whole),
             "half": pl.BlockSpec((half_rows, PAIR), whole),
+            "all": pl.BlockSpec((GROUPS * half_rows, PAIR), whole),
             "part": pl.BlockSpec((1, half_rows + EXTRA, PAIR), part),
             "seg": pl.BlockSpec((1, rows), whole),
             "table": pl.BlockSpec((1, table.shape[0]), whole),
@@ -361,13 +374,14 @@
         shapes = {
             "wide": (rows, width),
             "block": (rows, 2 * lanes),
-            "sums": (2 * GROUPS, lanes // PAIR, PAIR),
+            "sums": (2, lanes // PAIR, PAIR),
             "zero": (1, rows),
             "half": (half_rows, PAIR),
-            "part": (2 * GROUPS, half_rows + EXTRA, PAIR),
+            "all": (GROUPS * half_rows, PAIR),
+            "part": (2, half_rows + EXTRA, PAIR),
             "token": (1, PAIR),
         }
-        operands = [x for _, x in ins] + list(after)
+        operands = [in_hbm(x) if kind in PINNED else x for kind, x in ins] + list(after)
         kinds = [kind for kind, _ in ins] + [f"after{x.ndim}" for x in after]
         aliases = {}
         for out_at, x in alias:
@@ -376,7 +390,7 @@
                 operands.append(x)
                 kinds.append("any")
         out_shape = [
-            pltpu.HBM(shapes[kind], dtype) if kind in PINNED and (kind != "block" or len(outs) == 2) else jax.ShapeDtypeStruct(shapes[kind], dtype)
+            pltpu.HBM(shapes[kind], dtype) if kind in PINNED else jax.ShapeDtypeStruct(shapes[kind], dtype)
             for kind, dtype in outs
         ]
         moved = sum(rows * 2 * lanes * 2 for kind in kinds if kind in ("wide", "block"))
@@ -385,7 +399,7 @@
             kernel,
             grid_spec=pltpu.PrefetchScalarGridSpec(
                 num_scalar_prefetch=int(prefetch),
-                grid=steps,
+                grid=steps or (2 * sub,),
                 in_specs=[specs[kind] for kind in kinds],
                 out_specs=[specs[kind] for kind, _ in outs],
                 scratch_shapes=scratch,
@@ -400,49 +414,49 @@
     groups = range(GROUPS)
     chips = lax.axis_size("ctx") // 2
     chained = GROUPS < chips <= 8
-    buffers = [pltpu.VMEM((2, rows, lanes), BF16)] * 2 + [pltpu.SemaphoreType.DMA((2, 2))]
-
-    def own_states(g, after):
-        keep, send, zero = call(
-            functools.partial(states_kernel, g), g, [("hbm", in_hbm(k)), ("hbm", in_hbm(v))],
-            [("half", F32), ("half", F32), ("zero", jnp.int32)], 1.2, after=after, scratch=buffers, steps=(1,))
-        return within_chip(keep, send), zero
 
     def local_attn(g, after):
         return call(
             local_kernel, g, [("wide", q), ("wide", k), ("wide", v), ("mask", mask)],
-            [("block", F32), ("token", F32)], 2.3, after=after)
+            [("block", F32), ("token", F32)], 3.0, after=after, sub=SUB)
+
+    def first_part(g, after):
+        return call(
+            part_kernel, g, [("wide", k), ("wide", v), *edges],
+            [("part", F32), ("token", F32)], 1.3, after=after, prefetch=False)
 
     def norm(g, prefix, before, after):
-        output, dab, prv, gsum, keep, send = call(
+        output, dab, prv, gsum, keep, send, token = call(
             norm_kernel, g,
-            [("wide", q), ("wide", dy), ("block", local[g][0]), ("row", gain_row), *edges,
-             ("half", prefix[0]), ("half", prefix[1]), ("part", nxt)],
-            [("wide", BF16), ("wide", BF16), ("part", F32), ("sums", F32), ("half", F32), ("half", F32)],
-            3.0, after=after, alias=list(enumerate(before)))
-        return (output, dab, prv, gsum), within_chip(keep, send)
+            [("wide", q), ("wide", dy), ("block", local[g]), ("row", gain_row), *edges,
+             ("half", prefix[0]), ("half", prefix[1]), ("part", nxt[g])],
+            [("wide", BF16), ("wide", BF16), ("part", F32), ("sums", F32), ("half", F32), ("half", F32), ("token", F32)],
+            3.9, after=after, alias=list(enumerate(before)))
+        return (output, dab), prv, gsum, within_chip(keep, send), token
 
     def inner(g, before, after):
         return call(
             inner_kernel, g,
-            [("wide", q), ("wide", k), ("wide", v), ("wide", in_hbm(dab)), ("mask", mask), ("mask", mask_t), *edges,
-             ("half", prefix[g][0]), ("half", prefix[g][1]), ("part", nxt)],
-            [("wide", BF16), ("block", F32), ("block", F32), ("token", F32)], 6.0, after=after, alias=[(0, before)])
+            [("wide", q), ("wide", k), ("wide", v), ("wide", dab), ("mask", mask), ("mask", mask_t), *edges,
+             ("half", prefix[g][0]), ("half", prefix[g][1]), ("part", nxt[g])],
+            [("wide", BF16), ("block", F32), ("block", F32), ("token", F32)],
+            6.0, after=after, alias=[(0, before)], sub=SUB)
 
     def outer(g, suffix, before, after):
         return call(
             outer_kernel, g,
             [("wide", k), ("wide", v), ("block", inners[g][1]), ("block", inners[g][2]), *edges,
-             ("half", suffix[0]), ("half", suffix[1]), ("part", prv)],
-            [("wide", BF16), ("wide", BF16), ("token", F32)], 2.1, after=after, alias=list(enumerate(before)))
-
-    steps = chips - 2 + GROUPS
-    owns, arrivals, local, prefix = [], [], [], []
-    piece, zero = own_states(0, [])
-    owns.append(piece)
-    for g in groups[1:]:
-        piece, zero = own_states(g, [owns[0][2]])
-        owns.append(piece)
+             ("half", suffix[0]), ("half", suffix[1]), ("part", prv[g])],
+            [("wide", BF16), ("wide", BF16), ("token", F32)], 2.5, after=after, alias=list(enumerate(before)), sub=SUB)
+
+    last = chips - 3 + GROUPS
+    buffers = [pltpu.VMEM((2 * GROUPS, rows, lanes), BF16)] * 2 + [pltpu.SemaphoreType.DMA((2 * GROUPS, 2))]
+    keep, send, zero = call(
+        states_kernel, 0, [("hbm", in_hbm(k)), ("hbm", in_hbm(v))],
+        [("all", F32), ("all", F32), ("zero", jnp.int32)], 3.0, scratch=buffers, steps=(1,))
+    keep, received, total = within_chip(keep, send)
+    owns = [tuple(x[g * half_rows:(g + 1) * half_rows] for x in (keep, received, total)) for g in groups]
+    sums = [own for _, _, own in owns]
     seg = (segment_ids + zero)[0]
     onehot = seg[:, None] == jnp.arange(table.shape[0], dtype=jnp.int32)[None, :]
     img = jnp.sum(jnp.where(onehot, table[None, :], 0), axis=1)
@@ -450,59 +464,66 @@
     pos = jnp.arange(rows)
     mask = ((pos[:, None] >= pos[None, :]) | (imgseg[:, None] == seg[None, :])).astype(BF16)
     mask_t = ((pos[:, None] <= pos[None, :]) | (seg[:, None] == imgseg[None, :])).astype(BF16)
-    sums = [piece[2] for piece in owns]
-    load = chain_load(sums, None, 0, 1) if chained else sums[0]
-    local.append(local_attn(0, [load, sums[-1]]))
-    token = local[0][1]
-    nexts = None
-    for step in range(steps if chained else GROUPS):
+
+    local, nxt, arrivals = [], [], []
+    load = sums[0]
+    parts, tokens = zip(*[first_part(g, [load]) for g in groups])
+    token = sum(tokens)
+    for step in range(last + 1 if chained else GROUPS + 1):
         if chained:
             arrivals.append(chain_step(load, step, 1))
-        if step + 1 < steps and chained:
+        if 1 <= step <= GROUPS:
+            nxt.append(shifted(parts[step - 1], -1))
+            attn, token = local_attn(step - 1, [load])
+            local.append(attn)
+            token = token + nought(nxt[-1][0, :1])
+        if step < last and chained:
             load = chain_load(sums, arrivals[-1] + token, step + 1, 1)
-        if step == 0:
-            nexts, token = call(
-                part_kernel, 0, [("wide", k), ("wide", v), *edges],
-                [("part", F32), ("token", F32)], 2.0, after=[load], steps=(2 * GROUPS,), prefetch=False)
-            nxt = shifted(nexts, -1)
-        elif step < GROUPS:
-            local.append(local_attn(step, [load, nexts]))
-            token = local[step][1]
-        else:
-            token = jnp.zeros((1, PAIR), F32)
-    befores = [chain_result(arrivals, g, 1) if chained else chips_before(sums[g], 1) for g in groups]
-    prefix = [to_cores(before, piece, 1) for before, piece in zip(befores, owns)]
-
-    norms, owns, arrivals = [None] * 4, [], []
+    output, prefix, prv, gsums, pieces = [None] * 2, [], [], [], []
     for g in groups:
-        norms, piece = norm(g, prefix[g], norms, [piece[2] for piece in owns])
-        owns.append(piece)
-    output, dab, prv, gsum = norms
-    prv = shifted(prv, 1)
-    sums = [piece[2] for piece in owns]
-    inners, outers, suffix = [], [None] * 2, []
-    token = None
-    for step in range(steps if chained else GROUPS):
+        if g and chained:
+            arrivals[-1] = arrivals[-1] + token
+        before = chain_result(arrivals, g, 1) if chained else chips_before(sums[g], 1)
+        prefix.append(to_cores(before, owns[g], 1))
+        output, part, gsum, piece, token = norm(g, prefix[g], output, [load])
+        prv.append(part)
+        gsums.append(gsum)
+        pieces.append(piece)
+    output, dab = output
+
+    owns = pieces
+    sums = [own for _, _, own in owns]
+    arrivals, inners, outers = [], [], [None] * 2
+    gain_sum = jnp.concatenate(gsums, axis=0).reshape(-1, PAIR)
+    bits = [(axis, bit) for axis in ("dp", "ctx") for bit in reversed(range(lax.axis_size(axis).bit_length() - 1))]
+    load, token = sums[0], None
+    for step in range(last + 1 if chained else GROUPS + 1):
         if chained:
-            arrived = arrivals[-1] if arrivals else None
-            load = chain_load(sums, arrived if token is None else arrived + token, step, -1)
+            if step:
+                load = chain_load(sums, arrivals[-1] + token, step, -1)
             arrivals.append(chain_step(load, step, -1))
-        else:
-            load = sums[-1]
+        token = None
+        if bits and step < 4:
+            gain_sum = scatter_step(gain_sum + nought(load[:1]), *bits.pop(0))
+            token = nought(gain_sum[:1])
         if 1 <= step <= GROUPS:
-            inners.append(inner(step - 1, inners[-1][0] if inners else None, [load, norms[2]]))
-            token = inners[-1][3]
-    while len(inners) < GROUPS:
-        inners.append(inner(len(inners), inners[-1][0] if inners else None, [load]))
-    gain_sum = scatter_sum(gsum.reshape(-1, PAIR) + inners[0][3], "dp")
-    grad_gain = scatter_sum(gain_sum + inners[-1][3], "ctx").reshape(-1)
-    grad_q = inners[-1][0]
+            prv[step - 1] = shifted(prv[step - 1], 1)
+            tie = nought(prv[step - 1][0, :1])
+            token = tie if token is None else token + tie
+        if step < GROUPS:
+            inners.append(inner(step, inners[-1][0] if inners else None, [load, sums[-1]]))
+            token = token + inners[-1][3]
     for g in groups:
         if g and chained:
             arrivals[-1] = arrivals[-1] + token
         before = chain_result(arrivals, g, -1) if chained else chips_before(sums[g], -1)
-        *outers, token = outer(g, to_cores(before, owns[g], -1), outers, [])
+        *outers, done = outer(g, to_cores(before, owns[g], -1), outers, [load])
+        token = done if token is None else token + done
+    for axis, bit in bits:
+        gain_sum = scatter_step(gain_sum, axis, bit)
+    grad_q = inners[-1][0]
     grad_k, grad_v = outers
+    grad_gain = gain_sum.reshape(-1)
     return output[None], grad_q[None], grad_k[None], grad_v[None], grad_gain
 
 

time: 117 us -> 96.2 us (0.82)
  local copies, waits for them, and re-layouts: 12 us -> 0.87 us
  starting transfers between devices: 43.6 us -> 35.2 us
  Pallas kernels: 37.9 us -> 46.2 us
  waiting for transfers between devices: 18.8 us -> 10.5 us
  other arithmetic: 2.97 us -> 1.48 us
    ppermute x13 -> x12, starting transfers between devices: 26.9 us -> 13.8 us  [partner(): return lax.ppermute(x, axis, route)]
    unnamed x60 -> x6, local copies, waits for them, and re-layouts: 12 us -> 0.86 us
    pallas_call x11, Pallas kernels: 37.9 us -> 46.2 us  [call(): pl.pallas_call(kernel, grid_spec=pltpu.PrefetchScalarGridSpec(num_scalar_...]
    ppermute x13 -> x12, waiting for transfers between devices: 10.7 us -> 4.03 us  [partner(): return lax.ppermute(x, axis, route)]
    ppermute x2 -> x4, starting transfers between devices: 3.71 us -> 6.33 us  [shifted(): lax.ppermute(x, 'ctx', [(i, i + distance) for i in range(count) if 0 <= i...]
    ppermute x8, starting transfers between devices: 13 us -> 15 us  [chain_step(): return lax.ppermute(load, 'ctx', route)]
    add x5 -> x4, other arithmetic: 1.77 us -> 0.12 us  [chain_load(): return load if arrived is None else load + arrived]
    ppermute x8, waiting for transfers between devices: 7.9 us -> 6.49 us  [chain_step(): return lax.ppermute(load, 'ctx', route)]
  transfers between devices with their start and end apart: 23 -> 24, of which waited for: 11 -> 8; matrix products, arithmetic and copies ran while one was open for 2% -> 1% of each run, Pallas kernels for 19% -> 33%
where the time goes in v7:
time: 96.2 us; the launch traced here: 95.3 us
  Pallas kernels  46.2 us (48%)
  starting transfers between devices  35.2 us (37%)
  waiting for transfers between devices  10.5 us (11%)
  other arithmetic  1.48 us (2%)
  between operations  1.07 us (1%)
    pallas_call x11, Pallas kernels, call(): pl.pallas_call(kernel, grid_spec=pltpu.PrefetchScalarGridSpec(num_scalar_...  46.2 us
    ppermute x8, starting transfers between devices, chain_step(): return lax.ppermute(load, 'ctx', route)  15 us
    ppermute x12, starting transfers between devices, partner(): return lax.ppermute(x, axis, route)  13.8 us
    ppermute x8, waiting for transfers between devices, chain_step(): return lax.ppermute(load, 'ctx', route)  6.49 us
    ppermute x4, starting transfers between devices, shifted(): lax.ppermute(x, 'ctx', [(i, i + distance) for i in range(count) if 0 <= i...  6.33 us
    ppermute x12, waiting for transfers between devices, partner(): return lax.ppermute(x, axis, route)  4.03 us
  transfers between devices with their start and end apart: 24, of which 8 were waited for; matrix products, arithmetic and copies ran while one was open for 1% of the time, Pallas kernels for 33%

profile of v7, /device:TPU:0, one launch (start us, length us, event | category | flops | bytes accessed | tf_op | source)
XLA Modules:
  0.0 95.3 jit_solution(15681755744137534872)
XLA Ops:
  0.6 2.2 %shard_map.110 = (f32[512,128]{1,0:T(8,128)S(1)}, f32[512,128]{1,0:T(8,128)S(1)}, s32[1,256]{1,0:T(1,128)S(1)}) custom-call(s32[1]{0:T(128)} %bitcast.core, bf16[256,2048]{1,0:T(8,128)(2,1)} %bitcast.82, bf16[256,2048]{1,0:T(8,128)(2,1)} %bitcast.91), custom_call_target="tpu_custom_call" | custom-call | flops 3449999872 | tf_op jit(solution)/shard_map/pallas_call | solution.py:398
  4.6 1.8 %shard_map.111 = (f32[2,264,128]{2,1,0:T(8,128)S(1)}, f32[1,128]{1,0:T(1,128)S(1)}) custom-call(bf16[256,2048]{1,0:T(8,128)(2,1)} %bitcast.83, bf16[256,2048]{1,0:T(8,128)(2,1)} %bitcast.92, s32[1,256]{1,0:T(1,128)S(1)} %copy-done, s32[1,32]{1,0:T(1,128)S(1)} %copy-done.1, f32[256,128]{1,0:T(8,128)S(1)} %slice.68.rest_0_), custom_call_target="tpu_custom_call" | custom-call | flops 1495000064 | bytes 1048576 | tf_op jit(solution)/shard_map/pallas_call | solution.py:398
  6.4 1.8 %shard_map.112 = (f32[2,264,128]{2,1,0:T(8,128)S(1)}, f32[1,128]{1,0:T(1,128)S(1)}) custom-call(bf16[256,2048]{1,0:T(8,128)(2,1)} %bitcast.84, bf16[256,2048]{1,0:T(8,128)(2,1)} %bitcast.93, s32[1,256]{1,0:T(1,128)S(1)} %copy-done, s32[1,32]{1,0:T(1,128)S(1)} %copy-done.1, f32[256,128]{1,0:T(8,128)S(1)} %slice.68.rest_0_), custom_call_target="tpu_custom_call" | custom-call | flops 1495000064 | bytes 1048576 | tf_op jit(solution)/shard_map/pallas_call | solution.py:398
  8.3 4.9 %collective-permute-start.1 = (f32[256,128]{1,0:T(8,128)S(1)}, f32[256,128]{1,0:T(8,128)S(1)}, u32[]{:S(2)}, u32[]{:S(2)}) collective-permute-start(f32[256,128]{1,0:T(8,128)S(1)} %slice.68.rest_0_), channel_id=1, source_target_pairs={{0,2},{1,3},{8,10},{9,11},{16,18},{17,19},{24,26},{25,27}} | collective-permute-start | bytes 393224 | tf_op jit(solution)/shard_map/ppermute | solution.py:299
  13.2 1.3 %collective-permute-start.3 = (f32[2,264,128]{2,1,0:T(8,128)S(1)}, f32[2,264,128]{2,1,0:T(8,128)S(1)}, u32[]{:S(2)}, u32[]{:S(2)}) collective-permute-start(f32[2,264,128]{2,1,0:T(8,128)S(1)} %get-tuple-element.48), channel_id=1, source_target_pairs={{1,0},{2,1},{3,2},{4,3},{5,4},{6,5},{7,6},{9,8},{10,9},{11,10},{12... | collective-permute-start | bytes 811016 | tf_op jit(solution)/shard_map/ppermute | solution.py:256
  14.5 1.3 %collective-permute-start.5 = (f32[2,264,128]{2,1,0:T(8,128)S(1)}, f32[2,264,128]{2,1,0:T(8,128)S(1)}, u32[]{:S(2)}, u32[]{:S(2)}) collective-permute-start(f32[2,264,128]{2,1,0:T(8,128)S(1)} %get-tuple-element.51), channel_id=1, source_target_pairs={{1,0},{2,1},{3,2},{4,3},{5,4},{6,5},{7,6},{9,8},{10,9},{11,10},{12... | collective-permute-start | bytes 811016 | tf_op jit(solution)/shard_map/ppermute | solution.py:256
  16.2 4.9 %collective-permute-start.2 = (f32[256,128]{1,0:T(8,128)S(1)}, f32[256,128]{1,0:T(8,128)S(1)}, u32[]{:S(2)}, u32[]{:S(2)}) collective-permute-start(f32[256,128]{1,0:T(8,128)S(1)} %add_add_fusion.5.rest_0_), channel_id=1, source_target_pairs={{0,2},{1,3},{2,4},{3,5},{8,10},{9,11},{10,12},{11,13},{16,18},{17,... | collective-permute-start | bytes 393224 | tf_op jit(solution)/shard_map/ppermute | solution.py:299
  21.1 4.7 %shard_map.113 = (f32[256,1024]{1,0:T(8,128)}, f32[1,128]{1,0:T(1,128)S(1)}) custom-call(s32[1]{0:T(128)} %bitcast.core, bf16[256,2048]{1,0:T(8,128)(2,1)} %bitcast.76, bf16[256,2048]{1,0:T(8,128)(2,1)} %bitcast.85, bf16[256,2048]{1,0:T(8,128)(2,1)} %bitcast.94, bf16[256,256]{1,0:T(8,128)(2,1)S(1)} %get-tuple-element.94.mask, ...), custom_call_target="tpu_custom_call" | custom-call | flops 3449999872 | bytes 2097152 | tf_op jit(solution)/shard_map/pallas_call | solution.py:398
  26.6 4.8 %shard_map.114 = (f32[256,1024]{1,0:T(8,128)}, f32[1,128]{1,0:T(1,128)S(1)}) custom-call(s32[1]{0:T(128)} %bitcast.core, bf16[256,2048]{1,0:T(8,128)(2,1)} %bitcast.77, bf16[256,2048]{1,0:T(8,128)(2,1)} %bitcast.86, bf16[256,2048]{1,0:T(8,128)(2,1)} %bitcast.95, bf16[256,256]{1,0:T(8,128)(2,1)S(1)} %get-tuple-element.94.mask, ...), custom_call_target="tpu_custom_call" | custom-call | flops 3449999872 | bytes 2097152 | tf_op jit(solution)/shard_map/pallas_call | solution.py:398
  32.9 3.9 %shard_map.115 = (bf16[256,2048]{1,0:T(8,128)(2,1)}, bf16[256,2048]{1,0:T(8,128)(2,1)}, f32[2,264,128]{2,1,0:T(8,128)S(1)}, f32[2,4,128]{2,1,0:T(4,128)S(1)}, f3...) custom-call(s32[1]{0:T(128)} %bitcast.core, bf16[256,2048]{1,0:T(8,128)(2,1)} %bitcast.78, ...), custom_call_target="tpu_custom_call" | custom-call | flops 4485000192 | bytes 2621440 | tf_op jit(solution)/shard_map/pallas_call | solution.py:398
  38.9 4.0 %shard_map.116 = (bf16[256,2048]{1,0:T(8,128)(2,1)}, bf16[256,2048]{1,0:T(8,128)(2,1)}, f32[2,264,128]{2,1,0:T(8,128)S(1)}, f32[2,4,128]{2,1,0:T(4,128)S(1)}, f3...) custom-call(s32[1]{0:T(128)} %bitcast.core, ...), custom_call_target="tpu_custom_call", output_to_operand_aliasing={{0}: (11, {}), {1}: (12, {})} | custom-call | flops 4485000192 | bytes 2621440 | tf_op jit(solution)/shard_map/pallas_call | solution.py:398
  42.9 1.6 %collective-permute-start.12 = (f32[8,128]{1,0:T(8,128)S(1)}, f32[8,128]{1,0:T(8,128)S(1)}, u32[]{:S(2)}, u32[]{:S(2)}) collective-permute-start(f32[8,128]{1,0:T(8,128)S(1)} %slice_select_fusion), channel_id=1, source_target_pairs={{0,16},{8,24},{16,0},{24,8},{1,17},{9,25},{17,1},{25,9},{2,18},{10... | collective-permute-start | bytes 12296 | tf_op jit(solution)/shard_map/ppermute | solution.py:251
  44.5 1.8 %collective-permute-start.15 = (f32[2,264,128]{2,1,0:T(8,128)S(1)}, f32[2,264,128]{2,1,0:T(8,128)S(1)}, u32[]{:S(2)}, u32[]{:S(2)}) collective-permute-start(f32[2,264,128]{2,1,0:T(8,128)S(1)} %get-tuple-element.69), channel_id=1, source_target_pairs={{0,1},{1,2},{2,3},{3,4},{4,5},{5,6},{6,7},{8,9},{9,10},{10,11},{11... | collective-permute-start | bytes 811016 | tf_op jit(solution)/shard_map/ppermute | solution.py:256
  47.0 2.3 %collective-permute-start.10 = (f32[256,128]{1,0:T(8,128)S(1)}, f32[256,128]{1,0:T(8,128)S(1)}, u32[]{:S(2)}, u32[]{:S(2)}) collective-permute-start(f32[256,128]{1,0:T(8,128)S(1)} %get-tuple-element.61), channel_id=1, source_target_pairs={{0,1},{1,0},{2,3},{3,2},{4,5},{5,4},{6,7},{7,6},{8,9},{9,8},{10,11... | collective-permute-start | bytes 393224 | tf_op jit(solution)/shard_map/ppermute | solution.py:251
  49.3 1.9 %collective-permute-start.18 = (f32[2,264,128]{2,1,0:T(8,128)S(1)}, f32[2,264,128]{2,1,0:T(8,128)S(1)}, u32[]{:S(2)}, u32[]{:S(2)}) collective-permute-start(f32[2,264,128]{2,1,0:T(8,128)S(1)} %get-tuple-element.71), channel_id=1, source_target_pairs={{0,1},{1,2},{2,3},{3,4},{4,5},{5,6},{6,7},{8,9},{9,10},{10,11},{11... | collective-permute-start | bytes 811016 | tf_op jit(solution)/shard_map/ppermute | solution.py:256
  51.3 7.0 %shard_map.117 = (bf16[256,2048]{1,0:T(8,128)(2,1)}, f32[256,1024]{1,0:T(8,128)}, f32[256,1024]{1,0:T(8,128)}, f32[1,128]{1,0:T(1,128)S(1)}) custom-call(s32[1]{0:T(128)} %bitcast.core, bf16[256,2048]{1,0:T(8,128)(2,1)} %bitcast.80, bf16[256,2048]{1,0:T(8,128)(2,1)} %bitcast.87, bf16[256,2048]{1,0:T(8,128)(2,1)} %bitcast.96, ...), custom_call_target="tpu_custom_call" | custom-call | flops 6899999744 | bytes 3670016 | tf_op jit(solution)/shard_map/pallas_call | solution.py:398
  59.1 1.6 %collective-permute-start.14 = (f32[4,128]{1,0:T(4,128)S(1)}, f32[4,128]{1,0:T(4,128)S(1)}, u32[]{:S(2)}, u32[]{:S(2)}) collective-permute-start(f32[4,128]{1,0:T(4,128)S(1)} %slice_select_fusion.1), channel_id=1, source_target_pairs={{0,8},{8,0},{16,24},{24,16},{1,9},{9,1},{17,25},{25,17},{2,10},{10... | collective-permute-start | bytes 6152 | tf_op jit(solution)/shard_map/ppermute | solution.py:251
  60.6 7.0 %shard_map.118 = (bf16[256,2048]{1,0:T(8,128)(2,1)}, f32[256,1024]{1,0:T(8,128)}, f32[256,1024]{1,0:T(8,128)}, f32[1,128]{1,0:T(1,128)S(1)}) custom-call(s32[1]{0:T(128)} %bitcast.core, bf16[256,2048]{1,0:T(8,128)(2,1)} %bitcast.81, bf16[256,2048]{1,0:T(8,128)(2,1)} %bitcast.88, bf16[256,2048]{1,0:T(8,128)(2,1)} %bitcast.97, ...), custom_call_target="tpu_custom_call", output_to_operand_aliasing={{0}: (14, {})} | custom-call | flops 6899999744 | bytes 3670016 | tf_op jit(solution)/shard_map/pallas_call | solution.py:398
  67.7 3.9 %collective-permute-start.17 = (f32[2,128]{1,0:T(2,128)S(1)}, f32[2,128]{1,0:T(2,128)S(1)}, u32[]{:S(2)}, u32[]{:S(2)}) collective-permute-start(f32[2,128]{1,0:T(2,128)S(1)} %broadcast_select_fusion.4), channel_id=1, source_target_pairs={{0,4},{1,5},{2,6},{3,7},{4,0},{5,1},{6,2},{7,3},{8,12},{9,13},{10,... | collective-permute-start | bytes 3080 | tf_op jit(solution)/shard_map/ppermute | solution.py:251
  73.2 6.1 %collective-permute-done.16 = f32[256,128]{1,0:T(8,128)S(1)} collective-permute-done((f32[256,128]{1,0:T(8,128)S(1)}, f32[256,128]{1,0:T(8,128)S(1)}, u32[]{:S(2)}, u32[]{:S(2)}) %collective-permute-start.16) | collective-permute-done | bytes 131104 | tf_op jit(solution)/shard_map/ppermute | solution.py:299
  80.6 2.7 %collective-permute-start.20 = (f32[1,128]{1,0:T(1,128)S(1)}, f32[1,128]{1,0:T(1,128)S(1)}, u32[]{:S(2)}, u32[]{:S(2)}) collective-permute-start(f32[1,128]{1,0:T(1,128)S(1)} %broadcast_select_fusion.2), channel_id=1, source_target_pairs={{0,2},{1,3},{2,0},{3,1},{4,6},{5,7},{6,4},{7,5},{8,10},{9,11},{10,... | collective-permute-start | bytes 1544 | tf_op jit(solution)/shard_map/ppermute | solution.py:251
  83.4 1.3 %collective-permute-done.21.suf_recv = f32[256,128]{1,0:T(8,128)S(1)} collective-permute-done((f32[256,128]{1,0:T(8,128)S(1)}, f32[256,128]{1,0:T(8,128)S(1)}, u32[]{:S(2)}, u32[]{:S(2)}) %collective-permute-start.21) | collective-permute-done | bytes 131104 | tf_op jit(solution)/shard_map/ppermute | solution.py:251
  84.7 4.4 %shard_map.119 = (bf16[256,2048]{1,0:T(8,128)(2,1)}, bf16[256,2048]{1,0:T(8,128)(2,1)}, f32[1,128]{1,0:T(1,128)S(1)}) custom-call(s32[1]{0:T(128)} %bitcast.core, bf16[256,2048]{1,0:T(8,128)(2,1)} %bitcast.89, bf16[256,2048]{1,0:T(8,128)(2,1)} %bitcast.98, f32[256,1024]{1,0:T(8,128)} %get-tuple-element.72.gk_in, f32[256,1024]{1,0:T(8,128)} %get-tuple-element.73.gv_in, ...), custom_call_target="tpu_custom_call" | custom-call | flops 2875000064 | bytes 3145728 | tf_op jit(solution)/shard_map/pallas_call | solution.py:398
  90.9 4.4 %shard_map.120 = (bf16[256,2048]{1,0:T(8,128)(2,1)}, bf16[256,2048]{1,0:T(8,128)(2,1)}, f32[1,128]{1,0:T(1,128)}) custom-call(s32[1]{0:T(128)} %bitcast.core, bf16[256,2048]{1,0:T(8,128)(2,1)} %bitcast.90, bf16[256,2048]{1,0:T(8,128)(2,1)} %bitcast.99, f32[256,1024]{1,0:T(8,128)} %get-tuple-element.67.gk_in, ...), custom_call_target="tpu_custom_call", output_to_operand_aliasing={{0}: (11, {}), {1}: (12, {})} | custom-call | flops 2875000064 | bytes 3145728 | tf_op jit(solution)/shard_map/pallas_call | solution.py:398
  (87 shorter events, 12.6 us)
Async XLA Ops:
  2.9 1.7 %collective-permute-start = (f32[512,128]{1,0:T(8,128)S(1)}, f32[512,128]{1,0:T(8,128)S(1)}, u32[]{:S(2)}, u32[]{:S(2)}) collective-permute-start(f32[512,128]{1,0:T(8,128)S(1)} %get-tuple-element.44), channel_id=1, source_target_pairs={{0,1},{1,0},{2,3},{3,2},{4,5},{5,4},{6,7},{7,6},{8,9},{9,8},{10,11... | collective-permute-start | bytes 786440 | tf_op jit(solution)/shard_map/ppermute | solution.py:251
  8.3 7.9 %collective-permute-start.1 = (f32[256,128]{1,0:T(8,128)S(1)}, f32[256,128]{1,0:T(8,128)S(1)}, u32[]{:S(2)}, u32[]{:S(2)}) collective-permute-start(f32[256,128]{1,0:T(8,128)S(1)} %slice.68.rest_0_), channel_id=1, source_target_pairs={{0,2},{1,3},{8,10},{9,11},{16,18},{17,19},{24,26},{25,27}} | collective-permute-start | bytes 393224 | tf_op jit(solution)/shard_map/ppermute | solution.py:299
  13.2 12.7 %collective-permute-start.3 = (f32[2,264,128]{2,1,0:T(8,128)S(1)}, f32[2,264,128]{2,1,0:T(8,128)S(1)}, u32[]{:S(2)}, u32[]{:S(2)}) collective-permute-start(f32[2,264,128]{2,1,0:T(8,128)S(1)} %get-tuple-element.48), channel_id=1, source_target_pairs={{1,0},{2,1},{3,2},{4,3},{5,4},{6,5},{7,6},{9,8},{10,9},{11,10},{12... | collective-permute-start | bytes 811016 | tf_op jit(solution)/shard_map/ppermute | solution.py:256
  14.5 16.9 %collective-permute-start.5 = (f32[2,264,128]{2,1,0:T(8,128)S(1)}, f32[2,264,128]{2,1,0:T(8,128)S(1)}, u32[]{:S(2)}, u32[]{:S(2)}) collective-permute-start(f32[2,264,128]{2,1,0:T(8,128)S(1)} %get-tuple-element.51), channel_id=1, source_target_pairs={{1,0},{2,1},{3,2},{4,3},{5,4},{6,5},{7,6},{9,8},{10,9},{11,10},{12... | collective-permute-start | bytes 811016 | tf_op jit(solution)/shard_map/ppermute | solution.py:256
  16.2 9.7 %collective-permute-start.2 = (f32[256,128]{1,0:T(8,128)S(1)}, f32[256,128]{1,0:T(8,128)S(1)}, u32[]{:S(2)}, u32[]{:S(2)}) collective-permute-start(f32[256,128]{1,0:T(8,128)S(1)} %add_add_fusion.5.rest_0_), channel_id=1, source_target_pairs={{0,2},{1,3},{2,4},{3,5},{8,10},{9,11},{10,12},{11,13},{16,18},{17,... | collective-permute-start | bytes 393224 | tf_op jit(solution)/shard_map/ppermute | solution.py:299
  25.9 5.4 %collective-permute-start.4 = (f32[256,128]{1,0:T(8,128)S(1)}, f32[256,128]{1,0:T(8,128)S(1)}, u32[]{:S(2)}, u32[]{:S(2)}) collective-permute-start(f32[256,128]{1,0:T(8,128)S(1)} %add_add_fusion.4.rest_0_), channel_id=1, source_target_pairs={{2,4},{3,5},{4,6},{5,7},{10,12},{11,13},{12,14},{13,15},{18,20},{1... | collective-permute-start | bytes 393224 | tf_op jit(solution)/shard_map/ppermute | solution.py:299
  31.4 1.4 %collective-permute-start.7 = (f32[256,128]{1,0:T(8,128)S(1)}, f32[256,128]{1,0:T(8,128)S(1)}, u32[]{:S(2)}, u32[]{:S(2)}) collective-permute-start(f32[256,128]{1,0:T(8,128)S(1)} %get-tuple-element.87), channel_id=1, source_target_pairs={{0,1},{1,0},{2,3},{3,2},{4,5},{5,4},{6,7},{7,6},{8,9},{9,8},{10,11... | collective-permute-start | bytes 393224 | tf_op jit(solution)/shard_map/ppermute | solution.py:251
  31.5 5.3 %collective-permute-start.6 = (f32[256,128]{1,0:T(8,128)S(1)}, f32[256,128]{1,0:T(8,128)S(1)}, u32[]{:S(2)}, u32[]{:S(2)}) collective-permute-start(f32[256,128]{1,0:T(8,128)S(1)} %get-tuple-element.92.rest_0_), channel_id=1, source_target_pairs={{4,6},{5,7},{12,14},{13,15},{20,22},{21,23},{28,30},{29,31}} | collective-permute-start | bytes 393224 | tf_op jit(solution)/shard_map/ppermute | solution.py:299
  36.9 2.0 %collective-permute-start.8 = (f32[256,128]{1,0:T(8,128)S(1)}, f32[256,128]{1,0:T(8,128)S(1)}, u32[]{:S(2)}, u32[]{:S(2)}) collective-permute-start(f32[256,128]{1,0:T(8,128)S(1)} %get-tuple-element.85), channel_id=1, source_target_pairs={{0,1},{1,0},{2,3},{3,2},{4,5},{5,4},{6,7},{7,6},{8,9},{9,8},{10,11... | collective-permute-start | bytes 393224 | tf_op jit(solution)/shard_map/ppermute | solution.py:251
  37.5 1.3 %collective-permute-start.9 = (f32[256,128]{1,0:T(8,128)S(1)}, f32[256,128]{1,0:T(8,128)S(1)}, u32[]{:S(2)}, u32[]{:S(2)}) collective-permute-start(f32[256,128]{1,0:T(8,128)S(1)} %get-tuple-element.59), channel_id=1, source_target_pairs={{0,1},{1,0},{2,3},{3,2},{4,5},{5,4},{6,7},{7,6},{8,9},{9,8},{10,11... | collective-permute-start | bytes 393224 | tf_op jit(solution)/shard_map/ppermute | solution.py:251
  42.9 8.3 %collective-permute-start.12 = (f32[8,128]{1,0:T(8,128)S(1)}, f32[8,128]{1,0:T(8,128)S(1)}, u32[]{:S(2)}, u32[]{:S(2)}) collective-permute-start(f32[8,128]{1,0:T(8,128)S(1)} %slice_select_fusion), channel_id=1, source_target_pairs={{0,16},{8,24},{16,0},{24,8},{1,17},{9,25},{17,1},{25,9},{2,18},{10... | collective-permute-start | bytes 12296 | tf_op jit(solution)/shard_map/ppermute | solution.py:251
  44.5 23.1 %collective-permute-start.15 = (f32[2,264,128]{2,1,0:T(8,128)S(1)}, f32[2,264,128]{2,1,0:T(8,128)S(1)}, u32[]{:S(2)}, u32[]{:S(2)}) collective-permute-start(f32[2,264,128]{2,1,0:T(8,128)S(1)} %get-tuple-element.69), channel_id=1, source_target_pairs={{0,1},{1,2},{2,3},{3,4},{4,5},{5,6},{6,7},{8,9},{9,10},{10,11},{11... | collective-permute-start | bytes 811016 | tf_op jit(solution)/shard_map/ppermute | solution.py:256
  46.3 12.0 %collective-permute-start.11 = (f32[256,128]{1,0:T(8,128)S(1)}, f32[256,128]{1,0:T(8,128)S(1)}, u32[]{:S(2)}, u32[]{:S(2)}) collective-permute-start(f32[256,128]{1,0:T(8,128)S(1)} %add.238.rest_0_), channel_id=1, source_target_pairs={{6,4},{7,5},{14,12},{15,13},{22,20},{23,21},{30,28},{31,29}} | collective-permute-start | bytes 393224 | tf_op jit(solution)/shard_map/ppermute | solution.py:299
  47.0 4.2 %collective-permute-start.10 = (f32[256,128]{1,0:T(8,128)S(1)}, f32[256,128]{1,0:T(8,128)S(1)}, u32[]{:S(2)}, u32[]{:S(2)}) collective-permute-start(f32[256,128]{1,0:T(8,128)S(1)} %get-tuple-element.61), channel_id=1, source_target_pairs={{0,1},{1,0},{2,3},{3,2},{4,5},{5,4},{6,7},{7,6},{8,9},{9,8},{10,11... | collective-permute-start | bytes 393224 | tf_op jit(solution)/shard_map/ppermute | solution.py:251
  49.3 23.9 %collective-permute-start.18 = (f32[2,264,128]{2,1,0:T(8,128)S(1)}, f32[2,264,128]{2,1,0:T(8,128)S(1)}, u32[]{:S(2)}, u32[]{:S(2)}) collective-permute-start(f32[2,264,128]{2,1,0:T(8,128)S(1)} %get-tuple-element.71), channel_id=1, source_target_pairs={{0,1},{1,2},{2,3},{3,4},{4,5},{5,6},{6,7},{8,9},{9,10},{10,11},{11... | collective-permute-start | bytes 811016 | tf_op jit(solution)/shard_map/ppermute | solution.py:256
  58.4 9.3 %collective-permute-start.13 = (f32[256,128]{1,0:T(8,128)S(1)}, f32[256,128]{1,0:T(8,128)S(1)}, u32[]{:S(2)}, u32[]{:S(2)}) collective-permute-start(f32[256,128]{1,0:T(8,128)S(1)} %add_add_fusion.2.rest_0_), channel_id=1, source_target_pairs={{6,4},{7,5},{4,2},{5,3},{14,12},{15,13},{12,10},{13,11},{22,20},{2... | collective-permute-start | bytes 393224 | tf_op jit(solution)/shard_map/ppermute | solution.py:299
  59.1 8.5 %collective-permute-start.14 = (f32[4,128]{1,0:T(4,128)S(1)}, f32[4,128]{1,0:T(4,128)S(1)}, u32[]{:S(2)}, u32[]{:S(2)}) collective-permute-start(f32[4,128]{1,0:T(4,128)S(1)} %slice_select_fusion.1), channel_id=1, source_target_pairs={{0,8},{8,0},{16,24},{24,16},{1,9},{9,1},{17,25},{25,17},{2,10},{10... | collective-permute-start | bytes 6152 | tf_op jit(solution)/shard_map/ppermute | solution.py:251
  67.7 5.4 %collective-permute-start.17 = (f32[2,128]{1,0:T(2,128)S(1)}, f32[2,128]{1,0:T(2,128)S(1)}, u32[]{:S(2)}, u32[]{:S(2)}) collective-permute-start(f32[2,128]{1,0:T(2,128)S(1)} %broadcast_select_fusion.4), channel_id=1, source_target_pairs={{0,4},{1,5},{2,6},{3,7},{4,0},{5,1},{6,2},{7,3},{8,12},{9,13},{10,... | collective-permute-start | bytes 3080 | tf_op jit(solution)/shard_map/ppermute | solution.py:251
  71.6 7.6 %collective-permute-start.16 = (f32[256,128]{1,0:T(8,128)S(1)}, f32[256,128]{1,0:T(8,128)S(1)}, u32[]{:S(2)}, u32[]{:S(2)}) collective-permute-start(f32[256,128]{1,0:T(8,128)S(1)} %add_add_fusion.1), channel_id=1, source_target_pairs={{4,2},{5,3},{2,0},{3,1},{12,10},{13,11},{10,8},{11,9},{20,18},{21,... | collective-permute-start | bytes 393224 | tf_op jit(solution)/shard_map/ppermute | solution.py:299
  79.3 10.0 %collective-permute-start.19 = (f32[256,128]{1,0:T(8,128)S(1)}, f32[256,128]{1,0:T(8,128)S(1)}, u32[]{:S(2)}, u32[]{:S(2)}) collective-permute-start(f32[256,128]{1,0:T(8,128)S(1)} %get-tuple-element.91.rest_0_), channel_id=1, source_target_pairs={{2,0},{3,1},{10,8},{11,9},{18,16},{19,17},{26,24},{27,25}} | collective-permute-start | bytes 393224 | tf_op jit(solution)/shard_map/ppermute | solution.py:299
  80.6 8.4 %collective-permute-start.20 = (f32[1,128]{1,0:T(1,128)S(1)}, f32[1,128]{1,0:T(1,128)S(1)}, u32[]{:S(2)}, u32[]{:S(2)}) collective-permute-start(f32[1,128]{1,0:T(1,128)S(1)} %broadcast_select_fusion.2), channel_id=1, source_target_pairs={{0,2},{1,3},{2,0},{3,1},{4,6},{5,7},{6,4},{7,5},{8,10},{9,11},{10,... | collective-permute-start | bytes 1544 | tf_op jit(solution)/shard_map/ppermute | solution.py:251
  83.4 1.3 %collective-permute-start.21 = (f32[256,128]{1,0:T(8,128)S(1)}, f32[256,128]{1,0:T(8,128)S(1)}, u32[]{:S(2)}, u32[]{:S(2)}) collective-permute-start(f32[256,128]{1,0:T(8,128)S(1)} %get-tuple-element.83), channel_id=1, source_target_pairs={{0,1},{1,0},{2,3},{3,2},{4,5},{5,4},{6,7},{7,6},{8,9},{9,8},{10,11... | collective-permute-start | bytes 393224 | tf_op jit(solution)/shard_map/ppermute | solution.py:251
  89.2 1.1 %collective-permute-start.23 = (f32[1,64]{1,0:T(1,128)S(1)}, f32[1,64]{1,0:T(1,128)S(1)}, u32[]{:S(2)}, u32[]{:S(2)}) collective-permute-start(f32[1,64]{1,0:T(1,128)S(1)} %broadcast_select_fusion), channel_id=1, source_target_pairs={{0,1},{1,0},{2,3},{3,2},{4,5},{5,4},{6,7},{7,6},{8,9},{9,8},{10,11... | collective-permute-start | bytes 776 | tf_op jit(solution)/shard_map/ppermute | solution.py:251
  89.4 1.5 %collective-permute-start.22 = (f32[256,128]{1,0:T(8,128)S(1)}, f32[256,128]{1,0:T(8,128)S(1)}, u32[]{:S(2)}, u32[]{:S(2)}) collective-permute-start(f32[256,128]{1,0:T(8,128)S(1)} %get-tuple-element.79), channel_id=1, source_target_pairs={{0,1},{1,0},{2,3},{3,2},{4,5},{5,4},{6,7},{7,6},{8,9},{9,8},{10,11... | collective-permute-start | bytes 393224 | tf_op jit(solution)/shard_map/ppermute | solution.py:251
  (3 other events, 2.0 us)

commit v8 on v7

v8 whole, which is shorter than its diff:
```python
import functools

import jax
import jax.numpy as jnp
from jax import lax
from jax.experimental import pallas as pl
from jax.experimental.pallas import tpu as pltpu
from jax.sharding import PartitionSpec as P

E = 64
PAIR = 2 * E
GROUPS = 2
EXTRA = 8
VMEM = 10 * 2**20
SUB = 2
F32 = jnp.float32
BF16 = jnp.bfloat16


def dot(a, b, ca, cb):
    return lax.dot_general(a, b, (((ca,), (cb,)), ((), ())), preferred_element_type=F32)


def low_lanes(rows, cols):
    lane = lax.broadcasted_iota(jnp.int32, (rows, cols), 1)
    return lane % PAIR < E


def fold(product):
    return jnp.where(low_lanes(E, product.shape[1]), product[:E], product[E:])


def split(state):
    high = state.astype(BF16)
    return high, (state - high.astype(F32)).astype(BF16)


def spread(state):
    low = low_lanes(*state.shape)
    zero = jnp.zeros_like(state)
    return jnp.concatenate([jnp.where(low, state, zero), jnp.where(low, zero, state)], axis=0)


def heads_of(pair):
    low = low_lanes(*pair.shape)
    zero = jnp.zeros_like(pair)
    return jnp.where(low, pair, zero), jnp.where(low, zero, pair)


def twice(x):
    return jnp.concatenate([x, x], axis=1)


def pair_at(ref, p):
    return ref[:, p * PAIR:(p + 1) * PAIR]


def rows_at(p):
    return pl.ds(pl.multiple_of(p * E, E), E)


def own_or_received(keep, received, own, p):
    return jnp.where(own, keep[rows_at(p)], received[rows_at(p)])


def state_pair(a, b):
    return fold(dot(a, b, 0, 0))


def edge(seg, table, last):
    row = seg[...]
    count = row.shape[1]
    own = row[:, count - 1:] if last else row[:, :1]
    size = jnp.sum((row == own).astype(F32), axis=1, keepdims=True)
    at = lax.broadcasted_iota(jnp.int32, (count, PAIR), 0).astype(F32)
    rows = at >= count - size if last else at < size
    ids = lax.broadcasted_iota(jnp.int32, table.shape, 1)
    flag = jnp.sum(jnp.where(ids == own, table[...], 0).astype(F32), axis=1, keepdims=True)
    return rows, own.astype(F32), flag


def lanes_at(base, p):
    return pl.ds(pl.multiple_of(base + p * PAIR, PAIR), PAIR)


def place(group, core, lanes, sub):
    step = pl.program_id(0)
    half = (step // sub + core[0]) % 2
    base = half * lanes + step % sub * (lanes // sub)
    return half, base, 2 * group * lanes + base


def states_kernel(core, k_in, v_in, keep, send, zero, k, v, sems):
    lanes = k.shape[1] // GROUPS // 2
    count = lanes // PAIR
    copies = []
    for half in (1, 0):
        for group in range(GROUPS):
            slot = 2 * group + half
            at = pl.ds(pl.multiple_of((2 * group + (half + core[0]) % 2) * lanes, lanes), lanes)
            for i, (array, buf) in enumerate(((k_in, k), (v_in, v))):
                copies.append(pltpu.make_async_copy(array.at[:, at], buf.at[:, at], sems.at[slot, i]))
    for copy in copies:
        copy.start()
    zero[...] = jnp.zeros_like(zero)
    for half, out in ((1, send), (0, keep)):
        for group in range(GROUPS):
            copies.pop(0).wait()
            copies.pop(0).wait()
            base = (2 * group + (half + core[0]) % 2) * lanes
            for p in range(count):
                at = lanes_at(base, p)
                row = (group * count + p) * E
                out[row:row + E] = state_pair(k[:, at], v[:, at])


def part_kernel(q_in, dy_in, k, v, seg, table, *rest):
    *outs, q, dy, token, sems = rest[-GROUPS - 4:]
    copies = [pltpu.make_async_copy(a, b, sems.at[i]) for i, (a, b) in enumerate(((q_in, q), (dy_in, dy)))]
    for copy in copies:
        copy.start()
    token[...] = jnp.zeros_like(token)
    count = k.shape[1] // GROUPS // 2 // PAIR
    rows, own, _ = edge(seg, table, False)
    sel = rows.astype(BF16)
    for i in range(2 * GROUPS):
        out = outs[i // 2]
        for p in range(count):
            out[i % 2, p * E:(p + 1) * E] = state_pair(pair_at(k, i * count + p), pair_at(v, i * count + p) * sel)
        out[i % 2, count * E:] = jnp.broadcast_to(own, (EXTRA, PAIR))
    for copy in copies:
        copy.wait()


def local_kernel(group, core, q, k, v, mask, mask_t, *rest):
    attn, probs, token = rest[-3:]
    lanes = q.shape[1] // GROUPS // 2
    half, base, wide = place(group, core, lanes, 1)
    m, mt = mask[...], mask_t[...]
    token[...] = jnp.zeros_like(token)
    for p in range(lanes // PAIR):
        at = lanes_at(wide, p)
        kp = k[:, at]
        total = None
        for h, (qh, vh) in enumerate(zip(heads_of(q[:, at]), heads_of(v[:, at]))):
            prob = dot(qh, kp, 1, 1).astype(BF16) * m
            probs[half * (lanes // E) + 2 * p + h] = dot(kp, qh, 1, 1).astype(BF16) * mt
            term = dot(prob, vh, 1, 0)
            total = term if total is None else total + term
        attn[:, lanes_at(base, p)] = total


def head_mean(x):
    high, low = split(x)
    ones = spread(jnp.full((E, PAIR), 1.0 / E, BF16))
    return dot(jnp.concatenate([high, low], axis=1), jnp.concatenate([ones, ones], axis=0), 1, 0)


def side_by_side(state, part):
    sh, sl = split(state)
    ph, pll = split(part)
    left = jnp.concatenate([spread(sh), spread(sl)], axis=0)
    right = jnp.concatenate([spread(ph), spread(pll)], axis=0)
    return jnp.concatenate([left, right], axis=1)


def stacked(state, part):
    sh, sl = split(state)
    ph, pll = split(part)
    top = jnp.concatenate([spread(sh), spread(sl)], axis=1)
    bottom = jnp.concatenate([spread(ph), spread(pll)], axis=1)
    return jnp.concatenate([top, bottom], axis=0)


def on_rows(seg, table, last, part):
    rows, own, flag = edge(seg, table, last)
    met = part[0, part.shape[1] - EXTRA:part.shape[1] - EXTRA + 1] == own
    if last:
        met = met & (flag == 1)
    return rows.astype(F32) * met.astype(F32)


def norm_kernel(group, core, q, dy, local, gain, seg, table, pre_keep, pre_recv, nxt, *rest):
    out, dab, part, gsum, keep, send, token = rest[-7:]
    token[...] = jnp.zeros_like(token)
    step = pl.program_id(0)
    lanes = out.shape[1]
    count = lanes // PAIR
    _, base, wide = place(group, core, lanes, 1)
    on_next = on_rows(seg, table, True, nxt)
    last, own, flag = edge(seg, table, True)
    last = (last.astype(F32) * jnp.where(flag == 1, 1.0, 0.0)).astype(BF16)
    pairs = [slice(p * PAIR, (p + 1) * PAIR) for p in range(count)]
    bases = [lanes_at(base, p) for p in range(count)]
    wides = [lanes_at(wide, p) for p in range(count)]
    fars = [
        dot(twice(q[:, at]), side_by_side(own_or_received(pre_keep, pre_recv, step == 0, p), nxt[0, rows_at(p)]), 1, 0)
        for p, at in enumerate(wides)
    ]
    attns = [local[:, at] + far[:, :PAIR] + on_next * far[:, PAIR:] for at, far in zip(bases, fars)]
    squares = [head_mean(attn * attn) for attn in attns]
    scales = [lax.rsqrt(square + 1e-06) for square in squares]
    normeds = [attn * scale for attn, scale in zip(attns, scales)]
    gas = [dy[:, at].astype(F32) * gain[:, pair] for at, pair in zip(wides, pairs)]
    means = [head_mean(ga * normed) for ga, normed in zip(gas, normeds)]
    das = [
        (scale * (ga - normed * mean)).astype(BF16)
        for scale, ga, normed, mean in zip(scales, gas, normeds, means)
    ]
    states = [state_pair(q[:, at], jnp.concatenate([da, da * last], axis=1)) for at, da in zip(wides, das)]
    part[0, count * E:] = jnp.broadcast_to(own, (EXTRA, PAIR))
    for p, (at, normed, da) in enumerate(zip(pairs, normeds, das)):
        part[0, p * E:(p + 1) * E] = states[p][:, PAIR:]
        dab[:, bases[p]] = da
        out[:, at] = (normed * gain[:, at]).astype(BF16)
        gsum[0, p:p + 1] = jnp.sum(dy[:, wides[p]].astype(F32) * normed, axis=0, keepdims=True)

    @pl.when(step == 0)
    def _():
        for p, state in enumerate(states):
            keep[p * E:(p + 1) * E] = state[:, :PAIR]

    @pl.when(step == 1)
    def _():
        for p, state in enumerate(states):
            send[p * E:(p + 1) * E] = state[:, :PAIR]


def inner_kernel(group, core, q, k, v, dab, probs, mask, seg, table, pre_keep, pre_recv, nxt, *rest):
    gq, gk, gv, token = rest[-4:]
    step = pl.program_id(0)
    lanes = dab.shape[1] // 2
    count = lanes // SUB // PAIR
    half, base, wide = place(group, core, lanes, SUB)
    m = mask[...]
    token[...] = jnp.zeros_like(token)
    on_next = on_rows(seg, table, True, nxt)
    for p in range(count):
        in_half = step % SUB * count + p
        at = lanes_at(wide, p)
        da = dab[:, lanes_at(base, p)]
        vp = v[:, at]
        far = dot(
            twice(da),
            stacked(own_or_received(pre_keep, pre_recv, step < SUB, in_half), nxt[0, rows_at(in_half)]), 1, 1)
        tq = far[:, :PAIR] + on_next * far[:, PAIR:]
        tk = tv = None
        for h, (qh, kh, dh) in enumerate(zip(heads_of(q[:, at]), heads_of(k[:, at]), heads_of(da))):
            dprob = dot(dh, vp, 1, 1).astype(BF16) * m
            tq = tq + dot(dprob, kh, 1, 0)
            a = dot(dprob, qh, 0, 0)
            b = dot(probs[half * (lanes // E) + 2 * in_half + h], dh, 1, 0)
            tk = a if tk is None else tk + a
            tv = b if tv is None else tv + b
        gq[:, p * PAIR:(p + 1) * PAIR] = tq.astype(BF16)
        gk[:, lanes_at(base, p)] = tk
        gv[:, lanes_at(base, p)] = tv


def outer_kernel(group, core, k, v, gk_in, gv_in, seg, table, suf_keep, suf_recv, prv, *rest):
    gk, gv, token = rest[-3:]
    step = pl.program_id(0)
    lanes = gk_in.shape[1] // 2
    count = lanes // SUB // PAIR
    _, base, wide = place(group, core, lanes, SUB)
    token[...] = jnp.zeros_like(token)
    on_prev = on_rows(seg, table, False, prv)
    for p in range(count):
        in_half = step % SUB * count + p
        here, own, at = slice(p * PAIR, (p + 1) * PAIR), lanes_at(base, p), lanes_at(wide, p)
        s = own_or_received(suf_keep, suf_recv, step < SUB, in_half)
        g = prv[0, rows_at(in_half)]
        far = dot(twice(v[:, at]), stacked(s, g), 1, 1)
        gk[:, here] = (gk_in[:, own] + far[:, :PAIR] + on_prev * far[:, PAIR:]).astype(BF16)
        far = dot(twice(k[:, at]), side_by_side(s, g), 1, 0)
        gv[:, here] = (gv_in[:, own] + far[:, :PAIR] + on_prev * far[:, PAIR:]).astype(BF16)


def partner(x, axis, bit):
    route = [(i, i ^ (1 << bit)) for i in range(lax.axis_size(axis))]
    return lax.ppermute(x, axis, route)


def shifted(x, distance):
    count = lax.axis_size("ctx")
    return lax.ppermute(x, "ctx", [(i, i + distance) for i in range(count) if 0 <= i + distance < count])


def nought(x):
    return jnp.minimum(jnp.abs(x), 0.0)


def chip_rank(towards):
    chip = lax.axis_index("ctx") // 2
    return chip if towards == 1 else lax.axis_size("ctx") // 2 - 1 - chip


def chips_before(own, towards):
    chips = lax.axis_size("ctx") // 2
    total = shifted(own, 2 * towards)
    span = 1
    while span < chips:
        total = total + shifted(total, 2 * towards * span)
        span *= 2
    return total


def pick(rank, cases):
    value = cases[-1][1]
    for at, case in cases[:-1]:
        value = jnp.where(rank == at, case, value)
    return value


def chain_load(owns, starts, arrived, step, towards):
    chips = lax.axis_size("ctx") // 2
    cases = [(step - at, own) for own, at in zip(owns, starts) if 0 <= step - at <= chips - 2]
    load = pick(chip_rank(towards), cases)
    return load if arrived is None else load + arrived


def chain_step(load, starts, step, towards):
    chips = lax.axis_size("ctx") // 2
    route = []
    for rank in range(chips - 1):
        if step - rank in starts:
            chip = rank if towards == 1 else chips - 1 - rank
            route += [(2 * chip + c, 2 * (chip + towards) + c) for c in range(2)]
    return lax.ppermute(load, "ctx", route)


def chain_result(arrivals, start, towards):
    chips = lax.axis_size("ctx") // 2
    cases = [(rank, arrivals[start + rank - 1]) for rank in range(1, chips)]
    return pick(chip_rank(towards), cases + [(0, jnp.zeros_like(arrivals[0]))])


def within_chip(keep, send):
    received = partner(send, "ctx", 0)
    return keep, received, keep + received


def to_cores(before, piece, towards):
    keep, received, _ = piece
    is_source = lax.axis_index("ctx") & 1 == (0 if towards == 1 else 1)
    mine = jnp.where(is_source, before, before + received)
    return mine, partner(jnp.where(is_source, before + keep, before), "ctx", 0)


def pinned(x, space):
    return pltpu.with_memory_space_constraint(x, space)


def scatter_step(x, axis, bit):
    upper = lax.axis_index(axis) >> bit & 1 == 1
    low, high = jnp.split(x, 2, axis=0 if x.shape[0] > 1 else 1)
    return jnp.where(upper, high, low) + partner(jnp.where(upper, low, high), axis, bit)


def on_device(queries, keys, values, out_grad, segment_ids, image_flags, gain):
    rows, width = queries.shape[1:]
    q, k, v, dy = (x[0] for x in (queries, keys, values, out_grad))
    table = image_flags[0]
    gain_row = gain.reshape(1, width)
    core = (lax.axis_index("ctx") & 1).reshape(1).astype(jnp.int32)
    lanes = width // GROUPS // 2
    half_rows = lanes // PAIR * E
    heads = lanes // E

    def call(kernel, group, ins, outs, after=(), alias=(), scratch=(), sub=1, steps=None):
        def half_of(i, c):
            return (i // sub + c[0]) % 2

        def wide(i, c):
            return (0, (2 * group + half_of(i, c)) * sub + i % sub)

        def whole(*args):
            return (0, 0)

        def part(i, c):
            return (half_of(i, c), 0, 0)

        specs = {
            "vmem": pl.BlockSpec(memory_space=pltpu.VMEM),
            "hbm": pl.BlockSpec(memory_space=pltpu.HBM),
            "wide": pl.BlockSpec((rows, lanes // sub), wide),
            "row": pl.BlockSpec((1, lanes // sub), wide),
            "sums": pl.BlockSpec((1, lanes // PAIR, PAIR), part),
            "zero": pl.BlockSpec((1, rows), whole),
            "half": pl.BlockSpec((half_rows, PAIR), whole),
            "all": pl.BlockSpec((GROUPS * half_rows, PAIR), whole),
            "part": pl.BlockSpec((1, half_rows + EXTRA, PAIR), part),
            "parts": pl.BlockSpec((2, half_rows + EXTRA, PAIR), lambda *args: (0, 0, 0)),
            "seg": pl.BlockSpec((1, rows), whole),
            "table": pl.BlockSpec((1, table.shape[0]), whole),
            "mask": pl.BlockSpec((rows, rows), whole),
            "token": pl.BlockSpec((1, PAIR), whole),
            "after2": pl.BlockSpec((8, PAIR), whole),
            "after3": pl.BlockSpec((1, 8, PAIR), lambda *args: (0, 0, 0)),
            "any": pl.BlockSpec(memory_space=pl.ANY),
        }
        shapes = {
            "wide": (rows, width),
            "sums": (2, lanes // PAIR, PAIR),
            "zero": (1, rows),
            "half": (half_rows, PAIR),
            "all": (GROUPS * half_rows, PAIR),
            "part": (2, half_rows + EXTRA, PAIR),
            "parts": (2, half_rows + EXTRA, PAIR),
            "token": (1, PAIR),
        }
        spaces = {"vmem": pltpu.VMEM, "hbm": pltpu.HBM}
        operands = [pinned(x, spaces[kind]) if kind in spaces else x for kind, x in ins] + list(after)
        kinds = [kind for kind, _ in ins] + [f"after{x.ndim}" for x in after]
        aliases = {}
        for out_at, x in alias:
            if x is not None:
                aliases[1 + len(operands)] = out_at
                operands.append(x)
                kinds.append("any")
        out_shape = [
            pltpu.VMEM(*shape, dtype) if kind == "vmem" else jax.ShapeDtypeStruct(shapes[kind], dtype)
            for kind, dtype, *shape in outs
        ]
        return pl.pallas_call(
            kernel,
            grid_spec=pltpu.PrefetchScalarGridSpec(
                num_scalar_prefetch=1,
                grid=steps or (2 * sub,),
                in_specs=[specs[kind] for kind in kinds],
                out_specs=[specs[kind] for kind, *_ in outs],
                scratch_shapes=scratch,
            ),
            out_shape=out_shape,
            input_output_aliases=aliases,
            compiler_params=pltpu.CompilerParams(vmem_limit_bytes=VMEM),
            cost_estimate=pl.CostEstimate(flops=1, bytes_accessed=1, transcendentals=0),
        )(core, *operands)

    edges = [("seg", segment_ids), ("table", image_flags)]
    groups = range(GROUPS)
    chips = lax.axis_size("ctx") // 2
    chained = GROUPS < chips <= 8

    whole, group_of = (rows, width), (rows, 2 * lanes)

    def local_attn(g, after):
        return call(
            functools.partial(local_kernel, g), g,
            [("vmem", q), ("vmem", k), ("vmem", v), ("mask", mask), ("mask", mask_t)],
            [("vmem", F32, group_of), ("vmem", BF16, (2 * heads, rows, rows)), ("token", F32)], after=after)

    def norm(g, prefix, before, after):
        output, dab, prv, gsum, keep, send, token = call(
            functools.partial(norm_kernel, g), g,
            [("vmem", q), ("vmem", dy), ("vmem", local[g][0]), ("row", gain_row), *edges,
             ("half", prefix[0]), ("half", prefix[1]), ("part", nxt[g])],
            [("wide", BF16), ("vmem", BF16, group_of), ("part", F32), ("sums", F32), ("half", F32), ("half", F32),
             ("token", F32)],
            after=after, alias=[(0, before)])
        return output, dab, prv, gsum, (keep, send), token

    def inner(g, before, after):
        return call(
            functools.partial(inner_kernel, g), g,
            [("vmem", q), ("vmem", k), ("vmem", v), ("vmem", norms[g][1]), ("vmem", local[g][1]), ("mask", mask), *edges,
             ("half", prefix[g][0]), ("half", prefix[g][1]), ("part", nxt[g])],
            [("wide", BF16), ("vmem", F32, group_of), ("vmem", F32, group_of), ("token", F32)],
            after=after, alias=[(0, before)], sub=SUB)

    def outer(g, suffix, before, after):
        return call(
            functools.partial(outer_kernel, g), g,
            [("vmem", k), ("vmem", v), ("vmem", inners[g][1]), ("vmem", inners[g][2]), *edges,
             ("half", suffix[0]), ("half", suffix[1]), ("part", prv[g])],
            [("wide", BF16), ("wide", BF16), ("token", F32)], after=after, alias=list(enumerate(before)), sub=SUB)

    keep, send, zero, k, v = call(
        states_kernel, 0, [("hbm", k), ("hbm", v)],
        [("all", F32), ("all", F32), ("zero", jnp.int32), ("vmem", BF16, whole), ("vmem", BF16, whole)],
        scratch=[pltpu.SemaphoreType.DMA((2 * GROUPS, 2))], steps=(1,))
    keep, received, total = within_chip(keep, send)
    owns = [tuple(x[g * half_rows:(g + 1) * half_rows] for x in (keep, received, total)) for g in groups]
    sums = [own for _, _, own in owns]
    seg = (segment_ids + zero)[0]
    onehot = seg[:, None] == jnp.arange(table.shape[0], dtype=jnp.int32)[None, :]
    img = jnp.sum(jnp.where(onehot, table[None, :], 0), axis=1)
    imgseg = jnp.where(img == 1, seg, -1)
    pos = jnp.arange(rows)
    mask = ((pos[:, None] >= pos[None, :]) | (imgseg[:, None] == seg[None, :])).astype(BF16)
    mask_t = ((pos[:, None] <= pos[None, :]) | (seg[:, None] == imgseg[None, :])).astype(BF16)

    local, nxt, arrivals = [], [], []
    starts = list(groups)
    last = chips - 2 + starts[-1]
    load = sums[0]
    *parts, q, dy, token = call(
        lambda core, *refs: part_kernel(*refs), 0, [("hbm", q), ("hbm", dy), ("vmem", k), ("vmem", v), *edges],
        [("parts", F32)] * GROUPS + [("vmem", BF16, whole), ("vmem", BF16, whole), ("token", F32)],
        after=[load], scratch=[pltpu.SemaphoreType.DMA((2,))], steps=(1,))
    for step in range(last + 1 if chained else GROUPS + 1):
        if chained:
            arrivals.append(chain_step(load, starts, step, 1))
        if 1 <= step <= GROUPS:
            nxt.append(shifted(parts[step - 1], -1))
            *attn, token = local_attn(step - 1, [load])
            local.append(attn)
            token = token + nought(nxt[-1][0, :1])
        if step < last and chained:
            load = chain_load(sums, starts, arrivals[-1] + token, step + 1, 1)
    prefix, norms = [], []
    before = chain_result(arrivals, starts[0], 1) if chained else chips_before(sums[0], 1)
    prefix.append(to_cores(before, owns[0], 1))
    norms.append(norm(0, prefix[0], None, [load]))

    ins, ins_starts, ins_arrivals = owns, starts, arrivals
    owns = [within_chip(*norms[0][4])]
    sums = [owns[0][2]]
    load = sums[0]
    for g in groups[1:]:
        if chained:
            ins_arrivals[-1] = ins_arrivals[-1] + norms[-1][5]
        before = chain_result(ins_arrivals, ins_starts[g], 1) if chained else chips_before(ins[g][2], 1)
        prefix.append(to_cores(before, ins[g], 1))
        norms.append(norm(g, prefix[g], norms[-1][0], [load]))
        owns.append(within_chip(*norms[-1][4]))
        sums.append(owns[-1][2])
    output = norms[-1][0]
    prv = [n[2] for n in norms]
    gain_sum = jnp.concatenate([n[3] for n in norms], axis=0).reshape(-1, PAIR)
    bits = [(axis, bit) for axis in ("dp", "ctx") for bit in reversed(range(lax.axis_size(axis).bit_length() - 1))]
    arrivals, inners, outers = [], [], [None] * 2
    starts = [0] + [g + 1 for g in groups[1:]]
    last = chips - 2 + starts[-1]
    token = norms[-1][5]
    for step in range(last + 1 if chained else GROUPS + 1):
        if chained:
            if step:
                load = chain_load(sums, starts, arrivals[-1] + token, step, -1)
            arrivals.append(chain_step(load, starts, step, -1))
        if step == 0:
            prv[0] = shifted(prv[0], 1)
            token = token + nought(prv[0][0, :1])
            continue
        token = jnp.zeros((1, PAIR), F32)
        if 2 <= step and len(bits) > 2:
            gain_sum = scatter_step(gain_sum + nought(load[:1]), *bits.pop(0))
            token = token + nought(gain_sum[:1])
        if step == GROUPS + 1 or (not chained and step == 1):
            for g in groups[1:]:
                prv[g] = shifted(prv[g] + nought(load[:1]), 1)
                token = token + nought(prv[g][0, :1])
        if step <= GROUPS:
            inners.append(inner(step - 1, inners[-1][0] if inners else None, [load]))
            token = token + inners[-1][3]
    for g in groups:
        if g and chained:
            arrivals[-1] = arrivals[-1] + token
        before = chain_result(arrivals, starts[g], -1) if chained else chips_before(sums[g], -1)
        *outers, done = outer(g, to_cores(before, owns[g], -1), outers, [])
        token = token + done
    for axis, bit in bits:
        gain_sum = scatter_step(gain_sum, axis, bit)
    grad_q = inners[-1][0]
    grad_k, grad_v = outers
    grad_gain = gain_sum.reshape(-1)
    return output[None], grad_q[None], grad_k[None], grad_v[None], grad_gain


def solution(mesh):
    return jax.shard_map(
        on_device,
        mesh=mesh,
        in_specs=(
            P("dp", "ctx", None),
            P("dp", "ctx", None),
            P("dp", "ctx", None),
            P("dp", "ctx", None),
            P("dp", "ctx"),
            P("dp", None),
            P(),
        ),
        out_specs=(
            P("dp", "ctx", None),
            P("dp", "ctx", None),
            P("dp", "ctx", None),
            P("dp", "ctx", None),
            P(("dp", "ctx")),
        ),
        check_vma=False,
    )
```

time: 96.2 us -> 134 us (1.39)
  local copies, waits for them, and re-layouts: 0.87 us -> 27.5 us
  other arithmetic: 1.48 us -> 14.9 us
  Pallas kernels: 46.2 us -> 35.3 us
  starting transfers between devices: 35.2 us -> 42.9 us
    unnamed x6 -> x132, local copies, waits for them, and re-layouts: 0.86 us -> 27.5 us
    pallas_call x11 -> x10, Pallas kernels: 46.2 us -> 35.3 us  [call(): pl.pallas_call(kernel, grid_spec=pltpu.PrefetchScalarGridSpec(num_scalar_...]
    ppermute x12, starting transfers between devices: 13.8 us -> 18.1 us  [partner(): return lax.ppermute(x, axis, route)]
    add x4 -> x5, other arithmetic: 0.12 us -> 4.31 us  [chain_load(): return load if arrived is None else load + arrived]
    add x7 -> x6, other arithmetic: 0.04 us -> 2.77 us  [the longest x2 1.36 us: on_device(): load = chain_load(sums, starts, arrivals[-1] + token, step + 1, 1)]
    ppermute x8 -> x9, starting transfers between devices: 15 us -> 17.3 us  [chain_step(): return lax.ppermute(load, 'ctx', route)]
    add x3 -> x4, other arithmetic: 0.02 us -> 2.27 us  [scatter_step(): jnp.where(upper, high, low)]
    select_n x4, other arithmetic: 0.06 us -> 1.9 us  [to_cores(): mine = jnp.where(is_source, before, before + received)]
  transfers between devices with their start and end apart: 24 -> 25, of which waited for: 8 -> 7; matrix products, arithmetic and copies ran while one was open for 1% -> 7% of each run, Pallas kernels for 33% -> 22%
where the time goes in v8:
time: 134 us; the launch traced here: 133 us
  starting transfers between devices  42.9 us (32%)
  Pallas kernels  35.3 us (26%)
  local copies, waits for them, and re-layouts  27.5 us (21%)
  other arithmetic  14.9 us (11%)
  waiting for transfers between devices  10.9 us (8%)
    pallas_call x10, Pallas kernels, call(): pl.pallas_call(kernel, grid_spec=pltpu.PrefetchScalarGridSpec(num_scalar_...  35.3 us
    unnamed x132, local copies, waits for them, and re-layouts  27.5 us
    ppermute x12, starting transfers between devices, partner(): return lax.ppermute(x, axis, route)  18.1 us
    ppermute x9, starting transfers between devices, chain_step(): return lax.ppermute(load, 'ctx', route)  17.3 us
    ppermute x4, starting transfers between devices, shifted(): lax.ppermute(x, 'ctx', [(i, i + distance) for i in range(count) if 0 <= i...  7.47 us
    ppermute x9, waiting for transfers between devices, chain_step(): return lax.ppermute(load, 'ctx', route)  5.9 us
    ppermute x12, waiting for transfers between devices, partner(): return lax.ppermute(x, axis, route)  4.97 us
    add x5, other arithmetic, chain_load(): return load if arrived is None else load + arrived  4.31 us
  transfers between devices with their start and end apart: 25, of which 7 were waited for; matrix products, arithmetic and copies ran while one was open for 7% of the time, Pallas kernels for 22%

profile of v8, /device:TPU:0, one launch (start us, length us, event | category | flops | bytes accessed | tf_op | source)
XLA Modules:
  0.0 132.7 jit_solution(3594346862201195263)
XLA Ops:
  0.7 2.4 %shard_map.110 = (f32[512,128]{1,0:T(8,128)S(1)}, f32[512,128]{1,0:T(8,128)S(1)}, s32[1,256]{1,0:T(1,128)S(1)}, bf16[256,2048]{1,0:T(8,128)(2,1)S(1)}, bf16[256,2048]{1,0:T(8,128)(2,1)S(1)}) custom-call(s32[1]{0:T(128)} %bitcast.core, bf16[256,2048]{1,0:T(8,128)(2,1)} %bitcast.70, bf16[256,2048]{1,0:T(8,128)(2,1)} %bitcast.71), custom_call_target="tpu_custom_call" | custom-call | flops 1 | bytes 1 | tf_op jit(solution)/shard_map/pallas_call | solution.py:425
  4.8 5.5 %collective-permute-start.1 = (f32[256,128]{1,0:T(8,128)S(1)}, f32[256,128]{1,0:T(8,128)}, u32[]{:S(2)}, u32[]{:S(2)}) collective-permute-start(f32[256,128]{1,0:T(8,128)S(1)} %slice.65.refs_6_), channel_id=1, source_target_pairs={{0,2},{1,3},{8,10},{9,11},{16,18},{17,19},{24,26},{25,27}} | collective-permute-start | bytes 393224 | tf_op jit(solution)/shard_map/ppermute | solution.py:329
  10.3 2.3 %shard_map.111 = (f32[2,264,128]{2,1,0:T(8,128)}, f32[2,264,128]{2,1,0:T(8,128)S(1)}, bf16[256,2048]{1,0:T(8,128)(2,1)S(1)}, bf16[256,2048]{1,0:T(8,128)(2,1)S(1)}, f32[1,128]{1,0:T(1,128)S(1)}) custom-call(s32[1]{0:T(128)} %bitcast.core, bf16[256,2048]{1,0:T(8,128)(2,1)} %bitcast.72, bf16[256,2048]{1,0:T(8,128)(2,1)} %bitcast.73, ...), custom_call_target="tpu_custom_call" | custom-call | flops 1 | bytes 1 | tf_op jit(solution)/shard_map/pallas_call | solution.py:425
  18.3 5.3 %collective-permute-start.2 = (f32[256,128]{1,0:T(8,128)S(1)}, f32[256,128]{1,0:T(8,128)S(1)}, u32[]{:S(2)}, u32[]{:S(2)}) collective-permute-start(f32[256,128]{1,0:T(8,128)S(1)} %add_add_fusion.6.rest_0_), channel_id=1, source_target_pairs={{0,2},{1,3},{2,4},{3,5},{8,10},{9,11},{10,12},{11,13},{16,18},{17,... | collective-permute-start | bytes 393224 | tf_op jit(solution)/shard_map/ppermute | solution.py:329
  23.6 2.5 %shard_map.112 = (f32[256,1024]{1,0:T(8,128)S(1)}, bf16[16,256,256]{2,1,0:T(8,128)(2,1)S(1)}, f32[1,128]{1,0:T(1,128)S(1)}) custom-call(s32[1]{0:T(128)} %bitcast.core, bf16[256,2048]{1,0:T(8,128)(2,1)S(1)} %get-tuple-element.52.q, bf16[256,2048]{1,0:T(8,128)(2,1)S(1)} %get-tuple-element.48.refs_2_.k, bf16[256,2048]{1,0:T(8,128)(2,1)S(1)} %get-tuple-element.49.refs_3_.v, ...), custom_call_target="tpu_custom_call" | custom-call | flops 1 | bytes 1 | tf_op jit(solution)/shard_map/pallas_call | solution.py:425
  29.8 2.5 %shard_map.113 = (f32[256,1024]{1,0:T(8,128)S(1)}, bf16[16,256,256]{2,1,0:T(8,128)(2,1)S(1)}, f32[1,128]{1,0:T(1,128)S(1)}) custom-call(s32[1]{0:T(128)} %bitcast.core, bf16[256,2048]{1,0:T(8,128)(2,1)S(1)} %get-tuple-element.52.q, bf16[256,2048]{1,0:T(8,128)(2,1)S(1)} %get-tuple-element.48.refs_2_.k, bf16[256,2048]{1,0:T(8,128)(2,1)S(1)} %get-tuple-element.49.refs_3_.v, ...), custom_call_target="tpu_custom_call" | custom-call | flops 1 | bytes 1 | tf_op jit(solution)/shard_map/pallas_call | solution.py:425
  36.5 3.6 %shard_map.114 = (bf16[256,2048]{1,0:T(8,128)(2,1)}, bf16[256,1024]{1,0:T(8,128)(2,1)S(1)}, f32[2,264,128]{2,1,0:T(8,128)S(1)}, f32[2,4,128]{2,1,0:T(4,128)S(1)}...) custom-call(s32[1]{0:T(128)} %bitcast.core, bf16[256,2048]{1,0:T(8,128)(2,1)S(1)} %get-tuple-element.52.q, ...), custom_call_target="tpu_custom_call" | custom-call | flops 1 | bytes 1 | tf_op jit(solution)/shard_map/pallas_call | solution.py:425
  41.0 2.3 %collective-permute-start.12 = (f32[2,264,128]{2,1,0:T(8,128)S(1)}, f32[2,264,128]{2,1,0:T(8,128)S(1)}, u32[]{:S(2)}, u32[]{:S(2)}) collective-permute-start(f32[2,264,128]{2,1,0:T(8,128)S(1)} %get-tuple-element.72), channel_id=1, source_target_pairs={{0,1},{1,2},{2,3},{3,4},{4,5},{5,6},{6,7},{8,9},{9,10},{10,11},{11... | collective-permute-start | bytes 811016 | tf_op jit(solution)/shard_map/ppermute | solution.py:286
  43.4 3.8 %collective-permute-start.8 = (f32[256,128]{1,0:T(8,128)S(1)}, f32[256,128]{1,0:T(8,128)S(1)}, u32[]{:S(2)}, u32[]{:S(2)}) collective-permute-start(f32[256,128]{1,0:T(8,128)S(1)} %get-tuple-element.97), channel_id=1, source_target_pairs={{0,1},{1,0},{2,3},{3,2},{4,5},{5,4},{6,7},{7,6},{8,9},{9,8},{10,11... | collective-permute-start | bytes 393224 | tf_op jit(solution)/shard_map/ppermute | solution.py:281
  48.1 3.6 %shard_map.115 = (bf16[256,2048]{1,0:T(8,128)(2,1)}, bf16[256,1024]{1,0:T(8,128)(2,1)S(1)}, f32[2,264,128]{2,1,0:T(8,128)S(1)}, f32[2,4,128]{2,1,0:T(4,128)S(1)}...) custom-call(s32[1]{0:T(128)} %bitcast.core, ...), custom_call_target="tpu_custom_call", output_to_operand_aliasing={{0}: (11, {})} | custom-call | flops 1 | bytes 1 | tf_op jit(solution)/shard_map/pallas_call | solution.py:425
  57.7 1.6 %copy-done.5 = bf16[16,256,256]{2,1,0:T(8,128)(2,1)S(1)} copy-done((bf16[16,256,256]{2,1,0:T(8,128)(2,1)S(1)}, bf16[16,256,256]{2,1,0:T(8,128)(2,1)}, u32[]{:S(2)}) %copy-start.5) | copy-done | bytes 2097176
  62.1 6.1 %shard_map.116 = (bf16[256,2048]{1,0:T(8,128)(2,1)}, f32[256,1024]{1,0:T(8,128)S(1)}, f32[256,1024]{1,0:T(8,128)S(1)}, f32[1,128]{1,0:T(1,128)S(1)}) custom-call(s32[1]{0:T(128)} %bitcast.core, bf16[256,2048]{1,0:T(8,128)(2,1)S(1)} %get-tuple-element.52.q, bf16[256,2048]{1,0:T(8,128)(2,1)S(1)} %get-tuple-element.48.refs_2_.k, ...), custom_call_target="tpu_custom_call" | custom-call | flops 1 | bytes 1 | tf_op jit(solution)/shard_map/pallas_call | solution.py:425
  70.2 1.6 %add_add_fusion.2 = (f32[256,128]{1,0:T(8,128)S(1)}, f32[256,128]{1,0:T(8,128)}) fusion(f32[256,128]{1,0:T(8,128)} %collective-permute-done.13, f32[256,128]{1,0:T(8,128)S(1)} %add.242.rest_0_, f32[128]{0:T(128)S(1)} %bitcast.64, pred[]{:T(512)S(6)} %eq.131, f32[256,128]{1,0:T(8,128)S(1)} %copy-done.31, f32[256,128]{1,0:T(8,128)} %collective-permute-done.10), kind=kLoop, calls=%fused_computation.19 | loop fusion | flops 131072 | bytes 786945 | tf_op jit(solution)/shard_map/add | solution.py:319
  73.7 1.5 %collective-permute-start.15 = (f32[8,128]{1,0:T(8,128)}, f32[8,128]{1,0:T(8,128)}, u32[]{:S(2)}, u32[]{:S(2)}) collective-permute-start(f32[8,128]{1,0:T(8,128)} %slice_select_fusion), channel_id=1, source_target_pairs={{0,16},{8,24},{16,0},{24,8},{1,17},{9,25},{17,1},{25,9},{2,18},{10... | collective-permute-start | bytes 12296 | tf_op jit(solution)/shard_map/ppermute | solution.py:281
  76.5 1.6 %copy-done.3 = bf16[16,256,256]{2,1,0:T(8,128)(2,1)S(1)} copy-done((bf16[16,256,256]{2,1,0:T(8,128)(2,1)S(1)}, bf16[16,256,256]{2,1,0:T(8,128)(2,1)}, u32[]{:S(2)}) %copy-start.3) | copy-done | bytes 2097176
  80.9 6.2 %shard_map.117 = (bf16[256,2048]{1,0:T(8,128)(2,1)}, f32[256,1024]{1,0:T(8,128)S(1)}, f32[256,1024]{1,0:T(8,128)S(1)}, f32[1,128]{1,0:T(1,128)S(1)}) custom-call(s32[1]{0:T(128)} %bitcast.core, bf16[256,2048]{1,0:T(8,128)(2,1)S(1)} %get-tuple-element.52.q, bf16[256,2048]{1,0:T(8,128)(2,1)S(1)} %get-tuple-element.48.refs_2_.k, ...), custom_call_target="tpu_custom_call", output_to_operand_aliasing={{0}: (13, {})} | custom-call | flops 1 | bytes 1 | tf_op jit(solution)/shard_map/pallas_call | solution.py:425
  91.5 2.5 %collective-permute-start.18 = (f32[2,264,128]{2,1,0:T(8,128)}, f32[2,264,128]{2,1,0:T(8,128)}, u32[]{:S(2)}, u32[]{:S(2)}) collective-permute-start(f32[2,264,128]{2,1,0:T(8,128)} %broadcast_add_fusion), channel_id=1, source_target_pairs={{0,1},{1,2},{2,3},{3,4},{4,5},{5,6},{6,7},{8,9},{9,10},{10,11},{11... | collective-permute-start | bytes 811016 | tf_op jit(solution)/shard_map/ppermute | solution.py:286
  94.5 1.5 %collective-permute-start.17 = (f32[4,128]{1,0:T(4,128)}, f32[4,128]{1,0:T(4,128)}, u32[]{:S(2)}, u32[]{:S(2)}) collective-permute-start(f32[4,128]{1,0:T(4,128)} %slice_select_fusion.1), channel_id=1, source_target_pairs={{0,8},{8,0},{16,24},{24,16},{1,9},{9,1},{17,25},{25,17},{2,10},{10... | collective-permute-start | bytes 6152 | tf_op jit(solution)/shard_map/ppermute | solution.py:281
  96.7 1.7 %collective-permute-done.17 = f32[4,128]{1,0:T(4,128)} collective-permute-done((f32[4,128]{1,0:T(4,128)}, f32[4,128]{1,0:T(4,128)}, u32[]{:S(2)}, u32[]{:S(2)}) %collective-permute-start.17) | collective-permute-done | bytes 2080 | tf_op jit(solution)/shard_map/ppermute | solution.py:281
  103.2 5.6 %collective-permute-start.20 = (f32[2,128]{1,0:T(2,128)}, f32[2,128]{1,0:T(2,128)}, u32[]{:S(2)}, u32[]{:S(2)}) collective-permute-start(f32[2,128]{1,0:T(2,128)} %broadcast_select_fusion.4), channel_id=1, source_target_pairs={{0,4},{1,5},{2,6},{3,7},{4,0},{5,1},{6,2},{7,3},{8,12},{9,13},{10,... | collective-permute-start | bytes 3080 | tf_op jit(solution)/shard_map/ppermute | solution.py:281
  111.5 3.5 %collective-permute-start.23 = (f32[1,128]{1,0:T(1,128)S(1)}, f32[1,128]{1,0:T(1,128)S(1)}, u32[]{:S(2)}, u32[]{:S(2)}) collective-permute-start(f32[1,128]{1,0:T(1,128)S(1)} %broadcast_select_fusion), channel_id=1, source_target_pairs={{0,2},{1,3},{2,0},{3,1},{4,6},{5,7},{6,4},{7,5},{8,10},{9,11},{10,... | collective-permute-start | bytes 1544 | tf_op jit(solution)/shard_map/ppermute | solution.py:281
  117.2 2.5 %shard_map.118 = (bf16[256,2048]{1,0:T(8,128)(2,1)}, bf16[256,2048]{1,0:T(8,128)(2,1)}, f32[1,128]{1,0:T(1,128)S(1)}) custom-call(s32[1]{0:T(128)} %bitcast.core, bf16[256,2048]{1,0:T(8,128)(2,1)S(1)} %get-tuple-element.48.refs_2_.k, bf16[256,2048]{1,0:T(8,128)(2,1)S(1)} %get-tuple-element.49.refs_3_.v, f32[256,1024]{1,0:T(8,128)S(1)} %copy-done.17, ...), custom_call_target="tpu_custom_call" | custom-call | flops 1 | bytes 1 | tf_op jit(solution)/shard_map/pallas_call | solution.py:425
  121.7 5.9 %collective-permute-done.19 = f32[256,128]{1,0:T(8,128)S(1)} collective-permute-done((f32[256,128]{1,0:T(8,128)S(1)}, f32[256,128]{1,0:T(8,128)S(1)}, u32[]{:S(2)}, u32[]{:S(2)}) %collective-permute-start.19) | collective-permute-done | bytes 131104 | tf_op jit(solution)/shard_map/ppermute | solution.py:329
  129.1 3.6 %shard_map.119 = (bf16[256,2048]{1,0:T(8,128)(2,1)}, bf16[256,2048]{1,0:T(8,128)(2,1)}, f32[1,128]{1,0:T(1,128)}) custom-call(s32[1]{0:T(128)} %bitcast.core, bf16[256,2048]{1,0:T(8,128)(2,1)S(1)} %get-tuple-element.48.refs_2_.k, bf16[256,2048]{1,0:T(8,128)(2,1)S(1)} %get-tuple-element.49.refs_3_.v, ...), custom_call_target="tpu_custom_call", output_to_operand_aliasing={{0}: (10, {}), {1}: (11, {})} | custom-call | flops 1 | bytes 1 | tf_op jit(solution)/shard_map/pallas_call | solution.py:425
  (212 shorter events, 52.2 us)
Async XLA Ops:
  3.1 1.7 %collective-permute-start = (f32[512,128]{1,0:T(8,128)S(1)}, f32[512,128]{1,0:T(8,128)S(1)}, u32[]{:S(2)}, u32[]{:S(2)}) collective-permute-start(f32[512,128]{1,0:T(8,128)S(1)} %get-tuple-element.51), channel_id=1, source_target_pairs={{0,1},{1,0},{2,3},{3,2},{4,5},{5,4},{6,7},{7,6},{8,9},{9,8},{10,11... | collective-permute-start | bytes 786440 | tf_op jit(solution)/shard_map/ppermute | solution.py:281
  4.8 12.4 %collective-permute-start.1 = (f32[256,128]{1,0:T(8,128)S(1)}, f32[256,128]{1,0:T(8,128)}, u32[]{:S(2)}, u32[]{:S(2)}) collective-permute-start(f32[256,128]{1,0:T(8,128)S(1)} %slice.65.refs_6_), channel_id=1, source_target_pairs={{0,2},{1,3},{8,10},{9,11},{16,18},{17,19},{24,26},{25,27}} | collective-permute-start | bytes 393224 | tf_op jit(solution)/shard_map/ppermute | solution.py:329
  14.3 14.1 %collective-permute-start.3 = (f32[2,264,128]{2,1,0:T(8,128)}, f32[2,264,128]{2,1,0:T(8,128)}, u32[]{:S(2)}, u32[]{:S(2)}) collective-permute-start(f32[2,264,128]{2,1,0:T(8,128)} %get-tuple-element.57), channel_id=1, source_target_pairs={{1,0},{2,1},{3,2},{4,3},{5,4},{6,5},{7,6},{9,8},{10,9},{11,10},{12... | collective-permute-start | bytes 811016 | tf_op jit(solution)/shard_map/ppermute | solution.py:286
  15.8 18.5 %collective-permute-start.5 = (f32[2,264,128]{2,1,0:T(8,128)}, f32[2,264,128]{2,1,0:T(8,128)}, u32[]{:S(2)}, u32[]{:S(2)}) collective-permute-start(f32[2,264,128]{2,1,0:T(8,128)} %copy-done.42), channel_id=1, source_target_pairs={{1,0},{2,1},{3,2},{4,3},{5,4},{6,5},{7,6},{9,8},{10,9},{11,10},{12... | collective-permute-start | bytes 811016 | tf_op jit(solution)/shard_map/ppermute | solution.py:286
  18.3 10.8 %collective-permute-start.2 = (f32[256,128]{1,0:T(8,128)S(1)}, f32[256,128]{1,0:T(8,128)S(1)}, u32[]{:S(2)}, u32[]{:S(2)}) collective-permute-start(f32[256,128]{1,0:T(8,128)S(1)} %add_add_fusion.6.rest_0_), channel_id=1, source_target_pairs={{0,2},{1,3},{2,4},{3,5},{8,10},{9,11},{10,12},{11,13},{16,18},{17,... | collective-permute-start | bytes 393224 | tf_op jit(solution)/shard_map/ppermute | solution.py:329
  33.6 1.4 %collective-permute-start.4 = (f32[256,128]{1,0:T(8,128)S(1)}, f32[256,128]{1,0:T(8,128)S(1)}, u32[]{:S(2)}, u32[]{:S(2)}) collective-permute-start(f32[256,128]{1,0:T(8,128)S(1)} %add_add_fusion.5.rest_0_), channel_id=1, source_target_pairs={{2,4},{3,5},{4,6},{5,7},{10,12},{11,13},{12,14},{13,15},{18,20},{1... | collective-permute-start | bytes 393224 | tf_op jit(solution)/shard_map/ppermute | solution.py:329
  35.1 1.4 %collective-permute-start.7 = (f32[256,128]{1,0:T(8,128)S(1)}, f32[256,128]{1,0:T(8,128)S(1)}, u32[]{:S(2)}, u32[]{:S(2)}) collective-permute-start(f32[256,128]{1,0:T(8,128)S(1)} %get-tuple-element.99), channel_id=1, source_target_pairs={{0,1},{1,0},{2,3},{3,2},{4,5},{5,4},{6,7},{7,6},{8,9},{9,8},{10,11... | collective-permute-start | bytes 393224 | tf_op jit(solution)/shard_map/ppermute | solution.py:281
  35.1 8.2 %collective-permute-start.6 = (f32[256,128]{1,0:T(8,128)S(1)}, f32[256,128]{1,0:T(8,128)S(1)}, u32[]{:S(2)}, u32[]{:S(2)}) collective-permute-start(f32[256,128]{1,0:T(8,128)S(1)} %get-tuple-element.104.rest_0_), channel_id=1, source_target_pairs={{4,6},{5,7},{12,14},{13,15},{20,22},{21,23},{28,30},{29,31}} | collective-permute-start | bytes 393224 | tf_op jit(solution)/shard_map/ppermute | solution.py:329
  40.9 6.3 %collective-permute-start.9 = (f32[256,128]{1,0:T(8,128)S(1)}, f32[256,128]{1,0:T(8,128)S(1)}, u32[]{:S(2)}, u32[]{:S(2)}) collective-permute-start(f32[256,128]{1,0:T(8,128)S(1)} %get-tuple-element.64), channel_id=1, source_target_pairs={{0,1},{1,0},{2,3},{3,2},{4,5},{5,4},{6,7},{7,6},{8,9},{9,8},{10,11... | collective-permute-start | bytes 393224 | tf_op jit(solution)/shard_map/ppermute | solution.py:281
  41.0 13.3 %collective-permute-start.12 = (f32[2,264,128]{2,1,0:T(8,128)S(1)}, f32[2,264,128]{2,1,0:T(8,128)S(1)}, u32[]{:S(2)}, u32[]{:S(2)}) collective-permute-start(f32[2,264,128]{2,1,0:T(8,128)S(1)} %get-tuple-element.72), channel_id=1, source_target_pairs={{0,1},{1,2},{2,3},{3,4},{4,5},{5,6},{6,7},{8,9},{9,10},{10,11},{11... | collective-permute-start | bytes 811016 | tf_op jit(solution)/shard_map/ppermute | solution.py:286
  43.4 4.8 %collective-permute-start.8 = (f32[256,128]{1,0:T(8,128)S(1)}, f32[256,128]{1,0:T(8,128)S(1)}, u32[]{:S(2)}, u32[]{:S(2)}) collective-permute-start(f32[256,128]{1,0:T(8,128)S(1)} %get-tuple-element.97), channel_id=1, source_target_pairs={{0,1},{1,0},{2,3},{3,2},{4,5},{5,4},{6,7},{7,6},{8,9},{9,8},{10,11... | collective-permute-start | bytes 393224 | tf_op jit(solution)/shard_map/ppermute | solution.py:281
  47.2 7.8 %collective-permute-start.11 = (f32[256,128]{1,0:T(8,128)S(1)}, f32[256,128]{1,0:T(8,128)S(1)}, u32[]{:S(2)}, u32[]{:S(2)}) collective-permute-start(f32[256,128]{1,0:T(8,128)S(1)} %add.242.rest_0_), channel_id=1, source_target_pairs={{6,4},{7,5},{14,12},{15,13},{22,20},{23,21},{30,28},{31,29}} | collective-permute-start | bytes 393224 | tf_op jit(solution)/shard_map/ppermute | solution.py:329
  53.9 16.2 %collective-permute-start.10 = (f32[256,128]{1,0:T(8,128)}, f32[256,128]{1,0:T(8,128)}, u32[]{:S(2)}, u32[]{:S(2)}) collective-permute-start(f32[256,128]{1,0:T(8,128)} %get-tuple-element.70), channel_id=1, source_target_pairs={{0,1},{1,0},{2,3},{3,2},{4,5},{5,4},{6,7},{7,6},{8,9},{9,8},{10,11... | collective-permute-start | bytes 393224 | tf_op jit(solution)/shard_map/ppermute | solution.py:281
  56.3 13.8 %collective-permute-start.13 = (f32[256,128]{1,0:T(8,128)}, f32[256,128]{1,0:T(8,128)}, u32[]{:S(2)}, u32[]{:S(2)}) collective-permute-start(f32[256,128]{1,0:T(8,128)} %add_add_fusion.3.rest_0_), channel_id=1, source_target_pairs={{4,2},{5,3},{12,10},{13,11},{20,18},{21,19},{28,26},{29,27}} | collective-permute-start | bytes 393224 | tf_op jit(solution)/shard_map/ppermute | solution.py:329
  73.7 15.4 %collective-permute-start.15 = (f32[8,128]{1,0:T(8,128)}, f32[8,128]{1,0:T(8,128)}, u32[]{:S(2)}, u32[]{:S(2)}) collective-permute-start(f32[8,128]{1,0:T(8,128)} %slice_select_fusion), channel_id=1, source_target_pairs={{0,16},{8,24},{16,0},{24,8},{1,17},{9,25},{17,1},{25,9},{2,18},{10... | collective-permute-start | bytes 12296 | tf_op jit(solution)/shard_map/ppermute | solution.py:281
  75.2 14.7 %collective-permute-start.14 = (f32[256,128]{1,0:T(8,128)}, f32[256,128]{1,0:T(8,128)S(1)}, u32[]{:S(2)}, u32[]{:S(2)}) collective-permute-start(f32[256,128]{1,0:T(8,128)} %copy-done.22), channel_id=1, source_target_pairs={{6,4},{7,5},{2,0},{3,1},{14,12},{15,13},{10,8},{11,9},{22,20},{23,... | collective-permute-start | bytes 393224 | tf_op jit(solution)/shard_map/ppermute | solution.py:329
  91.5 7.7 %collective-permute-start.18 = (f32[2,264,128]{2,1,0:T(8,128)}, f32[2,264,128]{2,1,0:T(8,128)}, u32[]{:S(2)}, u32[]{:S(2)}) collective-permute-start(f32[2,264,128]{2,1,0:T(8,128)} %broadcast_add_fusion), channel_id=1, source_target_pairs={{0,1},{1,2},{2,3},{3,4},{4,5},{5,6},{6,7},{8,9},{9,10},{10,11},{11... | collective-permute-start | bytes 811016 | tf_op jit(solution)/shard_map/ppermute | solution.py:286
  94.5 3.9 %collective-permute-start.17 = (f32[4,128]{1,0:T(4,128)}, f32[4,128]{1,0:T(4,128)}, u32[]{:S(2)}, u32[]{:S(2)}) collective-permute-start(f32[4,128]{1,0:T(4,128)} %slice_select_fusion.1), channel_id=1, source_target_pairs={{0,8},{8,0},{16,24},{24,16},{1,9},{9,1},{17,25},{25,17},{2,10},{10... | collective-permute-start | bytes 6152 | tf_op jit(solution)/shard_map/ppermute | solution.py:281
  96.0 3.9 %collective-permute-start.16 = (f32[256,128]{1,0:T(8,128)}, f32[256,128]{1,0:T(8,128)S(1)}, u32[]{:S(2)}, u32[]{:S(2)}) collective-permute-start(f32[256,128]{1,0:T(8,128)} %copy-done.61), channel_id=1, source_target_pairs={{4,2},{5,3},{12,10},{13,11},{20,18},{21,19},{28,26},{29,27}} | collective-permute-start | bytes 393224 | tf_op jit(solution)/shard_map/ppermute | solution.py:329
  103.2 7.5 %collective-permute-start.20 = (f32[2,128]{1,0:T(2,128)}, f32[2,128]{1,0:T(2,128)}, u32[]{:S(2)}, u32[]{:S(2)}) collective-permute-start(f32[2,128]{1,0:T(2,128)} %broadcast_select_fusion.4), channel_id=1, source_target_pairs={{0,4},{1,5},{2,6},{3,7},{4,0},{5,1},{6,2},{7,3},{8,12},{9,13},{10,... | collective-permute-start | bytes 3080 | tf_op jit(solution)/shard_map/ppermute | solution.py:281
  108.9 7.1 %collective-permute-start.21 = (f32[256,128]{1,0:T(8,128)}, f32[256,128]{1,0:T(8,128)S(1)}, u32[]{:S(2)}, u32[]{:S(2)}) collective-permute-start(f32[256,128]{1,0:T(8,128)} %get-tuple-element.93), channel_id=1, source_target_pairs={{0,1},{1,0},{2,3},{3,2},{4,5},{5,4},{6,7},{7,6},{8,9},{9,8},{10,11... | collective-permute-start | bytes 393224 | tf_op jit(solution)/shard_map/ppermute | solution.py:281
  111.5 8.2 %collective-permute-start.23 = (f32[1,128]{1,0:T(1,128)S(1)}, f32[1,128]{1,0:T(1,128)S(1)}, u32[]{:S(2)}, u32[]{:S(2)}) collective-permute-start(f32[1,128]{1,0:T(1,128)S(1)} %broadcast_select_fusion), channel_id=1, source_target_pairs={{0,2},{1,3},{2,0},{3,1},{4,6},{5,7},{6,4},{7,5},{8,10},{9,11},{10,... | collective-permute-start | bytes 1544 | tf_op jit(solution)/shard_map/ppermute | solution.py:281
  119.8 7.8 %collective-permute-start.19 = (f32[256,128]{1,0:T(8,128)S(1)}, f32[256,128]{1,0:T(8,128)S(1)}, u32[]{:S(2)}, u32[]{:S(2)}) collective-permute-start(f32[256,128]{1,0:T(8,128)S(1)} %copy-done.60), channel_id=1, source_target_pairs={{2,0},{3,1},{10,8},{11,9},{18,16},{19,17},{26,24},{27,25}} | collective-permute-start | bytes 393224 | tf_op jit(solution)/shard_map/ppermute | solution.py:329
  127.7 1.4 %collective-permute-start.22 = (f32[256,128]{1,0:T(8,128)S(1)}, f32[256,128]{1,0:T(8,128)S(1)}, u32[]{:S(2)}, u32[]{:S(2)}) collective-permute-start(f32[256,128]{1,0:T(8,128)S(1)} %get-tuple-element.91), channel_id=1, source_target_pairs={{0,1},{1,0},{2,3},{3,2},{4,5},{5,4},{6,7},{7,6},{8,9},{9,8},{10,11... | collective-permute-start | bytes 393224 | tf_op jit(solution)/shard_map/ppermute | solution.py:281
  (67 other events, 334.2 us)

commit v9 on v8

--- a/solution.py
+++ b/solution.py
@@ -90,7 +90,10 @@
     return half, base, 2 * group * lanes + base
 
 
-def states_kernel(core, k_in, v_in, keep, send, zero, k, v, sems):
+def states_kernel(position, k_in, v_in, keep, send, zero, k, v, core_row, chip_row, ctx_row, dp_row, sems):
+    core = position
+    for i, row in enumerate((core_row, chip_row, ctx_row, dp_row)):
+        row[...] = jnp.full(row.shape, position[i], jnp.int32)
     lanes = k.shape[1] // GROUPS // 2
     count = lanes // PAIR
     copies = []
@@ -290,8 +293,7 @@
     return jnp.minimum(jnp.abs(x), 0.0)
 
 
-def chip_rank(towards):
-    chip = lax.axis_index("ctx") // 2
+def chip_rank(chip, towards):
     return chip if towards == 1 else lax.axis_size("ctx") // 2 - 1 - chip
 
 
@@ -312,10 +314,10 @@
     return value
 
 
-def chain_load(owns, starts, arrived, step, towards):
+def chain_load(chip, owns, starts, arrived, step, towards):
     chips = lax.axis_size("ctx") // 2
     cases = [(step - at, own) for own, at in zip(owns, starts) if 0 <= step - at <= chips - 2]
-    load = pick(chip_rank(towards), cases)
+    load = pick(chip_rank(chip, towards), cases)
     return load if arrived is None else load + arrived
 
 
@@ -329,10 +331,10 @@
     return lax.ppermute(load, "ctx", route)
 
 
-def chain_result(arrivals, start, towards):
+def chain_result(chip, arrivals, start, towards):
     chips = lax.axis_size("ctx") // 2
     cases = [(rank, arrivals[start + rank - 1]) for rank in range(1, chips)]
-    return pick(chip_rank(towards), cases + [(0, jnp.zeros_like(arrivals[0]))])
+    return pick(chip_rank(chip, towards), cases + [(0, jnp.zeros_like(arrivals[0]))])
 
 
 def within_chip(keep, send):
@@ -340,9 +342,9 @@
     return keep, received, keep + received
 
 
-def to_cores(before, piece, towards):
+def to_cores(core, before, piece, towards):
     keep, received, _ = piece
-    is_source = lax.axis_index("ctx") & 1 == (0 if towards == 1 else 1)
+    is_source = core == (0 if towards == 1 else 1)
     mine = jnp.where(is_source, before, before + received)
     return mine, partner(jnp.where(is_source, before + keep, before), "ctx", 0)
 
@@ -351,9 +353,9 @@
     return pltpu.with_memory_space_constraint(x, space)
 
 
-def scatter_step(x, axis, bit):
-    upper = lax.axis_index(axis) >> bit & 1 == 1
+def scatter_step(x, at, axis, bit):
     low, high = jnp.split(x, 2, axis=0 if x.shape[0] > 1 else 1)
+    upper = (at >> bit & 1 == 1)[:, :low.shape[1]]
     return jnp.where(upper, high, low) + partner(jnp.where(upper, low, high), axis, bit)
 
 
@@ -362,7 +364,8 @@
     q, k, v, dy = (x[0] for x in (queries, keys, values, out_grad))
     table = image_flags[0]
     gain_row = gain.reshape(1, width)
-    core = (lax.axis_index("ctx") & 1).reshape(1).astype(jnp.int32)
+    ctx = lax.axis_index("ctx")
+    core = jnp.stack([ctx & 1, ctx >> 1, ctx, lax.axis_index("dp")]).astype(jnp.int32)
     lanes = width // GROUPS // 2
     half_rows = lanes // PAIR * E
     heads = lanes // E
@@ -475,10 +478,12 @@
              ("half", suffix[0]), ("half", suffix[1]), ("part", prv[g])],
             [("wide", BF16), ("wide", BF16), ("token", F32)], after=after, alias=list(enumerate(before)), sub=SUB)
 
-    keep, send, zero, k, v = call(
+    keep, send, zero, k, v, core_row, chip_row, ctx_row, dp_row = call(
         states_kernel, 0, [("hbm", k), ("hbm", v)],
-        [("all", F32), ("all", F32), ("zero", jnp.int32), ("vmem", BF16, whole), ("vmem", BF16, whole)],
+        [("all", F32), ("all", F32), ("zero", jnp.int32), ("vmem", BF16, whole), ("vmem", BF16, whole)]
+        + [("token", jnp.int32)] * 4,
         scratch=[pltpu.SemaphoreType.DMA((2 * GROUPS, 2))], steps=(1,))
+    at = {"ctx": ctx_row, "dp": dp_row}
     keep, received, total = within_chip(keep, send)
     owns = [tuple(x[g * half_rows:(g + 1) * half_rows] for x in (keep, received, total)) for g in groups]
     sums = [own for _, _, own in owns]
@@ -507,10 +512,10 @@
             local.append(attn)
             token = token + nought(nxt[-1][0, :1])
         if step < last and chained:
-            load = chain_load(sums, starts, arrivals[-1] + token, step + 1, 1)
+            load = chain_load(chip_row, sums, starts, arrivals[-1] + token, step + 1, 1)
     prefix, norms = [], []
-    before = chain_result(arrivals, starts[0], 1) if chained else chips_before(sums[0], 1)
-    prefix.append(to_cores(before, owns[0], 1))
+    before = chain_result(chip_row, arrivals, starts[0], 1) if chained else chips_before(sums[0], 1)
+    prefix.append(to_cores(core_row, before, owns[0], 1))
     norms.append(norm(0, prefix[0], None, [load]))
 
     ins, ins_starts, ins_arrivals = owns, starts, arrivals
@@ -520,8 +525,8 @@
     for g in groups[1:]:
         if chained:
             ins_arrivals[-1] = ins_arrivals[-1] + norms[-1][5]
-        before = chain_result(ins_arrivals, ins_starts[g], 1) if chained else chips_before(ins[g][2], 1)
-        prefix.append(to_cores(before, ins[g], 1))
+        before = chain_result(chip_row, ins_arrivals, ins_starts[g], 1) if chained else chips_before(ins[g][2], 1)
+        prefix.append(to_cores(core_row, before, ins[g], 1))
         norms.append(norm(g, prefix[g], norms[-1][0], [load]))
         owns.append(within_chip(*norms[-1][4]))
         sums.append(owns[-1][2])
@@ -536,7 +541,7 @@
     for step in range(last + 1 if chained else GROUPS + 1):
         if chained:
             if step:
-                load = chain_load(sums, starts, arrivals[-1] + token, step, -1)
+                load = chain_load(chip_row, sums, starts, arrivals[-1] + token, step, -1)
             arrivals.append(chain_step(load, starts, step, -1))
         if step == 0:
             prv[0] = shifted(prv[0], 1)
@@ -544,7 +549,7 @@
             continue
         token = jnp.zeros((1, PAIR), F32)
         if 2 <= step and len(bits) > 2:
-            gain_sum = scatter_step(gain_sum + nought(load[:1]), *bits.pop(0))
+            gain_sum = scatter_step(gain_sum + nought(load[:1]), at[bits[0][0]], *bits.pop(0))
             token = token + nought(gain_sum[:1])
         if step == GROUPS + 1 or (not chained and step == 1):
             for g in groups[1:]:
@@ -556,11 +561,11 @@
     for g in groups:
         if g and chained:
             arrivals[-1] = arrivals[-1] + token
-        before = chain_result(arrivals, starts[g], -1) if chained else chips_before(sums[g], -1)
-        *outers, done = outer(g, to_cores(before, owns[g], -1), outers, [])
+        before = chain_result(chip_row, arrivals, starts[g], -1) if chained else chips_before(sums[g], -1)
+        *outers, done = outer(g, to_cores(core_row, before, owns[g], -1), outers, [])
         token = token + done
     for axis, bit in bits:
-        gain_sum = scatter_step(gain_sum, axis, bit)
+        gain_sum = scatter_step(gain_sum, at[axis], axis, bit)
     grad_q = inners[-1][0]
     grad_k, grad_v = outers
     grad_gain = gain_sum.reshape(-1)

time: 134 us -> 96.5 us (0.72)
  local copies, waits for them, and re-layouts: 27.5 us -> 0.02 us
  other arithmetic: 14.9 us -> 1.63 us
  starting transfers between devices: 42.9 us -> 45.4 us
  waiting for transfers between devices: 10.9 us -> 13 us
    unnamed x132 -> x6, local copies, waits for them, and re-layouts: 27.5 us -> 0.01 us
    ppermute x12, starting transfers between devices: 18.1 us -> 23.1 us  [partner(): return lax.ppermute(x, axis, route)]
    add x5, other arithmetic: 4.31 us -> 0.15 us  [chain_load(): return load if arrived is None else load + arrived]
    add x4, other arithmetic: 2.27 us -> 0.02 us  [scatter_step(): jnp.where(upper, high, low)]
    add x11, other arithmetic: 2.09 us -> 0.06 us  [the longest x6 0.03 us: on_device(): gain_sum + nought(load[:1])]
    ppermute x9, waiting for transfers between devices: 5.9 us -> 7.9 us  [chain_step(): return lax.ppermute(load, 'ctx', route)]
    select_n x4, other arithmetic: 1.9 us -> 0.09 us  [to_cores(): mine = jnp.where(is_source, before, before + received)]
    select_n x5, other arithmetic: 1.83 us -> 0.1 us  [scatter_step(): jnp.where(upper, low, high)]
  transfers between devices with their start and end apart: 25 -> 25, of which waited for: 7 -> 9; matrix products, arithmetic and copies ran while one was open for 7% -> 1% of each run, Pallas kernels for 22% -> 30%
where the time goes in v9:
time: 96.5 us; the launch traced here: 96.1 us
  starting transfers between devices  45.4 us (47%)
  Pallas kernels  35 us (36%)
  waiting for transfers between devices  13 us (13%)
  other arithmetic  1.63 us (2%)
  between operations  1.1 us (1%)
    pallas_call x10, Pallas kernels, call(): pl.pallas_call(kernel, grid_spec=pltpu.PrefetchScalarGridSpec(num_scalar_...  35 us
    ppermute x12, starting transfers between devices, partner(): return lax.ppermute(x, axis, route)  23.1 us
    ppermute x9, starting transfers between devices, chain_step(): return lax.ppermute(load, 'ctx', route)  16.1 us
    ppermute x9, waiting for transfers between devices, chain_step(): return lax.ppermute(load, 'ctx', route)  7.9 us
    ppermute x4, starting transfers between devices, shifted(): lax.ppermute(x, 'ctx', [(i, i + distance) for i in range(count) if 0 <= i...  6.16 us
    ppermute x12, waiting for transfers between devices, partner(): return lax.ppermute(x, axis, route)  4.72 us
  transfers between devices with their start and end apart: 25, of which 9 were waited for; matrix products, arithmetic and copies ran while one was open for 1% of the time, Pallas kernels for 30%

profile of v9, /device:TPU:0, one launch (start us, length us, event | category | flops | bytes accessed | tf_op | source)
XLA Modules:
  0.0 96.1 jit_solution(14877662676702037867)
XLA Ops:
  0.7 3.0 %shard_map.110 = (f32[512,128]{1,0:T(8,128)S(1)}, f32[512,128]{1,0:T(8,128)S(1)}, s32[1,256]{1,0:T(1,128)S(1)}, bf16[256,2048]{1,0:T(8,128)(2,1)S(1)}, bf16[256,...) custom-call(s32[4]{0:T(128)S(1)} %pad_add_fusion.position.core, ...), custom_call_target="tpu_custom_call" | custom-call | flops 1 | bytes 1 | tf_op jit(solution)/shard_map/pallas_call | solution.py:428
  5.4 4.9 %collective-permute-start.1 = (f32[256,128]{1,0:T(8,128)S(1)}, f32[256,128]{1,0:T(8,128)S(1)}, u32[]{:S(2)}, u32[]{:S(2)}) collective-permute-start(f32[256,128]{1,0:T(8,128)S(1)} %slice.69.refs_6_), channel_id=1, source_target_pairs={{0,2},{1,3},{8,10},{9,11},{16,18},{17,19},{24,26},{25,27}} | collective-permute-start | bytes 393224 | tf_op jit(solution)/shard_map/ppermute | solution.py:331
  10.3 2.1 %shard_map.111 = (f32[2,264,128]{2,1,0:T(8,128)S(1)}, f32[2,264,128]{2,1,0:T(8,128)S(1)}, bf16[256,2048]{1,0:T(8,128)(2,1)S(1)}, bf16[256,2048]{1,0:T(8,128)(2,1)S(1)}, f32[1,128]{1,0:T(1,128)S(1)}) custom-call(s32[4]{0:T(128)S(1)} %pad_add_fusion.position.core, bf16[256,2048]{1,0:T(8,128)(2,1)} %bitcast.97, bf16[256,2048]{1,0:T(8,128)(2,1)} %bitcast.98, ...), custom_call_target="tpu_custom_call" | custom-call | flops 1 | bytes 1 | tf_op jit(solution)/shard_map/pallas_call | solution.py:428
  12.4 1.3 %collective-permute-start.3 = (f32[2,264,128]{2,1,0:T(8,128)S(1)}, f32[2,264,128]{2,1,0:T(8,128)S(1)}, u32[]{:S(2)}, u32[]{:S(2)}) collective-permute-start(f32[2,264,128]{2,1,0:T(8,128)S(1)} %get-tuple-element.62), channel_id=1, source_target_pairs={{1,0},{2,1},{3,2},{4,3},{5,4},{6,5},{7,6},{9,8},{10,9},{11,10},{12... | collective-permute-start | bytes 811016 | tf_op jit(solution)/shard_map/ppermute | solution.py:289
  15.1 5.3 %collective-permute-start.2 = (f32[256,128]{1,0:T(8,128)S(1)}, f32[256,128]{1,0:T(8,128)S(1)}, u32[]{:S(2)}, u32[]{:S(2)}) collective-permute-start(f32[256,128]{1,0:T(8,128)S(1)} %add_add_fusion.6.rest_0_), channel_id=1, source_target_pairs={{0,2},{1,3},{2,4},{3,5},{8,10},{9,11},{10,12},{11,13},{16,18},{17,... | collective-permute-start | bytes 393224 | tf_op jit(solution)/shard_map/ppermute | solution.py:331
  20.4 3.0 %shard_map.112 = (f32[256,1024]{1,0:T(8,128)S(1)}, bf16[16,256,256]{2,1,0:T(8,128)(2,1)S(1)}, f32[1,128]{1,0:T(1,128)S(1)}) custom-call(s32[4]{0:T(128)S(1)} %pad_add_fusion.position.core, bf16[256,2048]{1,0:T(8,128)(2,1)S(1)} %get-tuple-element.56.q, bf16[256,2048]{1,0:T(8,128)(2,1)S(1)} %get-tuple-element.52.refs_2_.k, ...), custom_call_target="tpu_custom_call" | custom-call | flops 1 | bytes 1 | tf_op jit(solution)/shard_map/pallas_call | solution.py:428
  23.5 3.0 %shard_map.113 = (f32[256,1024]{1,0:T(8,128)S(1)}, bf16[16,256,256]{2,1,0:T(8,128)(2,1)S(1)}, f32[1,128]{1,0:T(1,128)S(1)}) custom-call(s32[4]{0:T(128)S(1)} %pad_add_fusion.position.core, bf16[256,2048]{1,0:T(8,128)(2,1)S(1)} %get-tuple-element.56.q, bf16[256,2048]{1,0:T(8,128)(2,1)S(1)} %get-tuple-element.52.refs_2_.k, ...), custom_call_target="tpu_custom_call" | custom-call | flops 1 | bytes 1 | tf_op jit(solution)/shard_map/pallas_call | solution.py:428
  28.7 3.2 %shard_map.114 = (bf16[256,2048]{1,0:T(8,128)(2,1)}, bf16[256,1024]{1,0:T(8,128)(2,1)S(1)}, f32[2,264,128]{2,1,0:T(8,128)S(1)}, f32[2,4,128]{2,1,0:T(4,128)S(1)}...) custom-call(s32[4]{0:T(128)S(1)} %pad_add_fusion.position.core, ...), custom_call_target="tpu_custom_call" | custom-call | flops 1 | bytes 1 | tf_op jit(solution)/shard_map/pallas_call | solution.py:428
  32.1 2.3 %collective-permute-start.12 = (f32[2,264,128]{2,1,0:T(8,128)S(1)}, f32[2,264,128]{2,1,0:T(8,128)S(1)}, u32[]{:S(2)}, u32[]{:S(2)}) collective-permute-start(f32[2,264,128]{2,1,0:T(8,128)S(1)} %get-tuple-element.78), channel_id=1, source_target_pairs={{0,1},{1,2},{2,3},{3,4},{4,5},{5,6},{6,7},{8,9},{9,10},{10,11},{11... | collective-permute-start | bytes 811016 | tf_op jit(solution)/shard_map/ppermute | solution.py:289
  34.4 6.0 %collective-permute-start.8 = (f32[256,128]{1,0:T(8,128)S(1)}, f32[256,128]{1,0:T(8,128)S(1)}, u32[]{:S(2)}, u32[]{:S(2)}) collective-permute-start(f32[256,128]{1,0:T(8,128)S(1)} %get-tuple-element.105), channel_id=1, source_target_pairs={{0,1},{1,0},{2,3},{3,2},{4,5},{5,4},{6,7},{7,6},{8,9},{9,8},{10,11... | collective-permute-start | bytes 393224 | tf_op jit(solution)/shard_map/ppermute | solution.py:284
  41.3 3.2 %shard_map.115 = (bf16[256,2048]{1,0:T(8,128)(2,1)}, bf16[256,1024]{1,0:T(8,128)(2,1)S(1)}, f32[2,264,128]{2,1,0:T(8,128)S(1)}, f32[2,4,128]{2,1,0:T(4,128)S(1)}...) custom-call(s32[4]{0:T(128)S(1)} %pad_add_fusion.position.core, ...), custom_call_target="tpu_custom_call", output_to_operand_aliasing={{0}: (11, {})} | custom-call | flops 1 | bytes 1 | tf_op jit(solution)/shard_map/pallas_call | solution.py:428
  45.7 5.8 %shard_map.116 = (bf16[256,2048]{1,0:T(8,128)(2,1)}, f32[256,1024]{1,0:T(8,128)S(1)}, f32[256,1024]{1,0:T(8,128)S(1)}, f32[1,128]{1,0:T(1,128)S(1)}) custom-call(s32[4]{0:T(128)S(1)} %pad_add_fusion.position.core, bf16[256,2048]{1,0:T(8,128)(2,1)S(1)} %get-tuple-element.56.q, bf16[256,2048]{1,0:T(8,128)(2,1)S(1)} %get-tuple-element.52.refs_2_.k, ...), custom_call_target="tpu_custom_call" | custom-call | flops 1 | bytes 1 | tf_op jit(solution)/shard_map/pallas_call | solution.py:428
  51.5 1.6 %collective-permute-start.15 = (f32[8,128]{1,0:T(8,128)S(1)}, f32[8,128]{1,0:T(8,128)S(1)}, u32[]{:S(2)}, u32[]{:S(2)}) collective-permute-start(f32[8,128]{1,0:T(8,128)S(1)} %slice_select_fusion), channel_id=1, source_target_pairs={{0,16},{8,24},{16,0},{24,8},{1,17},{9,25},{17,1},{25,9},{2,18},{10... | collective-permute-start | bytes 12296 | tf_op jit(solution)/shard_map/ppermute | solution.py:284
  54.4 5.7 %shard_map.117 = (bf16[256,2048]{1,0:T(8,128)(2,1)}, f32[256,1024]{1,0:T(8,128)S(1)}, f32[256,1024]{1,0:T(8,128)S(1)}, f32[1,128]{1,0:T(1,128)S(1)}) custom-call(s32[4]{0:T(128)S(1)} %pad_add_fusion.position.core, bf16[256,2048]{1,0:T(8,128)(2,1)S(1)} %get-tuple-element.56.q, ...), custom_call_target="tpu_custom_call", output_to_operand_aliasing={{0}: (13, {})} | custom-call | flops 1 | bytes 1 | tf_op jit(solution)/shard_map/pallas_call | solution.py:428
  60.2 2.0 %collective-permute-done.14 = f32[256,128]{1,0:T(8,128)S(1)} collective-permute-done((f32[256,128]{1,0:T(8,128)S(1)}, f32[256,128]{1,0:T(8,128)S(1)}, u32[]{:S(2)}, u32[]{:S(2)}) %collective-permute-start.14) | collective-permute-done | bytes 131104 | tf_op jit(solution)/shard_map/ppermute | solution.py:331
  62.2 1.6 %collective-permute-start.17 = (f32[4,128]{1,0:T(4,128)S(1)}, f32[4,128]{1,0:T(4,128)S(1)}, u32[]{:S(2)}, u32[]{:S(2)}) collective-permute-start(f32[4,128]{1,0:T(4,128)S(1)} %slice_select_fusion.1), channel_id=1, source_target_pairs={{0,8},{8,0},{16,24},{24,16},{1,9},{9,1},{17,25},{25,17},{2,10},{10... | collective-permute-start | bytes 6152 | tf_op jit(solution)/shard_map/ppermute | solution.py:284
  63.8 1.3 %collective-permute-start.18 = (f32[2,264,128]{2,1,0:T(8,128)S(1)}, f32[2,264,128]{2,1,0:T(8,128)S(1)}, u32[]{:S(2)}, u32[]{:S(2)}) collective-permute-start(f32[2,264,128]{2,1,0:T(8,128)S(1)} %broadcast_add_fusion), channel_id=1, source_target_pairs={{0,1},{1,2},{2,3},{3,4},{4,5},{5,6},{6,7},{8,9},{9,10},{10,11},{11... | collective-permute-start | bytes 811016 | tf_op jit(solution)/shard_map/ppermute | solution.py:289
  66.3 10.1 %collective-permute-start.20 = (f32[2,128]{1,0:T(2,128)S(1)}, f32[2,128]{1,0:T(2,128)S(1)}, u32[]{:S(2)}, u32[]{:S(2)}) collective-permute-start(f32[2,128]{1,0:T(2,128)S(1)} %broadcast_select_fusion), channel_id=1, source_target_pairs={{0,4},{1,5},{2,6},{3,7},{4,0},{5,1},{6,2},{7,3},{8,12},{9,13},{10,... | collective-permute-start | bytes 3080 | tf_op jit(solution)/shard_map/ppermute | solution.py:284
  76.5 1.5 %collective-permute-done.20 = f32[2,128]{1,0:T(2,128)S(1)} collective-permute-done((f32[2,128]{1,0:T(2,128)S(1)}, f32[2,128]{1,0:T(2,128)S(1)}, u32[]{:S(2)}, u32[]{:S(2)}) %collective-permute-start.20) | collective-permute-done | bytes 1056 | tf_op jit(solution)/shard_map/ppermute | solution.py:284
  78.0 2.7 %collective-permute-start.23 = (f32[1,128]{1,0:T(1,128)S(1)}, f32[1,128]{1,0:T(1,128)S(1)}, u32[]{:S(2)}, u32[]{:S(2)}) collective-permute-start(f32[1,128]{1,0:T(1,128)S(1)} %compare_select_fusion), channel_id=1, source_target_pairs={{0,2},{1,3},{2,0},{3,1},{4,6},{5,7},{6,4},{7,5},{8,10},{9,11},{10,... | collective-permute-start | bytes 1544 | tf_op jit(solution)/shard_map/ppermute | solution.py:284
  80.8 3.0 %shard_map.118 = (bf16[256,2048]{1,0:T(8,128)(2,1)}, bf16[256,2048]{1,0:T(8,128)(2,1)}, f32[1,128]{1,0:T(1,128)S(1)}) custom-call(s32[4]{0:T(128)S(1)} %pad_add_fusion.position.core, bf16[256,2048]{1,0:T(8,128)(2,1)S(1)} %get-tuple-element.52.refs_2_.k, bf16[256,2048]{1,0:T(8,128)(2,1)S(1)} %get-tuple-element.53.refs_3_.v, ...), custom_call_target="tpu_custom_call" | custom-call | flops 1 | bytes 1 | tf_op jit(solution)/shard_map/pallas_call | solution.py:428
  85.8 5.9 %collective-permute-done.19 = f32[256,128]{1,0:T(8,128)S(1)} collective-permute-done((f32[256,128]{1,0:T(8,128)S(1)}, f32[256,128]{1,0:T(8,128)S(1)}, u32[]{:S(2)}, u32[]{:S(2)}) %collective-permute-start.19) | collective-permute-done | bytes 131104 | tf_op jit(solution)/shard_map/ppermute | solution.py:331
  91.8 1.3 %collective-permute-done.22.suf_recv = f32[256,128]{1,0:T(8,128)S(1)} collective-permute-done((f32[256,128]{1,0:T(8,128)S(1)}, f32[256,128]{1,0:T(8,128)S(1)}, u32[]{:S(2)}, u32[]{:S(2)}) %collective-permute-start.22) | collective-permute-done | bytes 131104 | tf_op jit(solution)/shard_map/ppermute | solution.py:284
  93.1 3.0 %shard_map.119 = (bf16[256,2048]{1,0:T(8,128)(2,1)}, bf16[256,2048]{1,0:T(8,128)(2,1)}, f32[1,128]{1,0:T(1,128)}) custom-call(s32[4]{0:T(128)S(1)} %pad_add_fusion.position.core, bf16[256,2048]{1,0:T(8,128)(2,1)S(1)} %get-tuple-element.52.refs_2_.k, ...), custom_call_target="tpu_custom_call", output_to_operand_aliasing={{0}: (10, {}), {1}: (11, {})} | custom-call | flops 1 | bytes 1 | tf_op jit(solution)/shard_map/pallas_call | solution.py:428
  (91 shorter events, 12.3 us)
Async XLA Ops:
  3.7 1.7 %collective-permute-start = (f32[512,128]{1,0:T(8,128)S(1)}, f32[512,128]{1,0:T(8,128)S(1)}, u32[]{:S(2)}, u32[]{:S(2)}) collective-permute-start(f32[512,128]{1,0:T(8,128)S(1)} %get-tuple-element.55), channel_id=1, source_target_pairs={{0,1},{1,0},{2,3},{3,2},{4,5},{5,4},{6,7},{7,6},{8,9},{9,8},{10,11... | collective-permute-start | bytes 786440 | tf_op jit(solution)/shard_map/ppermute | solution.py:284
  5.4 9.6 %collective-permute-start.1 = (f32[256,128]{1,0:T(8,128)S(1)}, f32[256,128]{1,0:T(8,128)S(1)}, u32[]{:S(2)}, u32[]{:S(2)}) collective-permute-start(f32[256,128]{1,0:T(8,128)S(1)} %slice.69.refs_6_), channel_id=1, source_target_pairs={{0,2},{1,3},{8,10},{9,11},{16,18},{17,19},{24,26},{25,27}} | collective-permute-start | bytes 393224 | tf_op jit(solution)/shard_map/ppermute | solution.py:331
  12.4 11.0 %collective-permute-start.3 = (f32[2,264,128]{2,1,0:T(8,128)S(1)}, f32[2,264,128]{2,1,0:T(8,128)S(1)}, u32[]{:S(2)}, u32[]{:S(2)}) collective-permute-start(f32[2,264,128]{2,1,0:T(8,128)S(1)} %get-tuple-element.62), channel_id=1, source_target_pairs={{1,0},{2,1},{3,2},{4,3},{5,4},{6,5},{7,6},{9,8},{10,9},{11,10},{12... | collective-permute-start | bytes 811016 | tf_op jit(solution)/shard_map/ppermute | solution.py:289
  13.7 13.5 %collective-permute-start.5 = (f32[2,264,128]{2,1,0:T(8,128)S(1)}, f32[2,264,128]{2,1,0:T(8,128)S(1)}, u32[]{:S(2)}, u32[]{:S(2)}) collective-permute-start(f32[2,264,128]{2,1,0:T(8,128)S(1)} %get-tuple-element.66), channel_id=1, source_target_pairs={{1,0},{2,1},{3,2},{4,3},{5,4},{6,5},{7,6},{9,8},{10,9},{11,10},{12... | collective-permute-start | bytes 811016 | tf_op jit(solution)/shard_map/ppermute | solution.py:289
  15.1 8.3 %collective-permute-start.2 = (f32[256,128]{1,0:T(8,128)S(1)}, f32[256,128]{1,0:T(8,128)S(1)}, u32[]{:S(2)}, u32[]{:S(2)}) collective-permute-start(f32[256,128]{1,0:T(8,128)S(1)} %add_add_fusion.6.rest_0_), channel_id=1, source_target_pairs={{0,2},{1,3},{2,4},{3,5},{8,10},{9,11},{10,12},{11,13},{16,18},{17,... | collective-permute-start | bytes 393224 | tf_op jit(solution)/shard_map/ppermute | solution.py:331
  27.3 1.4 %collective-permute-start.7 = (f32[256,128]{1,0:T(8,128)S(1)}, f32[256,128]{1,0:T(8,128)S(1)}, u32[]{:S(2)}, u32[]{:S(2)}) collective-permute-start(f32[256,128]{1,0:T(8,128)S(1)} %get-tuple-element.107), channel_id=1, source_target_pairs={{0,1},{1,0},{2,3},{3,2},{4,5},{5,4},{6,7},{7,6},{8,9},{9,8},{10,11... | collective-permute-start | bytes 393224 | tf_op jit(solution)/shard_map/ppermute | solution.py:284
  27.4 7.0 %collective-permute-start.6 = (f32[256,128]{1,0:T(8,128)S(1)}, f32[256,128]{1,0:T(8,128)S(1)}, u32[]{:S(2)}, u32[]{:S(2)}) collective-permute-start(f32[256,128]{1,0:T(8,128)S(1)} %get-tuple-element.112.rest_0_), channel_id=1, source_target_pairs={{4,6},{5,7},{12,14},{13,15},{20,22},{21,23},{28,30},{29,31}} | collective-permute-start | bytes 393224 | tf_op jit(solution)/shard_map/ppermute | solution.py:331
  31.9 8.5 %collective-permute-start.9 = (f32[256,128]{1,0:T(8,128)S(1)}, f32[256,128]{1,0:T(8,128)S(1)}, u32[]{:S(2)}, u32[]{:S(2)}) collective-permute-start(f32[256,128]{1,0:T(8,128)S(1)} %get-tuple-element.70), channel_id=1, source_target_pairs={{0,1},{1,0},{2,3},{3,2},{4,5},{5,4},{6,7},{7,6},{8,9},{9,8},{10,11... | collective-permute-start | bytes 393224 | tf_op jit(solution)/shard_map/ppermute | solution.py:284
  32.1 12.9 %collective-permute-start.12 = (f32[2,264,128]{2,1,0:T(8,128)S(1)}, f32[2,264,128]{2,1,0:T(8,128)S(1)}, u32[]{:S(2)}, u32[]{:S(2)}) collective-permute-start(f32[2,264,128]{2,1,0:T(8,128)S(1)} %get-tuple-element.78), channel_id=1, source_target_pairs={{0,1},{1,2},{2,3},{3,4},{4,5},{5,6},{6,7},{8,9},{9,10},{10,11},{11... | collective-permute-start | bytes 811016 | tf_op jit(solution)/shard_map/ppermute | solution.py:289
  34.4 7.0 %collective-permute-start.8 = (f32[256,128]{1,0:T(8,128)S(1)}, f32[256,128]{1,0:T(8,128)S(1)}, u32[]{:S(2)}, u32[]{:S(2)}) collective-permute-start(f32[256,128]{1,0:T(8,128)S(1)} %get-tuple-element.105), channel_id=1, source_target_pairs={{0,1},{1,0},{2,3},{3,2},{4,5},{5,4},{6,7},{7,6},{8,9},{9,8},{10,11... | collective-permute-start | bytes 393224 | tf_op jit(solution)/shard_map/ppermute | solution.py:284
  40.4 4.5 %collective-permute-start.11 = (f32[256,128]{1,0:T(8,128)S(1)}, f32[256,128]{1,0:T(8,128)S(1)}, u32[]{:S(2)}, u32[]{:S(2)}) collective-permute-start(f32[256,128]{1,0:T(8,128)S(1)} %add.241.rest_0_), channel_id=1, source_target_pairs={{6,4},{7,5},{14,12},{15,13},{22,20},{23,21},{30,28},{31,29}} | collective-permute-start | bytes 393224 | tf_op jit(solution)/shard_map/ppermute | solution.py:331
  44.6 6.9 %collective-permute-start.10 = (f32[256,128]{1,0:T(8,128)S(1)}, f32[256,128]{1,0:T(8,128)S(1)}, u32[]{:S(2)}, u32[]{:S(2)}) collective-permute-start(f32[256,128]{1,0:T(8,128)S(1)} %get-tuple-element.76), channel_id=1, source_target_pairs={{0,1},{1,0},{2,3},{3,2},{4,5},{5,4},{6,7},{7,6},{8,9},{9,8},{10,11... | collective-permute-start | bytes 393224 | tf_op jit(solution)/shard_map/ppermute | solution.py:284
  45.0 6.5 %collective-permute-start.13 = (f32[256,128]{1,0:T(8,128)S(1)}, f32[256,128]{1,0:T(8,128)S(1)}, u32[]{:S(2)}, u32[]{:S(2)}) collective-permute-start(f32[256,128]{1,0:T(8,128)S(1)} %add_add_fusion.3.rest_0_), channel_id=1, source_target_pairs={{4,2},{5,3},{12,10},{13,11},{20,18},{21,19},{28,26},{29,27}} | collective-permute-start | bytes 393224 | tf_op jit(solution)/shard_map/ppermute | solution.py:331
  51.5 8.6 %collective-permute-start.15 = (f32[8,128]{1,0:T(8,128)S(1)}, f32[8,128]{1,0:T(8,128)S(1)}, u32[]{:S(2)}, u32[]{:S(2)}) collective-permute-start(f32[8,128]{1,0:T(8,128)S(1)} %slice_select_fusion), channel_id=1, source_target_pairs={{0,16},{8,24},{16,0},{24,8},{1,17},{9,25},{17,1},{25,9},{2,18},{10... | collective-permute-start | bytes 12296 | tf_op jit(solution)/shard_map/ppermute | solution.py:284
  53.1 9.0 %collective-permute-start.14 = (f32[256,128]{1,0:T(8,128)S(1)}, f32[256,128]{1,0:T(8,128)S(1)}, u32[]{:S(2)}, u32[]{:S(2)}) collective-permute-start(f32[256,128]{1,0:T(8,128)S(1)} %get-tuple-element.103.rest_0_), channel_id=1, source_target_pairs={{6,4},{7,5},{2,0},{3,1},{14,12},{15,13},{10,8},{11,9},{22,20},{23,... | collective-permute-start | bytes 393224 | tf_op jit(solution)/shard_map/ppermute | solution.py:331
  62.2 3.7 %collective-permute-start.17 = (f32[4,128]{1,0:T(4,128)S(1)}, f32[4,128]{1,0:T(4,128)S(1)}, u32[]{:S(2)}, u32[]{:S(2)}) collective-permute-start(f32[4,128]{1,0:T(4,128)S(1)} %slice_select_fusion.1), channel_id=1, source_target_pairs={{0,8},{8,0},{16,24},{24,16},{1,9},{9,1},{17,25},{25,17},{2,10},{10... | collective-permute-start | bytes 6152 | tf_op jit(solution)/shard_map/ppermute | solution.py:284
  63.8 2.5 %collective-permute-start.18 = (f32[2,264,128]{2,1,0:T(8,128)S(1)}, f32[2,264,128]{2,1,0:T(8,128)S(1)}, u32[]{:S(2)}, u32[]{:S(2)}) collective-permute-start(f32[2,264,128]{2,1,0:T(8,128)S(1)} %broadcast_add_fusion), channel_id=1, source_target_pairs={{0,1},{1,2},{2,3},{3,4},{4,5},{5,6},{6,7},{8,9},{9,10},{10,11},{11... | collective-permute-start | bytes 811016 | tf_op jit(solution)/shard_map/ppermute | solution.py:289
  65.1 1.1 %collective-permute-start.16 = (f32[256,128]{1,0:T(8,128)S(1)}, f32[256,128]{1,0:T(8,128)S(1)}, u32[]{:S(2)}, u32[]{:S(2)}) collective-permute-start(f32[256,128]{1,0:T(8,128)S(1)} %get-tuple-element.111), channel_id=1, source_target_pairs={{4,2},{5,3},{12,10},{13,11},{20,18},{21,19},{28,26},{29,27}} | collective-permute-start | bytes 393224 | tf_op jit(solution)/shard_map/ppermute | solution.py:331
  66.3 11.7 %collective-permute-start.20 = (f32[2,128]{1,0:T(2,128)S(1)}, f32[2,128]{1,0:T(2,128)S(1)}, u32[]{:S(2)}, u32[]{:S(2)}) collective-permute-start(f32[2,128]{1,0:T(2,128)S(1)} %broadcast_select_fusion), channel_id=1, source_target_pairs={{0,4},{1,5},{2,6},{3,7},{4,0},{5,1},{6,2},{7,3},{8,12},{9,13},{10,... | collective-permute-start | bytes 3080 | tf_op jit(solution)/shard_map/ppermute | solution.py:284
  76.5 4.3 %collective-permute-start.21 = (f32[256,128]{1,0:T(8,128)S(1)}, f32[256,128]{1,0:T(8,128)S(1)}, u32[]{:S(2)}, u32[]{:S(2)}) collective-permute-start(f32[256,128]{1,0:T(8,128)S(1)} %get-tuple-element.101), channel_id=1, source_target_pairs={{0,1},{1,0},{2,3},{3,2},{4,5},{5,4},{6,7},{7,6},{8,9},{9,8},{10,11... | collective-permute-start | bytes 393224 | tf_op jit(solution)/shard_map/ppermute | solution.py:284
  78.0 5.8 %collective-permute-start.23 = (f32[1,128]{1,0:T(1,128)S(1)}, f32[1,128]{1,0:T(1,128)S(1)}, u32[]{:S(2)}, u32[]{:S(2)}) collective-permute-start(f32[1,128]{1,0:T(1,128)S(1)} %compare_select_fusion), channel_id=1, source_target_pairs={{0,2},{1,3},{2,0},{3,1},{4,6},{5,7},{6,4},{7,5},{8,10},{9,11},{10,... | collective-permute-start | bytes 1544 | tf_op jit(solution)/shard_map/ppermute | solution.py:284
  83.9 1.3 %collective-permute-start.24 = (f32[1,64]{1,0:T(1,128)S(1)}, f32[1,64]{1,0:T(1,128)S(1)}, u32[]{:S(2)}, u32[]{:S(2)}) collective-permute-start(f32[1,64]{1,0:T(1,128)S(1)} %slice_select_fusion.2), channel_id=1, source_target_pairs={{0,1},{1,0},{2,3},{3,2},{4,5},{5,4},{6,7},{7,6},{8,9},{9,8},{10,11... | collective-permute-start | bytes 776 | tf_op jit(solution)/shard_map/ppermute | solution.py:284
  83.9 7.8 %collective-permute-start.19 = (f32[256,128]{1,0:T(8,128)S(1)}, f32[256,128]{1,0:T(8,128)S(1)}, u32[]{:S(2)}, u32[]{:S(2)}) collective-permute-start(f32[256,128]{1,0:T(8,128)S(1)} %add_add_fusion), channel_id=1, source_target_pairs={{2,0},{3,1},{10,8},{11,9},{18,16},{19,17},{26,24},{27,25}} | collective-permute-start | bytes 393224 | tf_op jit(solution)/shard_map/ppermute | solution.py:331
  91.7 1.4 %collective-permute-start.22 = (f32[256,128]{1,0:T(8,128)S(1)}, f32[256,128]{1,0:T(8,128)S(1)}, u32[]{:S(2)}, u32[]{:S(2)}) collective-permute-start(f32[256,128]{1,0:T(8,128)S(1)} %get-tuple-element.99), channel_id=1, source_target_pairs={{0,1},{1,0},{2,3},{3,2},{4,5},{5,4},{6,7},{7,6},{8,9},{9,8},{10,11... | collective-permute-start | bytes 393224 | tf_op jit(solution)/shard_map/ppermute | solution.py:284
  (4 other events, 13.1 us)

commit v10 on v9

v10 whole, which is shorter than its diff:
```python
import functools

import jax
import jax.numpy as jnp
from jax import lax
from jax.experimental import pallas as pl
from jax.experimental.pallas import tpu as pltpu
from jax.sharding import PartitionSpec as P

E = 64
PAIR = 2 * E
GROUPS = 2
EXTRA = 8
PAD = 32
VMEM = 10 * 2**20
SUB = 2
F32 = jnp.float32
BF16 = jnp.bfloat16


def dot(a, b, ca, cb):
    return lax.dot_general(a, b, (((ca,), (cb,)), ((), ())), preferred_element_type=F32)


def low_lanes(rows, cols):
    lane = lax.broadcasted_iota(jnp.int32, (rows, cols), 1)
    return lane % PAIR < E


def fold(product):
    return jnp.where(low_lanes(E, product.shape[1]), product[:E], product[E:])


def split(state):
    high = state.astype(BF16)
    return high, (state - high.astype(F32)).astype(BF16)


def spread(state):
    low = low_lanes(*state.shape)
    zero = jnp.zeros_like(state)
    return jnp.concatenate([jnp.where(low, state, zero), jnp.where(low, zero, state)], axis=0)


def heads_of(pair):
    low = low_lanes(*pair.shape)
    zero = jnp.zeros_like(pair)
    return jnp.where(low, pair, zero), jnp.where(low, zero, pair)


def twice(x):
    return jnp.concatenate([x, x], axis=1)


def pair_at(ref, p):
    return ref[:, p * PAIR:(p + 1) * PAIR]


def rows_at(base, p):
    return pl.ds(pl.multiple_of(base + p * E, E), E)


def twice(x):
    return jnp.concatenate([x, x], axis=1)


def pair_at(ref, p):
    return ref[:, p * PAIR:(p + 1) * PAIR]


def rows_at(base, p):
    return pl.ds(pl.multiple_of(base + p * E, E), E)


def own_or_received(keep, received, own, p):
    return jnp.where(own, keep[rows_at(p)], received[rows_at(p)])


def state_pair(a, b):
    return fold(dot(a, b, 0, 0))


def edge(seg, table, last):
    row = seg[...]
    count = row.shape[1]
    own = row[:, count - 1:] if last else row[:, :1]
    size = jnp.sum((row == own).astype(F32), axis=1, keepdims=True)
    at = lax.broadcasted_iota(jnp.int32, (count, PAIR), 0).astype(F32)
    rows = at >= count - size if last else at < size
    ids = lax.broadcasted_iota(jnp.int32, table.shape, 1)
    flag = jnp.sum(jnp.where(ids == own, table[...], 0).astype(F32), axis=1, keepdims=True)
    return rows, own.astype(F32), flag


def lanes_at(base, p):
    return pl.ds(pl.multiple_of(base + p * PAIR, PAIR), PAIR)


def place(sel, core, lanes, sub):
    step = pl.program_id(0)
    group, part = step // sub, step % sub
    half = (sel + core[0]) % 2
    base = group * lanes + part * (lanes // sub)
    return group, base, base + (group + half) * lanes, base // PAIR * E


def states_kernel(position, k_in, v_in, keep, send, zero, k, v, core_row, ctx_row, dp_row, sems):
    for i, row in enumerate((core_row, ctx_row, dp_row)):
        row[...] = jnp.full(row.shape, position[i], jnp.int32)
    lanes = k.shape[1] // GROUPS // 2
    count = lanes // PAIR
    copies = []
    for sel in (1, 0):
        for group in range(GROUPS):
            base = (2 * group + (sel + position[0]) % 2) * lanes
            at = pl.ds(pl.multiple_of(base, lanes), lanes)
            for i, (array, buf) in enumerate(((k_in, k), (v_in, v))):
                copies.append(pltpu.make_async_copy(array.at[:, at], buf.at[:, at], sems.at[2 * group + sel, i]))
    for copy in copies:
        copy.start()
    zero[...] = jnp.zeros_like(zero)
    for sel, out in ((1, send), (0, keep)):
        out[GROUPS * count * E:] = jnp.zeros((PAD, PAIR), F32)
        for group in range(GROUPS):
            copies.pop(0).wait()
            copies.pop(0).wait()
            base = (2 * group + (sel + position[0]) % 2) * lanes
            for p in range(count):
                at = lanes_at(base, p)
                row = (group * count + p) * E
                out[row:row + E] = state_pair(k[:, at], v[:, at])


def part_kernel(core, q_in, dy_in, k, v, seg, table, *rest):
    *outs, q, dy, token, sems = rest[-6:]
    copies = [pltpu.make_async_copy(a, b, sems.at[i]) for i, (a, b) in enumerate(((q_in, q), (dy_in, dy)))]
    for copy in copies:
        copy.start()
    token[...] = jnp.zeros_like(token)
    lanes = k.shape[1] // GROUPS // 2
    count = lanes // PAIR
    rows, own, _ = edge(seg, table, False)
    keep = rows.astype(BF16)
    for sel, out in enumerate(outs):
        for group in range(GROUPS):
            base = (2 * group + (sel + core[0]) % 2) * lanes
            for p in range(count):
                at = lanes_at(base, p)
                out[group, p * E:(p + 1) * E] = state_pair(k[:, at], v[:, at] * keep)
            out[group, count * E:] = jnp.broadcast_to(own, (EXTRA, PAIR))
    for copy in copies:
        copy.wait()


def local_kernel(sel, core, q, k, v, mask, mask_t, *rest):
    attn, probs, token = rest[-3:]
    lanes = attn.shape[1] // GROUPS
    group, base, wide, _ = place(sel, core, lanes, 1)
    m, mt = mask[...], mask_t[...]
    token[...] = jnp.zeros_like(token)
    for p in range(lanes // PAIR):
        at = lanes_at(wide, p)
        kp = k[:, at]
        total = None
        for h, (qh, vh) in enumerate(zip(heads_of(q[:, at]), heads_of(v[:, at]))):
            prob = dot(qh, kp, 1, 1).astype(BF16) * m
            probs[group * (lanes // E) + 2 * p + h] = dot(kp, qh, 1, 1).astype(BF16) * mt
            term = dot(prob, vh, 1, 0)
            total = term if total is None else total + term
        attn[:, lanes_at(base, p)] = total


def head_mean(x):
    high, low = split(x)
    ones = spread(jnp.full((E, PAIR), 1.0 / E, BF16))
    return dot(jnp.concatenate([high, low], axis=1), jnp.concatenate([ones, ones], axis=0), 1, 0)


def side_by_side(state, part):
    sh, sl = split(state)
    ph, pll = split(part)
    left = jnp.concatenate([spread(sh), spread(sl)], axis=0)
    right = jnp.concatenate([spread(ph), spread(pll)], axis=0)
    return jnp.concatenate([left, right], axis=1)


def stacked(state, part):
    sh, sl = split(state)
    ph, pll = split(part)
    top = jnp.concatenate([spread(sh), spread(sl)], axis=1)
    bottom = jnp.concatenate([spread(ph), spread(pll)], axis=1)
    return jnp.concatenate([top, bottom], axis=0)


def on_rows(seg, table, last, part):
    rows, own, flag = edge(seg, table, last)
    met = part[0, part.shape[1] - EXTRA:part.shape[1] - EXTRA + 1] == own
    if last:
        met = met & (flag == 1)
    return rows.astype(F32) * met.astype(F32)


def norm_kernel(sel, core, q, dy, local, gain, seg, table, prefix, nxt, *rest):
    out, dab, part, gsum, total, token = rest[-6:]
    token[...] = jnp.zeros_like(token)
    lanes = out.shape[1]
    count = lanes // PAIR
    _, base, wide, row = place(sel, core, lanes, 1)
    on_next = on_rows(seg, table, True, nxt)
    last, own, flag = edge(seg, table, True)
    last = (last.astype(F32) * jnp.where(flag == 1, 1.0, 0.0)).astype(BF16)
    pairs = [slice(p * PAIR, (p + 1) * PAIR) for p in range(count)]
    bases = [lanes_at(base, p) for p in range(count)]
    wides = [lanes_at(wide, p) for p in range(count)]
    fars = [
        dot(twice(q[:, at]), side_by_side(prefix[rows_at(row, p)], nxt[0, rows_at(0, p)]), 1, 0)
        for p, at in enumerate(wides)
    ]
    attns = [local[:, at] + far[:, :PAIR] + on_next * far[:, PAIR:] for at, far in zip(bases, fars)]
    squares = [head_mean(attn * attn) for attn in attns]
    scales = [lax.rsqrt(square + 1e-06) for square in squares]
    normeds = [attn * scale for attn, scale in zip(attns, scales)]
    gas = [dy[:, at].astype(F32) * gain[:, pair] for at, pair in zip(wides, pairs)]
    means = [head_mean(ga * normed) for ga, normed in zip(gas, normeds)]
    das = [
        (scale * (ga - normed * mean)).astype(BF16)
        for scale, ga, normed, mean in zip(scales, gas, normeds, means)
    ]
    states = [state_pair(q[:, at], jnp.concatenate([da, da * last], axis=1)) for at, da in zip(wides, das)]
    part[0, count * E:] = jnp.broadcast_to(own, (EXTRA, PAIR))
    total[GROUPS * count * E:] = jnp.zeros((PAD, PAIR), F32)
    for p, (at, normed, da) in enumerate(zip(pairs, normeds, das)):
        total[rows_at(row, p)] = states[p][:, :PAIR]
        part[0, p * E:(p + 1) * E] = states[p][:, PAIR:]
        dab[:, bases[p]] = da
        out[:, at] = (normed * gain[:, at]).astype(BF16)
        gsum[0, p:p + 1] = jnp.sum(dy[:, wides[p]].astype(F32) * normed, axis=0, keepdims=True)


def inner_kernel(sel, core, q, k, v, dab, probs, mask, seg, table, prefix, nxt, *rest):
    gq, gk, gv, token = rest[-4:]
    lanes = dab.shape[1] // GROUPS
    count = lanes // SUB // PAIR
    group, base, wide, row = place(sel, core, lanes, SUB)
    m = mask[...]
    token[...] = jnp.zeros_like(token)
    on_next = on_rows(seg, table, True, nxt)
    first = row - group * (lanes // 2)
    for p in range(count):
        at = lanes_at(wide, p)
        da = dab[:, lanes_at(base, p)]
        vp = v[:, at]
        far = dot(twice(da), stacked(prefix[rows_at(row, p)], nxt[0, rows_at(first, p)]), 1, 1)
        tq = far[:, :PAIR] + on_next * far[:, PAIR:]
        tk = tv = None
        for h, (qh, kh, dh) in enumerate(zip(heads_of(q[:, at]), heads_of(k[:, at]), heads_of(da))):
            dprob = dot(dh, vp, 1, 1).astype(BF16) * m
            tq = tq + dot(dprob, kh, 1, 0)
            a = dot(dprob, qh, 0, 0)
            b = dot(probs[row // (E // 2) + 2 * p + h], dh, 1, 0)
            tk = a if tk is None else tk + a
            tv = b if tv is None else tv + b
        gq[:, p * PAIR:(p + 1) * PAIR] = tq.astype(BF16)
        gk[:, lanes_at(base, p)] = tk
        gv[:, lanes_at(base, p)] = tv


def outer_kernel(sel, core, k, v, gk_in, gv_in, seg, table, suffix, prv, *rest):
    gk, gv, token = rest[-3:]
    lanes = gk_in.shape[1] // GROUPS
    count = lanes // SUB // PAIR
    group, base, wide, row = place(sel, core, lanes, SUB)
    token[...] = jnp.zeros_like(token)
    on_prev = on_rows(seg, table, False, prv)
    first = row - group * (lanes // 2)
    for p in range(count):
        here, own, at = slice(p * PAIR, (p + 1) * PAIR), lanes_at(base, p), lanes_at(wide, p)
        s = suffix[rows_at(row, p)]
        g = prv[0, rows_at(first, p)]
        far = dot(twice(v[:, at]), stacked(s, g), 1, 1)
        gk[:, here] = (gk_in[:, own] + far[:, :PAIR] + on_prev * far[:, PAIR:]).astype(BF16)
        far = dot(twice(k[:, at]), side_by_side(s, g), 1, 0)
        gv[:, here] = (gv_in[:, own] + far[:, :PAIR] + on_prev * far[:, PAIR:]).astype(BF16)


def partner(x, axis, bit):
    route = [(i, i ^ (1 << bit)) for i in range(lax.axis_size(axis))]
    return lax.ppermute(x, axis, route)


def shifted(x, distance):
    count = lax.axis_size("ctx")
    return lax.ppermute(x, "ctx", [(i, i + distance) for i in range(count) if 0 <= i + distance < count])


def nought(x):
    return jnp.minimum(jnp.abs(x), 0.0)


def within_chip(keep, send):
    received = partner(send, "ctx", 0)
    return keep, received, keep + received


def to_cores(core, before, piece, towards):
    keep, received, _ = piece
    is_source = core == (0 if towards == 1 else 1)
    mine = jnp.where(is_source, before, before + received)
    return mine, partner(jnp.where(is_source, before + keep, before), "ctx", 0)


def pinned(x, space):
    return pltpu.with_memory_space_constraint(x, space)


def scatter_step(x, at, axis, bit):
    low, high = jnp.split(x, 2, axis=1)
    upper = (at >> bit & 1 == 1)[:, :low.shape[1]]
    return jnp.where(upper, high, low) + partner(jnp.where(upper, low, high), axis, bit)


def scatter_stage(pieces, at, axis, low):
    def chosen(index):
        value = pieces[0]
        for i, piece in enumerate(pieces[1:]):
            value = jnp.where(index == i + 1, piece, value)
        return value

    own = at >> low & (len(pieces) - 1)
    total = chosen(own)
    for flip in range(1, len(pieces)):
        route = [(i, i ^ (flip << low)) for i in range(lax.axis_size(axis))]
        total = total + lax.ppermute(chosen(own ^ flip), axis, route)
    return total


def on_device(queries, keys, values, out_grad, segment_ids, image_flags, gain):
    rows, width = queries.shape[1:]
    q, k, v, dy = (x[0] for x in (queries, keys, values, out_grad))
    table = image_flags[0]
    gain_row = gain.reshape(1, width)
    ctx = lax.axis_index("ctx")
    core = jnp.stack([ctx & 1, ctx, lax.axis_index("dp")]).astype(jnp.int32)
    lanes = width // GROUPS // 2
    half_rows = lanes // PAIR * E
    heads = lanes // E

    def call(kernel, sel, ins, outs, after=(), alias=(), scratch=(), sub=1, steps=None):
        def wide(i, c):
            return (0, (i // sub * 2 + (sel + c[0]) % 2) * sub + i % sub)

        def whole(*args):
            return (0, 0)

        def part(i, c):
            return (i // sub, 0, 0)

        specs = {
            "vmem": pl.BlockSpec(memory_space=pltpu.VMEM),
            "hbm": pl.BlockSpec(memory_space=pltpu.HBM),
            "wide": pl.BlockSpec((rows, lanes // sub), wide),
            "row": pl.BlockSpec((1, lanes // sub), wide),
            "sums": pl.BlockSpec((1, lanes // PAIR, PAIR), part),
            "zero": pl.BlockSpec((1, rows), whole),
            "all": pl.BlockSpec((GROUPS * half_rows + PAD, PAIR), whole),
            "part": pl.BlockSpec((1, half_rows + EXTRA, PAIR), part),
            "parts": pl.BlockSpec((GROUPS, half_rows + EXTRA, PAIR), lambda *args: (0, 0, 0)),
            "seg": pl.BlockSpec((1, rows), whole),
            "table": pl.BlockSpec((1, table.shape[0]), whole),
            "mask": pl.BlockSpec((rows, rows), whole),
            "token": pl.BlockSpec((1, PAIR), whole),
            "after2": pl.BlockSpec((8, PAIR), whole),
            "after3": pl.BlockSpec((1, 8, PAIR), lambda *args: (0, 0, 0)),
            "any": pl.BlockSpec(memory_space=pl.ANY),
        }
        shapes = {
            "wide": (rows, width),
            "sums": (GROUPS, lanes // PAIR, PAIR),
            "zero": (1, rows),
            "all": (GROUPS * half_rows + PAD, PAIR),
            "part": (GROUPS, half_rows + EXTRA, PAIR),
            "parts": (GROUPS, half_rows + EXTRA, PAIR),
            "token": (1, PAIR),
        }
        spaces = {"vmem": pltpu.VMEM, "hbm": pltpu.HBM}
        operands = [pinned(x, spaces[kind]) if kind in spaces else x for kind, x in ins] + list(after)
        kinds = [kind for kind, _ in ins] + [f"after{x.ndim}" for x in after]
        aliases = {}
        for out_at, x in alias:
            if x is not None:
                aliases[1 + len(operands)] = out_at
                operands.append(x)
                kinds.append("any")
        out_shape = [
            pltpu.VMEM(*shape, dtype) if kind == "vmem" else jax.ShapeDtypeStruct(shapes[kind], dtype)
            for kind, dtype, *shape in outs
        ]
        return pl.pallas_call(
            kernel,
            grid_spec=pltpu.PrefetchScalarGridSpec(
                num_scalar_prefetch=1,
                grid=steps or (GROUPS * sub,),
                in_specs=[specs[kind] for kind in kinds],
                out_specs=[specs[kind] for kind, *_ in outs],
                scratch_shapes=scratch,
            ),
            out_shape=out_shape,
            input_output_aliases=aliases,
            compiler_params=pltpu.CompilerParams(vmem_limit_bytes=VMEM),
            cost_estimate=pl.CostEstimate(flops=1, bytes_accessed=1, transcendentals=0),
        )(core, *operands)

    edges = [("seg", segment_ids), ("table", image_flags)]
    chips = lax.axis_size("ctx") // 2
    whole, part_of = (rows, width), (rows, width // 2)

    def local_attn(sel, after):
        return call(
            functools.partial(local_kernel, sel), sel,
            [("vmem", q), ("vmem", k), ("vmem", v), ("mask", mask), ("mask", mask_t)],
            [("vmem", F32, part_of), ("vmem", BF16, (GROUPS * heads, rows, rows)), ("token", F32)], after=after)

    def norm(sel, before, after):
        return call(
            functools.partial(norm_kernel, sel), sel,
            [("vmem", q), ("vmem", dy), ("vmem", local[sel][0]), ("row", gain_row), *edges,
             ("all", prefix[sel]), ("part", nxt[sel])],
            [("wide", BF16), ("vmem", BF16, part_of), ("part", F32), ("sums", F32), ("all", F32), ("token", F32)],
            after=after, alias=[(0, before)])

    def inner(sel, before, after):
        return call(
            functools.partial(inner_kernel, sel), sel,
            [("vmem", q), ("vmem", k), ("vmem", v), ("vmem", norms[sel][1]), ("vmem", local[sel][1]), ("mask", mask),
             *edges, ("all", prefix[sel]), ("part", nxt[sel])],
            [("wide", BF16), ("vmem", F32, part_of), ("vmem", F32, part_of), ("token", F32)],
            after=after, alias=[(0, before)], sub=SUB)

    def outer(sel, before, after):
        return call(
            functools.partial(outer_kernel, sel), sel,
            [("vmem", k), ("vmem", v), ("vmem", inners[sel][1]), ("vmem", inners[sel][2]), *edges,
             ("all", suffix[sel]), ("part", prv[sel])],
            [("wide", BF16), ("wide", BF16), ("token", F32)], after=after, alias=list(enumerate(before)), sub=SUB)

    def summed_before(own, towards, works):
        load, before, span = own, None, 1
        while span < chips:
            arrived = shifted(load, 2 * towards * span)
            if works:
                arrived = arrived + works.pop(0)(load)
            before = arrived if before is None else before + arrived
            load = load + arrived
            span *= 2
        for work in works:
            before = before + work(load)
        return before

    keep, send, zero, k, v, core_row, ctx_row, dp_row = call(
        states_kernel, 0, [("hbm", k), ("hbm", v)],
        [("all", F32), ("all", F32), ("zero", jnp.int32), ("vmem", BF16, whole), ("vmem", BF16, whole)]
        + [("token", jnp.int32)] * 3,
        scratch=[pltpu.SemaphoreType.DMA((2 * GROUPS, 2))], steps=(1,))
    piece = within_chip(keep, send)
    seg = (segment_ids + zero)[0]
    onehot = seg[:, None] == jnp.arange(table.shape[0], dtype=jnp.int32)[None, :]
    img = jnp.sum(jnp.where(onehot, table[None, :], 0), axis=1)
    imgseg = jnp.where(img == 1, seg, -1)
    pos = jnp.arange(rows)
    mask = ((pos[:, None] >= pos[None, :]) | (imgseg[:, None] == seg[None, :])).astype(BF16)
    mask_t = ((pos[:, None] <= pos[None, :]) | (seg[:, None] == imgseg[None, :])).astype(BF16)

    parts = call(
        part_kernel, 0, [("hbm", q), ("hbm", dy), ("vmem", k), ("vmem", v), *edges],
        [("parts", F32)] * 2 + [("vmem", BF16, whole), ("vmem", BF16, whole), ("token", F32)],
        after=[piece[2]], scratch=[pltpu.SemaphoreType.DMA((2,))], steps=(1,))
    *parts, q, dy, _ = parts
    local, nxt = [], []

    def first_work(load):
        *made, token = local_attn(0, [parts[0]])
        local.append(made)
        return token

    def second_work(load):
        for part in reversed(parts):
            nxt.append(shifted(part + nought(load[:1]), -1))
        *made, token = local_attn(1, [load])
        local.append(made)
        return token + nought(nxt[0][0, :1]) + nought(nxt[1][0, :1])

    before = summed_before(piece[2], 1, [first_work, second_work])
    prefix = to_cores(core_row, before, piece, 1)
    norms = [norm(0, None, [])]
    norms.append(norm(1, norms[0][0], [norms[0][4]]))
    output = norms[1][0]
    piece = within_chip(norms[0][4], norms[1][4])
    sums = [jnp.where(core_row == sel, norms[0][3], norms[1][3]) for sel in range(2)]
    gain_sum = [[jnp.stack(sums, axis=1).reshape(-1, PAIR)]]
    inners, prv = [], []

    def third_work(load):
        x = (gain_sum[0][0] + nought(load[:1])).reshape(4, 4, PAIR)
        top = lax.axis_size("ctx").bit_length() - 3
        gain_sum.append(scatter_stage([x[:, i] for i in range(4)], ctx_row, "ctx", top))
        inners.append(inner(0, None, [load]))
        return inners[0][3] + nought(gain_sum[-1][:1])

    def fourth_work(load):
        x = gain_sum[-1] + nought(load[:1])
        gain_sum.append(scatter_stage([x[i:i + 1] for i in range(4)], dp_row, "dp", 0))
        for part in (norms[1][2], norms[0][2]):
            prv.append(shifted(part + nought(load[:1]), 1))
        inners.append(inner(1, inners[0][0], [load]))
        return inners[1][3] + nought(gain_sum[-1]) + nought(prv[0][0, :1]) + nought(prv[1][0, :1])

    before = summed_before(piece[2], -1, [third_work, fourth_work])
    suffix = to_cores(core_row, before, piece, -1)
    outers = outer(0, [None] * 2, [])
    grad_k, grad_v, _ = outer(1, outers[:2], [])
    grad_q = inners[1][0]
    grad_gain = gain_sum[-1]
    for bit in reversed(range(lax.axis_size("ctx").bit_length() - 3)):
        grad_gain = scatter_step(grad_gain, ctx_row, "ctx", bit)
    grad_gain = grad_gain.reshape(-1)
    return output[None], grad_q[None], grad_k[None], grad_v[None], grad_gain


def solution(mesh):
    return jax.shard_map(
        on_device,
        mesh=mesh,
        in_specs=(
            P("dp", "ctx", None),
            P("dp", "ctx", None),
            P("dp", "ctx", None),
            P("dp", "ctx", None),
            P("dp", "ctx"),
            P("dp", None),
            P(),
        ),
        out_specs=(
            P("dp", "ctx", None),
            P("dp", "ctx", None),
            P("dp", "ctx", None),
            P("dp", "ctx", None),
            P(("dp", "ctx")),
        ),
        check_vma=False,
    )
```

time: 96.5 us -> 92.9 us (0.963)
  starting transfers between devices: 45.4 us -> 40.3 us
  waiting for transfers between devices: 13 us -> 14.2 us
    ppermute x12 -> x5, starting transfers between devices: 23.1 us -> 1.62 us  [partner(): return lax.ppermute(x, axis, route)]
    ppermute x4 -> x8, starting transfers between devices: 6.16 us -> 22.2 us  [shifted(): lax.ppermute(x, 'ctx', [(i, i + distance) for i in range(count) if 0 <= i...]
    ppermute x4 -> x8, waiting for transfers between devices: 0.39 us -> 10.4 us  [shifted(): lax.ppermute(x, 'ctx', [(i, i + distance) for i in range(count) if 0 <= i...]
    ppermute x9 -> x6, waiting for transfers between devices: 7.9 us -> 0.54 us  [scatter_stage(): total = total + lax.ppermute(chosen(own ^ flip), axis, route)]
    ppermute x12 -> x5, waiting for transfers between devices: 4.72 us -> 3.21 us  [partner(): return lax.ppermute(x, axis, route)]
    ppermute x9 -> x6, starting transfers between devices: 16.1 us -> 16.5 us  [scatter_stage(): total = total + lax.ppermute(chosen(own ^ flip), axis, route)]
  transfers between devices with their start and end apart: 25 -> 19, of which waited for: 9 -> 7; matrix products, arithmetic and copies ran while one was open for 1% -> 1% of each run, Pallas kernels for 30% -> 29%
where the time goes in v10:
time: 92.9 us; the launch traced here: 92.5 us
  starting transfers between devices  40.3 us (43%)
  Pallas kernels  35.6 us (38%)
  waiting for transfers between devices  14.2 us (15%)
  other arithmetic  1.55 us (2%)
  between operations  0.97 us (1%)
    pallas_call x10, Pallas kernels, call(): pl.pallas_call(kernel, grid_spec=pltpu.PrefetchScalarGridSpec(num_scalar_...  35.6 us
    ppermute x8, starting transfers between devices, shifted(): lax.ppermute(x, 'ctx', [(i, i + distance) for i in range(count) if 0 <= i...  22.2 us
    ppermute x6, starting transfers between devices, scatter_stage(): total = total + lax.ppermute(chosen(own ^ flip), axis, route)  16.5 us
    ppermute x8, waiting for transfers between devices, shifted(): lax.ppermute(x, 'ctx', [(i, i + distance) for i in range(count) if 0 <= i...  10.4 us
    ppermute x5, waiting for transfers between devices, partner(): return lax.ppermute(x, axis, route)  3.21 us
  transfers between devices with their start and end apart: 19, of which 7 were waited for; matrix products, arithmetic and copies ran while one was open for 1% of the time, Pallas kernels for 29%

profile of v10, /device:TPU:0, one launch (start us, length us, event | category | flops | bytes accessed | tf_op | source)
XLA Modules:
  0.0 92.5 jit_solution(16333763120346960865)
XLA Ops:
  0.7 3.0 %shard_map.110 = (f32[544,128]{1,0:T(8,128)S(1)}, f32[544,128]{1,0:T(8,128)S(1)}, s32[1,256]{1,0:T(1,128)S(1)}, bf16[256,2048]{1,0:T(8,128)(2,1)S(1)}, bf16[256,...) custom-call(s32[3]{0:T(128)S(1)} %pad_add_fusion.position.core, ...), custom_call_target="tpu_custom_call" | custom-call | flops 1 | bytes 1 | tf_op jit(solution)/shard_map/pallas_call | solution.py:398
  5.4 4.9 %collective-permute-start.1 = (f32[544,128]{1,0:T(8,128)S(1)}, f32[544,128]{1,0:T(8,128)S(1)}, u32[]{:S(2)}, u32[]{:S(2)}) collective-permute-start(f32[544,128]{1,0:T(8,128)S(1)} %add.163.rest_0_), channel_id=1, source_target_pairs={{0,2},{1,3},{2,4},{3,5},{4,6},{5,7},{8,10},{9,11},{10,12},{11,13},... | collective-permute-start | bytes 835592 | tf_op jit(solution)/shard_map/ppermute | solution.py:293
  10.5 3.2 %shard_map.111 = (f32[2,264,128]{2,1,0:T(8,128)S(1)}, f32[2,264,128]{2,1,0:T(8,128)S(1)}, bf16[256,2048]{1,0:T(8,128)(2,1)S(1)}, bf16[256,2048]{1,0:T(8,128)(2,1)S(1)}, f32[1,128]{1,0:T(1,128)}) custom-call(s32[3]{0:T(128)S(1)} %pad_add_fusion.position.core, bf16[256,2048]{1,0:T(8,128)(2,1)} %bitcast.141, bf16[256,2048]{1,0:T(8,128)(2,1)} %bitcast.142, ...), custom_call_target="tpu_custom_call" | custom-call | flops 1 | bytes 1 | tf_op jit(solution)/shard_map/pallas_call | solution.py:398
  13.6 3.0 %shard_map.112 = (f32[256,1024]{1,0:T(8,128)S(1)}, bf16[16,256,256]{2,1,0:T(8,128)(2,1)S(1)}, f32[1,128]{1,0:T(1,128)S(1)}) custom-call(s32[3]{0:T(128)S(1)} %pad_add_fusion.position.core, bf16[256,2048]{1,0:T(8,128)(2,1)S(1)} %get-tuple-element.49.q, bf16[256,2048]{1,0:T(8,128)(2,1)S(1)} %get-tuple-element.45.k, bf16[256,2048]{1,0:T(8,128)(2,1)S(1)} %get-tuple-element.46.v, ...), custom_call_target="tpu_custom_call" | custom-call | flops 1 | bytes 1 | tf_op jit(solution)/shard_map/pallas_call | solution.py:398
  18.1 1.3 %collective-permute-start.4 = (f32[2,264,128]{2,1,0:T(8,128)S(1)}, f32[2,264,128]{2,1,0:T(8,128)S(1)}, u32[]{:S(2)}, u32[]{:S(2)}) collective-permute-start(f32[2,264,128]{2,1,0:T(8,128)S(1)} %get-tuple-element.120), channel_id=1, source_target_pairs={{1,0},{2,1},{3,2},{4,3},{5,4},{6,5},{7,6},{9,8},{10,9},{11,10},{12... | collective-permute-start | bytes 811016 | tf_op jit(solution)/shard_map/ppermute | solution.py:293
  19.4 7.0 %collective-permute-start.2 = (f32[544,128]{1,0:T(8,128)S(1)}, f32[544,128]{1,0:T(8,128)S(1)}, u32[]{:S(2)}, u32[]{:S(2)}) collective-permute-start(f32[544,128]{1,0:T(8,128)S(1)} %add_add_fusion.3.rest_0_), channel_id=1, source_target_pairs={{0,4},{1,5},{2,6},{3,7},{8,12},{9,13},{10,14},{11,15},{16,20},{17,... | collective-permute-start | bytes 835592 | tf_op jit(solution)/shard_map/ppermute | solution.py:293
  26.4 3.0 %shard_map.113 = (f32[256,1024]{1,0:T(8,128)S(1)}, bf16[16,256,256]{2,1,0:T(8,128)(2,1)S(1)}, f32[1,128]{1,0:T(1,128)S(1)}) custom-call(s32[3]{0:T(128)S(1)} %pad_add_fusion.position.core, bf16[256,2048]{1,0:T(8,128)(2,1)S(1)} %get-tuple-element.49.q, bf16[256,2048]{1,0:T(8,128)(2,1)S(1)} %get-tuple-element.45.k, bf16[256,2048]{1,0:T(8,128)(2,1)S(1)} %get-tuple-element.46.v, ...), custom_call_target="tpu_custom_call" | custom-call | flops 1 | bytes 1 | tf_op jit(solution)/shard_map/pallas_call | solution.py:398
  29.5 3.0 %collective-permute-done.2 = f32[544,128]{1,0:T(8,128)S(1)} collective-permute-done((f32[544,128]{1,0:T(8,128)S(1)}, f32[544,128]{1,0:T(8,128)S(1)}, u32[]{:S(2)}, u32[]{:S(2)}) %collective-permute-start.2) | collective-permute-done | bytes 278560 | tf_op jit(solution)/shard_map/ppermute | solution.py:293
  32.7 3.1 %shard_map.114 = (bf16[256,2048]{1,0:T(8,128)(2,1)}, bf16[256,1024]{1,0:T(8,128)(2,1)S(1)}, f32[2,264,128]{2,1,0:T(8,128)S(1)}, f32[2,4,128]{2,1,0:T(4,128)S(1)}...) custom-call(s32[3]{0:T(128)S(1)} %pad_add_fusion.position.core, bf16[256,2048]{1,0:T(8,128)(2,1)S(1)} %get-tuple-element.49.q, ...), custom_call_target="tpu_custom_call" | custom-call | flops 1 | bytes 1 | tf_op jit(solution)/shard_map/pallas_call | solution.py:398
  35.7 2.9 %shard_map.115 = (bf16[256,2048]{1,0:T(8,128)(2,1)}, bf16[256,1024]{1,0:T(8,128)(2,1)S(1)}, f32[2,264,128]{2,1,0:T(8,128)S(1)}, f32[2,4,128]{2,1,0:T(4,128)S(1)}...) custom-call(s32[3]{0:T(128)S(1)} %pad_add_fusion.position.core, ...), custom_call_target="tpu_custom_call", output_to_operand_aliasing={{0}: (10, {})} | custom-call | flops 1 | bytes 1 | tf_op jit(solution)/shard_map/pallas_call | solution.py:398
  40.4 7.5 %collective-permute-start.8 = (f32[4,128]{1,0:T(4,128)S(1)}, f32[4,128]{1,0:T(4,128)S(1)}, u32[]{:S(2)}, u32[]{:S(2)}) collective-permute-start(f32[4,128]{1,0:T(4,128)S(1)} %get-tuple-element.93), channel_id=1, source_target_pairs={{0,2},{1,3},{2,0},{3,1},{4,6},{5,7},{6,4},{7,5},{8,10},{9,11},{10,... | collective-permute-start | bytes 6152 | tf_op jit(solution)/shard_map/ppermute | solution.py:333
  47.9 2.9 %collective-permute-start.10 = (f32[4,128]{1,0:T(4,128)S(1)}, f32[4,128]{1,0:T(4,128)S(1)}, u32[]{:S(2)}, u32[]{:S(2)}) collective-permute-start(f32[4,128]{1,0:T(4,128)S(1)} %get-tuple-element.94), channel_id=1, source_target_pairs={{0,6},{1,7},{2,4},{3,5},{4,2},{5,3},{6,0},{7,1},{8,14},{9,15},{10,... | collective-permute-start | bytes 6152 | tf_op jit(solution)/shard_map/ppermute | solution.py:333
  52.7 5.7 %shard_map.116 = (bf16[256,2048]{1,0:T(8,128)(2,1)}, f32[256,1024]{1,0:T(8,128)S(1)}, f32[256,1024]{1,0:T(8,128)S(1)}, f32[1,128]{1,0:T(1,128)S(1)}) custom-call(s32[3]{0:T(128)S(1)} %pad_add_fusion.position.core, bf16[256,2048]{1,0:T(8,128)(2,1)S(1)} %get-tuple-element.49.q, bf16[256,2048]{1,0:T(8,128)(2,1)S(1)} %get-tuple-element.45.k, ...), custom_call_target="tpu_custom_call" | custom-call | flops 1 | bytes 1 | tf_op jit(solution)/shard_map/pallas_call | solution.py:398
  58.4 3.2 %collective-permute-done.7 = f32[544,128]{1,0:T(8,128)S(1)} collective-permute-done((f32[544,128]{1,0:T(8,128)S(1)}, f32[544,128]{1,0:T(8,128)S(1)}, u32[]{:S(2)}, u32[]{:S(2)}) %collective-permute-start.7) | collective-permute-done | bytes 278560 | tf_op jit(solution)/shard_map/ppermute | solution.py:293
  61.7 1.3 %collective-permute-start.15 = (f32[2,264,128]{2,1,0:T(8,128)S(1)}, f32[2,264,128]{2,1,0:T(8,128)S(1)}, u32[]{:S(2)}, u32[]{:S(2)}) collective-permute-start(f32[2,264,128]{2,1,0:T(8,128)S(1)} %get-tuple-element.115), channel_id=1, source_target_pairs={{0,1},{1,2},{2,3},{3,4},{4,5},{5,6},{6,7},{8,9},{9,10},{10,11},{11... | collective-permute-start | bytes 811016 | tf_op jit(solution)/shard_map/ppermute | solution.py:293
  63.0 3.8 %collective-permute-start.16 = (f32[2,264,128]{2,1,0:T(8,128)S(1)}, f32[2,264,128]{2,1,0:T(8,128)S(1)}, u32[]{:S(2)}, u32[]{:S(2)}) collective-permute-start(f32[2,264,128]{2,1,0:T(8,128)S(1)} %get-tuple-element.116), channel_id=1, source_target_pairs={{0,1},{1,2},{2,3},{3,4},{4,5},{5,6},{6,7},{8,9},{9,10},{10,11},{11... | collective-permute-start | bytes 811016 | tf_op jit(solution)/shard_map/ppermute | solution.py:293
  66.9 1.3 %collective-permute-start.11 = (f32[544,128]{1,0:T(8,128)S(1)}, f32[544,128]{1,0:T(8,128)S(1)}, u32[]{:S(2)}, u32[]{:S(2)}) collective-permute-start(f32[544,128]{1,0:T(8,128)S(1)} %add_add_fusion.2.rest_0_), channel_id=1, source_target_pairs={{4,0},{5,1},{6,2},{7,3},{12,8},{13,9},{14,10},{15,11},{20,16},{21,... | collective-permute-start | bytes 835592 | tf_op jit(solution)/shard_map/ppermute | solution.py:293
  68.2 1.6 %collective-permute-start.12 = (f32[1,128]{1,0:T(1,128)S(1)}, f32[1,128]{1,0:T(1,128)S(1)}, u32[]{:S(2)}, u32[]{:S(2)}) collective-permute-start(f32[1,128]{1,0:T(1,128)S(1)} %get-tuple-element.97), channel_id=1, source_target_pairs={{0,8},{8,0},{16,24},{24,16},{1,9},{9,1},{17,25},{25,17},{2,10},{10... | collective-permute-start | bytes 1544 | tf_op jit(solution)/shard_map/ppermute | solution.py:333
  69.8 1.5 %collective-permute-start.13 = (f32[1,128]{1,0:T(1,128)S(1)}, f32[1,128]{1,0:T(1,128)S(1)}, u32[]{:S(2)}, u32[]{:S(2)}) collective-permute-start(f32[1,128]{1,0:T(1,128)S(1)} %get-tuple-element.98), channel_id=1, source_target_pairs={{0,16},{8,24},{16,0},{24,8},{1,17},{9,25},{17,1},{25,9},{2,18},{10... | collective-permute-start | bytes 1544 | tf_op jit(solution)/shard_map/ppermute | solution.py:333
  71.8 2.4 %collective-permute-start.14 = (f32[1,128]{1,0:T(1,128)S(1)}, f32[1,128]{1,0:T(1,128)S(1)}, u32[]{:S(2)}, u32[]{:S(2)}) collective-permute-start(f32[1,128]{1,0:T(1,128)S(1)} %get-tuple-element.99), channel_id=1, source_target_pairs={{0,24},{8,16},{16,8},{24,0},{1,25},{9,17},{17,9},{25,1},{2,26},{10... | collective-permute-start | bytes 1544 | tf_op jit(solution)/shard_map/ppermute | solution.py:333
  74.3 5.7 %shard_map.117 = (bf16[256,2048]{1,0:T(8,128)(2,1)}, f32[256,1024]{1,0:T(8,128)S(1)}, f32[256,1024]{1,0:T(8,128)S(1)}, f32[1,128]{1,0:T(1,128)S(1)}) custom-call(s32[3]{0:T(128)S(1)} %pad_add_fusion.position.core, bf16[256,2048]{1,0:T(8,128)(2,1)S(1)} %get-tuple-element.49.q, ...), custom_call_target="tpu_custom_call", output_to_operand_aliasing={{0}: (12, {})} | custom-call | flops 1 | bytes 1 | tf_op jit(solution)/shard_map/pallas_call | solution.py:398
  80.0 4.2 %collective-permute-done.11 = f32[544,128]{1,0:T(8,128)S(1)} collective-permute-done((f32[544,128]{1,0:T(8,128)S(1)}, f32[544,128]{1,0:T(8,128)S(1)}, u32[]{:S(2)}, u32[]{:S(2)}) %collective-permute-start.11) | collective-permute-done | bytes 278560 | tf_op jit(solution)/shard_map/ppermute | solution.py:293
  86.5 3.0 %shard_map.118 = (bf16[256,2048]{1,0:T(8,128)(2,1)}, bf16[256,2048]{1,0:T(8,128)(2,1)}, f32[1,128]{1,0:T(1,128)}) custom-call(s32[3]{0:T(128)S(1)} %pad_add_fusion.position.core, bf16[256,2048]{1,0:T(8,128)(2,1)S(1)} %get-tuple-element.45.k, bf16[256,2048]{1,0:T(8,128)(2,1)S(1)} %get-tuple-element.46.v, f32[256,1024]{1,0:T(8,128)S(1)} %get-tuple-element.79.gk_in, ...), custom_call_target="tpu_custom_call" | custom-call | flops 1 | bytes 1 | tf_op jit(solution)/shard_map/pallas_call | solution.py:398
  89.5 3.0 %shard_map.119 = (bf16[256,2048]{1,0:T(8,128)(2,1)}, bf16[256,2048]{1,0:T(8,128)(2,1)}, f32[1,128]{1,0:T(1,128)}) custom-call(s32[3]{0:T(128)S(1)} %pad_add_fusion.position.core, bf16[256,2048]{1,0:T(8,128)(2,1)S(1)} %get-tuple-element.45.k, bf16[256,2048]{1,0:T(8,128)(2,1)S(1)} %get-tuple-element.46.v, ...), custom_call_target="tpu_custom_call", output_to_operand_aliasing={{0}: (9, {}), {1}: (10, {})} | custom-call | flops 1 | bytes 1 | tf_op jit(solution)/shard_map/pallas_call | solution.py:398
  (63 shorter events, 10.1 us)
Async XLA Ops:
  0.6 3.6 %copy-start = (s32[1,256]{1,0:T(1,128)S(1)}, s32[1,256]{1,0:T(1,128)}, u32[]{:S(2)}) copy-start(s32[1,256]{1,0:T(1,128)} %seg.13) | copy-start | bytes 3076
  0.6 3.6 %copy-start.2 = (s32[1,32]{1,0:T(1,128)S(1)}, s32[1,32]{1,0:T(1,128)}, u32[]{:S(2)}) copy-start(s32[1,32]{1,0:T(1,128)} %table.13) | copy-start | bytes 388
  3.7 1.7 %collective-permute-start = (f32[544,128]{1,0:T(8,128)S(1)}, f32[544,128]{1,0:T(8,128)S(1)}, u32[]{:S(2)}, u32[]{:S(2)}) collective-permute-start(f32[544,128]{1,0:T(8,128)S(1)} %get-tuple-element.48), channel_id=1, source_target_pairs={{0,1},{1,0},{2,3},{3,2},{4,5},{5,4},{6,7},{7,6},{8,9},{9,8},{10,11... | collective-permute-start | bytes 835592 | tf_op jit(solution)/shard_map/ppermute | solution.py:288
  5.4 11.2 %collective-permute-start.1 = (f32[544,128]{1,0:T(8,128)S(1)}, f32[544,128]{1,0:T(8,128)S(1)}, u32[]{:S(2)}, u32[]{:S(2)}) collective-permute-start(f32[544,128]{1,0:T(8,128)S(1)} %add.163.rest_0_), channel_id=1, source_target_pairs={{0,2},{1,3},{2,4},{3,5},{4,6},{5,7},{8,10},{9,11},{10,12},{11,13},... | collective-permute-start | bytes 835592 | tf_op jit(solution)/shard_map/ppermute | solution.py:293
  16.8 12.7 %collective-permute-start.3 = (f32[2,264,128]{2,1,0:T(8,128)S(1)}, f32[2,264,128]{2,1,0:T(8,128)S(1)}, u32[]{:S(2)}, u32[]{:S(2)}) collective-permute-start(f32[2,264,128]{2,1,0:T(8,128)S(1)} %get-tuple-element.119), channel_id=1, source_target_pairs={{1,0},{2,1},{3,2},{4,3},{5,4},{6,5},{7,6},{9,8},{10,9},{11,10},{12... | collective-permute-start | bytes 811016 | tf_op jit(solution)/shard_map/ppermute | solution.py:293
  18.1 11.4 %collective-permute-start.4 = (f32[2,264,128]{2,1,0:T(8,128)S(1)}, f32[2,264,128]{2,1,0:T(8,128)S(1)}, u32[]{:S(2)}, u32[]{:S(2)}) collective-permute-start(f32[2,264,128]{2,1,0:T(8,128)S(1)} %get-tuple-element.120), channel_id=1, source_target_pairs={{1,0},{2,1},{3,2},{4,3},{5,4},{6,5},{7,6},{9,8},{10,9},{11,10},{12... | collective-permute-start | bytes 811016 | tf_op jit(solution)/shard_map/ppermute | solution.py:293
  19.4 13.1 %collective-permute-start.2 = (f32[544,128]{1,0:T(8,128)S(1)}, f32[544,128]{1,0:T(8,128)S(1)}, u32[]{:S(2)}, u32[]{:S(2)}) collective-permute-start(f32[544,128]{1,0:T(8,128)S(1)} %add_add_fusion.3.rest_0_), channel_id=1, source_target_pairs={{0,4},{1,5},{2,6},{3,7},{8,12},{9,13},{10,14},{11,15},{16,20},{17,... | collective-permute-start | bytes 835592 | tf_op jit(solution)/shard_map/ppermute | solution.py:293
  26.4 6.2 %copy-start.1 = (f32[2048]{0:T(1024)S(1)}, f32[2048]{0:T(1024)}, u32[]{:S(2)}) copy-start(f32[2048]{0:T(1024)} %param.13) | copy-start | bytes 24580
  32.6 3.2 %collective-permute-start.5 = (f32[544,128]{1,0:T(8,128)S(1)}, f32[544,128]{1,0:T(8,128)S(1)}, u32[]{:S(2)}, u32[]{:S(2)}) collective-permute-start(f32[544,128]{1,0:T(8,128)S(1)} %get-tuple-element.92), channel_id=1, source_target_pairs={{0,1},{1,0},{2,3},{3,2},{4,5},{5,4},{6,7},{7,6},{8,9},{9,8},{10,11... | collective-permute-start | bytes 835592 | tf_op jit(solution)/shard_map/ppermute | solution.py:288
  38.7 1.6 %collective-permute-start.6 = (f32[544,128]{1,0:T(8,128)S(1)}, f32[544,128]{1,0:T(8,128)S(1)}, u32[]{:S(2)}, u32[]{:S(2)}) collective-permute-start(f32[544,128]{1,0:T(8,128)S(1)} %get-tuple-element.64), channel_id=1, source_target_pairs={{0,1},{1,0},{2,3},{3,2},{4,5},{5,4},{6,7},{7,6},{8,9},{9,8},{10,11... | collective-permute-start | bytes 835592 | tf_op jit(solution)/shard_map/ppermute | solution.py:288
  40.4 17.9 %collective-permute-start.8 = (f32[4,128]{1,0:T(4,128)S(1)}, f32[4,128]{1,0:T(4,128)S(1)}, u32[]{:S(2)}, u32[]{:S(2)}) collective-permute-start(f32[4,128]{1,0:T(4,128)S(1)} %get-tuple-element.93), channel_id=1, source_target_pairs={{0,2},{1,3},{2,0},{3,1},{4,6},{5,7},{6,4},{7,5},{8,10},{9,11},{10,... | collective-permute-start | bytes 6152 | tf_op jit(solution)/shard_map/ppermute | solution.py:333
  47.9 10.5 %collective-permute-start.10 = (f32[4,128]{1,0:T(4,128)S(1)}, f32[4,128]{1,0:T(4,128)S(1)}, u32[]{:S(2)}, u32[]{:S(2)}) collective-permute-start(f32[4,128]{1,0:T(4,128)S(1)} %get-tuple-element.94), channel_id=1, source_target_pairs={{0,6},{1,7},{2,4},{3,5},{4,2},{5,3},{6,0},{7,1},{8,14},{9,15},{10,... | collective-permute-start | bytes 6152 | tf_op jit(solution)/shard_map/ppermute | solution.py:333
  50.8 7.6 %collective-permute-start.9 = (f32[4,128]{1,0:T(4,128)S(1)}, f32[4,128]{1,0:T(4,128)S(1)}, u32[]{:S(2)}, u32[]{:S(2)}) collective-permute-start(f32[4,128]{1,0:T(4,128)S(1)} %select_select_fusion.1), channel_id=1, source_target_pairs={{0,4},{1,5},{2,6},{3,7},{4,0},{5,1},{6,2},{7,3},{8,12},{9,13},{10,... | collective-permute-start | bytes 6152 | tf_op jit(solution)/shard_map/ppermute | solution.py:333
  51.4 10.2 %collective-permute-start.7 = (f32[544,128]{1,0:T(8,128)S(1)}, f32[544,128]{1,0:T(8,128)S(1)}, u32[]{:S(2)}, u32[]{:S(2)}) collective-permute-start(f32[544,128]{1,0:T(8,128)S(1)} %add.181.rest_0_), channel_id=1, source_target_pairs={{2,0},{3,1},{4,2},{5,3},{6,4},{7,5},{10,8},{11,9},{12,10},{13,11},... | collective-permute-start | bytes 835592 | tf_op jit(solution)/shard_map/ppermute | solution.py:293
  61.7 18.3 %collective-permute-start.15 = (f32[2,264,128]{2,1,0:T(8,128)S(1)}, f32[2,264,128]{2,1,0:T(8,128)S(1)}, u32[]{:S(2)}, u32[]{:S(2)}) collective-permute-start(f32[2,264,128]{2,1,0:T(8,128)S(1)} %get-tuple-element.115), channel_id=1, source_target_pairs={{0,1},{1,2},{2,3},{3,4},{4,5},{5,6},{6,7},{8,9},{9,10},{10,11},{11... | collective-permute-start | bytes 811016 | tf_op jit(solution)/shard_map/ppermute | solution.py:293
  63.0 16.9 %collective-permute-start.16 = (f32[2,264,128]{2,1,0:T(8,128)S(1)}, f32[2,264,128]{2,1,0:T(8,128)S(1)}, u32[]{:S(2)}, u32[]{:S(2)}) collective-permute-start(f32[2,264,128]{2,1,0:T(8,128)S(1)} %get-tuple-element.116), channel_id=1, source_target_pairs={{0,1},{1,2},{2,3},{3,4},{4,5},{5,6},{6,7},{8,9},{9,10},{10,11},{11... | collective-permute-start | bytes 811016 | tf_op jit(solution)/shard_map/ppermute | solution.py:293
  66.9 17.3 %collective-permute-start.11 = (f32[544,128]{1,0:T(8,128)S(1)}, f32[544,128]{1,0:T(8,128)S(1)}, u32[]{:S(2)}, u32[]{:S(2)}) collective-permute-start(f32[544,128]{1,0:T(8,128)S(1)} %add_add_fusion.2.rest_0_), channel_id=1, source_target_pairs={{4,0},{5,1},{6,2},{7,3},{12,8},{13,9},{14,10},{15,11},{20,16},{21,... | collective-permute-start | bytes 835592 | tf_op jit(solution)/shard_map/ppermute | solution.py:293
  68.2 3.6 %collective-permute-start.12 = (f32[1,128]{1,0:T(1,128)S(1)}, f32[1,128]{1,0:T(1,128)S(1)}, u32[]{:S(2)}, u32[]{:S(2)}) collective-permute-start(f32[1,128]{1,0:T(1,128)S(1)} %get-tuple-element.97), channel_id=1, source_target_pairs={{0,8},{8,0},{16,24},{24,16},{1,9},{9,1},{17,25},{25,17},{2,10},{10... | collective-permute-start | bytes 1544 | tf_op jit(solution)/shard_map/ppermute | solution.py:333
  69.8 10.2 %collective-permute-start.13 = (f32[1,128]{1,0:T(1,128)S(1)}, f32[1,128]{1,0:T(1,128)S(1)}, u32[]{:S(2)}, u32[]{:S(2)}) collective-permute-start(f32[1,128]{1,0:T(1,128)S(1)} %get-tuple-element.98), channel_id=1, source_target_pairs={{0,16},{8,24},{16,0},{24,8},{1,17},{9,25},{17,1},{25,9},{2,18},{10... | collective-permute-start | bytes 1544 | tf_op jit(solution)/shard_map/ppermute | solution.py:333
  71.8 8.2 %collective-permute-start.14 = (f32[1,128]{1,0:T(1,128)S(1)}, f32[1,128]{1,0:T(1,128)S(1)}, u32[]{:S(2)}, u32[]{:S(2)}) collective-permute-start(f32[1,128]{1,0:T(1,128)S(1)} %get-tuple-element.99), channel_id=1, source_target_pairs={{0,24},{8,16},{16,8},{24,0},{1,25},{9,17},{17,9},{25,1},{2,26},{10... | collective-permute-start | bytes 1544 | tf_op jit(solution)/shard_map/ppermute | solution.py:333
  84.3 5.2 %collective-permute-start.17 = (f32[544,128]{1,0:T(8,128)S(1)}, f32[544,128]{1,0:T(8,128)S(1)}, u32[]{:S(2)}, u32[]{:S(2)}) collective-permute-start(f32[544,128]{1,0:T(8,128)S(1)} %get-tuple-element.90), channel_id=1, source_target_pairs={{0,1},{1,0},{2,3},{3,2},{4,5},{5,4},{6,7},{7,6},{8,9},{9,8},{10,11... | collective-permute-start | bytes 835592 | tf_op jit(solution)/shard_map/ppermute | solution.py:288
  84.5 1.5 %collective-permute-start.18 = (f32[1,64]{1,0:T(1,128)S(1)}, f32[1,64]{1,0:T(1,128)S(1)}, u32[]{:S(2)}, u32[]{:S(2)}) collective-permute-start(f32[1,64]{1,0:T(1,128)S(1)} %slice_select_fusion), channel_id=1, source_target_pairs={{0,1},{1,0},{2,3},{3,2},{4,5},{5,4},{6,7},{7,6},{8,9},{9,8},{10,11... | collective-permute-start | bytes 776 | tf_op jit(solution)/shard_map/ppermute | solution.py:288

commit v11 on v10

--- a/solution.py
+++ b/solution.py
@@ -11,7 +11,6 @@
 PAIR = 2 * E
 GROUPS = 2
 EXTRA = 8
-PAD = 32
 VMEM = 10 * 2**20
 SUB = 2
 F32 = jnp.float32
@@ -104,15 +103,15 @@
     return group, base, base + (group + half) * lanes, base // PAIR * E
 
 
-def states_kernel(position, k_in, v_in, keep, send, zero, k, v, core_row, ctx_row, dp_row, sems):
-    for i, row in enumerate((core_row, ctx_row, dp_row)):
-        row[...] = jnp.full(row.shape, position[i], jnp.int32)
+def states_kernel(core, ctx, dp, k_in, v_in, keep, send, zero, k, v, core_row, ctx_row, dp_row, sems):
+    for row, index in ((core_row, core), (ctx_row, ctx), (dp_row, dp)):
+        row[...] = jnp.full(row.shape, index[0], jnp.int32)
     lanes = k.shape[1] // GROUPS // 2
     count = lanes // PAIR
     copies = []
     for sel in (1, 0):
         for group in range(GROUPS):
-            base = (2 * group + (sel + position[0]) % 2) * lanes
+            base = (2 * group + (sel + core[0]) % 2) * lanes
             at = pl.ds(pl.multiple_of(base, lanes), lanes)
             for i, (array, buf) in enumerate(((k_in, k), (v_in, v))):
                 copies.append(pltpu.make_async_copy(array.at[:, at], buf.at[:, at], sems.at[2 * group + sel, i]))
@@ -120,11 +119,10 @@
         copy.start()
     zero[...] = jnp.zeros_like(zero)
     for sel, out in ((1, send), (0, keep)):
-        out[GROUPS * count * E:] = jnp.zeros((PAD, PAIR), F32)
         for group in range(GROUPS):
             copies.pop(0).wait()
             copies.pop(0).wait()
-            base = (2 * group + (sel + position[0]) % 2) * lanes
+            base = (2 * group + (sel + core[0]) % 2) * lanes
             for p in range(count):
                 at = lanes_at(base, p)
                 row = (group * count + p) * E
@@ -228,7 +226,6 @@
     ]
     states = [state_pair(q[:, at], jnp.concatenate([da, da * last], axis=1)) for at, da in zip(wides, das)]
     part[0, count * E:] = jnp.broadcast_to(own, (EXTRA, PAIR))
-    total[GROUPS * count * E:] = jnp.zeros((PAD, PAIR), F32)
     for p, (at, normed, da) in enumerate(zip(pairs, normeds, das)):
         total[rows_at(row, p)] = states[p][:, :PAIR]
         part[0, p * E:(p + 1) * E] = states[p][:, PAIR:]
@@ -314,24 +311,9 @@
 
 
 def scatter_step(x, at, axis, bit):
-    low, high = jnp.split(x, 2, axis=1)
+    low, high = jnp.split(x, 2, axis=0 if x.shape[0] > 1 else 1)
     upper = (at >> bit & 1 == 1)[:, :low.shape[1]]
     return jnp.where(upper, high, low) + partner(jnp.where(upper, low, high), axis, bit)
-
-
-def scatter_stage(pieces, at, axis, low):
-    def chosen(index):
-        value = pieces[0]
-        for i, piece in enumerate(pieces[1:]):
-            value = jnp.where(index == i + 1, piece, value)
-        return value
-
-    own = at >> low & (len(pieces) - 1)
-    total = chosen(own)
-    for flip in range(1, len(pieces)):
-        route = [(i, i ^ (flip << low)) for i in range(lax.axis_size(axis))]
-        total = total + lax.ppermute(chosen(own ^ flip), axis, route)
-    return total
 
 
 def on_device(queries, keys, values, out_grad, segment_ids, image_flags, gain):
@@ -340,19 +322,21 @@
     table = image_flags[0]
     gain_row = gain.reshape(1, width)
     ctx = lax.axis_index("ctx")
-    core = jnp.stack([ctx & 1, ctx, lax.axis_index("dp")]).astype(jnp.int32)
+    core, ctx, dp = (x.reshape(1).astype(jnp.int32) for x in (ctx & 1, ctx, lax.axis_index("dp")))
     lanes = width // GROUPS // 2
     half_rows = lanes // PAIR * E
     heads = lanes // E
 
-    def call(kernel, sel, ins, outs, after=(), alias=(), scratch=(), sub=1, steps=None):
-        def wide(i, c):
+    def call(kernel, sel, ins, outs, after=(), alias=(), scratch=(), sub=1, steps=None, scalars=None):
+        scalars = scalars or [core]
+
+        def wide(i, c, *_):
             return (0, (i // sub * 2 + (sel + c[0]) % 2) * sub + i % sub)
 
         def whole(*args):
             return (0, 0)
 
-        def part(i, c):
+        def part(i, c, *_):
             return (i // sub, 0, 0)
 
         specs = {
@@ -362,7 +346,7 @@
             "row": pl.BlockSpec((1, lanes // sub), wide),
             "sums": pl.BlockSpec((1, lanes // PAIR, PAIR), part),
             "zero": pl.BlockSpec((1, rows), whole),
-            "all": pl.BlockSpec((GROUPS * half_rows + PAD, PAIR), whole),
+            "all": pl.BlockSpec((GROUPS * half_rows, PAIR), whole),
             "part": pl.BlockSpec((1, half_rows + EXTRA, PAIR), part),
             "parts": pl.BlockSpec((GROUPS, half_rows + EXTRA, PAIR), lambda *args: (0, 0, 0)),
             "seg": pl.BlockSpec((1, rows), whole),
@@ -377,7 +361,7 @@
             "wide": (rows, width),
             "sums": (GROUPS, lanes // PAIR, PAIR),
             "zero": (1, rows),
-            "all": (GROUPS * half_rows + PAD, PAIR),
+            "all": (GROUPS * half_rows, PAIR),
             "part": (GROUPS, half_rows + EXTRA, PAIR),
             "parts": (GROUPS, half_rows + EXTRA, PAIR),
             "token": (1, PAIR),
@@ -388,7 +372,7 @@
         aliases = {}
         for out_at, x in alias:
             if x is not None:
-                aliases[1 + len(operands)] = out_at
+                aliases[len(scalars) + len(operands)] = out_at
                 operands.append(x)
                 kinds.append("any")
         out_shape = [
@@ -398,7 +382,7 @@
         return pl.pallas_call(
             kernel,
             grid_spec=pltpu.PrefetchScalarGridSpec(
-                num_scalar_prefetch=1,
+                num_scalar_prefetch=len(scalars),
                 grid=steps or (GROUPS * sub,),
                 in_specs=[specs[kind] for kind in kinds],
                 out_specs=[specs[kind] for kind, *_ in outs],
@@ -408,7 +392,7 @@
             input_output_aliases=aliases,
             compiler_params=pltpu.CompilerParams(vmem_limit_bytes=VMEM),
             cost_estimate=pl.CostEstimate(flops=1, bytes_accessed=1, transcendentals=0),
-        )(core, *operands)
+        )(*scalars, *operands)
 
     edges = [("seg", segment_ids), ("table", image_flags)]
     chips = lax.axis_size("ctx") // 2
@@ -460,7 +444,7 @@
         states_kernel, 0, [("hbm", k), ("hbm", v)],
         [("all", F32), ("all", F32), ("zero", jnp.int32), ("vmem", BF16, whole), ("vmem", BF16, whole)]
         + [("token", jnp.int32)] * 3,
-        scratch=[pltpu.SemaphoreType.DMA((2 * GROUPS, 2))], steps=(1,))
+        scratch=[pltpu.SemaphoreType.DMA((2 * GROUPS, 2))], steps=(1,), scalars=[core, ctx, dp])
     piece = within_chip(keep, send)
     seg = (segment_ids + zero)[0]
     onehot = seg[:, None] == jnp.arange(table.shape[0], dtype=jnp.int32)[None, :]
@@ -487,7 +471,7 @@
             nxt.append(shifted(part + nought(load[:1]), -1))
         *made, token = local_attn(1, [load])
         local.append(made)
-        return token + nought(nxt[0][0, :1]) + nought(nxt[1][0, :1])
+        return token
 
     before = summed_before(piece[2], 1, [first_work, second_work])
     prefix = to_cores(core_row, before, piece, 1)
@@ -500,19 +484,22 @@
     inners, prv = [], []
 
     def third_work(load):
-        x = (gain_sum[0][0] + nought(load[:1])).reshape(4, 4, PAIR)
-        top = lax.axis_size("ctx").bit_length() - 3
-        gain_sum.append(scatter_stage([x[:, i] for i in range(4)], ctx_row, "ctx", top))
+        top = lax.axis_size("ctx").bit_length() - 2
+        x = (gain_sum[0][0] + nought(load[:1])).reshape(4, 2, 2 * PAIR)
+        x = scatter_step(x.swapaxes(0, 1).reshape(16, PAIR), ctx_row, "ctx", top)
+        gain_sum.append(x)
         inners.append(inner(0, None, [load]))
-        return inners[0][3] + nought(gain_sum[-1][:1])
+        return inners[0][3]
 
     def fourth_work(load):
-        x = gain_sum[-1] + nought(load[:1])
-        gain_sum.append(scatter_stage([x[i:i + 1] for i in range(4)], dp_row, "dp", 0))
         for part in (norms[1][2], norms[0][2]):
             prv.append(shifted(part + nought(load[:1]), 1))
         inners.append(inner(1, inners[0][0], [load]))
-        return inners[1][3] + nought(gain_sum[-1]) + nought(prv[0][0, :1]) + nought(prv[1][0, :1])
+        x = gain_sum[-1] + inners[1][3]
+        for bit in (1, 0):
+            x = scatter_step(x, dp_row, "dp", bit)
+        gain_sum.append(x)
+        return inners[1][3]
 
     before = summed_before(piece[2], -1, [third_work, fourth_work])
     suffix = to_cores(core_row, before, piece, -1)
@@ -520,7 +507,7 @@
     grad_k, grad_v, _ = outer(1, outers[:2], [])
     grad_q = inners[1][0]
     grad_gain = gain_sum[-1]
-    for bit in reversed(range(lax.axis_size("ctx").bit_length() - 3)):
+    for bit in reversed(range(lax.axis_size("ctx").bit_length() - 2)):
         grad_gain = scatter_step(grad_gain, ctx_row, "ctx", bit)
     grad_gain = grad_gain.reshape(-1)
     return output[None], grad_q[None], grad_k[None], grad_v[None], grad_gain

time: 92.9 us -> 93.9 us (1.011)
  local copies, waits for them, and re-layouts: 0.02 us -> 10.1 us
  starting transfers between devices: 40.3 us -> 34.2 us
  Pallas kernels: 35.6 us -> 30.4 us
  other arithmetic: 1.55 us -> 5.83 us
  waiting for transfers between devices: 14.2 us -> 11.6 us
    ppermute x6 -> x0, starting transfers between devices: 16.5 us -> none  [scatter_stage(): total = total + lax.ppermute(chosen(own ^ flip), axis, route)]
    ppermute x5 -> x9, starting transfers between devices: 1.62 us -> 15 us  [partner(): return lax.ppermute(x, axis, route)]
    unnamed x6 -> x54, local copies, waits for them, and re-layouts: 0.01 us -> 8.2 us
    pallas_call x10, Pallas kernels: 35.6 us -> 30.4 us  [call(): pl.pallas_call(kernel, grid_spec=pltpu.PrefetchScalarGridSpec(num_scalar_...]
    ppermute x8, waiting for transfers between devices: 10.4 us -> 6.78 us  [shifted(): lax.ppermute(x, 'ctx', [(i, i + distance) for i in range(count) if 0 <= i...]
    ppermute x8, starting transfers between devices: 22.2 us -> 19.2 us  [shifted(): lax.ppermute(x, 'ctx', [(i, i + distance) for i in range(count) if 0 <= i...]
    ppermute x5 -> x9, waiting for transfers between devices: 3.21 us -> 4.84 us  [partner(): return lax.ppermute(x, axis, route)]
    reshape x0 -> x1, local copies, waits for them, and re-layouts: none -> 1.31 us  [on_device(): gain_sum = [[jnp.stack(sums, axis=1).reshape(-1, PAIR)]]]
  transfers between devices with their start and end apart: 19 -> 17, of which waited for: 7 -> 6; matrix products, arithmetic and copies ran while one was open for 1% -> 7% of each run, Pallas kernels for 29% -> 24%
where the time goes in v11:
time: 93.9 us; the launch traced here: 93.2 us
  starting transfers between devices  34.2 us (36%)
  Pallas kernels  30.4 us (32%)
  waiting for transfers between devices  11.6 us (12%)
  local copies, waits for them, and re-layouts  10.1 us (11%)
  other arithmetic  5.83 us (6%)
  between operations  1.08 us (1%)
    pallas_call x10, Pallas kernels, call(): pl.pallas_call(kernel, grid_spec=pltpu.PrefetchScalarGridSpec(num_scalar_...  30.4 us
    ppermute x8, starting transfers between devices, shifted(): lax.ppermute(x, 'ctx', [(i, i + distance) for i in range(count) if 0 <= i...  19.2 us
    ppermute x9, starting transfers between devices, partner(): return lax.ppermute(x, axis, route)  15 us
    unnamed x54, local copies, waits for them, and re-layouts  8.2 us
    ppermute x8, waiting for transfers between devices, shifted(): lax.ppermute(x, 'ctx', [(i, i + distance) for i in range(count) if 0 <= i...  6.78 us
    ppermute x9, waiting for transfers between devices, partner(): return lax.ppermute(x, axis, route)  4.84 us
  transfers between devices with their start and end apart: 17, of which 6 were waited for; matrix products, arithmetic and copies ran while one was open for 7% of the time, Pallas kernels for 24%

profile of v11, /device:TPU:0, one launch (start us, length us, event | category | flops | bytes accessed | tf_op | source)
XLA Modules:
  0.0 93.2 jit_solution(18287435308611638535)
XLA Ops:
  0.7 2.4 %shard_map.110 = (f32[512,128]{1,0:T(8,128)S(1)}, f32[512,128]{1,0:T(8,128)S(1)}, s32[1,256]{1,0:T(1,128)S(1)}, bf16[256,2048]{1,0:T(8,128)(2,1)S(1)}, bf16[256,...) custom-call(s32[1]{0:T(128)} %bitcast.core, s32[1]{0:T(128)} %bitcast.3.ctx, ...), custom_call_target="tpu_custom_call" | custom-call | flops 1 | bytes 1 | tf_op jit(solution)/shard_map/pallas_call | solution.py:382
  4.8 4.9 %collective-permute-start.1 = (f32[512,128]{1,0:T(8,128)S(1)}, f32[512,128]{1,0:T(8,128)S(1)}, u32[]{:S(2)}, u32[]{:S(2)}) collective-permute-start(f32[512,128]{1,0:T(8,128)S(1)} %add.143.rest_0_), channel_id=1, source_target_pairs={{0,2},{1,3},{2,4},{3,5},{4,6},{5,7},{8,10},{9,11},{10,12},{11,13},... | collective-permute-start | bytes 786440 | tf_op jit(solution)/shard_map/ppermute | solution.py:290
  9.8 2.6 %shard_map.111 = (f32[2,264,128]{2,1,0:T(8,128)S(1)}, f32[2,264,128]{2,1,0:T(8,128)S(1)}, bf16[256,2048]{1,0:T(8,128)(2,1)S(1)}, bf16[256,2048]{1,0:T(8,128)(2,1)S(1)}, f32[1,128]{1,0:T(1,128)}) custom-call(s32[1]{0:T(128)} %bitcast.core, bf16[256,2048]{1,0:T(8,128)(2,1)} %bitcast.62, bf16[256,2048]{1,0:T(8,128)(2,1)} %bitcast.63, ...), custom_call_target="tpu_custom_call" | custom-call | flops 1 | bytes 1 | tf_op jit(solution)/shard_map/pallas_call | solution.py:382
  12.5 2.5 %shard_map.112 = (f32[256,1024]{1,0:T(8,128)S(1)}, bf16[16,256,256]{2,1,0:T(8,128)(2,1)S(1)}, f32[1,128]{1,0:T(1,128)S(1)}) custom-call(s32[1]{0:T(128)} %bitcast.core, bf16[256,2048]{1,0:T(8,128)(2,1)S(1)} %get-tuple-element.49.q, bf16[256,2048]{1,0:T(8,128)(2,1)S(1)} %get-tuple-element.45.k, bf16[256,2048]{1,0:T(8,128)(2,1)S(1)} %get-tuple-element.46.v, ...), custom_call_target="tpu_custom_call" | custom-call | flops 1 | bytes 1 | tf_op jit(solution)/shard_map/pallas_call | solution.py:382
  15.0 1.4 %copy-done.4 = bf16[16,256,256]{2,1,0:T(8,128)(2,1)} copy-done((bf16[16,256,256]{2,1,0:T(8,128)(2,1)}, bf16[16,256,256]{2,1,0:T(8,128)(2,1)S(1)}, u32[]{:S(2)}) %copy-start.4) | copy-done | bytes 2097176
  16.4 4.6 %collective-permute-start.2 = (f32[512,128]{1,0:T(8,128)S(1)}, f32[512,128]{1,0:T(8,128)S(1)}, u32[]{:S(2)}, u32[]{:S(2)}) collective-permute-start(f32[512,128]{1,0:T(8,128)S(1)} %add_add_fusion.3.rest_0_), channel_id=1, source_target_pairs={{0,4},{1,5},{2,6},{3,7},{8,12},{9,13},{10,14},{11,15},{16,20},{17,... | collective-permute-start | bytes 786440 | tf_op jit(solution)/shard_map/ppermute | solution.py:290
  21.0 2.5 %shard_map.113 = (f32[256,1024]{1,0:T(8,128)S(1)}, bf16[16,256,256]{2,1,0:T(8,128)(2,1)S(1)}, f32[1,128]{1,0:T(1,128)S(1)}) custom-call(s32[1]{0:T(128)} %bitcast.core, bf16[256,2048]{1,0:T(8,128)(2,1)S(1)} %get-tuple-element.49.q, bf16[256,2048]{1,0:T(8,128)(2,1)S(1)} %get-tuple-element.45.k, bf16[256,2048]{1,0:T(8,128)(2,1)S(1)} %get-tuple-element.46.v, ...), custom_call_target="tpu_custom_call" | custom-call | flops 1 | bytes 1 | tf_op jit(solution)/shard_map/pallas_call | solution.py:382
  26.6 1.5 %collective-permute-start.3 = (f32[512,128]{1,0:T(8,128)S(1)}, f32[512,128]{1,0:T(8,128)S(1)}, u32[]{:S(2)}, u32[]{:S(2)}) collective-permute-start(f32[512,128]{1,0:T(8,128)S(1)} %get-tuple-element.90), channel_id=1, source_target_pairs={{0,1},{1,0},{2,3},{3,2},{4,5},{5,4},{6,7},{7,6},{8,9},{9,8},{10,11... | collective-permute-start | bytes 786440 | tf_op jit(solution)/shard_map/ppermute | solution.py:285
  29.3 2.5 %shard_map.114 = (bf16[256,2048]{1,0:T(8,128)(2,1)}, bf16[256,1024]{1,0:T(8,128)(2,1)S(1)}, f32[2,264,128]{2,1,0:T(8,128)S(1)}, f32[2,4,128]{2,1,0:T(4,128)S(1)}...) custom-call(s32[1]{0:T(128)} %bitcast.core, bf16[256,2048]{1,0:T(8,128)(2,1)S(1)} %get-tuple-element.49.q, ...), custom_call_target="tpu_custom_call" | custom-call | flops 1 | bytes 1 | tf_op jit(solution)/shard_map/pallas_call | solution.py:382
  32.5 2.7 %shard_map.115 = (bf16[256,2048]{1,0:T(8,128)(2,1)}, bf16[256,1024]{1,0:T(8,128)(2,1)S(1)}, f32[2,264,128]{2,1,0:T(8,128)S(1)}, f32[2,4,128]{2,1,0:T(4,128)S(1)}, f32[512,128]{1,0:T(8,128)}, /*index=5*/f32[1,128]{1,0:T(1,128)}) custom-call(s32[1]{0:T(128)} %bitcast.core, ...), custom_call_target="tpu_custom_call", output_to_operand_aliasing={{0}: (10, {})} | custom-call | flops 1 | bytes 1 | tf_op jit(solution)/shard_map/pallas_call | solution.py:382
  36.8 2.0 %collective-permute-start.6 = (f32[512,128]{1,0:T(8,128)}, f32[512,128]{1,0:T(8,128)}, u32[]{:S(2)}, u32[]{:S(2)}) collective-permute-start(f32[512,128]{1,0:T(8,128)} %get-tuple-element.64), channel_id=1, source_target_pairs={{0,1},{1,0},{2,3},{3,2},{4,5},{5,4},{6,7},{7,6},{8,9},{9,8},{10,11... | collective-permute-start | bytes 786440 | tf_op jit(solution)/shard_map/ppermute | solution.py:285
  39.4 1.3 %reshape.60 = f32[4,2,256]{2,1,0:T(2,128)} reshape(f32[2,2,4,128]{3,2,1,0:T(4,128)} %copy.17) | data formatting | bytes 16384 | tf_op jit(solution)/shard_map/reshape | solution.py:483
  44.4 5.8 %collective-permute-start.12 = (f32[8,128]{1,0:T(8,128)S(1)}, f32[8,128]{1,0:T(8,128)S(1)}, u32[]{:S(2)}, u32[]{:S(2)}) collective-permute-start(f32[8,128]{1,0:T(8,128)S(1)} %broadcast_select_fusion), channel_id=1, source_target_pairs={{0,4},{1,5},{2,6},{3,7},{4,0},{5,1},{6,2},{7,3},{8,12},{9,13},{10,... | collective-permute-start | bytes 12296 | tf_op jit(solution)/shard_map/ppermute | solution.py:285
  51.2 1.6 %copy-done.5 = bf16[16,256,256]{2,1,0:T(8,128)(2,1)S(1)} copy-done((bf16[16,256,256]{2,1,0:T(8,128)(2,1)S(1)}, bf16[16,256,256]{2,1,0:T(8,128)(2,1)}, u32[]{:S(2)}) %copy-start.5) | copy-done | bytes 2097176
  54.8 5.1 %shard_map.116 = (bf16[256,2048]{1,0:T(8,128)(2,1)}, f32[256,1024]{1,0:T(8,128)S(1)}, f32[256,1024]{1,0:T(8,128)S(1)}, f32[1,128]{1,0:T(1,128)S(1)}) custom-call(s32[1]{0:T(128)} %bitcast.core, bf16[256,2048]{1,0:T(8,128)(2,1)S(1)} %get-tuple-element.49.q, bf16[256,2048]{1,0:T(8,128)(2,1)S(1)} %get-tuple-element.45.k, ...), custom_call_target="tpu_custom_call" | custom-call | flops 1 | bytes 1 | tf_op jit(solution)/shard_map/pallas_call | solution.py:382
  60.0 5.2 %shard_map.117 = (bf16[256,2048]{1,0:T(8,128)(2,1)}, f32[256,1024]{1,0:T(8,128)S(1)}, f32[256,1024]{1,0:T(8,128)S(1)}, f32[1,128]{1,0:T(1,128)S(1)}) custom-call(s32[1]{0:T(128)} %bitcast.core, bf16[256,2048]{1,0:T(8,128)(2,1)S(1)} %get-tuple-element.49.q, bf16[256,2048]{1,0:T(8,128)(2,1)S(1)} %get-tuple-element.45.k, ...), custom_call_target="tpu_custom_call", output_to_operand_aliasing={{0}: (12, {})} | custom-call | flops 1 | bytes 1 | tf_op jit(solution)/shard_map/pallas_call | solution.py:382
  65.2 1.6 %collective-permute-start.13 = (f32[4,128]{1,0:T(4,128)S(1)}, f32[4,128]{1,0:T(4,128)S(1)}, u32[]{:S(2)}, u32[]{:S(2)}) collective-permute-start(f32[4,128]{1,0:T(4,128)S(1)} %slice_select_fusion), channel_id=1, source_target_pairs={{0,16},{8,24},{16,0},{24,8},{1,17},{9,25},{17,1},{25,9},{2,18},{10... | collective-permute-start | bytes 6152 | tf_op jit(solution)/shard_map/ppermute | solution.py:285
  66.8 2.1 %collective-permute-done.13 = f32[4,128]{1,0:T(4,128)S(1)} collective-permute-done((f32[4,128]{1,0:T(4,128)S(1)}, f32[4,128]{1,0:T(4,128)S(1)}, u32[]{:S(2)}, u32[]{:S(2)}) %collective-permute-start.13) | collective-permute-done | bytes 2080 | tf_op jit(solution)/shard_map/ppermute | solution.py:285
  68.9 1.6 %collective-permute-start.14 = (f32[2,128]{1,0:T(2,128)S(1)}, f32[2,128]{1,0:T(2,128)S(1)}, u32[]{:S(2)}, u32[]{:S(2)}) collective-permute-start(f32[2,128]{1,0:T(2,128)S(1)} %broadcast_select_fusion.1), channel_id=1, source_target_pairs={{0,8},{8,0},{16,24},{24,16},{1,9},{9,1},{17,25},{25,17},{2,10},{10... | collective-permute-start | bytes 3080 | tf_op jit(solution)/shard_map/ppermute | solution.py:285
  72.6 1.4 %collective-permute-start.15 = (f32[1,128]{1,0:T(1,128)S(1)}, f32[1,128]{1,0:T(1,128)S(1)}, u32[]{:S(2)}, u32[]{:S(2)}) collective-permute-start(f32[1,128]{1,0:T(1,128)S(1)} %compare_select_fusion), channel_id=1, source_target_pairs={{0,2},{1,3},{2,0},{3,1},{4,6},{5,7},{6,4},{7,5},{8,10},{9,11},{10,... | collective-permute-start | bytes 1544 | tf_op jit(solution)/shard_map/ppermute | solution.py:285
  75.3 3.3 %collective-permute-start.10 = (f32[2,264,128]{2,1,0:T(8,128)S(1)}, f32[2,264,128]{2,1,0:T(8,128)S(1)}, u32[]{:S(2)}, u32[]{:S(2)}) collective-permute-start(f32[2,264,128]{2,1,0:T(8,128)S(1)} %get-tuple-element.102), channel_id=1, source_target_pairs={{0,1},{1,2},{2,3},{3,4},{4,5},{5,6},{6,7},{8,9},{9,10},{10,11},{11... | collective-permute-start | bytes 811016 | tf_op jit(solution)/shard_map/ppermute | solution.py:290
  78.7 6.4 %collective-permute-done.8 = f32[512,128]{1,0:T(8,128)S(1)} collective-permute-done((f32[512,128]{1,0:T(8,128)S(1)}, f32[512,128]{1,0:T(8,128)S(1)}, u32[]{:S(2)}, u32[]{:S(2)}) %collective-permute-start.8) | collective-permute-done | bytes 262176 | tf_op jit(solution)/shard_map/ppermute | solution.py:290
  88.3 2.4 %shard_map.118 = (bf16[256,2048]{1,0:T(8,128)(2,1)}, bf16[256,2048]{1,0:T(8,128)(2,1)}, f32[1,128]{1,0:T(1,128)}) custom-call(s32[1]{0:T(128)} %bitcast.core, bf16[256,2048]{1,0:T(8,128)(2,1)S(1)} %get-tuple-element.45.k, bf16[256,2048]{1,0:T(8,128)(2,1)S(1)} %get-tuple-element.46.v, f32[256,1024]{1,0:T(8,128)S(1)} %get-tuple-element.74.gk_in, ...), custom_call_target="tpu_custom_call" | custom-call | flops 1 | bytes 1 | tf_op jit(solution)/shard_map/pallas_call | solution.py:382
  90.8 2.5 %shard_map.119 = (bf16[256,2048]{1,0:T(8,128)(2,1)}, bf16[256,2048]{1,0:T(8,128)(2,1)}, f32[1,128]{1,0:T(1,128)}) custom-call(s32[1]{0:T(128)} %bitcast.core, bf16[256,2048]{1,0:T(8,128)(2,1)S(1)} %get-tuple-element.45.k, bf16[256,2048]{1,0:T(8,128)(2,1)S(1)} %get-tuple-element.46.v, ...), custom_call_target="tpu_custom_call", output_to_operand_aliasing={{0}: (9, {}), {1}: (10, {})} | custom-call | flops 1 | bytes 1 | tf_op jit(solution)/shard_map/pallas_call | solution.py:382
  (110 shorter events, 22.4 us)
Async XLA Ops:
  3.1 1.7 %collective-permute-start = (f32[512,128]{1,0:T(8,128)S(1)}, f32[512,128]{1,0:T(8,128)S(1)}, u32[]{:S(2)}, u32[]{:S(2)}) collective-permute-start(f32[512,128]{1,0:T(8,128)S(1)} %get-tuple-element.48), channel_id=1, source_target_pairs={{0,1},{1,0},{2,3},{3,2},{4,5},{5,4},{6,7},{7,6},{8,9},{9,8},{10,11... | collective-permute-start | bytes 786440 | tf_op jit(solution)/shard_map/ppermute | solution.py:285
  4.8 11.6 %collective-permute-start.1 = (f32[512,128]{1,0:T(8,128)S(1)}, f32[512,128]{1,0:T(8,128)S(1)}, u32[]{:S(2)}, u32[]{:S(2)}) collective-permute-start(f32[512,128]{1,0:T(8,128)S(1)} %add.143.rest_0_), channel_id=1, source_target_pairs={{0,2},{1,3},{2,4},{3,5},{4,6},{5,7},{8,10},{9,11},{10,12},{11,13},... | collective-permute-start | bytes 786440 | tf_op jit(solution)/shard_map/ppermute | solution.py:290
  16.4 10.1 %collective-permute-start.2 = (f32[512,128]{1,0:T(8,128)S(1)}, f32[512,128]{1,0:T(8,128)S(1)}, u32[]{:S(2)}, u32[]{:S(2)}) collective-permute-start(f32[512,128]{1,0:T(8,128)S(1)} %add_add_fusion.3.rest_0_), channel_id=1, source_target_pairs={{0,4},{1,5},{2,6},{3,7},{8,12},{9,13},{10,14},{11,15},{16,20},{17,... | collective-permute-start | bytes 786440 | tf_op jit(solution)/shard_map/ppermute | solution.py:290
  23.4 5.8 %copy-start.2 = (bf16[16,256,256]{2,1,0:T(8,128)(2,1)}, bf16[16,256,256]{2,1,0:T(8,128)(2,1)S(1)}, u32[]{:S(2)}) copy-start(bf16[16,256,256]{2,1,0:T(8,128)(2,1)S(1)} %get-tuple-element.63.probs) | copy-start | bytes 6291460
  23.5 5.7 %collective-permute-start.5 = (f32[2,264,128]{2,1,0:T(8,128)S(1)}, f32[2,264,128]{2,1,0:T(8,128)S(1)}, u32[]{:S(2)}, u32[]{:S(2)}) collective-permute-start(f32[2,264,128]{2,1,0:T(8,128)S(1)} %get-tuple-element.105), channel_id=1, source_target_pairs={{1,0},{2,1},{3,2},{4,3},{5,4},{6,5},{7,6},{9,8},{10,9},{11,10},{12... | collective-permute-start | bytes 811016 | tf_op jit(solution)/shard_map/ppermute | solution.py:290
  24.8 7.7 %collective-permute-start.4 = (f32[2,264,128]{2,1,0:T(8,128)S(1)}, f32[2,264,128]{2,1,0:T(8,128)S(1)}, u32[]{:S(2)}, u32[]{:S(2)}) collective-permute-start(f32[2,264,128]{2,1,0:T(8,128)S(1)} %get-tuple-element.106), channel_id=1, source_target_pairs={{1,0},{2,1},{3,2},{4,3},{5,4},{6,5},{7,6},{9,8},{10,9},{11,10},{12... | collective-permute-start | bytes 811016 | tf_op jit(solution)/shard_map/ppermute | solution.py:290
  26.6 8.7 %copy-start = (f32[512,128]{1,0:T(8,128)}, f32[512,128]{1,0:T(8,128)S(1)}, u32[]{:S(2)}) copy-start(f32[512,128]{1,0:T(8,128)S(1)} %get-tuple-element.89.prefix) | copy-start | bytes 786436
  26.6 5.9 %collective-permute-start.3 = (f32[512,128]{1,0:T(8,128)S(1)}, f32[512,128]{1,0:T(8,128)S(1)}, u32[]{:S(2)}, u32[]{:S(2)}) collective-permute-start(f32[512,128]{1,0:T(8,128)S(1)} %get-tuple-element.90), channel_id=1, source_target_pairs={{0,1},{1,0},{2,3},{3,2},{4,5},{5,4},{6,7},{7,6},{8,9},{9,8},{10,11... | collective-permute-start | bytes 786440 | tf_op jit(solution)/shard_map/ppermute | solution.py:285
  29.3 6.0 %copy-start.8 = (f32[2,264,128]{2,1,0:T(8,128)}, f32[2,264,128]{2,1,0:T(8,128)S(1)}, u32[]{:S(2)}) copy-start(f32[2,264,128]{2,1,0:T(8,128)S(1)} %collective-permute-done.5.nxt) | copy-start | bytes 811012
  36.8 3.9 %collective-permute-start.6 = (f32[512,128]{1,0:T(8,128)}, f32[512,128]{1,0:T(8,128)}, u32[]{:S(2)}, u32[]{:S(2)}) collective-permute-start(f32[512,128]{1,0:T(8,128)} %get-tuple-element.64), channel_id=1, source_target_pairs={{0,1},{1,0},{2,3},{3,2},{4,5},{5,4},{6,7},{7,6},{8,9},{9,8},{10,11... | collective-permute-start | bytes 786440 | tf_op jit(solution)/shard_map/ppermute | solution.py:285
  41.7 18.2 %collective-permute-start.7 = (f32[512,128]{1,0:T(8,128)S(1)}, f32[512,128]{1,0:T(8,128)S(1)}, u32[]{:S(2)}, u32[]{:S(2)}) collective-permute-start(f32[512,128]{1,0:T(8,128)S(1)} %add.159.rest_0_), channel_id=1, source_target_pairs={{2,0},{3,1},{4,2},{5,3},{6,4},{7,5},{10,8},{11,9},{12,10},{13,11},... | collective-permute-start | bytes 786440 | tf_op jit(solution)/shard_map/ppermute | solution.py:290
  44.4 20.8 %collective-permute-start.12 = (f32[8,128]{1,0:T(8,128)S(1)}, f32[8,128]{1,0:T(8,128)S(1)}, u32[]{:S(2)}, u32[]{:S(2)}) collective-permute-start(f32[8,128]{1,0:T(8,128)S(1)} %broadcast_select_fusion), channel_id=1, source_target_pairs={{0,4},{1,5},{2,6},{3,7},{4,0},{5,1},{6,2},{7,3},{8,12},{9,13},{10,... | collective-permute-start | bytes 12296 | tf_op jit(solution)/shard_map/ppermute | solution.py:285
  60.0 8.9 %copy-start.23 = (pred[128]{0:T(512)(128)(4,1)S(1)}, pred[128]{0:T(512)(128)(4,1)}, u32[]{:S(2)}) copy-start(pred[128]{0:T(512)(128)(4,1)} %get-tuple-element.98) | copy-start | bytes 388
  60.0 13.9 %copy-start.17 = (f32[2,264,128]{2,1,0:T(8,128)S(1)}, f32[2,264,128]{2,1,0:T(8,128)}, u32[]{:S(2)}) copy-start(f32[2,264,128]{2,1,0:T(8,128)} %copy-done.16) | copy-start | bytes 811012
  60.0 13.9 %copy-start.19 = (f32[2,264,128]{2,1,0:T(8,128)S(1)}, f32[2,264,128]{2,1,0:T(8,128)}, u32[]{:S(2)}) copy-start(f32[2,264,128]{2,1,0:T(8,128)} %copy-done.18) | copy-start | bytes 811012
  65.2 21.1 %copy-start.25 = (pred[1,128]{1,0:T(4,128)(4,1)S(1)}, pred[1,128]{1,0:T(4,128)(4,1)}, u32[]{:S(2)}) copy-start(pred[1,128]{1,0:T(4,128)(4,1)} %get-tuple-element.100) | copy-start | bytes 388
  65.2 3.7 %collective-permute-start.13 = (f32[4,128]{1,0:T(4,128)S(1)}, f32[4,128]{1,0:T(4,128)S(1)}, u32[]{:S(2)}, u32[]{:S(2)}) collective-permute-start(f32[4,128]{1,0:T(4,128)S(1)} %slice_select_fusion), channel_id=1, source_target_pairs={{0,16},{8,24},{16,0},{24,8},{1,17},{9,25},{17,1},{25,9},{2,18},{10... | collective-permute-start | bytes 6152 | tf_op jit(solution)/shard_map/ppermute | solution.py:285
  68.9 3.6 %collective-permute-start.14 = (f32[2,128]{1,0:T(2,128)S(1)}, f32[2,128]{1,0:T(2,128)S(1)}, u32[]{:S(2)}, u32[]{:S(2)}) collective-permute-start(f32[2,128]{1,0:T(2,128)S(1)} %broadcast_select_fusion.1), channel_id=1, source_target_pairs={{0,8},{8,0},{16,24},{24,16},{1,9},{9,1},{17,25},{25,17},{2,10},{10... | collective-permute-start | bytes 3080 | tf_op jit(solution)/shard_map/ppermute | solution.py:285
  70.5 14.6 %collective-permute-start.8 = (f32[512,128]{1,0:T(8,128)S(1)}, f32[512,128]{1,0:T(8,128)S(1)}, u32[]{:S(2)}, u32[]{:S(2)}) collective-permute-start(f32[512,128]{1,0:T(8,128)S(1)} %add_add_fusion.2.rest_0_), channel_id=1, source_target_pairs={{4,0},{5,1},{6,2},{7,3},{12,8},{13,9},{14,10},{15,11},{20,16},{21,... | collective-permute-start | bytes 786440 | tf_op jit(solution)/shard_map/ppermute | solution.py:290
  72.6 6.1 %collective-permute-start.15 = (f32[1,128]{1,0:T(1,128)S(1)}, f32[1,128]{1,0:T(1,128)S(1)}, u32[]{:S(2)}, u32[]{:S(2)}) collective-permute-start(f32[1,128]{1,0:T(1,128)S(1)} %compare_select_fusion), channel_id=1, source_target_pairs={{0,2},{1,3},{2,0},{3,1},{4,6},{5,7},{6,4},{7,5},{8,10},{9,11},{10,... | collective-permute-start | bytes 1544 | tf_op jit(solution)/shard_map/ppermute | solution.py:285
  74.0 14.4 %collective-permute-start.11 = (f32[2,264,128]{2,1,0:T(8,128)S(1)}, f32[2,264,128]{2,1,0:T(8,128)S(1)}, u32[]{:S(2)}, u32[]{:S(2)}) collective-permute-start(f32[2,264,128]{2,1,0:T(8,128)S(1)} %get-tuple-element.101), channel_id=1, source_target_pairs={{0,1},{1,2},{2,3},{3,4},{4,5},{5,6},{6,7},{8,9},{9,10},{10,11},{11... | collective-permute-start | bytes 811016 | tf_op jit(solution)/shard_map/ppermute | solution.py:290
  75.3 15.5 %collective-permute-start.10 = (f32[2,264,128]{2,1,0:T(8,128)S(1)}, f32[2,264,128]{2,1,0:T(8,128)S(1)}, u32[]{:S(2)}, u32[]{:S(2)}) collective-permute-start(f32[2,264,128]{2,1,0:T(8,128)S(1)} %get-tuple-element.102), channel_id=1, source_target_pairs={{0,1},{1,2},{2,3},{3,4},{4,5},{5,6},{6,7},{8,9},{9,10},{10,11},{11... | collective-permute-start | bytes 811016 | tf_op jit(solution)/shard_map/ppermute | solution.py:290
  86.2 4.6 %collective-permute-start.9 = (f32[512,128]{1,0:T(8,128)S(1)}, f32[512,128]{1,0:T(8,128)S(1)}, u32[]{:S(2)}, u32[]{:S(2)}) collective-permute-start(f32[512,128]{1,0:T(8,128)S(1)} %get-tuple-element.88), channel_id=1, source_target_pairs={{0,1},{1,0},{2,3},{3,2},{4,5},{5,4},{6,7},{7,6},{8,9},{9,8},{10,11... | collective-permute-start | bytes 786440 | tf_op jit(solution)/shard_map/ppermute | solution.py:285
  86.3 1.4 %collective-permute-start.16 = (f32[1,64]{1,0:T(1,128)S(1)}, f32[1,64]{1,0:T(1,128)S(1)}, u32[]{:S(2)}, u32[]{:S(2)}) collective-permute-start(f32[1,64]{1,0:T(1,128)S(1)} %slice_select_fusion.1), channel_id=1, source_target_pairs={{0,1},{1,0},{2,3},{3,2},{4,5},{5,4},{6,7},{7,6},{8,9},{9,8},{10,11... | collective-permute-start | bytes 776 | tf_op jit(solution)/shard_map/ppermute | solution.py:285
  (20 other events, 59.4 us)

commit v12 on v11

--- a/solution.py
+++ b/solution.py
@@ -312,7 +312,7 @@
 
 def scatter_step(x, at, axis, bit):
     low, high = jnp.split(x, 2, axis=0 if x.shape[0] > 1 else 1)
-    upper = (at >> bit & 1 == 1)[:, :low.shape[1]]
+    upper = (at >> bit & 1 == 1)[:, :low.shape[-1]]
     return jnp.where(upper, high, low) + partner(jnp.where(upper, low, high), axis, bit)
 
 
@@ -479,37 +479,33 @@
     norms.append(norm(1, norms[0][0], [norms[0][4]]))
     output = norms[1][0]
     piece = within_chip(norms[0][4], norms[1][4])
-    sums = [jnp.where(core_row == sel, norms[0][3], norms[1][3]) for sel in range(2)]
-    gain_sum = [[jnp.stack(sums, axis=1).reshape(-1, PAIR)]]
+    gain_sum = [jnp.concatenate([jnp.where(core_row == half, norms[0][3], norms[1][3]) for half in range(2)], axis=0)]
+    gain_sum.append(scatter_step(gain_sum[-1], dp_row, "dp", 0))
+    bits = list(reversed(range(lax.axis_size("ctx").bit_length() - 1)))
     inners, prv = [], []
 
     def third_work(load):
-        top = lax.axis_size("ctx").bit_length() - 2
-        x = (gain_sum[0][0] + nought(load[:1])).reshape(4, 2, 2 * PAIR)
-        x = scatter_step(x.swapaxes(0, 1).reshape(16, PAIR), ctx_row, "ctx", top)
-        gain_sum.append(x)
+        x = scatter_step(gain_sum[-1] + nought(load[:1]), dp_row, "dp", 1)
+        gain_sum.append(x.reshape(-1, PAIR))
         inners.append(inner(0, None, [load]))
         return inners[0][3]
 
     def fourth_work(load):
+        gain_sum.append(scatter_step(gain_sum[-1] + nought(load[:1]), ctx_row, "ctx", bits[0]))
         for part in (norms[1][2], norms[0][2]):
             prv.append(shifted(part + nought(load[:1]), 1))
         inners.append(inner(1, inners[0][0], [load]))
-        x = gain_sum[-1] + inners[1][3]
-        for bit in (1, 0):
-            x = scatter_step(x, dp_row, "dp", bit)
-        gain_sum.append(x)
         return inners[1][3]
 
     before = summed_before(piece[2], -1, [third_work, fourth_work])
     suffix = to_cores(core_row, before, piece, -1)
     outers = outer(0, [None] * 2, [])
+    grad_gain = gain_sum[-1] + outers[2]
+    for bit in bits[1:]:
+        grad_gain = scatter_step(grad_gain, ctx_row, "ctx", bit)
     grad_k, grad_v, _ = outer(1, outers[:2], [])
+    grad_gain = grad_gain.reshape(-1)
     grad_q = inners[1][0]
-    grad_gain = gain_sum[-1]
-    for bit in reversed(range(lax.axis_size("ctx").bit_length() - 2)):
-        grad_gain = scatter_step(grad_gain, ctx_row, "ctx", bit)
-    grad_gain = grad_gain.reshape(-1)
     return output[None], grad_q[None], grad_k[None], grad_v[None], grad_gain
 
 

time: 93.9 us -> 77.3 us (0.82)
  local copies, waits for them, and re-layouts: 10.1 us -> 0.01 us
  other arithmetic: 5.83 us -> 1.41 us
  waiting for transfers between devices: 11.6 us -> 9.17 us
    unnamed x54 -> x6, local copies, waits for them, and re-layouts: 8.2 us -> 0.01 us
    ppermute x9, waiting for transfers between devices: 4.84 us -> 2.9 us  [partner(): return lax.ppermute(x, axis, route)]
    reshape x1 -> x0, local copies, waits for them, and re-layouts: 1.31 us -> none  [on_device(): gain_sum = [[jnp.stack(sums, axis=1).reshape(-1, PAIR)]]]
    broadcast_in_dim x2 -> x1, other arithmetic: 1.18 us -> 0.01 us  [scatter_step(): jnp.where(upper, high, low)]
    ppermute x9, starting transfers between devices: 15 us -> 16.1 us  [partner(): return lax.ppermute(x, axis, route)]
    ppermute x8, starting transfers between devices: 19.2 us -> 18.1 us  [shifted(): lax.ppermute(x, 'ctx', [(i, i + distance) for i in range(count) if 0 <= i...]
    select_n x2, other arithmetic: 1.12 us -> 0.17 us  [to_cores(): mine = jnp.where(is_source, before, before + received)]
    add x2, other arithmetic: 1.02 us -> 0.08 us  [within_chip(): return (keep, received, keep + received)]
  transfers between devices with their start and end apart: 17 -> 17, of which waited for: 6 -> 6; matrix products, arithmetic and copies ran while one was open for 7% -> 2% of each run, Pallas kernels for 24% -> 30%
where the time goes in v12:
time: 77.3 us; the launch traced here: 75.8 us
  starting transfers between devices  34.2 us (44%)
  Pallas kernels  30.1 us (39%)
  waiting for transfers between devices  9.17 us (12%)
  other arithmetic  1.41 us (2%)
  between operations  0.91 us (1%)
    pallas_call x10, Pallas kernels, call(): pl.pallas_call(kernel, grid_spec=pltpu.PrefetchScalarGridSpec(num_scalar_...  30.1 us
    ppermute x8, starting transfers between devices, shifted(): lax.ppermute(x, 'ctx', [(i, i + distance) for i in range(count) if 0 <= i...  18.1 us
    ppermute x9, starting transfers between devices, partner(): return lax.ppermute(x, axis, route)  16.1 us
    ppermute x8, waiting for transfers between devices, shifted(): lax.ppermute(x, 'ctx', [(i, i + distance) for i in range(count) if 0 <= i...  6.26 us
    ppermute x9, waiting for transfers between devices, partner(): return lax.ppermute(x, axis, route)  2.9 us
  transfers between devices with their start and end apart: 17, of which 6 were waited for; matrix products, arithmetic and copies ran while one was open for 2% of the time, Pallas kernels for 30%

profile of v12, /device:TPU:0, one launch (start us, length us, event | category | flops | bytes accessed | tf_op | source)
XLA Modules:
  0.0 75.8 jit_solution(4432890702516034051)
XLA Ops:
  0.7 2.4 %shard_map.110 = (f32[512,128]{1,0:T(8,128)S(1)}, f32[512,128]{1,0:T(8,128)S(1)}, s32[1,256]{1,0:T(1,128)S(1)}, bf16[256,2048]{1,0:T(8,128)(2,1)S(1)}, bf16[256,...) custom-call(s32[1]{0:T(128)} %bitcast.core, s32[1]{0:T(128)} %bitcast.3.ctx, ...), custom_call_target="tpu_custom_call" | custom-call | flops 1 | bytes 1 | tf_op jit(solution)/shard_map/pallas_call | solution.py:382
  4.8 4.9 %collective-permute-start.1 = (f32[512,128]{1,0:T(8,128)S(1)}, f32[512,128]{1,0:T(8,128)S(1)}, u32[]{:S(2)}, u32[]{:S(2)}) collective-permute-start(f32[512,128]{1,0:T(8,128)S(1)} %add.148.rest_0_), channel_id=1, source_target_pairs={{0,2},{1,3},{2,4},{3,5},{4,6},{5,7},{8,10},{9,11},{10,12},{11,13},... | collective-permute-start | bytes 786440 | tf_op jit(solution)/shard_map/ppermute | solution.py:290
  9.8 2.6 %shard_map.111 = (f32[2,264,128]{2,1,0:T(8,128)S(1)}, f32[2,264,128]{2,1,0:T(8,128)S(1)}, bf16[256,2048]{1,0:T(8,128)(2,1)S(1)}, bf16[256,2048]{1,0:T(8,128)(2,1)S(1)}, f32[1,128]{1,0:T(1,128)}) custom-call(s32[1]{0:T(128)} %bitcast.core, bf16[256,2048]{1,0:T(8,128)(2,1)} %bitcast.55, bf16[256,2048]{1,0:T(8,128)(2,1)} %bitcast.56, ...), custom_call_target="tpu_custom_call" | custom-call | flops 1 | bytes 1 | tf_op jit(solution)/shard_map/pallas_call | solution.py:382
  12.5 2.5 %shard_map.112 = (f32[256,1024]{1,0:T(8,128)S(1)}, bf16[16,256,256]{2,1,0:T(8,128)(2,1)S(1)}, f32[1,128]{1,0:T(1,128)S(1)}) custom-call(s32[1]{0:T(128)} %bitcast.core, bf16[256,2048]{1,0:T(8,128)(2,1)S(1)} %get-tuple-element.50.q, bf16[256,2048]{1,0:T(8,128)(2,1)S(1)} %get-tuple-element.46.k, bf16[256,2048]{1,0:T(8,128)(2,1)S(1)} %get-tuple-element.47.v, ...), custom_call_target="tpu_custom_call" | custom-call | flops 1 | bytes 1 | tf_op jit(solution)/shard_map/pallas_call | solution.py:382
  15.5 5.4 %collective-permute-start.2 = (f32[512,128]{1,0:T(8,128)S(1)}, f32[512,128]{1,0:T(8,128)S(1)}, u32[]{:S(2)}, u32[]{:S(2)}) collective-permute-start(f32[512,128]{1,0:T(8,128)S(1)} %add_add_fusion.3.rest_0_), channel_id=1, source_target_pairs={{0,4},{1,5},{2,6},{3,7},{8,12},{9,13},{10,14},{11,15},{16,20},{17,... | collective-permute-start | bytes 786440 | tf_op jit(solution)/shard_map/ppermute | solution.py:290
  21.0 2.5 %shard_map.113 = (f32[256,1024]{1,0:T(8,128)S(1)}, bf16[16,256,256]{2,1,0:T(8,128)(2,1)S(1)}, f32[1,128]{1,0:T(1,128)S(1)}) custom-call(s32[1]{0:T(128)} %bitcast.core, bf16[256,2048]{1,0:T(8,128)(2,1)S(1)} %get-tuple-element.50.q, bf16[256,2048]{1,0:T(8,128)(2,1)S(1)} %get-tuple-element.46.k, bf16[256,2048]{1,0:T(8,128)(2,1)S(1)} %get-tuple-element.47.v, ...), custom_call_target="tpu_custom_call" | custom-call | flops 1 | bytes 1 | tf_op jit(solution)/shard_map/pallas_call | solution.py:382
  23.5 1.3 %collective-permute-start.5 = (f32[2,264,128]{2,1,0:T(8,128)S(1)}, f32[2,264,128]{2,1,0:T(8,128)S(1)}, u32[]{:S(2)}, u32[]{:S(2)}) collective-permute-start(f32[2,264,128]{2,1,0:T(8,128)S(1)} %get-tuple-element.103), channel_id=1, source_target_pairs={{1,0},{2,1},{3,2},{4,3},{5,4},{6,5},{7,6},{9,8},{10,9},{11,10},{12... | collective-permute-start | bytes 811016 | tf_op jit(solution)/shard_map/ppermute | solution.py:290
  24.8 1.3 %collective-permute-start.4 = (f32[2,264,128]{2,1,0:T(8,128)S(1)}, f32[2,264,128]{2,1,0:T(8,128)S(1)}, u32[]{:S(2)}, u32[]{:S(2)}) collective-permute-start(f32[2,264,128]{2,1,0:T(8,128)S(1)} %get-tuple-element.104), channel_id=1, source_target_pairs={{1,0},{2,1},{3,2},{4,3},{5,4},{6,5},{7,6},{9,8},{10,9},{11,10},{12... | collective-permute-start | bytes 811016 | tf_op jit(solution)/shard_map/ppermute | solution.py:290
  26.2 1.8 %collective-permute-start.3 = (f32[512,128]{1,0:T(8,128)S(1)}, f32[512,128]{1,0:T(8,128)S(1)}, u32[]{:S(2)}, u32[]{:S(2)}) collective-permute-start(f32[512,128]{1,0:T(8,128)S(1)} %get-tuple-element.92), channel_id=1, source_target_pairs={{0,1},{1,0},{2,3},{3,2},{4,5},{5,4},{6,7},{7,6},{8,9},{9,8},{10,11... | collective-permute-start | bytes 786440 | tf_op jit(solution)/shard_map/ppermute | solution.py:285
  28.1 2.5 %shard_map.114 = (bf16[256,2048]{1,0:T(8,128)(2,1)}, bf16[256,1024]{1,0:T(8,128)(2,1)S(1)}, f32[2,264,128]{2,1,0:T(8,128)S(1)}, f32[2,4,128]{2,1,0:T(4,128)S(1)}...) custom-call(s32[1]{0:T(128)} %bitcast.core, bf16[256,2048]{1,0:T(8,128)(2,1)S(1)} %get-tuple-element.50.q, ...), custom_call_target="tpu_custom_call" | custom-call | flops 1 | bytes 1 | tf_op jit(solution)/shard_map/pallas_call | solution.py:382
  30.6 2.4 %shard_map.115 = (bf16[256,2048]{1,0:T(8,128)(2,1)}, bf16[256,1024]{1,0:T(8,128)(2,1)S(1)}, f32[2,264,128]{2,1,0:T(8,128)S(1)}, f32[2,4,128]{2,1,0:T(4,128)S(1)}...) custom-call(s32[1]{0:T(128)} %bitcast.core, ...), custom_call_target="tpu_custom_call", output_to_operand_aliasing={{0}: (10, {})} | custom-call | flops 1 | bytes 1 | tf_op jit(solution)/shard_map/pallas_call | solution.py:382
  33.0 3.5 %collective-permute-start.6 = (f32[512,128]{1,0:T(8,128)S(1)}, f32[512,128]{1,0:T(8,128)S(1)}, u32[]{:S(2)}, u32[]{:S(2)}) collective-permute-start(f32[512,128]{1,0:T(8,128)S(1)} %get-tuple-element.65), channel_id=1, source_target_pairs={{0,1},{1,0},{2,3},{3,2},{4,5},{5,4},{6,7},{7,6},{8,9},{9,8},{10,11... | collective-permute-start | bytes 786440 | tf_op jit(solution)/shard_map/ppermute | solution.py:285
  36.5 1.6 %collective-permute-start.12 = (f32[2,4,128]{2,1,0:T(4,128)S(1)}, f32[2,4,128]{2,1,0:T(4,128)S(1)}, u32[]{:S(2)}, u32[]{:S(2)}) collective-permute-start(f32[2,4,128]{2,1,0:T(4,128)S(1)} %broadcast_select_fusion.2), channel_id=1, source_target_pairs={{0,8},{8,0},{16,24},{24,16},{1,9},{9,1},{17,25},{25,17},{2,10},{10... | collective-permute-start | bytes 12296 | tf_op jit(solution)/shard_map/ppermute | solution.py:285
  40.2 1.6 %collective-permute-start.13 = (f32[1,4,128]{2,1,0:T(4,128)S(1)}, f32[1,4,128]{2,1,0:T(4,128)S(1)}, u32[]{:S(2)}, u32[]{:S(2)}) collective-permute-start(f32[1,4,128]{2,1,0:T(4,128)S(1)} %slice_select_fusion), channel_id=1, source_target_pairs={{0,16},{8,24},{16,0},{24,8},{1,17},{9,25},{17,1},{25,9},{2,18},{10... | collective-permute-start | bytes 6152 | tf_op jit(solution)/shard_map/ppermute | solution.py:285
  41.8 5.1 %shard_map.116 = (bf16[256,2048]{1,0:T(8,128)(2,1)}, f32[256,1024]{1,0:T(8,128)S(1)}, f32[256,1024]{1,0:T(8,128)S(1)}, f32[1,128]{1,0:T(1,128)S(1)}) custom-call(s32[1]{0:T(128)} %bitcast.core, bf16[256,2048]{1,0:T(8,128)(2,1)S(1)} %get-tuple-element.50.q, bf16[256,2048]{1,0:T(8,128)(2,1)S(1)} %get-tuple-element.46.k, ...), custom_call_target="tpu_custom_call" | custom-call | flops 1 | bytes 1 | tf_op jit(solution)/shard_map/pallas_call | solution.py:382
  46.9 1.7 %collective-permute-done.7 = f32[512,128]{1,0:T(8,128)S(1)} collective-permute-done((f32[512,128]{1,0:T(8,128)S(1)}, f32[512,128]{1,0:T(8,128)S(1)}, u32[]{:S(2)}, u32[]{:S(2)}) %collective-permute-start.7) | collective-permute-done | bytes 262176 | tf_op jit(solution)/shard_map/ppermute | solution.py:290
  50.0 1.3 %collective-permute-start.11 = (f32[2,264,128]{2,1,0:T(8,128)S(1)}, f32[2,264,128]{2,1,0:T(8,128)S(1)}, u32[]{:S(2)}, u32[]{:S(2)}) collective-permute-start(f32[2,264,128]{2,1,0:T(8,128)S(1)} %get-tuple-element.99), channel_id=1, source_target_pairs={{0,1},{1,2},{2,3},{3,4},{4,5},{5,6},{6,7},{8,9},{9,10},{10,11},{11... | collective-permute-start | bytes 811016 | tf_op jit(solution)/shard_map/ppermute | solution.py:290
  51.4 4.2 %collective-permute-start.14 = (f32[2,128]{1,0:T(2,128)S(1)}, f32[2,128]{1,0:T(2,128)S(1)}, u32[]{:S(2)}, u32[]{:S(2)}) collective-permute-start(f32[2,128]{1,0:T(2,128)S(1)} %broadcast_select_fusion.3), channel_id=1, source_target_pairs={{0,4},{1,5},{2,6},{3,7},{4,0},{5,1},{6,2},{7,3},{8,12},{9,13},{10,... | collective-permute-start | bytes 3080 | tf_op jit(solution)/shard_map/ppermute | solution.py:285
  55.6 5.1 %shard_map.117 = (bf16[256,2048]{1,0:T(8,128)(2,1)}, f32[256,1024]{1,0:T(8,128)S(1)}, f32[256,1024]{1,0:T(8,128)S(1)}, f32[1,128]{1,0:T(1,128)S(1)}) custom-call(s32[1]{0:T(128)} %bitcast.core, bf16[256,2048]{1,0:T(8,128)(2,1)S(1)} %get-tuple-element.50.q, bf16[256,2048]{1,0:T(8,128)(2,1)S(1)} %get-tuple-element.46.k, ...), custom_call_target="tpu_custom_call", output_to_operand_aliasing={{0}: (12, {})} | custom-call | flops 1 | bytes 1 | tf_op jit(solution)/shard_map/pallas_call | solution.py:382
  60.7 4.0 %collective-permute-done.8 = f32[512,128]{1,0:T(8,128)S(1)} collective-permute-done((f32[512,128]{1,0:T(8,128)S(1)}, f32[512,128]{1,0:T(8,128)S(1)}, u32[]{:S(2)}, u32[]{:S(2)}) %collective-permute-start.8) | collective-permute-done | bytes 262176 | tf_op jit(solution)/shard_map/ppermute | solution.py:290
  64.8 2.5 %shard_map.118 = (bf16[256,2048]{1,0:T(8,128)(2,1)}, bf16[256,2048]{1,0:T(8,128)(2,1)}, f32[1,128]{1,0:T(1,128)S(1)}) custom-call(s32[1]{0:T(128)} %bitcast.core, bf16[256,2048]{1,0:T(8,128)(2,1)S(1)} %get-tuple-element.46.k, bf16[256,2048]{1,0:T(8,128)(2,1)S(1)} %get-tuple-element.47.v, f32[256,1024]{1,0:T(8,128)S(1)} %get-tuple-element.75.gk_in, ...), custom_call_target="tpu_custom_call" | custom-call | flops 1 | bytes 1 | tf_op jit(solution)/shard_map/pallas_call | solution.py:382
  67.4 1.3 %collective-permute-start.10 = (f32[2,264,128]{2,1,0:T(8,128)S(1)}, f32[2,264,128]{2,1,0:T(8,128)S(1)}, u32[]{:S(2)}, u32[]{:S(2)}) collective-permute-start(f32[2,264,128]{2,1,0:T(8,128)S(1)} %get-tuple-element.100), channel_id=1, source_target_pairs={{0,1},{1,2},{2,3},{3,4},{4,5},{5,6},{6,7},{8,9},{9,10},{10,11},{11... | collective-permute-start | bytes 811016 | tf_op jit(solution)/shard_map/ppermute | solution.py:290
  68.7 2.8 %collective-permute-start.9 = (f32[512,128]{1,0:T(8,128)S(1)}, f32[512,128]{1,0:T(8,128)S(1)}, u32[]{:S(2)}, u32[]{:S(2)}) collective-permute-start(f32[512,128]{1,0:T(8,128)S(1)} %get-tuple-element.90), channel_id=1, source_target_pairs={{0,1},{1,0},{2,3},{3,2},{4,5},{5,4},{6,7},{7,6},{8,9},{9,8},{10,11... | collective-permute-start | bytes 786440 | tf_op jit(solution)/shard_map/ppermute | solution.py:285
  73.3 2.5 %shard_map.119 = (bf16[256,2048]{1,0:T(8,128)(2,1)}, bf16[256,2048]{1,0:T(8,128)(2,1)}, f32[1,128]{1,0:T(1,128)}) custom-call(s32[1]{0:T(128)} %bitcast.core, bf16[256,2048]{1,0:T(8,128)(2,1)S(1)} %get-tuple-element.46.k, bf16[256,2048]{1,0:T(8,128)(2,1)S(1)} %get-tuple-element.47.v, ...), custom_call_target="tpu_custom_call", output_to_operand_aliasing={{0}: (9, {}), {1}: (10, {})} | custom-call | flops 1 | bytes 1 | tf_op jit(solution)/shard_map/pallas_call | solution.py:382
  (55 shorter events, 8.1 us)
Async XLA Ops:
  0.6 3.0 %copy-start = (s32[1,256]{1,0:T(1,128)S(1)}, s32[1,256]{1,0:T(1,128)}, u32[]{:S(2)}) copy-start(s32[1,256]{1,0:T(1,128)} %seg.13) | copy-start | bytes 3076
  0.6 2.9 %copy-start.2 = (s32[1,32]{1,0:T(1,128)S(1)}, s32[1,32]{1,0:T(1,128)}, u32[]{:S(2)}) copy-start(s32[1,32]{1,0:T(1,128)} %table.13) | copy-start | bytes 388
  3.1 1.7 %collective-permute-start = (f32[512,128]{1,0:T(8,128)S(1)}, f32[512,128]{1,0:T(8,128)S(1)}, u32[]{:S(2)}, u32[]{:S(2)}) collective-permute-start(f32[512,128]{1,0:T(8,128)S(1)} %get-tuple-element.49), channel_id=1, source_target_pairs={{0,1},{1,0},{2,3},{3,2},{4,5},{5,4},{6,7},{7,6},{8,9},{9,8},{10,11... | collective-permute-start | bytes 786440 | tf_op jit(solution)/shard_map/ppermute | solution.py:285
  4.8 10.7 %collective-permute-start.1 = (f32[512,128]{1,0:T(8,128)S(1)}, f32[512,128]{1,0:T(8,128)S(1)}, u32[]{:S(2)}, u32[]{:S(2)}) collective-permute-start(f32[512,128]{1,0:T(8,128)S(1)} %add.148.rest_0_), channel_id=1, source_target_pairs={{0,2},{1,3},{2,4},{3,5},{4,6},{5,7},{8,10},{9,11},{10,12},{11,13},... | collective-permute-start | bytes 786440 | tf_op jit(solution)/shard_map/ppermute | solution.py:290
  15.5 10.6 %collective-permute-start.2 = (f32[512,128]{1,0:T(8,128)S(1)}, f32[512,128]{1,0:T(8,128)S(1)}, u32[]{:S(2)}, u32[]{:S(2)}) collective-permute-start(f32[512,128]{1,0:T(8,128)S(1)} %add_add_fusion.3.rest_0_), channel_id=1, source_target_pairs={{0,4},{1,5},{2,6},{3,7},{8,12},{9,13},{10,14},{11,15},{16,20},{17,... | collective-permute-start | bytes 786440 | tf_op jit(solution)/shard_map/ppermute | solution.py:290
  23.5 4.6 %copy-start.1 = (f32[2048]{0:T(1024)S(1)}, f32[2048]{0:T(1024)}, u32[]{:S(2)}) copy-start(f32[2048]{0:T(1024)} %param.13) | copy-start | bytes 24580
  23.5 4.5 %collective-permute-start.5 = (f32[2,264,128]{2,1,0:T(8,128)S(1)}, f32[2,264,128]{2,1,0:T(8,128)S(1)}, u32[]{:S(2)}, u32[]{:S(2)}) collective-permute-start(f32[2,264,128]{2,1,0:T(8,128)S(1)} %get-tuple-element.103), channel_id=1, source_target_pairs={{1,0},{2,1},{3,2},{4,3},{5,4},{6,5},{7,6},{9,8},{10,9},{11,10},{12... | collective-permute-start | bytes 811016 | tf_op jit(solution)/shard_map/ppermute | solution.py:290
  24.8 5.8 %collective-permute-start.4 = (f32[2,264,128]{2,1,0:T(8,128)S(1)}, f32[2,264,128]{2,1,0:T(8,128)S(1)}, u32[]{:S(2)}, u32[]{:S(2)}) collective-permute-start(f32[2,264,128]{2,1,0:T(8,128)S(1)} %get-tuple-element.104), channel_id=1, source_target_pairs={{1,0},{2,1},{3,2},{4,3},{5,4},{6,5},{7,6},{9,8},{10,9},{11,10},{12... | collective-permute-start | bytes 811016 | tf_op jit(solution)/shard_map/ppermute | solution.py:290
  26.2 4.4 %collective-permute-start.3 = (f32[512,128]{1,0:T(8,128)S(1)}, f32[512,128]{1,0:T(8,128)S(1)}, u32[]{:S(2)}, u32[]{:S(2)}) collective-permute-start(f32[512,128]{1,0:T(8,128)S(1)} %get-tuple-element.92), channel_id=1, source_target_pairs={{0,1},{1,0},{2,3},{3,2},{4,5},{5,4},{6,7},{7,6},{8,9},{9,8},{10,11... | collective-permute-start | bytes 786440 | tf_op jit(solution)/shard_map/ppermute | solution.py:285
  33.0 5.1 %collective-permute-start.6 = (f32[512,128]{1,0:T(8,128)S(1)}, f32[512,128]{1,0:T(8,128)S(1)}, u32[]{:S(2)}, u32[]{:S(2)}) collective-permute-start(f32[512,128]{1,0:T(8,128)S(1)} %get-tuple-element.65), channel_id=1, source_target_pairs={{0,1},{1,0},{2,3},{3,2},{4,5},{5,4},{6,7},{7,6},{8,9},{9,8},{10,11... | collective-permute-start | bytes 786440 | tf_op jit(solution)/shard_map/ppermute | solution.py:285
  36.5 3.7 %collective-permute-start.12 = (f32[2,4,128]{2,1,0:T(4,128)S(1)}, f32[2,4,128]{2,1,0:T(4,128)S(1)}, u32[]{:S(2)}, u32[]{:S(2)}) collective-permute-start(f32[2,4,128]{2,1,0:T(4,128)S(1)} %broadcast_select_fusion.2), channel_id=1, source_target_pairs={{0,8},{8,0},{16,24},{24,16},{1,9},{9,1},{17,25},{25,17},{2,10},{10... | collective-permute-start | bytes 12296 | tf_op jit(solution)/shard_map/ppermute | solution.py:285
  38.2 10.4 %collective-permute-start.7 = (f32[512,128]{1,0:T(8,128)S(1)}, f32[512,128]{1,0:T(8,128)S(1)}, u32[]{:S(2)}, u32[]{:S(2)}) collective-permute-start(f32[512,128]{1,0:T(8,128)S(1)} %add.164.rest_0_), channel_id=1, source_target_pairs={{2,0},{3,1},{4,2},{5,3},{6,4},{7,5},{10,8},{11,9},{12,10},{13,11},... | collective-permute-start | bytes 786440 | tf_op jit(solution)/shard_map/ppermute | solution.py:290
  40.2 11.1 %collective-permute-start.13 = (f32[1,4,128]{2,1,0:T(4,128)S(1)}, f32[1,4,128]{2,1,0:T(4,128)S(1)}, u32[]{:S(2)}, u32[]{:S(2)}) collective-permute-start(f32[1,4,128]{2,1,0:T(4,128)S(1)} %slice_select_fusion), channel_id=1, source_target_pairs={{0,16},{8,24},{16,0},{24,8},{1,17},{9,25},{17,1},{25,9},{2,18},{10... | collective-permute-start | bytes 6152 | tf_op jit(solution)/shard_map/ppermute | solution.py:285
  48.7 16.1 %collective-permute-start.8 = (f32[512,128]{1,0:T(8,128)S(1)}, f32[512,128]{1,0:T(8,128)S(1)}, u32[]{:S(2)}, u32[]{:S(2)}) collective-permute-start(f32[512,128]{1,0:T(8,128)S(1)} %add_add_fusion.2.rest_0_), channel_id=1, source_target_pairs={{4,0},{5,1},{6,2},{7,3},{12,8},{13,9},{14,10},{15,11},{20,16},{21,... | collective-permute-start | bytes 786440 | tf_op jit(solution)/shard_map/ppermute | solution.py:290
  50.0 14.8 %collective-permute-start.11 = (f32[2,264,128]{2,1,0:T(8,128)S(1)}, f32[2,264,128]{2,1,0:T(8,128)S(1)}, u32[]{:S(2)}, u32[]{:S(2)}) collective-permute-start(f32[2,264,128]{2,1,0:T(8,128)S(1)} %get-tuple-element.99), channel_id=1, source_target_pairs={{0,1},{1,2},{2,3},{3,4},{4,5},{5,6},{6,7},{8,9},{9,10},{10,11},{11... | collective-permute-start | bytes 811016 | tf_op jit(solution)/shard_map/ppermute | solution.py:290
  51.4 15.9 %collective-permute-start.14 = (f32[2,128]{1,0:T(2,128)S(1)}, f32[2,128]{1,0:T(2,128)S(1)}, u32[]{:S(2)}, u32[]{:S(2)}) collective-permute-start(f32[2,128]{1,0:T(2,128)S(1)} %broadcast_select_fusion.3), channel_id=1, source_target_pairs={{0,4},{1,5},{2,6},{3,7},{4,0},{5,1},{6,2},{7,3},{8,12},{9,13},{10,... | collective-permute-start | bytes 3080 | tf_op jit(solution)/shard_map/ppermute | solution.py:285
  67.3 4.2 %collective-permute-start.15 = (f32[1,128]{1,0:T(1,128)S(1)}, f32[1,128]{1,0:T(1,128)S(1)}, u32[]{:S(2)}, u32[]{:S(2)}) collective-permute-start(f32[1,128]{1,0:T(1,128)S(1)} %compare_select_fusion), channel_id=1, source_target_pairs={{0,2},{1,3},{2,0},{3,1},{4,6},{5,7},{6,4},{7,5},{8,10},{9,11},{10,... | collective-permute-start | bytes 1544 | tf_op jit(solution)/shard_map/ppermute | solution.py:285
  67.4 5.9 %collective-permute-start.10 = (f32[2,264,128]{2,1,0:T(8,128)S(1)}, f32[2,264,128]{2,1,0:T(8,128)S(1)}, u32[]{:S(2)}, u32[]{:S(2)}) collective-permute-start(f32[2,264,128]{2,1,0:T(8,128)S(1)} %get-tuple-element.100), channel_id=1, source_target_pairs={{0,1},{1,2},{2,3},{3,4},{4,5},{5,6},{6,7},{8,9},{9,10},{10,11},{11... | collective-permute-start | bytes 811016 | tf_op jit(solution)/shard_map/ppermute | solution.py:290
  68.7 4.6 %collective-permute-start.9 = (f32[512,128]{1,0:T(8,128)S(1)}, f32[512,128]{1,0:T(8,128)S(1)}, u32[]{:S(2)}, u32[]{:S(2)}) collective-permute-start(f32[512,128]{1,0:T(8,128)S(1)} %get-tuple-element.90), channel_id=1, source_target_pairs={{0,1},{1,0},{2,3},{3,2},{4,5},{5,4},{6,7},{7,6},{8,9},{9,8},{10,11... | collective-permute-start | bytes 786440 | tf_op jit(solution)/shard_map/ppermute | solution.py:285
  71.6 1.1 %collective-permute-start.16 = (f32[1,64]{1,0:T(1,128)S(1)}, f32[1,64]{1,0:T(1,128)S(1)}, u32[]{:S(2)}, u32[]{:S(2)}) collective-permute-start(f32[1,64]{1,0:T(1,128)S(1)} %slice_select_fusion.1), channel_id=1, source_target_pairs={{0,1},{1,0},{2,3},{3,2},{4,5},{5,4},{6,7},{7,6},{8,9},{9,8},{10,11... | collective-permute-start | bytes 776 | tf_op jit(solution)/shard_map/ppermute | solution.py:285

commit v13 on v12

--- a/solution.py
+++ b/solution.py
@@ -348,6 +348,7 @@
             "zero": pl.BlockSpec((1, rows), whole),
             "all": pl.BlockSpec((GROUPS * half_rows, PAIR), whole),
             "part": pl.BlockSpec((1, half_rows + EXTRA, PAIR), part),
+            "later": pl.BlockSpec((1, half_rows + EXTRA, PAIR), lambda i, *_: (GROUPS + i // sub, 0, 0)),
             "parts": pl.BlockSpec((GROUPS, half_rows + EXTRA, PAIR), lambda *args: (0, 0, 0)),
             "seg": pl.BlockSpec((1, rows), whole),
             "table": pl.BlockSpec((1, table.shape[0]), whole),
@@ -424,7 +425,7 @@
         return call(
             functools.partial(outer_kernel, sel), sel,
             [("vmem", k), ("vmem", v), ("vmem", inners[sel][1]), ("vmem", inners[sel][2]), *edges,
-             ("all", suffix[sel]), ("part", prv[sel])],
+             ("all", suffix[sel]), ("later" if sel else "part", prv[0])],
             [("wide", BF16), ("wide", BF16), ("token", F32)], after=after, alias=list(enumerate(before)), sub=SUB)
 
     def summed_before(own, towards, works):
@@ -492,16 +493,17 @@
 
     def fourth_work(load):
         gain_sum.append(scatter_step(gain_sum[-1] + nought(load[:1]), ctx_row, "ctx", bits[0]))
-        for part in (norms[1][2], norms[0][2]):
-            prv.append(shifted(part + nought(load[:1]), 1))
+        both = jnp.concatenate([norms[1][2], norms[0][2]], axis=0) + nought(load[:1])
+        prv.append(shifted(both, 1))
         inners.append(inner(1, inners[0][0], [load]))
         return inners[1][3]
 
     before = summed_before(piece[2], -1, [third_work, fourth_work])
     suffix = to_cores(core_row, before, piece, -1)
+    grad_gain = scatter_step(gain_sum[-1] + nought(before[:1]), ctx_row, "ctx", bits[1])
     outers = outer(0, [None] * 2, [])
-    grad_gain = gain_sum[-1] + outers[2]
-    for bit in bits[1:]:
+    grad_gain = grad_gain + outers[2]
+    for bit in bits[2:]:
         grad_gain = scatter_step(grad_gain, ctx_row, "ctx", bit)
     grad_k, grad_v, _ = outer(1, outers[:2], [])
     grad_gain = grad_gain.reshape(-1)

time: 77.3 us -> 71.9 us (0.930); the launches traced: 75.8 us -> 71.6 us
  starting transfers between devices: 34.2 us -> 29.6 us
    ppermute x9, starting transfers between devices: 16.1 us -> 12.8 us  [partner(): return lax.ppermute(x, axis, route)]
    ppermute x8 -> x7, starting transfers between devices: 18.1 us -> 16.8 us  [shifted(): lax.ppermute(x, 'ctx', [(i, i + distance) for i in range(count) if 0 <= i...]
    ppermute x8 -> x7, waiting for transfers between devices: 6.26 us -> 6.77 us  [shifted(): lax.ppermute(x, 'ctx', [(i, i + distance) for i in range(count) if 0 <= i...]
  transfers between devices with their start and end apart: 17 -> 16, of which waited for: 6 -> 6; matrix products, arithmetic and copies ran while one was open for 2% -> 1% of each run, Pallas kernels for 30% -> 35%
where the time goes in v13:
time: 71.9 us; the launch traced here: 71.6 us
  Pallas kernels  30.1 us (42%)
  starting transfers between devices  29.6 us (41%)
  waiting for transfers between devices  9.52 us (13%)
  other arithmetic  1.43 us (2%)
  between operations  0.95 us (1%)
    pallas_call x10, Pallas kernels, call(): pl.pallas_call(kernel, grid_spec=pltpu.PrefetchScalarGridSpec(num_scalar_...  30.1 us
    ppermute x7, starting transfers between devices, shifted(): lax.ppermute(x, 'ctx', [(i, i + distance) for i in range(count) if 0 <= i...  16.8 us
    ppermute x9, starting transfers between devices, partner(): return lax.ppermute(x, axis, route)  12.8 us
    ppermute x7, waiting for transfers between devices, shifted(): lax.ppermute(x, 'ctx', [(i, i + distance) for i in range(count) if 0 <= i...  6.77 us
    ppermute x9, waiting for transfers between devices, partner(): return lax.ppermute(x, axis, route)  2.75 us
  transfers between devices with their start and end apart: 16, of which 6 were waited for; matrix products, arithmetic and copies ran while one was open for 1% of the time, Pallas kernels for 35%

profile of v13, /device:TPU:0, one launch (start us, length us, event | category | flops | bytes accessed | tf_op | source)
XLA Modules:
  0.0 71.6 jit_solution(15904736680164162216)
XLA Ops:
  0.7 2.4 %shard_map.110 = (f32[512,128]{1,0:T(8,128)S(1)}, f32[512,128]{1,0:T(8,128)S(1)}, s32[1,256]{1,0:T(1,128)S(1)}, bf16[256,2048]{1,0:T(8,128)(2,1)S(1)}, bf16[256,...) custom-call(s32[1]{0:T(128)} %bitcast.core, s32[1]{0:T(128)} %bitcast.3.ctx, ...), custom_call_target="tpu_custom_call" | custom-call | flops 1 | bytes 1 | tf_op jit(solution)/shard_map/pallas_call | solution.py:383
  4.8 4.9 %collective-permute-start.1 = (f32[512,128]{1,0:T(8,128)S(1)}, f32[512,128]{1,0:T(8,128)S(1)}, u32[]{:S(2)}, u32[]{:S(2)}) collective-permute-start(f32[512,128]{1,0:T(8,128)S(1)} %add.145.rest_0_), channel_id=1, source_target_pairs={{0,2},{1,3},{2,4},{3,5},{4,6},{5,7},{8,10},{9,11},{10,12},{11,13},... | collective-permute-start | bytes 786440 | tf_op jit(solution)/shard_map/ppermute | solution.py:290
  9.8 2.6 %shard_map.111 = (f32[2,264,128]{2,1,0:T(8,128)S(1)}, f32[2,264,128]{2,1,0:T(8,128)S(1)}, bf16[256,2048]{1,0:T(8,128)(2,1)S(1)}, bf16[256,2048]{1,0:T(8,128)(2,1)S(1)}, f32[1,128]{1,0:T(1,128)}) custom-call(s32[1]{0:T(128)} %bitcast.core, bf16[256,2048]{1,0:T(8,128)(2,1)} %bitcast.53, bf16[256,2048]{1,0:T(8,128)(2,1)} %bitcast.54, ...), custom_call_target="tpu_custom_call" | custom-call | flops 1 | bytes 1 | tf_op jit(solution)/shard_map/pallas_call | solution.py:383
  12.5 2.5 %shard_map.112 = (f32[256,1024]{1,0:T(8,128)S(1)}, bf16[16,256,256]{2,1,0:T(8,128)(2,1)S(1)}, f32[1,128]{1,0:T(1,128)S(1)}) custom-call(s32[1]{0:T(128)} %bitcast.core, bf16[256,2048]{1,0:T(8,128)(2,1)S(1)} %get-tuple-element.50.q, bf16[256,2048]{1,0:T(8,128)(2,1)S(1)} %get-tuple-element.46.k, bf16[256,2048]{1,0:T(8,128)(2,1)S(1)} %get-tuple-element.47.v, ...), custom_call_target="tpu_custom_call" | custom-call | flops 1 | bytes 1 | tf_op jit(solution)/shard_map/pallas_call | solution.py:383
  15.5 5.4 %collective-permute-start.2 = (f32[512,128]{1,0:T(8,128)S(1)}, f32[512,128]{1,0:T(8,128)S(1)}, u32[]{:S(2)}, u32[]{:S(2)}) collective-permute-start(f32[512,128]{1,0:T(8,128)S(1)} %add_add_fusion.3.rest_0_), channel_id=1, source_target_pairs={{0,4},{1,5},{2,6},{3,7},{8,12},{9,13},{10,14},{11,15},{16,20},{17,... | collective-permute-start | bytes 786440 | tf_op jit(solution)/shard_map/ppermute | solution.py:290
  21.0 2.5 %shard_map.113 = (f32[256,1024]{1,0:T(8,128)S(1)}, bf16[16,256,256]{2,1,0:T(8,128)(2,1)S(1)}, f32[1,128]{1,0:T(1,128)S(1)}) custom-call(s32[1]{0:T(128)} %bitcast.core, bf16[256,2048]{1,0:T(8,128)(2,1)S(1)} %get-tuple-element.50.q, bf16[256,2048]{1,0:T(8,128)(2,1)S(1)} %get-tuple-element.46.k, bf16[256,2048]{1,0:T(8,128)(2,1)S(1)} %get-tuple-element.47.v, ...), custom_call_target="tpu_custom_call" | custom-call | flops 1 | bytes 1 | tf_op jit(solution)/shard_map/pallas_call | solution.py:383
  23.5 1.3 %collective-permute-start.5 = (f32[2,264,128]{2,1,0:T(8,128)S(1)}, f32[2,264,128]{2,1,0:T(8,128)S(1)}, u32[]{:S(2)}, u32[]{:S(2)}) collective-permute-start(f32[2,264,128]{2,1,0:T(8,128)S(1)} %get-tuple-element.101), channel_id=1, source_target_pairs={{1,0},{2,1},{3,2},{4,3},{5,4},{6,5},{7,6},{9,8},{10,9},{11,10},{12... | collective-permute-start | bytes 811016 | tf_op jit(solution)/shard_map/ppermute | solution.py:290
  24.8 1.3 %collective-permute-start.4 = (f32[2,264,128]{2,1,0:T(8,128)S(1)}, f32[2,264,128]{2,1,0:T(8,128)S(1)}, u32[]{:S(2)}, u32[]{:S(2)}) collective-permute-start(f32[2,264,128]{2,1,0:T(8,128)S(1)} %get-tuple-element.102), channel_id=1, source_target_pairs={{1,0},{2,1},{3,2},{4,3},{5,4},{6,5},{7,6},{9,8},{10,9},{11,10},{12... | collective-permute-start | bytes 811016 | tf_op jit(solution)/shard_map/ppermute | solution.py:290
  26.2 1.8 %collective-permute-start.3 = (f32[512,128]{1,0:T(8,128)S(1)}, f32[512,128]{1,0:T(8,128)S(1)}, u32[]{:S(2)}, u32[]{:S(2)}) collective-permute-start(f32[512,128]{1,0:T(8,128)S(1)} %get-tuple-element.92), channel_id=1, source_target_pairs={{0,1},{1,0},{2,3},{3,2},{4,5},{5,4},{6,7},{7,6},{8,9},{9,8},{10,11... | collective-permute-start | bytes 786440 | tf_op jit(solution)/shard_map/ppermute | solution.py:285
  28.1 2.5 %shard_map.114 = (bf16[256,2048]{1,0:T(8,128)(2,1)}, bf16[256,1024]{1,0:T(8,128)(2,1)S(1)}, f32[2,264,128]{2,1,0:T(8,128)S(1)}, f32[2,4,128]{2,1,0:T(4,128)S(1)}...) custom-call(s32[1]{0:T(128)} %bitcast.core, bf16[256,2048]{1,0:T(8,128)(2,1)S(1)} %get-tuple-element.50.q, ...), custom_call_target="tpu_custom_call" | custom-call | flops 1 | bytes 1 | tf_op jit(solution)/shard_map/pallas_call | solution.py:383
  30.6 2.4 %shard_map.115 = (bf16[256,2048]{1,0:T(8,128)(2,1)}, bf16[256,1024]{1,0:T(8,128)(2,1)S(1)}, f32[2,264,128]{2,1,0:T(8,128)S(1)}, f32[2,4,128]{2,1,0:T(4,128)S(1)}...) custom-call(s32[1]{0:T(128)} %bitcast.core, ...), custom_call_target="tpu_custom_call", output_to_operand_aliasing={{0}: (10, {})} | custom-call | flops 1 | bytes 1 | tf_op jit(solution)/shard_map/pallas_call | solution.py:383
  33.0 3.5 %collective-permute-start.6 = (f32[512,128]{1,0:T(8,128)S(1)}, f32[512,128]{1,0:T(8,128)S(1)}, u32[]{:S(2)}, u32[]{:S(2)}) collective-permute-start(f32[512,128]{1,0:T(8,128)S(1)} %get-tuple-element.65), channel_id=1, source_target_pairs={{0,1},{1,0},{2,3},{3,2},{4,5},{5,4},{6,7},{7,6},{8,9},{9,8},{10,11... | collective-permute-start | bytes 786440 | tf_op jit(solution)/shard_map/ppermute | solution.py:285
  36.6 1.6 %collective-permute-start.11 = (f32[2,4,128]{2,1,0:T(4,128)S(1)}, f32[2,4,128]{2,1,0:T(4,128)S(1)}, u32[]{:S(2)}, u32[]{:S(2)}) collective-permute-start(f32[2,4,128]{2,1,0:T(4,128)S(1)} %broadcast_select_fusion.2), channel_id=1, source_target_pairs={{0,8},{8,0},{16,24},{24,16},{1,9},{9,1},{17,25},{25,17},{2,10},{10... | collective-permute-start | bytes 12296 | tf_op jit(solution)/shard_map/ppermute | solution.py:285
  38.2 1.3 %collective-permute-start.7 = (f32[512,128]{1,0:T(8,128)S(1)}, f32[512,128]{1,0:T(8,128)S(1)}, u32[]{:S(2)}, u32[]{:S(2)}) collective-permute-start(f32[512,128]{1,0:T(8,128)S(1)} %add.161.rest_0_), channel_id=1, source_target_pairs={{2,0},{3,1},{4,2},{5,3},{6,4},{7,5},{10,8},{11,9},{12,10},{13,11},... | collective-permute-start | bytes 786440 | tf_op jit(solution)/shard_map/ppermute | solution.py:290
  40.3 1.6 %collective-permute-start.12 = (f32[1,4,128]{2,1,0:T(4,128)S(1)}, f32[1,4,128]{2,1,0:T(4,128)S(1)}, u32[]{:S(2)}, u32[]{:S(2)}) collective-permute-start(f32[1,4,128]{2,1,0:T(4,128)S(1)} %slice_select_fusion), channel_id=1, source_target_pairs={{0,16},{8,24},{16,0},{24,8},{1,17},{9,25},{17,1},{25,9},{2,18},{10... | collective-permute-start | bytes 6152 | tf_op jit(solution)/shard_map/ppermute | solution.py:285
  41.8 5.1 %shard_map.116 = (bf16[256,2048]{1,0:T(8,128)(2,1)}, f32[256,1024]{1,0:T(8,128)S(1)}, f32[256,1024]{1,0:T(8,128)S(1)}, f32[1,128]{1,0:T(1,128)S(1)}) custom-call(s32[1]{0:T(128)} %bitcast.core, bf16[256,2048]{1,0:T(8,128)(2,1)S(1)} %get-tuple-element.50.q, bf16[256,2048]{1,0:T(8,128)(2,1)S(1)} %get-tuple-element.46.k, ...), custom_call_target="tpu_custom_call" | custom-call | flops 1 | bytes 1 | tf_op jit(solution)/shard_map/pallas_call | solution.py:383
  46.9 1.7 %collective-permute-done.7 = f32[512,128]{1,0:T(8,128)S(1)} collective-permute-done((f32[512,128]{1,0:T(8,128)S(1)}, f32[512,128]{1,0:T(8,128)S(1)}, u32[]{:S(2)}, u32[]{:S(2)}) %collective-permute-start.7) | collective-permute-done | bytes 262176 | tf_op jit(solution)/shard_map/ppermute | solution.py:290
  48.6 1.3 %collective-permute-start.8 = (f32[512,128]{1,0:T(8,128)S(1)}, f32[512,128]{1,0:T(8,128)S(1)}, u32[]{:S(2)}, u32[]{:S(2)}) collective-permute-start(f32[512,128]{1,0:T(8,128)S(1)} %add_add_fusion.2.rest_0_), channel_id=1, source_target_pairs={{4,0},{5,1},{6,2},{7,3},{12,8},{13,9},{14,10},{15,11},{20,16},{21,... | collective-permute-start | bytes 786440 | tf_op jit(solution)/shard_map/ppermute | solution.py:290
  50.0 3.6 %collective-permute-start.13 = (f32[2,128]{1,0:T(2,128)S(1)}, f32[2,128]{1,0:T(2,128)S(1)}, u32[]{:S(2)}, u32[]{:S(2)}) collective-permute-start(f32[2,128]{1,0:T(2,128)S(1)} %broadcast_select_fusion.3), channel_id=1, source_target_pairs={{0,4},{1,5},{2,6},{3,7},{4,0},{5,1},{6,2},{7,3},{8,12},{9,13},{10,... | collective-permute-start | bytes 3080 | tf_op jit(solution)/shard_map/ppermute | solution.py:285
  53.6 1.3 %collective-permute-start.10 = (f32[4,264,128]{2,1,0:T(8,128)S(1)}, f32[4,264,128]{2,1,0:T(8,128)S(1)}, u32[]{:S(2)}, u32[]{:S(2)}) collective-permute-start(f32[4,264,128]{2,1,0:T(8,128)S(1)} %maximum_add_fusion), channel_id=1, source_target_pairs={{0,1},{1,2},{2,3},{3,4},{4,5},{5,6},{6,7},{8,9},{9,10},{10,11},{11... | collective-permute-start | bytes 1622024 | tf_op jit(solution)/shard_map/ppermute | solution.py:290
  55.0 5.2 %shard_map.117 = (bf16[256,2048]{1,0:T(8,128)(2,1)}, f32[256,1024]{1,0:T(8,128)S(1)}, f32[256,1024]{1,0:T(8,128)S(1)}, f32[1,128]{1,0:T(1,128)S(1)}) custom-call(s32[1]{0:T(128)} %bitcast.core, bf16[256,2048]{1,0:T(8,128)(2,1)S(1)} %get-tuple-element.50.q, bf16[256,2048]{1,0:T(8,128)(2,1)S(1)} %get-tuple-element.46.k, ...), custom_call_target="tpu_custom_call", output_to_operand_aliasing={{0}: (12, {})} | custom-call | flops 1 | bytes 1 | tf_op jit(solution)/shard_map/pallas_call | solution.py:383
  60.1 4.6 %collective-permute-done.8 = f32[512,128]{1,0:T(8,128)S(1)} collective-permute-done((f32[512,128]{1,0:T(8,128)S(1)}, f32[512,128]{1,0:T(8,128)S(1)}, u32[]{:S(2)}, u32[]{:S(2)}) %collective-permute-start.8) | collective-permute-done | bytes 262176 | tf_op jit(solution)/shard_map/ppermute | solution.py:290
  65.0 2.5 %shard_map.118 = (bf16[256,2048]{1,0:T(8,128)(2,1)}, bf16[256,2048]{1,0:T(8,128)(2,1)}, f32[1,128]{1,0:T(1,128)S(1)}) custom-call(s32[1]{0:T(128)} %bitcast.core, bf16[256,2048]{1,0:T(8,128)(2,1)S(1)} %get-tuple-element.46.k, bf16[256,2048]{1,0:T(8,128)(2,1)S(1)} %get-tuple-element.47.v, f32[256,1024]{1,0:T(8,128)S(1)} %get-tuple-element.76.gk_in, ...), custom_call_target="tpu_custom_call" | custom-call | flops 1 | bytes 1 | tf_op jit(solution)/shard_map/pallas_call | solution.py:383
  68.5 2.5 %shard_map.119 = (bf16[256,2048]{1,0:T(8,128)(2,1)}, bf16[256,2048]{1,0:T(8,128)(2,1)}, f32[1,128]{1,0:T(1,128)}) custom-call(s32[1]{0:T(128)} %bitcast.core, bf16[256,2048]{1,0:T(8,128)(2,1)S(1)} %get-tuple-element.46.k, bf16[256,2048]{1,0:T(8,128)(2,1)S(1)} %get-tuple-element.47.v, ...), custom_call_target="tpu_custom_call", output_to_operand_aliasing={{0}: (9, {}), {1}: (10, {})} | custom-call | flops 1 | bytes 1 | tf_op jit(solution)/shard_map/pallas_call | solution.py:383
  (55 shorter events, 5.4 us)
Async XLA Ops:
  0.6 3.0 %copy-start = (s32[1,256]{1,0:T(1,128)S(1)}, s32[1,256]{1,0:T(1,128)}, u32[]{:S(2)}) copy-start(s32[1,256]{1,0:T(1,128)} %seg.13) | copy-start | bytes 3076
  0.6 2.9 %copy-start.2 = (s32[1,32]{1,0:T(1,128)S(1)}, s32[1,32]{1,0:T(1,128)}, u32[]{:S(2)}) copy-start(s32[1,32]{1,0:T(1,128)} %table.13) | copy-start | bytes 388
  3.1 1.7 %collective-permute-start = (f32[512,128]{1,0:T(8,128)S(1)}, f32[512,128]{1,0:T(8,128)S(1)}, u32[]{:S(2)}, u32[]{:S(2)}) collective-permute-start(f32[512,128]{1,0:T(8,128)S(1)} %get-tuple-element.49), channel_id=1, source_target_pairs={{0,1},{1,0},{2,3},{3,2},{4,5},{5,4},{6,7},{7,6},{8,9},{9,8},{10,11... | collective-permute-start | bytes 786440 | tf_op jit(solution)/shard_map/ppermute | solution.py:285
  4.8 10.7 %collective-permute-start.1 = (f32[512,128]{1,0:T(8,128)S(1)}, f32[512,128]{1,0:T(8,128)S(1)}, u32[]{:S(2)}, u32[]{:S(2)}) collective-permute-start(f32[512,128]{1,0:T(8,128)S(1)} %add.145.rest_0_), channel_id=1, source_target_pairs={{0,2},{1,3},{2,4},{3,5},{4,6},{5,7},{8,10},{9,11},{10,12},{11,13},... | collective-permute-start | bytes 786440 | tf_op jit(solution)/shard_map/ppermute | solution.py:290
  15.5 10.6 %collective-permute-start.2 = (f32[512,128]{1,0:T(8,128)S(1)}, f32[512,128]{1,0:T(8,128)S(1)}, u32[]{:S(2)}, u32[]{:S(2)}) collective-permute-start(f32[512,128]{1,0:T(8,128)S(1)} %add_add_fusion.3.rest_0_), channel_id=1, source_target_pairs={{0,4},{1,5},{2,6},{3,7},{8,12},{9,13},{10,14},{11,15},{16,20},{17,... | collective-permute-start | bytes 786440 | tf_op jit(solution)/shard_map/ppermute | solution.py:290
  23.4 4.6 %copy-start.1 = (f32[2048]{0:T(1024)S(1)}, f32[2048]{0:T(1024)}, u32[]{:S(2)}) copy-start(f32[2048]{0:T(1024)} %param.13) | copy-start | bytes 24580
  23.5 4.5 %collective-permute-start.5 = (f32[2,264,128]{2,1,0:T(8,128)S(1)}, f32[2,264,128]{2,1,0:T(8,128)S(1)}, u32[]{:S(2)}, u32[]{:S(2)}) collective-permute-start(f32[2,264,128]{2,1,0:T(8,128)S(1)} %get-tuple-element.101), channel_id=1, source_target_pairs={{1,0},{2,1},{3,2},{4,3},{5,4},{6,5},{7,6},{9,8},{10,9},{11,10},{12... | collective-permute-start | bytes 811016 | tf_op jit(solution)/shard_map/ppermute | solution.py:290
  24.8 5.8 %collective-permute-start.4 = (f32[2,264,128]{2,1,0:T(8,128)S(1)}, f32[2,264,128]{2,1,0:T(8,128)S(1)}, u32[]{:S(2)}, u32[]{:S(2)}) collective-permute-start(f32[2,264,128]{2,1,0:T(8,128)S(1)} %get-tuple-element.102), channel_id=1, source_target_pairs={{1,0},{2,1},{3,2},{4,3},{5,4},{6,5},{7,6},{9,8},{10,9},{11,10},{12... | collective-permute-start | bytes 811016 | tf_op jit(solution)/shard_map/ppermute | solution.py:290
  26.2 4.4 %collective-permute-start.3 = (f32[512,128]{1,0:T(8,128)S(1)}, f32[512,128]{1,0:T(8,128)S(1)}, u32[]{:S(2)}, u32[]{:S(2)}) collective-permute-start(f32[512,128]{1,0:T(8,128)S(1)} %get-tuple-element.92), channel_id=1, source_target_pairs={{0,1},{1,0},{2,3},{3,2},{4,5},{5,4},{6,7},{7,6},{8,9},{9,8},{10,11... | collective-permute-start | bytes 786440 | tf_op jit(solution)/shard_map/ppermute | solution.py:285
  33.0 5.1 %collective-permute-start.6 = (f32[512,128]{1,0:T(8,128)S(1)}, f32[512,128]{1,0:T(8,128)S(1)}, u32[]{:S(2)}, u32[]{:S(2)}) collective-permute-start(f32[512,128]{1,0:T(8,128)S(1)} %get-tuple-element.65), channel_id=1, source_target_pairs={{0,1},{1,0},{2,3},{3,2},{4,5},{5,4},{6,7},{7,6},{8,9},{9,8},{10,11... | collective-permute-start | bytes 786440 | tf_op jit(solution)/shard_map/ppermute | solution.py:285
  36.6 3.7 %collective-permute-start.11 = (f32[2,4,128]{2,1,0:T(4,128)S(1)}, f32[2,4,128]{2,1,0:T(4,128)S(1)}, u32[]{:S(2)}, u32[]{:S(2)}) collective-permute-start(f32[2,4,128]{2,1,0:T(4,128)S(1)} %broadcast_select_fusion.2), channel_id=1, source_target_pairs={{0,8},{8,0},{16,24},{24,16},{1,9},{9,1},{17,25},{25,17},{2,10},{10... | collective-permute-start | bytes 12296 | tf_op jit(solution)/shard_map/ppermute | solution.py:285
  38.2 10.4 %collective-permute-start.7 = (f32[512,128]{1,0:T(8,128)S(1)}, f32[512,128]{1,0:T(8,128)S(1)}, u32[]{:S(2)}, u32[]{:S(2)}) collective-permute-start(f32[512,128]{1,0:T(8,128)S(1)} %add.161.rest_0_), channel_id=1, source_target_pairs={{2,0},{3,1},{4,2},{5,3},{6,4},{7,5},{10,8},{11,9},{12,10},{13,11},... | collective-permute-start | bytes 786440 | tf_op jit(solution)/shard_map/ppermute | solution.py:290
  40.3 9.7 %collective-permute-start.12 = (f32[1,4,128]{2,1,0:T(4,128)S(1)}, f32[1,4,128]{2,1,0:T(4,128)S(1)}, u32[]{:S(2)}, u32[]{:S(2)}) collective-permute-start(f32[1,4,128]{2,1,0:T(4,128)S(1)} %slice_select_fusion), channel_id=1, source_target_pairs={{0,16},{8,24},{16,0},{24,8},{1,17},{9,25},{17,1},{25,9},{2,18},{10... | collective-permute-start | bytes 6152 | tf_op jit(solution)/shard_map/ppermute | solution.py:285
  48.6 16.1 %collective-permute-start.8 = (f32[512,128]{1,0:T(8,128)S(1)}, f32[512,128]{1,0:T(8,128)S(1)}, u32[]{:S(2)}, u32[]{:S(2)}) collective-permute-start(f32[512,128]{1,0:T(8,128)S(1)} %add_add_fusion.2.rest_0_), channel_id=1, source_target_pairs={{4,0},{5,1},{6,2},{7,3},{12,8},{13,9},{14,10},{15,11},{20,16},{21,... | collective-permute-start | bytes 786440 | tf_op jit(solution)/shard_map/ppermute | solution.py:290
  50.0 14.8 %collective-permute-start.13 = (f32[2,128]{1,0:T(2,128)S(1)}, f32[2,128]{1,0:T(2,128)S(1)}, u32[]{:S(2)}, u32[]{:S(2)}) collective-permute-start(f32[2,128]{1,0:T(2,128)S(1)} %broadcast_select_fusion.3), channel_id=1, source_target_pairs={{0,4},{1,5},{2,6},{3,7},{4,0},{5,1},{6,2},{7,3},{8,12},{9,13},{10,... | collective-permute-start | bytes 3080 | tf_op jit(solution)/shard_map/ppermute | solution.py:285
  53.6 11.4 %collective-permute-start.10 = (f32[4,264,128]{2,1,0:T(8,128)S(1)}, f32[4,264,128]{2,1,0:T(8,128)S(1)}, u32[]{:S(2)}, u32[]{:S(2)}) collective-permute-start(f32[4,264,128]{2,1,0:T(8,128)S(1)} %maximum_add_fusion), channel_id=1, source_target_pairs={{0,1},{1,2},{2,3},{3,4},{4,5},{5,6},{6,7},{8,9},{9,10},{10,11},{11... | collective-permute-start | bytes 1622024 | tf_op jit(solution)/shard_map/ppermute | solution.py:290
  64.8 3.6 %collective-permute-start.14 = (f32[1,128]{1,0:T(1,128)S(1)}, f32[1,128]{1,0:T(1,128)S(1)}, u32[]{:S(2)}, u32[]{:S(2)}) collective-permute-start(f32[1,128]{1,0:T(1,128)S(1)} %compare_select_fusion), channel_id=1, source_target_pairs={{0,2},{1,3},{2,0},{3,1},{4,6},{5,7},{6,4},{7,5},{8,10},{9,11},{10,... | collective-permute-start | bytes 1544 | tf_op jit(solution)/shard_map/ppermute | solution.py:285
  65.0 3.6 %collective-permute-start.9 = (f32[512,128]{1,0:T(8,128)S(1)}, f32[512,128]{1,0:T(8,128)S(1)}, u32[]{:S(2)}, u32[]{:S(2)}) collective-permute-start(f32[512,128]{1,0:T(8,128)S(1)} %add_select_fusion.1), channel_id=1, source_target_pairs={{0,1},{1,0},{2,3},{3,2},{4,5},{5,4},{6,7},{7,6},{8,9},{9,8},{10,11... | collective-permute-start | bytes 786440 | tf_op jit(solution)/shard_map/ppermute | solution.py:285
  68.5 2.5 %collective-permute-start.15 = (f32[1,64]{1,0:T(1,128)S(1)}, f32[1,64]{1,0:T(1,128)S(1)}, u32[]{:S(2)}, u32[]{:S(2)}) collective-permute-start(f32[1,64]{1,0:T(1,128)S(1)} %slice_select_fusion.1), channel_id=1, source_target_pairs={{0,1},{1,0},{2,3},{3,2},{4,5},{5,4},{6,7},{7,6},{8,9},{9,8},{10,11... | collective-permute-start | bytes 776 | tf_op jit(solution)/shard_map/ppermute | solution.py:285

commit v14 on v13

--- a/solution.py
+++ b/solution.py
@@ -95,12 +95,16 @@
     return pl.ds(pl.multiple_of(base + p * PAIR, PAIR), PAIR)
 
 
-def place(sel, core, lanes, sub):
+def place(group, core, lanes, sub):
     step = pl.program_id(0)
-    group, part = step // sub, step % sub
+    sel, part = step // sub, step % sub
     half = (sel + core[0]) % 2
-    base = group * lanes + part * (lanes // sub)
-    return group, base, base + (group + half) * lanes, base // PAIR * E
+    inside = part * (lanes // sub)
+    return sel, sel * lanes + inside, (2 * group + half) * lanes + inside, inside // PAIR * E
+
+
+def own_or_received(keep, received, sel, at):
+    return jnp.where(sel == 0, keep[at], received[at])
 
 
 def states_kernel(core, ctx, dp, k_in, v_in, keep, send, zero, k, v, core_row, ctx_row, dp_row, sems):
@@ -130,7 +134,7 @@
 
 
 def part_kernel(core, q_in, dy_in, k, v, seg, table, *rest):
-    *outs, q, dy, token, sems = rest[-6:]
+    *outs, q, dy, token, sems = rest[-4 - GROUPS:]
     copies = [pltpu.make_async_copy(a, b, sems.at[i]) for i, (a, b) in enumerate(((q_in, q), (dy_in, dy)))]
     for copy in copies:
         copy.start()
@@ -139,21 +143,21 @@
     count = lanes // PAIR
     rows, own, _ = edge(seg, table, False)
     keep = rows.astype(BF16)
-    for sel, out in enumerate(outs):
-        for group in range(GROUPS):
+    for group, out in enumerate(outs):
+        for sel in range(2):
             base = (2 * group + (sel + core[0]) % 2) * lanes
             for p in range(count):
                 at = lanes_at(base, p)
-                out[group, p * E:(p + 1) * E] = state_pair(k[:, at], v[:, at] * keep)
-            out[group, count * E:] = jnp.broadcast_to(own, (EXTRA, PAIR))
+                out[sel, p * E:(p + 1) * E] = state_pair(k[:, at], v[:, at] * keep)
+            out[sel, count * E:] = jnp.broadcast_to(own, (EXTRA, PAIR))
     for copy in copies:
         copy.wait()
 
 
-def local_kernel(sel, core, q, k, v, mask, mask_t, *rest):
+def local_kernel(group, core, q, k, v, mask, mask_t, *rest):
     attn, probs, token = rest[-3:]
-    lanes = attn.shape[1] // GROUPS
-    group, base, wide, _ = place(sel, core, lanes, 1)
+    lanes = attn.shape[1] // 2
+    sel, base, wide, _ = place(group, core, lanes, 1)
     m, mt = mask[...], mask_t[...]
     token[...] = jnp.zeros_like(token)
     for p in range(lanes // PAIR):
@@ -162,7 +166,7 @@
         total = None
         for h, (qh, vh) in enumerate(zip(heads_of(q[:, at]), heads_of(v[:, at]))):
             prob = dot(qh, kp, 1, 1).astype(BF16) * m
-            probs[group * (lanes // E) + 2 * p + h] = dot(kp, qh, 1, 1).astype(BF16) * mt
+            probs[sel * (lanes // E) + 2 * p + h] = dot(kp, qh, 1, 1).astype(BF16) * mt
             term = dot(prob, vh, 1, 0)
             total = term if total is None else total + term
         attn[:, lanes_at(base, p)] = total
@@ -198,12 +202,12 @@
     return rows.astype(F32) * met.astype(F32)
 
 
-def norm_kernel(sel, core, q, dy, local, gain, seg, table, prefix, nxt, *rest):
-    out, dab, part, gsum, total, token = rest[-6:]
+def norm_kernel(group, core, q, dy, local, gain, seg, table, mine, theirs, nxt, *rest):
+    out, dab, part, gsum, keep, send, token = rest[-7:]
     token[...] = jnp.zeros_like(token)
     lanes = out.shape[1]
     count = lanes // PAIR
-    _, base, wide, row = place(sel, core, lanes, 1)
+    sel, base, wide, _ = place(group, core, lanes, 1)
     on_next = on_rows(seg, table, True, nxt)
     last, own, flag = edge(seg, table, True)
     last = (last.astype(F32) * jnp.where(flag == 1, 1.0, 0.0)).astype(BF16)
@@ -211,7 +215,7 @@
     bases = [lanes_at(base, p) for p in range(count)]
     wides = [lanes_at(wide, p) for p in range(count)]
     fars = [
-        dot(twice(q[:, at]), side_by_side(prefix[rows_at(row, p)], nxt[0, rows_at(0, p)]), 1, 0)
+        dot(twice(q[:, at]), side_by_side(own_or_received(mine, theirs, sel, rows_at(0, p)), nxt[0, rows_at(0, p)]), 1, 0)
         for p, at in enumerate(wides)
     ]
     attns = [local[:, at] + far[:, :PAIR] + on_next * far[:, PAIR:] for at, far in zip(bases, fars)]
@@ -227,34 +231,42 @@
     states = [state_pair(q[:, at], jnp.concatenate([da, da * last], axis=1)) for at, da in zip(wides, das)]
     part[0, count * E:] = jnp.broadcast_to(own, (EXTRA, PAIR))
     for p, (at, normed, da) in enumerate(zip(pairs, normeds, das)):
-        total[rows_at(row, p)] = states[p][:, :PAIR]
         part[0, p * E:(p + 1) * E] = states[p][:, PAIR:]
         dab[:, bases[p]] = da
         out[:, at] = (normed * gain[:, at]).astype(BF16)
         gsum[0, p:p + 1] = jnp.sum(dy[:, wides[p]].astype(F32) * normed, axis=0, keepdims=True)
 
-
-def inner_kernel(sel, core, q, k, v, dab, probs, mask, seg, table, prefix, nxt, *rest):
+    @pl.when(sel == 0)
+    def _():
+        for p, state in enumerate(states):
+            keep[rows_at(0, p)] = state[:, :PAIR]
+
+    @pl.when(sel == 1)
+    def _():
+        for p, state in enumerate(states):
+            send[rows_at(0, p)] = state[:, :PAIR]
+
+
+def inner_kernel(group, core, q, k, v, dab, probs, mask, seg, table, mine, theirs, nxt, *rest):
     gq, gk, gv, token = rest[-4:]
-    lanes = dab.shape[1] // GROUPS
+    lanes = dab.shape[1] // 2
     count = lanes // SUB // PAIR
-    group, base, wide, row = place(sel, core, lanes, SUB)
+    sel, base, wide, row = place(group, core, lanes, SUB)
     m = mask[...]
     token[...] = jnp.zeros_like(token)
     on_next = on_rows(seg, table, True, nxt)
-    first = row - group * (lanes // 2)
     for p in range(count):
         at = lanes_at(wide, p)
         da = dab[:, lanes_at(base, p)]
         vp = v[:, at]
-        far = dot(twice(da), stacked(prefix[rows_at(row, p)], nxt[0, rows_at(first, p)]), 1, 1)
+        far = dot(twice(da), stacked(own_or_received(mine, theirs, sel, rows_at(row, p)), nxt[0, rows_at(row, p)]), 1, 1)
         tq = far[:, :PAIR] + on_next * far[:, PAIR:]
         tk = tv = None
         for h, (qh, kh, dh) in enumerate(zip(heads_of(q[:, at]), heads_of(k[:, at]), heads_of(da))):
             dprob = dot(dh, vp, 1, 1).astype(BF16) * m
             tq = tq + dot(dprob, kh, 1, 0)
             a = dot(dprob, qh, 0, 0)
-            b = dot(probs[row // (E // 2) + 2 * p + h], dh, 1, 0)
+            b = dot(probs[base // E + 2 * p + h], dh, 1, 0)
             tk = a if tk is None else tk + a
             tv = b if tv is None else tv + b
         gq[:, p * PAIR:(p + 1) * PAIR] = tq.astype(BF16)
@@ -262,18 +274,17 @@
         gv[:, lanes_at(base, p)] = tv
 
 
-def outer_kernel(sel, core, k, v, gk_in, gv_in, seg, table, suffix, prv, *rest):
+def outer_kernel(group, core, k, v, gk_in, gv_in, seg, table, mine, theirs, prv, *rest):
     gk, gv, token = rest[-3:]
-    lanes = gk_in.shape[1] // GROUPS
+    lanes = gk_in.shape[1] // 2
     count = lanes // SUB // PAIR
-    group, base, wide, row = place(sel, core, lanes, SUB)
+    sel, base, wide, row = place(group, core, lanes, SUB)
     token[...] = jnp.zeros_like(token)
     on_prev = on_rows(seg, table, False, prv)
-    first = row - group * (lanes // 2)
     for p in range(count):
         here, own, at = slice(p * PAIR, (p + 1) * PAIR), lanes_at(base, p), lanes_at(wide, p)
-        s = suffix[rows_at(row, p)]
-        g = prv[0, rows_at(first, p)]
+        s = own_or_received(mine, theirs, sel, rows_at(row, p))
+        g = prv[0, rows_at(row, p)]
         far = dot(twice(v[:, at]), stacked(s, g), 1, 1)
         gk[:, here] = (gk_in[:, own] + far[:, :PAIR] + on_prev * far[:, PAIR:]).astype(BF16)
         far = dot(twice(k[:, at]), side_by_side(s, g), 1, 0)
@@ -327,11 +338,11 @@
     half_rows = lanes // PAIR * E
     heads = lanes // E
 
-    def call(kernel, sel, ins, outs, after=(), alias=(), scratch=(), sub=1, steps=None, scalars=None):
+    def call(kernel, group, ins, outs, after=(), alias=(), scratch=(), sub=1, steps=None, scalars=None):
         scalars = scalars or [core]
 
         def wide(i, c, *_):
-            return (0, (i // sub * 2 + (sel + c[0]) % 2) * sub + i % sub)
+            return (0, (2 * group + (i // sub + c[0]) % 2) * sub + i % sub)
 
         def whole(*args):
             return (0, 0)
@@ -348,8 +359,10 @@
             "zero": pl.BlockSpec((1, rows), whole),
             "all": pl.BlockSpec((GROUPS * half_rows, PAIR), whole),
             "part": pl.BlockSpec((1, half_rows + EXTRA, PAIR), part),
-            "later": pl.BlockSpec((1, half_rows + EXTRA, PAIR), lambda i, *_: (GROUPS + i // sub, 0, 0)),
-            "parts": pl.BlockSpec((GROUPS, half_rows + EXTRA, PAIR), lambda *args: (0, 0, 0)),
+            "got": pl.BlockSpec((1, half_rows + EXTRA, PAIR), lambda i, *_: (1 - i // sub, 0, 0)),
+            "got1": pl.BlockSpec((1, half_rows + EXTRA, PAIR), lambda i, *_: (3 - i // sub, 0, 0)),
+            "half": pl.BlockSpec((half_rows, PAIR), whole),
+            "parts": pl.BlockSpec((2, half_rows + EXTRA, PAIR), lambda *args: (0, 0, 0)),
             "seg": pl.BlockSpec((1, rows), whole),
             "table": pl.BlockSpec((1, table.shape[0]), whole),
             "mask": pl.BlockSpec((rows, rows), whole),
@@ -360,11 +373,12 @@
         }
         shapes = {
             "wide": (rows, width),
-            "sums": (GROUPS, lanes // PAIR, PAIR),
+            "sums": (2, lanes // PAIR, PAIR),
+            "half": (half_rows, PAIR),
             "zero": (1, rows),
             "all": (GROUPS * half_rows, PAIR),
-            "part": (GROUPS, half_rows + EXTRA, PAIR),
-            "parts": (GROUPS, half_rows + EXTRA, PAIR),
+            "part": (2, half_rows + EXTRA, PAIR),
+            "parts": (2, half_rows + EXTRA, PAIR),
             "token": (1, PAIR),
         }
         spaces = {"vmem": pltpu.VMEM, "hbm": pltpu.HBM}
@@ -384,7 +398,7 @@
             kernel,
             grid_spec=pltpu.PrefetchScalarGridSpec(
                 num_scalar_prefetch=len(scalars),
-                grid=steps or (GROUPS * sub,),
+                grid=steps or (2 * sub,),
                 in_specs=[specs[kind] for kind in kinds],
                 out_specs=[specs[kind] for kind, *_ in outs],
                 scratch_shapes=scratch,
@@ -397,48 +411,45 @@
 
     edges = [("seg", segment_ids), ("table", image_flags)]
     chips = lax.axis_size("ctx") // 2
-    whole, part_of = (rows, width), (rows, width // 2)
-
-    def local_attn(sel, after):
+    whole, group_of = (rows, width), (rows, 2 * lanes)
+    groups = range(GROUPS)
+
+    def local_attn(g, after):
         return call(
-            functools.partial(local_kernel, sel), sel,
+            functools.partial(local_kernel, g), g,
             [("vmem", q), ("vmem", k), ("vmem", v), ("mask", mask), ("mask", mask_t)],
-            [("vmem", F32, part_of), ("vmem", BF16, (GROUPS * heads, rows, rows)), ("token", F32)], after=after)
-
-    def norm(sel, before, after):
+            [("vmem", F32, group_of), ("vmem", BF16, (2 * heads, rows, rows)), ("token", F32)], after=after)
+
+    def norm(g, before, after):
         return call(
-            functools.partial(norm_kernel, sel), sel,
-            [("vmem", q), ("vmem", dy), ("vmem", local[sel][0]), ("row", gain_row), *edges,
-             ("all", prefix[sel]), ("part", nxt[sel])],
-            [("wide", BF16), ("vmem", BF16, part_of), ("part", F32), ("sums", F32), ("all", F32), ("token", F32)],
+            functools.partial(norm_kernel, g), g,
+            [("vmem", q), ("vmem", dy), ("vmem", local[g][0]), ("row", gain_row), *edges,
+             ("half", prefix[g][0]), ("half", prefix[g][1]), ("got", nxt[g])],
+            [("wide", BF16), ("vmem", BF16, group_of), ("part", F32), ("sums", F32), ("half", F32), ("half", F32),
+             ("token", F32)],
             after=after, alias=[(0, before)])
 
-    def inner(sel, before, after):
+    def inner(g, before, after):
         return call(
-            functools.partial(inner_kernel, sel), sel,
-            [("vmem", q), ("vmem", k), ("vmem", v), ("vmem", norms[sel][1]), ("vmem", local[sel][1]), ("mask", mask),
-             *edges, ("all", prefix[sel]), ("part", nxt[sel])],
-            [("wide", BF16), ("vmem", F32, part_of), ("vmem", F32, part_of), ("token", F32)],
+            functools.partial(inner_kernel, g), g,
+            [("vmem", q), ("vmem", k), ("vmem", v), ("vmem", norms[g][1]), ("vmem", local[g][1]), ("mask", mask),
+             *edges, ("half", prefix[g][0]), ("half", prefix[g][1]), ("got", nxt[g])],
+            [("wide", BF16), ("vmem", F32, group_of), ("vmem", F32, group_of), ("token", F32)],
             after=after, alias=[(0, before)], sub=SUB)
 
-    def outer(sel, before, after):
+    def outer(g, before, after):
         return call(
-            functools.partial(outer_kernel, sel), sel,
-            [("vmem", k), ("vmem", v), ("vmem", inners[sel][1]), ("vmem", inners[sel][2]), *edges,
-             ("all", suffix[sel]), ("later" if sel else "part", prv[0])],
+            functools.partial(outer_kernel, g), g,
+            [("vmem", k), ("vmem", v), ("vmem", inners[g][1]), ("vmem", inners[g][2]), *edges,
+             ("half", suffix[g][0]), ("half", suffix[g][1]), ("got1" if g else "got", prv)],
             [("wide", BF16), ("wide", BF16), ("token", F32)], after=after, alias=list(enumerate(before)), sub=SUB)
 
-    def summed_before(own, towards, works):
-        load, before, span = own, None, 1
+    def hops_after_first(load, before, towards):
+        span = 2
         while span < chips:
             arrived = shifted(load, 2 * towards * span)
-            if works:
-                arrived = arrived + works.pop(0)(load)
-            before = arrived if before is None else before + arrived
-            load = load + arrived
+            load, before = load + arrived, before + arrived
             span *= 2
-        for work in works:
-            before = before + work(load)
         return before
 
     keep, send, zero, k, v, core_row, ctx_row, dp_row = call(
@@ -455,59 +466,57 @@
     mask = ((pos[:, None] >= pos[None, :]) | (imgseg[:, None] == seg[None, :])).astype(BF16)
     mask_t = ((pos[:, None] <= pos[None, :]) | (seg[:, None] == imgseg[None, :])).astype(BF16)
 
+    pieces = [tuple(x[g * half_rows:(g + 1) * half_rows] for x in piece) for g in groups]
     parts = call(
         part_kernel, 0, [("hbm", q), ("hbm", dy), ("vmem", k), ("vmem", v), *edges],
-        [("parts", F32)] * 2 + [("vmem", BF16, whole), ("vmem", BF16, whole), ("token", F32)],
+        [("parts", F32)] * GROUPS + [("vmem", BF16, whole), ("vmem", BF16, whole), ("token", F32)],
         after=[piece[2]], scratch=[pltpu.SemaphoreType.DMA((2,))], steps=(1,))
     *parts, q, dy, _ = parts
-    local, nxt = [], []
-
-    def first_work(load):
-        *made, token = local_attn(0, [parts[0]])
-        local.append(made)
-        return token
-
-    def second_work(load):
-        for part in reversed(parts):
-            nxt.append(shifted(part + nought(load[:1]), -1))
-        *made, token = local_attn(1, [load])
-        local.append(made)
-        return token
-
-    before = summed_before(piece[2], 1, [first_work, second_work])
-    prefix = to_cores(core_row, before, piece, 1)
+
+    local = [local_attn(0, [parts[0]])]
+    first = shifted(piece[2], 2) + local[0][2]
+    load = piece[2] + first
+    arrived, loads = ([x[g * half_rows:(g + 1) * half_rows] for g in groups] for x in (first, load))
+    nxt = [shifted(part + nought(load[:1]), -1) for part in parts]
+    local.append(local_attn(1, [loads[1]]))
+    befores = [hops_after_first(load, first, 1) for load, first in zip(loads, arrived)]
+    befores[0] = befores[0] + local[1][2]
+    prefix = [to_cores(core_row, befores[0], pieces[0], 1)]
     norms = [norm(0, None, [])]
-    norms.append(norm(1, norms[0][0], [norms[0][4]]))
+    late = [within_chip(norms[0][4], norms[0][5])]
+    befores[1] = befores[1] + norms[0][6]
+    prefix.append(to_cores(core_row, befores[1], pieces[1], 1))
+    norms.append(norm(1, norms[0][0], [late[0][2]]))
     output = norms[1][0]
-    piece = within_chip(norms[0][4], norms[1][4])
-    gain_sum = [jnp.concatenate([jnp.where(core_row == half, norms[0][3], norms[1][3]) for half in range(2)], axis=0)]
-    gain_sum.append(scatter_step(gain_sum[-1], dp_row, "dp", 0))
+
+    gain_sum = jnp.concatenate(
+        [jnp.where(core_row == half, n[3][:1], n[3][1:]) for half in range(2) for n in norms], axis=0)
+    gain_sum = scatter_step(gain_sum, dp_row, "dp", 0)
     bits = list(reversed(range(lax.axis_size("ctx").bit_length() - 1)))
-    inners, prv = [], []
-
-    def third_work(load):
-        x = scatter_step(gain_sum[-1] + nought(load[:1]), dp_row, "dp", 1)
-        gain_sum.append(x.reshape(-1, PAIR))
-        inners.append(inner(0, None, [load]))
-        return inners[0][3]
-
-    def fourth_work(load):
-        gain_sum.append(scatter_step(gain_sum[-1] + nought(load[:1]), ctx_row, "ctx", bits[0]))
-        both = jnp.concatenate([norms[1][2], norms[0][2]], axis=0) + nought(load[:1])
-        prv.append(shifted(both, 1))
-        inners.append(inner(1, inners[0][0], [load]))
-        return inners[1][3]
-
-    before = summed_before(piece[2], -1, [third_work, fourth_work])
-    suffix = to_cores(core_row, before, piece, -1)
-    grad_gain = scatter_step(gain_sum[-1] + nought(before[:1]), ctx_row, "ctx", bits[1])
+
+    arrived = [shifted(late[0][2], -2) + norms[1][6]]
+    loads = [late[0][2] + arrived[0]]
+    keep, received, total = within_chip(norms[1][4], norms[1][5])
+    late.append((keep, received, total + nought(loads[0][:1])))
+    gain_sum = scatter_step(gain_sum + nought(late[1][2][:1]), dp_row, "dp", 1).reshape(-1, PAIR)
+    inners = [inner(0, None, [late[1][2], loads[0]])]
+    arrived.append(shifted(late[1][2], -2) + inners[0][3])
+    loads.append(late[1][2] + arrived[1])
+    gain_sum = scatter_step(gain_sum + nought(loads[1][:1]), ctx_row, "ctx", bits[0])
+    prv = shifted(jnp.concatenate([n[2] for n in norms], axis=0) + nought(loads[1][:1]), 1)
+    inners.append(inner(1, inners[0][0], [loads[1]]))
+    grad_q = inners[1][0]
+    befores = [hops_after_first(load, first, -1) for load, first in zip(loads, arrived)]
+    befores[0] = befores[0] + inners[1][3]
+    suffix = [to_cores(core_row, befores[0], late[0], -1)]
+    grad_gain = scatter_step(gain_sum + nought(befores[0][:1]), ctx_row, "ctx", bits[1])
     outers = outer(0, [None] * 2, [])
-    grad_gain = grad_gain + outers[2]
+    befores[1] = befores[1] + outers[2]
+    suffix.append(to_cores(core_row, befores[1], late[1], -1))
     for bit in bits[2:]:
-        grad_gain = scatter_step(grad_gain, ctx_row, "ctx", bit)
+        grad_gain = scatter_step(grad_gain + nought(befores[1][:1])[:, :grad_gain.shape[1]], ctx_row, "ctx", bit)
     grad_k, grad_v, _ = outer(1, outers[:2], [])
     grad_gain = grad_gain.reshape(-1)
-    grad_q = inners[1][0]
     return output[None], grad_q[None], grad_k[None], grad_v[None], grad_gain
 
 

time: 71.9 us -> 80.8 us (1.12)
  starting transfers between devices: 29.6 us -> 38.6 us
  waiting for transfers between devices: 9.52 us -> 8.52 us
    ppermute x9 -> x12, starting transfers between devices: 12.8 us -> 17.9 us  [partner(): return lax.ppermute(x, axis, route)]
    ppermute x7 -> x10, starting transfers between devices: 16.8 us -> 20.7 us  [shifted(): lax.ppermute(x, 'ctx', [(i, i + distance) for i in range(count) if 0 <= i...]
    ppermute x7 -> x10, waiting for transfers between devices: 6.77 us -> 4.94 us  [shifted(): lax.ppermute(x, 'ctx', [(i, i + distance) for i in range(count) if 0 <= i...]
    ppermute x9 -> x12, waiting for transfers between devices: 2.75 us -> 3.58 us  [partner(): return lax.ppermute(x, axis, route)]
  transfers between devices with their start and end apart: 16 -> 22, of which waited for: 6 -> 8; matrix products, arithmetic and copies ran while one was open for 1% -> 2% of each run, Pallas kernels for 35% -> 29%
where the time goes in v14:
time: 80.8 us; the launch traced here: 80.1 us
  starting transfers between devices  38.6 us (48%)
  Pallas kernels  30.5 us (38%)
  waiting for transfers between devices  8.52 us (11%)
  other arithmetic  1.45 us (2%)
  between operations  1.03 us (1%)
    pallas_call x10, Pallas kernels, call(): pl.pallas_call(kernel, grid_spec=pltpu.PrefetchScalarGridSpec(num_scalar_...  30.5 us
    ppermute x10, starting transfers between devices, shifted(): lax.ppermute(x, 'ctx', [(i, i + distance) for i in range(count) if 0 <= i...  20.7 us
    ppermute x12, starting transfers between devices, partner(): return lax.ppermute(x, axis, route)  17.9 us
    ppermute x10, waiting for transfers between devices, shifted(): lax.ppermute(x, 'ctx', [(i, i + distance) for i in range(count) if 0 <= i...  4.94 us
    ppermute x12, waiting for transfers between devices, partner(): return lax.ppermute(x, axis, route)  3.58 us
  transfers between devices with their start and end apart: 22, of which 8 were waited for; matrix products, arithmetic and copies ran while one was open for 2% of the time, Pallas kernels for 29%

profile of v14, /device:TPU:0, one launch (start us, length us, event | category | flops | bytes accessed | tf_op | source)
XLA Modules:
  0.0 80.1 jit_solution(692417529715425313)
XLA Ops:
  0.7 2.4 %shard_map.110 = (f32[512,128]{1,0:T(8,128)S(1)}, f32[512,128]{1,0:T(8,128)S(1)}, s32[1,256]{1,0:T(1,128)S(1)}, bf16[256,2048]{1,0:T(8,128)(2,1)S(1)}, bf16[256,...) custom-call(s32[1]{0:T(128)} %bitcast.core, s32[1]{0:T(128)} %bitcast.3.ctx, ...), custom_call_target="tpu_custom_call" | custom-call | flops 1 | bytes 1 | tf_op jit(solution)/shard_map/pallas_call | solution.py:397
  4.8 4.9 %collective-permute-start.1 = (f32[512,128]{1,0:T(8,128)S(1)}, f32[512,128]{1,0:T(8,128)S(1)}, u32[]{:S(2)}, u32[]{:S(2)}) collective-permute-start(f32[512,128]{1,0:T(8,128)S(1)} %add.209.rest_0_), channel_id=1, source_target_pairs={{0,2},{1,3},{2,4},{3,5},{4,6},{5,7},{8,10},{9,11},{10,12},{11,13},... | collective-permute-start | bytes 786440 | tf_op jit(solution)/shard_map/ppermute | solution.py:301
  9.8 2.7 %shard_map.111 = (f32[2,264,128]{2,1,0:T(8,128)S(1)}, f32[2,264,128]{2,1,0:T(8,128)S(1)}, bf16[256,2048]{1,0:T(8,128)(2,1)S(1)}, bf16[256,2048]{1,0:T(8,128)(2,1)S(1)}, f32[1,128]{1,0:T(1,128)}) custom-call(s32[1]{0:T(128)} %bitcast.core, bf16[256,2048]{1,0:T(8,128)(2,1)} %bitcast.61, bf16[256,2048]{1,0:T(8,128)(2,1)} %bitcast.62, ...), custom_call_target="tpu_custom_call" | custom-call | flops 1 | bytes 1 | tf_op jit(solution)/shard_map/pallas_call | solution.py:397
  12.5 2.5 %shard_map.112 = (f32[256,1024]{1,0:T(8,128)S(1)}, bf16[16,256,256]{2,1,0:T(8,128)(2,1)S(1)}, f32[1,128]{1,0:T(1,128)S(1)}) custom-call(s32[1]{0:T(128)} %bitcast.core, bf16[256,2048]{1,0:T(8,128)(2,1)S(1)} %get-tuple-element.54.q, bf16[256,2048]{1,0:T(8,128)(2,1)S(1)} %get-tuple-element.50.k, bf16[256,2048]{1,0:T(8,128)(2,1)S(1)} %get-tuple-element.51.v, ...), custom_call_target="tpu_custom_call" | custom-call | flops 1 | bytes 1 | tf_op jit(solution)/shard_map/pallas_call | solution.py:397
  15.6 2.5 %shard_map.113 = (f32[256,1024]{1,0:T(8,128)S(1)}, bf16[16,256,256]{2,1,0:T(8,128)(2,1)S(1)}, f32[1,128]{1,0:T(1,128)S(1)}) custom-call(s32[1]{0:T(128)} %bitcast.core, bf16[256,2048]{1,0:T(8,128)(2,1)S(1)} %get-tuple-element.54.q, bf16[256,2048]{1,0:T(8,128)(2,1)S(1)} %get-tuple-element.50.k, bf16[256,2048]{1,0:T(8,128)(2,1)S(1)} %get-tuple-element.51.v, ...), custom_call_target="tpu_custom_call" | custom-call | flops 1 | bytes 1 | tf_op jit(solution)/shard_map/pallas_call | solution.py:397
  18.1 5.4 %collective-permute-start.2 = (f32[256,128]{1,0:T(8,128)S(1)}, f32[256,128]{1,0:T(8,128)S(1)}, u32[]{:S(2)}, u32[]{:S(2)}) collective-permute-start(f32[256,128]{1,0:T(8,128)S(1)} %get-tuple-element.108.rest_0_), channel_id=1, source_target_pairs={{0,4},{1,5},{2,6},{3,7},{8,12},{9,13},{10,14},{11,15},{16,20},{17,... | collective-permute-start | bytes 393224 | tf_op jit(solution)/shard_map/ppermute | solution.py:301
  23.5 1.3 %collective-permute-start.3 = (f32[256,128]{1,0:T(8,128)S(1)}, f32[256,128]{1,0:T(8,128)S(1)}, u32[]{:S(2)}, u32[]{:S(2)}) collective-permute-start(f32[256,128]{1,0:T(8,128)S(1)} %get-tuple-element.107), channel_id=1, source_target_pairs={{0,4},{1,5},{2,6},{3,7},{8,12},{9,13},{10,14},{11,15},{16,20},{17,... | collective-permute-start | bytes 393224 | tf_op jit(solution)/shard_map/ppermute | solution.py:301
  24.8 1.3 %collective-permute-start.5 = (f32[2,264,128]{2,1,0:T(8,128)S(1)}, f32[2,264,128]{2,1,0:T(8,128)S(1)}, u32[]{:S(2)}, u32[]{:S(2)}) collective-permute-start(f32[2,264,128]{2,1,0:T(8,128)S(1)} %get-tuple-element.124), channel_id=1, source_target_pairs={{1,0},{2,1},{3,2},{4,3},{5,4},{6,5},{7,6},{9,8},{10,9},{11,10},{12... | collective-permute-start | bytes 811016 | tf_op jit(solution)/shard_map/ppermute | solution.py:301
  26.1 2.4 %collective-permute-done.3 = f32[256,128]{1,0:T(8,128)S(1)} collective-permute-done((f32[256,128]{1,0:T(8,128)S(1)}, f32[256,128]{1,0:T(8,128)S(1)}, u32[]{:S(2)}, u32[]{:S(2)}) %collective-permute-start.3) | collective-permute-done | bytes 131104 | tf_op jit(solution)/shard_map/ppermute | solution.py:301
  28.7 1.3 %collective-permute-start.7 = (f32[2,264,128]{2,1,0:T(8,128)S(1)}, f32[2,264,128]{2,1,0:T(8,128)S(1)}, u32[]{:S(2)}, u32[]{:S(2)}) collective-permute-start(f32[2,264,128]{2,1,0:T(8,128)S(1)} %get-tuple-element.123), channel_id=1, source_target_pairs={{1,0},{2,1},{3,2},{4,3},{5,4},{6,5},{7,6},{9,8},{10,9},{11,10},{12... | collective-permute-start | bytes 811016 | tf_op jit(solution)/shard_map/ppermute | solution.py:301
  30.0 2.7 %shard_map.114 = (bf16[256,2048]{1,0:T(8,128)(2,1)}, bf16[256,1024]{1,0:T(8,128)(2,1)S(1)}, f32[2,264,128]{2,1,0:T(8,128)S(1)}, f32[2,4,128]{2,1,0:T(4,128)S(1)}...) custom-call(s32[1]{0:T(128)} %bitcast.core, bf16[256,2048]{1,0:T(8,128)(2,1)S(1)} %get-tuple-element.54.q, ...), custom_call_target="tpu_custom_call" | custom-call | flops 1 | bytes 1 | tf_op jit(solution)/shard_map/pallas_call | solution.py:397
  32.7 2.5 %collective-permute-start.8 = (f32[256,128]{1,0:T(8,128)S(1)}, f32[256,128]{1,0:T(8,128)S(1)}, u32[]{:S(2)}, u32[]{:S(2)}) collective-permute-start(f32[256,128]{1,0:T(8,128)S(1)} %get-tuple-element.66), channel_id=1, source_target_pairs={{0,1},{1,0},{2,3},{3,2},{4,5},{5,4},{6,7},{7,6},{8,9},{9,8},{10,11... | collective-permute-start | bytes 393224 | tf_op jit(solution)/shard_map/ppermute | solution.py:296
  37.5 2.7 %shard_map.115 = (bf16[256,2048]{1,0:T(8,128)(2,1)}, bf16[256,1024]{1,0:T(8,128)(2,1)S(1)}, f32[2,264,128]{2,1,0:T(8,128)S(1)}, f32[2,4,128]{2,1,0:T(4,128)S(1)}...) custom-call(s32[1]{0:T(128)} %bitcast.core, ...), custom_call_target="tpu_custom_call", output_to_operand_aliasing={{0}: (11, {})} | custom-call | flops 1 | bytes 1 | tf_op jit(solution)/shard_map/pallas_call | solution.py:397
  40.2 1.6 %collective-permute-start.17 = (f32[2,4,128]{2,1,0:T(4,128)S(1)}, f32[2,4,128]{2,1,0:T(4,128)S(1)}, u32[]{:S(2)}, u32[]{:S(2)}) collective-permute-start(f32[2,4,128]{2,1,0:T(4,128)S(1)} %fusion.6), channel_id=1, source_target_pairs={{0,8},{8,0},{16,24},{24,16},{1,9},{9,1},{17,25},{25,17},{2,10},{10... | collective-permute-start | bytes 12296 | tf_op jit(solution)/shard_map/ppermute | solution.py:296
  41.8 4.0 %collective-permute-start.9 = (f32[256,128]{1,0:T(8,128)S(1)}, f32[256,128]{1,0:T(8,128)S(1)}, u32[]{:S(2)}, u32[]{:S(2)}) collective-permute-start(f32[256,128]{1,0:T(8,128)S(1)} %get-tuple-element.72), channel_id=1, source_target_pairs={{0,1},{1,0},{2,3},{3,2},{4,5},{5,4},{6,7},{7,6},{8,9},{9,8},{10,11... | collective-permute-start | bytes 393224 | tf_op jit(solution)/shard_map/ppermute | solution.py:296
  45.8 2.0 %collective-permute-done.10 = f32[256,128]{1,0:T(8,128)S(1)} collective-permute-done((f32[256,128]{1,0:T(8,128)S(1)}, f32[256,128]{1,0:T(8,128)S(1)}, u32[]{:S(2)}, u32[]{:S(2)}) %collective-permute-start.10) | collective-permute-done | bytes 131104 | tf_op jit(solution)/shard_map/ppermute | solution.py:301
  50.5 1.6 %collective-permute-start.18 = (f32[1,4,128]{2,1,0:T(4,128)S(1)}, f32[1,4,128]{2,1,0:T(4,128)S(1)}, u32[]{:S(2)}, u32[]{:S(2)}) collective-permute-start(f32[1,4,128]{2,1,0:T(4,128)S(1)} %slice_select_fusion), channel_id=1, source_target_pairs={{0,16},{8,24},{16,0},{24,8},{1,17},{9,25},{17,1},{25,9},{2,18},{10... | collective-permute-start | bytes 6152 | tf_op jit(solution)/shard_map/ppermute | solution.py:296
  52.1 5.1 %shard_map.116 = (bf16[256,2048]{1,0:T(8,128)(2,1)}, f32[256,1024]{1,0:T(8,128)S(1)}, f32[256,1024]{1,0:T(8,128)S(1)}, f32[1,128]{1,0:T(1,128)S(1)}) custom-call(s32[1]{0:T(128)} %bitcast.core, bf16[256,2048]{1,0:T(8,128)(2,1)S(1)} %get-tuple-element.54.q, bf16[256,2048]{1,0:T(8,128)(2,1)S(1)} %get-tuple-element.50.k, ...), custom_call_target="tpu_custom_call" | custom-call | flops 1 | bytes 1 | tf_op jit(solution)/shard_map/pallas_call | solution.py:397
  58.6 3.9 %collective-permute-start.19 = (f32[2,128]{1,0:T(2,128)S(1)}, f32[2,128]{1,0:T(2,128)S(1)}, u32[]{:S(2)}, u32[]{:S(2)}) collective-permute-start(f32[2,128]{1,0:T(2,128)S(1)} %broadcast_select_fusion), channel_id=1, source_target_pairs={{0,4},{1,5},{2,6},{3,7},{4,0},{5,1},{6,2},{7,3},{8,12},{9,13},{10,... | collective-permute-start | bytes 3080 | tf_op jit(solution)/shard_map/ppermute | solution.py:296
  62.6 1.4 %collective-permute-start.15 = (f32[4,264,128]{2,1,0:T(8,128)S(1)}, f32[4,264,128]{2,1,0:T(8,128)S(1)}, u32[]{:S(2)}, u32[]{:S(2)}) collective-permute-start(f32[4,264,128]{2,1,0:T(8,128)S(1)} %maximum_add_fusion), channel_id=1, source_target_pairs={{0,1},{1,2},{2,3},{3,4},{4,5},{5,6},{6,7},{8,9},{9,10},{10,11},{11... | collective-permute-start | bytes 1622024 | tf_op jit(solution)/shard_map/ppermute | solution.py:301
  63.9 5.2 %shard_map.117 = (bf16[256,2048]{1,0:T(8,128)(2,1)}, f32[256,1024]{1,0:T(8,128)S(1)}, f32[256,1024]{1,0:T(8,128)S(1)}, f32[1,128]{1,0:T(1,128)S(1)}) custom-call(s32[1]{0:T(128)} %bitcast.core, bf16[256,2048]{1,0:T(8,128)(2,1)S(1)} %get-tuple-element.54.q, bf16[256,2048]{1,0:T(8,128)(2,1)S(1)} %get-tuple-element.50.k, ...), custom_call_target="tpu_custom_call", output_to_operand_aliasing={{0}: (13, {})} | custom-call | flops 1 | bytes 1 | tf_op jit(solution)/shard_map/pallas_call | solution.py:397
  69.2 3.1 %collective-permute-start.14 = (f32[256,128]{1,0:T(8,128)S(1)}, f32[256,128]{1,0:T(8,128)S(1)}, u32[]{:S(2)}, u32[]{:S(2)}) collective-permute-start(f32[256,128]{1,0:T(8,128)S(1)} %get-tuple-element.97), channel_id=1, source_target_pairs={{0,1},{1,0},{2,3},{3,2},{4,5},{5,4},{6,7},{7,6},{8,9},{9,8},{10,11... | collective-permute-start | bytes 393224 | tf_op jit(solution)/shard_map/ppermute | solution.py:296
  73.2 2.4 %shard_map.118 = (bf16[256,2048]{1,0:T(8,128)(2,1)}, bf16[256,2048]{1,0:T(8,128)(2,1)}, f32[1,128]{1,0:T(1,128)S(1)}) custom-call(s32[1]{0:T(128)} %bitcast.core, bf16[256,2048]{1,0:T(8,128)(2,1)S(1)} %get-tuple-element.50.k, bf16[256,2048]{1,0:T(8,128)(2,1)S(1)} %get-tuple-element.51.v, f32[256,1024]{1,0:T(8,128)S(1)} %get-tuple-element.81.gk_in, ...), custom_call_target="tpu_custom_call" | custom-call | flops 1 | bytes 1 | tf_op jit(solution)/shard_map/pallas_call | solution.py:397
  77.7 2.4 %shard_map.119 = (bf16[256,2048]{1,0:T(8,128)(2,1)}, bf16[256,2048]{1,0:T(8,128)(2,1)}, f32[1,128]{1,0:T(1,128)}) custom-call(s32[1]{0:T(128)} %bitcast.core, bf16[256,2048]{1,0:T(8,128)(2,1)S(1)} %get-tuple-element.50.k, bf16[256,2048]{1,0:T(8,128)(2,1)S(1)} %get-tuple-element.51.v, ...), custom_call_target="tpu_custom_call", output_to_operand_aliasing={{0}: (10, {}), {1}: (11, {})} | custom-call | flops 1 | bytes 1 | tf_op jit(solution)/shard_map/pallas_call | solution.py:397
  (75 shorter events, 12.0 us)
Async XLA Ops:
  0.6 3.0 %copy-start = (s32[1,256]{1,0:T(1,128)S(1)}, s32[1,256]{1,0:T(1,128)}, u32[]{:S(2)}) copy-start(s32[1,256]{1,0:T(1,128)} %seg.13) | copy-start | bytes 3076
  3.1 1.7 %collective-permute-start = (f32[512,128]{1,0:T(8,128)S(1)}, f32[512,128]{1,0:T(8,128)S(1)}, u32[]{:S(2)}, u32[]{:S(2)}) collective-permute-start(f32[512,128]{1,0:T(8,128)S(1)} %get-tuple-element.53), channel_id=1, source_target_pairs={{0,1},{1,0},{2,3},{3,2},{4,5},{5,4},{6,7},{7,6},{8,9},{9,8},{10,11... | collective-permute-start | bytes 786440 | tf_op jit(solution)/shard_map/ppermute | solution.py:296
  4.8 10.7 %collective-permute-start.1 = (f32[512,128]{1,0:T(8,128)S(1)}, f32[512,128]{1,0:T(8,128)S(1)}, u32[]{:S(2)}, u32[]{:S(2)}) collective-permute-start(f32[512,128]{1,0:T(8,128)S(1)} %add.209.rest_0_), channel_id=1, source_target_pairs={{0,2},{1,3},{2,4},{3,5},{4,6},{5,7},{8,10},{9,11},{10,12},{11,13},... | collective-permute-start | bytes 786440 | tf_op jit(solution)/shard_map/ppermute | solution.py:301
  15.6 14.4 %copy-start.1 = (f32[2048]{0:T(1024)S(1)}, f32[2048]{0:T(1024)}, u32[]{:S(2)}) copy-start(f32[2048]{0:T(1024)} %param.13) | copy-start | bytes 24580
  18.1 17.1 %collective-permute-start.2 = (f32[256,128]{1,0:T(8,128)S(1)}, f32[256,128]{1,0:T(8,128)S(1)}, u32[]{:S(2)}, u32[]{:S(2)}) collective-permute-start(f32[256,128]{1,0:T(8,128)S(1)} %get-tuple-element.108.rest_0_), channel_id=1, source_target_pairs={{0,4},{1,5},{2,6},{3,7},{8,12},{9,13},{10,14},{11,15},{16,20},{17,... | collective-permute-start | bytes 393224 | tf_op jit(solution)/shard_map/ppermute | solution.py:301
  23.5 5.1 %collective-permute-start.3 = (f32[256,128]{1,0:T(8,128)S(1)}, f32[256,128]{1,0:T(8,128)S(1)}, u32[]{:S(2)}, u32[]{:S(2)}) collective-permute-start(f32[256,128]{1,0:T(8,128)S(1)} %get-tuple-element.107), channel_id=1, source_target_pairs={{0,4},{1,5},{2,6},{3,7},{8,12},{9,13},{10,14},{11,15},{16,20},{17,... | collective-permute-start | bytes 393224 | tf_op jit(solution)/shard_map/ppermute | solution.py:301
  24.8 5.2 %collective-permute-start.5 = (f32[2,264,128]{2,1,0:T(8,128)S(1)}, f32[2,264,128]{2,1,0:T(8,128)S(1)}, u32[]{:S(2)}, u32[]{:S(2)}) collective-permute-start(f32[2,264,128]{2,1,0:T(8,128)S(1)} %get-tuple-element.124), channel_id=1, source_target_pairs={{1,0},{2,1},{3,2},{4,3},{5,4},{6,5},{7,6},{9,8},{10,9},{11,10},{12... | collective-permute-start | bytes 811016 | tf_op jit(solution)/shard_map/ppermute | solution.py:301
  28.6 1.4 %collective-permute-start.4 = (f32[256,128]{1,0:T(8,128)S(1)}, f32[256,128]{1,0:T(8,128)S(1)}, u32[]{:S(2)}, u32[]{:S(2)}) collective-permute-start(f32[256,128]{1,0:T(8,128)S(1)} %get-tuple-element.105), channel_id=1, source_target_pairs={{0,1},{1,0},{2,3},{3,2},{4,5},{5,4},{6,7},{7,6},{8,9},{9,8},{10,11... | collective-permute-start | bytes 393224 | tf_op jit(solution)/shard_map/ppermute | solution.py:296
  28.7 8.8 %collective-permute-start.7 = (f32[2,264,128]{2,1,0:T(8,128)S(1)}, f32[2,264,128]{2,1,0:T(8,128)S(1)}, u32[]{:S(2)}, u32[]{:S(2)}) collective-permute-start(f32[2,264,128]{2,1,0:T(8,128)S(1)} %get-tuple-element.123), channel_id=1, source_target_pairs={{1,0},{2,1},{3,2},{4,3},{5,4},{6,5},{7,6},{9,8},{10,9},{11,10},{12... | collective-permute-start | bytes 811016 | tf_op jit(solution)/shard_map/ppermute | solution.py:301
  32.7 3.5 %collective-permute-start.8 = (f32[256,128]{1,0:T(8,128)S(1)}, f32[256,128]{1,0:T(8,128)S(1)}, u32[]{:S(2)}, u32[]{:S(2)}) collective-permute-start(f32[256,128]{1,0:T(8,128)S(1)} %get-tuple-element.66), channel_id=1, source_target_pairs={{0,1},{1,0},{2,3},{3,2},{4,5},{5,4},{6,7},{7,6},{8,9},{9,8},{10,11... | collective-permute-start | bytes 393224 | tf_op jit(solution)/shard_map/ppermute | solution.py:296
  35.2 2.3 %collective-permute-start.6 = (f32[256,128]{1,0:T(8,128)S(1)}, f32[256,128]{1,0:T(8,128)S(1)}, u32[]{:S(2)}, u32[]{:S(2)}) collective-permute-start(f32[256,128]{1,0:T(8,128)S(1)} %get-tuple-element.103), channel_id=1, source_target_pairs={{0,1},{1,0},{2,3},{3,2},{4,5},{5,4},{6,7},{7,6},{8,9},{9,8},{10,11... | collective-permute-start | bytes 393224 | tf_op jit(solution)/shard_map/ppermute | solution.py:296
  36.2 11.6 %collective-permute-start.10 = (f32[256,128]{1,0:T(8,128)S(1)}, f32[256,128]{1,0:T(8,128)S(1)}, u32[]{:S(2)}, u32[]{:S(2)}) collective-permute-start(f32[256,128]{1,0:T(8,128)S(1)} %add.231.rest_0_), channel_id=1, source_target_pairs={{2,0},{3,1},{4,2},{5,3},{6,4},{7,5},{10,8},{11,9},{12,10},{13,11},... | collective-permute-start | bytes 393224 | tf_op jit(solution)/shard_map/ppermute | solution.py:301
  40.2 10.2 %collective-permute-start.17 = (f32[2,4,128]{2,1,0:T(4,128)S(1)}, f32[2,4,128]{2,1,0:T(4,128)S(1)}, u32[]{:S(2)}, u32[]{:S(2)}) collective-permute-start(f32[2,4,128]{2,1,0:T(4,128)S(1)} %fusion.6), channel_id=1, source_target_pairs={{0,8},{8,0},{16,24},{24,16},{1,9},{9,1},{17,25},{25,17},{2,10},{10... | collective-permute-start | bytes 12296 | tf_op jit(solution)/shard_map/ppermute | solution.py:296
  41.8 6.0 %collective-permute-start.9 = (f32[256,128]{1,0:T(8,128)S(1)}, f32[256,128]{1,0:T(8,128)S(1)}, u32[]{:S(2)}, u32[]{:S(2)}) collective-permute-start(f32[256,128]{1,0:T(8,128)S(1)} %get-tuple-element.72), channel_id=1, source_target_pairs={{0,1},{1,0},{2,3},{3,2},{4,5},{5,4},{6,7},{7,6},{8,9},{9,8},{10,11... | collective-permute-start | bytes 393224 | tf_op jit(solution)/shard_map/ppermute | solution.py:296
  47.9 9.4 %collective-permute-start.11 = (f32[256,128]{1,0:T(8,128)S(1)}, f32[256,128]{1,0:T(8,128)S(1)}, u32[]{:S(2)}, u32[]{:S(2)}) collective-permute-start(f32[256,128]{1,0:T(8,128)S(1)} %add_add_fusion.2.rest_0_), channel_id=1, source_target_pairs={{2,0},{3,1},{4,2},{5,3},{6,4},{7,5},{10,8},{11,9},{12,10},{13,11},... | collective-permute-start | bytes 393224 | tf_op jit(solution)/shard_map/ppermute | solution.py:301
  49.2 20.0 %collective-permute-start.13 = (f32[256,128]{1,0:T(8,128)S(1)}, f32[256,128]{1,0:T(8,128)S(1)}, u32[]{:S(2)}, u32[]{:S(2)}) collective-permute-start(f32[256,128]{1,0:T(8,128)S(1)} %add_add_fusion.4.rest_1_), channel_id=1, source_target_pairs={{4,0},{5,1},{6,2},{7,3},{12,8},{13,9},{14,10},{15,11},{20,16},{21,... | collective-permute-start | bytes 393224 | tf_op jit(solution)/shard_map/ppermute | solution.py:301
  50.5 8.1 %collective-permute-start.18 = (f32[1,4,128]{2,1,0:T(4,128)S(1)}, f32[1,4,128]{2,1,0:T(4,128)S(1)}, u32[]{:S(2)}, u32[]{:S(2)}) collective-permute-start(f32[1,4,128]{2,1,0:T(4,128)S(1)} %slice_select_fusion), channel_id=1, source_target_pairs={{0,16},{8,24},{16,0},{24,8},{1,17},{9,25},{17,1},{25,9},{2,18},{10... | collective-permute-start | bytes 6152 | tf_op jit(solution)/shard_map/ppermute | solution.py:296
  57.3 18.4 %collective-permute-start.12 = (f32[256,128]{1,0:T(8,128)S(1)}, f32[256,128]{1,0:T(8,128)S(1)}, u32[]{:S(2)}, u32[]{:S(2)}) collective-permute-start(f32[256,128]{1,0:T(8,128)S(1)} %add_add_fusion.3.rest_0_), channel_id=1, source_target_pairs={{4,0},{5,1},{6,2},{7,3},{12,8},{13,9},{14,10},{15,11},{20,16},{21,... | collective-permute-start | bytes 393224 | tf_op jit(solution)/shard_map/ppermute | solution.py:301
  58.6 13.7 %collective-permute-start.19 = (f32[2,128]{1,0:T(2,128)S(1)}, f32[2,128]{1,0:T(2,128)S(1)}, u32[]{:S(2)}, u32[]{:S(2)}) collective-permute-start(f32[2,128]{1,0:T(2,128)S(1)} %broadcast_select_fusion), channel_id=1, source_target_pairs={{0,4},{1,5},{2,6},{3,7},{4,0},{5,1},{6,2},{7,3},{8,12},{9,13},{10,... | collective-permute-start | bytes 3080 | tf_op jit(solution)/shard_map/ppermute | solution.py:296
  62.6 10.7 %collective-permute-start.15 = (f32[4,264,128]{2,1,0:T(8,128)S(1)}, f32[4,264,128]{2,1,0:T(8,128)S(1)}, u32[]{:S(2)}, u32[]{:S(2)}) collective-permute-start(f32[4,264,128]{2,1,0:T(8,128)S(1)} %maximum_add_fusion), channel_id=1, source_target_pairs={{0,1},{1,2},{2,3},{3,4},{4,5},{5,6},{6,7},{8,9},{9,10},{10,11},{11... | collective-permute-start | bytes 1622024 | tf_op jit(solution)/shard_map/ppermute | solution.py:301
  69.2 4.1 %collective-permute-start.14 = (f32[256,128]{1,0:T(8,128)S(1)}, f32[256,128]{1,0:T(8,128)S(1)}, u32[]{:S(2)}, u32[]{:S(2)}) collective-permute-start(f32[256,128]{1,0:T(8,128)S(1)} %get-tuple-element.97), channel_id=1, source_target_pairs={{0,1},{1,0},{2,3},{3,2},{4,5},{5,4},{6,7},{7,6},{8,9},{9,8},{10,11... | collective-permute-start | bytes 393224 | tf_op jit(solution)/shard_map/ppermute | solution.py:296
  72.3 3.6 %collective-permute-start.20 = (f32[1,128]{1,0:T(1,128)S(1)}, f32[1,128]{1,0:T(1,128)S(1)}, u32[]{:S(2)}, u32[]{:S(2)}) collective-permute-start(f32[1,128]{1,0:T(1,128)S(1)} %compare_select_fusion), channel_id=1, source_target_pairs={{0,2},{1,3},{2,0},{3,1},{4,6},{5,7},{6,4},{7,5},{8,10},{9,11},{10,... | collective-permute-start | bytes 1544 | tf_op jit(solution)/shard_map/ppermute | solution.py:296
  76.0 1.1 %collective-permute-start.21 = (f32[1,64]{1,0:T(1,128)S(1)}, f32[1,64]{1,0:T(1,128)S(1)}, u32[]{:S(2)}, u32[]{:S(2)}) collective-permute-start(f32[1,64]{1,0:T(1,128)S(1)} %slice_select_fusion.5), channel_id=1, source_target_pairs={{0,1},{1,0},{2,3},{3,2},{4,5},{5,4},{6,7},{7,6},{8,9},{9,8},{10,11... | collective-permute-start | bytes 776 | tf_op jit(solution)/shard_map/ppermute | solution.py:296
  76.2 1.5 %collective-permute-start.16 = (f32[256,128]{1,0:T(8,128)S(1)}, f32[256,128]{1,0:T(8,128)S(1)}, u32[]{:S(2)}, u32[]{:S(2)}) collective-permute-start(f32[256,128]{1,0:T(8,128)S(1)} %get-tuple-element.95), channel_id=1, source_target_pairs={{0,1},{1,0},{2,3},{3,2},{4,5},{5,4},{6,7},{7,6},{8,9},{9,8},{10,11... | collective-permute-start | bytes 393224 | tf_op jit(solution)/shard_map/ppermute | solution.py:296
  (1 other events, 2.9 us)

commit v15 on v13

--- a/solution.py
+++ b/solution.py
@@ -95,12 +95,10 @@
     return pl.ds(pl.multiple_of(base + p * PAIR, PAIR), PAIR)
 
 
-def place(sel, core, lanes, sub):
-    step = pl.program_id(0)
-    group, part = step // sub, step % sub
+def place(sel, group, core, lanes, sub):
+    inside = pl.program_id(0) % sub * (lanes // sub)
     half = (sel + core[0]) % 2
-    base = group * lanes + part * (lanes // sub)
-    return group, base, base + (group + half) * lanes, base // PAIR * E
+    return inside, (2 * group + half) * lanes + inside, inside // PAIR * E
 
 
 def states_kernel(core, ctx, dp, k_in, v_in, keep, send, zero, k, v, core_row, ctx_row, dp_row, sems):
@@ -153,7 +151,9 @@
 def local_kernel(sel, core, q, k, v, mask, mask_t, *rest):
     attn, probs, token = rest[-3:]
     lanes = attn.shape[1] // GROUPS
-    group, base, wide, _ = place(sel, core, lanes, 1)
+    group = pl.program_id(0)
+    base = group * lanes
+    wide = base + (group + (sel + core[0]) % 2) * lanes
     m, mt = mask[...], mask_t[...]
     token[...] = jnp.zeros_like(token)
     for p in range(lanes // PAIR):
@@ -198,12 +198,12 @@
     return rows.astype(F32) * met.astype(F32)
 
 
-def norm_kernel(sel, core, q, dy, local, gain, seg, table, prefix, nxt, *rest):
+def norm_kernel(sel, group, core, q, dy, local, gain, seg, table, prefix, nxt, *rest):
     out, dab, part, gsum, total, token = rest[-6:]
     token[...] = jnp.zeros_like(token)
     lanes = out.shape[1]
     count = lanes // PAIR
-    _, base, wide, row = place(sel, core, lanes, 1)
+    base, wide, row = place(sel, group, core, lanes, 1)
     on_next = on_rows(seg, table, True, nxt)
     last, own, flag = edge(seg, table, True)
     last = (last.astype(F32) * jnp.where(flag == 1, 1.0, 0.0)).astype(BF16)
@@ -214,7 +214,9 @@
         dot(twice(q[:, at]), side_by_side(prefix[rows_at(row, p)], nxt[0, rows_at(0, p)]), 1, 0)
         for p, at in enumerate(wides)
     ]
-    attns = [local[:, at] + far[:, :PAIR] + on_next * far[:, PAIR:] for at, far in zip(bases, fars)]
+    attns = [
+        local[:, lanes_at(group * lanes, p)] + far[:, :PAIR] + on_next * far[:, PAIR:] for p, far in enumerate(fars)
+    ]
     squares = [head_mean(attn * attn) for attn in attns]
     scales = [lax.rsqrt(square + 1e-06) for square in squares]
     normeds = [attn * scale for attn, scale in zip(attns, scales)]
@@ -234,27 +236,26 @@
         gsum[0, p:p + 1] = jnp.sum(dy[:, wides[p]].astype(F32) * normed, axis=0, keepdims=True)
 
 
-def inner_kernel(sel, core, q, k, v, dab, probs, mask, seg, table, prefix, nxt, *rest):
+def inner_kernel(sel, group, core, q, k, v, dab, probs, mask, seg, table, prefix, nxt, *rest):
     gq, gk, gv, token = rest[-4:]
-    lanes = dab.shape[1] // GROUPS
+    lanes = dab.shape[1]
     count = lanes // SUB // PAIR
-    group, base, wide, row = place(sel, core, lanes, SUB)
+    base, wide, row = place(sel, group, core, lanes, SUB)
     m = mask[...]
     token[...] = jnp.zeros_like(token)
     on_next = on_rows(seg, table, True, nxt)
-    first = row - group * (lanes // 2)
     for p in range(count):
         at = lanes_at(wide, p)
         da = dab[:, lanes_at(base, p)]
         vp = v[:, at]
-        far = dot(twice(da), stacked(prefix[rows_at(row, p)], nxt[0, rows_at(first, p)]), 1, 1)
+        far = dot(twice(da), stacked(prefix[rows_at(row, p)], nxt[0, rows_at(row, p)]), 1, 1)
         tq = far[:, :PAIR] + on_next * far[:, PAIR:]
         tk = tv = None
         for h, (qh, kh, dh) in enumerate(zip(heads_of(q[:, at]), heads_of(k[:, at]), heads_of(da))):
             dprob = dot(dh, vp, 1, 1).astype(BF16) * m
             tq = tq + dot(dprob, kh, 1, 0)
             a = dot(dprob, qh, 0, 0)
-            b = dot(probs[row // (E // 2) + 2 * p + h], dh, 1, 0)
+            b = dot(probs[group * (lanes // E) + base // E + 2 * p + h], dh, 1, 0)
             tk = a if tk is None else tk + a
             tv = b if tv is None else tv + b
         gq[:, p * PAIR:(p + 1) * PAIR] = tq.astype(BF16)
@@ -262,18 +263,17 @@
         gv[:, lanes_at(base, p)] = tv
 
 
-def outer_kernel(sel, core, k, v, gk_in, gv_in, seg, table, suffix, prv, *rest):
+def outer_kernel(sel, group, core, k, v, gk_in, gv_in, seg, table, suffix, prv, *rest):
     gk, gv, token = rest[-3:]
-    lanes = gk_in.shape[1] // GROUPS
+    lanes = gk_in.shape[1]
     count = lanes // SUB // PAIR
-    group, base, wide, row = place(sel, core, lanes, SUB)
+    base, wide, row = place(sel, group, core, lanes, SUB)
     token[...] = jnp.zeros_like(token)
     on_prev = on_rows(seg, table, False, prv)
-    first = row - group * (lanes // 2)
     for p in range(count):
         here, own, at = slice(p * PAIR, (p + 1) * PAIR), lanes_at(base, p), lanes_at(wide, p)
         s = suffix[rows_at(row, p)]
-        g = prv[0, rows_at(first, p)]
+        g = prv[0, rows_at(row, p)]
         far = dot(twice(v[:, at]), stacked(s, g), 1, 1)
         gk[:, here] = (gk_in[:, own] + far[:, :PAIR] + on_prev * far[:, PAIR:]).astype(BF16)
         far = dot(twice(k[:, at]), side_by_side(s, g), 1, 0)
@@ -327,28 +327,33 @@
     half_rows = lanes // PAIR * E
     heads = lanes // E
 
-    def call(kernel, sel, ins, outs, after=(), alias=(), scratch=(), sub=1, steps=None, scalars=None):
+    def call(kernel, sel, ins, outs, group=0, after=(), alias=(), scratch=(), sub=1, steps=None, scalars=None):
         scalars = scalars or [core]
 
         def wide(i, c, *_):
-            return (0, (i // sub * 2 + (sel + c[0]) % 2) * sub + i % sub)
+            return (0, (2 * group + (sel + c[0]) % 2) * sub + i % sub)
 
         def whole(*args):
             return (0, 0)
 
         def part(i, c, *_):
-            return (i // sub, 0, 0)
+            return (group, 0, 0)
+
+        def single(*args):
+            return (0, 0, 0)
 
         specs = {
             "vmem": pl.BlockSpec(memory_space=pltpu.VMEM),
             "hbm": pl.BlockSpec(memory_space=pltpu.HBM),
             "wide": pl.BlockSpec((rows, lanes // sub), wide),
             "row": pl.BlockSpec((1, lanes // sub), wide),
-            "sums": pl.BlockSpec((1, lanes // PAIR, PAIR), part),
+            "sums": pl.BlockSpec((1, lanes // PAIR, PAIR), single),
             "zero": pl.BlockSpec((1, rows), whole),
             "all": pl.BlockSpec((GROUPS * half_rows, PAIR), whole),
             "part": pl.BlockSpec((1, half_rows + EXTRA, PAIR), part),
-            "later": pl.BlockSpec((1, half_rows + EXTRA, PAIR), lambda i, *_: (GROUPS + i // sub, 0, 0)),
+            "later": pl.BlockSpec((1, half_rows + EXTRA, PAIR), lambda *args: (GROUPS + group, 0, 0)),
+            "one": pl.BlockSpec((1, half_rows + EXTRA, PAIR), single),
+            "half": pl.BlockSpec((half_rows, PAIR), whole),
             "parts": pl.BlockSpec((GROUPS, half_rows + EXTRA, PAIR), lambda *args: (0, 0, 0)),
             "seg": pl.BlockSpec((1, rows), whole),
             "table": pl.BlockSpec((1, table.shape[0]), whole),
@@ -360,7 +365,9 @@
         }
         shapes = {
             "wide": (rows, width),
-            "sums": (GROUPS, lanes // PAIR, PAIR),
+            "sums": (1, lanes // PAIR, PAIR),
+            "one": (1, half_rows + EXTRA, PAIR),
+            "half": (half_rows, PAIR),
             "zero": (1, rows),
             "all": (GROUPS * half_rows, PAIR),
             "part": (GROUPS, half_rows + EXTRA, PAIR),
@@ -384,7 +391,7 @@
             kernel,
             grid_spec=pltpu.PrefetchScalarGridSpec(
                 num_scalar_prefetch=len(scalars),
-                grid=steps or (GROUPS * sub,),
+                grid=steps or (sub,),
                 in_specs=[specs[kind] for kind in kinds],
                 out_specs=[specs[kind] for kind, *_ in outs],
                 scratch_shapes=scratch,
@@ -397,48 +404,49 @@
 
     edges = [("seg", segment_ids), ("table", image_flags)]
     chips = lax.axis_size("ctx") // 2
-    whole, part_of = (rows, width), (rows, width // 2)
+    whole, part_of, one_of = (rows, width), (rows, width // 2), (rows, lanes)
+    groups = range(GROUPS)
 
     def local_attn(sel, after):
         return call(
             functools.partial(local_kernel, sel), sel,
             [("vmem", q), ("vmem", k), ("vmem", v), ("mask", mask), ("mask", mask_t)],
-            [("vmem", F32, part_of), ("vmem", BF16, (GROUPS * heads, rows, rows)), ("token", F32)], after=after)
-
-    def norm(sel, before, after):
+            [("vmem", F32, part_of), ("vmem", BF16, (GROUPS * heads, rows, rows)), ("token", F32)],
+            after=after, steps=(GROUPS,))
+
+    def norm(sel, g, before, after):
         return call(
-            functools.partial(norm_kernel, sel), sel,
+            functools.partial(norm_kernel, sel, g), sel,
             [("vmem", q), ("vmem", dy), ("vmem", local[sel][0]), ("row", gain_row), *edges,
-             ("all", prefix[sel]), ("part", nxt[sel])],
-            [("wide", BF16), ("vmem", BF16, part_of), ("part", F32), ("sums", F32), ("all", F32), ("token", F32)],
-            after=after, alias=[(0, before)])
-
-    def inner(sel, before, after):
+             ("half", prefix[g][sel]), ("part", nxt[sel])],
+            [("wide", BF16), ("vmem", BF16, one_of), ("one", F32), ("sums", F32), ("half", F32), ("token", F32)],
+            group=g, after=after, alias=[(0, before)])
+
+    def inner(sel, g, before, after):
         return call(
-            functools.partial(inner_kernel, sel), sel,
-            [("vmem", q), ("vmem", k), ("vmem", v), ("vmem", norms[sel][1]), ("vmem", local[sel][1]), ("mask", mask),
-             *edges, ("all", prefix[sel]), ("part", nxt[sel])],
-            [("wide", BF16), ("vmem", F32, part_of), ("vmem", F32, part_of), ("token", F32)],
-            after=after, alias=[(0, before)], sub=SUB)
-
-    def outer(sel, before, after):
+            functools.partial(inner_kernel, sel, g), sel,
+            [("vmem", q), ("vmem", k), ("vmem", v), ("vmem", norms[g][sel][1]), ("vmem", local[sel][1]), ("mask", mask),
+             *edges, ("half", prefix[g][sel]), ("part", nxt[sel])],
+            [("wide", BF16), ("vmem", F32, one_of), ("vmem", F32, one_of), ("token", F32)],
+            group=g, after=after, alias=[(0, before)], sub=SUB)
+
+    def outer(sel, g, before, after):
         return call(
-            functools.partial(outer_kernel, sel), sel,
-            [("vmem", k), ("vmem", v), ("vmem", inners[sel][1]), ("vmem", inners[sel][2]), *edges,
-             ("all", suffix[sel]), ("later" if sel else "part", prv[0])],
-            [("wide", BF16), ("wide", BF16), ("token", F32)], after=after, alias=list(enumerate(before)), sub=SUB)
-
-    def summed_before(own, towards, works):
-        load, before, span = own, None, 1
+            functools.partial(outer_kernel, sel, g), sel,
+            [("vmem", k), ("vmem", v), ("vmem", inners[sel, g][1]), ("vmem", inners[sel, g][2]), *edges,
+             ("half", suffix[g][sel]), ("later" if sel else "part", prv)],
+            [("wide", BF16), ("wide", BF16), ("token", F32)],
+            group=g, after=after, alias=list(enumerate(before)), sub=SUB)
+
+    def rows_of_group(x, g):
+        return x[g * half_rows:(g + 1) * half_rows]
+
+    def more_hops(load, before, towards):
+        span = 2
         while span < chips:
             arrived = shifted(load, 2 * towards * span)
-            if works:
-                arrived = arrived + works.pop(0)(load)
-            before = arrived if before is None else before + arrived
-            load = load + arrived
+            load, before = load + arrived, before + arrived
             span *= 2
-        for work in works:
-            before = before + work(load)
         return before
 
     keep, send, zero, k, v, core_row, ctx_row, dp_row = call(
@@ -460,54 +468,58 @@
         [("parts", F32)] * 2 + [("vmem", BF16, whole), ("vmem", BF16, whole), ("token", F32)],
         after=[piece[2]], scratch=[pltpu.SemaphoreType.DMA((2,))], steps=(1,))
     *parts, q, dy, _ = parts
-    local, nxt = [], []
-
-    def first_work(load):
-        *made, token = local_attn(0, [parts[0]])
-        local.append(made)
-        return token
-
-    def second_work(load):
-        for part in reversed(parts):
-            nxt.append(shifted(part + nought(load[:1]), -1))
-        *made, token = local_attn(1, [load])
-        local.append(made)
-        return token
-
-    before = summed_before(piece[2], 1, [first_work, second_work])
-    prefix = to_cores(core_row, before, piece, 1)
-    norms = [norm(0, None, [])]
-    norms.append(norm(1, norms[0][0], [norms[0][4]]))
-    output = norms[1][0]
-    piece = within_chip(norms[0][4], norms[1][4])
-    gain_sum = [jnp.concatenate([jnp.where(core_row == half, norms[0][3], norms[1][3]) for half in range(2)], axis=0)]
-    gain_sum.append(scatter_step(gain_sum[-1], dp_row, "dp", 0))
+    local = [local_attn(0, [parts[0]])]
+    local.append(local_attn(1, [parts[0]]))
+    first = shifted(piece[2], 2) + local[0][2] + local[1][2]
+    load = piece[2] + first
+    loads = [rows_of_group(load, g) for g in groups]
+    nxt = [shifted(part + nought(loads[1][:1]), -1) for part in reversed(parts)]
+    prefix, norms, late, output, token = [], [], [], None, None
+    for g in groups:
+        before = more_hops(loads[g], rows_of_group(first, g), 1)
+        if g:
+            before = before + token
+        prefix.append(to_cores(core_row, before, [rows_of_group(x, g) for x in piece], 1))
+        norms.append([norm(0, g, output, [])])
+        norms[g].append(norm(1, g, norms[g][0][0], [norms[g][0][4]]))
+        output, token = norms[g][1][0], norms[g][1][5]
+        late.append(within_chip(norms[g][0][4], norms[g][1][4]))
+
+    gain_sum = jnp.concatenate(
+        [jnp.where(core_row == half, n[0][3], n[1][3]) for half in range(2) for n in norms], axis=0)
+    gain_sum = scatter_step(gain_sum, dp_row, "dp", 0)
     bits = list(reversed(range(lax.axis_size("ctx").bit_length() - 1)))
-    inners, prv = [], []
-
-    def third_work(load):
-        x = scatter_step(gain_sum[-1] + nought(load[:1]), dp_row, "dp", 1)
-        gain_sum.append(x.reshape(-1, PAIR))
-        inners.append(inner(0, None, [load]))
-        return inners[0][3]
-
-    def fourth_work(load):
-        gain_sum.append(scatter_step(gain_sum[-1] + nought(load[:1]), ctx_row, "ctx", bits[0]))
-        both = jnp.concatenate([norms[1][2], norms[0][2]], axis=0) + nought(load[:1])
-        prv.append(shifted(both, 1))
-        inners.append(inner(1, inners[0][0], [load]))
-        return inners[1][3]
-
-    before = summed_before(piece[2], -1, [third_work, fourth_work])
-    suffix = to_cores(core_row, before, piece, -1)
-    grad_gain = scatter_step(gain_sum[-1] + nought(before[:1]), ctx_row, "ctx", bits[1])
-    outers = outer(0, [None] * 2, [])
-    grad_gain = grad_gain + outers[2]
+
+    load = jnp.concatenate([own for _, _, own in late], axis=0)
+    first = shifted(load, -2)
+    gain_sum = scatter_step(gain_sum + nought(load[:1]), dp_row, "dp", 1).reshape(-1, PAIR)
+    inners = {(0, 0): inner(0, 0, None, [load])}
+    inners[0, 1] = inner(0, 1, inners[0, 0][0], [load])
+    first = first + inners[0, 1][3]
+    load = load + first
+    loads = [rows_of_group(load, 0)]
+    inners[1, 0] = inner(1, 0, inners[0, 1][0], [loads[0]])
+    loads.append(rows_of_group(load, 1) + inners[1, 0][3])
+    gain_sum = scatter_step(gain_sum + nought(loads[1][:1]), ctx_row, "ctx", bits[0])
+    both = jnp.concatenate([norms[g][sel][2] for sel in (1, 0) for g in groups], axis=0)
+    prv = shifted(both + nought(loads[1][:1]), 1)
+    inners[1, 1] = inner(1, 1, inners[1, 0][0], [loads[1]])
+    grad_q, token = inners[1, 1][0], inners[1, 1][3]
+    suffix, outers, grad_gain = [], [None] * 2, gain_sum
+    for g in groups:
+        before = more_hops(loads[g], rows_of_group(first, g), -1) + token
+        if g:
+            grad_gain = scatter_step(gain_sum + nought(before[:1]), ctx_row, "ctx", bits[1])
+        suffix.append(to_cores(core_row, before, late[g], -1))
+        outers = outer(0, g, outers[:2], [])
+        if g:
+            grad_gain = grad_gain + outers[2]
+        outers = outer(1, g, outers[:2], [])
+        token = outers[2]
     for bit in bits[2:]:
         grad_gain = scatter_step(grad_gain, ctx_row, "ctx", bit)
-    grad_k, grad_v, _ = outer(1, outers[:2], [])
     grad_gain = grad_gain.reshape(-1)
-    grad_q = inners[1][0]
+    grad_k, grad_v, _ = outers
     return output[None], grad_q[None], grad_k[None], grad_v[None], grad_gain
 
 

time: 71.9 us -> 76.3 us (1.061)
  Pallas kernels: 30.1 us -> 32.2 us
  starting transfers between devices: 29.6 us -> 31.7 us
    ppermute x7 -> x9, starting transfers between devices: 16.8 us -> 22.5 us  [shifted(): lax.ppermute(x, 'ctx', [(i, i + distance) for i in range(count) if 0 <= i...]
    ppermute x9 -> x12, starting transfers between devices: 12.8 us -> 9.16 us  [partner(): return lax.ppermute(x, axis, route)]
    pallas_call x10 -> x16, Pallas kernels: 30.1 us -> 32.2 us  [call(): pl.pallas_call(kernel, grid_spec=pltpu.PrefetchScalarGridSpec(num_scalar_...]
    ppermute x7 -> x9, waiting for transfers between devices: 6.77 us -> 6.07 us  [shifted(): lax.ppermute(x, 'ctx', [(i, i + distance) for i in range(count) if 0 <= i...]
    ppermute x9 -> x12, waiting for transfers between devices: 2.75 us -> 3.11 us  [partner(): return lax.ppermute(x, axis, route)]
  transfers between devices with their start and end apart: 16 -> 21, of which waited for: 6 -> 7; matrix products, arithmetic and copies ran while one was open for 1% -> 2% of each run, Pallas kernels for 35% -> 38%
where the time goes in v15:
time: 76.3 us; the launch traced here: 75.6 us
  Pallas kernels  32.2 us (42%)
  starting transfers between devices  31.7 us (42%)
  waiting for transfers between devices  9.19 us (12%)
  other arithmetic  1.45 us (2%)
  between operations  1.02 us (1%)
    pallas_call x16, Pallas kernels, call(): pl.pallas_call(kernel, grid_spec=pltpu.PrefetchScalarGridSpec(num_scalar_...  32.2 us
    ppermute x9, starting transfers between devices, shifted(): lax.ppermute(x, 'ctx', [(i, i + distance) for i in range(count) if 0 <= i...  22.5 us
    ppermute x12, starting transfers between devices, partner(): return lax.ppermute(x, axis, route)  9.16 us
    ppermute x9, waiting for transfers between devices, shifted(): lax.ppermute(x, 'ctx', [(i, i + distance) for i in range(count) if 0 <= i...  6.07 us
    ppermute x12, waiting for transfers between devices, partner(): return lax.ppermute(x, axis, route)  3.11 us
  transfers between devices with their start and end apart: 21, of which 7 were waited for; matrix products, arithmetic and copies ran while one was open for 2% of the time, Pallas kernels for 38%

profile of v15, /device:TPU:0, one launch (start us, length us, event | category | flops | bytes accessed | tf_op | source)
XLA Modules:
  0.0 75.6 jit_solution(7171689419116682875)
XLA Ops:
  0.7 2.4 %shard_map.110 = (f32[512,128]{1,0:T(8,128)S(1)}, f32[512,128]{1,0:T(8,128)S(1)}, s32[1,256]{1,0:T(1,128)S(1)}, bf16[256,2048]{1,0:T(8,128)(2,1)S(1)}, bf16[256,...) custom-call(s32[1]{0:T(128)} %bitcast.core, s32[1]{0:T(128)} %bitcast.3.ctx, ...), custom_call_target="tpu_custom_call" | custom-call | flops 1 | bytes 1 | tf_op jit(solution)/shard_map/pallas_call | solution.py:390
  4.8 4.9 %collective-permute-start.1 = (f32[512,128]{1,0:T(8,128)S(1)}, f32[512,128]{1,0:T(8,128)S(1)}, u32[]{:S(2)}, u32[]{:S(2)}) collective-permute-start(f32[512,128]{1,0:T(8,128)S(1)} %add.196.rest_0_), channel_id=1, source_target_pairs={{0,2},{1,3},{2,4},{3,5},{4,6},{5,7},{8,10},{9,11},{10,12},{11,13},... | collective-permute-start | bytes 786440 | tf_op jit(solution)/shard_map/ppermute | solution.py:290
  9.8 2.6 %shard_map.111 = (f32[2,264,128]{2,1,0:T(8,128)S(1)}, f32[2,264,128]{2,1,0:T(8,128)S(1)}, bf16[256,2048]{1,0:T(8,128)(2,1)S(1)}, bf16[256,2048]{1,0:T(8,128)(2,1)S(1)}, f32[1,128]{1,0:T(1,128)}) custom-call(s32[1]{0:T(128)} %bitcast.core, bf16[256,2048]{1,0:T(8,128)(2,1)} %bitcast.62, bf16[256,2048]{1,0:T(8,128)(2,1)} %bitcast.63, ...), custom_call_target="tpu_custom_call" | custom-call | flops 1 | bytes 1 | tf_op jit(solution)/shard_map/pallas_call | solution.py:390
  12.5 2.5 %shard_map.113 = (f32[256,1024]{1,0:T(8,128)S(1)}, bf16[16,256,256]{2,1,0:T(8,128)(2,1)S(1)}, f32[1,128]{1,0:T(1,128)S(1)}) custom-call(s32[1]{0:T(128)} %bitcast.core, bf16[256,2048]{1,0:T(8,128)(2,1)S(1)} %get-tuple-element.73.q, bf16[256,2048]{1,0:T(8,128)(2,1)S(1)} %get-tuple-element.69.k, bf16[256,2048]{1,0:T(8,128)(2,1)S(1)} %get-tuple-element.70.v, ...), custom_call_target="tpu_custom_call" | custom-call | flops 1 | bytes 1 | tf_op jit(solution)/shard_map/pallas_call | solution.py:390
  15.0 2.5 %shard_map.112 = (f32[256,1024]{1,0:T(8,128)S(1)}, bf16[16,256,256]{2,1,0:T(8,128)(2,1)S(1)}, f32[1,128]{1,0:T(1,128)S(1)}) custom-call(s32[1]{0:T(128)} %bitcast.core, bf16[256,2048]{1,0:T(8,128)(2,1)S(1)} %get-tuple-element.73.q, bf16[256,2048]{1,0:T(8,128)(2,1)S(1)} %get-tuple-element.69.k, bf16[256,2048]{1,0:T(8,128)(2,1)S(1)} %get-tuple-element.70.v, ...), custom_call_target="tpu_custom_call" | custom-call | flops 1 | bytes 1 | tf_op jit(solution)/shard_map/pallas_call | solution.py:390
  17.6 4.5 %collective-permute-start.3 = (f32[256,128]{1,0:T(8,128)S(1)}, f32[256,128]{1,0:T(8,128)S(1)}, u32[]{:S(2)}, u32[]{:S(2)}) collective-permute-start(f32[256,128]{1,0:T(8,128)S(1)} %get-tuple-element.148), channel_id=1, source_target_pairs={{0,4},{1,5},{2,6},{3,7},{8,12},{9,13},{10,14},{11,15},{16,20},{17,... | collective-permute-start | bytes 393224 | tf_op jit(solution)/shard_map/ppermute | solution.py:290
  24.7 5.2 %collective-permute-start.2 = (f32[256,128]{1,0:T(8,128)S(1)}, f32[256,128]{1,0:T(8,128)S(1)}, u32[]{:S(2)}, u32[]{:S(2)}) collective-permute-start(f32[256,128]{1,0:T(8,128)S(1)} %get-tuple-element.147), channel_id=1, source_target_pairs={{0,4},{1,5},{2,6},{3,7},{8,12},{9,13},{10,14},{11,15},{16,20},{17,... | collective-permute-start | bytes 393224 | tf_op jit(solution)/shard_map/ppermute | solution.py:290
  35.2 1.3 %shard_map.117 = (bf16[256,2048]{1,0:T(8,128)(2,1)}, bf16[256,512]{1,0:T(8,128)(2,1)S(1)}, f32[1,264,128]{2,1,0:T(8,128)S(1)}, f32[1,4,128]{2,1,0:T(4,128)S(1)},...) custom-call(s32[1]{0:T(128)} %bitcast.core, ...), custom_call_target="tpu_custom_call", output_to_operand_aliasing={{0}: (10, {})} | custom-call | flops 1 | bytes 1 | tf_op jit(solution)/shard_map/pallas_call | solution.py:390
  36.5 1.6 %collective-permute-start.16 = (f32[2,4,128]{2,1,0:T(4,128)S(1)}, f32[2,4,128]{2,1,0:T(4,128)S(1)}, u32[]{:S(2)}, u32[]{:S(2)}) collective-permute-start(f32[2,4,128]{2,1,0:T(4,128)S(1)} %fusion.7), channel_id=1, source_target_pairs={{0,8},{8,0},{16,24},{24,16},{1,9},{9,1},{17,25},{25,17},{2,10},{10... | collective-permute-start | bytes 12296 | tf_op jit(solution)/shard_map/ppermute | solution.py:285
  40.8 1.6 %collective-permute-start.17 = (f32[1,4,128]{2,1,0:T(4,128)S(1)}, f32[1,4,128]{2,1,0:T(4,128)S(1)}, u32[]{:S(2)}, u32[]{:S(2)}) collective-permute-start(f32[1,4,128]{2,1,0:T(4,128)S(1)} %slice_select_fusion), channel_id=1, source_target_pairs={{0,16},{8,24},{16,0},{24,8},{1,17},{9,25},{17,1},{25,9},{2,18},{10... | collective-permute-start | bytes 6152 | tf_op jit(solution)/shard_map/ppermute | solution.py:285
  42.4 2.8 %shard_map.118 = (bf16[256,2048]{1,0:T(8,128)(2,1)}, f32[256,512]{1,0:T(8,128)S(1)}, f32[256,512]{1,0:T(8,128)S(1)}, f32[1,128]{1,0:T(1,128)}) custom-call(s32[1]{0:T(128)} %bitcast.core, bf16[256,2048]{1,0:T(8,128)(2,1)S(1)} %get-tuple-element.73.q, bf16[256,2048]{1,0:T(8,128)(2,1)S(1)} %get-tuple-element.69.k, bf16[256,2048]{1,0:T(8,128)(2,1)S(1)} %get-tuple-element.70.v, ...), custom_call_target="tpu_custom_call" | custom-call | flops 1 | bytes 1 | tf_op jit(solution)/shard_map/pallas_call | solution.py:390
  45.2 2.8 %shard_map.119 = (bf16[256,2048]{1,0:T(8,128)(2,1)}, f32[256,512]{1,0:T(8,128)S(1)}, f32[256,512]{1,0:T(8,128)S(1)}, f32[1,128]{1,0:T(1,128)S(1)}) custom-call(s32[1]{0:T(128)} %bitcast.core, bf16[256,2048]{1,0:T(8,128)(2,1)S(1)} %get-tuple-element.73.q, bf16[256,2048]{1,0:T(8,128)(2,1)S(1)} %get-tuple-element.69.k, ...), custom_call_target="tpu_custom_call", output_to_operand_aliasing={{0}: (12, {})} | custom-call | flops 1 | bytes 1 | tf_op jit(solution)/shard_map/pallas_call | solution.py:390
  48.1 1.7 %collective-permute-done.10 = f32[512,128]{1,0:T(8,128)S(1)} collective-permute-done((f32[512,128]{1,0:T(8,128)S(1)}, f32[512,128]{1,0:T(8,128)S(1)}, u32[]{:S(2)}, u32[]{:S(2)}) %collective-permute-start.10) | collective-permute-done | bytes 262176 | tf_op jit(solution)/shard_map/ppermute | solution.py:290
  49.8 1.5 %collective-permute-start.12 = (f32[256,128]{1,0:T(8,128)S(1)}, f32[256,128]{1,0:T(8,128)S(1)}, u32[]{:S(2)}, u32[]{:S(2)}) collective-permute-start(f32[256,128]{1,0:T(8,128)S(1)} %slice.81.rest_0_), channel_id=1, source_target_pairs={{4,0},{5,1},{6,2},{7,3},{12,8},{13,9},{14,10},{15,11},{20,16},{21,... | collective-permute-start | bytes 393224 | tf_op jit(solution)/shard_map/ppermute | solution.py:290
  51.3 2.9 %shard_map.120 = (bf16[256,2048]{1,0:T(8,128)(2,1)}, f32[256,512]{1,0:T(8,128)S(1)}, f32[256,512]{1,0:T(8,128)S(1)}, f32[1,128]{1,0:T(1,128)S(1)}) custom-call(s32[1]{0:T(128)} %bitcast.core, bf16[256,2048]{1,0:T(8,128)(2,1)S(1)} %get-tuple-element.73.q, bf16[256,2048]{1,0:T(8,128)(2,1)S(1)} %get-tuple-element.69.k, ...), custom_call_target="tpu_custom_call", output_to_operand_aliasing={{0}: (12, {})} | custom-call | flops 1 | bytes 1 | tf_op jit(solution)/shard_map/pallas_call | solution.py:390
  55.5 1.3 %collective-permute-start.14 = (f32[4,264,128]{2,1,0:T(8,128)S(1)}, f32[4,264,128]{2,1,0:T(8,128)S(1)}, u32[]{:S(2)}, u32[]{:S(2)}) collective-permute-start(f32[4,264,128]{2,1,0:T(8,128)S(1)} %maximum_add_fusion), channel_id=1, source_target_pairs={{0,1},{1,2},{2,3},{3,4},{4,5},{5,6},{6,7},{8,9},{9,10},{10,11},{11... | collective-permute-start | bytes 1622024 | tf_op jit(solution)/shard_map/ppermute | solution.py:290
  56.9 2.9 %shard_map.121 = (bf16[256,2048]{1,0:T(8,128)(2,1)}, f32[256,512]{1,0:T(8,128)S(1)}, f32[256,512]{1,0:T(8,128)S(1)}, f32[1,128]{1,0:T(1,128)S(1)}) custom-call(s32[1]{0:T(128)} %bitcast.core, bf16[256,2048]{1,0:T(8,128)(2,1)S(1)} %get-tuple-element.73.q, bf16[256,2048]{1,0:T(8,128)(2,1)S(1)} %get-tuple-element.69.k, ...), custom_call_target="tpu_custom_call", output_to_operand_aliasing={{0}: (12, {})} | custom-call | flops 1 | bytes 1 | tf_op jit(solution)/shard_map/pallas_call | solution.py:390
  59.8 4.4 %collective-permute-done.12 = f32[256,128]{1,0:T(8,128)S(1)} collective-permute-done((f32[256,128]{1,0:T(8,128)S(1)}, f32[256,128]{1,0:T(8,128)S(1)}, u32[]{:S(2)}, u32[]{:S(2)}) %collective-permute-start.12) | collective-permute-done | bytes 131104 | tf_op jit(solution)/shard_map/ppermute | solution.py:290
  64.3 1.5 %collective-permute-start.18 = (f32[2,128]{1,0:T(2,128)S(1)}, f32[2,128]{1,0:T(2,128)S(1)}, u32[]{:S(2)}, u32[]{:S(2)}) collective-permute-start(f32[2,128]{1,0:T(2,128)S(1)} %broadcast_select_fusion.4), channel_id=1, source_target_pairs={{0,4},{1,5},{2,6},{3,7},{4,0},{5,1},{6,2},{7,3},{8,12},{9,13},{10,... | collective-permute-start | bytes 3080 | tf_op jit(solution)/shard_map/ppermute | solution.py:285
  65.8 1.4 %shard_map.122 = (bf16[256,2048]{1,0:T(8,128)(2,1)}, bf16[256,2048]{1,0:T(8,128)(2,1)}, f32[1,128]{1,0:T(1,128)}) custom-call(s32[1]{0:T(128)} %bitcast.core, bf16[256,2048]{1,0:T(8,128)(2,1)S(1)} %get-tuple-element.69.k, bf16[256,2048]{1,0:T(8,128)(2,1)S(1)} %get-tuple-element.70.v, f32[256,512]{1,0:T(8,128)S(1)} %get-tuple-element.113.gk_in, ...), custom_call_target="tpu_custom_call" | custom-call | flops 1 | bytes 1 | tf_op jit(solution)/shard_map/pallas_call | solution.py:390
  67.2 1.4 %shard_map.123 = (bf16[256,2048]{1,0:T(8,128)(2,1)}, bf16[256,2048]{1,0:T(8,128)(2,1)}, f32[1,128]{1,0:T(1,128)S(1)}) custom-call(s32[1]{0:T(128)} %bitcast.core, bf16[256,2048]{1,0:T(8,128)(2,1)S(1)} %get-tuple-element.69.k, bf16[256,2048]{1,0:T(8,128)(2,1)S(1)} %get-tuple-element.70.v, ...), custom_call_target="tpu_custom_call", output_to_operand_aliasing={{0}: (9, {}), {1}: (10, {})} | custom-call | flops 1 | bytes 1 | tf_op jit(solution)/shard_map/pallas_call | solution.py:390
  68.8 2.0 %collective-permute-start.19 = (f32[1,128]{1,0:T(1,128)S(1)}, f32[1,128]{1,0:T(1,128)S(1)}, u32[]{:S(2)}, u32[]{:S(2)}) collective-permute-start(f32[1,128]{1,0:T(1,128)S(1)} %compare_select_fusion), channel_id=1, source_target_pairs={{0,2},{1,3},{2,0},{3,1},{4,6},{5,7},{6,4},{7,5},{8,10},{9,11},{10,... | collective-permute-start | bytes 1544 | tf_op jit(solution)/shard_map/ppermute | solution.py:285
  70.8 1.4 %shard_map.124 = (bf16[256,2048]{1,0:T(8,128)(2,1)}, bf16[256,2048]{1,0:T(8,128)(2,1)}, f32[1,128]{1,0:T(1,128)S(1)}) custom-call(s32[1]{0:T(128)} %bitcast.core, bf16[256,2048]{1,0:T(8,128)(2,1)S(1)} %get-tuple-element.69.k, bf16[256,2048]{1,0:T(8,128)(2,1)S(1)} %get-tuple-element.70.v, ...), custom_call_target="tpu_custom_call", output_to_operand_aliasing={{0}: (9, {}), {1}: (10, {})} | custom-call | flops 1 | bytes 1 | tf_op jit(solution)/shard_map/pallas_call | solution.py:390
  74.2 1.4 %shard_map.125 = (bf16[256,2048]{1,0:T(8,128)(2,1)}, bf16[256,2048]{1,0:T(8,128)(2,1)}, f32[1,128]{1,0:T(1,128)}) custom-call(s32[1]{0:T(128)} %bitcast.core, bf16[256,2048]{1,0:T(8,128)(2,1)S(1)} %get-tuple-element.69.k, bf16[256,2048]{1,0:T(8,128)(2,1)S(1)} %get-tuple-element.70.v, ...), custom_call_target="tpu_custom_call", output_to_operand_aliasing={{0}: (9, {}), {1}: (10, {})} | custom-call | flops 1 | bytes 1 | tf_op jit(solution)/shard_map/pallas_call | solution.py:390
  (79 shorter events, 16.2 us)
Async XLA Ops:
  0.6 3.0 %copy-start = (s32[1,256]{1,0:T(1,128)S(1)}, s32[1,256]{1,0:T(1,128)}, u32[]{:S(2)}) copy-start(s32[1,256]{1,0:T(1,128)} %seg.25) | copy-start | bytes 3076
  0.6 2.9 %copy-start.2 = (s32[1,32]{1,0:T(1,128)S(1)}, s32[1,32]{1,0:T(1,128)}, u32[]{:S(2)}) copy-start(s32[1,32]{1,0:T(1,128)} %table.25) | copy-start | bytes 388
  3.1 1.7 %collective-permute-start = (f32[512,128]{1,0:T(8,128)S(1)}, f32[512,128]{1,0:T(8,128)S(1)}, u32[]{:S(2)}, u32[]{:S(2)}) collective-permute-start(f32[512,128]{1,0:T(8,128)S(1)} %get-tuple-element.72), channel_id=1, source_target_pairs={{0,1},{1,0},{2,3},{3,2},{4,5},{5,4},{6,7},{7,6},{8,9},{9,8},{10,11... | collective-permute-start | bytes 786440 | tf_op jit(solution)/shard_map/ppermute | solution.py:285
  4.8 12.7 %collective-permute-start.1 = (f32[512,128]{1,0:T(8,128)S(1)}, f32[512,128]{1,0:T(8,128)S(1)}, u32[]{:S(2)}, u32[]{:S(2)}) collective-permute-start(f32[512,128]{1,0:T(8,128)S(1)} %add.196.rest_0_), channel_id=1, source_target_pairs={{0,2},{1,3},{2,4},{3,5},{4,6},{5,7},{8,10},{9,11},{10,12},{11,13},... | collective-permute-start | bytes 786440 | tf_op jit(solution)/shard_map/ppermute | solution.py:290
  17.4 12.6 %copy-start.1 = (f32[2048]{0:T(1024)S(1)}, f32[2048]{0:T(1024)}, u32[]{:S(2)}) copy-start(f32[2048]{0:T(1024)} %param.13) | copy-start | bytes 24580
  17.6 12.4 %collective-permute-start.3 = (f32[256,128]{1,0:T(8,128)S(1)}, f32[256,128]{1,0:T(8,128)S(1)}, u32[]{:S(2)}, u32[]{:S(2)}) collective-permute-start(f32[256,128]{1,0:T(8,128)S(1)} %get-tuple-element.148), channel_id=1, source_target_pairs={{0,4},{1,5},{2,6},{3,7},{8,12},{9,13},{10,14},{11,15},{16,20},{17,... | collective-permute-start | bytes 393224 | tf_op jit(solution)/shard_map/ppermute | solution.py:290
  22.1 8.0 %collective-permute-start.6 = (f32[2,264,128]{2,1,0:T(8,128)S(1)}, f32[2,264,128]{2,1,0:T(8,128)S(1)}, u32[]{:S(2)}, u32[]{:S(2)}) collective-permute-start(f32[2,264,128]{2,1,0:T(8,128)S(1)} %get-tuple-element.163), channel_id=1, source_target_pairs={{1,0},{2,1},{3,2},{4,3},{5,4},{6,5},{7,6},{9,8},{10,9},{11,10},{12... | collective-permute-start | bytes 811016 | tf_op jit(solution)/shard_map/ppermute | solution.py:290
  23.4 8.0 %collective-permute-start.5 = (f32[2,264,128]{2,1,0:T(8,128)S(1)}, f32[2,264,128]{2,1,0:T(8,128)S(1)}, u32[]{:S(2)}, u32[]{:S(2)}) collective-permute-start(f32[2,264,128]{2,1,0:T(8,128)S(1)} %get-tuple-element.164), channel_id=1, source_target_pairs={{1,0},{2,1},{3,2},{4,3},{5,4},{6,5},{7,6},{9,8},{10,9},{11,10},{12... | collective-permute-start | bytes 811016 | tf_op jit(solution)/shard_map/ppermute | solution.py:290
  24.7 8.0 %collective-permute-start.2 = (f32[256,128]{1,0:T(8,128)S(1)}, f32[256,128]{1,0:T(8,128)S(1)}, u32[]{:S(2)}, u32[]{:S(2)}) collective-permute-start(f32[256,128]{1,0:T(8,128)S(1)} %get-tuple-element.147), channel_id=1, source_target_pairs={{0,4},{1,5},{2,6},{3,7},{8,12},{9,13},{10,14},{11,15},{16,20},{17,... | collective-permute-start | bytes 393224 | tf_op jit(solution)/shard_map/ppermute | solution.py:290
  30.0 1.4 %collective-permute-start.4 = (f32[256,128]{1,0:T(8,128)S(1)}, f32[256,128]{1,0:T(8,128)S(1)}, u32[]{:S(2)}, u32[]{:S(2)}) collective-permute-start(f32[256,128]{1,0:T(8,128)S(1)} %get-tuple-element.146), channel_id=1, source_target_pairs={{0,1},{1,0},{2,3},{3,2},{4,5},{5,4},{6,7},{7,6},{8,9},{9,8},{10,11... | collective-permute-start | bytes 393224 | tf_op jit(solution)/shard_map/ppermute | solution.py:285
  32.8 2.4 %collective-permute-start.7 = (f32[256,128]{1,0:T(8,128)S(1)}, f32[256,128]{1,0:T(8,128)S(1)}, u32[]{:S(2)}, u32[]{:S(2)}) collective-permute-start(f32[256,128]{1,0:T(8,128)S(1)} %get-tuple-element.144), channel_id=1, source_target_pairs={{0,1},{1,0},{2,3},{3,2},{4,5},{5,4},{6,7},{7,6},{8,9},{9,8},{10,11... | collective-permute-start | bytes 393224 | tf_op jit(solution)/shard_map/ppermute | solution.py:285
  33.8 4.4 %collective-permute-start.8 = (f32[256,128]{1,0:T(8,128)S(1)}, f32[256,128]{1,0:T(8,128)S(1)}, u32[]{:S(2)}, u32[]{:S(2)}) collective-permute-start(f32[256,128]{1,0:T(8,128)S(1)} %get-tuple-element.92), channel_id=1, source_target_pairs={{0,1},{1,0},{2,3},{3,2},{4,5},{5,4},{6,7},{7,6},{8,9},{9,8},{10,11... | collective-permute-start | bytes 393224 | tf_op jit(solution)/shard_map/ppermute | solution.py:285
  36.5 4.3 %collective-permute-start.16 = (f32[2,4,128]{2,1,0:T(4,128)S(1)}, f32[2,4,128]{2,1,0:T(4,128)S(1)}, u32[]{:S(2)}, u32[]{:S(2)}) collective-permute-start(f32[2,4,128]{2,1,0:T(4,128)S(1)} %fusion.7), channel_id=1, source_target_pairs={{0,8},{8,0},{16,24},{24,16},{1,9},{9,1},{17,25},{25,17},{2,10},{10... | collective-permute-start | bytes 12296 | tf_op jit(solution)/shard_map/ppermute | solution.py:285
  38.1 1.3 %collective-permute-start.9 = (f32[256,128]{1,0:T(8,128)S(1)}, f32[256,128]{1,0:T(8,128)S(1)}, u32[]{:S(2)}, u32[]{:S(2)}) collective-permute-start(f32[256,128]{1,0:T(8,128)S(1)} %get-tuple-element.93), channel_id=1, source_target_pairs={{0,1},{1,0},{2,3},{3,2},{4,5},{5,4},{6,7},{7,6},{8,9},{9,8},{10,11... | collective-permute-start | bytes 393224 | tf_op jit(solution)/shard_map/ppermute | solution.py:285
  39.5 10.3 %collective-permute-start.10 = (f32[512,128]{1,0:T(8,128)S(1)}, f32[512,128]{1,0:T(8,128)S(1)}, u32[]{:S(2)}, u32[]{:S(2)}) collective-permute-start(f32[512,128]{1,0:T(8,128)S(1)} %pad_maximum_fusion.rest_0_), channel_id=1, source_target_pairs={{2,0},{3,1},{4,2},{5,3},{6,4},{7,5},{10,8},{11,9},{12,10},{13,11},... | collective-permute-start | bytes 786440 | tf_op jit(solution)/shard_map/ppermute | solution.py:290
  40.8 16.1 %collective-permute-start.17 = (f32[1,4,128]{2,1,0:T(4,128)S(1)}, f32[1,4,128]{2,1,0:T(4,128)S(1)}, u32[]{:S(2)}, u32[]{:S(2)}) collective-permute-start(f32[1,4,128]{2,1,0:T(4,128)S(1)} %slice_select_fusion), channel_id=1, source_target_pairs={{0,16},{8,24},{16,0},{24,8},{1,17},{9,25},{17,1},{25,9},{2,18},{10... | collective-permute-start | bytes 6152 | tf_op jit(solution)/shard_map/ppermute | solution.py:285
  49.8 14.4 %collective-permute-start.12 = (f32[256,128]{1,0:T(8,128)S(1)}, f32[256,128]{1,0:T(8,128)S(1)}, u32[]{:S(2)}, u32[]{:S(2)}) collective-permute-start(f32[256,128]{1,0:T(8,128)S(1)} %slice.81.rest_0_), channel_id=1, source_target_pairs={{4,0},{5,1},{6,2},{7,3},{12,8},{13,9},{14,10},{15,11},{20,16},{21,... | collective-permute-start | bytes 393224 | tf_op jit(solution)/shard_map/ppermute | solution.py:290
  54.2 14.4 %collective-permute-start.11 = (f32[256,128]{1,0:T(8,128)S(1)}, f32[256,128]{1,0:T(8,128)S(1)}, u32[]{:S(2)}, u32[]{:S(2)}) collective-permute-start(f32[256,128]{1,0:T(8,128)S(1)} %slice_add_fusion.2.rest_0_), channel_id=1, source_target_pairs={{4,0},{5,1},{6,2},{7,3},{12,8},{13,9},{14,10},{15,11},{20,16},{21,... | collective-permute-start | bytes 393224 | tf_op jit(solution)/shard_map/ppermute | solution.py:290
  55.5 10.3 %collective-permute-start.14 = (f32[4,264,128]{2,1,0:T(8,128)S(1)}, f32[4,264,128]{2,1,0:T(8,128)S(1)}, u32[]{:S(2)}, u32[]{:S(2)}) collective-permute-start(f32[4,264,128]{2,1,0:T(8,128)S(1)} %maximum_add_fusion), channel_id=1, source_target_pairs={{0,1},{1,2},{2,3},{3,4},{4,5},{5,6},{6,7},{8,9},{9,10},{10,11},{11... | collective-permute-start | bytes 1622024 | tf_op jit(solution)/shard_map/ppermute | solution.py:290
  64.2 3.0 %collective-permute-start.13 = (f32[256,128]{1,0:T(8,128)S(1)}, f32[256,128]{1,0:T(8,128)S(1)}, u32[]{:S(2)}, u32[]{:S(2)}) collective-permute-start(f32[256,128]{1,0:T(8,128)S(1)} %get-tuple-element.142), channel_id=1, source_target_pairs={{0,1},{1,0},{2,3},{3,2},{4,5},{5,4},{6,7},{7,6},{8,9},{9,8},{10,11... | collective-permute-start | bytes 393224 | tf_op jit(solution)/shard_map/ppermute | solution.py:285
  64.3 4.5 %collective-permute-start.18 = (f32[2,128]{1,0:T(2,128)S(1)}, f32[2,128]{1,0:T(2,128)S(1)}, u32[]{:S(2)}, u32[]{:S(2)}) collective-permute-start(f32[2,128]{1,0:T(2,128)S(1)} %broadcast_select_fusion.4), channel_id=1, source_target_pairs={{0,4},{1,5},{2,6},{3,7},{4,0},{5,1},{6,2},{7,3},{8,12},{9,13},{10,... | collective-permute-start | bytes 3080 | tf_op jit(solution)/shard_map/ppermute | solution.py:285
  68.8 3.6 %collective-permute-start.19 = (f32[1,128]{1,0:T(1,128)S(1)}, f32[1,128]{1,0:T(1,128)S(1)}, u32[]{:S(2)}, u32[]{:S(2)}) collective-permute-start(f32[1,128]{1,0:T(1,128)S(1)} %compare_select_fusion), channel_id=1, source_target_pairs={{0,2},{1,3},{2,0},{3,1},{4,6},{5,7},{6,4},{7,5},{8,10},{9,11},{10,... | collective-permute-start | bytes 1544 | tf_op jit(solution)/shard_map/ppermute | solution.py:285
  72.5 1.1 %collective-permute-start.20 = (f32[1,64]{1,0:T(1,128)S(1)}, f32[1,64]{1,0:T(1,128)S(1)}, u32[]{:S(2)}, u32[]{:S(2)}) collective-permute-start(f32[1,64]{1,0:T(1,128)S(1)} %slice_select_fusion.1), channel_id=1, source_target_pairs={{0,1},{1,0},{2,3},{3,2},{4,5},{5,4},{6,7},{7,6},{8,9},{9,8},{10,11... | collective-permute-start | bytes 776 | tf_op jit(solution)/shard_map/ppermute | solution.py:285
  72.6 1.7 %collective-permute-start.15 = (f32[256,128]{1,0:T(8,128)S(1)}, f32[256,128]{1,0:T(8,128)S(1)}, u32[]{:S(2)}, u32[]{:S(2)}) collective-permute-start(f32[256,128]{1,0:T(8,128)S(1)} %add_select_fusion.1), channel_id=1, source_target_pairs={{0,1},{1,0},{2,3},{3,2},{4,5},{5,4},{6,7},{7,6},{8,9},{9,8},{10,11... | collective-permute-start | bytes 393224 | tf_op jit(solution)/shard_map/ppermute | solution.py:285

commit v16 on v13

--- a/solution.py
+++ b/solution.py
@@ -103,11 +103,21 @@
     return group, base, base + (group + half) * lanes, base // PAIR * E
 
 
-def states_kernel(core, ctx, dp, k_in, v_in, keep, send, zero, k, v, core_row, ctx_row, dp_row, sems):
+def put_half(sel, core, k, v, out):
+    lanes = k.shape[1] // GROUPS // 2
+    count = lanes // PAIR
+    for group in range(GROUPS):
+        base = (2 * group + (sel + core[0]) % 2) * lanes
+        for p in range(count):
+            at = lanes_at(base, p)
+            row = (group * count + p) * E
+            out[row:row + E] = state_pair(k[:, at], v[:, at])
+
+
+def send_kernel(core, ctx, dp, k_in, v_in, send, zero, k, v, core_row, ctx_row, dp_row, sems):
     for row, index in ((core_row, core), (ctx_row, ctx), (dp_row, dp)):
         row[...] = jnp.full(row.shape, index[0], jnp.int32)
     lanes = k.shape[1] // GROUPS // 2
-    count = lanes // PAIR
     copies = []
     for sel in (1, 0):
         for group in range(GROUPS):
@@ -118,19 +128,19 @@
     for copy in copies:
         copy.start()
     zero[...] = jnp.zeros_like(zero)
-    for sel, out in ((1, send), (0, keep)):
-        for group in range(GROUPS):
-            copies.pop(0).wait()
-            copies.pop(0).wait()
-            base = (2 * group + (sel + core[0]) % 2) * lanes
-            for p in range(count):
-                at = lanes_at(base, p)
-                row = (group * count + p) * E
-                out[row:row + E] = state_pair(k[:, at], v[:, at])
+    for copy in copies[:2 * GROUPS]:
+        copy.wait()
+    put_half(1, core, k, v, send)
+    for copy in copies[2 * GROUPS:]:
+        copy.wait()
+
+
+def keep_kernel(core, k, v, *rest):
+    put_half(0, core, k, v, rest[-1])
 
 
 def part_kernel(core, q_in, dy_in, k, v, seg, table, *rest):
-    *outs, q, dy, token, sems = rest[-6:]
+    out, q, dy, token, sems = rest[-5:]
     copies = [pltpu.make_async_copy(a, b, sems.at[i]) for i, (a, b) in enumerate(((q_in, q), (dy_in, dy)))]
     for copy in copies:
         copy.start()
@@ -139,13 +149,14 @@
     count = lanes // PAIR
     rows, own, _ = edge(seg, table, False)
     keep = rows.astype(BF16)
-    for sel, out in enumerate(outs):
+    for sel in range(2):
         for group in range(GROUPS):
             base = (2 * group + (sel + core[0]) % 2) * lanes
+            place_at = (1 - sel) * GROUPS + group
             for p in range(count):
                 at = lanes_at(base, p)
-                out[group, p * E:(p + 1) * E] = state_pair(k[:, at], v[:, at] * keep)
-            out[group, count * E:] = jnp.broadcast_to(own, (EXTRA, PAIR))
+                out[place_at, p * E:(p + 1) * E] = state_pair(k[:, at], v[:, at] * keep)
+            out[place_at, count * E:] = jnp.broadcast_to(own, (EXTRA, PAIR))
     for copy in copies:
         copy.wait()
 
@@ -198,12 +209,13 @@
     return rows.astype(F32) * met.astype(F32)
 
 
-def norm_kernel(sel, core, q, dy, local, gain, seg, table, prefix, nxt, *rest):
+def norm_kernel(sel, group, core, q, dy, local, gain, seg, table, prefix, nxt, *rest):
     out, dab, part, gsum, total, token = rest[-6:]
     token[...] = jnp.zeros_like(token)
     lanes = out.shape[1]
     count = lanes // PAIR
-    _, base, wide, row = place(sel, core, lanes, 1)
+    base = group * lanes
+    wide = base + (group + (sel + core[0]) % 2) * lanes
     on_next = on_rows(seg, table, True, nxt)
     last, own, flag = edge(seg, table, True)
     last = (last.astype(F32) * jnp.where(flag == 1, 1.0, 0.0)).astype(BF16)
@@ -211,7 +223,7 @@
     bases = [lanes_at(base, p) for p in range(count)]
     wides = [lanes_at(wide, p) for p in range(count)]
     fars = [
-        dot(twice(q[:, at]), side_by_side(prefix[rows_at(row, p)], nxt[0, rows_at(0, p)]), 1, 0)
+        dot(twice(q[:, at]), side_by_side(prefix[rows_at(0, p)], nxt[0, rows_at(0, p)]), 1, 0)
         for p, at in enumerate(wides)
     ]
     attns = [local[:, at] + far[:, :PAIR] + on_next * far[:, PAIR:] for at, far in zip(bases, fars)]
@@ -227,14 +239,14 @@
     states = [state_pair(q[:, at], jnp.concatenate([da, da * last], axis=1)) for at, da in zip(wides, das)]
     part[0, count * E:] = jnp.broadcast_to(own, (EXTRA, PAIR))
     for p, (at, normed, da) in enumerate(zip(pairs, normeds, das)):
-        total[rows_at(row, p)] = states[p][:, :PAIR]
+        total[p * E:(p + 1) * E] = states[p][:, :PAIR]
         part[0, p * E:(p + 1) * E] = states[p][:, PAIR:]
         dab[:, bases[p]] = da
         out[:, at] = (normed * gain[:, at]).astype(BF16)
         gsum[0, p:p + 1] = jnp.sum(dy[:, wides[p]].astype(F32) * normed, axis=0, keepdims=True)
 
 
-def inner_kernel(sel, core, q, k, v, dab, probs, mask, seg, table, prefix, nxt, *rest):
+def inner_kernel(sel, core, q, k, v, dab, probs, mask, seg, table, prefix_a, prefix_b, nxt, *rest):
     gq, gk, gv, token = rest[-4:]
     lanes = dab.shape[1] // GROUPS
     count = lanes // SUB // PAIR
@@ -247,7 +259,7 @@
         at = lanes_at(wide, p)
         da = dab[:, lanes_at(base, p)]
         vp = v[:, at]
-        far = dot(twice(da), stacked(prefix[rows_at(row, p)], nxt[0, rows_at(first, p)]), 1, 1)
+        far = dot(twice(da), stacked(jnp.where(group == 0, prefix_a[rows_at(first, p)], prefix_b[rows_at(first, p)]), nxt[0, rows_at(first, p)]), 1, 1)
         tq = far[:, :PAIR] + on_next * far[:, PAIR:]
         tk = tv = None
         for h, (qh, kh, dh) in enumerate(zip(heads_of(q[:, at]), heads_of(k[:, at]), heads_of(da))):
@@ -327,29 +339,36 @@
     half_rows = lanes // PAIR * E
     heads = lanes // E
 
-    def call(kernel, sel, ins, outs, after=(), alias=(), scratch=(), sub=1, steps=None, scalars=None):
+    def call(kernel, sel, ins, outs, group=None, after=(), alias=(), scratch=(), sub=1, steps=None, scalars=None):
         scalars = scalars or [core]
 
+        def group_at(i):
+            return i // sub if group is None else group
+
         def wide(i, c, *_):
-            return (0, (i // sub * 2 + (sel + c[0]) % 2) * sub + i % sub)
+            return (0, (2 * group_at(i) + (sel + c[0]) % 2) * sub + i % sub)
 
         def whole(*args):
             return (0, 0)
 
         def part(i, c, *_):
-            return (i // sub, 0, 0)
+            return (sel * GROUPS + group_at(i), 0, 0)
+
+        def single(*args):
+            return (0, 0, 0)
 
         specs = {
             "vmem": pl.BlockSpec(memory_space=pltpu.VMEM),
             "hbm": pl.BlockSpec(memory_space=pltpu.HBM),
             "wide": pl.BlockSpec((rows, lanes // sub), wide),
             "row": pl.BlockSpec((1, lanes // sub), wide),
-            "sums": pl.BlockSpec((1, lanes // PAIR, PAIR), part),
+            "sums": pl.BlockSpec((1, lanes // PAIR, PAIR), single),
             "zero": pl.BlockSpec((1, rows), whole),
             "all": pl.BlockSpec((GROUPS * half_rows, PAIR), whole),
             "part": pl.BlockSpec((1, half_rows + EXTRA, PAIR), part),
-            "later": pl.BlockSpec((1, half_rows + EXTRA, PAIR), lambda i, *_: (GROUPS + i // sub, 0, 0)),
-            "parts": pl.BlockSpec((GROUPS, half_rows + EXTRA, PAIR), lambda *args: (0, 0, 0)),
+            "one": pl.BlockSpec((1, half_rows + EXTRA, PAIR), single),
+            "half": pl.BlockSpec((half_rows, PAIR), whole),
+            "parts": pl.BlockSpec((2 * GROUPS, half_rows + EXTRA, PAIR), lambda *args: (0, 0, 0)),
             "seg": pl.BlockSpec((1, rows), whole),
             "table": pl.BlockSpec((1, table.shape[0]), whole),
             "mask": pl.BlockSpec((rows, rows), whole),
@@ -360,11 +379,13 @@
         }
         shapes = {
             "wide": (rows, width),
-            "sums": (GROUPS, lanes // PAIR, PAIR),
+            "sums": (1, lanes // PAIR, PAIR),
+            "one": (1, half_rows + EXTRA, PAIR),
+            "half": (half_rows, PAIR),
             "zero": (1, rows),
             "all": (GROUPS * half_rows, PAIR),
             "part": (GROUPS, half_rows + EXTRA, PAIR),
-            "parts": (GROUPS, half_rows + EXTRA, PAIR),
+            "parts": (2 * GROUPS, half_rows + EXTRA, PAIR),
             "token": (1, PAIR),
         }
         spaces = {"vmem": pltpu.VMEM, "hbm": pltpu.HBM}
@@ -374,8 +395,9 @@
         for out_at, x in alias:
             if x is not None:
                 aliases[len(scalars) + len(operands)] = out_at
-                operands.append(x)
-                kinds.append("any")
+                in_vmem = outs[out_at][0] == "vmem"
+                operands.append(pinned(x, pltpu.VMEM) if in_vmem else x)
+                kinds.append("vmem" if in_vmem else "any")
         out_shape = [
             pltpu.VMEM(*shape, dtype) if kind == "vmem" else jax.ShapeDtypeStruct(shapes[kind], dtype)
             for kind, dtype, *shape in outs
@@ -384,7 +406,7 @@
             kernel,
             grid_spec=pltpu.PrefetchScalarGridSpec(
                 num_scalar_prefetch=len(scalars),
-                grid=steps or (GROUPS * sub,),
+                grid=steps or ((GROUPS if group is None else 1) * sub,),
                 in_specs=[specs[kind] for kind in kinds],
                 out_specs=[specs[kind] for kind, *_ in outs],
                 scratch_shapes=scratch,
@@ -398,6 +420,7 @@
     edges = [("seg", segment_ids), ("table", image_flags)]
     chips = lax.axis_size("ctx") // 2
     whole, part_of = (rows, width), (rows, width // 2)
+    groups = range(GROUPS)
 
     def local_attn(sel, after):
         return call(
@@ -405,19 +428,19 @@
             [("vmem", q), ("vmem", k), ("vmem", v), ("mask", mask), ("mask", mask_t)],
             [("vmem", F32, part_of), ("vmem", BF16, (GROUPS * heads, rows, rows)), ("token", F32)], after=after)
 
-    def norm(sel, before, after):
+    def norm(sel, g, before, after):
         return call(
-            functools.partial(norm_kernel, sel), sel,
+            functools.partial(norm_kernel, sel, g), sel,
             [("vmem", q), ("vmem", dy), ("vmem", local[sel][0]), ("row", gain_row), *edges,
-             ("all", prefix[sel]), ("part", nxt[sel])],
-            [("wide", BF16), ("vmem", BF16, part_of), ("part", F32), ("sums", F32), ("all", F32), ("token", F32)],
-            after=after, alias=[(0, before)])
+             ("half", prefix[g][sel]), ("part", nxt)],
+            [("wide", BF16), ("vmem", BF16, part_of), ("one", F32), ("sums", F32), ("half", F32), ("token", F32)],
+            group=g, after=after, alias=list(enumerate(before)))
 
     def inner(sel, before, after):
         return call(
             functools.partial(inner_kernel, sel), sel,
-            [("vmem", q), ("vmem", k), ("vmem", v), ("vmem", norms[sel][1]), ("vmem", local[sel][1]), ("mask", mask),
-             *edges, ("all", prefix[sel]), ("part", nxt[sel])],
+            [("vmem", q), ("vmem", k), ("vmem", v), ("vmem", norms[sel][-1][1]), ("vmem", local[sel][1]),
+             ("mask", mask), *edges, *[("half", p[sel]) for p in prefix], ("part", nxt)],
             [("wide", BF16), ("vmem", F32, part_of), ("vmem", F32, part_of), ("token", F32)],
             after=after, alias=[(0, before)], sub=SUB)
 
@@ -425,7 +448,7 @@
         return call(
             functools.partial(outer_kernel, sel), sel,
             [("vmem", k), ("vmem", v), ("vmem", inners[sel][1]), ("vmem", inners[sel][2]), *edges,
-             ("all", suffix[sel]), ("later" if sel else "part", prv[0])],
+             ("all", suffix[sel]), ("part", prv[0])],
             [("wide", BF16), ("wide", BF16), ("token", F32)], after=after, alias=list(enumerate(before)), sub=SUB)
 
     def summed_before(own, towards, works):
@@ -441,11 +464,12 @@
             before = before + work(load)
         return before
 
-    keep, send, zero, k, v, core_row, ctx_row, dp_row = call(
-        states_kernel, 0, [("hbm", k), ("hbm", v)],
-        [("all", F32), ("all", F32), ("zero", jnp.int32), ("vmem", BF16, whole), ("vmem", BF16, whole)]
+    send, zero, k, v, core_row, ctx_row, dp_row = call(
+        send_kernel, 0, [("hbm", k), ("hbm", v)],
+        [("all", F32), ("zero", jnp.int32), ("vmem", BF16, whole), ("vmem", BF16, whole)]
         + [("token", jnp.int32)] * 3,
         scratch=[pltpu.SemaphoreType.DMA((2 * GROUPS, 2))], steps=(1,), scalars=[core, ctx, dp])
+    keep, = call(keep_kernel, 0, [("vmem", k), ("vmem", v)], [("all", F32)], steps=(1,))
     piece = within_chip(keep, send)
     seg = (segment_ids + zero)[0]
     onehot = seg[:, None] == jnp.arange(table.shape[0], dtype=jnp.int32)[None, :]
@@ -457,30 +481,37 @@
 
     parts = call(
         part_kernel, 0, [("hbm", q), ("hbm", dy), ("vmem", k), ("vmem", v), *edges],
-        [("parts", F32)] * 2 + [("vmem", BF16, whole), ("vmem", BF16, whole), ("token", F32)],
+        [("parts", F32)] + [("vmem", BF16, whole), ("vmem", BF16, whole), ("token", F32)],
         after=[piece[2]], scratch=[pltpu.SemaphoreType.DMA((2,))], steps=(1,))
-    *parts, q, dy, _ = parts
-    local, nxt = [], []
-
-    def first_work(load):
-        *made, token = local_attn(0, [parts[0]])
-        local.append(made)
-        return token
-
-    def second_work(load):
-        for part in reversed(parts):
-            nxt.append(shifted(part + nought(load[:1]), -1))
-        *made, token = local_attn(1, [load])
-        local.append(made)
-        return token
-
-    before = summed_before(piece[2], 1, [first_work, second_work])
-    prefix = to_cores(core_row, before, piece, 1)
-    norms = [norm(0, None, [])]
-    norms.append(norm(1, norms[0][0], [norms[0][4]]))
-    output = norms[1][0]
-    piece = within_chip(norms[0][4], norms[1][4])
-    gain_sum = [jnp.concatenate([jnp.where(core_row == half, norms[0][3], norms[1][3]) for half in range(2)], axis=0)]
+    parts, q, dy, _ = parts
+
+    def rows_of_group(x, g):
+        return x[g * half_rows:(g + 1) * half_rows]
+
+    local = [local_attn(0, [parts])]
+    local.append(local_attn(1, [parts]))
+    first = shifted(piece[2], 2) + local[0][2] + local[1][2]
+    load = piece[2] + first
+    nxt = shifted(parts + nought(load[:1]), -1)
+    prefix, norms, before = [], [[], []], [None] * 2
+    output, token = None, None
+    for g in groups:
+        summed, load_g, span = rows_of_group(first, g), rows_of_group(load, g), 2
+        while span < chips:
+            arrived = shifted(load_g, 2 * span)
+            summed, load_g = summed + arrived, load_g + arrived
+            span *= 2
+        if g:
+            summed = summed + token
+        prefix.append(to_cores(core_row, summed, [rows_of_group(x, g) for x in piece], 1))
+        for sel in range(2):
+            made = norm(sel, g, [output, before[sel]], [])
+            norms[sel].append(made)
+            output, before[sel], token = made[0], made[1], made[5]
+    piece = within_chip(*[jnp.concatenate([n[4] for n in norms[sel]], axis=0) for sel in range(2)])
+
+    gain_sum = [jnp.concatenate(
+        [jnp.where(core_row == half, norms[0][g][3], norms[1][g][3]) for half in range(2) for g in groups], axis=0)]
     gain_sum.append(scatter_step(gain_sum[-1], dp_row, "dp", 0))
     bits = list(reversed(range(lax.axis_size("ctx").bit_length() - 1)))
     inners, prv = [], []
@@ -493,7 +524,7 @@
 
     def fourth_work(load):
         gain_sum.append(scatter_step(gain_sum[-1] + nought(load[:1]), ctx_row, "ctx", bits[0]))
-        both = jnp.concatenate([norms[1][2], norms[0][2]], axis=0) + nought(load[:1])
+        both = jnp.concatenate([n[2] for n in norms[1] + norms[0]], axis=0) + nought(load[:1])
         prv.append(shifted(both, 1))
         inners.append(inner(1, inners[0][0], [load]))
         return inners[1][3]

time: 71.9 us -> 72.4 us (level)
  starting transfers between devices: 29.6 us -> 31.6 us
  waiting for transfers between devices: 9.52 us -> 7.76 us
    ppermute x7, waiting for transfers between devices: 6.77 us -> 5.5 us  [shifted(): lax.ppermute(x, 'ctx', [(i, i + distance) for i in range(count) if 0 <= i...]
    ppermute x9 -> x10, starting transfers between devices: 12.8 us -> 13.8 us  [partner(): return lax.ppermute(x, axis, route)]
    ppermute x7, starting transfers between devices: 16.8 us -> 17.7 us  [shifted(): lax.ppermute(x, 'ctx', [(i, i + distance) for i in range(count) if 0 <= i...]
    ppermute x9 -> x10, waiting for transfers between devices: 2.75 us -> 2.26 us  [partner(): return lax.ppermute(x, axis, route)]
    pallas_call x10 -> x13, Pallas kernels: 30.1 us -> 30.2 us  [call(): pl.pallas_call(kernel, grid_spec=pltpu.PrefetchScalarGridSpec(num_scalar_...]
  transfers between devices with their start and end apart: 16 -> 17, of which waited for: 6 -> 5; matrix products, arithmetic and copies ran while one was open for 1% -> 1% of each run, Pallas kernels for 35% -> 38%
where the time goes in v16:
time: 72.4 us; the launch traced here: 72 us
  starting transfers between devices  31.6 us (44%)
  Pallas kernels  30.2 us (42%)
  waiting for transfers between devices  7.76 us (11%)
  other arithmetic  1.4 us (2%)
  between operations  1.05 us (1%)
    pallas_call x13, Pallas kernels, call(): pl.pallas_call(kernel, grid_spec=pltpu.PrefetchScalarGridSpec(num_scalar_...  30.2 us
    ppermute x7, starting transfers between devices, shifted(): lax.ppermute(x, 'ctx', [(i, i + distance) for i in range(count) if 0 <= i...  17.7 us
    ppermute x10, starting transfers between devices, partner(): return lax.ppermute(x, axis, route)  13.8 us
    ppermute x7, waiting for transfers between devices, shifted(): lax.ppermute(x, 'ctx', [(i, i + distance) for i in range(count) if 0 <= i...  5.5 us
    ppermute x10, waiting for transfers between devices, partner(): return lax.ppermute(x, axis, route)  2.26 us
  transfers between devices with their start and end apart: 17, of which 5 were waited for; matrix products, arithmetic and copies ran while one was open for 1% of the time, Pallas kernels for 38%

profile of v16, /device:TPU:0, one launch (start us, length us, event | category | flops | bytes accessed | tf_op | source)
XLA Modules:
  0.0 72.0 jit_solution(12630943415685805718)
XLA Ops:
  0.7 1.8 %shard_map.110 = (f32[512,128]{1,0:T(8,128)S(1)}, s32[1,256]{1,0:T(1,128)S(1)}, bf16[256,2048]{1,0:T(8,128)(2,1)S(1)}, bf16[256,2048]{1,0:T(8,128)(2,1)S(1)}, s3...) custom-call(s32[1]{0:T(128)} %bitcast.core, s32[1]{0:T(128)} %bitcast.3.ctx, s32[1]{0:T(128)} %bitcast.4.dp, ...), custom_call_target="tpu_custom_call" | custom-call | flops 1 | bytes 1 | tf_op jit(solution)/shard_map/pallas_call | solution.py:405
  4.1 4.9 %collective-permute-start.1 = (f32[512,128]{1,0:T(8,128)S(1)}, f32[512,128]{1,0:T(8,128)S(1)}, u32[]{:S(2)}, u32[]{:S(2)}) collective-permute-start(f32[512,128]{1,0:T(8,128)S(1)} %add.158.rest_0_), channel_id=1, source_target_pairs={{0,2},{1,3},{2,4},{3,5},{4,6},{5,7},{8,10},{9,11},{10,12},{11,13},... | collective-permute-start | bytes 786440 | tf_op jit(solution)/shard_map/ppermute | solution.py:302
  9.2 2.6 %shard_map.112 = (f32[4,264,128]{2,1,0:T(8,128)S(1)}, bf16[256,2048]{1,0:T(8,128)(2,1)S(1)}, bf16[256,2048]{1,0:T(8,128)(2,1)S(1)}, f32[1,128]{1,0:T(1,128)}) custom-call(s32[1]{0:T(128)} %bitcast.core, bf16[256,2048]{1,0:T(8,128)(2,1)} %bitcast.57, bf16[256,2048]{1,0:T(8,128)(2,1)} %bitcast.58, bf16[256,2048]{1,0:T(8,128)(2,1)S(1)} %get-tuple-element.55.k, ...), custom_call_target="tpu_custom_call" | custom-call | flops 1 | bytes 1 | tf_op jit(solution)/shard_map/pallas_call | solution.py:405
  11.8 2.5 %shard_map.113 = (f32[256,1024]{1,0:T(8,128)S(1)}, bf16[16,256,256]{2,1,0:T(8,128)(2,1)S(1)}, f32[1,128]{1,0:T(1,128)S(1)}) custom-call(s32[1]{0:T(128)} %bitcast.core, bf16[256,2048]{1,0:T(8,128)(2,1)S(1)} %get-tuple-element.58.q, bf16[256,2048]{1,0:T(8,128)(2,1)S(1)} %get-tuple-element.55.k, bf16[256,2048]{1,0:T(8,128)(2,1)S(1)} %get-tuple-element.56.v, ...), custom_call_target="tpu_custom_call" | custom-call | flops 1 | bytes 1 | tf_op jit(solution)/shard_map/pallas_call | solution.py:405
  14.2 2.5 %shard_map.114 = (f32[256,1024]{1,0:T(8,128)S(1)}, bf16[16,256,256]{2,1,0:T(8,128)(2,1)S(1)}, f32[1,128]{1,0:T(1,128)S(1)}) custom-call(s32[1]{0:T(128)} %bitcast.core, bf16[256,2048]{1,0:T(8,128)(2,1)S(1)} %get-tuple-element.58.q, bf16[256,2048]{1,0:T(8,128)(2,1)S(1)} %get-tuple-element.55.k, bf16[256,2048]{1,0:T(8,128)(2,1)S(1)} %get-tuple-element.56.v, ...), custom_call_target="tpu_custom_call" | custom-call | flops 1 | bytes 1 | tf_op jit(solution)/shard_map/pallas_call | solution.py:405
  16.9 4.5 %collective-permute-start.3 = (f32[256,128]{1,0:T(8,128)S(1)}, f32[256,128]{1,0:T(8,128)S(1)}, u32[]{:S(2)}, u32[]{:S(2)}) collective-permute-start(f32[256,128]{1,0:T(8,128)S(1)} %get-tuple-element.116), channel_id=1, source_target_pairs={{0,4},{1,5},{2,6},{3,7},{8,12},{9,13},{10,14},{11,15},{16,20},{17,... | collective-permute-start | bytes 393224 | tf_op jit(solution)/shard_map/ppermute | solution.py:302
  21.4 1.3 %collective-permute-start.5 = (f32[4,264,128]{2,1,0:T(8,128)S(1)}, f32[4,264,128]{2,1,0:T(8,128)S(1)}, u32[]{:S(2)}, u32[]{:S(2)}) collective-permute-start(f32[4,264,128]{2,1,0:T(8,128)S(1)} %broadcast_add_fusion), channel_id=1, source_target_pairs={{1,0},{2,1},{3,2},{4,3},{5,4},{6,5},{7,6},{9,8},{10,9},{11,10},{12... | collective-permute-start | bytes 1622024 | tf_op jit(solution)/shard_map/ppermute | solution.py:302
  22.7 3.2 %collective-permute-start.2 = (f32[256,128]{1,0:T(8,128)S(1)}, f32[256,128]{1,0:T(8,128)S(1)}, u32[]{:S(2)}, u32[]{:S(2)}) collective-permute-start(f32[256,128]{1,0:T(8,128)S(1)} %get-tuple-element.115), channel_id=1, source_target_pairs={{0,4},{1,5},{2,6},{3,7},{8,12},{9,13},{10,14},{11,15},{16,20},{17,... | collective-permute-start | bytes 393224 | tf_op jit(solution)/shard_map/ppermute | solution.py:302
  26.1 1.3 %shard_map.115 = (bf16[256,2048]{1,0:T(8,128)(2,1)}, bf16[256,1024]{1,0:T(8,128)(2,1)S(1)}, f32[1,264,128]{2,1,0:T(8,128)S(1)}, f32[1,4,128]{2,1,0:T(4,128)S(1)}...) custom-call(s32[1]{0:T(128)} %bitcast.core, bf16[256,2048]{1,0:T(8,128)(2,1)S(1)} %get-tuple-element.58.q, ...), custom_call_target="tpu_custom_call" | custom-call | flops 1 | bytes 1 | tf_op jit(solution)/shard_map/pallas_call | solution.py:405
  27.4 1.3 %shard_map.116 = (bf16[256,2048]{1,0:T(8,128)(2,1)}, bf16[256,1024]{1,0:T(8,128)(2,1)S(1)}, f32[1,264,128]{2,1,0:T(8,128)S(1)}, f32[1,4,128]{2,1,0:T(4,128)S(1)}...) custom-call(s32[1]{0:T(128)} %bitcast.core, ...), custom_call_target="tpu_custom_call", output_to_operand_aliasing={{0}: (9, {})} | custom-call | flops 1 | bytes 1 | tf_op jit(solution)/shard_map/pallas_call | solution.py:405
  28.7 5.6 %collective-permute-start.6 = (f32[256,128]{1,0:T(8,128)S(1)}, f32[256,128]{1,0:T(8,128)S(1)}, u32[]{:S(2)}, u32[]{:S(2)}) collective-permute-start(f32[256,128]{1,0:T(8,128)S(1)} %get-tuple-element.112), channel_id=1, source_target_pairs={{0,1},{1,0},{2,3},{3,2},{4,5},{5,4},{6,7},{7,6},{8,9},{9,8},{10,11... | collective-permute-start | bytes 393224 | tf_op jit(solution)/shard_map/ppermute | solution.py:297
  34.4 1.3 %shard_map.117 = (bf16[256,2048]{1,0:T(8,128)(2,1)}, bf16[256,1024]{1,0:T(8,128)(2,1)S(1)}, f32[1,264,128]{2,1,0:T(8,128)S(1)}, f32[1,4,128]{2,1,0:T(4,128)S(1)}...) custom-call(s32[1]{0:T(128)} %bitcast.core, ...), custom_call_target="tpu_custom_call", output_to_operand_aliasing={{0}: (9, {}), {1}: (10, {})} | custom-call | flops 1 | bytes 1 | tf_op jit(solution)/shard_map/pallas_call | solution.py:405
  35.7 1.3 %shard_map.118 = (bf16[256,2048]{1,0:T(8,128)(2,1)}, bf16[256,1024]{1,0:T(8,128)(2,1)S(1)}, f32[1,264,128]{2,1,0:T(8,128)S(1)}, f32[1,4,128]{2,1,0:T(4,128)S(1)}...) custom-call(s32[1]{0:T(128)} %bitcast.core, ...), custom_call_target="tpu_custom_call", output_to_operand_aliasing={{0}: (9, {}), {1}: (10, {})} | custom-call | flops 1 | bytes 1 | tf_op jit(solution)/shard_map/pallas_call | solution.py:405
  37.2 1.6 %collective-permute-start.12 = (f32[2,4,128]{2,1,0:T(4,128)S(1)}, f32[2,4,128]{2,1,0:T(4,128)S(1)}, u32[]{:S(2)}, u32[]{:S(2)}) collective-permute-start(f32[2,4,128]{2,1,0:T(4,128)S(1)} %fusion.5), channel_id=1, source_target_pairs={{0,8},{8,0},{16,24},{24,16},{1,9},{9,1},{17,25},{25,17},{2,10},{10... | collective-permute-start | bytes 12296 | tf_op jit(solution)/shard_map/ppermute | solution.py:297
  40.9 1.6 %collective-permute-start.13 = (f32[1,4,128]{2,1,0:T(4,128)S(1)}, f32[1,4,128]{2,1,0:T(4,128)S(1)}, u32[]{:S(2)}, u32[]{:S(2)}) collective-permute-start(f32[1,4,128]{2,1,0:T(4,128)S(1)} %slice_select_fusion), channel_id=1, source_target_pairs={{0,16},{8,24},{16,0},{24,8},{1,17},{9,25},{17,1},{25,9},{2,18},{10... | collective-permute-start | bytes 6152 | tf_op jit(solution)/shard_map/ppermute | solution.py:297
  42.5 5.1 %shard_map.119 = (bf16[256,2048]{1,0:T(8,128)(2,1)}, f32[256,1024]{1,0:T(8,128)S(1)}, f32[256,1024]{1,0:T(8,128)S(1)}, f32[1,128]{1,0:T(1,128)S(1)}) custom-call(s32[1]{0:T(128)} %bitcast.core, bf16[256,2048]{1,0:T(8,128)(2,1)S(1)} %get-tuple-element.58.q, bf16[256,2048]{1,0:T(8,128)(2,1)S(1)} %get-tuple-element.55.k, ...), custom_call_target="tpu_custom_call" | custom-call | flops 1 | bytes 1 | tf_op jit(solution)/shard_map/pallas_call | solution.py:405
  47.6 1.5 %collective-permute-done.8 = f32[512,128]{1,0:T(8,128)S(1)} collective-permute-done((f32[512,128]{1,0:T(8,128)S(1)}, f32[512,128]{1,0:T(8,128)S(1)}, u32[]{:S(2)}, u32[]{:S(2)}) %collective-permute-start.8) | collective-permute-done | bytes 262176 | tf_op jit(solution)/shard_map/ppermute | solution.py:302
  49.1 1.3 %collective-permute-start.9 = (f32[512,128]{1,0:T(8,128)S(1)}, f32[512,128]{1,0:T(8,128)S(1)}, u32[]{:S(2)}, u32[]{:S(2)}) collective-permute-start(f32[512,128]{1,0:T(8,128)S(1)} %add_add_fusion.2.rest_0_), channel_id=1, source_target_pairs={{4,0},{5,1},{6,2},{7,3},{12,8},{13,9},{14,10},{15,11},{20,16},{21,... | collective-permute-start | bytes 786440 | tf_op jit(solution)/shard_map/ppermute | solution.py:302
  50.5 1.3 %collective-permute-start.11 = (f32[4,264,128]{2,1,0:T(8,128)S(1)}, f32[4,264,128]{2,1,0:T(8,128)S(1)}, u32[]{:S(2)}, u32[]{:S(2)}) collective-permute-start(f32[4,264,128]{2,1,0:T(8,128)S(1)} %maximum_add_fusion), channel_id=1, source_target_pairs={{0,1},{1,2},{2,3},{3,4},{4,5},{5,6},{6,7},{8,9},{9,10},{10,11},{11... | collective-permute-start | bytes 1622024 | tf_op jit(solution)/shard_map/ppermute | solution.py:302
  51.8 4.2 %collective-permute-start.14 = (f32[2,128]{1,0:T(2,128)S(1)}, f32[2,128]{1,0:T(2,128)S(1)}, u32[]{:S(2)}, u32[]{:S(2)}) collective-permute-start(f32[2,128]{1,0:T(2,128)S(1)} %broadcast_select_fusion.4), channel_id=1, source_target_pairs={{0,4},{1,5},{2,6},{3,7},{4,0},{5,1},{6,2},{7,3},{8,12},{9,13},{10,... | collective-permute-start | bytes 3080 | tf_op jit(solution)/shard_map/ppermute | solution.py:297
  56.1 5.1 %shard_map.120 = (bf16[256,2048]{1,0:T(8,128)(2,1)}, f32[256,1024]{1,0:T(8,128)S(1)}, f32[256,1024]{1,0:T(8,128)S(1)}, f32[1,128]{1,0:T(1,128)S(1)}) custom-call(s32[1]{0:T(128)} %bitcast.core, bf16[256,2048]{1,0:T(8,128)(2,1)S(1)} %get-tuple-element.58.q, bf16[256,2048]{1,0:T(8,128)(2,1)S(1)} %get-tuple-element.55.k, ...), custom_call_target="tpu_custom_call", output_to_operand_aliasing={{0}: (13, {})} | custom-call | flops 1 | bytes 1 | tf_op jit(solution)/shard_map/pallas_call | solution.py:405
  61.2 4.0 %collective-permute-done.9 = f32[512,128]{1,0:T(8,128)S(1)} collective-permute-done((f32[512,128]{1,0:T(8,128)S(1)}, f32[512,128]{1,0:T(8,128)S(1)}, u32[]{:S(2)}, u32[]{:S(2)}) %collective-permute-start.9) | collective-permute-done | bytes 262176 | tf_op jit(solution)/shard_map/ppermute | solution.py:302
  65.5 2.5 %shard_map.121 = (bf16[256,2048]{1,0:T(8,128)(2,1)}, bf16[256,2048]{1,0:T(8,128)(2,1)}, f32[1,128]{1,0:T(1,128)S(1)}) custom-call(s32[1]{0:T(128)} %bitcast.core, bf16[256,2048]{1,0:T(8,128)(2,1)S(1)} %get-tuple-element.55.k, bf16[256,2048]{1,0:T(8,128)(2,1)S(1)} %get-tuple-element.56.v, f32[256,1024]{1,0:T(8,128)S(1)} %get-tuple-element.92.gk_in, ...), custom_call_target="tpu_custom_call" | custom-call | flops 1 | bytes 1 | tf_op jit(solution)/shard_map/pallas_call | solution.py:405
  69.0 2.5 %shard_map.122 = (bf16[256,2048]{1,0:T(8,128)(2,1)}, bf16[256,2048]{1,0:T(8,128)(2,1)}, f32[1,128]{1,0:T(1,128)}) custom-call(s32[1]{0:T(128)} %bitcast.core, bf16[256,2048]{1,0:T(8,128)(2,1)S(1)} %get-tuple-element.55.k, bf16[256,2048]{1,0:T(8,128)(2,1)S(1)} %get-tuple-element.56.v, ...), custom_call_target="tpu_custom_call", output_to_operand_aliasing={{0}: (9, {}), {1}: (10, {})} | custom-call | flops 1 | bytes 1 | tf_op jit(solution)/shard_map/pallas_call | solution.py:405
  (66 shorter events, 6.3 us)
Async XLA Ops:
  0.6 2.3 %copy-start.1 = (s32[1,256]{1,0:T(1,128)S(1)}, s32[1,256]{1,0:T(1,128)}, u32[]{:S(2)}) copy-start(s32[1,256]{1,0:T(1,128)} %seg.17) | copy-start | bytes 3076
  0.6 2.3 %copy-start.2 = (s32[1,32]{1,0:T(1,128)S(1)}, s32[1,32]{1,0:T(1,128)}, u32[]{:S(2)}) copy-start(s32[1,32]{1,0:T(1,128)} %table.17) | copy-start | bytes 388
  2.4 1.7 %collective-permute-start = (f32[512,128]{1,0:T(8,128)S(1)}, f32[512,128]{1,0:T(8,128)S(1)}, u32[]{:S(2)}, u32[]{:S(2)}) collective-permute-start(f32[512,128]{1,0:T(8,128)S(1)} %get-tuple-element.57), channel_id=1, source_target_pairs={{0,1},{1,0},{2,3},{3,2},{4,5},{5,4},{6,7},{7,6},{8,9},{9,8},{10,11... | collective-permute-start | bytes 786440 | tf_op jit(solution)/shard_map/ppermute | solution.py:297
  4.1 12.6 %collective-permute-start.1 = (f32[512,128]{1,0:T(8,128)S(1)}, f32[512,128]{1,0:T(8,128)S(1)}, u32[]{:S(2)}, u32[]{:S(2)}) collective-permute-start(f32[512,128]{1,0:T(8,128)S(1)} %add.158.rest_0_), channel_id=1, source_target_pairs={{0,2},{1,3},{2,4},{3,5},{4,6},{5,7},{8,10},{9,11},{10,12},{11,13},... | collective-permute-start | bytes 786440 | tf_op jit(solution)/shard_map/ppermute | solution.py:302
  16.7 9.3 %copy-start = (f32[2048]{0:T(1024)S(1)}, f32[2048]{0:T(1024)}, u32[]{:S(2)}) copy-start(f32[2048]{0:T(1024)} %param.13) | copy-start | bytes 24580
  16.9 9.1 %collective-permute-start.3 = (f32[256,128]{1,0:T(8,128)S(1)}, f32[256,128]{1,0:T(8,128)S(1)}, u32[]{:S(2)}, u32[]{:S(2)}) collective-permute-start(f32[256,128]{1,0:T(8,128)S(1)} %get-tuple-element.116), channel_id=1, source_target_pairs={{0,4},{1,5},{2,6},{3,7},{8,12},{9,13},{10,14},{11,15},{16,20},{17,... | collective-permute-start | bytes 393224 | tf_op jit(solution)/shard_map/ppermute | solution.py:302
  21.4 4.7 %collective-permute-start.5 = (f32[4,264,128]{2,1,0:T(8,128)S(1)}, f32[4,264,128]{2,1,0:T(8,128)S(1)}, u32[]{:S(2)}, u32[]{:S(2)}) collective-permute-start(f32[4,264,128]{2,1,0:T(8,128)S(1)} %broadcast_add_fusion), channel_id=1, source_target_pairs={{1,0},{2,1},{3,2},{4,3},{5,4},{6,5},{7,6},{9,8},{10,9},{11,10},{12... | collective-permute-start | bytes 1622024 | tf_op jit(solution)/shard_map/ppermute | solution.py:302
  22.7 6.0 %collective-permute-start.2 = (f32[256,128]{1,0:T(8,128)S(1)}, f32[256,128]{1,0:T(8,128)S(1)}, u32[]{:S(2)}, u32[]{:S(2)}) collective-permute-start(f32[256,128]{1,0:T(8,128)S(1)} %get-tuple-element.115), channel_id=1, source_target_pairs={{0,4},{1,5},{2,6},{3,7},{8,12},{9,13},{10,14},{11,15},{16,20},{17,... | collective-permute-start | bytes 393224 | tf_op jit(solution)/shard_map/ppermute | solution.py:302
  26.0 1.4 %collective-permute-start.4 = (f32[256,128]{1,0:T(8,128)S(1)}, f32[256,128]{1,0:T(8,128)S(1)}, u32[]{:S(2)}, u32[]{:S(2)}) collective-permute-start(f32[256,128]{1,0:T(8,128)S(1)} %get-tuple-element.114), channel_id=1, source_target_pairs={{0,1},{1,0},{2,3},{3,2},{4,5},{5,4},{6,7},{7,6},{8,9},{9,8},{10,11... | collective-permute-start | bytes 393224 | tf_op jit(solution)/shard_map/ppermute | solution.py:297
  28.7 7.0 %collective-permute-start.6 = (f32[256,128]{1,0:T(8,128)S(1)}, f32[256,128]{1,0:T(8,128)S(1)}, u32[]{:S(2)}, u32[]{:S(2)}) collective-permute-start(f32[256,128]{1,0:T(8,128)S(1)} %get-tuple-element.112), channel_id=1, source_target_pairs={{0,1},{1,0},{2,3},{3,2},{4,5},{5,4},{6,7},{7,6},{8,9},{9,8},{10,11... | collective-permute-start | bytes 393224 | tf_op jit(solution)/shard_map/ppermute | solution.py:297
  37.1 1.7 %collective-permute-start.7 = (f32[512,128]{1,0:T(8,128)S(1)}, f32[512,128]{1,0:T(8,128)S(1)}, u32[]{:S(2)}, u32[]{:S(2)}) collective-permute-start(f32[512,128]{1,0:T(8,128)S(1)} %pad_maximum_fusion), channel_id=1, source_target_pairs={{0,1},{1,0},{2,3},{3,2},{4,5},{5,4},{6,7},{7,6},{8,9},{9,8},{10,11... | collective-permute-start | bytes 786440 | tf_op jit(solution)/shard_map/ppermute | solution.py:297
  37.2 3.7 %collective-permute-start.12 = (f32[2,4,128]{2,1,0:T(4,128)S(1)}, f32[2,4,128]{2,1,0:T(4,128)S(1)}, u32[]{:S(2)}, u32[]{:S(2)}) collective-permute-start(f32[2,4,128]{2,1,0:T(4,128)S(1)} %fusion.5), channel_id=1, source_target_pairs={{0,8},{8,0},{16,24},{24,16},{1,9},{9,1},{17,25},{25,17},{2,10},{10... | collective-permute-start | bytes 12296 | tf_op jit(solution)/shard_map/ppermute | solution.py:297
  38.8 10.3 %collective-permute-start.8 = (f32[512,128]{1,0:T(8,128)S(1)}, f32[512,128]{1,0:T(8,128)S(1)}, u32[]{:S(2)}, u32[]{:S(2)}) collective-permute-start(f32[512,128]{1,0:T(8,128)S(1)} %add.179.rest_0_), channel_id=1, source_target_pairs={{2,0},{3,1},{4,2},{5,3},{6,4},{7,5},{10,8},{11,9},{12,10},{13,11},... | collective-permute-start | bytes 786440 | tf_op jit(solution)/shard_map/ppermute | solution.py:302
  40.9 10.9 %collective-permute-start.13 = (f32[1,4,128]{2,1,0:T(4,128)S(1)}, f32[1,4,128]{2,1,0:T(4,128)S(1)}, u32[]{:S(2)}, u32[]{:S(2)}) collective-permute-start(f32[1,4,128]{2,1,0:T(4,128)S(1)} %slice_select_fusion), channel_id=1, source_target_pairs={{0,16},{8,24},{16,0},{24,8},{1,17},{9,25},{17,1},{25,9},{2,18},{10... | collective-permute-start | bytes 6152 | tf_op jit(solution)/shard_map/ppermute | solution.py:297
  49.1 16.0 %collective-permute-start.9 = (f32[512,128]{1,0:T(8,128)S(1)}, f32[512,128]{1,0:T(8,128)S(1)}, u32[]{:S(2)}, u32[]{:S(2)}) collective-permute-start(f32[512,128]{1,0:T(8,128)S(1)} %add_add_fusion.2.rest_0_), channel_id=1, source_target_pairs={{4,0},{5,1},{6,2},{7,3},{12,8},{13,9},{14,10},{15,11},{20,16},{21,... | collective-permute-start | bytes 786440 | tf_op jit(solution)/shard_map/ppermute | solution.py:302
  50.5 15.0 %collective-permute-start.11 = (f32[4,264,128]{2,1,0:T(8,128)S(1)}, f32[4,264,128]{2,1,0:T(8,128)S(1)}, u32[]{:S(2)}, u32[]{:S(2)}) collective-permute-start(f32[4,264,128]{2,1,0:T(8,128)S(1)} %maximum_add_fusion), channel_id=1, source_target_pairs={{0,1},{1,2},{2,3},{3,4},{4,5},{5,6},{6,7},{8,9},{9,10},{10,11},{11... | collective-permute-start | bytes 1622024 | tf_op jit(solution)/shard_map/ppermute | solution.py:302
  51.8 13.4 %collective-permute-start.14 = (f32[2,128]{1,0:T(2,128)S(1)}, f32[2,128]{1,0:T(2,128)S(1)}, u32[]{:S(2)}, u32[]{:S(2)}) collective-permute-start(f32[2,128]{1,0:T(2,128)S(1)} %broadcast_select_fusion.4), channel_id=1, source_target_pairs={{0,4},{1,5},{2,6},{3,7},{4,0},{5,1},{6,2},{7,3},{8,12},{9,13},{10,... | collective-permute-start | bytes 3080 | tf_op jit(solution)/shard_map/ppermute | solution.py:297
  65.3 3.6 %collective-permute-start.15 = (f32[1,128]{1,0:T(1,128)S(1)}, f32[1,128]{1,0:T(1,128)S(1)}, u32[]{:S(2)}, u32[]{:S(2)}) collective-permute-start(f32[1,128]{1,0:T(1,128)S(1)} %compare_select_fusion), channel_id=1, source_target_pairs={{0,2},{1,3},{2,0},{3,1},{4,6},{5,7},{6,4},{7,5},{8,10},{9,11},{10,... | collective-permute-start | bytes 1544 | tf_op jit(solution)/shard_map/ppermute | solution.py:297
  65.4 3.6 %collective-permute-start.10 = (f32[512,128]{1,0:T(8,128)S(1)}, f32[512,128]{1,0:T(8,128)S(1)}, u32[]{:S(2)}, u32[]{:S(2)}) collective-permute-start(f32[512,128]{1,0:T(8,128)S(1)} %add_select_fusion.1), channel_id=1, source_target_pairs={{0,1},{1,0},{2,3},{3,2},{4,5},{5,4},{6,7},{7,6},{8,9},{9,8},{10,11... | collective-permute-start | bytes 786440 | tf_op jit(solution)/shard_map/ppermute | solution.py:297
  68.9 2.5 %collective-permute-start.16 = (f32[1,64]{1,0:T(1,128)S(1)}, f32[1,64]{1,0:T(1,128)S(1)}, u32[]{:S(2)}, u32[]{:S(2)}) collective-permute-start(f32[1,64]{1,0:T(1,128)S(1)} %slice_select_fusion.1), channel_id=1, source_target_pairs={{0,1},{1,0},{2,3},{3,2},{4,5},{5,4},{6,7},{7,6},{8,9},{9,8},{10,11... | collective-permute-start | bytes 776 | tf_op jit(solution)/shard_map/ppermute | solution.py:297

commit v17 on v13

--- a/solution.py
+++ b/solution.py
@@ -103,11 +103,21 @@
     return group, base, base + (group + half) * lanes, base // PAIR * E
 
 
-def states_kernel(core, ctx, dp, k_in, v_in, keep, send, zero, k, v, core_row, ctx_row, dp_row, sems):
+def put_half(sel, core, k, v, out):
+    lanes = k.shape[1] // GROUPS // 2
+    count = lanes // PAIR
+    for group in range(GROUPS):
+        base = (2 * group + (sel + core[0]) % 2) * lanes
+        for p in range(count):
+            at = lanes_at(base, p)
+            row = (group * count + p) * E
+            out[row:row + E] = state_pair(k[:, at], v[:, at])
+
+
+def send_kernel(core, ctx, dp, k_in, v_in, send, zero, k, v, core_row, ctx_row, dp_row, sems):
     for row, index in ((core_row, core), (ctx_row, ctx), (dp_row, dp)):
         row[...] = jnp.full(row.shape, index[0], jnp.int32)
     lanes = k.shape[1] // GROUPS // 2
-    count = lanes // PAIR
     copies = []
     for sel in (1, 0):
         for group in range(GROUPS):
@@ -118,15 +128,15 @@
     for copy in copies:
         copy.start()
     zero[...] = jnp.zeros_like(zero)
-    for sel, out in ((1, send), (0, keep)):
-        for group in range(GROUPS):
-            copies.pop(0).wait()
-            copies.pop(0).wait()
-            base = (2 * group + (sel + core[0]) % 2) * lanes
-            for p in range(count):
-                at = lanes_at(base, p)
-                row = (group * count + p) * E
-                out[row:row + E] = state_pair(k[:, at], v[:, at])
+    for copy in copies[:2 * GROUPS]:
+        copy.wait()
+    put_half(1, core, k, v, send)
+    for copy in copies[2 * GROUPS:]:
+        copy.wait()
+
+
+def keep_kernel(core, k, v, *rest):
+    put_half(0, core, k, v, rest[-1])
 
 
 def part_kernel(core, q_in, dy_in, k, v, seg, table, *rest):
@@ -441,11 +451,12 @@
             before = before + work(load)
         return before
 
-    keep, send, zero, k, v, core_row, ctx_row, dp_row = call(
-        states_kernel, 0, [("hbm", k), ("hbm", v)],
-        [("all", F32), ("all", F32), ("zero", jnp.int32), ("vmem", BF16, whole), ("vmem", BF16, whole)]
+    send, zero, k, v, core_row, ctx_row, dp_row = call(
+        send_kernel, 0, [("hbm", k), ("hbm", v)],
+        [("all", F32), ("zero", jnp.int32), ("vmem", BF16, whole), ("vmem", BF16, whole)]
         + [("token", jnp.int32)] * 3,
         scratch=[pltpu.SemaphoreType.DMA((2 * GROUPS, 2))], steps=(1,), scalars=[core, ctx, dp])
+    keep, = call(keep_kernel, 0, [("vmem", k), ("vmem", v)], [("all", F32)], steps=(1,))
     piece = within_chip(keep, send)
     seg = (segment_ids + zero)[0]
     onehot = seg[:, None] == jnp.arange(table.shape[0], dtype=jnp.int32)[None, :]
@@ -463,16 +474,17 @@
     local, nxt = [], []
 
     def first_work(load):
-        *made, token = local_attn(0, [parts[0]])
-        local.append(made)
-        return token
+        tokens = []
+        for sel in range(2):
+            *made, token = local_attn(sel, [parts[0]])
+            local.append(made)
+            tokens.append(token)
+        return sum(tokens)
 
     def second_work(load):
         for part in reversed(parts):
             nxt.append(shifted(part + nought(load[:1]), -1))
-        *made, token = local_attn(1, [load])
-        local.append(made)
-        return token
+        return jnp.zeros((1, PAIR), F32)
 
     before = summed_before(piece[2], 1, [first_work, second_work])
     prefix = to_cores(core_row, before, piece, 1)

time: 71.9 us -> 71.4 us (level)
  starting transfers between devices: 29.6 us -> 25.3 us
  waiting for transfers between devices: 9.52 us -> 13.4 us
    ppermute x7, waiting for transfers between devices: 6.77 us -> 11.3 us  [shifted(): lax.ppermute(x, 'ctx', [(i, i + distance) for i in range(count) if 0 <= i...]
    ppermute x9, starting transfers between devices: 12.8 us -> 9.48 us  [partner(): return lax.ppermute(x, axis, route)]
    ppermute x7, starting transfers between devices: 16.8 us -> 15.8 us  [shifted(): lax.ppermute(x, 'ctx', [(i, i + distance) for i in range(count) if 0 <= i...]
    pallas_call x10 -> x11, Pallas kernels: 30.1 us -> 30 us  [call(): pl.pallas_call(kernel, grid_spec=pltpu.PrefetchScalarGridSpec(num_scalar_...]
  transfers between devices with their start and end apart: 16 -> 16, of which waited for: 6 -> 6; matrix products, arithmetic and copies ran while one was open for 1% -> 1% of each run, Pallas kernels for 35% -> 36%
where the time goes in v17:
time: 71.4 us; the launch traced here: 71.1 us
  Pallas kernels  30 us (42%)
  starting transfers between devices  25.3 us (35%)
  waiting for transfers between devices  13.4 us (19%)
  other arithmetic  1.38 us (2%)
  between operations  1 us (1%)
    pallas_call x11, Pallas kernels, call(): pl.pallas_call(kernel, grid_spec=pltpu.PrefetchScalarGridSpec(num_scalar_...  30 us
    ppermute x7, starting transfers between devices, shifted(): lax.ppermute(x, 'ctx', [(i, i + distance) for i in range(count) if 0 <= i...  15.8 us
    ppermute x7, waiting for transfers between devices, shifted(): lax.ppermute(x, 'ctx', [(i, i + distance) for i in range(count) if 0 <= i...  11.3 us
    ppermute x9, starting transfers between devices, partner(): return lax.ppermute(x, axis, route)  9.48 us
    ppermute x9, waiting for transfers between devices, partner(): return lax.ppermute(x, axis, route)  2.12 us
  transfers between devices with their start and end apart: 16, of which 6 were waited for; matrix products, arithmetic and copies ran while one was open for 1% of the time, Pallas kernels for 36%

profile of v17, /device:TPU:0, one launch (start us, length us, event | category | flops | bytes accessed | tf_op | source)
XLA Modules:
  0.0 71.1 jit_solution(7006458682358831324)
XLA Ops:
  0.7 1.8 %shard_map.110 = (f32[512,128]{1,0:T(8,128)S(1)}, s32[1,256]{1,0:T(1,128)S(1)}, bf16[256,2048]{1,0:T(8,128)(2,1)S(1)}, bf16[256,2048]{1,0:T(8,128)(2,1)S(1)}, s3...) custom-call(s32[1]{0:T(128)} %bitcast.core, s32[1]{0:T(128)} %bitcast.3.ctx, s32[1]{0:T(128)} %bitcast.4.dp, ...), custom_call_target="tpu_custom_call" | custom-call | flops 1 | bytes 1 | tf_op jit(solution)/shard_map/pallas_call | solution.py:393
  4.1 4.9 %collective-permute-start.1 = (f32[512,128]{1,0:T(8,128)S(1)}, f32[512,128]{1,0:T(8,128)S(1)}, u32[]{:S(2)}, u32[]{:S(2)}) collective-permute-start(f32[512,128]{1,0:T(8,128)S(1)} %add.138.rest_0_), channel_id=1, source_target_pairs={{0,2},{1,3},{2,4},{3,5},{4,6},{5,7},{8,10},{9,11},{10,12},{11,13},... | collective-permute-start | bytes 786440 | tf_op jit(solution)/shard_map/ppermute | solution.py:300
  9.0 2.6 %shard_map.112 = (f32[2,264,128]{2,1,0:T(8,128)S(1)}, f32[2,264,128]{2,1,0:T(8,128)S(1)}, bf16[256,2048]{1,0:T(8,128)(2,1)S(1)}, bf16[256,2048]{1,0:T(8,128)(2,1)S(1)}, f32[1,128]{1,0:T(1,128)}) custom-call(s32[1]{0:T(128)} %bitcast.core, bf16[256,2048]{1,0:T(8,128)(2,1)} %bitcast.50, bf16[256,2048]{1,0:T(8,128)(2,1)} %bitcast.51, ...), custom_call_target="tpu_custom_call" | custom-call | flops 1 | bytes 1 | tf_op jit(solution)/shard_map/pallas_call | solution.py:393
  11.7 2.5 %shard_map.114 = (f32[256,1024]{1,0:T(8,128)S(1)}, bf16[16,256,256]{2,1,0:T(8,128)(2,1)S(1)}, f32[1,128]{1,0:T(1,128)S(1)}) custom-call(s32[1]{0:T(128)} %bitcast.core, bf16[256,2048]{1,0:T(8,128)(2,1)S(1)} %get-tuple-element.48.q, bf16[256,2048]{1,0:T(8,128)(2,1)S(1)} %get-tuple-element.45.k, bf16[256,2048]{1,0:T(8,128)(2,1)S(1)} %get-tuple-element.46.v, ...), custom_call_target="tpu_custom_call" | custom-call | flops 1 | bytes 1 | tf_op jit(solution)/shard_map/pallas_call | solution.py:393
  14.2 2.5 %shard_map.113 = (f32[256,1024]{1,0:T(8,128)S(1)}, bf16[16,256,256]{2,1,0:T(8,128)(2,1)S(1)}, f32[1,128]{1,0:T(1,128)S(1)}) custom-call(s32[1]{0:T(128)} %bitcast.core, bf16[256,2048]{1,0:T(8,128)(2,1)S(1)} %get-tuple-element.48.q, bf16[256,2048]{1,0:T(8,128)(2,1)S(1)} %get-tuple-element.45.k, bf16[256,2048]{1,0:T(8,128)(2,1)S(1)} %get-tuple-element.46.v, ...), custom_call_target="tpu_custom_call" | custom-call | flops 1 | bytes 1 | tf_op jit(solution)/shard_map/pallas_call | solution.py:393
  16.7 4.5 %collective-permute-start.2 = (f32[512,128]{1,0:T(8,128)S(1)}, f32[512,128]{1,0:T(8,128)S(1)}, u32[]{:S(2)}, u32[]{:S(2)}) collective-permute-start(f32[512,128]{1,0:T(8,128)S(1)} %add_add_fusion.3), channel_id=1, source_target_pairs={{0,4},{1,5},{2,6},{3,7},{8,12},{9,13},{10,14},{11,15},{16,20},{17,... | collective-permute-start | bytes 786440 | tf_op jit(solution)/shard_map/ppermute | solution.py:300
  21.3 1.3 %collective-permute-start.5 = (f32[2,264,128]{2,1,0:T(8,128)S(1)}, f32[2,264,128]{2,1,0:T(8,128)S(1)}, u32[]{:S(2)}, u32[]{:S(2)}) collective-permute-start(f32[2,264,128]{2,1,0:T(8,128)S(1)} %get-tuple-element.99), channel_id=1, source_target_pairs={{1,0},{2,1},{3,2},{4,3},{5,4},{6,5},{7,6},{9,8},{10,9},{11,10},{12... | collective-permute-start | bytes 811016 | tf_op jit(solution)/shard_map/ppermute | solution.py:300
  22.6 1.3 %collective-permute-start.4 = (f32[2,264,128]{2,1,0:T(8,128)S(1)}, f32[2,264,128]{2,1,0:T(8,128)S(1)}, u32[]{:S(2)}, u32[]{:S(2)}) collective-permute-start(f32[2,264,128]{2,1,0:T(8,128)S(1)} %get-tuple-element.100), channel_id=1, source_target_pairs={{1,0},{2,1},{3,2},{4,3},{5,4},{6,5},{7,6},{9,8},{10,9},{11,10},{12... | collective-permute-start | bytes 811016 | tf_op jit(solution)/shard_map/ppermute | solution.py:300
  23.9 2.9 %collective-permute-done.2 = f32[512,128]{1,0:T(8,128)S(1)} collective-permute-done((f32[512,128]{1,0:T(8,128)S(1)}, f32[512,128]{1,0:T(8,128)S(1)}, u32[]{:S(2)}, u32[]{:S(2)}) %collective-permute-start.2) | collective-permute-done | bytes 262176 | tf_op jit(solution)/shard_map/ppermute | solution.py:300
  27.0 2.5 %shard_map.115 = (bf16[256,2048]{1,0:T(8,128)(2,1)}, bf16[256,1024]{1,0:T(8,128)(2,1)S(1)}, f32[2,264,128]{2,1,0:T(8,128)S(1)}, f32[2,4,128]{2,1,0:T(4,128)S(1)}...) custom-call(s32[1]{0:T(128)} %bitcast.core, bf16[256,2048]{1,0:T(8,128)(2,1)S(1)} %get-tuple-element.48.q, ...), custom_call_target="tpu_custom_call" | custom-call | flops 1 | bytes 1 | tf_op jit(solution)/shard_map/pallas_call | solution.py:393
  29.6 2.4 %shard_map.116 = (bf16[256,2048]{1,0:T(8,128)(2,1)}, bf16[256,1024]{1,0:T(8,128)(2,1)S(1)}, f32[2,264,128]{2,1,0:T(8,128)S(1)}, f32[2,4,128]{2,1,0:T(4,128)S(1)}...) custom-call(s32[1]{0:T(128)} %bitcast.core, ...), custom_call_target="tpu_custom_call", output_to_operand_aliasing={{0}: (10, {})} | custom-call | flops 1 | bytes 1 | tf_op jit(solution)/shard_map/pallas_call | solution.py:393
  32.0 2.0 %collective-permute-start.6 = (f32[512,128]{1,0:T(8,128)S(1)}, f32[512,128]{1,0:T(8,128)S(1)}, u32[]{:S(2)}, u32[]{:S(2)}) collective-permute-start(f32[512,128]{1,0:T(8,128)S(1)} %get-tuple-element.63), channel_id=1, source_target_pairs={{0,1},{1,0},{2,3},{3,2},{4,5},{5,4},{6,7},{7,6},{8,9},{9,8},{10,11... | collective-permute-start | bytes 786440 | tf_op jit(solution)/shard_map/ppermute | solution.py:295
  33.9 1.6 %collective-permute-start.11 = (f32[2,4,128]{2,1,0:T(4,128)S(1)}, f32[2,4,128]{2,1,0:T(4,128)S(1)}, u32[]{:S(2)}, u32[]{:S(2)}) collective-permute-start(f32[2,4,128]{2,1,0:T(4,128)S(1)} %broadcast_select_fusion.2), channel_id=1, source_target_pairs={{0,8},{8,0},{16,24},{24,16},{1,9},{9,1},{17,25},{25,17},{2,10},{10... | collective-permute-start | bytes 12296 | tf_op jit(solution)/shard_map/ppermute | solution.py:295
  35.6 1.3 %collective-permute-start.7 = (f32[512,128]{1,0:T(8,128)S(1)}, f32[512,128]{1,0:T(8,128)S(1)}, u32[]{:S(2)}, u32[]{:S(2)}) collective-permute-start(f32[512,128]{1,0:T(8,128)S(1)} %add.152.rest_0_), channel_id=1, source_target_pairs={{2,0},{3,1},{4,2},{5,3},{6,4},{7,5},{10,8},{11,9},{12,10},{13,11},... | collective-permute-start | bytes 786440 | tf_op jit(solution)/shard_map/ppermute | solution.py:300
  37.6 1.6 %collective-permute-start.12 = (f32[1,4,128]{2,1,0:T(4,128)S(1)}, f32[1,4,128]{2,1,0:T(4,128)S(1)}, u32[]{:S(2)}, u32[]{:S(2)}) collective-permute-start(f32[1,4,128]{2,1,0:T(4,128)S(1)} %slice_select_fusion), channel_id=1, source_target_pairs={{0,16},{8,24},{16,0},{24,8},{1,17},{9,25},{17,1},{25,9},{2,18},{10... | collective-permute-start | bytes 6152 | tf_op jit(solution)/shard_map/ppermute | solution.py:295
  39.2 5.1 %shard_map.117 = (bf16[256,2048]{1,0:T(8,128)(2,1)}, f32[256,1024]{1,0:T(8,128)S(1)}, f32[256,1024]{1,0:T(8,128)S(1)}, f32[1,128]{1,0:T(1,128)S(1)}) custom-call(s32[1]{0:T(128)} %bitcast.core, bf16[256,2048]{1,0:T(8,128)(2,1)S(1)} %get-tuple-element.48.q, bf16[256,2048]{1,0:T(8,128)(2,1)S(1)} %get-tuple-element.45.k, ...), custom_call_target="tpu_custom_call" | custom-call | flops 1 | bytes 1 | tf_op jit(solution)/shard_map/pallas_call | solution.py:393
  44.3 3.7 %collective-permute-done.7 = f32[512,128]{1,0:T(8,128)S(1)} collective-permute-done((f32[512,128]{1,0:T(8,128)S(1)}, f32[512,128]{1,0:T(8,128)S(1)}, u32[]{:S(2)}, u32[]{:S(2)}) %collective-permute-start.7) | collective-permute-done | bytes 262176 | tf_op jit(solution)/shard_map/ppermute | solution.py:300
  48.1 1.3 %collective-permute-start.8 = (f32[512,128]{1,0:T(8,128)S(1)}, f32[512,128]{1,0:T(8,128)S(1)}, u32[]{:S(2)}, u32[]{:S(2)}) collective-permute-start(f32[512,128]{1,0:T(8,128)S(1)} %add_add_fusion.1.rest_0_), channel_id=1, source_target_pairs={{4,0},{5,1},{6,2},{7,3},{12,8},{13,9},{14,10},{15,11},{20,16},{21,... | collective-permute-start | bytes 786440 | tf_op jit(solution)/shard_map/ppermute | solution.py:300
  49.4 3.6 %collective-permute-start.13 = (f32[2,128]{1,0:T(2,128)S(1)}, f32[2,128]{1,0:T(2,128)S(1)}, u32[]{:S(2)}, u32[]{:S(2)}) collective-permute-start(f32[2,128]{1,0:T(2,128)S(1)} %broadcast_select_fusion.3), channel_id=1, source_target_pairs={{0,4},{1,5},{2,6},{3,7},{4,0},{5,1},{6,2},{7,3},{8,12},{9,13},{10,... | collective-permute-start | bytes 3080 | tf_op jit(solution)/shard_map/ppermute | solution.py:295
  53.1 1.3 %collective-permute-start.10 = (f32[4,264,128]{2,1,0:T(8,128)S(1)}, f32[4,264,128]{2,1,0:T(8,128)S(1)}, u32[]{:S(2)}, u32[]{:S(2)}) collective-permute-start(f32[4,264,128]{2,1,0:T(8,128)S(1)} %maximum_add_fusion), channel_id=1, source_target_pairs={{0,1},{1,2},{2,3},{3,4},{4,5},{5,6},{6,7},{8,9},{9,10},{10,11},{11... | collective-permute-start | bytes 1622024 | tf_op jit(solution)/shard_map/ppermute | solution.py:300
  54.4 5.2 %shard_map.118 = (bf16[256,2048]{1,0:T(8,128)(2,1)}, f32[256,1024]{1,0:T(8,128)S(1)}, f32[256,1024]{1,0:T(8,128)S(1)}, f32[1,128]{1,0:T(1,128)S(1)}) custom-call(s32[1]{0:T(128)} %bitcast.core, bf16[256,2048]{1,0:T(8,128)(2,1)S(1)} %get-tuple-element.48.q, bf16[256,2048]{1,0:T(8,128)(2,1)S(1)} %get-tuple-element.45.k, ...), custom_call_target="tpu_custom_call", output_to_operand_aliasing={{0}: (12, {})} | custom-call | flops 1 | bytes 1 | tf_op jit(solution)/shard_map/pallas_call | solution.py:393
  59.6 4.6 %collective-permute-done.8 = f32[512,128]{1,0:T(8,128)S(1)} collective-permute-done((f32[512,128]{1,0:T(8,128)S(1)}, f32[512,128]{1,0:T(8,128)S(1)}, u32[]{:S(2)}, u32[]{:S(2)}) %collective-permute-start.8) | collective-permute-done | bytes 262176 | tf_op jit(solution)/shard_map/ppermute | solution.py:300
  64.5 2.5 %shard_map.119 = (bf16[256,2048]{1,0:T(8,128)(2,1)}, bf16[256,2048]{1,0:T(8,128)(2,1)}, f32[1,128]{1,0:T(1,128)S(1)}) custom-call(s32[1]{0:T(128)} %bitcast.core, bf16[256,2048]{1,0:T(8,128)(2,1)S(1)} %get-tuple-element.45.k, bf16[256,2048]{1,0:T(8,128)(2,1)S(1)} %get-tuple-element.46.v, f32[256,1024]{1,0:T(8,128)S(1)} %get-tuple-element.74.gk_in, ...), custom_call_target="tpu_custom_call" | custom-call | flops 1 | bytes 1 | tf_op jit(solution)/shard_map/pallas_call | solution.py:393
  68.0 2.5 %shard_map.120 = (bf16[256,2048]{1,0:T(8,128)(2,1)}, bf16[256,2048]{1,0:T(8,128)(2,1)}, f32[1,128]{1,0:T(1,128)}) custom-call(s32[1]{0:T(128)} %bitcast.core, bf16[256,2048]{1,0:T(8,128)(2,1)S(1)} %get-tuple-element.45.k, bf16[256,2048]{1,0:T(8,128)(2,1)S(1)} %get-tuple-element.46.v, ...), custom_call_target="tpu_custom_call", output_to_operand_aliasing={{0}: (9, {}), {1}: (10, {})} | custom-call | flops 1 | bytes 1 | tf_op jit(solution)/shard_map/pallas_call | solution.py:393
  (57 shorter events, 4.7 us)
Async XLA Ops:
  0.6 2.3 %copy-start = (s32[1,256]{1,0:T(1,128)S(1)}, s32[1,256]{1,0:T(1,128)}, u32[]{:S(2)}) copy-start(s32[1,256]{1,0:T(1,128)} %seg.13) | copy-start | bytes 3076
  0.6 2.3 %copy-start.2 = (s32[1,32]{1,0:T(1,128)S(1)}, s32[1,32]{1,0:T(1,128)}, u32[]{:S(2)}) copy-start(s32[1,32]{1,0:T(1,128)} %table.13) | copy-start | bytes 388
  2.4 1.7 %collective-permute-start = (f32[512,128]{1,0:T(8,128)S(1)}, f32[512,128]{1,0:T(8,128)S(1)}, u32[]{:S(2)}, u32[]{:S(2)}) collective-permute-start(f32[512,128]{1,0:T(8,128)S(1)} %get-tuple-element.47), channel_id=1, source_target_pairs={{0,1},{1,0},{2,3},{3,2},{4,5},{5,4},{6,7},{7,6},{8,9},{9,8},{10,11... | collective-permute-start | bytes 786440 | tf_op jit(solution)/shard_map/ppermute | solution.py:295
  4.1 12.5 %collective-permute-start.1 = (f32[512,128]{1,0:T(8,128)S(1)}, f32[512,128]{1,0:T(8,128)S(1)}, u32[]{:S(2)}, u32[]{:S(2)}) collective-permute-start(f32[512,128]{1,0:T(8,128)S(1)} %add.138.rest_0_), channel_id=1, source_target_pairs={{0,2},{1,3},{2,4},{3,5},{4,6},{5,7},{8,10},{9,11},{10,12},{11,13},... | collective-permute-start | bytes 786440 | tf_op jit(solution)/shard_map/ppermute | solution.py:300
  16.7 10.4 %copy-start.1 = (f32[2048]{0:T(1024)S(1)}, f32[2048]{0:T(1024)}, u32[]{:S(2)}) copy-start(f32[2048]{0:T(1024)} %param.13) | copy-start | bytes 24580
  16.7 10.1 %collective-permute-start.2 = (f32[512,128]{1,0:T(8,128)S(1)}, f32[512,128]{1,0:T(8,128)S(1)}, u32[]{:S(2)}, u32[]{:S(2)}) collective-permute-start(f32[512,128]{1,0:T(8,128)S(1)} %add_add_fusion.3), channel_id=1, source_target_pairs={{0,4},{1,5},{2,6},{3,7},{8,12},{9,13},{10,14},{11,15},{16,20},{17,... | collective-permute-start | bytes 786440 | tf_op jit(solution)/shard_map/ppermute | solution.py:300
  21.3 5.7 %collective-permute-start.5 = (f32[2,264,128]{2,1,0:T(8,128)S(1)}, f32[2,264,128]{2,1,0:T(8,128)S(1)}, u32[]{:S(2)}, u32[]{:S(2)}) collective-permute-start(f32[2,264,128]{2,1,0:T(8,128)S(1)} %get-tuple-element.99), channel_id=1, source_target_pairs={{1,0},{2,1},{3,2},{4,3},{5,4},{6,5},{7,6},{9,8},{10,9},{11,10},{12... | collective-permute-start | bytes 811016 | tf_op jit(solution)/shard_map/ppermute | solution.py:300
  22.6 7.0 %collective-permute-start.4 = (f32[2,264,128]{2,1,0:T(8,128)S(1)}, f32[2,264,128]{2,1,0:T(8,128)S(1)}, u32[]{:S(2)}, u32[]{:S(2)}) collective-permute-start(f32[2,264,128]{2,1,0:T(8,128)S(1)} %get-tuple-element.100), channel_id=1, source_target_pairs={{1,0},{2,1},{3,2},{4,3},{5,4},{6,5},{7,6},{9,8},{10,9},{11,10},{12... | collective-permute-start | bytes 811016 | tf_op jit(solution)/shard_map/ppermute | solution.py:300
  26.9 2.6 %collective-permute-start.3 = (f32[512,128]{1,0:T(8,128)S(1)}, f32[512,128]{1,0:T(8,128)S(1)}, u32[]{:S(2)}, u32[]{:S(2)}) collective-permute-start(f32[512,128]{1,0:T(8,128)S(1)} %get-tuple-element.90), channel_id=1, source_target_pairs={{0,1},{1,0},{2,3},{3,2},{4,5},{5,4},{6,7},{7,6},{8,9},{9,8},{10,11... | collective-permute-start | bytes 786440 | tf_op jit(solution)/shard_map/ppermute | solution.py:295
  32.0 3.6 %collective-permute-start.6 = (f32[512,128]{1,0:T(8,128)S(1)}, f32[512,128]{1,0:T(8,128)S(1)}, u32[]{:S(2)}, u32[]{:S(2)}) collective-permute-start(f32[512,128]{1,0:T(8,128)S(1)} %get-tuple-element.63), channel_id=1, source_target_pairs={{0,1},{1,0},{2,3},{3,2},{4,5},{5,4},{6,7},{7,6},{8,9},{9,8},{10,11... | collective-permute-start | bytes 786440 | tf_op jit(solution)/shard_map/ppermute | solution.py:295
  33.9 3.7 %collective-permute-start.11 = (f32[2,4,128]{2,1,0:T(4,128)S(1)}, f32[2,4,128]{2,1,0:T(4,128)S(1)}, u32[]{:S(2)}, u32[]{:S(2)}) collective-permute-start(f32[2,4,128]{2,1,0:T(4,128)S(1)} %broadcast_select_fusion.2), channel_id=1, source_target_pairs={{0,8},{8,0},{16,24},{24,16},{1,9},{9,1},{17,25},{25,17},{2,10},{10... | collective-permute-start | bytes 12296 | tf_op jit(solution)/shard_map/ppermute | solution.py:295
  35.6 12.5 %collective-permute-start.7 = (f32[512,128]{1,0:T(8,128)S(1)}, f32[512,128]{1,0:T(8,128)S(1)}, u32[]{:S(2)}, u32[]{:S(2)}) collective-permute-start(f32[512,128]{1,0:T(8,128)S(1)} %add.152.rest_0_), channel_id=1, source_target_pairs={{2,0},{3,1},{4,2},{5,3},{6,4},{7,5},{10,8},{11,9},{12,10},{13,11},... | collective-permute-start | bytes 786440 | tf_op jit(solution)/shard_map/ppermute | solution.py:300
  37.6 11.8 %collective-permute-start.12 = (f32[1,4,128]{2,1,0:T(4,128)S(1)}, f32[1,4,128]{2,1,0:T(4,128)S(1)}, u32[]{:S(2)}, u32[]{:S(2)}) collective-permute-start(f32[1,4,128]{2,1,0:T(4,128)S(1)} %slice_select_fusion), channel_id=1, source_target_pairs={{0,16},{8,24},{16,0},{24,8},{1,17},{9,25},{17,1},{25,9},{2,18},{10... | collective-permute-start | bytes 6152 | tf_op jit(solution)/shard_map/ppermute | solution.py:295
  48.1 16.1 %collective-permute-start.8 = (f32[512,128]{1,0:T(8,128)S(1)}, f32[512,128]{1,0:T(8,128)S(1)}, u32[]{:S(2)}, u32[]{:S(2)}) collective-permute-start(f32[512,128]{1,0:T(8,128)S(1)} %add_add_fusion.1.rest_0_), channel_id=1, source_target_pairs={{4,0},{5,1},{6,2},{7,3},{12,8},{13,9},{14,10},{15,11},{20,16},{21,... | collective-permute-start | bytes 786440 | tf_op jit(solution)/shard_map/ppermute | solution.py:300
  49.4 14.8 %collective-permute-start.13 = (f32[2,128]{1,0:T(2,128)S(1)}, f32[2,128]{1,0:T(2,128)S(1)}, u32[]{:S(2)}, u32[]{:S(2)}) collective-permute-start(f32[2,128]{1,0:T(2,128)S(1)} %broadcast_select_fusion.3), channel_id=1, source_target_pairs={{0,4},{1,5},{2,6},{3,7},{4,0},{5,1},{6,2},{7,3},{8,12},{9,13},{10,... | collective-permute-start | bytes 3080 | tf_op jit(solution)/shard_map/ppermute | solution.py:295
  53.1 11.4 %collective-permute-start.10 = (f32[4,264,128]{2,1,0:T(8,128)S(1)}, f32[4,264,128]{2,1,0:T(8,128)S(1)}, u32[]{:S(2)}, u32[]{:S(2)}) collective-permute-start(f32[4,264,128]{2,1,0:T(8,128)S(1)} %maximum_add_fusion), channel_id=1, source_target_pairs={{0,1},{1,2},{2,3},{3,4},{4,5},{5,6},{6,7},{8,9},{9,10},{10,11},{11... | collective-permute-start | bytes 1622024 | tf_op jit(solution)/shard_map/ppermute | solution.py:300
  64.3 3.6 %collective-permute-start.14 = (f32[1,128]{1,0:T(1,128)S(1)}, f32[1,128]{1,0:T(1,128)S(1)}, u32[]{:S(2)}, u32[]{:S(2)}) collective-permute-start(f32[1,128]{1,0:T(1,128)S(1)} %compare_select_fusion), channel_id=1, source_target_pairs={{0,2},{1,3},{2,0},{3,1},{4,6},{5,7},{6,4},{7,5},{8,10},{9,11},{10,... | collective-permute-start | bytes 1544 | tf_op jit(solution)/shard_map/ppermute | solution.py:295
  64.4 3.6 %collective-permute-start.9 = (f32[512,128]{1,0:T(8,128)S(1)}, f32[512,128]{1,0:T(8,128)S(1)}, u32[]{:S(2)}, u32[]{:S(2)}) collective-permute-start(f32[512,128]{1,0:T(8,128)S(1)} %add_select_fusion.1), channel_id=1, source_target_pairs={{0,1},{1,0},{2,3},{3,2},{4,5},{5,4},{6,7},{7,6},{8,9},{9,8},{10,11... | collective-permute-start | bytes 786440 | tf_op jit(solution)/shard_map/ppermute | solution.py:295
  68.0 2.5 %collective-permute-start.15 = (f32[1,64]{1,0:T(1,128)S(1)}, f32[1,64]{1,0:T(1,128)S(1)}, u32[]{:S(2)}, u32[]{:S(2)}) collective-permute-start(f32[1,64]{1,0:T(1,128)S(1)} %slice_select_fusion.1), channel_id=1, source_target_pairs={{0,1},{1,0},{2,3},{3,2},{4,5},{5,4},{6,7},{7,6},{8,9},{9,8},{10,11... | collective-permute-start | bytes 776 | tf_op jit(solution)/shard_map/ppermute | solution.py:295

commit v18 on v17

--- a/solution.py
+++ b/solution.py
@@ -103,11 +103,20 @@
     return group, base, base + (group + half) * lanes, base // PAIR * E
 
 
-def put_half(sel, core, k, v, out):
+def put_half(sel, core, k_in, v_in, k, v, out, sems):
     lanes = k.shape[1] // GROUPS // 2
     count = lanes // PAIR
-    for group in range(GROUPS):
-        base = (2 * group + (sel + core[0]) % 2) * lanes
+    bases = [(2 * group + (sel + core[0]) % 2) * lanes for group in range(GROUPS)]
+    copies = []
+    for group, base in enumerate(bases):
+        at = pl.ds(pl.multiple_of(base, lanes), lanes)
+        for i, (array, buf) in enumerate(((k_in, k), (v_in, v))):
+            copies.append(pltpu.make_async_copy(array.at[:, at], buf.at[:, at], sems.at[group, i]))
+    for copy in copies:
+        copy.start()
+    for group, base in enumerate(bases):
+        copies[2 * group].wait()
+        copies[2 * group + 1].wait()
         for p in range(count):
             at = lanes_at(base, p)
             row = (group * count + p) * E
@@ -117,26 +126,13 @@
 def send_kernel(core, ctx, dp, k_in, v_in, send, zero, k, v, core_row, ctx_row, dp_row, sems):
     for row, index in ((core_row, core), (ctx_row, ctx), (dp_row, dp)):
         row[...] = jnp.full(row.shape, index[0], jnp.int32)
-    lanes = k.shape[1] // GROUPS // 2
-    copies = []
-    for sel in (1, 0):
-        for group in range(GROUPS):
-            base = (2 * group + (sel + core[0]) % 2) * lanes
-            at = pl.ds(pl.multiple_of(base, lanes), lanes)
-            for i, (array, buf) in enumerate(((k_in, k), (v_in, v))):
-                copies.append(pltpu.make_async_copy(array.at[:, at], buf.at[:, at], sems.at[2 * group + sel, i]))
-    for copy in copies:
-        copy.start()
     zero[...] = jnp.zeros_like(zero)
-    for copy in copies[:2 * GROUPS]:
-        copy.wait()
-    put_half(1, core, k, v, send)
-    for copy in copies[2 * GROUPS:]:
-        copy.wait()
-
-
-def keep_kernel(core, k, v, *rest):
-    put_half(0, core, k, v, rest[-1])
+    put_half(1, core, k_in, v_in, k, v, send, sems)
+
+
+def keep_kernel(core, k_in, v_in, *rest):
+    keep, k, v, sems = rest[-4:]
+    put_half(0, core, k_in, v_in, k, v, keep, sems)
 
 
 def part_kernel(core, q_in, dy_in, k, v, seg, table, *rest):
@@ -302,6 +298,11 @@
 
 def nought(x):
     return jnp.minimum(jnp.abs(x), 0.0)
+
+
+def cycled(x, distance):
+    count = lax.axis_size("ctx")
+    return lax.ppermute(x, "ctx", [(i, (i + distance) % count) for i in range(count)])
 
 
 def within_chip(keep, send):
@@ -384,8 +385,9 @@
         for out_at, x in alias:
             if x is not None:
                 aliases[len(scalars) + len(operands)] = out_at
-                operands.append(x)
-                kinds.append("any")
+                in_vmem = outs[out_at][0] == "vmem"
+                operands.append(pinned(x, pltpu.VMEM) if in_vmem else x)
+                kinds.append("vmem" if in_vmem else "any")
         out_shape = [
             pltpu.VMEM(*shape, dtype) if kind == "vmem" else jax.ShapeDtypeStruct(shapes[kind], dtype)
             for kind, dtype, *shape in outs
@@ -441,7 +443,11 @@
     def summed_before(own, towards, works):
         load, before, span = own, None, 1
         while span < chips:
-            arrived = shifted(load, 2 * towards * span)
+            if span == 1:
+                first = ctx_row >> 1 == (0 if towards == 1 else chips - 1)
+                arrived = jnp.where(first, 0.0, cycled(load, 2 * towards))
+            else:
+                arrived = shifted(load, 2 * towards * span)
             if works:
                 arrived = arrived + works.pop(0)(load)
             before = arrived if before is None else before + arrived
@@ -451,12 +457,16 @@
             before = before + work(load)
         return before
 
+    in_hbm = [("hbm", k), ("hbm", v)]
+    semaphores = [pltpu.SemaphoreType.DMA((GROUPS, 2))]
     send, zero, k, v, core_row, ctx_row, dp_row = call(
-        send_kernel, 0, [("hbm", k), ("hbm", v)],
+        send_kernel, 0, in_hbm,
         [("all", F32), ("zero", jnp.int32), ("vmem", BF16, whole), ("vmem", BF16, whole)]
         + [("token", jnp.int32)] * 3,
-        scratch=[pltpu.SemaphoreType.DMA((2 * GROUPS, 2))], steps=(1,), scalars=[core, ctx, dp])
-    keep, = call(keep_kernel, 0, [("vmem", k), ("vmem", v)], [("all", F32)], steps=(1,))
+        scratch=semaphores, steps=(1,), scalars=[core, ctx, dp])
+    keep, k, v = call(
+        keep_kernel, 0, in_hbm, [("all", F32), ("vmem", BF16, whole), ("vmem", BF16, whole)],
+        alias=[(1, k), (2, v)], scratch=semaphores, steps=(1,))
     piece = within_chip(keep, send)
     seg = (segment_ids + zero)[0]
     onehot = seg[:, None] == jnp.arange(table.shape[0], dtype=jnp.int32)[None, :]

time: 71.4 us -> 71.6 us (level)
  waiting for transfers between devices: 13.4 us -> 9.78 us
  starting transfers between devices: 25.3 us -> 27.9 us
  Pallas kernels: 30 us -> 31.2 us
    ppermute x0 -> x2, starting transfers between devices: none -> 10.1 us  [cycled(): lax.ppermute(x, 'ctx', [(i, (i + distance) % count) for i in range(count)])]
    ppermute x7 -> x5, starting transfers between devices: 15.8 us -> 8.4 us  [shifted(): lax.ppermute(x, 'ctx', [(i, i + distance) for i in range(count) if 0 <= i...]
    ppermute x7 -> x5, waiting for transfers between devices: 11.3 us -> 7.52 us  [shifted(): lax.ppermute(x, 'ctx', [(i, i + distance) for i in range(count) if 0 <= i...]
    ppermute x0 -> x2, waiting for transfers between devices: none -> 1.31 us  [cycled(): lax.ppermute(x, 'ctx', [(i, (i + distance) % count) for i in range(count)])]
    pallas_call x11, Pallas kernels: 30 us -> 31.2 us  [call(): pl.pallas_call(kernel, grid_spec=pltpu.PrefetchScalarGridSpec(num_scalar_...]
    ppermute x9, waiting for transfers between devices: 2.12 us -> 0.94 us  [partner(): return lax.ppermute(x, axis, route)]
  transfers between devices with their start and end apart: 16 -> 16, of which waited for: 6 -> 4; matrix products, arithmetic and copies ran while one was open for 1% -> 1% of each run, Pallas kernels for 36% -> 38%
where the time goes in v18:
time: 71.6 us; the launch traced here: 71.3 us
  Pallas kernels  31.2 us (44%)
  starting transfers between devices  27.9 us (39%)
  waiting for transfers between devices  9.78 us (14%)
  other arithmetic  1.45 us (2%)
  between operations  0.95 us (1%)
    pallas_call x11, Pallas kernels, call(): pl.pallas_call(kernel, grid_spec=pltpu.PrefetchScalarGridSpec(num_scalar_...  31.2 us
    ppermute x2, starting transfers between devices, cycled(): lax.ppermute(x, 'ctx', [(i, (i + distance) % count) for i in range(count)])  10.1 us
    ppermute x9, starting transfers between devices, partner(): return lax.ppermute(x, axis, route)  9.47 us
    ppermute x5, starting transfers between devices, shifted(): lax.ppermute(x, 'ctx', [(i, i + distance) for i in range(count) if 0 <= i...  8.4 us
    ppermute x5, waiting for transfers between devices, shifted(): lax.ppermute(x, 'ctx', [(i, i + distance) for i in range(count) if 0 <= i...  7.52 us
  transfers between devices with their start and end apart: 16, of which 4 were waited for; matrix products, arithmetic and copies ran while one was open for 1% of the time, Pallas kernels for 38%

profile of v18, /device:TPU:0, one launch (start us, length us, event | category | flops | bytes accessed | tf_op | source)
XLA Modules:
  0.0 71.3 jit_solution(8884376594869454819)
XLA Ops:
  0.7 1.7 %shard_map.110 = (f32[512,128]{1,0:T(8,128)S(1)}, s32[1,256]{1,0:T(1,128)S(1)}, bf16[256,2048]{1,0:T(8,128)(2,1)S(1)}, bf16[256,2048]{1,0:T(8,128)(2,1)S(1)}, s3...) custom-call(s32[1]{0:T(128)} %bitcast.core, s32[1]{0:T(128)} %bitcast.5.ctx, s32[1]{0:T(128)} %bitcast.6.dp, ...), custom_call_target="tpu_custom_call" | custom-call | flops 1 | bytes 1 | tf_op jit(solution)/shard_map/pallas_call | solution.py:395
  3.0 1.7 %shard_map.111 = (f32[512,128]{1,0:T(8,128)S(1)}, bf16[256,2048]{1,0:T(8,128)(2,1)S(1)}, bf16[256,2048]{1,0:T(8,128)(2,1)S(1)}) custom-call(s32[1]{0:T(128)} %bitcast.core, bf16[256,2048]{1,0:T(8,128)(2,1)} %bitcast.52, bf16[256,2048]{1,0:T(8,128)(2,1)} %bitcast.54, ...), custom_call_target="tpu_custom_call", output_to_operand_aliasing={{1}: (3, {}), {2}: (4, {})} | custom-call | flops 1 | bytes 1 | tf_op jit(solution)/shard_map/pallas_call | solution.py:395
  5.0 2.7 %collective-permute-start.1 = (f32[512,128]{1,0:T(8,128)S(1)}, f32[512,128]{1,0:T(8,128)S(1)}, u32[]{:S(2)}, u32[]{:S(2)}) collective-permute-start(f32[512,128]{1,0:T(8,128)S(1)} %add.138.rest_0_), channel_id=1, source_target_pairs={{0,2},{1,3},{2,4},{3,5},{4,6},{5,7},{6,0},{7,1},{8,10},{9,11},{10,... | collective-permute-start | bytes 786440 | tf_op jit(solution)/shard_map/ppermute | solution.py:305
  7.6 2.6 %shard_map.112 = (f32[2,264,128]{2,1,0:T(8,128)S(1)}, f32[2,264,128]{2,1,0:T(8,128)S(1)}, bf16[256,2048]{1,0:T(8,128)(2,1)S(1)}, bf16[256,2048]{1,0:T(8,128)(2,1)S(1)}, f32[1,128]{1,0:T(1,128)}) custom-call(s32[1]{0:T(128)} %bitcast.core, bf16[256,2048]{1,0:T(8,128)(2,1)} %bitcast.56, bf16[256,2048]{1,0:T(8,128)(2,1)} %bitcast.57, ...), custom_call_target="tpu_custom_call" | custom-call | flops 1 | bytes 1 | tf_op jit(solution)/shard_map/pallas_call | solution.py:395
  10.3 2.5 %shard_map.114 = (f32[256,1024]{1,0:T(8,128)S(1)}, bf16[16,256,256]{2,1,0:T(8,128)(2,1)S(1)}, f32[1,128]{1,0:T(1,128)S(1)}) custom-call(s32[1]{0:T(128)} %bitcast.core, bf16[256,2048]{1,0:T(8,128)(2,1)S(1)} %get-tuple-element.54.q, bf16[256,2048]{1,0:T(8,128)(2,1)S(1)} %get-tuple-element.50.k, bf16[256,2048]{1,0:T(8,128)(2,1)S(1)} %get-tuple-element.51.v, ...), custom_call_target="tpu_custom_call" | custom-call | flops 1 | bytes 1 | tf_op jit(solution)/shard_map/pallas_call | solution.py:395
  12.8 2.5 %shard_map.113 = (f32[256,1024]{1,0:T(8,128)S(1)}, bf16[16,256,256]{2,1,0:T(8,128)(2,1)S(1)}, f32[1,128]{1,0:T(1,128)S(1)}) custom-call(s32[1]{0:T(128)} %bitcast.core, bf16[256,2048]{1,0:T(8,128)(2,1)S(1)} %get-tuple-element.54.q, bf16[256,2048]{1,0:T(8,128)(2,1)S(1)} %get-tuple-element.50.k, bf16[256,2048]{1,0:T(8,128)(2,1)S(1)} %get-tuple-element.51.v, ...), custom_call_target="tpu_custom_call" | custom-call | flops 1 | bytes 1 | tf_op jit(solution)/shard_map/pallas_call | solution.py:395
  15.3 1.3 %collective-permute-done.1 = f32[512,128]{1,0:T(8,128)S(1)} collective-permute-done((f32[512,128]{1,0:T(8,128)S(1)}, f32[512,128]{1,0:T(8,128)S(1)}, u32[]{:S(2)}, u32[]{:S(2)}) %collective-permute-start.1) | collective-permute-done | bytes 262176 | tf_op jit(solution)/shard_map/ppermute | solution.py:305
  16.6 3.2 %collective-permute-start.2 = (f32[512,128]{1,0:T(8,128)S(1)}, f32[512,128]{1,0:T(8,128)S(1)}, u32[]{:S(2)}, u32[]{:S(2)}) collective-permute-start(f32[512,128]{1,0:T(8,128)S(1)} %fusion.5), channel_id=1, source_target_pairs={{0,4},{1,5},{2,6},{3,7},{8,12},{9,13},{10,14},{11,15},{16,20},{17,... | collective-permute-start | bytes 786440 | tf_op jit(solution)/shard_map/ppermute | solution.py:296
  19.9 1.3 %collective-permute-start.5 = (f32[2,264,128]{2,1,0:T(8,128)S(1)}, f32[2,264,128]{2,1,0:T(8,128)S(1)}, u32[]{:S(2)}, u32[]{:S(2)}) collective-permute-start(f32[2,264,128]{2,1,0:T(8,128)S(1)} %get-tuple-element.107), channel_id=1, source_target_pairs={{1,0},{2,1},{3,2},{4,3},{5,4},{6,5},{7,6},{9,8},{10,9},{11,10},{12... | collective-permute-start | bytes 811016 | tf_op jit(solution)/shard_map/ppermute | solution.py:296
  21.2 1.3 %collective-permute-start.4 = (f32[2,264,128]{2,1,0:T(8,128)S(1)}, f32[2,264,128]{2,1,0:T(8,128)S(1)}, u32[]{:S(2)}, u32[]{:S(2)}) collective-permute-start(f32[2,264,128]{2,1,0:T(8,128)S(1)} %get-tuple-element.108), channel_id=1, source_target_pairs={{1,0},{2,1},{3,2},{4,3},{5,4},{6,5},{7,6},{9,8},{10,9},{11,10},{12... | collective-permute-start | bytes 811016 | tf_op jit(solution)/shard_map/ppermute | solution.py:296
  22.5 3.3 %collective-permute-done.2 = f32[512,128]{1,0:T(8,128)S(1)} collective-permute-done((f32[512,128]{1,0:T(8,128)S(1)}, f32[512,128]{1,0:T(8,128)S(1)}, u32[]{:S(2)}, u32[]{:S(2)}) %collective-permute-start.2) | collective-permute-done | bytes 262176 | tf_op jit(solution)/shard_map/ppermute | solution.py:296
  26.0 2.5 %shard_map.115 = (bf16[256,2048]{1,0:T(8,128)(2,1)}, bf16[256,1024]{1,0:T(8,128)(2,1)S(1)}, f32[2,264,128]{2,1,0:T(8,128)S(1)}, f32[2,4,128]{2,1,0:T(4,128)S(1)}...) custom-call(s32[1]{0:T(128)} %bitcast.core, bf16[256,2048]{1,0:T(8,128)(2,1)S(1)} %get-tuple-element.54.q, ...), custom_call_target="tpu_custom_call" | custom-call | flops 1 | bytes 1 | tf_op jit(solution)/shard_map/pallas_call | solution.py:395
  28.5 2.4 %shard_map.116 = (bf16[256,2048]{1,0:T(8,128)(2,1)}, bf16[256,1024]{1,0:T(8,128)(2,1)S(1)}, f32[2,264,128]{2,1,0:T(8,128)S(1)}, f32[2,4,128]{2,1,0:T(4,128)S(1)}...) custom-call(s32[1]{0:T(128)} %bitcast.core, ...), custom_call_target="tpu_custom_call", output_to_operand_aliasing={{0}: (10, {})} | custom-call | flops 1 | bytes 1 | tf_op jit(solution)/shard_map/pallas_call | solution.py:395
  30.9 2.0 %collective-permute-start.6 = (f32[512,128]{1,0:T(8,128)S(1)}, f32[512,128]{1,0:T(8,128)S(1)}, u32[]{:S(2)}, u32[]{:S(2)}) collective-permute-start(f32[512,128]{1,0:T(8,128)S(1)} %get-tuple-element.70), channel_id=1, source_target_pairs={{0,1},{1,0},{2,3},{3,2},{4,5},{5,4},{6,7},{7,6},{8,9},{9,8},{10,11... | collective-permute-start | bytes 786440 | tf_op jit(solution)/shard_map/ppermute | solution.py:291
  32.9 1.6 %collective-permute-start.11 = (f32[2,4,128]{2,1,0:T(4,128)S(1)}, f32[2,4,128]{2,1,0:T(4,128)S(1)}, u32[]{:S(2)}, u32[]{:S(2)}) collective-permute-start(f32[2,4,128]{2,1,0:T(4,128)S(1)} %broadcast_select_fusion.2), channel_id=1, source_target_pairs={{0,8},{8,0},{16,24},{24,16},{1,9},{9,1},{17,25},{25,17},{2,10},{10... | collective-permute-start | bytes 12296 | tf_op jit(solution)/shard_map/ppermute | solution.py:291
  34.5 7.4 %collective-permute-start.7 = (f32[512,128]{1,0:T(8,128)S(1)}, f32[512,128]{1,0:T(8,128)S(1)}, u32[]{:S(2)}, u32[]{:S(2)}) collective-permute-start(f32[512,128]{1,0:T(8,128)S(1)} %add.152.rest_0_), channel_id=1, source_target_pairs={{0,6},{1,7},{2,0},{3,1},{4,2},{5,3},{6,4},{7,5},{8,14},{9,15},{10,... | collective-permute-start | bytes 786440 | tf_op jit(solution)/shard_map/ppermute | solution.py:305
  41.9 1.6 %collective-permute-start.12 = (f32[1,4,128]{2,1,0:T(4,128)S(1)}, f32[1,4,128]{2,1,0:T(4,128)S(1)}, u32[]{:S(2)}, u32[]{:S(2)}) collective-permute-start(f32[1,4,128]{2,1,0:T(4,128)S(1)} %slice_select_fusion), channel_id=1, source_target_pairs={{0,16},{8,24},{16,0},{24,8},{1,17},{9,25},{17,1},{25,9},{2,18},{10... | collective-permute-start | bytes 6152 | tf_op jit(solution)/shard_map/ppermute | solution.py:291
  43.5 5.1 %shard_map.117 = (bf16[256,2048]{1,0:T(8,128)(2,1)}, f32[256,1024]{1,0:T(8,128)S(1)}, f32[256,1024]{1,0:T(8,128)S(1)}, f32[1,128]{1,0:T(1,128)S(1)}) custom-call(s32[1]{0:T(128)} %bitcast.core, bf16[256,2048]{1,0:T(8,128)(2,1)S(1)} %get-tuple-element.54.q, bf16[256,2048]{1,0:T(8,128)(2,1)S(1)} %get-tuple-element.50.k, ...), custom_call_target="tpu_custom_call" | custom-call | flops 1 | bytes 1 | tf_op jit(solution)/shard_map/pallas_call | solution.py:395
  50.0 3.6 %collective-permute-start.13 = (f32[2,128]{1,0:T(2,128)S(1)}, f32[2,128]{1,0:T(2,128)S(1)}, u32[]{:S(2)}, u32[]{:S(2)}) collective-permute-start(f32[2,128]{1,0:T(2,128)S(1)} %broadcast_select_fusion.3), channel_id=1, source_target_pairs={{0,4},{1,5},{2,6},{3,7},{4,0},{5,1},{6,2},{7,3},{8,12},{9,13},{10,... | collective-permute-start | bytes 3080 | tf_op jit(solution)/shard_map/ppermute | solution.py:291
  53.7 1.3 %collective-permute-start.10 = (f32[4,264,128]{2,1,0:T(8,128)S(1)}, f32[4,264,128]{2,1,0:T(8,128)S(1)}, u32[]{:S(2)}, u32[]{:S(2)}) collective-permute-start(f32[4,264,128]{2,1,0:T(8,128)S(1)} %maximum_add_fusion), channel_id=1, source_target_pairs={{0,1},{1,2},{2,3},{3,4},{4,5},{5,6},{6,7},{8,9},{9,10},{10,11},{11... | collective-permute-start | bytes 1622024 | tf_op jit(solution)/shard_map/ppermute | solution.py:296
  55.0 5.2 %shard_map.118 = (bf16[256,2048]{1,0:T(8,128)(2,1)}, f32[256,1024]{1,0:T(8,128)S(1)}, f32[256,1024]{1,0:T(8,128)S(1)}, f32[1,128]{1,0:T(1,128)S(1)}) custom-call(s32[1]{0:T(128)} %bitcast.core, bf16[256,2048]{1,0:T(8,128)(2,1)S(1)} %get-tuple-element.54.q, bf16[256,2048]{1,0:T(8,128)(2,1)S(1)} %get-tuple-element.50.k, ...), custom_call_target="tpu_custom_call", output_to_operand_aliasing={{0}: (12, {})} | custom-call | flops 1 | bytes 1 | tf_op jit(solution)/shard_map/pallas_call | solution.py:395
  60.2 4.2 %collective-permute-done.8 = f32[512,128]{1,0:T(8,128)S(1)} collective-permute-done((f32[512,128]{1,0:T(8,128)S(1)}, f32[512,128]{1,0:T(8,128)S(1)}, u32[]{:S(2)}, u32[]{:S(2)}) %collective-permute-start.8) | collective-permute-done | bytes 262176 | tf_op jit(solution)/shard_map/ppermute | solution.py:296
  64.8 2.5 %shard_map.119 = (bf16[256,2048]{1,0:T(8,128)(2,1)}, bf16[256,2048]{1,0:T(8,128)(2,1)}, f32[1,128]{1,0:T(1,128)S(1)}) custom-call(s32[1]{0:T(128)} %bitcast.core, bf16[256,2048]{1,0:T(8,128)(2,1)S(1)} %get-tuple-element.50.k, bf16[256,2048]{1,0:T(8,128)(2,1)S(1)} %get-tuple-element.51.v, f32[256,1024]{1,0:T(8,128)S(1)} %get-tuple-element.81.gk_in, ...), custom_call_target="tpu_custom_call" | custom-call | flops 1 | bytes 1 | tf_op jit(solution)/shard_map/pallas_call | solution.py:395
  68.3 2.5 %shard_map.120 = (bf16[256,2048]{1,0:T(8,128)(2,1)}, bf16[256,2048]{1,0:T(8,128)(2,1)}, f32[1,128]{1,0:T(1,128)}) custom-call(s32[1]{0:T(128)} %bitcast.core, bf16[256,2048]{1,0:T(8,128)(2,1)S(1)} %get-tuple-element.50.k, bf16[256,2048]{1,0:T(8,128)(2,1)S(1)} %get-tuple-element.51.v, ...), custom_call_target="tpu_custom_call", output_to_operand_aliasing={{0}: (9, {}), {1}: (10, {})} | custom-call | flops 1 | bytes 1 | tf_op jit(solution)/shard_map/pallas_call | solution.py:395
  (57 shorter events, 4.4 us)
Async XLA Ops:
  0.6 2.3 %copy-start = (s32[1,256]{1,0:T(1,128)S(1)}, s32[1,256]{1,0:T(1,128)}, u32[]{:S(2)}) copy-start(s32[1,256]{1,0:T(1,128)} %seg.13) | copy-start | bytes 3076
  0.6 2.3 %copy-start.2 = (s32[1,32]{1,0:T(1,128)S(1)}, s32[1,32]{1,0:T(1,128)}, u32[]{:S(2)}) copy-start(s32[1,32]{1,0:T(1,128)} %table.13) | copy-start | bytes 388
  2.4 2.5 %collective-permute-start = (f32[512,128]{1,0:T(8,128)S(1)}, f32[512,128]{1,0:T(8,128)S(1)}, u32[]{:S(2)}, u32[]{:S(2)}) collective-permute-start(f32[512,128]{1,0:T(8,128)S(1)} %get-tuple-element.53), channel_id=1, source_target_pairs={{0,1},{1,0},{2,3},{3,2},{4,5},{5,4},{6,7},{7,6},{8,9},{9,8},{10,11... | collective-permute-start | bytes 786440 | tf_op jit(solution)/shard_map/ppermute | solution.py:291
  5.0 11.6 %collective-permute-start.1 = (f32[512,128]{1,0:T(8,128)S(1)}, f32[512,128]{1,0:T(8,128)S(1)}, u32[]{:S(2)}, u32[]{:S(2)}) collective-permute-start(f32[512,128]{1,0:T(8,128)S(1)} %add.138.rest_0_), channel_id=1, source_target_pairs={{0,2},{1,3},{2,4},{3,5},{4,6},{5,7},{6,0},{7,1},{8,10},{9,11},{10,... | collective-permute-start | bytes 786440 | tf_op jit(solution)/shard_map/ppermute | solution.py:305
  15.2 10.7 %copy-start.1 = (f32[2048]{0:T(1024)S(1)}, f32[2048]{0:T(1024)}, u32[]{:S(2)}) copy-start(f32[2048]{0:T(1024)} %param.13) | copy-start | bytes 24580
  16.6 9.2 %collective-permute-start.2 = (f32[512,128]{1,0:T(8,128)S(1)}, f32[512,128]{1,0:T(8,128)S(1)}, u32[]{:S(2)}, u32[]{:S(2)}) collective-permute-start(f32[512,128]{1,0:T(8,128)S(1)} %fusion.5), channel_id=1, source_target_pairs={{0,4},{1,5},{2,6},{3,7},{8,12},{9,13},{10,14},{11,15},{16,20},{17,... | collective-permute-start | bytes 786440 | tf_op jit(solution)/shard_map/ppermute | solution.py:296
  19.9 6.1 %collective-permute-start.5 = (f32[2,264,128]{2,1,0:T(8,128)S(1)}, f32[2,264,128]{2,1,0:T(8,128)S(1)}, u32[]{:S(2)}, u32[]{:S(2)}) collective-permute-start(f32[2,264,128]{2,1,0:T(8,128)S(1)} %get-tuple-element.107), channel_id=1, source_target_pairs={{1,0},{2,1},{3,2},{4,3},{5,4},{6,5},{7,6},{9,8},{10,9},{11,10},{12... | collective-permute-start | bytes 811016 | tf_op jit(solution)/shard_map/ppermute | solution.py:296
  21.2 7.3 %collective-permute-start.4 = (f32[2,264,128]{2,1,0:T(8,128)S(1)}, f32[2,264,128]{2,1,0:T(8,128)S(1)}, u32[]{:S(2)}, u32[]{:S(2)}) collective-permute-start(f32[2,264,128]{2,1,0:T(8,128)S(1)} %get-tuple-element.108), channel_id=1, source_target_pairs={{1,0},{2,1},{3,2},{4,3},{5,4},{6,5},{7,6},{9,8},{10,9},{11,10},{12... | collective-permute-start | bytes 811016 | tf_op jit(solution)/shard_map/ppermute | solution.py:296
  25.9 2.6 %collective-permute-start.3 = (f32[512,128]{1,0:T(8,128)S(1)}, f32[512,128]{1,0:T(8,128)S(1)}, u32[]{:S(2)}, u32[]{:S(2)}) collective-permute-start(f32[512,128]{1,0:T(8,128)S(1)} %get-tuple-element.96), channel_id=1, source_target_pairs={{0,1},{1,0},{2,3},{3,2},{4,5},{5,4},{6,7},{7,6},{8,9},{9,8},{10,11... | collective-permute-start | bytes 786440 | tf_op jit(solution)/shard_map/ppermute | solution.py:291
  30.9 3.6 %collective-permute-start.6 = (f32[512,128]{1,0:T(8,128)S(1)}, f32[512,128]{1,0:T(8,128)S(1)}, u32[]{:S(2)}, u32[]{:S(2)}) collective-permute-start(f32[512,128]{1,0:T(8,128)S(1)} %get-tuple-element.70), channel_id=1, source_target_pairs={{0,1},{1,0},{2,3},{3,2},{4,5},{5,4},{6,7},{7,6},{8,9},{9,8},{10,11... | collective-permute-start | bytes 786440 | tf_op jit(solution)/shard_map/ppermute | solution.py:291
  32.9 9.0 %collective-permute-start.11 = (f32[2,4,128]{2,1,0:T(4,128)S(1)}, f32[2,4,128]{2,1,0:T(4,128)S(1)}, u32[]{:S(2)}, u32[]{:S(2)}) collective-permute-start(f32[2,4,128]{2,1,0:T(4,128)S(1)} %broadcast_select_fusion.2), channel_id=1, source_target_pairs={{0,8},{8,0},{16,24},{24,16},{1,9},{9,1},{17,25},{25,17},{2,10},{10... | collective-permute-start | bytes 12296 | tf_op jit(solution)/shard_map/ppermute | solution.py:291
  34.5 14.1 %collective-permute-start.7 = (f32[512,128]{1,0:T(8,128)S(1)}, f32[512,128]{1,0:T(8,128)S(1)}, u32[]{:S(2)}, u32[]{:S(2)}) collective-permute-start(f32[512,128]{1,0:T(8,128)S(1)} %add.152.rest_0_), channel_id=1, source_target_pairs={{0,6},{1,7},{2,0},{3,1},{4,2},{5,3},{6,4},{7,5},{8,14},{9,15},{10,... | collective-permute-start | bytes 786440 | tf_op jit(solution)/shard_map/ppermute | solution.py:305
  41.9 8.0 %collective-permute-start.12 = (f32[1,4,128]{2,1,0:T(4,128)S(1)}, f32[1,4,128]{2,1,0:T(4,128)S(1)}, u32[]{:S(2)}, u32[]{:S(2)}) collective-permute-start(f32[1,4,128]{2,1,0:T(4,128)S(1)} %slice_select_fusion), channel_id=1, source_target_pairs={{0,16},{8,24},{16,0},{24,8},{1,17},{9,25},{17,1},{25,9},{2,18},{10... | collective-permute-start | bytes 6152 | tf_op jit(solution)/shard_map/ppermute | solution.py:291
  48.7 15.7 %collective-permute-start.8 = (f32[512,128]{1,0:T(8,128)S(1)}, f32[512,128]{1,0:T(8,128)S(1)}, u32[]{:S(2)}, u32[]{:S(2)}) collective-permute-start(f32[512,128]{1,0:T(8,128)S(1)} %fusion.6.rest_0_), channel_id=1, source_target_pairs={{4,0},{5,1},{6,2},{7,3},{12,8},{13,9},{14,10},{15,11},{20,16},{21,... | collective-permute-start | bytes 786440 | tf_op jit(solution)/shard_map/ppermute | solution.py:296
  50.0 14.5 %collective-permute-start.13 = (f32[2,128]{1,0:T(2,128)S(1)}, f32[2,128]{1,0:T(2,128)S(1)}, u32[]{:S(2)}, u32[]{:S(2)}) collective-permute-start(f32[2,128]{1,0:T(2,128)S(1)} %broadcast_select_fusion.3), channel_id=1, source_target_pairs={{0,4},{1,5},{2,6},{3,7},{4,0},{5,1},{6,2},{7,3},{8,12},{9,13},{10,... | collective-permute-start | bytes 3080 | tf_op jit(solution)/shard_map/ppermute | solution.py:291
  53.7 11.1 %collective-permute-start.10 = (f32[4,264,128]{2,1,0:T(8,128)S(1)}, f32[4,264,128]{2,1,0:T(8,128)S(1)}, u32[]{:S(2)}, u32[]{:S(2)}) collective-permute-start(f32[4,264,128]{2,1,0:T(8,128)S(1)} %maximum_add_fusion), channel_id=1, source_target_pairs={{0,1},{1,2},{2,3},{3,4},{4,5},{5,6},{6,7},{8,9},{9,10},{10,11},{11... | collective-permute-start | bytes 1622024 | tf_op jit(solution)/shard_map/ppermute | solution.py:296
  64.5 3.6 %collective-permute-start.14 = (f32[1,128]{1,0:T(1,128)S(1)}, f32[1,128]{1,0:T(1,128)S(1)}, u32[]{:S(2)}, u32[]{:S(2)}) collective-permute-start(f32[1,128]{1,0:T(1,128)S(1)} %compare_select_fusion), channel_id=1, source_target_pairs={{0,2},{1,3},{2,0},{3,1},{4,6},{5,7},{6,4},{7,5},{8,10},{9,11},{10,... | collective-permute-start | bytes 1544 | tf_op jit(solution)/shard_map/ppermute | solution.py:291
  64.7 3.6 %collective-permute-start.9 = (f32[512,128]{1,0:T(8,128)S(1)}, f32[512,128]{1,0:T(8,128)S(1)}, u32[]{:S(2)}, u32[]{:S(2)}) collective-permute-start(f32[512,128]{1,0:T(8,128)S(1)} %add_select_fusion.1), channel_id=1, source_target_pairs={{0,1},{1,0},{2,3},{3,2},{4,5},{5,4},{6,7},{7,6},{8,9},{9,8},{10,11... | collective-permute-start | bytes 786440 | tf_op jit(solution)/shard_map/ppermute | solution.py:291
  68.2 2.5 %collective-permute-start.15 = (f32[1,64]{1,0:T(1,128)S(1)}, f32[1,64]{1,0:T(1,128)S(1)}, u32[]{:S(2)}, u32[]{:S(2)}) collective-permute-start(f32[1,64]{1,0:T(1,128)S(1)} %slice_select_fusion.1), channel_id=1, source_target_pairs={{0,1},{1,0},{2,3},{3,2},{4,5},{5,4},{6,7},{7,6},{8,9},{9,8},{10,11... | collective-permute-start | bytes 776 | tf_op jit(solution)/shard_map/ppermute | solution.py:291

commit v19 on v17

--- a/solution.py
+++ b/solution.py
@@ -302,6 +302,11 @@
 
 def nought(x):
     return jnp.minimum(jnp.abs(x), 0.0)
+
+
+def cycled(x, distance):
+    count = lax.axis_size("ctx")
+    return lax.ppermute(x, "ctx", [(i, (i + distance) % count) for i in range(count)])
 
 
 def within_chip(keep, send):
@@ -441,7 +446,10 @@
     def summed_before(own, towards, works):
         load, before, span = own, None, 1
         while span < chips:
-            arrived = shifted(load, 2 * towards * span)
+            if span == 1 and towards == 1:
+                arrived = jnp.where(ctx_row < 2, 0.0, cycled(load, 2))
+            else:
+                arrived = shifted(load, 2 * towards * span)
             if works:
                 arrived = arrived + works.pop(0)(load)
             before = arrived if before is None else before + arrived

time: 71.4 us -> 69.7 us (0.976)
  starting transfers between devices: 25.3 us -> 22.5 us
  waiting for transfers between devices: 13.4 us -> 14.5 us
    ppermute x7 -> x6, starting transfers between devices: 15.8 us -> 10 us  [shifted(): lax.ppermute(x, 'ctx', [(i, i + distance) for i in range(count) if 0 <= i...]
    ppermute x0 -> x1, starting transfers between devices: none -> 3 us  [cycled(): lax.ppermute(x, 'ctx', [(i, (i + distance) % count) for i in range(count)])]
    ppermute x0 -> x1, waiting for transfers between devices: none -> 0.97 us  [cycled(): lax.ppermute(x, 'ctx', [(i, (i + distance) % count) for i in range(count)])]
    ppermute x7 -> x6, waiting for transfers between devices: 11.3 us -> 11.4 us  [shifted(): lax.ppermute(x, 'ctx', [(i, i + distance) for i in range(count) if 0 <= i...]
  transfers between devices with their start and end apart: 16 -> 16, of which waited for: 6 -> 7; matrix products, arithmetic and copies ran while one was open for 1% -> 1% of each run, Pallas kernels for 36% -> 37%
where the time goes in v19:
time: 69.7 us; the launch traced here: 69.4 us
  Pallas kernels  30 us (43%)
  starting transfers between devices  22.5 us (32%)
  waiting for transfers between devices  14.5 us (21%)
  other arithmetic  1.42 us (2%)
  between operations  0.96 us (1%)
    pallas_call x11, Pallas kernels, call(): pl.pallas_call(kernel, grid_spec=pltpu.PrefetchScalarGridSpec(num_scalar_...  30 us
    ppermute x6, waiting for transfers between devices, shifted(): lax.ppermute(x, 'ctx', [(i, i + distance) for i in range(count) if 0 <= i...  11.4 us
    ppermute x6, starting transfers between devices, shifted(): lax.ppermute(x, 'ctx', [(i, i + distance) for i in range(count) if 0 <= i...  10 us
    ppermute x9, starting transfers between devices, partner(): return lax.ppermute(x, axis, route)  9.49 us
    ppermute x1, starting transfers between devices, cycled(): lax.ppermute(x, 'ctx', [(i, (i + distance) % count) for i in range(count)])  3 us
    ppermute x9, waiting for transfers between devices, partner(): return lax.ppermute(x, axis, route)  2.11 us
  transfers between devices with their start and end apart: 16, of which 7 were waited for; matrix products, arithmetic and copies ran while one was open for 1% of the time, Pallas kernels for 37%

profile of v19, /device:TPU:0, one launch (start us, length us, event | category | flops | bytes accessed | tf_op | source)
XLA Modules:
  0.0 69.4 jit_solution(8329554118057980024)
XLA Ops:
  0.7 1.8 %shard_map.110 = (f32[512,128]{1,0:T(8,128)S(1)}, s32[1,256]{1,0:T(1,128)S(1)}, bf16[256,2048]{1,0:T(8,128)(2,1)S(1)}, bf16[256,2048]{1,0:T(8,128)(2,1)S(1)}, s3...) custom-call(s32[1]{0:T(128)} %bitcast.core, s32[1]{0:T(128)} %bitcast.3.ctx, s32[1]{0:T(128)} %bitcast.4.dp, ...), custom_call_target="tpu_custom_call" | custom-call | flops 1 | bytes 1 | tf_op jit(solution)/shard_map/pallas_call | solution.py:398
  4.1 3.0 %collective-permute-start.1 = (f32[512,128]{1,0:T(8,128)S(1)}, f32[512,128]{1,0:T(8,128)S(1)}, u32[]{:S(2)}, u32[]{:S(2)}) collective-permute-start(f32[512,128]{1,0:T(8,128)S(1)} %add.138.rest_0_), channel_id=1, source_target_pairs={{0,2},{1,3},{2,4},{3,5},{4,6},{5,7},{6,0},{7,1},{8,10},{9,11},{10,... | collective-permute-start | bytes 786440 | tf_op jit(solution)/shard_map/ppermute | solution.py:309
  7.1 2.6 %shard_map.112 = (f32[2,264,128]{2,1,0:T(8,128)S(1)}, f32[2,264,128]{2,1,0:T(8,128)S(1)}, bf16[256,2048]{1,0:T(8,128)(2,1)S(1)}, bf16[256,2048]{1,0:T(8,128)(2,1)S(1)}, f32[1,128]{1,0:T(1,128)}) custom-call(s32[1]{0:T(128)} %bitcast.core, bf16[256,2048]{1,0:T(8,128)(2,1)} %bitcast.52, bf16[256,2048]{1,0:T(8,128)(2,1)} %bitcast.53, ...), custom_call_target="tpu_custom_call" | custom-call | flops 1 | bytes 1 | tf_op jit(solution)/shard_map/pallas_call | solution.py:398
  9.8 2.5 %shard_map.114 = (f32[256,1024]{1,0:T(8,128)S(1)}, bf16[16,256,256]{2,1,0:T(8,128)(2,1)S(1)}, f32[1,128]{1,0:T(1,128)S(1)}) custom-call(s32[1]{0:T(128)} %bitcast.core, bf16[256,2048]{1,0:T(8,128)(2,1)S(1)} %get-tuple-element.48.q, bf16[256,2048]{1,0:T(8,128)(2,1)S(1)} %get-tuple-element.45.k, bf16[256,2048]{1,0:T(8,128)(2,1)S(1)} %get-tuple-element.46.v, ...), custom_call_target="tpu_custom_call" | custom-call | flops 1 | bytes 1 | tf_op jit(solution)/shard_map/pallas_call | solution.py:398
  12.3 2.5 %shard_map.113 = (f32[256,1024]{1,0:T(8,128)S(1)}, bf16[16,256,256]{2,1,0:T(8,128)(2,1)S(1)}, f32[1,128]{1,0:T(1,128)S(1)}) custom-call(s32[1]{0:T(128)} %bitcast.core, bf16[256,2048]{1,0:T(8,128)(2,1)S(1)} %get-tuple-element.48.q, bf16[256,2048]{1,0:T(8,128)(2,1)S(1)} %get-tuple-element.45.k, bf16[256,2048]{1,0:T(8,128)(2,1)S(1)} %get-tuple-element.46.v, ...), custom_call_target="tpu_custom_call" | custom-call | flops 1 | bytes 1 | tf_op jit(solution)/shard_map/pallas_call | solution.py:398
  15.8 3.5 %collective-permute-start.2 = (f32[512,128]{1,0:T(8,128)S(1)}, f32[512,128]{1,0:T(8,128)S(1)}, u32[]{:S(2)}, u32[]{:S(2)}) collective-permute-start(f32[512,128]{1,0:T(8,128)S(1)} %fusion.5), channel_id=1, source_target_pairs={{0,4},{1,5},{2,6},{3,7},{8,12},{9,13},{10,14},{11,15},{16,20},{17,... | collective-permute-start | bytes 786440 | tf_op jit(solution)/shard_map/ppermute | solution.py:300
  19.4 1.3 %collective-permute-start.5 = (f32[2,264,128]{2,1,0:T(8,128)S(1)}, f32[2,264,128]{2,1,0:T(8,128)S(1)}, u32[]{:S(2)}, u32[]{:S(2)}) collective-permute-start(f32[2,264,128]{2,1,0:T(8,128)S(1)} %get-tuple-element.100), channel_id=1, source_target_pairs={{1,0},{2,1},{3,2},{4,3},{5,4},{6,5},{7,6},{9,8},{10,9},{11,10},{12... | collective-permute-start | bytes 811016 | tf_op jit(solution)/shard_map/ppermute | solution.py:300
  20.7 1.3 %collective-permute-start.4 = (f32[2,264,128]{2,1,0:T(8,128)S(1)}, f32[2,264,128]{2,1,0:T(8,128)S(1)}, u32[]{:S(2)}, u32[]{:S(2)}) collective-permute-start(f32[2,264,128]{2,1,0:T(8,128)S(1)} %get-tuple-element.101), channel_id=1, source_target_pairs={{1,0},{2,1},{3,2},{4,3},{5,4},{6,5},{7,6},{9,8},{10,9},{11,10},{12... | collective-permute-start | bytes 811016 | tf_op jit(solution)/shard_map/ppermute | solution.py:300
  22.0 3.0 %collective-permute-done.2 = f32[512,128]{1,0:T(8,128)S(1)} collective-permute-done((f32[512,128]{1,0:T(8,128)S(1)}, f32[512,128]{1,0:T(8,128)S(1)}, u32[]{:S(2)}, u32[]{:S(2)}) %collective-permute-start.2) | collective-permute-done | bytes 262176 | tf_op jit(solution)/shard_map/ppermute | solution.py:300
  25.2 2.5 %shard_map.115 = (bf16[256,2048]{1,0:T(8,128)(2,1)}, bf16[256,1024]{1,0:T(8,128)(2,1)S(1)}, f32[2,264,128]{2,1,0:T(8,128)S(1)}, f32[2,4,128]{2,1,0:T(4,128)S(1)}...) custom-call(s32[1]{0:T(128)} %bitcast.core, bf16[256,2048]{1,0:T(8,128)(2,1)S(1)} %get-tuple-element.48.q, ...), custom_call_target="tpu_custom_call" | custom-call | flops 1 | bytes 1 | tf_op jit(solution)/shard_map/pallas_call | solution.py:398
  27.7 2.4 %shard_map.116 = (bf16[256,2048]{1,0:T(8,128)(2,1)}, bf16[256,1024]{1,0:T(8,128)(2,1)S(1)}, f32[2,264,128]{2,1,0:T(8,128)S(1)}, f32[2,4,128]{2,1,0:T(4,128)S(1)}...) custom-call(s32[1]{0:T(128)} %bitcast.core, ...), custom_call_target="tpu_custom_call", output_to_operand_aliasing={{0}: (10, {})} | custom-call | flops 1 | bytes 1 | tf_op jit(solution)/shard_map/pallas_call | solution.py:398
  30.1 2.0 %collective-permute-start.6 = (f32[512,128]{1,0:T(8,128)S(1)}, f32[512,128]{1,0:T(8,128)S(1)}, u32[]{:S(2)}, u32[]{:S(2)}) collective-permute-start(f32[512,128]{1,0:T(8,128)S(1)} %get-tuple-element.64), channel_id=1, source_target_pairs={{0,1},{1,0},{2,3},{3,2},{4,5},{5,4},{6,7},{7,6},{8,9},{9,8},{10,11... | collective-permute-start | bytes 786440 | tf_op jit(solution)/shard_map/ppermute | solution.py:295
  32.1 1.6 %collective-permute-start.11 = (f32[2,4,128]{2,1,0:T(4,128)S(1)}, f32[2,4,128]{2,1,0:T(4,128)S(1)}, u32[]{:S(2)}, u32[]{:S(2)}) collective-permute-start(f32[2,4,128]{2,1,0:T(4,128)S(1)} %broadcast_select_fusion.2), channel_id=1, source_target_pairs={{0,8},{8,0},{16,24},{24,16},{1,9},{9,1},{17,25},{25,17},{2,10},{10... | collective-permute-start | bytes 12296 | tf_op jit(solution)/shard_map/ppermute | solution.py:295
  33.7 1.3 %collective-permute-start.7 = (f32[512,128]{1,0:T(8,128)S(1)}, f32[512,128]{1,0:T(8,128)S(1)}, u32[]{:S(2)}, u32[]{:S(2)}) collective-permute-start(f32[512,128]{1,0:T(8,128)S(1)} %add.152.rest_0_), channel_id=1, source_target_pairs={{2,0},{3,1},{4,2},{5,3},{6,4},{7,5},{10,8},{11,9},{12,10},{13,11},... | collective-permute-start | bytes 786440 | tf_op jit(solution)/shard_map/ppermute | solution.py:300
  35.8 1.6 %collective-permute-start.12 = (f32[1,4,128]{2,1,0:T(4,128)S(1)}, f32[1,4,128]{2,1,0:T(4,128)S(1)}, u32[]{:S(2)}, u32[]{:S(2)}) collective-permute-start(f32[1,4,128]{2,1,0:T(4,128)S(1)} %slice_select_fusion), channel_id=1, source_target_pairs={{0,16},{8,24},{16,0},{24,8},{1,17},{9,25},{17,1},{25,9},{2,18},{10... | collective-permute-start | bytes 6152 | tf_op jit(solution)/shard_map/ppermute | solution.py:295
  37.4 5.1 %shard_map.117 = (bf16[256,2048]{1,0:T(8,128)(2,1)}, f32[256,1024]{1,0:T(8,128)S(1)}, f32[256,1024]{1,0:T(8,128)S(1)}, f32[1,128]{1,0:T(1,128)S(1)}) custom-call(s32[1]{0:T(128)} %bitcast.core, bf16[256,2048]{1,0:T(8,128)(2,1)S(1)} %get-tuple-element.48.q, bf16[256,2048]{1,0:T(8,128)(2,1)S(1)} %get-tuple-element.45.k, ...), custom_call_target="tpu_custom_call" | custom-call | flops 1 | bytes 1 | tf_op jit(solution)/shard_map/pallas_call | solution.py:398
  42.5 3.9 %collective-permute-done.7 = f32[512,128]{1,0:T(8,128)S(1)} collective-permute-done((f32[512,128]{1,0:T(8,128)S(1)}, f32[512,128]{1,0:T(8,128)S(1)}, u32[]{:S(2)}, u32[]{:S(2)}) %collective-permute-start.7) | collective-permute-done | bytes 262176 | tf_op jit(solution)/shard_map/ppermute | solution.py:300
  46.4 1.3 %collective-permute-start.8 = (f32[512,128]{1,0:T(8,128)S(1)}, f32[512,128]{1,0:T(8,128)S(1)}, u32[]{:S(2)}, u32[]{:S(2)}) collective-permute-start(f32[512,128]{1,0:T(8,128)S(1)} %add_add_fusion.1.rest_0_), channel_id=1, source_target_pairs={{4,0},{5,1},{6,2},{7,3},{12,8},{13,9},{14,10},{15,11},{20,16},{21,... | collective-permute-start | bytes 786440 | tf_op jit(solution)/shard_map/ppermute | solution.py:300
  47.7 3.6 %collective-permute-start.13 = (f32[2,128]{1,0:T(2,128)S(1)}, f32[2,128]{1,0:T(2,128)S(1)}, u32[]{:S(2)}, u32[]{:S(2)}) collective-permute-start(f32[2,128]{1,0:T(2,128)S(1)} %broadcast_select_fusion.3), channel_id=1, source_target_pairs={{0,4},{1,5},{2,6},{3,7},{4,0},{5,1},{6,2},{7,3},{8,12},{9,13},{10,... | collective-permute-start | bytes 3080 | tf_op jit(solution)/shard_map/ppermute | solution.py:295
  51.4 1.3 %collective-permute-start.10 = (f32[4,264,128]{2,1,0:T(8,128)S(1)}, f32[4,264,128]{2,1,0:T(8,128)S(1)}, u32[]{:S(2)}, u32[]{:S(2)}) collective-permute-start(f32[4,264,128]{2,1,0:T(8,128)S(1)} %maximum_add_fusion), channel_id=1, source_target_pairs={{0,1},{1,2},{2,3},{3,4},{4,5},{5,6},{6,7},{8,9},{9,10},{10,11},{11... | collective-permute-start | bytes 1622024 | tf_op jit(solution)/shard_map/ppermute | solution.py:300
  52.7 5.2 %shard_map.118 = (bf16[256,2048]{1,0:T(8,128)(2,1)}, f32[256,1024]{1,0:T(8,128)S(1)}, f32[256,1024]{1,0:T(8,128)S(1)}, f32[1,128]{1,0:T(1,128)S(1)}) custom-call(s32[1]{0:T(128)} %bitcast.core, bf16[256,2048]{1,0:T(8,128)(2,1)S(1)} %get-tuple-element.48.q, bf16[256,2048]{1,0:T(8,128)(2,1)S(1)} %get-tuple-element.45.k, ...), custom_call_target="tpu_custom_call", output_to_operand_aliasing={{0}: (12, {})} | custom-call | flops 1 | bytes 1 | tf_op jit(solution)/shard_map/pallas_call | solution.py:398
  57.9 4.6 %collective-permute-done.8 = f32[512,128]{1,0:T(8,128)S(1)} collective-permute-done((f32[512,128]{1,0:T(8,128)S(1)}, f32[512,128]{1,0:T(8,128)S(1)}, u32[]{:S(2)}, u32[]{:S(2)}) %collective-permute-start.8) | collective-permute-done | bytes 262176 | tf_op jit(solution)/shard_map/ppermute | solution.py:300
  62.8 2.5 %shard_map.119 = (bf16[256,2048]{1,0:T(8,128)(2,1)}, bf16[256,2048]{1,0:T(8,128)(2,1)}, f32[1,128]{1,0:T(1,128)S(1)}) custom-call(s32[1]{0:T(128)} %bitcast.core, bf16[256,2048]{1,0:T(8,128)(2,1)S(1)} %get-tuple-element.45.k, bf16[256,2048]{1,0:T(8,128)(2,1)S(1)} %get-tuple-element.46.v, f32[256,1024]{1,0:T(8,128)S(1)} %get-tuple-element.75.gk_in, ...), custom_call_target="tpu_custom_call" | custom-call | flops 1 | bytes 1 | tf_op jit(solution)/shard_map/pallas_call | solution.py:398
  66.3 2.5 %shard_map.120 = (bf16[256,2048]{1,0:T(8,128)(2,1)}, bf16[256,2048]{1,0:T(8,128)(2,1)}, f32[1,128]{1,0:T(1,128)}) custom-call(s32[1]{0:T(128)} %bitcast.core, bf16[256,2048]{1,0:T(8,128)(2,1)S(1)} %get-tuple-element.45.k, bf16[256,2048]{1,0:T(8,128)(2,1)S(1)} %get-tuple-element.46.v, ...), custom_call_target="tpu_custom_call", output_to_operand_aliasing={{0}: (9, {}), {1}: (10, {})} | custom-call | flops 1 | bytes 1 | tf_op jit(solution)/shard_map/pallas_call | solution.py:398
  (57 shorter events, 5.7 us)
Async XLA Ops:
  0.6 2.3 %copy-start = (s32[1,256]{1,0:T(1,128)S(1)}, s32[1,256]{1,0:T(1,128)}, u32[]{:S(2)}) copy-start(s32[1,256]{1,0:T(1,128)} %seg.13) | copy-start | bytes 3076
  0.6 2.3 %copy-start.2 = (s32[1,32]{1,0:T(1,128)S(1)}, s32[1,32]{1,0:T(1,128)}, u32[]{:S(2)}) copy-start(s32[1,32]{1,0:T(1,128)} %table.13) | copy-start | bytes 388
  2.4 1.7 %collective-permute-start = (f32[512,128]{1,0:T(8,128)S(1)}, f32[512,128]{1,0:T(8,128)S(1)}, u32[]{:S(2)}, u32[]{:S(2)}) collective-permute-start(f32[512,128]{1,0:T(8,128)S(1)} %get-tuple-element.47), channel_id=1, source_target_pairs={{0,1},{1,0},{2,3},{3,2},{4,5},{5,4},{6,7},{7,6},{8,9},{9,8},{10,11... | collective-permute-start | bytes 786440 | tf_op jit(solution)/shard_map/ppermute | solution.py:295
  4.1 11.6 %collective-permute-start.1 = (f32[512,128]{1,0:T(8,128)S(1)}, f32[512,128]{1,0:T(8,128)S(1)}, u32[]{:S(2)}, u32[]{:S(2)}) collective-permute-start(f32[512,128]{1,0:T(8,128)S(1)} %add.138.rest_0_), channel_id=1, source_target_pairs={{0,2},{1,3},{2,4},{3,5},{4,6},{5,7},{6,0},{7,1},{8,10},{9,11},{10,... | collective-permute-start | bytes 786440 | tf_op jit(solution)/shard_map/ppermute | solution.py:309
  14.8 10.4 %copy-start.1 = (f32[2048]{0:T(1024)S(1)}, f32[2048]{0:T(1024)}, u32[]{:S(2)}) copy-start(f32[2048]{0:T(1024)} %param.13) | copy-start | bytes 24580
  15.8 9.2 %collective-permute-start.2 = (f32[512,128]{1,0:T(8,128)S(1)}, f32[512,128]{1,0:T(8,128)S(1)}, u32[]{:S(2)}, u32[]{:S(2)}) collective-permute-start(f32[512,128]{1,0:T(8,128)S(1)} %fusion.5), channel_id=1, source_target_pairs={{0,4},{1,5},{2,6},{3,7},{8,12},{9,13},{10,14},{11,15},{16,20},{17,... | collective-permute-start | bytes 786440 | tf_op jit(solution)/shard_map/ppermute | solution.py:300
  19.4 5.7 %collective-permute-start.5 = (f32[2,264,128]{2,1,0:T(8,128)S(1)}, f32[2,264,128]{2,1,0:T(8,128)S(1)}, u32[]{:S(2)}, u32[]{:S(2)}) collective-permute-start(f32[2,264,128]{2,1,0:T(8,128)S(1)} %get-tuple-element.100), channel_id=1, source_target_pairs={{1,0},{2,1},{3,2},{4,3},{5,4},{6,5},{7,6},{9,8},{10,9},{11,10},{12... | collective-permute-start | bytes 811016 | tf_op jit(solution)/shard_map/ppermute | solution.py:300
  20.7 7.0 %collective-permute-start.4 = (f32[2,264,128]{2,1,0:T(8,128)S(1)}, f32[2,264,128]{2,1,0:T(8,128)S(1)}, u32[]{:S(2)}, u32[]{:S(2)}) collective-permute-start(f32[2,264,128]{2,1,0:T(8,128)S(1)} %get-tuple-element.101), channel_id=1, source_target_pairs={{1,0},{2,1},{3,2},{4,3},{5,4},{6,5},{7,6},{9,8},{10,9},{11,10},{12... | collective-permute-start | bytes 811016 | tf_op jit(solution)/shard_map/ppermute | solution.py:300
  25.1 2.6 %collective-permute-start.3 = (f32[512,128]{1,0:T(8,128)S(1)}, f32[512,128]{1,0:T(8,128)S(1)}, u32[]{:S(2)}, u32[]{:S(2)}) collective-permute-start(f32[512,128]{1,0:T(8,128)S(1)} %get-tuple-element.90), channel_id=1, source_target_pairs={{0,1},{1,0},{2,3},{3,2},{4,5},{5,4},{6,7},{7,6},{8,9},{9,8},{10,11... | collective-permute-start | bytes 786440 | tf_op jit(solution)/shard_map/ppermute | solution.py:295
  30.1 3.6 %collective-permute-start.6 = (f32[512,128]{1,0:T(8,128)S(1)}, f32[512,128]{1,0:T(8,128)S(1)}, u32[]{:S(2)}, u32[]{:S(2)}) collective-permute-start(f32[512,128]{1,0:T(8,128)S(1)} %get-tuple-element.64), channel_id=1, source_target_pairs={{0,1},{1,0},{2,3},{3,2},{4,5},{5,4},{6,7},{7,6},{8,9},{9,8},{10,11... | collective-permute-start | bytes 786440 | tf_op jit(solution)/shard_map/ppermute | solution.py:295
  32.1 3.7 %collective-permute-start.11 = (f32[2,4,128]{2,1,0:T(4,128)S(1)}, f32[2,4,128]{2,1,0:T(4,128)S(1)}, u32[]{:S(2)}, u32[]{:S(2)}) collective-permute-start(f32[2,4,128]{2,1,0:T(4,128)S(1)} %broadcast_select_fusion.2), channel_id=1, source_target_pairs={{0,8},{8,0},{16,24},{24,16},{1,9},{9,1},{17,25},{25,17},{2,10},{10... | collective-permute-start | bytes 12296 | tf_op jit(solution)/shard_map/ppermute | solution.py:295
  33.7 12.7 %collective-permute-start.7 = (f32[512,128]{1,0:T(8,128)S(1)}, f32[512,128]{1,0:T(8,128)S(1)}, u32[]{:S(2)}, u32[]{:S(2)}) collective-permute-start(f32[512,128]{1,0:T(8,128)S(1)} %add.152.rest_0_), channel_id=1, source_target_pairs={{2,0},{3,1},{4,2},{5,3},{6,4},{7,5},{10,8},{11,9},{12,10},{13,11},... | collective-permute-start | bytes 786440 | tf_op jit(solution)/shard_map/ppermute | solution.py:300
  35.8 11.9 %collective-permute-start.12 = (f32[1,4,128]{2,1,0:T(4,128)S(1)}, f32[1,4,128]{2,1,0:T(4,128)S(1)}, u32[]{:S(2)}, u32[]{:S(2)}) collective-permute-start(f32[1,4,128]{2,1,0:T(4,128)S(1)} %slice_select_fusion), channel_id=1, source_target_pairs={{0,16},{8,24},{16,0},{24,8},{1,17},{9,25},{17,1},{25,9},{2,18},{10... | collective-permute-start | bytes 6152 | tf_op jit(solution)/shard_map/ppermute | solution.py:295
  46.4 16.1 %collective-permute-start.8 = (f32[512,128]{1,0:T(8,128)S(1)}, f32[512,128]{1,0:T(8,128)S(1)}, u32[]{:S(2)}, u32[]{:S(2)}) collective-permute-start(f32[512,128]{1,0:T(8,128)S(1)} %add_add_fusion.1.rest_0_), channel_id=1, source_target_pairs={{4,0},{5,1},{6,2},{7,3},{12,8},{13,9},{14,10},{15,11},{20,16},{21,... | collective-permute-start | bytes 786440 | tf_op jit(solution)/shard_map/ppermute | solution.py:300
  47.7 14.8 %collective-permute-start.13 = (f32[2,128]{1,0:T(2,128)S(1)}, f32[2,128]{1,0:T(2,128)S(1)}, u32[]{:S(2)}, u32[]{:S(2)}) collective-permute-start(f32[2,128]{1,0:T(2,128)S(1)} %broadcast_select_fusion.3), channel_id=1, source_target_pairs={{0,4},{1,5},{2,6},{3,7},{4,0},{5,1},{6,2},{7,3},{8,12},{9,13},{10,... | collective-permute-start | bytes 3080 | tf_op jit(solution)/shard_map/ppermute | solution.py:295
  51.4 11.4 %collective-permute-start.10 = (f32[4,264,128]{2,1,0:T(8,128)S(1)}, f32[4,264,128]{2,1,0:T(8,128)S(1)}, u32[]{:S(2)}, u32[]{:S(2)}) collective-permute-start(f32[4,264,128]{2,1,0:T(8,128)S(1)} %maximum_add_fusion), channel_id=1, source_target_pairs={{0,1},{1,2},{2,3},{3,4},{4,5},{5,6},{6,7},{8,9},{9,10},{10,11},{11... | collective-permute-start | bytes 1622024 | tf_op jit(solution)/shard_map/ppermute | solution.py:300
  62.6 3.6 %collective-permute-start.14 = (f32[1,128]{1,0:T(1,128)S(1)}, f32[1,128]{1,0:T(1,128)S(1)}, u32[]{:S(2)}, u32[]{:S(2)}) collective-permute-start(f32[1,128]{1,0:T(1,128)S(1)} %compare_select_fusion), channel_id=1, source_target_pairs={{0,2},{1,3},{2,0},{3,1},{4,6},{5,7},{6,4},{7,5},{8,10},{9,11},{10,... | collective-permute-start | bytes 1544 | tf_op jit(solution)/shard_map/ppermute | solution.py:295
  62.7 3.6 %collective-permute-start.9 = (f32[512,128]{1,0:T(8,128)S(1)}, f32[512,128]{1,0:T(8,128)S(1)}, u32[]{:S(2)}, u32[]{:S(2)}) collective-permute-start(f32[512,128]{1,0:T(8,128)S(1)} %add_select_fusion.1), channel_id=1, source_target_pairs={{0,1},{1,0},{2,3},{3,2},{4,5},{5,4},{6,7},{7,6},{8,9},{9,8},{10,11... | collective-permute-start | bytes 786440 | tf_op jit(solution)/shard_map/ppermute | solution.py:295
  66.3 2.5 %collective-permute-start.15 = (f32[1,64]{1,0:T(1,128)S(1)}, f32[1,64]{1,0:T(1,128)S(1)}, u32[]{:S(2)}, u32[]{:S(2)}) collective-permute-start(f32[1,64]{1,0:T(1,128)S(1)} %slice_select_fusion.1), channel_id=1, source_target_pairs={{0,1},{1,0},{2,3},{3,2},{4,5},{5,4},{6,7},{7,6},{8,9},{9,8},{10,11... | collective-permute-start | bytes 776 | tf_op jit(solution)/shard_map/ppermute | solution.py:295

commit v20 on v19

--- a/solution.py
+++ b/solution.py
@@ -95,9 +95,9 @@
     return pl.ds(pl.multiple_of(base + p * PAIR, PAIR), PAIR)
 
 
-def place(sel, core, lanes, sub):
+def place(sel, core, lanes, sub, first=0):
     step = pl.program_id(0)
-    group, part = step // sub, step % sub
+    group, part = first + step // sub, step % sub
     half = (sel + core[0]) % 2
     base = group * lanes + part * (lanes // sub)
     return group, base, base + (group + half) * lanes, base // PAIR * E
@@ -244,11 +244,11 @@
         gsum[0, p:p + 1] = jnp.sum(dy[:, wides[p]].astype(F32) * normed, axis=0, keepdims=True)
 
 
-def inner_kernel(sel, core, q, k, v, dab, probs, mask, seg, table, prefix, nxt, *rest):
+def inner_kernel(sel, start, core, q, k, v, dab, probs, mask, seg, table, prefix, nxt, *rest):
     gq, gk, gv, token = rest[-4:]
     lanes = dab.shape[1] // GROUPS
     count = lanes // SUB // PAIR
-    group, base, wide, row = place(sel, core, lanes, SUB)
+    group, base, wide, row = place(sel, core, lanes, SUB, start)
     m = mask[...]
     token[...] = jnp.zeros_like(token)
     on_next = on_rows(seg, table, True, nxt)
@@ -342,17 +342,17 @@
     half_rows = lanes // PAIR * E
     heads = lanes // E
 
-    def call(kernel, sel, ins, outs, after=(), alias=(), scratch=(), sub=1, steps=None, scalars=None):
+    def call(kernel, sel, ins, outs, first=0, after=(), alias=(), scratch=(), sub=1, steps=None, scalars=None):
         scalars = scalars or [core]
 
         def wide(i, c, *_):
-            return (0, (i // sub * 2 + (sel + c[0]) % 2) * sub + i % sub)
+            return (0, ((first + i // sub) * 2 + (sel + c[0]) % 2) * sub + i % sub)
 
         def whole(*args):
             return (0, 0)
 
         def part(i, c, *_):
-            return (i // sub, 0, 0)
+            return (first + i // sub, 0, 0)
 
         specs = {
             "vmem": pl.BlockSpec(memory_space=pltpu.VMEM),
@@ -389,8 +389,9 @@
         for out_at, x in alias:
             if x is not None:
                 aliases[len(scalars) + len(operands)] = out_at
-                operands.append(x)
-                kinds.append("any")
+                in_vmem = outs[out_at][0] == "vmem"
+                operands.append(pinned(x, pltpu.VMEM) if in_vmem else x)
+                kinds.append("vmem" if in_vmem else "any")
         out_shape = [
             pltpu.VMEM(*shape, dtype) if kind == "vmem" else jax.ShapeDtypeStruct(shapes[kind], dtype)
             for kind, dtype, *shape in outs
@@ -428,13 +429,14 @@
             [("wide", BF16), ("vmem", BF16, part_of), ("part", F32), ("sums", F32), ("all", F32), ("token", F32)],
             after=after, alias=[(0, before)])
 
-    def inner(sel, before, after):
+    def inner(sel, start, before, after):
+        count = 1 if sel == 0 else GROUPS
         return call(
-            functools.partial(inner_kernel, sel), sel,
+            functools.partial(inner_kernel, sel, start), sel,
             [("vmem", q), ("vmem", k), ("vmem", v), ("vmem", norms[sel][1]), ("vmem", local[sel][1]), ("mask", mask),
              *edges, ("all", prefix[sel]), ("part", nxt[sel])],
             [("wide", BF16), ("vmem", F32, part_of), ("vmem", F32, part_of), ("token", F32)],
-            after=after, alias=[(0, before)], sub=SUB)
+            first=start, after=after, alias=list(enumerate(before)), sub=SUB, steps=(count * SUB,))
 
     def outer(sel, before, after):
         return call(
@@ -446,8 +448,9 @@
     def summed_before(own, towards, works):
         load, before, span = own, None, 1
         while span < chips:
-            if span == 1 and towards == 1:
-                arrived = jnp.where(ctx_row < 2, 0.0, cycled(load, 2))
+            if span == 1:
+                first = ctx_row >> 1 == (0 if towards == 1 else chips - 1)
+                arrived = jnp.where(first, 0.0, cycled(load, 2 * towards))
             else:
                 arrived = shifted(load, 2 * towards * span)
             if works:
@@ -508,15 +511,16 @@
     def third_work(load):
         x = scatter_step(gain_sum[-1] + nought(load[:1]), dp_row, "dp", 1)
         gain_sum.append(x.reshape(-1, PAIR))
-        inners.append(inner(0, None, [load]))
+        inners.append(inner(0, 0, [None] * 3, [load]))
         return inners[0][3]
 
     def fourth_work(load):
         gain_sum.append(scatter_step(gain_sum[-1] + nought(load[:1]), ctx_row, "ctx", bits[0]))
         both = jnp.concatenate([norms[1][2], norms[0][2]], axis=0) + nought(load[:1])
         prv.append(shifted(both, 1))
-        inners.append(inner(1, inners[0][0], [load]))
-        return inners[1][3]
+        inners[0] = inner(0, 1, inners[0][:3], [load])
+        inners.append(inner(1, 0, [inners[0][0], None, None], [load]))
+        return inners[0][3] + inners[1][3]
 
     before = summed_before(piece[2], -1, [third_work, fourth_work])
     suffix = to_cores(core_row, before, piece, -1)

time: 69.7 us -> 69.5 us (level)
  waiting for transfers between devices: 14.5 us -> 7.38 us
  starting transfers between devices: 22.5 us -> 29 us
    ppermute x1 -> x2, starting transfers between devices: 3 us -> 10.2 us  [cycled(): lax.ppermute(x, 'ctx', [(i, (i + distance) % count) for i in range(count)])]
    ppermute x6 -> x5, waiting for transfers between devices: 11.4 us -> 4.35 us  [shifted(): lax.ppermute(x, 'ctx', [(i, i + distance) for i in range(count) if 0 <= i...]
    ppermute x6 -> x5, starting transfers between devices: 10 us -> 8.74 us  [shifted(): lax.ppermute(x, 'ctx', [(i, i + distance) for i in range(count) if 0 <= i...]
    ppermute x9, waiting for transfers between devices: 2.11 us -> 0.83 us  [partner(): return lax.ppermute(x, axis, route)]
    ppermute x1 -> x2, waiting for transfers between devices: 0.97 us -> 2.21 us  [cycled(): lax.ppermute(x, 'ctx', [(i, (i + distance) % count) for i in range(count)])]
    pallas_call x11 -> x12, Pallas kernels: 30 us -> 30.5 us  [call(): pl.pallas_call(kernel, grid_spec=pltpu.PrefetchScalarGridSpec(num_scalar_...]
  transfers between devices with their start and end apart: 16 -> 16, of which waited for: 7 -> 6; matrix products, arithmetic and copies ran while one was open for 1% -> 1% of each run, Pallas kernels for 37% -> 38%
where the time goes in v20:
time: 69.5 us; the launch traced here: 69.3 us
  Pallas kernels  30.5 us (44%)
  starting transfers between devices  29 us (42%)
  waiting for transfers between devices  7.38 us (11%)
  other arithmetic  1.38 us (2%)
  between operations  0.94 us (1%)
    pallas_call x12, Pallas kernels, call(): pl.pallas_call(kernel, grid_spec=pltpu.PrefetchScalarGridSpec(num_scalar_...  30.5 us
    ppermute x2, starting transfers between devices, cycled(): lax.ppermute(x, 'ctx', [(i, (i + distance) % count) for i in range(count)])  10.2 us
    ppermute x9, starting transfers between devices, partner(): return lax.ppermute(x, axis, route)  10.1 us
    ppermute x5, starting transfers between devices, shifted(): lax.ppermute(x, 'ctx', [(i, i + distance) for i in range(count) if 0 <= i...  8.74 us
    ppermute x5, waiting for transfers between devices, shifted(): lax.ppermute(x, 'ctx', [(i, i + distance) for i in range(count) if 0 <= i...  4.35 us
    ppermute x2, waiting for transfers between devices, cycled(): lax.ppermute(x, 'ctx', [(i, (i + distance) % count) for i in range(count)])  2.21 us
  transfers between devices with their start and end apart: 16, of which 6 were waited for; matrix products, arithmetic and copies ran while one was open for 1% of the time, Pallas kernels for 38%

profile of v20, /device:TPU:0, one launch (start us, length us, event | category | flops | bytes accessed | tf_op | source)
XLA Modules:
  0.0 69.3 jit_solution(12113526264545486469)
XLA Ops:
  0.7 1.8 %shard_map.110 = (f32[512,128]{1,0:T(8,128)S(1)}, s32[1,256]{1,0:T(1,128)S(1)}, bf16[256,2048]{1,0:T(8,128)(2,1)S(1)}, bf16[256,2048]{1,0:T(8,128)(2,1)S(1)}, s3...) custom-call(s32[1]{0:T(128)} %bitcast.core, s32[1]{0:T(128)} %bitcast.3.ctx, s32[1]{0:T(128)} %bitcast.4.dp, ...), custom_call_target="tpu_custom_call" | custom-call | flops 1 | bytes 1 | tf_op jit(solution)/shard_map/pallas_call | solution.py:399
  4.1 3.0 %collective-permute-start.1 = (f32[512,128]{1,0:T(8,128)S(1)}, f32[512,128]{1,0:T(8,128)S(1)}, u32[]{:S(2)}, u32[]{:S(2)}) collective-permute-start(f32[512,128]{1,0:T(8,128)S(1)} %add.141.rest_0_), channel_id=1, source_target_pairs={{0,2},{1,3},{2,4},{3,5},{4,6},{5,7},{6,0},{7,1},{8,10},{9,11},{10,... | collective-permute-start | bytes 786440 | tf_op jit(solution)/shard_map/ppermute | solution.py:309
  7.1 2.6 %shard_map.112 = (f32[2,264,128]{2,1,0:T(8,128)S(1)}, f32[2,264,128]{2,1,0:T(8,128)S(1)}, bf16[256,2048]{1,0:T(8,128)(2,1)S(1)}, bf16[256,2048]{1,0:T(8,128)(2,1)S(1)}, f32[1,128]{1,0:T(1,128)}) custom-call(s32[1]{0:T(128)} %bitcast.core, bf16[256,2048]{1,0:T(8,128)(2,1)} %bitcast.54, bf16[256,2048]{1,0:T(8,128)(2,1)} %bitcast.55, ...), custom_call_target="tpu_custom_call" | custom-call | flops 1 | bytes 1 | tf_op jit(solution)/shard_map/pallas_call | solution.py:399
  9.8 2.5 %shard_map.114 = (f32[256,1024]{1,0:T(8,128)S(1)}, bf16[16,256,256]{2,1,0:T(8,128)(2,1)S(1)}, f32[1,128]{1,0:T(1,128)S(1)}) custom-call(s32[1]{0:T(128)} %bitcast.core, bf16[256,2048]{1,0:T(8,128)(2,1)S(1)} %get-tuple-element.52.q, bf16[256,2048]{1,0:T(8,128)(2,1)S(1)} %get-tuple-element.49.k, bf16[256,2048]{1,0:T(8,128)(2,1)S(1)} %get-tuple-element.50.v, ...), custom_call_target="tpu_custom_call" | custom-call | flops 1 | bytes 1 | tf_op jit(solution)/shard_map/pallas_call | solution.py:399
  12.3 2.5 %shard_map.113 = (f32[256,1024]{1,0:T(8,128)S(1)}, bf16[16,256,256]{2,1,0:T(8,128)(2,1)S(1)}, f32[1,128]{1,0:T(1,128)S(1)}) custom-call(s32[1]{0:T(128)} %bitcast.core, bf16[256,2048]{1,0:T(8,128)(2,1)S(1)} %get-tuple-element.52.q, bf16[256,2048]{1,0:T(8,128)(2,1)S(1)} %get-tuple-element.49.k, bf16[256,2048]{1,0:T(8,128)(2,1)S(1)} %get-tuple-element.50.v, ...), custom_call_target="tpu_custom_call" | custom-call | flops 1 | bytes 1 | tf_op jit(solution)/shard_map/pallas_call | solution.py:399
  15.8 3.5 %collective-permute-start.2 = (f32[512,128]{1,0:T(8,128)S(1)}, f32[512,128]{1,0:T(8,128)S(1)}, u32[]{:S(2)}, u32[]{:S(2)}) collective-permute-start(f32[512,128]{1,0:T(8,128)S(1)} %fusion.5), channel_id=1, source_target_pairs={{0,4},{1,5},{2,6},{3,7},{8,12},{9,13},{10,14},{11,15},{16,20},{17,... | collective-permute-start | bytes 786440 | tf_op jit(solution)/shard_map/ppermute | solution.py:300
  19.4 1.3 %collective-permute-start.5 = (f32[2,264,128]{2,1,0:T(8,128)S(1)}, f32[2,264,128]{2,1,0:T(8,128)S(1)}, u32[]{:S(2)}, u32[]{:S(2)}) collective-permute-start(f32[2,264,128]{2,1,0:T(8,128)S(1)} %get-tuple-element.109), channel_id=1, source_target_pairs={{1,0},{2,1},{3,2},{4,3},{5,4},{6,5},{7,6},{9,8},{10,9},{11,10},{12... | collective-permute-start | bytes 811016 | tf_op jit(solution)/shard_map/ppermute | solution.py:300
  20.7 1.3 %collective-permute-start.4 = (f32[2,264,128]{2,1,0:T(8,128)S(1)}, f32[2,264,128]{2,1,0:T(8,128)S(1)}, u32[]{:S(2)}, u32[]{:S(2)}) collective-permute-start(f32[2,264,128]{2,1,0:T(8,128)S(1)} %get-tuple-element.110), channel_id=1, source_target_pairs={{1,0},{2,1},{3,2},{4,3},{5,4},{6,5},{7,6},{9,8},{10,9},{11,10},{12... | collective-permute-start | bytes 811016 | tf_op jit(solution)/shard_map/ppermute | solution.py:300
  22.0 3.0 %collective-permute-done.2 = f32[512,128]{1,0:T(8,128)S(1)} collective-permute-done((f32[512,128]{1,0:T(8,128)S(1)}, f32[512,128]{1,0:T(8,128)S(1)}, u32[]{:S(2)}, u32[]{:S(2)}) %collective-permute-start.2) | collective-permute-done | bytes 262176 | tf_op jit(solution)/shard_map/ppermute | solution.py:300
  25.1 2.5 %shard_map.115 = (bf16[256,2048]{1,0:T(8,128)(2,1)}, bf16[256,1024]{1,0:T(8,128)(2,1)S(1)}, f32[2,264,128]{2,1,0:T(8,128)S(1)}, f32[2,4,128]{2,1,0:T(4,128)S(1)}...) custom-call(s32[1]{0:T(128)} %bitcast.core, bf16[256,2048]{1,0:T(8,128)(2,1)S(1)} %get-tuple-element.52.q, ...), custom_call_target="tpu_custom_call" | custom-call | flops 1 | bytes 1 | tf_op jit(solution)/shard_map/pallas_call | solution.py:399
  27.7 2.4 %shard_map.116 = (bf16[256,2048]{1,0:T(8,128)(2,1)}, bf16[256,1024]{1,0:T(8,128)(2,1)S(1)}, f32[2,264,128]{2,1,0:T(8,128)S(1)}, f32[2,4,128]{2,1,0:T(4,128)S(1)}...) custom-call(s32[1]{0:T(128)} %bitcast.core, ...), custom_call_target="tpu_custom_call", output_to_operand_aliasing={{0}: (10, {})} | custom-call | flops 1 | bytes 1 | tf_op jit(solution)/shard_map/pallas_call | solution.py:399
  30.1 2.0 %collective-permute-start.6 = (f32[512,128]{1,0:T(8,128)S(1)}, f32[512,128]{1,0:T(8,128)S(1)}, u32[]{:S(2)}, u32[]{:S(2)}) collective-permute-start(f32[512,128]{1,0:T(8,128)S(1)} %get-tuple-element.68), channel_id=1, source_target_pairs={{0,1},{1,0},{2,3},{3,2},{4,5},{5,4},{6,7},{7,6},{8,9},{9,8},{10,11... | collective-permute-start | bytes 786440 | tf_op jit(solution)/shard_map/ppermute | solution.py:295
  32.1 1.6 %collective-permute-start.11 = (f32[2,4,128]{2,1,0:T(4,128)S(1)}, f32[2,4,128]{2,1,0:T(4,128)S(1)}, u32[]{:S(2)}, u32[]{:S(2)}) collective-permute-start(f32[2,4,128]{2,1,0:T(4,128)S(1)} %broadcast_select_fusion.2), channel_id=1, source_target_pairs={{0,8},{8,0},{16,24},{24,16},{1,9},{9,1},{17,25},{25,17},{2,10},{10... | collective-permute-start | bytes 12296 | tf_op jit(solution)/shard_map/ppermute | solution.py:295
  33.7 7.2 %collective-permute-start.7 = (f32[512,128]{1,0:T(8,128)S(1)}, f32[512,128]{1,0:T(8,128)S(1)}, u32[]{:S(2)}, u32[]{:S(2)}) collective-permute-start(f32[512,128]{1,0:T(8,128)S(1)} %add.155.rest_0_), channel_id=1, source_target_pairs={{0,6},{1,7},{2,0},{3,1},{4,2},{5,3},{6,4},{7,5},{8,14},{9,15},{10,... | collective-permute-start | bytes 786440 | tf_op jit(solution)/shard_map/ppermute | solution.py:309
  40.9 1.6 %collective-permute-start.12 = (f32[1,4,128]{2,1,0:T(4,128)S(1)}, f32[1,4,128]{2,1,0:T(4,128)S(1)}, u32[]{:S(2)}, u32[]{:S(2)}) collective-permute-start(f32[1,4,128]{2,1,0:T(4,128)S(1)} %slice_select_fusion), channel_id=1, source_target_pairs={{0,16},{8,24},{16,0},{24,8},{1,17},{9,25},{17,1},{25,9},{2,18},{10... | collective-permute-start | bytes 6152 | tf_op jit(solution)/shard_map/ppermute | solution.py:295
  42.5 2.8 %shard_map.117 = (bf16[256,2048]{1,0:T(8,128)(2,1)}, f32[256,1024]{1,0:T(8,128)S(1)}, f32[256,1024]{1,0:T(8,128)S(1)}, f32[1,128]{1,0:T(1,128)S(1)}) custom-call(s32[1]{0:T(128)} %bitcast.core, bf16[256,2048]{1,0:T(8,128)(2,1)S(1)} %get-tuple-element.52.q, bf16[256,2048]{1,0:T(8,128)(2,1)S(1)} %get-tuple-element.49.k, ...), custom_call_target="tpu_custom_call" | custom-call | flops 1 | bytes 1 | tf_op jit(solution)/shard_map/pallas_call | solution.py:399
  46.6 1.3 %collective-permute-start.8 = (f32[512,128]{1,0:T(8,128)S(1)}, f32[512,128]{1,0:T(8,128)S(1)}, u32[]{:S(2)}, u32[]{:S(2)}) collective-permute-start(f32[512,128]{1,0:T(8,128)S(1)} %fusion.6.rest_0_), channel_id=1, source_target_pairs={{4,0},{5,1},{6,2},{7,3},{12,8},{13,9},{14,10},{15,11},{20,16},{21,... | collective-permute-start | bytes 786440 | tf_op jit(solution)/shard_map/ppermute | solution.py:300
  48.0 3.6 %collective-permute-start.13 = (f32[2,128]{1,0:T(2,128)S(1)}, f32[2,128]{1,0:T(2,128)S(1)}, u32[]{:S(2)}, u32[]{:S(2)}) collective-permute-start(f32[2,128]{1,0:T(2,128)S(1)} %broadcast_select_fusion.3), channel_id=1, source_target_pairs={{0,4},{1,5},{2,6},{3,7},{4,0},{5,1},{6,2},{7,3},{8,12},{9,13},{10,... | collective-permute-start | bytes 3080 | tf_op jit(solution)/shard_map/ppermute | solution.py:295
  51.6 1.3 %collective-permute-start.10 = (f32[4,264,128]{2,1,0:T(8,128)S(1)}, f32[4,264,128]{2,1,0:T(8,128)S(1)}, u32[]{:S(2)}, u32[]{:S(2)}) collective-permute-start(f32[4,264,128]{2,1,0:T(8,128)S(1)} %maximum_add_fusion), channel_id=1, source_target_pairs={{0,1},{1,2},{2,3},{3,4},{4,5},{5,6},{6,7},{8,9},{9,10},{10,11},{11... | collective-permute-start | bytes 1622024 | tf_op jit(solution)/shard_map/ppermute | solution.py:300
  53.0 2.9 %shard_map.118 = (bf16[256,2048]{1,0:T(8,128)(2,1)}, f32[256,1024]{1,0:T(8,128)S(1)}, f32[256,1024]{1,0:T(8,128)S(1)}, f32[1,128]{1,0:T(1,128)S(1)}) custom-call(s32[1]{0:T(128)} %bitcast.core, bf16[256,2048]{1,0:T(8,128)(2,1)S(1)} %get-tuple-element.52.q, ...), custom_call_target="tpu_custom_call", output_to_operand_aliasing={{0}: (12, {}), {1}: (13, {}), {2}: (14, {})} | custom-call | flops 1 | bytes 1 | tf_op jit(solution)/shard_map/pallas_call | solution.py:399
  55.9 5.1 %shard_map.119 = (bf16[256,2048]{1,0:T(8,128)(2,1)}, f32[256,1024]{1,0:T(8,128)S(1)}, f32[256,1024]{1,0:T(8,128)S(1)}, f32[1,128]{1,0:T(1,128)S(1)}) custom-call(s32[1]{0:T(128)} %bitcast.core, bf16[256,2048]{1,0:T(8,128)(2,1)S(1)} %get-tuple-element.52.q, bf16[256,2048]{1,0:T(8,128)(2,1)S(1)} %get-tuple-element.49.k, ...), custom_call_target="tpu_custom_call", output_to_operand_aliasing={{0}: (12, {})} | custom-call | flops 1 | bytes 1 | tf_op jit(solution)/shard_map/pallas_call | solution.py:399
  61.0 1.4 %collective-permute-done.8 = f32[512,128]{1,0:T(8,128)S(1)} collective-permute-done((f32[512,128]{1,0:T(8,128)S(1)}, f32[512,128]{1,0:T(8,128)S(1)}, u32[]{:S(2)}, u32[]{:S(2)}) %collective-permute-start.8) | collective-permute-done | bytes 262176 | tf_op jit(solution)/shard_map/ppermute | solution.py:300
  63.3 2.4 %shard_map.120 = (bf16[256,2048]{1,0:T(8,128)(2,1)}, bf16[256,2048]{1,0:T(8,128)(2,1)}, f32[1,128]{1,0:T(1,128)S(1)}) custom-call(s32[1]{0:T(128)} %bitcast.core, bf16[256,2048]{1,0:T(8,128)(2,1)S(1)} %get-tuple-element.49.k, bf16[256,2048]{1,0:T(8,128)(2,1)S(1)} %get-tuple-element.50.v, f32[256,1024]{1,0:T(8,128)S(1)} %get-tuple-element.83.gk_in, ...), custom_call_target="tpu_custom_call" | custom-call | flops 1 | bytes 1 | tf_op jit(solution)/shard_map/pallas_call | solution.py:399
  66.2 2.5 %shard_map.121 = (bf16[256,2048]{1,0:T(8,128)(2,1)}, bf16[256,2048]{1,0:T(8,128)(2,1)}, f32[1,128]{1,0:T(1,128)}) custom-call(s32[1]{0:T(128)} %bitcast.core, bf16[256,2048]{1,0:T(8,128)(2,1)S(1)} %get-tuple-element.49.k, bf16[256,2048]{1,0:T(8,128)(2,1)S(1)} %get-tuple-element.50.v, ...), custom_call_target="tpu_custom_call", output_to_operand_aliasing={{0}: (9, {}), {1}: (10, {})} | custom-call | flops 1 | bytes 1 | tf_op jit(solution)/shard_map/pallas_call | solution.py:399
  (59 shorter events, 6.3 us)
Async XLA Ops:
  0.6 2.3 %copy-start = (s32[1,256]{1,0:T(1,128)S(1)}, s32[1,256]{1,0:T(1,128)}, u32[]{:S(2)}) copy-start(s32[1,256]{1,0:T(1,128)} %seg.15) | copy-start | bytes 3076
  0.6 2.3 %copy-start.1 = (s32[1,32]{1,0:T(1,128)S(1)}, s32[1,32]{1,0:T(1,128)}, u32[]{:S(2)}) copy-start(s32[1,32]{1,0:T(1,128)} %table.15) | copy-start | bytes 388
  2.4 1.7 %collective-permute-start = (f32[512,128]{1,0:T(8,128)S(1)}, f32[512,128]{1,0:T(8,128)S(1)}, u32[]{:S(2)}, u32[]{:S(2)}) collective-permute-start(f32[512,128]{1,0:T(8,128)S(1)} %get-tuple-element.51), channel_id=1, source_target_pairs={{0,1},{1,0},{2,3},{3,2},{4,5},{5,4},{6,7},{7,6},{8,9},{9,8},{10,11... | collective-permute-start | bytes 786440 | tf_op jit(solution)/shard_map/ppermute | solution.py:295
  4.1 11.6 %collective-permute-start.1 = (f32[512,128]{1,0:T(8,128)S(1)}, f32[512,128]{1,0:T(8,128)S(1)}, u32[]{:S(2)}, u32[]{:S(2)}) collective-permute-start(f32[512,128]{1,0:T(8,128)S(1)} %add.141.rest_0_), channel_id=1, source_target_pairs={{0,2},{1,3},{2,4},{3,5},{4,6},{5,7},{6,0},{7,1},{8,10},{9,11},{10,... | collective-permute-start | bytes 786440 | tf_op jit(solution)/shard_map/ppermute | solution.py:309
  14.8 10.4 %copy-start.2 = (f32[2048]{0:T(1024)S(1)}, f32[2048]{0:T(1024)}, u32[]{:S(2)}) copy-start(f32[2048]{0:T(1024)} %param.13) | copy-start | bytes 24580
  15.8 9.2 %collective-permute-start.2 = (f32[512,128]{1,0:T(8,128)S(1)}, f32[512,128]{1,0:T(8,128)S(1)}, u32[]{:S(2)}, u32[]{:S(2)}) collective-permute-start(f32[512,128]{1,0:T(8,128)S(1)} %fusion.5), channel_id=1, source_target_pairs={{0,4},{1,5},{2,6},{3,7},{8,12},{9,13},{10,14},{11,15},{16,20},{17,... | collective-permute-start | bytes 786440 | tf_op jit(solution)/shard_map/ppermute | solution.py:300
  19.4 5.7 %collective-permute-start.5 = (f32[2,264,128]{2,1,0:T(8,128)S(1)}, f32[2,264,128]{2,1,0:T(8,128)S(1)}, u32[]{:S(2)}, u32[]{:S(2)}) collective-permute-start(f32[2,264,128]{2,1,0:T(8,128)S(1)} %get-tuple-element.109), channel_id=1, source_target_pairs={{1,0},{2,1},{3,2},{4,3},{5,4},{6,5},{7,6},{9,8},{10,9},{11,10},{12... | collective-permute-start | bytes 811016 | tf_op jit(solution)/shard_map/ppermute | solution.py:300
  20.7 7.0 %collective-permute-start.4 = (f32[2,264,128]{2,1,0:T(8,128)S(1)}, f32[2,264,128]{2,1,0:T(8,128)S(1)}, u32[]{:S(2)}, u32[]{:S(2)}) collective-permute-start(f32[2,264,128]{2,1,0:T(8,128)S(1)} %get-tuple-element.110), channel_id=1, source_target_pairs={{1,0},{2,1},{3,2},{4,3},{5,4},{6,5},{7,6},{9,8},{10,9},{11,10},{12... | collective-permute-start | bytes 811016 | tf_op jit(solution)/shard_map/ppermute | solution.py:300
  25.1 2.6 %collective-permute-start.3 = (f32[512,128]{1,0:T(8,128)S(1)}, f32[512,128]{1,0:T(8,128)S(1)}, u32[]{:S(2)}, u32[]{:S(2)}) collective-permute-start(f32[512,128]{1,0:T(8,128)S(1)} %get-tuple-element.98), channel_id=1, source_target_pairs={{0,1},{1,0},{2,3},{3,2},{4,5},{5,4},{6,7},{7,6},{8,9},{9,8},{10,11... | collective-permute-start | bytes 786440 | tf_op jit(solution)/shard_map/ppermute | solution.py:295
  30.1 3.6 %collective-permute-start.6 = (f32[512,128]{1,0:T(8,128)S(1)}, f32[512,128]{1,0:T(8,128)S(1)}, u32[]{:S(2)}, u32[]{:S(2)}) collective-permute-start(f32[512,128]{1,0:T(8,128)S(1)} %get-tuple-element.68), channel_id=1, source_target_pairs={{0,1},{1,0},{2,3},{3,2},{4,5},{5,4},{6,7},{7,6},{8,9},{9,8},{10,11... | collective-permute-start | bytes 786440 | tf_op jit(solution)/shard_map/ppermute | solution.py:295
  32.1 8.8 %collective-permute-start.11 = (f32[2,4,128]{2,1,0:T(4,128)S(1)}, f32[2,4,128]{2,1,0:T(4,128)S(1)}, u32[]{:S(2)}, u32[]{:S(2)}) collective-permute-start(f32[2,4,128]{2,1,0:T(4,128)S(1)} %broadcast_select_fusion.2), channel_id=1, source_target_pairs={{0,8},{8,0},{16,24},{24,16},{1,9},{9,1},{17,25},{25,17},{2,10},{10... | collective-permute-start | bytes 12296 | tf_op jit(solution)/shard_map/ppermute | solution.py:295
  33.7 12.9 %collective-permute-start.7 = (f32[512,128]{1,0:T(8,128)S(1)}, f32[512,128]{1,0:T(8,128)S(1)}, u32[]{:S(2)}, u32[]{:S(2)}) collective-permute-start(f32[512,128]{1,0:T(8,128)S(1)} %add.155.rest_0_), channel_id=1, source_target_pairs={{0,6},{1,7},{2,0},{3,1},{4,2},{5,3},{6,4},{7,5},{8,14},{9,15},{10,... | collective-permute-start | bytes 786440 | tf_op jit(solution)/shard_map/ppermute | solution.py:309
  40.9 7.0 %collective-permute-start.12 = (f32[1,4,128]{2,1,0:T(4,128)S(1)}, f32[1,4,128]{2,1,0:T(4,128)S(1)}, u32[]{:S(2)}, u32[]{:S(2)}) collective-permute-start(f32[1,4,128]{2,1,0:T(4,128)S(1)} %slice_select_fusion), channel_id=1, source_target_pairs={{0,16},{8,24},{16,0},{24,8},{1,17},{9,25},{17,1},{25,9},{2,18},{10... | collective-permute-start | bytes 6152 | tf_op jit(solution)/shard_map/ppermute | solution.py:295
  46.6 15.8 %collective-permute-start.8 = (f32[512,128]{1,0:T(8,128)S(1)}, f32[512,128]{1,0:T(8,128)S(1)}, u32[]{:S(2)}, u32[]{:S(2)}) collective-permute-start(f32[512,128]{1,0:T(8,128)S(1)} %fusion.6.rest_0_), channel_id=1, source_target_pairs={{4,0},{5,1},{6,2},{7,3},{12,8},{13,9},{14,10},{15,11},{20,16},{21,... | collective-permute-start | bytes 786440 | tf_op jit(solution)/shard_map/ppermute | solution.py:300
  48.0 14.5 %collective-permute-start.13 = (f32[2,128]{1,0:T(2,128)S(1)}, f32[2,128]{1,0:T(2,128)S(1)}, u32[]{:S(2)}, u32[]{:S(2)}) collective-permute-start(f32[2,128]{1,0:T(2,128)S(1)} %broadcast_select_fusion.3), channel_id=1, source_target_pairs={{0,4},{1,5},{2,6},{3,7},{4,0},{5,1},{6,2},{7,3},{8,12},{9,13},{10,... | collective-permute-start | bytes 3080 | tf_op jit(solution)/shard_map/ppermute | solution.py:295
  51.6 11.7 %collective-permute-start.10 = (f32[4,264,128]{2,1,0:T(8,128)S(1)}, f32[4,264,128]{2,1,0:T(8,128)S(1)}, u32[]{:S(2)}, u32[]{:S(2)}) collective-permute-start(f32[4,264,128]{2,1,0:T(8,128)S(1)} %maximum_add_fusion), channel_id=1, source_target_pairs={{0,1},{1,2},{2,3},{3,4},{4,5},{5,6},{6,7},{8,9},{9,10},{10,11},{11... | collective-permute-start | bytes 1622024 | tf_op jit(solution)/shard_map/ppermute | solution.py:300
  62.5 3.6 %collective-permute-start.14 = (f32[1,128]{1,0:T(1,128)S(1)}, f32[1,128]{1,0:T(1,128)S(1)}, u32[]{:S(2)}, u32[]{:S(2)}) collective-permute-start(f32[1,128]{1,0:T(1,128)S(1)} %compare_select_fusion), channel_id=1, source_target_pairs={{0,2},{1,3},{2,0},{3,1},{4,6},{5,7},{6,4},{7,5},{8,10},{9,11},{10,... | collective-permute-start | bytes 1544 | tf_op jit(solution)/shard_map/ppermute | solution.py:295
  63.1 3.1 %collective-permute-start.9 = (f32[512,128]{1,0:T(8,128)S(1)}, f32[512,128]{1,0:T(8,128)S(1)}, u32[]{:S(2)}, u32[]{:S(2)}) collective-permute-start(f32[512,128]{1,0:T(8,128)S(1)} %add_select_fusion.1), channel_id=1, source_target_pairs={{0,1},{1,0},{2,3},{3,2},{4,5},{5,4},{6,7},{7,6},{8,9},{9,8},{10,11... | collective-permute-start | bytes 786440 | tf_op jit(solution)/shard_map/ppermute | solution.py:295
  66.2 2.5 %collective-permute-start.15 = (f32[1,64]{1,0:T(1,128)S(1)}, f32[1,64]{1,0:T(1,128)S(1)}, u32[]{:S(2)}, u32[]{:S(2)}) collective-permute-start(f32[1,64]{1,0:T(1,128)S(1)} %slice_select_fusion.1), channel_id=1, source_target_pairs={{0,1},{1,0},{2,3},{3,2},{4,5},{5,4},{6,7},{7,6},{8,9},{9,8},{10,11... | collective-permute-start | bytes 776 | tf_op jit(solution)/shard_map/ppermute | solution.py:295

commit v21 on v20

--- a/solution.py
+++ b/solution.py
@@ -275,19 +275,19 @@
 def outer_kernel(sel, core, k, v, gk_in, gv_in, seg, table, suffix, prv, *rest):
     gk, gv, token = rest[-3:]
     lanes = gk_in.shape[1] // GROUPS
-    count = lanes // SUB // PAIR
-    group, base, wide, row = place(sel, core, lanes, SUB)
+    count = lanes // PAIR
+    group, base, wide, row = place(sel, core, lanes, 1)
     token[...] = jnp.zeros_like(token)
     on_prev = on_rows(seg, table, False, prv)
     first = row - group * (lanes // 2)
-    for p in range(count):
-        here, own, at = slice(p * PAIR, (p + 1) * PAIR), lanes_at(base, p), lanes_at(wide, p)
-        s = suffix[rows_at(row, p)]
-        g = prv[0, rows_at(first, p)]
-        far = dot(twice(v[:, at]), stacked(s, g), 1, 1)
-        gk[:, here] = (gk_in[:, own] + far[:, :PAIR] + on_prev * far[:, PAIR:]).astype(BF16)
-        far = dot(twice(k[:, at]), side_by_side(s, g), 1, 0)
-        gv[:, here] = (gv_in[:, own] + far[:, :PAIR] + on_prev * far[:, PAIR:]).astype(BF16)
+    wides = [lanes_at(wide, p) for p in range(count)]
+    states = [(suffix[rows_at(row, p)], prv[0, rows_at(first, p)]) for p in range(count)]
+    fars_k = [dot(twice(v[:, at]), stacked(*state), 1, 1) for at, state in zip(wides, states)]
+    fars_v = [dot(twice(k[:, at]), side_by_side(*state), 1, 0) for at, state in zip(wides, states)]
+    for fars, inside, out in ((fars_k, gk_in, gk), (fars_v, gv_in, gv)):
+        for p, far in enumerate(fars):
+            total = inside[:, lanes_at(base, p)] + far[:, :PAIR] + on_prev * far[:, PAIR:]
+            out[:, p * PAIR:(p + 1) * PAIR] = total.astype(BF16)
 
 
 def partner(x, axis, bit):
@@ -443,7 +443,7 @@
             functools.partial(outer_kernel, sel), sel,
             [("vmem", k), ("vmem", v), ("vmem", inners[sel][1]), ("vmem", inners[sel][2]), *edges,
              ("all", suffix[sel]), ("later" if sel else "part", prv[0])],
-            [("wide", BF16), ("wide", BF16), ("token", F32)], after=after, alias=list(enumerate(before)), sub=SUB)
+            [("wide", BF16), ("wide", BF16), ("token", F32)], after=after, alias=list(enumerate(before)))
 
     def summed_before(own, towards, works):
         load, before, span = own, None, 1

time: 69.5 us -> 68.8 us (0.990)
  Pallas kernels: 30.5 us -> 29.1 us
    pallas_call x12, Pallas kernels: 30.5 us -> 29.1 us  [call(): pl.pallas_call(kernel, grid_spec=pltpu.PrefetchScalarGridSpec(num_scalar_...]
  transfers between devices with their start and end apart: 16 -> 16, of which waited for: 6 -> 6; matrix products, arithmetic and copies ran while one was open for 1% -> 1% of each run, Pallas kernels for 38% -> 36%
where the time goes in v21:
time: 68.8 us; the launch traced here: 68.6 us
  starting transfers between devices  29.4 us (43%)
  Pallas kernels  29.1 us (42%)
  waiting for transfers between devices  7.67 us (11%)
  other arithmetic  1.38 us (2%)
  between operations  0.94 us (1%)
    pallas_call x12, Pallas kernels, call(): pl.pallas_call(kernel, grid_spec=pltpu.PrefetchScalarGridSpec(num_scalar_...  29.1 us
    ppermute x9, starting transfers between devices, partner(): return lax.ppermute(x, axis, route)  10.3 us
    ppermute x2, starting transfers between devices, cycled(): lax.ppermute(x, 'ctx', [(i, (i + distance) % count) for i in range(count)])  10.2 us
    ppermute x5, starting transfers between devices, shifted(): lax.ppermute(x, 'ctx', [(i, i + distance) for i in range(count) if 0 <= i...  8.93 us
    ppermute x5, waiting for transfers between devices, shifted(): lax.ppermute(x, 'ctx', [(i, i + distance) for i in range(count) if 0 <= i...  4.15 us
    ppermute x2, waiting for transfers between devices, cycled(): lax.ppermute(x, 'ctx', [(i, (i + distance) % count) for i in range(count)])  2.2 us
  transfers between devices with their start and end apart: 16, of which 6 were waited for; matrix products, arithmetic and copies ran while one was open for 1% of the time, Pallas kernels for 36%

profile of v21, /device:TPU:0, one launch (start us, length us, event | category | flops | bytes accessed | tf_op | source)
XLA Modules:
  0.0 68.6 jit_solution(11075634932555854302)
XLA Ops:
  0.7 1.8 %shard_map.110 = (f32[512,128]{1,0:T(8,128)S(1)}, s32[1,256]{1,0:T(1,128)S(1)}, bf16[256,2048]{1,0:T(8,128)(2,1)S(1)}, bf16[256,2048]{1,0:T(8,128)(2,1)S(1)}, s3...) custom-call(s32[1]{0:T(128)} %bitcast.core, s32[1]{0:T(128)} %bitcast.3.ctx, s32[1]{0:T(128)} %bitcast.4.dp, ...), custom_call_target="tpu_custom_call" | custom-call | flops 1 | bytes 1 | tf_op jit(solution)/shard_map/pallas_call | solution.py:399
  4.1 3.0 %collective-permute-start.1 = (f32[512,128]{1,0:T(8,128)S(1)}, f32[512,128]{1,0:T(8,128)S(1)}, u32[]{:S(2)}, u32[]{:S(2)}) collective-permute-start(f32[512,128]{1,0:T(8,128)S(1)} %add.141.rest_0_), channel_id=1, source_target_pairs={{0,2},{1,3},{2,4},{3,5},{4,6},{5,7},{6,0},{7,1},{8,10},{9,11},{10,... | collective-permute-start | bytes 786440 | tf_op jit(solution)/shard_map/ppermute | solution.py:309
  7.1 2.6 %shard_map.112 = (f32[2,264,128]{2,1,0:T(8,128)S(1)}, f32[2,264,128]{2,1,0:T(8,128)S(1)}, bf16[256,2048]{1,0:T(8,128)(2,1)S(1)}, bf16[256,2048]{1,0:T(8,128)(2,1)S(1)}, f32[1,128]{1,0:T(1,128)}) custom-call(s32[1]{0:T(128)} %bitcast.core, bf16[256,2048]{1,0:T(8,128)(2,1)} %bitcast.54, bf16[256,2048]{1,0:T(8,128)(2,1)} %bitcast.55, ...), custom_call_target="tpu_custom_call" | custom-call | flops 1 | bytes 1 | tf_op jit(solution)/shard_map/pallas_call | solution.py:399
  9.8 2.5 %shard_map.114 = (f32[256,1024]{1,0:T(8,128)S(1)}, bf16[16,256,256]{2,1,0:T(8,128)(2,1)S(1)}, f32[1,128]{1,0:T(1,128)S(1)}) custom-call(s32[1]{0:T(128)} %bitcast.core, bf16[256,2048]{1,0:T(8,128)(2,1)S(1)} %get-tuple-element.52.q, bf16[256,2048]{1,0:T(8,128)(2,1)S(1)} %get-tuple-element.49.k, bf16[256,2048]{1,0:T(8,128)(2,1)S(1)} %get-tuple-element.50.v, ...), custom_call_target="tpu_custom_call" | custom-call | flops 1 | bytes 1 | tf_op jit(solution)/shard_map/pallas_call | solution.py:399
  12.3 2.5 %shard_map.113 = (f32[256,1024]{1,0:T(8,128)S(1)}, bf16[16,256,256]{2,1,0:T(8,128)(2,1)S(1)}, f32[1,128]{1,0:T(1,128)S(1)}) custom-call(s32[1]{0:T(128)} %bitcast.core, bf16[256,2048]{1,0:T(8,128)(2,1)S(1)} %get-tuple-element.52.q, bf16[256,2048]{1,0:T(8,128)(2,1)S(1)} %get-tuple-element.49.k, bf16[256,2048]{1,0:T(8,128)(2,1)S(1)} %get-tuple-element.50.v, ...), custom_call_target="tpu_custom_call" | custom-call | flops 1 | bytes 1 | tf_op jit(solution)/shard_map/pallas_call | solution.py:399
  15.8 3.5 %collective-permute-start.2 = (f32[512,128]{1,0:T(8,128)S(1)}, f32[512,128]{1,0:T(8,128)S(1)}, u32[]{:S(2)}, u32[]{:S(2)}) collective-permute-start(f32[512,128]{1,0:T(8,128)S(1)} %fusion.5), channel_id=1, source_target_pairs={{0,4},{1,5},{2,6},{3,7},{8,12},{9,13},{10,14},{11,15},{16,20},{17,... | collective-permute-start | bytes 786440 | tf_op jit(solution)/shard_map/ppermute | solution.py:300
  19.4 1.3 %collective-permute-start.5 = (f32[2,264,128]{2,1,0:T(8,128)S(1)}, f32[2,264,128]{2,1,0:T(8,128)S(1)}, u32[]{:S(2)}, u32[]{:S(2)}) collective-permute-start(f32[2,264,128]{2,1,0:T(8,128)S(1)} %get-tuple-element.109), channel_id=1, source_target_pairs={{1,0},{2,1},{3,2},{4,3},{5,4},{6,5},{7,6},{9,8},{10,9},{11,10},{12... | collective-permute-start | bytes 811016 | tf_op jit(solution)/shard_map/ppermute | solution.py:300
  20.7 1.3 %collective-permute-start.4 = (f32[2,264,128]{2,1,0:T(8,128)S(1)}, f32[2,264,128]{2,1,0:T(8,128)S(1)}, u32[]{:S(2)}, u32[]{:S(2)}) collective-permute-start(f32[2,264,128]{2,1,0:T(8,128)S(1)} %get-tuple-element.110), channel_id=1, source_target_pairs={{1,0},{2,1},{3,2},{4,3},{5,4},{6,5},{7,6},{9,8},{10,9},{11,10},{12... | collective-permute-start | bytes 811016 | tf_op jit(solution)/shard_map/ppermute | solution.py:300
  22.0 2.9 %collective-permute-done.2 = f32[512,128]{1,0:T(8,128)S(1)} collective-permute-done((f32[512,128]{1,0:T(8,128)S(1)}, f32[512,128]{1,0:T(8,128)S(1)}, u32[]{:S(2)}, u32[]{:S(2)}) %collective-permute-start.2) | collective-permute-done | bytes 262176 | tf_op jit(solution)/shard_map/ppermute | solution.py:300
  25.1 2.5 %shard_map.115 = (bf16[256,2048]{1,0:T(8,128)(2,1)}, bf16[256,1024]{1,0:T(8,128)(2,1)S(1)}, f32[2,264,128]{2,1,0:T(8,128)S(1)}, f32[2,4,128]{2,1,0:T(4,128)S(1)}...) custom-call(s32[1]{0:T(128)} %bitcast.core, bf16[256,2048]{1,0:T(8,128)(2,1)S(1)} %get-tuple-element.52.q, ...), custom_call_target="tpu_custom_call" | custom-call | flops 1 | bytes 1 | tf_op jit(solution)/shard_map/pallas_call | solution.py:399
  27.7 2.4 %shard_map.116 = (bf16[256,2048]{1,0:T(8,128)(2,1)}, bf16[256,1024]{1,0:T(8,128)(2,1)S(1)}, f32[2,264,128]{2,1,0:T(8,128)S(1)}, f32[2,4,128]{2,1,0:T(4,128)S(1)}...) custom-call(s32[1]{0:T(128)} %bitcast.core, ...), custom_call_target="tpu_custom_call", output_to_operand_aliasing={{0}: (10, {})} | custom-call | flops 1 | bytes 1 | tf_op jit(solution)/shard_map/pallas_call | solution.py:399
  30.1 2.0 %collective-permute-start.6 = (f32[512,128]{1,0:T(8,128)S(1)}, f32[512,128]{1,0:T(8,128)S(1)}, u32[]{:S(2)}, u32[]{:S(2)}) collective-permute-start(f32[512,128]{1,0:T(8,128)S(1)} %get-tuple-element.68), channel_id=1, source_target_pairs={{0,1},{1,0},{2,3},{3,2},{4,5},{5,4},{6,7},{7,6},{8,9},{9,8},{10,11... | collective-permute-start | bytes 786440 | tf_op jit(solution)/shard_map/ppermute | solution.py:295
  32.1 1.6 %collective-permute-start.11 = (f32[2,4,128]{2,1,0:T(4,128)S(1)}, f32[2,4,128]{2,1,0:T(4,128)S(1)}, u32[]{:S(2)}, u32[]{:S(2)}) collective-permute-start(f32[2,4,128]{2,1,0:T(4,128)S(1)} %broadcast_select_fusion.2), channel_id=1, source_target_pairs={{0,8},{8,0},{16,24},{24,16},{1,9},{9,1},{17,25},{25,17},{2,10},{10... | collective-permute-start | bytes 12296 | tf_op jit(solution)/shard_map/ppermute | solution.py:295
  33.7 7.2 %collective-permute-start.7 = (f32[512,128]{1,0:T(8,128)S(1)}, f32[512,128]{1,0:T(8,128)S(1)}, u32[]{:S(2)}, u32[]{:S(2)}) collective-permute-start(f32[512,128]{1,0:T(8,128)S(1)} %add.155.rest_0_), channel_id=1, source_target_pairs={{0,6},{1,7},{2,0},{3,1},{4,2},{5,3},{6,4},{7,5},{8,14},{9,15},{10,... | collective-permute-start | bytes 786440 | tf_op jit(solution)/shard_map/ppermute | solution.py:309
  40.9 1.6 %collective-permute-start.12 = (f32[1,4,128]{2,1,0:T(4,128)S(1)}, f32[1,4,128]{2,1,0:T(4,128)S(1)}, u32[]{:S(2)}, u32[]{:S(2)}) collective-permute-start(f32[1,4,128]{2,1,0:T(4,128)S(1)} %slice_select_fusion), channel_id=1, source_target_pairs={{0,16},{8,24},{16,0},{24,8},{1,17},{9,25},{17,1},{25,9},{2,18},{10... | collective-permute-start | bytes 6152 | tf_op jit(solution)/shard_map/ppermute | solution.py:295
  42.5 2.8 %shard_map.117 = (bf16[256,2048]{1,0:T(8,128)(2,1)}, f32[256,1024]{1,0:T(8,128)S(1)}, f32[256,1024]{1,0:T(8,128)S(1)}, f32[1,128]{1,0:T(1,128)S(1)}) custom-call(s32[1]{0:T(128)} %bitcast.core, bf16[256,2048]{1,0:T(8,128)(2,1)S(1)} %get-tuple-element.52.q, bf16[256,2048]{1,0:T(8,128)(2,1)S(1)} %get-tuple-element.49.k, ...), custom_call_target="tpu_custom_call" | custom-call | flops 1 | bytes 1 | tf_op jit(solution)/shard_map/pallas_call | solution.py:399
  45.4 1.2 %collective-permute-done.7 = f32[512,128]{1,0:T(8,128)S(1)} collective-permute-done((f32[512,128]{1,0:T(8,128)S(1)}, f32[512,128]{1,0:T(8,128)S(1)}, u32[]{:S(2)}, u32[]{:S(2)}) %collective-permute-start.7) | collective-permute-done | bytes 262176 | tf_op jit(solution)/shard_map/ppermute | solution.py:309
  46.6 1.3 %collective-permute-start.8 = (f32[512,128]{1,0:T(8,128)S(1)}, f32[512,128]{1,0:T(8,128)S(1)}, u32[]{:S(2)}, u32[]{:S(2)}) collective-permute-start(f32[512,128]{1,0:T(8,128)S(1)} %fusion.6.rest_0_), channel_id=1, source_target_pairs={{4,0},{5,1},{6,2},{7,3},{12,8},{13,9},{14,10},{15,11},{20,16},{21,... | collective-permute-start | bytes 786440 | tf_op jit(solution)/shard_map/ppermute | solution.py:300
  48.0 3.6 %collective-permute-start.13 = (f32[2,128]{1,0:T(2,128)S(1)}, f32[2,128]{1,0:T(2,128)S(1)}, u32[]{:S(2)}, u32[]{:S(2)}) collective-permute-start(f32[2,128]{1,0:T(2,128)S(1)} %broadcast_select_fusion.3), channel_id=1, source_target_pairs={{0,4},{1,5},{2,6},{3,7},{4,0},{5,1},{6,2},{7,3},{8,12},{9,13},{10,... | collective-permute-start | bytes 3080 | tf_op jit(solution)/shard_map/ppermute | solution.py:295
  51.6 1.5 %collective-permute-start.10 = (f32[4,264,128]{2,1,0:T(8,128)S(1)}, f32[4,264,128]{2,1,0:T(8,128)S(1)}, u32[]{:S(2)}, u32[]{:S(2)}) collective-permute-start(f32[4,264,128]{2,1,0:T(8,128)S(1)} %maximum_add_fusion), channel_id=1, source_target_pairs={{0,1},{1,2},{2,3},{3,4},{4,5},{5,6},{6,7},{8,9},{9,10},{10,11},{11... | collective-permute-start | bytes 1622024 | tf_op jit(solution)/shard_map/ppermute | solution.py:300
  53.1 2.9 %shard_map.118 = (bf16[256,2048]{1,0:T(8,128)(2,1)}, f32[256,1024]{1,0:T(8,128)S(1)}, f32[256,1024]{1,0:T(8,128)S(1)}, f32[1,128]{1,0:T(1,128)S(1)}) custom-call(s32[1]{0:T(128)} %bitcast.core, bf16[256,2048]{1,0:T(8,128)(2,1)S(1)} %get-tuple-element.52.q, ...), custom_call_target="tpu_custom_call", output_to_operand_aliasing={{0}: (12, {}), {1}: (13, {}), {2}: (14, {})} | custom-call | flops 1 | bytes 1 | tf_op jit(solution)/shard_map/pallas_call | solution.py:399
  56.1 5.1 %shard_map.119 = (bf16[256,2048]{1,0:T(8,128)(2,1)}, f32[256,1024]{1,0:T(8,128)S(1)}, f32[256,1024]{1,0:T(8,128)S(1)}, f32[1,128]{1,0:T(1,128)S(1)}) custom-call(s32[1]{0:T(128)} %bitcast.core, bf16[256,2048]{1,0:T(8,128)(2,1)S(1)} %get-tuple-element.52.q, bf16[256,2048]{1,0:T(8,128)(2,1)S(1)} %get-tuple-element.49.k, ...), custom_call_target="tpu_custom_call", output_to_operand_aliasing={{0}: (12, {})} | custom-call | flops 1 | bytes 1 | tf_op jit(solution)/shard_map/pallas_call | solution.py:399
  63.5 1.7 %shard_map.120 = (bf16[256,2048]{1,0:T(8,128)(2,1)}, bf16[256,2048]{1,0:T(8,128)(2,1)}, f32[1,128]{1,0:T(1,128)S(1)}) custom-call(s32[1]{0:T(128)} %bitcast.core, bf16[256,2048]{1,0:T(8,128)(2,1)S(1)} %get-tuple-element.49.k, bf16[256,2048]{1,0:T(8,128)(2,1)S(1)} %get-tuple-element.50.v, f32[256,1024]{1,0:T(8,128)S(1)} %get-tuple-element.83.gk_in, ...), custom_call_target="tpu_custom_call" | custom-call | flops 1 | bytes 1 | tf_op jit(solution)/shard_map/pallas_call | solution.py:399
  66.2 1.8 %shard_map.121 = (bf16[256,2048]{1,0:T(8,128)(2,1)}, bf16[256,2048]{1,0:T(8,128)(2,1)}, f32[1,128]{1,0:T(1,128)}) custom-call(s32[1]{0:T(128)} %bitcast.core, bf16[256,2048]{1,0:T(8,128)(2,1)S(1)} %get-tuple-element.49.k, bf16[256,2048]{1,0:T(8,128)(2,1)S(1)} %get-tuple-element.50.v, ...), custom_call_target="tpu_custom_call", output_to_operand_aliasing={{0}: (9, {}), {1}: (10, {})} | custom-call | flops 1 | bytes 1 | tf_op jit(solution)/shard_map/pallas_call | solution.py:399
  (59 shorter events, 6.9 us)
Async XLA Ops:
  0.6 2.3 %copy-start = (s32[1,256]{1,0:T(1,128)S(1)}, s32[1,256]{1,0:T(1,128)}, u32[]{:S(2)}) copy-start(s32[1,256]{1,0:T(1,128)} %seg.15) | copy-start | bytes 3076
  0.6 2.3 %copy-start.1 = (s32[1,32]{1,0:T(1,128)S(1)}, s32[1,32]{1,0:T(1,128)}, u32[]{:S(2)}) copy-start(s32[1,32]{1,0:T(1,128)} %table.15) | copy-start | bytes 388
  2.4 1.7 %collective-permute-start = (f32[512,128]{1,0:T(8,128)S(1)}, f32[512,128]{1,0:T(8,128)S(1)}, u32[]{:S(2)}, u32[]{:S(2)}) collective-permute-start(f32[512,128]{1,0:T(8,128)S(1)} %get-tuple-element.51), channel_id=1, source_target_pairs={{0,1},{1,0},{2,3},{3,2},{4,5},{5,4},{6,7},{7,6},{8,9},{9,8},{10,11... | collective-permute-start | bytes 786440 | tf_op jit(solution)/shard_map/ppermute | solution.py:295
  4.1 11.6 %collective-permute-start.1 = (f32[512,128]{1,0:T(8,128)S(1)}, f32[512,128]{1,0:T(8,128)S(1)}, u32[]{:S(2)}, u32[]{:S(2)}) collective-permute-start(f32[512,128]{1,0:T(8,128)S(1)} %add.141.rest_0_), channel_id=1, source_target_pairs={{0,2},{1,3},{2,4},{3,5},{4,6},{5,7},{6,0},{7,1},{8,10},{9,11},{10,... | collective-permute-start | bytes 786440 | tf_op jit(solution)/shard_map/ppermute | solution.py:309
  14.8 10.4 %copy-start.2 = (f32[2048]{0:T(1024)S(1)}, f32[2048]{0:T(1024)}, u32[]{:S(2)}) copy-start(f32[2048]{0:T(1024)} %param.13) | copy-start | bytes 24580
  15.8 9.2 %collective-permute-start.2 = (f32[512,128]{1,0:T(8,128)S(1)}, f32[512,128]{1,0:T(8,128)S(1)}, u32[]{:S(2)}, u32[]{:S(2)}) collective-permute-start(f32[512,128]{1,0:T(8,128)S(1)} %fusion.5), channel_id=1, source_target_pairs={{0,4},{1,5},{2,6},{3,7},{8,12},{9,13},{10,14},{11,15},{16,20},{17,... | collective-permute-start | bytes 786440 | tf_op jit(solution)/shard_map/ppermute | solution.py:300
  19.4 5.7 %collective-permute-start.5 = (f32[2,264,128]{2,1,0:T(8,128)S(1)}, f32[2,264,128]{2,1,0:T(8,128)S(1)}, u32[]{:S(2)}, u32[]{:S(2)}) collective-permute-start(f32[2,264,128]{2,1,0:T(8,128)S(1)} %get-tuple-element.109), channel_id=1, source_target_pairs={{1,0},{2,1},{3,2},{4,3},{5,4},{6,5},{7,6},{9,8},{10,9},{11,10},{12... | collective-permute-start | bytes 811016 | tf_op jit(solution)/shard_map/ppermute | solution.py:300
  20.7 7.0 %collective-permute-start.4 = (f32[2,264,128]{2,1,0:T(8,128)S(1)}, f32[2,264,128]{2,1,0:T(8,128)S(1)}, u32[]{:S(2)}, u32[]{:S(2)}) collective-permute-start(f32[2,264,128]{2,1,0:T(8,128)S(1)} %get-tuple-element.110), channel_id=1, source_target_pairs={{1,0},{2,1},{3,2},{4,3},{5,4},{6,5},{7,6},{9,8},{10,9},{11,10},{12... | collective-permute-start | bytes 811016 | tf_op jit(solution)/shard_map/ppermute | solution.py:300
  25.0 2.6 %collective-permute-start.3 = (f32[512,128]{1,0:T(8,128)S(1)}, f32[512,128]{1,0:T(8,128)S(1)}, u32[]{:S(2)}, u32[]{:S(2)}) collective-permute-start(f32[512,128]{1,0:T(8,128)S(1)} %get-tuple-element.98), channel_id=1, source_target_pairs={{0,1},{1,0},{2,3},{3,2},{4,5},{5,4},{6,7},{7,6},{8,9},{9,8},{10,11... | collective-permute-start | bytes 786440 | tf_op jit(solution)/shard_map/ppermute | solution.py:295
  30.1 3.6 %collective-permute-start.6 = (f32[512,128]{1,0:T(8,128)S(1)}, f32[512,128]{1,0:T(8,128)S(1)}, u32[]{:S(2)}, u32[]{:S(2)}) collective-permute-start(f32[512,128]{1,0:T(8,128)S(1)} %get-tuple-element.68), channel_id=1, source_target_pairs={{0,1},{1,0},{2,3},{3,2},{4,5},{5,4},{6,7},{7,6},{8,9},{9,8},{10,11... | collective-permute-start | bytes 786440 | tf_op jit(solution)/shard_map/ppermute | solution.py:295
  32.1 8.8 %collective-permute-start.11 = (f32[2,4,128]{2,1,0:T(4,128)S(1)}, f32[2,4,128]{2,1,0:T(4,128)S(1)}, u32[]{:S(2)}, u32[]{:S(2)}) collective-permute-start(f32[2,4,128]{2,1,0:T(4,128)S(1)} %broadcast_select_fusion.2), channel_id=1, source_target_pairs={{0,8},{8,0},{16,24},{24,16},{1,9},{9,1},{17,25},{25,17},{2,10},{10... | collective-permute-start | bytes 12296 | tf_op jit(solution)/shard_map/ppermute | solution.py:295
  33.7 12.9 %collective-permute-start.7 = (f32[512,128]{1,0:T(8,128)S(1)}, f32[512,128]{1,0:T(8,128)S(1)}, u32[]{:S(2)}, u32[]{:S(2)}) collective-permute-start(f32[512,128]{1,0:T(8,128)S(1)} %add.155.rest_0_), channel_id=1, source_target_pairs={{0,6},{1,7},{2,0},{3,1},{4,2},{5,3},{6,4},{7,5},{8,14},{9,15},{10,... | collective-permute-start | bytes 786440 | tf_op jit(solution)/shard_map/ppermute | solution.py:309
  40.9 7.0 %collective-permute-start.12 = (f32[1,4,128]{2,1,0:T(4,128)S(1)}, f32[1,4,128]{2,1,0:T(4,128)S(1)}, u32[]{:S(2)}, u32[]{:S(2)}) collective-permute-start(f32[1,4,128]{2,1,0:T(4,128)S(1)} %slice_select_fusion), channel_id=1, source_target_pairs={{0,16},{8,24},{16,0},{24,8},{1,17},{9,25},{17,1},{25,9},{2,18},{10... | collective-permute-start | bytes 6152 | tf_op jit(solution)/shard_map/ppermute | solution.py:295
  46.6 15.8 %collective-permute-start.8 = (f32[512,128]{1,0:T(8,128)S(1)}, f32[512,128]{1,0:T(8,128)S(1)}, u32[]{:S(2)}, u32[]{:S(2)}) collective-permute-start(f32[512,128]{1,0:T(8,128)S(1)} %fusion.6.rest_0_), channel_id=1, source_target_pairs={{4,0},{5,1},{6,2},{7,3},{12,8},{13,9},{14,10},{15,11},{20,16},{21,... | collective-permute-start | bytes 786440 | tf_op jit(solution)/shard_map/ppermute | solution.py:300
  48.0 14.5 %collective-permute-start.13 = (f32[2,128]{1,0:T(2,128)S(1)}, f32[2,128]{1,0:T(2,128)S(1)}, u32[]{:S(2)}, u32[]{:S(2)}) collective-permute-start(f32[2,128]{1,0:T(2,128)S(1)} %broadcast_select_fusion.3), channel_id=1, source_target_pairs={{0,4},{1,5},{2,6},{3,7},{4,0},{5,1},{6,2},{7,3},{8,12},{9,13},{10,... | collective-permute-start | bytes 3080 | tf_op jit(solution)/shard_map/ppermute | solution.py:295
  51.6 11.9 %collective-permute-start.10 = (f32[4,264,128]{2,1,0:T(8,128)S(1)}, f32[4,264,128]{2,1,0:T(8,128)S(1)}, u32[]{:S(2)}, u32[]{:S(2)}) collective-permute-start(f32[4,264,128]{2,1,0:T(8,128)S(1)} %maximum_add_fusion), channel_id=1, source_target_pairs={{0,1},{1,2},{2,3},{3,4},{4,5},{5,6},{6,7},{8,9},{9,10},{10,11},{11... | collective-permute-start | bytes 1622024 | tf_op jit(solution)/shard_map/ppermute | solution.py:300
  62.5 3.6 %collective-permute-start.14 = (f32[1,128]{1,0:T(1,128)S(1)}, f32[1,128]{1,0:T(1,128)S(1)}, u32[]{:S(2)}, u32[]{:S(2)}) collective-permute-start(f32[1,128]{1,0:T(1,128)S(1)} %compare_select_fusion), channel_id=1, source_target_pairs={{0,2},{1,3},{2,0},{3,1},{4,6},{5,7},{6,4},{7,5},{8,10},{9,11},{10,... | collective-permute-start | bytes 1544 | tf_op jit(solution)/shard_map/ppermute | solution.py:295
  63.3 2.9 %collective-permute-start.9 = (f32[512,128]{1,0:T(8,128)S(1)}, f32[512,128]{1,0:T(8,128)S(1)}, u32[]{:S(2)}, u32[]{:S(2)}) collective-permute-start(f32[512,128]{1,0:T(8,128)S(1)} %add_select_fusion.1), channel_id=1, source_target_pairs={{0,1},{1,0},{2,3},{3,2},{4,5},{5,4},{6,7},{7,6},{8,9},{9,8},{10,11... | collective-permute-start | bytes 786440 | tf_op jit(solution)/shard_map/ppermute | solution.py:295
  66.2 1.8 %collective-permute-start.15 = (f32[1,64]{1,0:T(1,128)S(1)}, f32[1,64]{1,0:T(1,128)S(1)}, u32[]{:S(2)}, u32[]{:S(2)}) collective-permute-start(f32[1,64]{1,0:T(1,128)S(1)} %slice_select_fusion.1), channel_id=1, source_target_pairs={{0,1},{1,0},{2,3},{3,2},{4,5},{5,4},{6,7},{7,6},{8,9},{9,8},{10,11... | collective-permute-start | bytes 776 | tf_op jit(solution)/shard_map/ppermute | solution.py:295

commit v22 on v21

--- a/solution.py
+++ b/solution.py
@@ -106,12 +106,11 @@
 def put_half(sel, core, k, v, out):
     lanes = k.shape[1] // GROUPS // 2
     count = lanes // PAIR
-    for group in range(GROUPS):
-        base = (2 * group + (sel + core[0]) % 2) * lanes
-        for p in range(count):
-            at = lanes_at(base, p)
-            row = (group * count + p) * E
-            out[row:row + E] = state_pair(k[:, at], v[:, at])
+    bases = [(2 * group + (sel + core[0]) % 2) * lanes for group in range(GROUPS)]
+    ats = [lanes_at(base, p) for base in bases for p in range(count)]
+    products = [dot(k[:, at], v[:, at], 0, 0) for at in ats]
+    for i, product in enumerate(products):
+        out[i * E:(i + 1) * E] = fold(product)
 
 
 def send_kernel(core, ctx, dp, k_in, v_in, send, zero, k, v, core_row, ctx_row, dp_row, sems):
@@ -260,8 +259,9 @@
         far = dot(twice(da), stacked(prefix[rows_at(row, p)], nxt[0, rows_at(first, p)]), 1, 1)
         tq = far[:, :PAIR] + on_next * far[:, PAIR:]
         tk = tv = None
-        for h, (qh, kh, dh) in enumerate(zip(heads_of(q[:, at]), heads_of(k[:, at]), heads_of(da))):
-            dprob = dot(dh, vp, 1, 1).astype(BF16) * m
+        heads = list(zip(heads_of(q[:, at]), heads_of(k[:, at]), heads_of(da)))
+        dprobs = [dot(dh, vp, 1, 1).astype(BF16) * m for _, _, dh in heads]
+        for h, ((qh, kh, dh), dprob) in enumerate(zip(heads, dprobs)):
             tq = tq + dot(dprob, kh, 1, 0)
             a = dot(dprob, qh, 0, 0)
             b = dot(probs[row // (E // 2) + 2 * p + h], dh, 1, 0)

time: 68.8 us -> 68.8 us (level)
  no operation moved by 1% of the time
where the time goes in v22:
time: 68.8 us; the launch traced here: 68.6 us
  starting transfers between devices  29.3 us (43%)
  Pallas kernels  28.9 us (42%)
  waiting for transfers between devices  8.06 us (12%)
  other arithmetic  1.38 us (2%)
  between operations  0.94 us (1%)
    pallas_call x12, Pallas kernels, call(): pl.pallas_call(kernel, grid_spec=pltpu.PrefetchScalarGridSpec(num_scalar_...  28.9 us
    ppermute x2, starting transfers between devices, cycled(): lax.ppermute(x, 'ctx', [(i, (i + distance) % count) for i in range(count)])  10.2 us
    ppermute x9, starting transfers between devices, partner(): return lax.ppermute(x, axis, route)  10.1 us
    ppermute x5, starting transfers between devices, shifted(): lax.ppermute(x, 'ctx', [(i, i + distance) for i in range(count) if 0 <= i...  8.93 us
    ppermute x5, waiting for transfers between devices, shifted(): lax.ppermute(x, 'ctx', [(i, i + distance) for i in range(count) if 0 <= i...  4.32 us
    ppermute x2, waiting for transfers between devices, cycled(): lax.ppermute(x, 'ctx', [(i, (i + distance) % count) for i in range(count)])  2.26 us
    ppermute x9, waiting for transfers between devices, partner(): return lax.ppermute(x, axis, route)  1.48 us
  transfers between devices with their start and end apart: 16, of which 6 were waited for; matrix products, arithmetic and copies ran while one was open for 1% of the time, Pallas kernels for 36%

profile of v22, /device:TPU:0, one launch (start us, length us, event | category | flops | bytes accessed | tf_op | source)
XLA Modules:
  0.0 68.6 jit_solution(9750242307210086218)
XLA Ops:
  0.7 1.8 %shard_map.110 = (f32[512,128]{1,0:T(8,128)S(1)}, s32[1,256]{1,0:T(1,128)S(1)}, bf16[256,2048]{1,0:T(8,128)(2,1)S(1)}, bf16[256,2048]{1,0:T(8,128)(2,1)S(1)}, s3...) custom-call(s32[1]{0:T(128)} %bitcast.core, s32[1]{0:T(128)} %bitcast.3.ctx, s32[1]{0:T(128)} %bitcast.4.dp, ...), custom_call_target="tpu_custom_call" | custom-call | flops 1 | bytes 1 | tf_op jit(solution)/shard_map/pallas_call | solution.py:399
  4.1 3.0 %collective-permute-start.1 = (f32[512,128]{1,0:T(8,128)S(1)}, f32[512,128]{1,0:T(8,128)S(1)}, u32[]{:S(2)}, u32[]{:S(2)}) collective-permute-start(f32[512,128]{1,0:T(8,128)S(1)} %add.141.rest_0_), channel_id=1, source_target_pairs={{0,2},{1,3},{2,4},{3,5},{4,6},{5,7},{6,0},{7,1},{8,10},{9,11},{10,... | collective-permute-start | bytes 786440 | tf_op jit(solution)/shard_map/ppermute | solution.py:309
  7.1 2.6 %shard_map.112 = (f32[2,264,128]{2,1,0:T(8,128)S(1)}, f32[2,264,128]{2,1,0:T(8,128)S(1)}, bf16[256,2048]{1,0:T(8,128)(2,1)S(1)}, bf16[256,2048]{1,0:T(8,128)(2,1)S(1)}, f32[1,128]{1,0:T(1,128)}) custom-call(s32[1]{0:T(128)} %bitcast.core, bf16[256,2048]{1,0:T(8,128)(2,1)} %bitcast.54, bf16[256,2048]{1,0:T(8,128)(2,1)} %bitcast.55, ...), custom_call_target="tpu_custom_call" | custom-call | flops 1 | bytes 1 | tf_op jit(solution)/shard_map/pallas_call | solution.py:399
  9.8 2.5 %shard_map.114 = (f32[256,1024]{1,0:T(8,128)S(1)}, bf16[16,256,256]{2,1,0:T(8,128)(2,1)S(1)}, f32[1,128]{1,0:T(1,128)S(1)}) custom-call(s32[1]{0:T(128)} %bitcast.core, bf16[256,2048]{1,0:T(8,128)(2,1)S(1)} %get-tuple-element.52.q, bf16[256,2048]{1,0:T(8,128)(2,1)S(1)} %get-tuple-element.49.k, bf16[256,2048]{1,0:T(8,128)(2,1)S(1)} %get-tuple-element.50.v, ...), custom_call_target="tpu_custom_call" | custom-call | flops 1 | bytes 1 | tf_op jit(solution)/shard_map/pallas_call | solution.py:399
  12.3 2.5 %shard_map.113 = (f32[256,1024]{1,0:T(8,128)S(1)}, bf16[16,256,256]{2,1,0:T(8,128)(2,1)S(1)}, f32[1,128]{1,0:T(1,128)S(1)}) custom-call(s32[1]{0:T(128)} %bitcast.core, bf16[256,2048]{1,0:T(8,128)(2,1)S(1)} %get-tuple-element.52.q, bf16[256,2048]{1,0:T(8,128)(2,1)S(1)} %get-tuple-element.49.k, bf16[256,2048]{1,0:T(8,128)(2,1)S(1)} %get-tuple-element.50.v, ...), custom_call_target="tpu_custom_call" | custom-call | flops 1 | bytes 1 | tf_op jit(solution)/shard_map/pallas_call | solution.py:399
  15.8 3.5 %collective-permute-start.2 = (f32[512,128]{1,0:T(8,128)S(1)}, f32[512,128]{1,0:T(8,128)S(1)}, u32[]{:S(2)}, u32[]{:S(2)}) collective-permute-start(f32[512,128]{1,0:T(8,128)S(1)} %fusion.5), channel_id=1, source_target_pairs={{0,4},{1,5},{2,6},{3,7},{8,12},{9,13},{10,14},{11,15},{16,20},{17,... | collective-permute-start | bytes 786440 | tf_op jit(solution)/shard_map/ppermute | solution.py:300
  19.4 1.3 %collective-permute-start.5 = (f32[2,264,128]{2,1,0:T(8,128)S(1)}, f32[2,264,128]{2,1,0:T(8,128)S(1)}, u32[]{:S(2)}, u32[]{:S(2)}) collective-permute-start(f32[2,264,128]{2,1,0:T(8,128)S(1)} %get-tuple-element.109), channel_id=1, source_target_pairs={{1,0},{2,1},{3,2},{4,3},{5,4},{6,5},{7,6},{9,8},{10,9},{11,10},{12... | collective-permute-start | bytes 811016 | tf_op jit(solution)/shard_map/ppermute | solution.py:300
  20.7 1.3 %collective-permute-start.4 = (f32[2,264,128]{2,1,0:T(8,128)S(1)}, f32[2,264,128]{2,1,0:T(8,128)S(1)}, u32[]{:S(2)}, u32[]{:S(2)}) collective-permute-start(f32[2,264,128]{2,1,0:T(8,128)S(1)} %get-tuple-element.110), channel_id=1, source_target_pairs={{1,0},{2,1},{3,2},{4,3},{5,4},{6,5},{7,6},{9,8},{10,9},{11,10},{12... | collective-permute-start | bytes 811016 | tf_op jit(solution)/shard_map/ppermute | solution.py:300
  22.0 2.9 %collective-permute-done.2 = f32[512,128]{1,0:T(8,128)S(1)} collective-permute-done((f32[512,128]{1,0:T(8,128)S(1)}, f32[512,128]{1,0:T(8,128)S(1)}, u32[]{:S(2)}, u32[]{:S(2)}) %collective-permute-start.2) | collective-permute-done | bytes 262176 | tf_op jit(solution)/shard_map/ppermute | solution.py:300
  25.1 2.5 %shard_map.115 = (bf16[256,2048]{1,0:T(8,128)(2,1)}, bf16[256,1024]{1,0:T(8,128)(2,1)S(1)}, f32[2,264,128]{2,1,0:T(8,128)S(1)}, f32[2,4,128]{2,1,0:T(4,128)S(1)}...) custom-call(s32[1]{0:T(128)} %bitcast.core, bf16[256,2048]{1,0:T(8,128)(2,1)S(1)} %get-tuple-element.52.q, ...), custom_call_target="tpu_custom_call" | custom-call | flops 1 | bytes 1 | tf_op jit(solution)/shard_map/pallas_call | solution.py:399
  27.7 2.4 %shard_map.116 = (bf16[256,2048]{1,0:T(8,128)(2,1)}, bf16[256,1024]{1,0:T(8,128)(2,1)S(1)}, f32[2,264,128]{2,1,0:T(8,128)S(1)}, f32[2,4,128]{2,1,0:T(4,128)S(1)}...) custom-call(s32[1]{0:T(128)} %bitcast.core, ...), custom_call_target="tpu_custom_call", output_to_operand_aliasing={{0}: (10, {})} | custom-call | flops 1 | bytes 1 | tf_op jit(solution)/shard_map/pallas_call | solution.py:399
  30.1 2.0 %collective-permute-start.6 = (f32[512,128]{1,0:T(8,128)S(1)}, f32[512,128]{1,0:T(8,128)S(1)}, u32[]{:S(2)}, u32[]{:S(2)}) collective-permute-start(f32[512,128]{1,0:T(8,128)S(1)} %get-tuple-element.68), channel_id=1, source_target_pairs={{0,1},{1,0},{2,3},{3,2},{4,5},{5,4},{6,7},{7,6},{8,9},{9,8},{10,11... | collective-permute-start | bytes 786440 | tf_op jit(solution)/shard_map/ppermute | solution.py:295
  32.1 1.6 %collective-permute-start.11 = (f32[2,4,128]{2,1,0:T(4,128)S(1)}, f32[2,4,128]{2,1,0:T(4,128)S(1)}, u32[]{:S(2)}, u32[]{:S(2)}) collective-permute-start(f32[2,4,128]{2,1,0:T(4,128)S(1)} %broadcast_select_fusion.2), channel_id=1, source_target_pairs={{0,8},{8,0},{16,24},{24,16},{1,9},{9,1},{17,25},{25,17},{2,10},{10... | collective-permute-start | bytes 12296 | tf_op jit(solution)/shard_map/ppermute | solution.py:295
  33.7 7.2 %collective-permute-start.7 = (f32[512,128]{1,0:T(8,128)S(1)}, f32[512,128]{1,0:T(8,128)S(1)}, u32[]{:S(2)}, u32[]{:S(2)}) collective-permute-start(f32[512,128]{1,0:T(8,128)S(1)} %add.155.rest_0_), channel_id=1, source_target_pairs={{0,6},{1,7},{2,0},{3,1},{4,2},{5,3},{6,4},{7,5},{8,14},{9,15},{10,... | collective-permute-start | bytes 786440 | tf_op jit(solution)/shard_map/ppermute | solution.py:309
  40.9 1.6 %collective-permute-start.12 = (f32[1,4,128]{2,1,0:T(4,128)S(1)}, f32[1,4,128]{2,1,0:T(4,128)S(1)}, u32[]{:S(2)}, u32[]{:S(2)}) collective-permute-start(f32[1,4,128]{2,1,0:T(4,128)S(1)} %slice_select_fusion), channel_id=1, source_target_pairs={{0,16},{8,24},{16,0},{24,8},{1,17},{9,25},{17,1},{25,9},{2,18},{10... | collective-permute-start | bytes 6152 | tf_op jit(solution)/shard_map/ppermute | solution.py:295
  42.5 2.8 %shard_map.117 = (bf16[256,2048]{1,0:T(8,128)(2,1)}, f32[256,1024]{1,0:T(8,128)S(1)}, f32[256,1024]{1,0:T(8,128)S(1)}, f32[1,128]{1,0:T(1,128)S(1)}) custom-call(s32[1]{0:T(128)} %bitcast.core, bf16[256,2048]{1,0:T(8,128)(2,1)S(1)} %get-tuple-element.52.q, bf16[256,2048]{1,0:T(8,128)(2,1)S(1)} %get-tuple-element.49.k, ...), custom_call_target="tpu_custom_call" | custom-call | flops 1 | bytes 1 | tf_op jit(solution)/shard_map/pallas_call | solution.py:399
  46.6 1.3 %collective-permute-start.8 = (f32[512,128]{1,0:T(8,128)S(1)}, f32[512,128]{1,0:T(8,128)S(1)}, u32[]{:S(2)}, u32[]{:S(2)}) collective-permute-start(f32[512,128]{1,0:T(8,128)S(1)} %fusion.6.rest_0_), channel_id=1, source_target_pairs={{4,0},{5,1},{6,2},{7,3},{12,8},{13,9},{14,10},{15,11},{20,16},{21,... | collective-permute-start | bytes 786440 | tf_op jit(solution)/shard_map/ppermute | solution.py:300
  48.0 3.6 %collective-permute-start.13 = (f32[2,128]{1,0:T(2,128)S(1)}, f32[2,128]{1,0:T(2,128)S(1)}, u32[]{:S(2)}, u32[]{:S(2)}) collective-permute-start(f32[2,128]{1,0:T(2,128)S(1)} %broadcast_select_fusion.3), channel_id=1, source_target_pairs={{0,4},{1,5},{2,6},{3,7},{4,0},{5,1},{6,2},{7,3},{8,12},{9,13},{10,... | collective-permute-start | bytes 3080 | tf_op jit(solution)/shard_map/ppermute | solution.py:295
  51.6 1.5 %collective-permute-start.10 = (f32[4,264,128]{2,1,0:T(8,128)S(1)}, f32[4,264,128]{2,1,0:T(8,128)S(1)}, u32[]{:S(2)}, u32[]{:S(2)}) collective-permute-start(f32[4,264,128]{2,1,0:T(8,128)S(1)} %maximum_add_fusion), channel_id=1, source_target_pairs={{0,1},{1,2},{2,3},{3,4},{4,5},{5,6},{6,7},{8,9},{9,10},{10,11},{11... | collective-permute-start | bytes 1622024 | tf_op jit(solution)/shard_map/ppermute | solution.py:300
  53.1 2.9 %shard_map.118 = (bf16[256,2048]{1,0:T(8,128)(2,1)}, f32[256,1024]{1,0:T(8,128)S(1)}, f32[256,1024]{1,0:T(8,128)S(1)}, f32[1,128]{1,0:T(1,128)S(1)}) custom-call(s32[1]{0:T(128)} %bitcast.core, bf16[256,2048]{1,0:T(8,128)(2,1)S(1)} %get-tuple-element.52.q, ...), custom_call_target="tpu_custom_call", output_to_operand_aliasing={{0}: (12, {}), {1}: (13, {}), {2}: (14, {})} | custom-call | flops 1 | bytes 1 | tf_op jit(solution)/shard_map/pallas_call | solution.py:399
  56.0 5.0 %shard_map.119 = (bf16[256,2048]{1,0:T(8,128)(2,1)}, f32[256,1024]{1,0:T(8,128)S(1)}, f32[256,1024]{1,0:T(8,128)S(1)}, f32[1,128]{1,0:T(1,128)S(1)}) custom-call(s32[1]{0:T(128)} %bitcast.core, bf16[256,2048]{1,0:T(8,128)(2,1)S(1)} %get-tuple-element.52.q, bf16[256,2048]{1,0:T(8,128)(2,1)S(1)} %get-tuple-element.49.k, ...), custom_call_target="tpu_custom_call", output_to_operand_aliasing={{0}: (12, {})} | custom-call | flops 1 | bytes 1 | tf_op jit(solution)/shard_map/pallas_call | solution.py:399
  61.0 1.4 %collective-permute-done.8 = f32[512,128]{1,0:T(8,128)S(1)} collective-permute-done((f32[512,128]{1,0:T(8,128)S(1)}, f32[512,128]{1,0:T(8,128)S(1)}, u32[]{:S(2)}, u32[]{:S(2)}) %collective-permute-start.8) | collective-permute-done | bytes 262176 | tf_op jit(solution)/shard_map/ppermute | solution.py:300
  63.3 1.7 %shard_map.120 = (bf16[256,2048]{1,0:T(8,128)(2,1)}, bf16[256,2048]{1,0:T(8,128)(2,1)}, f32[1,128]{1,0:T(1,128)S(1)}) custom-call(s32[1]{0:T(128)} %bitcast.core, bf16[256,2048]{1,0:T(8,128)(2,1)S(1)} %get-tuple-element.49.k, bf16[256,2048]{1,0:T(8,128)(2,1)S(1)} %get-tuple-element.50.v, f32[256,1024]{1,0:T(8,128)S(1)} %get-tuple-element.83.gk_in, ...), custom_call_target="tpu_custom_call" | custom-call | flops 1 | bytes 1 | tf_op jit(solution)/shard_map/pallas_call | solution.py:399
  66.2 1.8 %shard_map.121 = (bf16[256,2048]{1,0:T(8,128)(2,1)}, bf16[256,2048]{1,0:T(8,128)(2,1)}, f32[1,128]{1,0:T(1,128)}) custom-call(s32[1]{0:T(128)} %bitcast.core, bf16[256,2048]{1,0:T(8,128)(2,1)S(1)} %get-tuple-element.49.k, bf16[256,2048]{1,0:T(8,128)(2,1)S(1)} %get-tuple-element.50.v, ...), custom_call_target="tpu_custom_call", output_to_operand_aliasing={{0}: (9, {}), {1}: (10, {})} | custom-call | flops 1 | bytes 1 | tf_op jit(solution)/shard_map/pallas_call | solution.py:399
  (59 shorter events, 7.0 us)
Async XLA Ops:
  0.6 2.3 %copy-start = (s32[1,256]{1,0:T(1,128)S(1)}, s32[1,256]{1,0:T(1,128)}, u32[]{:S(2)}) copy-start(s32[1,256]{1,0:T(1,128)} %seg.15) | copy-start | bytes 3076
  0.6 2.3 %copy-start.1 = (s32[1,32]{1,0:T(1,128)S(1)}, s32[1,32]{1,0:T(1,128)}, u32[]{:S(2)}) copy-start(s32[1,32]{1,0:T(1,128)} %table.15) | copy-start | bytes 388
  2.4 1.7 %collective-permute-start = (f32[512,128]{1,0:T(8,128)S(1)}, f32[512,128]{1,0:T(8,128)S(1)}, u32[]{:S(2)}, u32[]{:S(2)}) collective-permute-start(f32[512,128]{1,0:T(8,128)S(1)} %get-tuple-element.51), channel_id=1, source_target_pairs={{0,1},{1,0},{2,3},{3,2},{4,5},{5,4},{6,7},{7,6},{8,9},{9,8},{10,11... | collective-permute-start | bytes 786440 | tf_op jit(solution)/shard_map/ppermute | solution.py:295
  4.1 11.6 %collective-permute-start.1 = (f32[512,128]{1,0:T(8,128)S(1)}, f32[512,128]{1,0:T(8,128)S(1)}, u32[]{:S(2)}, u32[]{:S(2)}) collective-permute-start(f32[512,128]{1,0:T(8,128)S(1)} %add.141.rest_0_), channel_id=1, source_target_pairs={{0,2},{1,3},{2,4},{3,5},{4,6},{5,7},{6,0},{7,1},{8,10},{9,11},{10,... | collective-permute-start | bytes 786440 | tf_op jit(solution)/shard_map/ppermute | solution.py:309
  14.8 10.4 %copy-start.2 = (f32[2048]{0:T(1024)S(1)}, f32[2048]{0:T(1024)}, u32[]{:S(2)}) copy-start(f32[2048]{0:T(1024)} %param.13) | copy-start | bytes 24580
  15.8 9.2 %collective-permute-start.2 = (f32[512,128]{1,0:T(8,128)S(1)}, f32[512,128]{1,0:T(8,128)S(1)}, u32[]{:S(2)}, u32[]{:S(2)}) collective-permute-start(f32[512,128]{1,0:T(8,128)S(1)} %fusion.5), channel_id=1, source_target_pairs={{0,4},{1,5},{2,6},{3,7},{8,12},{9,13},{10,14},{11,15},{16,20},{17,... | collective-permute-start | bytes 786440 | tf_op jit(solution)/shard_map/ppermute | solution.py:300
  19.4 5.7 %collective-permute-start.5 = (f32[2,264,128]{2,1,0:T(8,128)S(1)}, f32[2,264,128]{2,1,0:T(8,128)S(1)}, u32[]{:S(2)}, u32[]{:S(2)}) collective-permute-start(f32[2,264,128]{2,1,0:T(8,128)S(1)} %get-tuple-element.109), channel_id=1, source_target_pairs={{1,0},{2,1},{3,2},{4,3},{5,4},{6,5},{7,6},{9,8},{10,9},{11,10},{12... | collective-permute-start | bytes 811016 | tf_op jit(solution)/shard_map/ppermute | solution.py:300
  20.7 7.0 %collective-permute-start.4 = (f32[2,264,128]{2,1,0:T(8,128)S(1)}, f32[2,264,128]{2,1,0:T(8,128)S(1)}, u32[]{:S(2)}, u32[]{:S(2)}) collective-permute-start(f32[2,264,128]{2,1,0:T(8,128)S(1)} %get-tuple-element.110), channel_id=1, source_target_pairs={{1,0},{2,1},{3,2},{4,3},{5,4},{6,5},{7,6},{9,8},{10,9},{11,10},{12... | collective-permute-start | bytes 811016 | tf_op jit(solution)/shard_map/ppermute | solution.py:300
  25.0 2.6 %collective-permute-start.3 = (f32[512,128]{1,0:T(8,128)S(1)}, f32[512,128]{1,0:T(8,128)S(1)}, u32[]{:S(2)}, u32[]{:S(2)}) collective-permute-start(f32[512,128]{1,0:T(8,128)S(1)} %get-tuple-element.98), channel_id=1, source_target_pairs={{0,1},{1,0},{2,3},{3,2},{4,5},{5,4},{6,7},{7,6},{8,9},{9,8},{10,11... | collective-permute-start | bytes 786440 | tf_op jit(solution)/shard_map/ppermute | solution.py:295
  30.1 3.6 %collective-permute-start.6 = (f32[512,128]{1,0:T(8,128)S(1)}, f32[512,128]{1,0:T(8,128)S(1)}, u32[]{:S(2)}, u32[]{:S(2)}) collective-permute-start(f32[512,128]{1,0:T(8,128)S(1)} %get-tuple-element.68), channel_id=1, source_target_pairs={{0,1},{1,0},{2,3},{3,2},{4,5},{5,4},{6,7},{7,6},{8,9},{9,8},{10,11... | collective-permute-start | bytes 786440 | tf_op jit(solution)/shard_map/ppermute | solution.py:295
  32.1 8.8 %collective-permute-start.11 = (f32[2,4,128]{2,1,0:T(4,128)S(1)}, f32[2,4,128]{2,1,0:T(4,128)S(1)}, u32[]{:S(2)}, u32[]{:S(2)}) collective-permute-start(f32[2,4,128]{2,1,0:T(4,128)S(1)} %broadcast_select_fusion.2), channel_id=1, source_target_pairs={{0,8},{8,0},{16,24},{24,16},{1,9},{9,1},{17,25},{25,17},{2,10},{10... | collective-permute-start | bytes 12296 | tf_op jit(solution)/shard_map/ppermute | solution.py:295
  33.7 12.9 %collective-permute-start.7 = (f32[512,128]{1,0:T(8,128)S(1)}, f32[512,128]{1,0:T(8,128)S(1)}, u32[]{:S(2)}, u32[]{:S(2)}) collective-permute-start(f32[512,128]{1,0:T(8,128)S(1)} %add.155.rest_0_), channel_id=1, source_target_pairs={{0,6},{1,7},{2,0},{3,1},{4,2},{5,3},{6,4},{7,5},{8,14},{9,15},{10,... | collective-permute-start | bytes 786440 | tf_op jit(solution)/shard_map/ppermute | solution.py:309
  40.9 7.0 %collective-permute-start.12 = (f32[1,4,128]{2,1,0:T(4,128)S(1)}, f32[1,4,128]{2,1,0:T(4,128)S(1)}, u32[]{:S(2)}, u32[]{:S(2)}) collective-permute-start(f32[1,4,128]{2,1,0:T(4,128)S(1)} %slice_select_fusion), channel_id=1, source_target_pairs={{0,16},{8,24},{16,0},{24,8},{1,17},{9,25},{17,1},{25,9},{2,18},{10... | collective-permute-start | bytes 6152 | tf_op jit(solution)/shard_map/ppermute | solution.py:295
  46.6 15.8 %collective-permute-start.8 = (f32[512,128]{1,0:T(8,128)S(1)}, f32[512,128]{1,0:T(8,128)S(1)}, u32[]{:S(2)}, u32[]{:S(2)}) collective-permute-start(f32[512,128]{1,0:T(8,128)S(1)} %fusion.6.rest_0_), channel_id=1, source_target_pairs={{4,0},{5,1},{6,2},{7,3},{12,8},{13,9},{14,10},{15,11},{20,16},{21,... | collective-permute-start | bytes 786440 | tf_op jit(solution)/shard_map/ppermute | solution.py:300
  48.0 14.5 %collective-permute-start.13 = (f32[2,128]{1,0:T(2,128)S(1)}, f32[2,128]{1,0:T(2,128)S(1)}, u32[]{:S(2)}, u32[]{:S(2)}) collective-permute-start(f32[2,128]{1,0:T(2,128)S(1)} %broadcast_select_fusion.3), channel_id=1, source_target_pairs={{0,4},{1,5},{2,6},{3,7},{4,0},{5,1},{6,2},{7,3},{8,12},{9,13},{10,... | collective-permute-start | bytes 3080 | tf_op jit(solution)/shard_map/ppermute | solution.py:295
  51.6 11.7 %collective-permute-start.10 = (f32[4,264,128]{2,1,0:T(8,128)S(1)}, f32[4,264,128]{2,1,0:T(8,128)S(1)}, u32[]{:S(2)}, u32[]{:S(2)}) collective-permute-start(f32[4,264,128]{2,1,0:T(8,128)S(1)} %maximum_add_fusion), channel_id=1, source_target_pairs={{0,1},{1,2},{2,3},{3,4},{4,5},{5,6},{6,7},{8,9},{9,10},{10,11},{11... | collective-permute-start | bytes 1622024 | tf_op jit(solution)/shard_map/ppermute | solution.py:300
  62.5 3.6 %collective-permute-start.14 = (f32[1,128]{1,0:T(1,128)S(1)}, f32[1,128]{1,0:T(1,128)S(1)}, u32[]{:S(2)}, u32[]{:S(2)}) collective-permute-start(f32[1,128]{1,0:T(1,128)S(1)} %compare_select_fusion), channel_id=1, source_target_pairs={{0,2},{1,3},{2,0},{3,1},{4,6},{5,7},{6,4},{7,5},{8,10},{9,11},{10,... | collective-permute-start | bytes 1544 | tf_op jit(solution)/shard_map/ppermute | solution.py:295
  63.1 3.1 %collective-permute-start.9 = (f32[512,128]{1,0:T(8,128)S(1)}, f32[512,128]{1,0:T(8,128)S(1)}, u32[]{:S(2)}, u32[]{:S(2)}) collective-permute-start(f32[512,128]{1,0:T(8,128)S(1)} %add_select_fusion.1), channel_id=1, source_target_pairs={{0,1},{1,0},{2,3},{3,2},{4,5},{5,4},{6,7},{7,6},{8,9},{9,8},{10,11... | collective-permute-start | bytes 786440 | tf_op jit(solution)/shard_map/ppermute | solution.py:295
  66.2 1.8 %collective-permute-start.15 = (f32[1,64]{1,0:T(1,128)S(1)}, f32[1,64]{1,0:T(1,128)S(1)}, u32[]{:S(2)}, u32[]{:S(2)}) collective-permute-start(f32[1,64]{1,0:T(1,128)S(1)} %slice_select_fusion.1), channel_id=1, source_target_pairs={{0,1},{1,0},{2,3},{3,2},{4,5},{5,4},{6,7},{7,6},{8,9},{9,8},{10,11... | collective-permute-start | bytes 776 | tf_op jit(solution)/shard_map/ppermute | solution.py:295
